TPU v7x, 32 devices: a whole 2x2x4 slice. The times are simulated.
32 devices in a mesh: replica: 4 (over y, x), sparse: 8 (over z, core).
Axes of the slice: x: 2, y: 2, z: 4, core: 2. Of those that a mesh axis runs over, the one named last changes fastest.
Arguments:
- item_table: bfloat16 [4096, 512], P('sparse'), may hold values from -5 to 5
- action_table: bfloat16 [4096, 512], P('sparse'), may hold values from -5 to 5
- item_owner: int32 [16384, 1], P(('replica', 'sparse')), may hold values from 0 to 7; in each aligned block of 512 rows (0 to 511, 512 to 1023, ...) at most 128 rows name the same one
- item_row: int32 [16384], P(('replica', 'sparse')), may hold values from 0 to 511
- action_owner: int32 [16384, 1], P(('replica', 'sparse')), may hold values from 0 to 7; in each aligned block of 512 rows (0 to 511, 512 to 1023, ...) at most 128 rows name the same one
- action_row: int32 [16384], P(('replica', 'sparse')), may hold values from 0 to 511
- input_norm_gain: float32 [512], replicated, may hold values from 0.4 to 1.6
- w_proj: bfloat16 [512, 2048], replicated, may hold values from -0.25 to 0.25
- w_out: bfloat16 [512, 512], replicated, may hold values from -0.25 to 0.25
- cotangent: bfloat16 [16384, 512], P(('replica', 'sparse')), may hold values from -0.59765625 to 0.59765625
Outputs:
- layer_out: bfloat16 [16384, 512], P(('replica', 'sparse'))
- item_grad: float32 [4096, 512], P('sparse', 'replica')
- action_grad: float32 [4096, 512], P('sparse', 'replica')
- grad_proj: float32 [512, 2048], P('sparse')
- grad_out: float32 [512, 512], P('sparse')
Inputs may be any that keep to these rules, and one draw needn't show every extreme that they name: `item_owner`: in the rows of one device, no owner is named by more than 128 rows, a bound that some block reaches. `action_owner`: in the rows of one device, no owner is named by more than 128 rows, a bound that some block reaches.
All inputs are finite; a program needn't handle non-finite values.
Results may differ from a plain program's by a relative error of at most 0.015.
Values may be sent and summed in bfloat16 or wider, within the bound.
No kernel may reach another device: no remote copies, remote signals or barrier semaphores. Data moves between devices by JAX's collectives and lax.ppermute only.
A program may use at most 64 MiB of HBM per device.

v0:
```python
import jax
import jax.numpy as jnp
from jax import lax
from jax.sharding import PartitionSpec as P

HEADS = 4


EPS = 1e-05


def silu_grad(value):
    sig = jax.nn.sigmoid(value)
    return sig * (1.0 + value * (1.0 - sig))


def apply_input_norm(value):
    centered = value - jnp.mean(value, axis=-1, keepdims=True)
    scale = lax.rsqrt(jnp.mean(centered * centered, axis=-1, keepdims=True) + EPS)
    return (centered * scale, scale)


def norm_backward(upper, hat, scale):
    return scale * (
        upper
        - jnp.mean(upper, axis=-1, keepdims=True)
        - hat * jnp.mean(upper * hat, axis=-1, keepdims=True)
    )


def mix(form, left, right):
    return jnp.einsum(form, left, right, preferred_element_type=jnp.float32)


def sequence_pass(embedded, cotangent, input_norm_gain, w_proj, w_out):
    length, width = embedded.shape
    head_dim = width // HEADS
    factor = head_dim ** (-0.5)
    full_input_rows = embedded.astype(jnp.float32)
    centered_scaled_input, input_inverse_scale = apply_input_norm(full_input_rows)
    normalized_rows = (centered_scaled_input * input_norm_gain).astype(jnp.bfloat16)
    proj = jnp.dot(normalized_rows, w_proj, preferred_element_type=jnp.float32)
    act = jax.nn.silu(proj).astype(jnp.bfloat16)
    upart = act[:, :width]
    vheads = act[:, width : 2 * width].reshape(length, HEADS, head_dim)
    qheads = act[:, 2 * width : 3 * width].reshape(length, HEADS, head_dim)
    kheads = act[:, 3 * width :].reshape(length, HEADS, head_dim)
    causal = (jnp.arange(length)[None, :] <= jnp.arange(length)[:, None]).astype(jnp.float32)
    scores = mix("qhd,khd->hqk", qheads, kheads) * factor
    attn = (jax.nn.silu(scores) * causal / length).astype(jnp.bfloat16)
    attended = mix("hqk,khd->qhd", attn, vheads).reshape(length, width)
    ohat, oscale = apply_input_norm(attended)
    gated = (ohat * upart.astype(jnp.float32)).astype(jnp.bfloat16)
    layer_out = (
        full_input_rows + jnp.dot(gated, w_out, preferred_element_type=jnp.float32)
    ).astype(jnp.bfloat16)
    dgated = lax.dot_general(
        cotangent, w_out, (((1,), (1,)), ((), ())), preferred_element_type=jnp.float32
    )
    dupart = dgated * ohat
    dattended = norm_backward(dgated * upart.astype(jnp.float32), ohat, oscale).astype(jnp.bfloat16)
    dheads = dattended.reshape(length, HEADS, head_dim)
    dattn = mix("qhd,khd->hqk", dheads, vheads)
    dvalues = mix("hqk,qhd->khd", attn, dheads).reshape(length, width)
    dscores = (dattn * causal * silu_grad(scores) * (factor / length)).astype(jnp.bfloat16)
    dquery = mix("hqk,khd->qhd", dscores, kheads).reshape(length, width)
    dkeys = mix("hqk,qhd->khd", dscores, qheads).reshape(length, width)
    dact = jnp.concatenate([dupart, dvalues, dquery, dkeys], axis=1)
    dproj = (dact * silu_grad(proj)).astype(jnp.bfloat16)
    normalized_gradient = lax.dot_general(
        dproj, w_proj, (((1,), (1,)), ((), ())), preferred_element_type=jnp.float32
    )
    token_gradient = (
        cotangent.astype(jnp.float32)
        + norm_backward(
            normalized_gradient * input_norm_gain, centered_scaled_input, input_inverse_scale
        )
    ).astype(jnp.bfloat16)
    return (layer_out, token_gradient, normalized_rows, dproj, gated)


def slots_of(owner, shards, counted):
    onehot = (owner[:, None] == jnp.arange(shards, dtype=jnp.int32)[None, :]).astype(
        jnp.int32
    ) * counted[:, None]
    before = jnp.cumsum(onehot, axis=0) - onehot
    return jnp.sum(before * onehot, axis=1)


def placement(owner, slot, shards, capacity):
    flat = owner * capacity + slot
    every_slot = jnp.arange(shards * capacity, dtype=jnp.int32)
    return every_slot[:, None] == flat[None, :]


def asks_of(placed, row, shards, capacity):
    return jnp.max(jnp.where(placed, row[None, :], 0), axis=1).reshape(shards, capacity)


def pick_rows(placed_bf, fetched):
    flat = fetched.reshape(-1, fetched.shape[-1])
    return lax.dot_general(
        placed_bf, flat, (((0,), (0,)), ((), ())), preferred_element_type=jnp.float32
    )


def local(
    item_table,
    action_table,
    item_owner,
    item_row,
    action_owner,
    action_row,
    input_norm_gain,
    w_proj,
    w_out,
    cotangent,
):
    shards = lax.axis_size("sparse")
    length = item_row.shape[0]
    rows_dev = item_table.shape[0]
    width = item_table.shape[1]
    capacity = 2 * length // shards
    item_own = item_owner[:, 0]
    action_own = action_owner[:, 0]
    every_one = jnp.ones((length,), jnp.int32)
    item_slot = slots_of(item_own, shards, every_one)
    action_slot = slots_of(action_own, shards, every_one)
    item_placed = placement(item_own, item_slot, shards, capacity)
    action_placed = placement(action_own, action_slot, shards, capacity)
    item_asks = asks_of(item_placed, item_row, shards, capacity)
    action_asks = asks_of(action_placed, action_row, shards, capacity)
    item_placed_bf = item_placed.astype(jnp.bfloat16)
    action_placed_bf = action_placed.astype(jnp.bfloat16)
    received = (
        lax.all_to_all(item_asks, "sparse", split_axis=0, concat_axis=0, tiled=True),
        lax.all_to_all(action_asks, "sparse", split_axis=0, concat_axis=0, tiled=True),
    )
    fetched_item = lax.all_to_all(
        item_table[received[0]], "sparse", split_axis=0, concat_axis=0, tiled=True
    )
    fetched_action = lax.all_to_all(
        action_table[received[1]], "sparse", split_axis=0, concat_axis=0, tiled=True
    )
    item_seen = received[0]
    action_seen = received[1]
    item_rows = pick_rows(item_placed_bf, fetched_item)
    action_rows = pick_rows(action_placed_bf, fetched_action)
    embedded = (item_rows + action_rows).astype(jnp.bfloat16)
    layer_out, token_gradient, normalized_rows, dproj, gated = sequence_pass(
        embedded, cotangent, input_norm_gain, w_proj, w_out
    )
    first = lax.dot_general(
        normalized_rows, dproj, (((0,), (0,)), ((), ())), preferred_element_type=jnp.float32
    )
    second = lax.dot_general(
        gated, cotangent, (((0,), (0,)), ((), ())), preferred_element_type=jnp.float32
    )
    own_dense = lax.psum_scatter(
        jnp.concatenate([first, second], axis=1), "sparse", scatter_dimension=0, tiled=True
    )
    dense_total = lax.psum(own_dense.astype(jnp.bfloat16), "replica").astype(jnp.float32)
    local_rows = jnp.arange(rows_dev, dtype=jnp.int32)[:, None]
    item_sums = jnp.dot(item_placed_bf, token_gradient, preferred_element_type=jnp.float32).reshape(
        shards, capacity, width
    )
    action_sums = jnp.dot(
        action_placed_bf, token_gradient, preferred_element_type=jnp.float32
    ).reshape(shards, capacity, width)
    item_hot = (item_seen.reshape(-1)[None, :] == local_rows).astype(jnp.bfloat16)
    action_hot = (action_seen.reshape(-1)[None, :] == local_rows).astype(jnp.bfloat16)
    item_send = item_sums.astype(jnp.bfloat16)
    action_send = action_sums.astype(jnp.bfloat16)
    item_recv, action_recv = (
        lax.all_to_all(item_send, "sparse", split_axis=0, concat_axis=0, tiled=True),
        lax.all_to_all(action_send, "sparse", split_axis=0, concat_axis=0, tiled=True),
    )
    owned_item = jnp.dot(item_hot, item_recv.reshape(-1, width), preferred_element_type=jnp.float32)
    owned_action = jnp.dot(
        action_hot, action_recv.reshape(-1, width), preferred_element_type=jnp.float32
    )
    item_grad, action_grad = (
        lax.psum_scatter(
            owned_item.astype(jnp.bfloat16), "replica", scatter_dimension=1, tiled=True
        ).astype(jnp.float32),
        lax.psum_scatter(
            owned_action.astype(jnp.bfloat16), "replica", scatter_dimension=1, tiled=True
        ).astype(jnp.float32),
    )
    return (
        layer_out,
        item_grad,
        action_grad,
        dense_total[:, : 4 * width],
        dense_total[:, 4 * width :],
    )


def solution(mesh):
    in_specs = (
        P("sparse", None),
        P("sparse", None),
        P(("replica", "sparse"), None),
        P(("replica", "sparse")),
        P(("replica", "sparse"), None),
        P(("replica", "sparse")),
        P(),
        P(),
        P(),
        P(("replica", "sparse"), None),
    )
    out_specs = (
        P(("replica", "sparse"), None),
        P("sparse", "replica"),
        P("sparse", "replica"),
        P("sparse", None),
        P("sparse", None),
    )
    return jax.shard_map(local, mesh=mesh, in_specs=in_specs, out_specs=out_specs, check_vma=False)
```

profile of v0, /device:TPU:0, one launch (start us, length us, event | category | flops | bytes accessed | tf_op | source)
XLA Modules:
  0.0 357.9 jit_solution(13424140482974993999)
XLA Ops:
  7.2 0.8 fusion.58
  8.0 1.1 reduce-window.16
  9.4 0.8 fusion.54
  10.2 0.7 multiply_add_fusion
  10.9 1.6 select_reduce_fusion
  12.5 6.3 %all-to-all-start.2 = ((s32[8,1,128]{2,1,0:T(1,128)}), s32[8,1,128]{2,1,0:T(1,128)S(1)}, u32[]{:S(2)}, u32[]{:S(2)}) async-start(s32[8,1,128]{2,1,0:T(1,128)} %bitcast.13), calls=%async_computation.2 | async-start | bytes 8192 | tf_op jit(solution)/shard_map/all_to_all | solution.py:137
  18.8 0.7 fusion.57
  19.5 1.1 reduce-window.14
  20.9 0.8 fusion.56
  22.3 1.6 select_reduce_fusion.1
  24.3 4.8 %all-to-all-start = ((s32[8,1,128]{2,1,0:T(1,128)}), s32[8,1,128]{2,1,0:T(1,128)S(1)}, u32[]{:S(2)}, u32[]{:S(2)}) async-start(s32[8,1,128]{2,1,0:T(1,128)} %bitcast.4), calls=%async_computation | async-start | bytes 8192 | tf_op jit(solution)/shard_map/all_to_all | solution.py:136
  29.1 6.3 %gather_fusion.1 = bf16[1024,512]{1,0:T(8,128)(2,1)} fusion(bf16[512,512]{1,0:T(8,128)(2,1)} %param.11, s32[1024]{0:T(1024)S(1)} %fusion.62), kind=kCustom, calls=%fused_computation.1 | custom fusion | bytes 2101248 | tf_op jit(solution)/shard_map/gather | solution.py:143
  35.4 5.1 %all-to-all-start.3 = ((bf16[8,128,512]{2,1,0:T(8,128)(2,1)}), bf16[8,128,512]{2,1,0:T(8,128)(2,1)}, u32[]{:S(2)}, u32[]{:S(2)}) async-start(bf16[8,128,512]{2,1,0:T(8,128)(2,1)} %bitcast.107), calls=%async_computation.3 | async-start | bytes 2097152 | tf_op jit(solution)/shard_map/all_to_all | solution.py:142
  40.5 5.1 %gather_fusion = bf16[1024,512]{1,0:T(8,128)(2,1)} fusion(bf16[512,512]{1,0:T(8,128)(2,1)S(1)} %copy-done.1, s32[1024]{0:T(1024)S(1)} %fusion.60), kind=kCustom, calls=%fused_computation | custom fusion | bytes 2101248 | tf_op jit(solution)/shard_map/gather | solution.py:140
  45.6 21.6 %all-to-all-done.3 = bf16[8,128,512]{2,1,0:T(8,128)(2,1)} async-done(((bf16[8,128,512]{2,1,0:T(8,128)(2,1)}), bf16[8,128,512]{2,1,0:T(8,128)(2,1)}, u32[]{:S(2)}, u32[]{:S(2)}) %all-to-all-start.3) | async-done | bytes 1048608 | tf_op jit(solution)/shard_map/all_to_all | solution.py:142
  67.2 3.6 all-to-all-start.1
  70.8 1.2 fusion.35
  72.0 3.0 fusion.2
  75.0 22.3 %all-to-all-done.1 = bf16[8,128,512]{2,1,0:T(8,128)(2,1)S(1)} async-done(((bf16[8,128,512]{2,1,0:T(8,128)(2,1)}), bf16[8,128,512]{2,1,0:T(8,128)(2,1)S(1)}, u32[]{:S(2)}, u32[]{:S(2)}) %all-to-all-start.1) | async-done | bytes 1048608 | tf_op jit(solution)/shard_map/all_to_all | solution.py:139
  97.3 2.0 convert_reduce_fusion
  99.5 3.9 %multiply_convert_fusion.2 = (bf16[512,2048]{1,0:T(8,128)(2,1)S(1)}, f32[512,2048]{1,0:T(8,128)}) fusion(bf16[512,2048]{1,0:T(8,128)(2,1)S(1)} %copy-done, bf16[512,512]{0,1:T(8,128)(2,1)S(1)} %get-tuple-element.41, f32[512]{0:T(512)S(1)} %copy-done.20, f32[512]{0:T(512)S(1)} %add_rsqrt_fusion.1, f32[512]{0:T(512)S(1)} %broadcast_multiply_fusion.5), kind=kOutput, calls=%fused_computation.8 | convolution fusion | flops 1080295424 | bytes 8919040 | tf_op jit(solution)/shard_map/dot_general | solution.py:42
  103.4 1.4 copy-done.11
  104.8 1.2 slice_bitcast_fusion
  106.1 1.4 copy.117
  107.6 5.0 %multiply_convert_fusion.1 = (bf16[4,512,512]{2,1,0:T(8,128)(2,1)S(1)}, f32[4,512,512]{2,1,0:T(8,128)}) fusion(f32[512,512]{1,0:T(8,128)} %fusion.35, bf16[512,4,128]{0,2,1:T(8,128)(2,1)S(1)} %bitcast.111, bf16[512,4,128]{0,2,1:T(8,128)(2,1)S(1)} %bitcast.113), kind=kOutput, calls=%fused_computation.6 | convolution fusion | flops 276824064 | bytes 8388608 | tf_op jit(solution)/shard_map/qhd,khd->hqk/dot_general | solution.py:32
  112.6 1.3 copy-done.4
  113.9 0.8 fusion.64
  115.0 1.3 copy.108
  116.3 2.5 fusion.48
  118.8 2.8 fusion.37
  122.2 2.4 multiply_convert_fusion
  124.6 1.8 fusion.65
  126.5 1.4 fusion.66
  127.9 1.4 copy.109
  129.2 2.5 copy.110
  131.8 2.6 copy.111
  134.3 4.3 %fusion = bf16[512,2048]{1,0:T(8,128)(2,1)S(1)} fusion(f32[512,512]{1,0:T(8,128)} %copy.111, f32[512,512]{1,0:T(8,128)} %copy.110, f32[512,512]{1,0:T(8,128)} %copy.109, f32[512,512]{1,0:T(8,128)} %get-tuple-element.36, f32[512,2048]{1,0:T(8,128)} %get-tuple-element.43), kind=kLoop, calls=%fused_computation.4 | loop fusion | flops 12582912 | bytes 10485760 | tf_op jit(solution)/shard_map/convert_element_type | solution.py:69
  138.7 1.4 copy-done.3
  140.0 1.3 fusion.49
  141.8 2.8 pad_maximum_fusion
  144.6 1.0 copy.92
  145.6 3.0 fusion.63
  149.0 1.8 fusion.8
  150.8 4.2 %all-to-all-start.5 = ((bf16[8,128,512]{2,1,0:T(8,128)(2,1)}), bf16[8,128,512]{2,1,0:T(8,128)(2,1)}, u32[]{:S(2)}, u32[]{:S(2)}) async-start(bf16[8,128,512]{2,1,0:T(8,128)(2,1)} %bitcast.119), calls=%async_computation.5 | async-start | bytes 2097152 | tf_op jit(solution)/shard_map/all_to_all | solution.py:176
  155.0 1.8 fusion.7
  156.8 42.0 %all-to-all-done.5 = bf16[8,128,512]{2,1,0:T(8,128)(2,1)} async-done(((bf16[8,128,512]{2,1,0:T(8,128)(2,1)}), bf16[8,128,512]{2,1,0:T(8,128)(2,1)}, u32[]{:S(2)}, u32[]{:S(2)}) %all-to-all-start.5) | async-done | bytes 1048608 | tf_op jit(solution)/shard_map/all_to_all | solution.py:176
  198.8 4.2 %all-to-all-start.4 = ((bf16[8,128,512]{2,1,0:T(8,128)(2,1)}), bf16[8,128,512]{2,1,0:T(8,128)(2,1)}, u32[]{:S(2)}, u32[]{:S(2)}) async-start(bf16[8,128,512]{2,1,0:T(8,128)(2,1)} %bitcast.117), calls=%async_computation.4 | async-start | bytes 2097152 | tf_op jit(solution)/shard_map/all_to_all | solution.py:175
  203.1 2.7 fusion.10
  205.8 2.1 copy.114
  208.0 33.4 %all-to-all-done.4 = bf16[8,128,512]{2,1,0:T(8,128)(2,1)} async-done(((bf16[8,128,512]{2,1,0:T(8,128)(2,1)}), bf16[8,128,512]{2,1,0:T(8,128)(2,1)}, u32[]{:S(2)}, u32[]{:S(2)}) %all-to-all-start.4) | async-done | bytes 1048608 | tf_op jit(solution)/shard_map/all_to_all | solution.py:175
  241.5 2.7 fusion.11
  244.2 2.1 copy.112
  246.4 1.8 convert_element_type.123
  248.2 2.3 fusion.12
  250.6 2.0 copy.104
  252.6 21.2 %reduce-scatter.12.cloned.1.call-done = bf16[128,512]{1,0:T(8,128)(2,1)} async-done(((bf16[512,512]{1,0:T(8,128)(2,1)}), bf16[128,512]{1,0:T(8,128)(2,1)}) %reduce-scatter.12.cloned.1.call-update) | async-done | bytes 131088
  273.8 1.0 copy.115
  274.8 0.7 convert_element_type.122
  275.6 26.1 %reduce-scatter.10.cloned.1.call-done = bf16[128,512]{1,0:T(8,128)(2,1)} async-done(((bf16[512,512]{1,0:T(8,128)(2,1)}), bf16[128,512]{1,0:T(8,128)(2,1)}) %reduce-scatter.10.cloned.1.call-update) | async-done | bytes 131088
  301.7 1.0 copy.113
  302.7 0.7 convert_element_type.118
  303.4 44.6 %all-reduce.2.cloned.1.call-done = bf16[64,2560]{1,0:T(8,128)(2,1)} async-done(((bf16[64,2560]{1,0:T(8,128)(2,1)}), bf16[64,2560]{1,0:T(8,128)(2,1)}) %all-reduce.2.cloned.1.call-update) | async-done | bytes 327696 | tf_op jit(solution)/shard_map/psum | solution.py:162
  348.1 1.8 slice.50
  349.8 1.5 slice.51
  (74 shorter events, 3.8 us)
Async XLA Ops:
  7.2 92.3 %copy-start = (bf16[512,2048]{1,0:T(8,128)(2,1)S(1)}, bf16[512,2048]{1,0:T(8,128)(2,1)}, u32[]{:S(2)}) copy-start(bf16[512,2048]{1,0:T(8,128)(2,1)} %param.17) | copy-start | bytes 6291460
  12.5 11.8 %all-to-all-start.2 = ((s32[8,1,128]{2,1,0:T(1,128)}), s32[8,1,128]{2,1,0:T(1,128)S(1)}, u32[]{:S(2)}, u32[]{:S(2)}) async-start(s32[8,1,128]{2,1,0:T(1,128)} %bitcast.13), calls=%async_computation.2 | async-start | bytes 8192 | tf_op jit(solution)/shard_map/all_to_all | solution.py:137
  24.3 11.1 %all-to-all-start = ((s32[8,1,128]{2,1,0:T(1,128)}), s32[8,1,128]{2,1,0:T(1,128)S(1)}, u32[]{:S(2)}, u32[]{:S(2)}) async-start(s32[8,1,128]{2,1,0:T(1,128)} %bitcast.4), calls=%async_computation | async-start | bytes 8192 | tf_op jit(solution)/shard_map/all_to_all | solution.py:136
  29.1 11.4 %copy-start.1 = (bf16[512,512]{1,0:T(8,128)(2,1)S(1)}, bf16[512,512]{1,0:T(8,128)(2,1)}, u32[]{:S(2)}) copy-start(bf16[512,512]{1,0:T(8,128)(2,1)} %param.10) | copy-start | bytes 1572868
  35.4 31.8 %all-to-all-start.3 = ((bf16[8,128,512]{2,1,0:T(8,128)(2,1)}), bf16[8,128,512]{2,1,0:T(8,128)(2,1)}, u32[]{:S(2)}, u32[]{:S(2)}) async-start(bf16[8,128,512]{2,1,0:T(8,128)(2,1)} %bitcast.107), calls=%async_computation.3 | async-start | bytes 2097152 | tf_op jit(solution)/shard_map/all_to_all | solution.py:142
  67.2 30.1 %all-to-all-start.1 = ((bf16[8,128,512]{2,1,0:T(8,128)(2,1)}), bf16[8,128,512]{2,1,0:T(8,128)(2,1)S(1)}, u32[]{:S(2)}, u32[]{:S(2)}) async-start(bf16[8,128,512]{2,1,0:T(8,128)(2,1)} %bitcast.106), calls=%async_computation.1 | async-start | bytes 2097152 | tf_op jit(solution)/shard_map/all_to_all | solution.py:139
  70.7 175.6 %reduce-scatter.8.cloned.1.call-start = ((), (), s32[]{:S(2)}) async-start(), calls=%async_computation.9 | async-start | bytes 5898240 | tf_op jit(solution)/shard_map/reduce_scatter | solution.py:159
  72.0 27.5 %copy-start.20 = (f32[512]{0:T(512)S(1)}, f32[512]{0:T(512)}, u32[]{:S(2)}) copy-start(f32[512]{0:T(512)} %param.16) | copy-start | bytes 6148
  99.3 4.1 %copy-start.6 = (bf16[512,512]{0,1:T(8,128)(2,1)}, bf16[512,512]{0,1:T(8,128)(2,1)S(1)}, u32[]{:S(2)}) copy-start(bf16[512,512]{0,1:T(8,128)(2,1)S(1)} %get-tuple-element.41) | copy-start | bytes 1572868
  103.4 1.4 copy-start.11
  106.1 6.5 %copy-start.12 = (bf16[512,512]{0,1:T(8,128)(2,1)}, bf16[512,512]{0,1:T(8,128)(2,1)S(1)}, u32[]{:S(2)}) copy-start(bf16[512,512]{0,1:T(8,128)(2,1)S(1)} %copy.116) | copy-start | bytes 1572868
  107.6 5.0 %copy-start.14 = (bf16[512,512]{0,1:T(8,128)(2,1)}, bf16[512,512]{0,1:T(8,128)(2,1)S(1)}, u32[]{:S(2)}) copy-start(bf16[512,512]{0,1:T(8,128)(2,1)S(1)} %copy.117) | copy-start | bytes 1572868
  107.6 6.3 %copy-start.17 = (bf16[64,4,8,128]{3,2,1,0:T(8,128)(2,1)S(1)}, bf16[64,4,8,128]{3,2,1,0:T(8,128)(2,1)}, u32[]{:S(2)}) copy-start(bf16[64,4,8,128]{3,2,1,0:T(8,128)(2,1)} %get-tuple-element.37) | copy-start | bytes 1572868
  112.6 1.3 copy-start.4
  116.3 2.5 copy-start.2
  116.3 5.4 %copy-start.5 = (bf16[4,512,512]{2,1,0:T(8,128)(2,1)S(1)}, bf16[4,512,512]{2,1,0:T(8,128)(2,1)}, u32[]{:S(2)}) copy-start(bf16[4,512,512]{2,1,0:T(8,128)(2,1)} %copy-done.4) | copy-start | bytes 6291460
  118.8 3.4 copy-start.18
  118.8 3.4 copy-start.19
  118.8 3.4 copy-start.21
  122.2 2.4 copy-start.15
  122.2 4.2 %copy-start.13 = (bf16[512,512]{0,1:T(8,128)(2,1)S(1)}, bf16[512,512]{0,1:T(8,128)(2,1)}, u32[]{:S(2)}) copy-start(bf16[512,512]{0,1:T(8,128)(2,1)} %copy-done.12) | copy-start | bytes 1572868
  134.3 5.7 %copy-start.7 = (bf16[512,512]{0,1:T(8,128)(2,1)S(1)}, bf16[512,512]{0,1:T(8,128)(2,1)}, u32[]{:S(2)}) copy-start(bf16[512,512]{0,1:T(8,128)(2,1)} %copy-done.6) | copy-start | bytes 1572868
  138.6 1.4 copy-start.3
  140.0 1.3 copy-start.8
  140.0 1.3 copy-start.9
  145.6 3.0 copy-start.16
  150.8 48.0 %all-to-all-start.5 = ((bf16[8,128,512]{2,1,0:T(8,128)(2,1)}), bf16[8,128,512]{2,1,0:T(8,128)(2,1)}, u32[]{:S(2)}, u32[]{:S(2)}) async-start(bf16[8,128,512]{2,1,0:T(8,128)(2,1)} %bitcast.119), calls=%async_computation.5 | async-start | bytes 2097152 | tf_op jit(solution)/shard_map/all_to_all | solution.py:176
  198.8 42.7 %all-to-all-start.4 = ((bf16[8,128,512]{2,1,0:T(8,128)(2,1)}), bf16[8,128,512]{2,1,0:T(8,128)(2,1)}, u32[]{:S(2)}, u32[]{:S(2)}) async-start(bf16[8,128,512]{2,1,0:T(8,128)(2,1)} %bitcast.117), calls=%async_computation.4 | async-start | bytes 2097152 | tf_op jit(solution)/shard_map/all_to_all | solution.py:175
  203.0 70.8 %reduce-scatter.12.cloned.1.call-start = ((), (), s32[]{:S(2)}) async-start(), calls=%async_computation.12 | async-start | bytes 655360
  205.8 42.4 %copy-start.10 = (bf16[512,512]{1,0:T(8,128)(2,1)S(1)}, bf16[512,512]{1,0:T(8,128)(2,1)}, u32[]{:S(2)}) copy-start(bf16[512,512]{1,0:T(8,128)(2,1)} %get-tuple-element.35) | copy-start | bytes 1572868
  208.0 93.7 %reduce-scatter.10.cloned.1.call-start = ((), (), s32[]{:S(2)}) async-start(), calls=%async_computation.11 | async-start | bytes 655360
  246.3 101.8 %all-reduce.2.cloned.1.call-start = ((), (), s32[]{:S(2)}) async-start(), calls=%async_computation.10 | async-start | bytes 655360 | tf_op jit(solution)/shard_map/psum | solution.py:162
Sparse Core Ops, SparseCore 0:
  144.7 84.9 reduce-scatter.7
  232.5 41.2 reduce-scatter.11
  276.9 24.7 reduce-scatter.9
  304.5 43.5 all-reduce.1
where the time goes:
time: 359 us; the launch traced here: 358 us
  waiting for transfers between devices  212 us (59%)
  matrix products  39.5 us (11%)
  local copies, waits for them, and re-layouts  39 us (11%)
  starting transfers between devices  28.4 us (8%)
  other arithmetic  25.1 us (7%)
  between operations  14.1 us (4%)
    unnamed x6, waiting for transfers between devices  47.4 us
    psum x1, waiting for transfers between devices, local(): lax.psum(own_dense.astype(jnp.bfloat16), 'replica').astype(jnp.float32)  44.6 us
    all_to_all x1, waiting for transfers between devices, local(): lax.all_to_all(action_send, 'sparse', split_axis=0, concat_axis=0, tiled=...  42 us
    all_to_all x1, waiting for transfers between devices, local(): lax.all_to_all(item_send, 'sparse', split_axis=0, concat_axis=0, tiled=True)  33.4 us
    all_to_all x1, waiting for transfers between devices, local(): lax.all_to_all(item_table[received[0]], 'sparse', split_axis=0, concat_ax...  22.3 us
    all_to_all x1, waiting for transfers between devices, local(): lax.all_to_all(action_table[received[1]], 'sparse', split_axis=0, concat_...  21.6 us
    unnamed x51, local copies, waits for them, and re-layouts  14.5 us
    dot_general x6, matrix products, mix(): return jnp.einsum(form, left, right, preferred_element_type=jnp.float32)  12 us
  transfers between devices with their start and end apart: 10, of which 8 were waited for; matrix products, arithmetic and copies ran while one was open for 13% of the time, Pallas kernels for 0%

commit v1 on v0

v1 whole, which is shorter than its diff:
```python
import jax
import jax.numpy as jnp
from jax import lax
from jax.experimental import pallas as pl
from jax.experimental.pallas import tpu as pltpu
from jax.sharding import PartitionSpec as P

HEADS = 4
EPS = 1e-05
LANES = 128
F32 = jnp.float32
BF16 = jnp.bfloat16
I32 = jnp.int32
VMEM_BYTES = 48 * 1024 * 1024

NN = ((1,), (0,))
NT = ((1,), (1,))
TN = ((0,), (0,))


def dot(left, right, dims=NN):
    return lax.dot_general(left, right, (dims, ((), ())), preferred_element_type=F32)


def sigmoid(value):
    return 0.5 * jnp.tanh(0.5 * value) + 0.5


def run(name, body, outs, args, smem=0, scratch=(), flops=0):
    outs = [jax.ShapeDtypeStruct(shape, dtype) for shape, dtype in outs]
    size = sum(a.size * a.dtype.itemsize for a in args)
    size += sum(o.size * o.dtype.itemsize for o in outs)
    in_smem = pl.BlockSpec(memory_space=pltpu.SMEM)
    in_vmem = pl.BlockSpec(memory_space=pltpu.VMEM)
    results = pl.pallas_call(
        body,
        out_shape=outs,
        in_specs=[in_smem] * smem + [in_vmem] * (len(args) - smem),
        out_specs=[in_vmem] * len(outs),
        scratch_shapes=list(scratch),
        compiler_params=pltpu.CompilerParams(vmem_limit_bytes=VMEM_BYTES),
        cost_estimate=pl.CostEstimate(flops=flops, bytes_accessed=size, transcendentals=0),
        name=name,
    )(*args)
    return list(results)


class Grid:
    def __init__(self):
        self.replicas = lax.axis_size("replica")
        self.shards = lax.axis_size("sparse")
        self.cores = 2 if self.shards % 2 == 0 else 1
        self.line = self.shards // self.cores
        self.r = lax.axis_index("replica")
        self.s = lax.axis_index("sparse")
        self.z = self.s // self.cores
        self.c = self.s % self.cores

    def peer(self, index, size, step):
        if size & (size - 1) == 0:
            return index ^ step
        return (step - index) % size

    def over_replica(self, value, step):
        n = self.replicas
        return lax.ppermute(value, "replica", [(i, self.peer(i, n, step)) for i in range(n)])

    def over_line(self, value, step):
        n, c = self.line, self.cores
        pairs = [(i, self.peer(i // c, n, step) * c + i % c) for i in range(n * c)]
        return lax.ppermute(value, "sparse", pairs)

    def over_pair(self, value):
        return lax.ppermute(value, "sparse", [(i, i ^ 1) for i in range(self.shards)])

    def replica_peer(self, step):
        return self.peer(self.r, self.replicas, step)

    def line_peer(self, step):
        return self.peer(self.z, self.line, step)


def fetch(keys, chunks, bases, before):
    count, many = len(keys), len(chunks)
    tokens = keys[0].shape[1]
    rows, cols = chunks[0].shape[0] // 2, chunks[0].shape[1]

    def body(base_ref, *refs):
        key_refs, chunk_refs = refs[:count], refs[count : count + many]
        before_refs, out_refs = refs[count + many : -count], refs[-count:]
        lane = lax.broadcasted_iota(I32, (tokens, LANES), 1)
        for k in range(count):
            total = before_refs[k][...].astype(F32) if before_refs else None
            for m in range(many):
                hot = []
                for table in range(2):
                    place = key_refs[k][table] - base_ref[m]
                    for start in range(0, rows, LANES):
                        hot.append(jnp.where(place == lane + start, 1.0, 0.0).astype(BF16))
                found = dot(jnp.concatenate(hot, axis=1), chunk_refs[m][...])
                total = found if total is None else total + found
            out_refs[k][...] = total.astype(BF16)

    return run(
        "fetch",
        body,
        [((tokens, cols), BF16)] * count,
        [bases, *keys, *chunks, *before],
        smem=1,
        flops=2 * count * many * tokens * 2 * rows * cols,
    )


def gather_grad(keys, pieces, bases, rows):
    count, many = len(keys), bases.shape[0]
    tokens, cols = pieces[0].shape

    def body(base_ref, *refs):
        key_refs, piece_refs, out_refs = refs[:count], refs[count : 2 * count], refs[2 * count :]
        piece = jnp.concatenate([ref[...] for ref in piece_refs], axis=0)
        row = lax.broadcasted_iota(I32, (rows, tokens), 0)
        for m in range(many):
            for table in range(2):
                hot = []
                for k in range(count):
                    place = key_refs[k][table : table + 1, :] - base_ref[m]
                    hot.append(jnp.where(place == row, 1.0, 0.0).astype(BF16))
                sums = dot(jnp.concatenate(hot, axis=1), piece)
                out_refs[m][table * rows : (table + 1) * rows, :] = sums.astype(BF16)

    return run(
        "gather_grad",
        body,
        [((2 * rows, cols), BF16)] * many,
        [bases, *keys, *pieces],
        smem=1,
        flops=2 * count * many * tokens * 2 * rows * cols,
    )


def sequence(blocks, pieces, cotangent, gain, w_proj, w_out):
    count = len(pieces)
    length, width = cotangent.shape
    cols = width // count
    head_dim = width // HEADS
    factor = head_dim ** (-0.5)
    tile = min(256, length)
    step = min(256, 4 * width)

    def body(block_ref, *refs):
        piece_refs = refs[:count]
        cot_ref, gain_ref, wp_ref, wo_ref = refs[count : count + 4]
        out_ref, *grad_refs = refs[count + 4 : 2 * count + 5]
        normed_ref, dproj_ref, gated_ref = refs[2 * count + 5 : 2 * count + 8]
        emb, act, slope, att, attn, dscale, dkey, dval, tok = refs[2 * count + 8 :]

        def start_of(k):
            return pl.multiple_of(block_ref[k] * cols, cols)

        for k in range(count):
            emb[:, pl.ds(start_of(k), cols)] = piece_refs[k][...]

        def norm_of(value):
            centred = value - jnp.mean(value, axis=-1, keepdims=True)
            scale = lax.rsqrt(jnp.mean(centred * centred, axis=-1, keepdims=True) + EPS)
            return centred * scale, scale

        def norm_back(upper, hat, scale):
            return scale * (
                upper
                - jnp.mean(upper, axis=-1, keepdims=True)
                - hat * jnp.mean(upper * hat, axis=-1, keepdims=True)
            )

        for at in range(0, length, tile):
            span = slice(at, at + tile)
            hat, _ = norm_of(emb[span, :].astype(F32))
            normed_ref[span, :] = (hat * gain_ref[...]).astype(BF16)

        normed = normed_ref[...]

        @pl.loop(0, 4 * width // step)
        def _(j):
            span = pl.ds(pl.multiple_of(j * step, step), step)
            proj = dot(normed, wp_ref[:, span])
            sig = sigmoid(proj)
            act[:, span] = (proj * sig).astype(BF16)
            slope[:, span] = sig * (1.0 + proj * (1.0 - sig))

        dkey[...] = jnp.zeros_like(dkey)
        dval[...] = jnp.zeros_like(dval)

        for at in range(0, length, tile):
            span = slice(at, at + tile)
            seen = at + tile
            past = slice(0, seen)
            keep = lax.broadcasted_iota(I32, (tile, seen), 1) <= at + lax.broadcasted_iota(
                I32, (tile, seen), 0
            )
            for h in range(HEADS):
                head = [slice(p * width + h * head_dim, p * width + (h + 1) * head_dim) for p in range(4)]
                scores = dot(act[span, head[2]], act[past, head[3]], NT) * factor
                sig = sigmoid(scores)
                soft = jnp.where(keep, scores * sig * (1.0 / length), 0.0).astype(BF16)
                attn[h, :, :seen] = soft
                grad = sig * (1.0 + scores * (1.0 - sig)) * (factor / length)
                dscale[h, :, :seen] = jnp.where(keep, grad, 0.0)
                att[:, head[0]] = dot(soft, act[past, head[1]])
            hat, scale = norm_of(att[...])
            gate = act[span, :width].astype(F32)
            gated = (hat * gate).astype(BF16)
            gated_ref[span, :] = gated
            out_ref[span, :] = (emb[span, :].astype(F32) + dot(gated, wo_ref[...])).astype(BF16)
            dgated = dot(cot_ref[span, :], wo_ref[...], NT)
            dproj_ref[span, :width] = (dgated * hat * slope[span, :width]).astype(BF16)
            datt = norm_back(dgated * gate, hat, scale).astype(BF16)
            for h in range(HEADS):
                head = [slice(p * width + h * head_dim, p * width + (h + 1) * head_dim) for p in range(4)]
                dhead = datt[:, head[0]]
                dattn = dot(dhead, act[past, head[1]], NT)
                dscores = (dattn * dscale[h, :, :seen]).astype(BF16)
                dquery = dot(dscores, act[past, head[3]])
                dproj_ref[span, head[2]] = (dquery * slope[span, head[2]]).astype(BF16)
                dkey[past, head[0]] += dot(dscores, act[span, head[2]], TN)
                dval[past, head[0]] += dot(attn[h, :, :seen], dhead, TN)

        dproj_ref[:, width : 2 * width] = (dval[...] * slope[:, width : 2 * width]).astype(BF16)
        dproj_ref[:, 3 * width :] = (dkey[...] * slope[:, 3 * width :]).astype(BF16)

        for at in range(0, length, tile):
            span = slice(at, at + tile)
            hat, scale = norm_of(emb[span, :].astype(F32))
            upper = dot(dproj_ref[span, :], wp_ref[...], NT) * gain_ref[...]
            grad = cot_ref[span, :].astype(F32) + norm_back(upper, hat, scale)
            tok[span, :] = grad.astype(BF16)

        for k in range(count):
            grad_refs[k][...] = tok[:, pl.ds(start_of(k), cols)]

    return run(
        "sequence",
        body,
        [((length, width), BF16)]
        + [((length, cols), BF16)] * count
        + [((length, width), BF16), ((length, 4 * width), BF16), ((length, width), BF16)],
        [blocks, *pieces, cotangent, gain, w_proj, w_out],
        smem=1,
        scratch=[
            pltpu.VMEM((length, width), BF16),
            pltpu.VMEM((length, 4 * width), BF16),
            pltpu.VMEM((length, 4 * width), F32),
            pltpu.VMEM((tile, width), F32),
            pltpu.VMEM((HEADS, tile, length), BF16),
            pltpu.VMEM((HEADS, tile, length), F32),
            pltpu.VMEM((length, width), F32),
            pltpu.VMEM((length, width), F32),
            pltpu.VMEM((length, width), BF16),
        ],
        flops=28 * length * width * width,
    )


def weight_grad(core, normed, dproj, gated, cotangent, cores, line):
    length, width = normed.shape
    rows = width // (cores * line)
    half = width // cores
    total = dproj.shape[1] + cotangent.shape[1]

    def body(core_ref, n_ref, d_ref, g_ref, c_ref, *out_refs):
        feature = lax.broadcasted_iota(I32, (width, half), 0)
        column = lax.broadcasted_iota(I32, (width, half), 1)
        for m, out_ref in enumerate(out_refs):
            parity = (core_ref[0] + cores - 1 - m) % cores
            wanted = (column // rows * cores + parity) * rows + column % rows
            pick = jnp.where(feature == wanted, 1.0, 0.0).astype(BF16)
            n_part = dot(n_ref[...], pick).astype(BF16)
            g_part = dot(g_ref[...], pick).astype(BF16)
            edge = d_ref.shape[1]
            for at in range(0, edge, width):
                out_ref[:, at : at + width] = dot(n_part, d_ref[:, at : at + width], TN).astype(BF16)
            out_ref[:, edge:] = dot(g_part, c_ref[...], TN).astype(BF16)

    return run(
        "weight_grad",
        body,
        [((half, total), BF16)] * cores,
        [core, normed, dproj, gated, cotangent],
        smem=1,
        flops=2 * length * width * (total + 2 * width),
    )


def add_and_split(blocks, parts, along, out_first=F32):
    count = blocks.shape[0]
    shape = list(parts[0].shape)
    whole = tuple(shape)
    shape[along] //= count
    size = shape[along]

    def body(block_ref, *refs):
        part_refs, out_refs, held = refs[: len(parts)], refs[len(parts) : -1], refs[-1]
        total = part_refs[0][...].astype(F32)
        for ref in part_refs[1:]:
            total = total + ref[...].astype(F32)
        held[...] = total
        for k in range(count):
            span = pl.ds(pl.multiple_of(block_ref[k] * size, size), size)
            piece = held[:, span] if along == 1 else held[span, :]
            out_refs[k][...] = piece.astype(out_refs[k].dtype)

    dtypes = [out_first] + [BF16] * (count - 1)
    return run(
        "add_and_split",
        body,
        [(tuple(shape), dtype) for dtype in dtypes],
        [blocks, *parts],
        smem=1,
        scratch=[pltpu.VMEM(whole, F32)],
    )


def assemble(blocks, parts, edge):
    rows, cols = parts[0].shape
    total = cols * len(parts)

    def body(block_ref, *refs):
        part_refs, (left_ref, right_ref, held) = refs[: len(parts)], refs[len(parts) :]
        for k, ref in enumerate(part_refs):
            held[:, pl.ds(pl.multiple_of(block_ref[k] * cols, cols), cols)] = ref[...].astype(F32)
        left_ref[...] = held[:, :edge]
        right_ref[...] = held[:, edge:]

    return run(
        "assemble",
        body,
        [((rows, edge), F32), ((rows, total - edge), F32)],
        [blocks, *parts],
        smem=1,
        scratch=[pltpu.VMEM((rows, total), F32)],
    )


def local(
    item_table,
    action_table,
    item_owner,
    item_row,
    action_owner,
    action_row,
    input_norm_gain,
    w_proj,
    w_out,
    cotangent,
):
    grid = Grid()
    rows, width = item_table.shape
    replicas, line, cores = grid.replicas, grid.line, grid.cores
    length = item_row.shape[0]
    cols = width // replicas
    blocks = jnp.stack([grid.replica_peer(k) for k in range(replicas)]).astype(I32)
    planes = jnp.stack([grid.line_peer(k) for k in range(line)]).astype(I32)

    def bases_of(k):
        first = grid.line_peer(k) * cores
        return jnp.stack([(first + (grid.c + m) % cores) * rows for m in range(cores)]).astype(I32)

    own = jnp.concatenate(
        [
            lax.dynamic_slice_in_dim(item_table, grid.r * cols, cols, 1),
            lax.dynamic_slice_in_dim(action_table, grid.r * cols, cols, 1),
        ],
        axis=0,
    )
    keys = jnp.stack(
        [item_owner[:, 0] * rows + item_row, action_owner[:, 0] * rows + action_row]
    ).astype(I32)

    held = [own] + [grid.over_line(own, k) for k in range(1, line)]
    key_rows = [keys] + [grid.over_replica(keys, k) for k in range(1, replicas)]
    key_cols = [jnp.broadcast_to(k[:, :, None], (2, length, LANES)) for k in key_rows]

    found = []
    for k in range(line):
        chunks = [held[k]] + ([grid.over_pair(held[k])] if cores == 2 else [])
        found = fetch(key_cols, chunks, bases_of(k), found)
    pieces = found[:1] + [grid.over_replica(found[k], k) for k in range(1, replicas)]

    layer_out, *rest = sequence(
        blocks, pieces, cotangent, input_norm_gain.reshape(1, width), w_proj, w_out
    )
    tokens, (normed, dproj, gated) = rest[:replicas], rest[replicas:]
    tokens = tokens[:1] + [grid.over_replica(tokens[k], k) for k in range(1, replicas)]

    order = list(range(1, line)) + [0]
    sums = {}
    for k in order:
        mine, *other = gather_grad(key_rows, tokens, bases_of(k), rows)
        total = mine.astype(F32)
        for part in other:
            total = total + grid.over_pair(part).astype(F32)
        sums[k] = grid.over_line(total.astype(BF16), k) if k else total
    table_grad = sums[0]
    for k in range(1, line):
        table_grad = table_grad + sums[k].astype(F32)

    parts = weight_grad(grid.c.reshape(1), normed, dproj, gated, cotangent, cores, line)
    mine, other = parts[-1], parts[:-1]
    split = add_and_split(blocks, [mine] + [grid.over_pair(o) for o in other], 1)
    parts = split[:1] + [grid.over_replica(split[k], k) for k in range(1, replicas)]
    split = add_and_split(planes, parts, 0)
    parts = split[:1] + [grid.over_line(split[k], k) for k in range(1, line)]
    total = parts[0]
    for part in parts[1:]:
        total = total + part.astype(F32)
    total = total.astype(BF16)
    parts = [total] + [grid.over_replica(total, k) for k in range(1, replicas)]
    grad_proj, grad_out = assemble(blocks, parts, 4 * width)

    return layer_out, table_grad[:rows], table_grad[rows:], grad_proj, grad_out


def solution(mesh):
    tokens = ("replica", "sparse")
    in_specs = (
        P("sparse", None),
        P("sparse", None),
        P(tokens, None),
        P(tokens),
        P(tokens, None),
        P(tokens),
        P(),
        P(),
        P(),
        P(tokens, None),
    )
    out_specs = (
        P(tokens, None),
        P("sparse", "replica"),
        P("sparse", "replica"),
        P("sparse", None),
        P("sparse", None),
    )
    return jax.shard_map(local, mesh=mesh, in_specs=in_specs, out_specs=out_specs, check_vma=False)
```

time: 359 us -> 134 us (0.37)
  waiting for transfers between devices: 212 us -> 38.2 us
  Pallas kernels: 0 us -> 43 us
  matrix products: 39.5 us -> 0 us
  local copies, waits for them, and re-layouts: 39 us -> 3.94 us
  other arithmetic: 25.1 us -> 3.63 us
  starting transfers between devices: 28.4 us -> 44 us
  between operations: 14.1 us -> 0.91 us
    all_to_all x6 -> x0, waiting for transfers between devices: 120 us -> none  [the longest x1 42 us: local(): lax.all_to_all(action_send, 'sparse', split_axis=0, concat_axis=0, tiled=...]
    unnamed x6 -> x0, waiting for transfers between devices: 47.4 us -> none
    psum x1 -> x0, waiting for transfers between devices: 44.6 us -> none  [local(): lax.psum(own_dense.astype(jnp.bfloat16), 'replica').astype(jnp.float32)]
    ppermute x0 -> x33, starting transfers between devices: none -> 44 us  [the longest x9 20.9 us: over_line(): return lax.ppermute(value, 'sparse', pairs)]
    pallas_call x0 -> x13, Pallas kernels: none -> 43 us  [run(): pl.pallas_call(body, out_shape=outs, in_specs=[in_smem] * smem + [in_vmem...]
    dot_general x18 -> x0, matrix products: 39.5 us -> none  [the longest x6 12 us: mix(): return jnp.einsum(form, left, right, preferred_element_type=jnp.float32)]
    ppermute x0 -> x33, waiting for transfers between devices: none -> 38.2 us  [the longest x15 26.3 us: over_replica(): lax.ppermute(value, 'replica', [(i, self.peer(i, n, step)) for i in range...]
    all_to_all x6 -> x0, starting transfers between devices: 28.2 us -> none  [the longest x1 6.33 us: local(): lax.all_to_all(action_asks, 'sparse', split_axis=0, concat_axis=0, tiled=...]
  transfers between devices with their start and end apart: 10 -> 33, of which waited for: 8 -> 17; matrix products, arithmetic and copies ran while one was open for 13% -> 4% of each run, Pallas kernels for 0% -> 16%
where the time goes in v1:
time: 134 us
  starting transfers between devices  44 us (33%)
  Pallas kernels  43 us (32%)
  waiting for transfers between devices  38.2 us (29%)
  local copies, waits for them, and re-layouts  3.94 us (3%)
  other arithmetic  3.63 us (3%)
    pallas_call x13, Pallas kernels, run(): pl.pallas_call(body, out_shape=outs, in_specs=[in_smem] * smem + [in_vmem...  43 us
    ppermute x15, waiting for transfers between devices, over_replica(): lax.ppermute(value, 'replica', [(i, self.peer(i, n, step)) for i in range...  26.3 us
    ppermute x9, starting transfers between devices, over_line(): return lax.ppermute(value, 'sparse', pairs)  20.9 us
    ppermute x15, starting transfers between devices, over_replica(): lax.ppermute(value, 'replica', [(i, self.peer(i, n, step)) for i in range...  20.5 us
    ppermute x9, waiting for transfers between devices, over_line(): return lax.ppermute(value, 'sparse', pairs)  11.8 us
  transfers between devices with their start and end apart: 33, of which 17 were waited for; matrix products, arithmetic and copies ran while one was open for 4% of the time, Pallas kernels for 16%

profile of v1, /device:TPU:0, one launch (start us, length us, event | category | flops | bytes accessed | tf_op | source)
XLA Modules:
  0.0 133.6 jit_solution(12534847542479159512)
XLA Ops:
  0.6 1.0 constant_dynamic-slice_fusion
  1.7 0.5 collective-permute-start.9
  2.2 2.6 %collective-permute-start.7 = (bf16[1024,128]{1,0:T(8,128)(2,1)S(1)}, bf16[1024,128]{1,0:T(8,128)(2,1)S(1)}, u32[]{:S(2)}, u32[]{:S(2)}) collective-permute-start(bf16[1024,128]{1,0:T(8,128)(2,1)S(1)} %pad_maximum_fusion.refs_4_), channel_id=1, source_target_pairs={{0,2},{1,3},{2,0},{3,1},{4,6},{5,7},{6,4},{7,5},{8,10},{9,11},{10,... | collective-permute-start | bytes 786440 | tf_op jit(solution)/shard_map/ppermute | solution.py:71
  4.8 2.6 %collective-permute-start.5 = (bf16[1024,128]{1,0:T(8,128)(2,1)S(1)}, bf16[1024,128]{1,0:T(8,128)(2,1)S(1)}, u32[]{:S(2)}, u32[]{:S(2)}) collective-permute-start(bf16[1024,128]{1,0:T(8,128)(2,1)S(1)} %pad_maximum_fusion.refs_4_), channel_id=1, source_target_pairs={{0,4},{1,5},{2,6},{3,7},{4,0},{5,1},{6,2},{7,3},{8,12},{9,13},{10,... | collective-permute-start | bytes 786440 | tf_op jit(solution)/shard_map/ppermute | solution.py:71
  7.4 0.7 broadcast_multiply_fusion.1
  8.1 0.7 broadcast_multiply_fusion
  8.8 0.7 add.113
  9.5 0.7 add.114
  10.2 2.7 %collective-permute-start.2 = (s32[2,512]{1,0:T(2,128)S(1)}, s32[2,512]{1,0:T(2,128)S(1)}, u32[]{:S(2)}, u32[]{:S(2)}) collective-permute-start(s32[2,512]{1,0:T(2,128)S(1)} %pad_add_fusion.refs_0_), channel_id=1, source_target_pairs={{0,24},{8,16},{16,8},{24,0},{1,25},{9,17},{17,9},{25,1},{2,26},{10... | collective-permute-start | bytes 12296 | tf_op jit(solution)/shard_map/ppermute | solution.py:66
  13.1 1.7 %collective-permute-done.2.refs_3_ = s32[2,512]{1,0:T(2,128)S(1)} collective-permute-done((s32[2,512]{1,0:T(2,128)S(1)}, s32[2,512]{1,0:T(2,128)S(1)}, u32[]{:S(2)}, u32[]{:S(2)}) %collective-permute-start.2) | collective-permute-done | bytes 4128 | tf_op jit(solution)/shard_map/ppermute | solution.py:66
  14.7 1.7 %collective-permute-start.1 = (s32[2,512]{1,0:T(2,128)S(1)}, s32[2,512]{1,0:T(2,128)S(1)}, u32[]{:S(2)}, u32[]{:S(2)}) collective-permute-start(s32[2,512]{1,0:T(2,128)S(1)} %pad_add_fusion.refs_0_), channel_id=1, source_target_pairs={{0,16},{8,24},{16,0},{24,8},{1,17},{9,25},{17,1},{25,9},{2,18},{10... | collective-permute-start | bytes 12296 | tf_op jit(solution)/shard_map/ppermute | solution.py:66
  16.5 0.4 collective-permute-done.7.refs_4_
  17.0 1.4 %collective-permute-done.1.refs_2_ = s32[2,512]{1,0:T(2,128)S(1)} collective-permute-done((s32[2,512]{1,0:T(2,128)S(1)}, s32[2,512]{1,0:T(2,128)S(1)}, u32[]{:S(2)}, u32[]{:S(2)}) %collective-permute-start.1) | collective-permute-done | bytes 4128 | tf_op jit(solution)/shard_map/ppermute | solution.py:66
  18.4 1.7 %collective-permute-start = (s32[2,512]{1,0:T(2,128)S(1)}, s32[2,512]{1,0:T(2,128)S(1)}, u32[]{:S(2)}, u32[]{:S(2)}) collective-permute-start(s32[2,512]{1,0:T(2,128)S(1)} %pad_add_fusion.refs_0_), channel_id=1, source_target_pairs={{0,8},{8,0},{16,24},{24,16},{1,9},{9,1},{17,25},{25,17},{2,10},{10... | collective-permute-start | bytes 12296 | tf_op jit(solution)/shard_map/ppermute | solution.py:66
  20.1 6.1 %collective-permute-done.5.refs_4_ = bf16[1024,128]{1,0:T(8,128)(2,1)S(1)} collective-permute-done((bf16[1024,128]{1,0:T(8,128)(2,1)S(1)}, bf16[1024,128]{1,0:T(8,128)(2,1)S(1)}, u32[]{:S(2)}, u32[]{:S(2)}) %collective-permute-start.5) | collective-permute-done | bytes 262176 | tf_op jit(solution)/shard_map/ppermute | solution.py:71
  26.2 0.5 collective-permute-start.4
  27.0 0.2 broadcast_in_dim.10.refs_2_
  27.6 2.9 %fetch.4 = (bf16[512,128]{1,0:T(8,128)(2,1)S(1)}, bf16[512,128]{1,0:T(8,128)(2,1)S(1)}, bf16[512,128]{1,0:T(8,128)(2,1)S(1)}, bf16[512,128]{1,0:T(8,128)(2,1)S(1)}) custom-call(s32[2]{0:T(128)S(1)} %pad_add_fusion.5.base_ref, s32[2,512,128]{2,1,0:T(8,128)S(1)} %broadcast_in_dim.8.refs_0_, s32[2,512,128]{2,1,0:T(8,128)S(1)} %broadcast_in_dim.9.refs_1_, ...), custom_call_target="tpu_custom_call" | custom-call | flops 1073741824 | bytes 3145736 | tf_op jit(solution)/shard_map/fetch/pallas_call | solution.py:35
  30.4 2.9 %fetch.5 = (bf16[512,128]{1,0:T(8,128)(2,1)S(1)}, bf16[512,128]{1,0:T(8,128)(2,1)S(1)}, bf16[512,128]{1,0:T(8,128)(2,1)S(1)}, bf16[512,128]{1,0:T(8,128)(2,1)S(1)}) custom-call(s32[2]{0:T(128)S(1)} %pad_add_fusion.4.base_ref, s32[2,512,128]{2,1,0:T(8,128)S(1)} %broadcast_in_dim.8.refs_0_, s32[2,512,128]{2,1,0:T(8,128)S(1)} %broadcast_in_dim.9.refs_1_, ...), custom_call_target="tpu_custom_call" | custom-call | flops 1073741824 | bytes 3670024 | tf_op jit(solution)/shard_map/fetch/pallas_call | solution.py:35
  33.3 2.9 %fetch.6 = (bf16[512,128]{1,0:T(8,128)(2,1)S(1)}, bf16[512,128]{1,0:T(8,128)(2,1)S(1)}, bf16[512,128]{1,0:T(8,128)(2,1)S(1)}, bf16[512,128]{1,0:T(8,128)(2,1)S(1)}) custom-call(s32[2]{0:T(128)S(1)} %pad_add_fusion.3.base_ref, s32[2,512,128]{2,1,0:T(8,128)S(1)} %broadcast_in_dim.8.refs_0_, s32[2,512,128]{2,1,0:T(8,128)S(1)} %broadcast_in_dim.9.refs_1_, ...), custom_call_target="tpu_custom_call" | custom-call | flops 1073741824 | bytes 3670024 | tf_op jit(solution)/shard_map/fetch/pallas_call | solution.py:35
  36.3 2.9 %fetch.7 = (bf16[512,128]{1,0:T(8,128)(2,1)S(1)}, bf16[512,128]{1,0:T(8,128)(2,1)S(1)}, bf16[512,128]{1,0:T(8,128)(2,1)S(1)}, bf16[512,128]{1,0:T(8,128)(2,1)S(1)}) custom-call(s32[2]{0:T(128)S(1)} %pad_add_fusion.2.base_ref, s32[2,512,128]{2,1,0:T(8,128)S(1)} %broadcast_in_dim.8.refs_0_, s32[2,512,128]{2,1,0:T(8,128)S(1)} %broadcast_in_dim.9.refs_1_, ...), custom_call_target="tpu_custom_call" | custom-call | flops 1073741824 | bytes 3670024 | tf_op jit(solution)/shard_map/fetch/pallas_call | solution.py:35
  39.1 1.6 %collective-permute-start.10 = (bf16[512,128]{1,0:T(8,128)(2,1)S(1)}, bf16[512,128]{1,0:T(8,128)(2,1)S(1)}, u32[]{:S(2)}, u32[]{:S(2)}) collective-permute-start(bf16[512,128]{1,0:T(8,128)(2,1)S(1)} %get-tuple-element.62), channel_id=1, source_target_pairs={{0,8},{8,0},{16,24},{24,16},{1,9},{9,1},{17,25},{25,17},{2,10},{10... | collective-permute-start | bytes 393224 | tf_op jit(solution)/shard_map/ppermute | solution.py:66
  40.7 1.5 %collective-permute-start.11 = (bf16[512,128]{1,0:T(8,128)(2,1)S(1)}, bf16[512,128]{1,0:T(8,128)(2,1)S(1)}, u32[]{:S(2)}, u32[]{:S(2)}) collective-permute-start(bf16[512,128]{1,0:T(8,128)(2,1)S(1)} %get-tuple-element.63), channel_id=1, source_target_pairs={{0,16},{8,24},{16,0},{24,8},{1,17},{9,25},{17,1},{25,9},{2,18},{10... | collective-permute-start | bytes 393224 | tf_op jit(solution)/shard_map/ppermute | solution.py:66
  42.2 0.5 collective-permute-start.12
  42.8 2.2 %collective-permute-done.10.refs_1_ = bf16[512,128]{1,0:T(8,128)(2,1)S(1)} collective-permute-done((bf16[512,128]{1,0:T(8,128)(2,1)S(1)}, bf16[512,128]{1,0:T(8,128)(2,1)S(1)}, u32[]{:S(2)}, u32[]{:S(2)}) %collective-permute-start.10) | collective-permute-done | bytes 131104 | tf_op jit(solution)/shard_map/ppermute | solution.py:66
  45.0 3.7 %collective-permute-done.11.refs_2_ = bf16[512,128]{1,0:T(8,128)(2,1)S(1)} collective-permute-done((bf16[512,128]{1,0:T(8,128)(2,1)S(1)}, bf16[512,128]{1,0:T(8,128)(2,1)S(1)}, u32[]{:S(2)}, u32[]{:S(2)}) %collective-permute-start.11) | collective-permute-done | bytes 131104 | tf_op jit(solution)/shard_map/ppermute | solution.py:66
  48.7 12.8 %sequence.1 = (bf16[512,512]{1,0:T(8,128)(2,1)}, bf16[512,128]{1,0:T(8,128)(2,1)S(1)}, bf16[512,128]{1,0:T(8,128)(2,1)S(1)}, bf16[512,128]{1,0:T(8,128)(2,1)S(1)...) custom-call(s32[4]{0:T(128)S(1)} %pad_add_fusion.1.block_ref, ...), custom_call_target="tpu_custom_call" | custom-call | flops 3758096384 | bytes 7866384 | tf_op jit(solution)/shard_map/sequence/pallas_call | solution.py:35
  61.5 1.3 copy-done.3
  62.8 3.9 %weight_grad.1 = (bf16[256,2560]{1,0:T(8,128)(2,1)S(1)}, bf16[256,2560]{1,0:T(8,128)(2,1)S(1)}) custom-call(s32[1]{0:T(128)} %bitcast.21.core_ref, bf16[512,512]{1,0:T(8,128)(2,1)S(1)} %get-tuple-element.78.n_ref, bf16[512,2048]{1,0:T(8,128)(2,1)} %copy-done.3, bf16[512,512]{1,0:T(8,128)(2,1)S(1)} %get-tuple-element.80.g_ref, bf16[512,512]{1,0:T(8,128)(2,1)S(1)} %copy-done.1), custom_call_target="tpu_custom_call" | custom-call | flops 1879048192 | bytes 6291460 | tf_op jit(solution)/shard_map/weight_grad/pallas_call | solution.py:35
  66.8 1.3 collective-permute-start.13
  68.1 0.8 collective-permute-start.14
  68.9 1.4 %collective-permute-start.15 = (bf16[512,128]{1,0:T(8,128)(2,1)S(1)}, bf16[512,128]{1,0:T(8,128)(2,1)S(1)}, u32[]{:S(2)}, u32[]{:S(2)}) collective-permute-start(bf16[512,128]{1,0:T(8,128)(2,1)S(1)} %get-tuple-element.69), channel_id=1, source_target_pairs={{0,24},{8,16},{16,8},{24,0},{1,25},{9,17},{17,9},{25,1},{2,26},{10... | collective-permute-start | bytes 393224 | tf_op jit(solution)/shard_map/ppermute | solution.py:66
  70.4 2.8 %collective-permute-done.13.refs_5_ = bf16[512,128]{1,0:T(8,128)(2,1)S(1)} collective-permute-done((bf16[512,128]{1,0:T(8,128)(2,1)S(1)}, bf16[512,128]{1,0:T(8,128)(2,1)S(1)}, u32[]{:S(2)}, u32[]{:S(2)}) %collective-permute-start.13) | collective-permute-done | bytes 131104 | tf_op jit(solution)/shard_map/ppermute | solution.py:66
  73.2 1.7 %collective-permute-done.14.refs_6_ = bf16[512,128]{1,0:T(8,128)(2,1)S(1)} collective-permute-done((bf16[512,128]{1,0:T(8,128)(2,1)S(1)}, bf16[512,128]{1,0:T(8,128)(2,1)S(1)}, u32[]{:S(2)}, u32[]{:S(2)}) %collective-permute-start.14) | collective-permute-done | bytes 131104 | tf_op jit(solution)/shard_map/ppermute | solution.py:66
  74.8 1.6 %collective-permute-done.15.refs_7_ = bf16[512,128]{1,0:T(8,128)(2,1)S(1)} collective-permute-done((bf16[512,128]{1,0:T(8,128)(2,1)S(1)}, bf16[512,128]{1,0:T(8,128)(2,1)S(1)}, u32[]{:S(2)}, u32[]{:S(2)}) %collective-permute-start.15) | collective-permute-done | bytes 131104 | tf_op jit(solution)/shard_map/ppermute | solution.py:66
  76.5 2.9 %gather_grad.7 = (bf16[1024,128]{1,0:T(8,128)(2,1)S(1)}, bf16[1024,128]{1,0:T(8,128)(2,1)S(1)}) custom-call(s32[2]{0:T(128)S(1)} %pad_add_fusion.2.base_ref, s32[2,512]{1,0:T(2,128)S(1)} %pad_add_fusion.refs_0_, s32[2,512]{1,0:T(2,128)S(1)} %collective-permute-done.refs_1_, s32[2,512]{1,0:T(2,128)S(1)} %collective-permute-done.1.refs_2_, ...), custom_call_target="tpu_custom_call" | custom-call | flops 1073741824 | bytes 1064968 | tf_op jit(solution)/shard_map/gather_grad/pallas_call | solution.py:35
  79.4 2.9 %gather_grad.6 = (bf16[1024,128]{1,0:T(8,128)(2,1)S(1)}, bf16[1024,128]{1,0:T(8,128)(2,1)S(1)}) custom-call(s32[2]{0:T(128)S(1)} %pad_add_fusion.3.base_ref, s32[2,512]{1,0:T(2,128)S(1)} %pad_add_fusion.refs_0_, s32[2,512]{1,0:T(2,128)S(1)} %collective-permute-done.refs_1_, s32[2,512]{1,0:T(2,128)S(1)} %collective-permute-done.1.refs_2_, ...), custom_call_target="tpu_custom_call" | custom-call | flops 1073741824 | bytes 1064968 | tf_op jit(solution)/shard_map/gather_grad/pallas_call | solution.py:35
  82.3 0.8 collective-permute-start.19
  83.1 2.9 %gather_grad.5 = (bf16[1024,128]{1,0:T(8,128)(2,1)S(1)}, bf16[1024,128]{1,0:T(8,128)(2,1)S(1)}) custom-call(s32[2]{0:T(128)S(1)} %pad_add_fusion.4.base_ref, s32[2,512]{1,0:T(2,128)S(1)} %pad_add_fusion.refs_0_, s32[2,512]{1,0:T(2,128)S(1)} %collective-permute-done.refs_1_, s32[2,512]{1,0:T(2,128)S(1)} %collective-permute-done.1.refs_2_, ...), custom_call_target="tpu_custom_call" | custom-call | flops 1073741824 | bytes 1064968 | tf_op jit(solution)/shard_map/gather_grad/pallas_call | solution.py:35
  86.0 2.9 %gather_grad.4 = (bf16[1024,128]{1,0:T(8,128)(2,1)S(1)}, bf16[1024,128]{1,0:T(8,128)(2,1)S(1)}) custom-call(s32[2]{0:T(128)S(1)} %pad_add_fusion.5.base_ref, s32[2,512]{1,0:T(2,128)S(1)} %pad_add_fusion.refs_0_, s32[2,512]{1,0:T(2,128)S(1)} %collective-permute-done.refs_1_, s32[2,512]{1,0:T(2,128)S(1)} %collective-permute-done.1.refs_2_, ...), custom_call_target="tpu_custom_call" | custom-call | flops 1073741824 | bytes 1064968 | tf_op jit(solution)/shard_map/gather_grad/pallas_call | solution.py:35
  88.9 0.6 collective-permute-start.16
  89.5 2.5 %collective-permute-start.22 = (bf16[1024,128]{1,0:T(8,128)(2,1)S(1)}, bf16[1024,128]{1,0:T(8,128)(2,1)S(1)}, u32[]{:S(2)}, u32[]{:S(2)}) collective-permute-start(bf16[1024,128]{1,0:T(8,128)(2,1)S(1)} %add_convert_fusion), channel_id=1, source_target_pairs={{0,6},{1,7},{2,4},{3,5},{4,2},{5,3},{6,0},{7,1},{8,14},{9,15},{10,... | collective-permute-start | bytes 786440 | tf_op jit(solution)/shard_map/ppermute | solution.py:71
  92.1 1.1 add_and_split.2
  93.2 0.9 collective-permute-start.24
  94.0 1.5 %collective-permute-start.25 = (bf16[256,640]{1,0:T(8,128)(2,1)S(1)}, bf16[256,640]{1,0:T(8,128)(2,1)S(1)}, u32[]{:S(2)}, u32[]{:S(2)}) collective-permute-start(bf16[256,640]{1,0:T(8,128)(2,1)S(1)} %get-tuple-element.85), channel_id=1, source_target_pairs={{0,16},{8,24},{16,0},{24,8},{1,17},{9,25},{17,1},{25,9},{2,18},{10... | collective-permute-start | bytes 983048 | tf_op jit(solution)/shard_map/ppermute | solution.py:66
  95.6 1.2 collective-permute-start.26
  97.0 6.9 %collective-permute-done.24.refs_1_ = bf16[256,640]{1,0:T(8,128)(2,1)S(1)} collective-permute-done((bf16[256,640]{1,0:T(8,128)(2,1)S(1)}, bf16[256,640]{1,0:T(8,128)(2,1)S(1)}, u32[]{:S(2)}, u32[]{:S(2)}) %collective-permute-start.24) | collective-permute-done | bytes 327712 | tf_op jit(solution)/shard_map/ppermute | solution.py:66
  103.8 4.3 %collective-permute-start.20 = (bf16[1024,128]{1,0:T(8,128)(2,1)S(1)}, bf16[1024,128]{1,0:T(8,128)(2,1)S(1)}, u32[]{:S(2)}, u32[]{:S(2)}) collective-permute-start(bf16[1024,128]{1,0:T(8,128)(2,1)S(1)} %add_convert_fusion.1), channel_id=1, source_target_pairs={{0,4},{1,5},{2,6},{3,7},{4,0},{5,1},{6,2},{7,3},{8,12},{9,13},{10,... | collective-permute-start | bytes 786440 | tf_op jit(solution)/shard_map/ppermute | solution.py:71
  108.1 2.0 %collective-permute-done.25.refs_2_ = bf16[256,640]{1,0:T(8,128)(2,1)S(1)} collective-permute-done((bf16[256,640]{1,0:T(8,128)(2,1)S(1)}, bf16[256,640]{1,0:T(8,128)(2,1)S(1)}, u32[]{:S(2)}, u32[]{:S(2)}) %collective-permute-start.25) | collective-permute-done | bytes 327712 | tf_op jit(solution)/shard_map/ppermute | solution.py:66
  110.1 4.4 %collective-permute-start.18 = (bf16[1024,128]{1,0:T(8,128)(2,1)S(1)}, bf16[1024,128]{1,0:T(8,128)(2,1)S(1)}, u32[]{:S(2)}, u32[]{:S(2)}) collective-permute-start(bf16[1024,128]{1,0:T(8,128)(2,1)S(1)} %add_convert_fusion.2), channel_id=1, source_target_pairs={{0,2},{1,3},{2,0},{3,1},{4,6},{5,7},{6,4},{7,5},{8,10},{9,11},{10,... | collective-permute-start | bytes 786440 | tf_op jit(solution)/shard_map/ppermute | solution.py:71
  114.6 0.8 add_and_split.3
  115.5 1.9 %collective-permute-start.28 = (bf16[64,640]{1,0:T(8,128)(2,1)S(1)}, bf16[64,640]{1,0:T(8,128)(2,1)S(1)}, u32[]{:S(2)}, u32[]{:S(2)}) collective-permute-start(bf16[64,640]{1,0:T(8,128)(2,1)S(1)} %get-tuple-element.89), channel_id=1, source_target_pairs={{0,4},{1,5},{2,6},{3,7},{4,0},{5,1},{6,2},{7,3},{8,12},{9,13},{10,... | collective-permute-start | bytes 245768 | tf_op jit(solution)/shard_map/ppermute | solution.py:71
  117.4 2.5 %collective-permute-start.29 = (bf16[64,640]{1,0:T(8,128)(2,1)S(1)}, bf16[64,640]{1,0:T(8,128)(2,1)S(1)}, u32[]{:S(2)}, u32[]{:S(2)}) collective-permute-start(bf16[64,640]{1,0:T(8,128)(2,1)S(1)} %get-tuple-element.90), channel_id=1, source_target_pairs={{0,6},{1,7},{2,4},{3,5},{4,2},{5,3},{6,0},{7,1},{8,14},{9,15},{10,... | collective-permute-start | bytes 245768 | tf_op jit(solution)/shard_map/ppermute | solution.py:71
  119.9 2.8 %collective-permute-done.18 = bf16[1024,128]{1,0:T(8,128)(2,1)S(1)} collective-permute-done((bf16[1024,128]{1,0:T(8,128)(2,1)S(1)}, bf16[1024,128]{1,0:T(8,128)(2,1)S(1)}, u32[]{:S(2)}, u32[]{:S(2)}) %collective-permute-start.18) | collective-permute-done | bytes 262176 | tf_op jit(solution)/shard_map/ppermute | solution.py:71
  122.9 0.7 collective-permute-done.27
  123.6 1.8 %collective-permute-done.29 = bf16[64,640]{1,0:T(8,128)(2,1)S(1)} collective-permute-done((bf16[64,640]{1,0:T(8,128)(2,1)S(1)}, bf16[64,640]{1,0:T(8,128)(2,1)S(1)}, u32[]{:S(2)}, u32[]{:S(2)}) %collective-permute-start.29) | collective-permute-done | bytes 81952 | tf_op jit(solution)/shard_map/ppermute | solution.py:71
  125.4 1.8 %collective-permute-start.32 = (bf16[64,640]{1,0:T(8,128)(2,1)S(1)}, bf16[64,640]{1,0:T(8,128)(2,1)S(1)}, u32[]{:S(2)}, u32[]{:S(2)}) collective-permute-start(bf16[64,640]{1,0:T(8,128)(2,1)S(1)} %add_convert_fusion.3.refs_0_), channel_id=1, source_target_pairs={{0,24},{8,16},{16,8},{24,0},{1,25},{9,17},{17,9},{25,1},{2,26},{10... | collective-permute-start | bytes 245768 | tf_op jit(solution)/shard_map/ppermute | solution.py:66
  127.2 0.5 collective-permute-start.31
  127.7 1.2 collective-permute-start.30
  128.9 0.8 fusion
  129.8 1.0 collective-permute-done.32.refs_3_
  130.8 0.9 collective-permute-done.31.refs_2_
  131.7 0.5 collective-permute-done.30.refs_1_
  132.1 1.5 %assemble.1 = (f32[64,2048]{1,0:T(8,128)}, f32[64,512]{1,0:T(8,128)}) custom-call(s32[4]{0:T(128)S(1)} %pad_add_fusion.1.block_ref, bf16[64,640]{1,0:T(8,128)(2,1)S(1)} %add_convert_fusion.3.refs_0_, bf16[64,640]{1,0:T(8,128)(2,1)S(1)} %collective-permute-done.30.refs_1_, bf16[64,640]{1,0:T(8,128)(2,1)S(1)} %collective-permute-done.31.refs_2_, ...), custom_call_target="tpu_custom_call" | custom-call | bytes 983056 | tf_op jit(solution)/shard_map/assemble/pallas_call | solution.py:35
  (46 shorter events, 1.8 us)
Async XLA Ops:
  1.7 25.1 %collective-permute-start.9 = (bf16[1024,128]{1,0:T(8,128)(2,1)S(1)}, bf16[1024,128]{1,0:T(8,128)(2,1)S(1)}, u32[]{:S(2)}, u32[]{:S(2)}) collective-permute-start(bf16[1024,128]{1,0:T(8,128)(2,1)S(1)} %pad_maximum_fusion.refs_4_), channel_id=1, source_target_pairs={{0,1},{1,0},{2,3},{3,2},{4,5},{5,4},{6,7},{7,6},{8,9},{9,8},{10,11... | collective-permute-start | bytes 786440 | tf_op jit(solution)/shard_map/ppermute | solution.py:74
  2.2 14.7 %collective-permute-start.7 = (bf16[1024,128]{1,0:T(8,128)(2,1)S(1)}, bf16[1024,128]{1,0:T(8,128)(2,1)S(1)}, u32[]{:S(2)}, u32[]{:S(2)}) collective-permute-start(bf16[1024,128]{1,0:T(8,128)(2,1)S(1)} %pad_maximum_fusion.refs_4_), channel_id=1, source_target_pairs={{0,2},{1,3},{2,0},{3,1},{4,6},{5,7},{6,4},{7,5},{8,10},{9,11},{10,... | collective-permute-start | bytes 786440 | tf_op jit(solution)/shard_map/ppermute | solution.py:71
  4.8 21.3 %collective-permute-start.5 = (bf16[1024,128]{1,0:T(8,128)(2,1)S(1)}, bf16[1024,128]{1,0:T(8,128)(2,1)S(1)}, u32[]{:S(2)}, u32[]{:S(2)}) collective-permute-start(bf16[1024,128]{1,0:T(8,128)(2,1)S(1)} %pad_maximum_fusion.refs_4_), channel_id=1, source_target_pairs={{0,4},{1,5},{2,6},{3,7},{4,0},{5,1},{6,2},{7,3},{8,12},{9,13},{10,... | collective-permute-start | bytes 786440 | tf_op jit(solution)/shard_map/ppermute | solution.py:71
  7.4 18.8 %collective-permute-start.3 = (bf16[1024,128]{1,0:T(8,128)(2,1)S(1)}, bf16[1024,128]{1,0:T(8,128)(2,1)S(1)}, u32[]{:S(2)}, u32[]{:S(2)}) collective-permute-start(bf16[1024,128]{1,0:T(8,128)(2,1)S(1)} %pad_maximum_fusion.refs_4_), channel_id=1, source_target_pairs={{0,6},{1,7},{2,4},{3,5},{4,2},{5,3},{6,0},{7,1},{8,14},{9,15},{10,... | collective-permute-start | bytes 786440 | tf_op jit(solution)/shard_map/ppermute | solution.py:71
  10.2 4.6 %collective-permute-start.2 = (s32[2,512]{1,0:T(2,128)S(1)}, s32[2,512]{1,0:T(2,128)S(1)}, u32[]{:S(2)}, u32[]{:S(2)}) collective-permute-start(s32[2,512]{1,0:T(2,128)S(1)} %pad_add_fusion.refs_0_), channel_id=1, source_target_pairs={{0,24},{8,16},{16,8},{24,0},{1,25},{9,17},{17,9},{25,1},{2,26},{10... | collective-permute-start | bytes 12296 | tf_op jit(solution)/shard_map/ppermute | solution.py:66
  14.7 3.6 %collective-permute-start.1 = (s32[2,512]{1,0:T(2,128)S(1)}, s32[2,512]{1,0:T(2,128)S(1)}, u32[]{:S(2)}, u32[]{:S(2)}) collective-permute-start(s32[2,512]{1,0:T(2,128)S(1)} %pad_add_fusion.refs_0_), channel_id=1, source_target_pairs={{0,16},{8,24},{16,0},{24,8},{1,17},{9,25},{17,1},{25,9},{2,18},{10... | collective-permute-start | bytes 12296 | tf_op jit(solution)/shard_map/ppermute | solution.py:66
  16.9 13.5 %collective-permute-start.8 = (bf16[1024,128]{1,0:T(8,128)(2,1)S(1)}, bf16[1024,128]{1,0:T(8,128)(2,1)S(1)}, u32[]{:S(2)}, u32[]{:S(2)}) collective-permute-start(bf16[1024,128]{1,0:T(8,128)(2,1)S(1)} %collective-permute-done.7.refs_4_), channel_id=1, source_target_pairs={{0,1},{1,0},{2,3},{3,2},{4,5},{5,4},{6,7},{7,6},{8,9},{9,8},{10,11... | collective-permute-start | bytes 786440 | tf_op jit(solution)/shard_map/ppermute | solution.py:74
  18.4 8.4 %collective-permute-start = (s32[2,512]{1,0:T(2,128)S(1)}, s32[2,512]{1,0:T(2,128)S(1)}, u32[]{:S(2)}, u32[]{:S(2)}) collective-permute-start(s32[2,512]{1,0:T(2,128)S(1)} %pad_add_fusion.refs_0_), channel_id=1, source_target_pairs={{0,8},{8,0},{16,24},{24,16},{1,9},{9,1},{17,25},{25,17},{2,10},{10... | collective-permute-start | bytes 12296 | tf_op jit(solution)/shard_map/ppermute | solution.py:66
  26.2 7.2 %collective-permute-start.6 = (bf16[1024,128]{1,0:T(8,128)(2,1)S(1)}, bf16[1024,128]{1,0:T(8,128)(2,1)S(1)}, u32[]{:S(2)}, u32[]{:S(2)}) collective-permute-start(bf16[1024,128]{1,0:T(8,128)(2,1)S(1)} %collective-permute-done.5.refs_4_), channel_id=1, source_target_pairs={{0,1},{1,0},{2,3},{3,2},{4,5},{5,4},{6,7},{7,6},{8,9},{9,8},{10,11... | collective-permute-start | bytes 786440 | tf_op jit(solution)/shard_map/ppermute | solution.py:74
  26.2 10.0 %collective-permute-start.4 = (bf16[1024,128]{1,0:T(8,128)(2,1)S(1)}, bf16[1024,128]{1,0:T(8,128)(2,1)S(1)}, u32[]{:S(2)}, u32[]{:S(2)}) collective-permute-start(bf16[1024,128]{1,0:T(8,128)(2,1)S(1)} %collective-permute-done.3.refs_4_), channel_id=1, source_target_pairs={{0,1},{1,0},{2,3},{3,2},{4,5},{5,4},{6,7},{7,6},{8,9},{9,8},{10,11... | collective-permute-start | bytes 786440 | tf_op jit(solution)/shard_map/ppermute | solution.py:74
  36.2 12.4 %copy-start = (bf16[512,512]{1,0:T(8,128)(2,1)S(1)}, bf16[512,512]{1,0:T(8,128)(2,1)}, u32[]{:S(2)}) copy-start(bf16[512,512]{1,0:T(8,128)(2,1)} %refs_7_.1) | copy-start | bytes 1572868
  36.2 12.4 %copy-start.1 = (bf16[512,512]{1,0:T(8,128)(2,1)S(1)}, bf16[512,512]{1,0:T(8,128)(2,1)}, u32[]{:S(2)}) copy-start(bf16[512,512]{1,0:T(8,128)(2,1)} %c_ref.1) | copy-start | bytes 1572868
  36.3 12.4 %copy-start.2 = (f32[512]{0:T(512)S(1)}, f32[512]{0:T(512)}, u32[]{:S(2)}) copy-start(f32[512]{0:T(512)} %param.16) | copy-start | bytes 6148
  39.1 5.8 %collective-permute-start.10 = (bf16[512,128]{1,0:T(8,128)(2,1)S(1)}, bf16[512,128]{1,0:T(8,128)(2,1)S(1)}, u32[]{:S(2)}, u32[]{:S(2)}) collective-permute-start(bf16[512,128]{1,0:T(8,128)(2,1)S(1)} %get-tuple-element.62), channel_id=1, source_target_pairs={{0,8},{8,0},{16,24},{24,16},{1,9},{9,1},{17,25},{25,17},{2,10},{10... | collective-permute-start | bytes 393224 | tf_op jit(solution)/shard_map/ppermute | solution.py:66
  40.7 8.0 %collective-permute-start.11 = (bf16[512,128]{1,0:T(8,128)(2,1)S(1)}, bf16[512,128]{1,0:T(8,128)(2,1)S(1)}, u32[]{:S(2)}, u32[]{:S(2)}) collective-permute-start(bf16[512,128]{1,0:T(8,128)(2,1)S(1)} %get-tuple-element.63), channel_id=1, source_target_pairs={{0,16},{8,24},{16,0},{24,8},{1,17},{9,25},{17,1},{25,9},{2,18},{10... | collective-permute-start | bytes 393224 | tf_op jit(solution)/shard_map/ppermute | solution.py:66
  42.2 6.4 %collective-permute-start.12 = (bf16[512,128]{1,0:T(8,128)(2,1)S(1)}, bf16[512,128]{1,0:T(8,128)(2,1)S(1)}, u32[]{:S(2)}, u32[]{:S(2)}) collective-permute-start(bf16[512,128]{1,0:T(8,128)(2,1)S(1)} %get-tuple-element.64), channel_id=1, source_target_pairs={{0,24},{8,16},{16,8},{24,0},{1,25},{9,17},{17,9},{25,1},{2,26},{10... | collective-permute-start | bytes 393224 | tf_op jit(solution)/shard_map/ppermute | solution.py:66
  61.5 1.3 %copy-start.3 = (bf16[512,2048]{1,0:T(8,128)(2,1)}, bf16[512,2048]{1,0:T(8,128)(2,1)S(1)}, u32[]{:S(2)}) copy-start(bf16[512,2048]{1,0:T(8,128)(2,1)S(1)} %get-tuple-element.79.d_ref) | copy-start | bytes 6291460
  66.7 25.3 %collective-permute-start.23 = (bf16[256,2560]{1,0:T(8,128)(2,1)S(1)}, bf16[256,2560]{1,0:T(8,128)(2,1)S(1)}, u32[]{:S(2)}, u32[]{:S(2)}) collective-permute-start(bf16[256,2560]{1,0:T(8,128)(2,1)S(1)} %get-tuple-element.82), channel_id=1, source_target_pairs={{0,1},{1,0},{2,3},{3,2},{4,5},{5,4},{6,7},{7,6},{8,9},{9,8},{10,11... | collective-permute-start | bytes 3932168 | tf_op jit(solution)/shard_map/ppermute | solution.py:74
  66.8 6.4 %collective-permute-start.13 = (bf16[512,128]{1,0:T(8,128)(2,1)S(1)}, bf16[512,128]{1,0:T(8,128)(2,1)S(1)}, u32[]{:S(2)}, u32[]{:S(2)}) collective-permute-start(bf16[512,128]{1,0:T(8,128)(2,1)S(1)} %get-tuple-element.67), channel_id=1, source_target_pairs={{0,8},{8,0},{16,24},{24,16},{1,9},{9,1},{17,25},{25,17},{2,10},{10... | collective-permute-start | bytes 393224 | tf_op jit(solution)/shard_map/ppermute | solution.py:66
  68.1 6.7 %collective-permute-start.14 = (bf16[512,128]{1,0:T(8,128)(2,1)S(1)}, bf16[512,128]{1,0:T(8,128)(2,1)S(1)}, u32[]{:S(2)}, u32[]{:S(2)}) collective-permute-start(bf16[512,128]{1,0:T(8,128)(2,1)S(1)} %get-tuple-element.68), channel_id=1, source_target_pairs={{0,16},{8,24},{16,0},{24,8},{1,17},{9,25},{17,1},{25,9},{2,18},{10... | collective-permute-start | bytes 393224 | tf_op jit(solution)/shard_map/ppermute | solution.py:66
  68.9 7.6 %collective-permute-start.15 = (bf16[512,128]{1,0:T(8,128)(2,1)S(1)}, bf16[512,128]{1,0:T(8,128)(2,1)S(1)}, u32[]{:S(2)}, u32[]{:S(2)}) collective-permute-start(bf16[512,128]{1,0:T(8,128)(2,1)S(1)} %get-tuple-element.69), channel_id=1, source_target_pairs={{0,24},{8,16},{16,8},{24,0},{1,25},{9,17},{17,9},{25,1},{2,26},{10... | collective-permute-start | bytes 393224 | tf_op jit(solution)/shard_map/ppermute | solution.py:66
  79.3 10.1 %collective-permute-start.21 = (bf16[1024,128]{1,0:T(8,128)(2,1)S(1)}, bf16[1024,128]{1,0:T(8,128)(2,1)S(1)}, u32[]{:S(2)}, u32[]{:S(2)}) collective-permute-start(bf16[1024,128]{1,0:T(8,128)(2,1)S(1)} %get-tuple-element.77), channel_id=1, source_target_pairs={{0,1},{1,0},{2,3},{3,2},{4,5},{5,4},{6,7},{7,6},{8,9},{9,8},{10,11... | collective-permute-start | bytes 786440 | tf_op jit(solution)/shard_map/ppermute | solution.py:74
  82.3 11.8 %collective-permute-start.19 = (bf16[1024,128]{1,0:T(8,128)(2,1)S(1)}, bf16[1024,128]{1,0:T(8,128)(2,1)S(1)}, u32[]{:S(2)}, u32[]{:S(2)}) collective-permute-start(bf16[1024,128]{1,0:T(8,128)(2,1)S(1)} %get-tuple-element.75), channel_id=1, source_target_pairs={{0,1},{1,0},{2,3},{3,2},{4,5},{5,4},{6,7},{7,6},{8,9},{9,8},{10,11... | collective-permute-start | bytes 786440 | tf_op jit(solution)/shard_map/ppermute | solution.py:74
  85.9 9.7 %collective-permute-start.17 = (bf16[1024,128]{1,0:T(8,128)(2,1)S(1)}, bf16[1024,128]{1,0:T(8,128)(2,1)S(1)}, u32[]{:S(2)}, u32[]{:S(2)}) collective-permute-start(bf16[1024,128]{1,0:T(8,128)(2,1)S(1)} %get-tuple-element.73), channel_id=1, source_target_pairs={{0,1},{1,0},{2,3},{3,2},{4,5},{5,4},{6,7},{7,6},{8,9},{9,8},{10,11... | collective-permute-start | bytes 786440 | tf_op jit(solution)/shard_map/ppermute | solution.py:74
  88.9 26.6 %collective-permute-start.16 = (bf16[1024,128]{1,0:T(8,128)(2,1)S(1)}, bf16[1024,128]{1,0:T(8,128)(2,1)S(1)}, u32[]{:S(2)}, u32[]{:S(2)}) collective-permute-start(bf16[1024,128]{1,0:T(8,128)(2,1)S(1)} %get-tuple-element.71), channel_id=1, source_target_pairs={{0,1},{1,0},{2,3},{3,2},{4,5},{5,4},{6,7},{7,6},{8,9},{9,8},{10,11... | collective-permute-start | bytes 786440 | tf_op jit(solution)/shard_map/ppermute | solution.py:74
  89.5 27.9 %collective-permute-start.22 = (bf16[1024,128]{1,0:T(8,128)(2,1)S(1)}, bf16[1024,128]{1,0:T(8,128)(2,1)S(1)}, u32[]{:S(2)}, u32[]{:S(2)}) collective-permute-start(bf16[1024,128]{1,0:T(8,128)(2,1)S(1)} %add_convert_fusion), channel_id=1, source_target_pairs={{0,6},{1,7},{2,4},{3,5},{4,2},{5,3},{6,0},{7,1},{8,14},{9,15},{10,... | collective-permute-start | bytes 786440 | tf_op jit(solution)/shard_map/ppermute | solution.py:71
  93.2 10.7 %collective-permute-start.24 = (bf16[256,640]{1,0:T(8,128)(2,1)S(1)}, bf16[256,640]{1,0:T(8,128)(2,1)S(1)}, u32[]{:S(2)}, u32[]{:S(2)}) collective-permute-start(bf16[256,640]{1,0:T(8,128)(2,1)S(1)} %get-tuple-element.84), channel_id=1, source_target_pairs={{0,8},{8,0},{16,24},{24,16},{1,9},{9,1},{17,25},{25,17},{2,10},{10... | collective-permute-start | bytes 983048 | tf_op jit(solution)/shard_map/ppermute | solution.py:66
  94.0 16.1 %collective-permute-start.25 = (bf16[256,640]{1,0:T(8,128)(2,1)S(1)}, bf16[256,640]{1,0:T(8,128)(2,1)S(1)}, u32[]{:S(2)}, u32[]{:S(2)}) collective-permute-start(bf16[256,640]{1,0:T(8,128)(2,1)S(1)} %get-tuple-element.85), channel_id=1, source_target_pairs={{0,16},{8,24},{16,0},{24,8},{1,17},{9,25},{17,1},{25,9},{2,18},{10... | collective-permute-start | bytes 983048 | tf_op jit(solution)/shard_map/ppermute | solution.py:66
  95.6 19.0 %collective-permute-start.26 = (bf16[256,640]{1,0:T(8,128)(2,1)S(1)}, bf16[256,640]{1,0:T(8,128)(2,1)S(1)}, u32[]{:S(2)}, u32[]{:S(2)}) collective-permute-start(bf16[256,640]{1,0:T(8,128)(2,1)S(1)} %get-tuple-element.86), channel_id=1, source_target_pairs={{0,24},{8,16},{16,8},{24,0},{1,25},{9,17},{17,9},{25,1},{2,26},{10... | collective-permute-start | bytes 983048 | tf_op jit(solution)/shard_map/ppermute | solution.py:66
  103.8 16.1 %collective-permute-start.20 = (bf16[1024,128]{1,0:T(8,128)(2,1)S(1)}, bf16[1024,128]{1,0:T(8,128)(2,1)S(1)}, u32[]{:S(2)}, u32[]{:S(2)}) collective-permute-start(bf16[1024,128]{1,0:T(8,128)(2,1)S(1)} %add_convert_fusion.1), channel_id=1, source_target_pairs={{0,4},{1,5},{2,6},{3,7},{4,0},{5,1},{6,2},{7,3},{8,12},{9,13},{10,... | collective-permute-start | bytes 786440 | tf_op jit(solution)/shard_map/ppermute | solution.py:71
  110.1 12.6 %collective-permute-start.18 = (bf16[1024,128]{1,0:T(8,128)(2,1)S(1)}, bf16[1024,128]{1,0:T(8,128)(2,1)S(1)}, u32[]{:S(2)}, u32[]{:S(2)}) collective-permute-start(bf16[1024,128]{1,0:T(8,128)(2,1)S(1)} %add_convert_fusion.2), channel_id=1, source_target_pairs={{0,2},{1,3},{2,0},{3,1},{4,6},{5,7},{6,4},{7,5},{8,10},{9,11},{10,... | collective-permute-start | bytes 786440 | tf_op jit(solution)/shard_map/ppermute | solution.py:71
  115.4 8.1 %collective-permute-start.27 = (bf16[64,640]{1,0:T(8,128)(2,1)S(1)}, bf16[64,640]{1,0:T(8,128)(2,1)S(1)}, u32[]{:S(2)}, u32[]{:S(2)}) collective-permute-start(bf16[64,640]{1,0:T(8,128)(2,1)S(1)} %get-tuple-element.88), channel_id=1, source_target_pairs={{0,2},{1,3},{2,0},{3,1},{4,6},{5,7},{6,4},{7,5},{8,10},{9,11},{10,... | collective-permute-start | bytes 245768 | tf_op jit(solution)/shard_map/ppermute | solution.py:71
  115.5 8.1 %collective-permute-start.28 = (bf16[64,640]{1,0:T(8,128)(2,1)S(1)}, bf16[64,640]{1,0:T(8,128)(2,1)S(1)}, u32[]{:S(2)}, u32[]{:S(2)}) collective-permute-start(bf16[64,640]{1,0:T(8,128)(2,1)S(1)} %get-tuple-element.89), channel_id=1, source_target_pairs={{0,4},{1,5},{2,6},{3,7},{4,0},{5,1},{6,2},{7,3},{8,12},{9,13},{10,... | collective-permute-start | bytes 245768 | tf_op jit(solution)/shard_map/ppermute | solution.py:71
  117.4 7.9 %collective-permute-start.29 = (bf16[64,640]{1,0:T(8,128)(2,1)S(1)}, bf16[64,640]{1,0:T(8,128)(2,1)S(1)}, u32[]{:S(2)}, u32[]{:S(2)}) collective-permute-start(bf16[64,640]{1,0:T(8,128)(2,1)S(1)} %get-tuple-element.90), channel_id=1, source_target_pairs={{0,6},{1,7},{2,4},{3,5},{4,2},{5,3},{6,0},{7,1},{8,14},{9,15},{10,... | collective-permute-start | bytes 245768 | tf_op jit(solution)/shard_map/ppermute | solution.py:71
  125.4 5.4 %collective-permute-start.32 = (bf16[64,640]{1,0:T(8,128)(2,1)S(1)}, bf16[64,640]{1,0:T(8,128)(2,1)S(1)}, u32[]{:S(2)}, u32[]{:S(2)}) collective-permute-start(bf16[64,640]{1,0:T(8,128)(2,1)S(1)} %add_convert_fusion.3.refs_0_), channel_id=1, source_target_pairs={{0,24},{8,16},{16,8},{24,0},{1,25},{9,17},{17,9},{25,1},{2,26},{10... | collective-permute-start | bytes 245768 | tf_op jit(solution)/shard_map/ppermute | solution.py:66
  127.2 4.5 %collective-permute-start.31 = (bf16[64,640]{1,0:T(8,128)(2,1)S(1)}, bf16[64,640]{1,0:T(8,128)(2,1)S(1)}, u32[]{:S(2)}, u32[]{:S(2)}) collective-permute-start(bf16[64,640]{1,0:T(8,128)(2,1)S(1)} %add_convert_fusion.3.refs_0_), channel_id=1, source_target_pairs={{0,16},{8,24},{16,0},{24,8},{1,17},{9,25},{17,1},{25,9},{2,18},{10... | collective-permute-start | bytes 245768 | tf_op jit(solution)/shard_map/ppermute | solution.py:66
  127.7 4.4 %collective-permute-start.30 = (bf16[64,640]{1,0:T(8,128)(2,1)S(1)}, bf16[64,640]{1,0:T(8,128)(2,1)S(1)}, u32[]{:S(2)}, u32[]{:S(2)}) collective-permute-start(bf16[64,640]{1,0:T(8,128)(2,1)S(1)} %add_convert_fusion.3.refs_0_), channel_id=1, source_target_pairs={{0,8},{8,0},{16,24},{24,16},{1,9},{9,1},{17,25},{25,17},{2,10},{10... | collective-permute-start | bytes 245768 | tf_op jit(solution)/shard_map/ppermute | solution.py:66

commit v2 on v1

v2 whole, which is shorter than its diff:
```python
import jax
import jax.numpy as jnp
from jax import lax
from jax.experimental import pallas as pl
from jax.experimental.pallas import tpu as pltpu
from jax.sharding import PartitionSpec as P

HEADS = 4
EPS = 1e-05
LANES = 128
F32 = jnp.float32
BF16 = jnp.bfloat16
I32 = jnp.int32
VMEM_BYTES = 32 * 1024 * 1024

NN = ((1,), (0,))
NT = ((1,), (1,))
TN = ((0,), (0,))


def dot(left, right, dims=NN):
    return lax.dot_general(left, right, (dims, ((), ())), preferred_element_type=F32)


def sigmoid(value):
    return 0.5 * jnp.tanh(0.5 * value) + 0.5


def run(name, body, outs, args, smem=0, scratch=()):
    outs = [jax.ShapeDtypeStruct(shape, dtype) for shape, dtype in outs]
    in_smem = pl.BlockSpec(memory_space=pltpu.SMEM)
    in_vmem = pl.BlockSpec(memory_space=pltpu.VMEM)
    results = pl.pallas_call(
        body,
        out_shape=outs,
        in_specs=[in_smem] * smem + [in_vmem] * (len(args) - smem),
        out_specs=[in_vmem] * len(outs),
        scratch_shapes=list(scratch),
        compiler_params=pltpu.CompilerParams(vmem_limit_bytes=VMEM_BYTES),
        cost_estimate=pl.CostEstimate(flops=0, bytes_accessed=0, transcendentals=0),
        name=name,
    )(*args)
    return list(results)


class Grid:
    def __init__(self):
        self.replicas = lax.axis_size("replica")
        self.shards = lax.axis_size("sparse")
        self.cores = 2 if self.shards % 2 == 0 else 1
        self.line = self.shards // self.cores
        self.r = lax.axis_index("replica")
        self.s = lax.axis_index("sparse")
        self.z = self.s // self.cores
        self.c = self.s % self.cores

    def peer(self, index, size, step):
        if size & (size - 1) == 0:
            return index ^ step
        return (step - index) % size

    def over_replica(self, value, step):
        n = self.replicas
        return lax.ppermute(value, "replica", [(i, self.peer(i, n, step)) for i in range(n)])

    def swap_replica(self, value):
        return lax.all_to_all(value, "replica", split_axis=0, concat_axis=0, tiled=True)

    def swap_line(self, value):
        groups = [list(range(c, self.shards, self.cores)) for c in range(self.cores)]
        return lax.all_to_all(
            value, "sparse", split_axis=0, concat_axis=0, axis_index_groups=groups, tiled=True
        )

    def over_line(self, value, step):
        n, c = self.line, self.cores
        pairs = [(i, self.peer(i // c, n, step) * c + i % c) for i in range(n * c)]
        return lax.ppermute(value, "sparse", pairs)

    def over_pair(self, value):
        return lax.ppermute(value, "sparse", [(i, i ^ 1) for i in range(self.shards)])

    def replica_peer(self, step):
        return self.peer(self.r, self.replicas, step)

    def line_peer(self, step):
        return self.peer(self.z, self.line, step)


def make_keys(rows, item_owner, item_row, action_owner, action_row, copies):
    length = item_row.shape[0]

    def body(*refs):
        *in_refs, out_ref = refs
        for table in range(2):
            owner, row = in_refs[2 * table : 2 * table + 2]
            number = owner[...] * rows + row[...]
            for k in range(copies):
                out_ref[k, table : table + 1, :] = number

    args = [a.reshape(1, length) for a in (item_owner, item_row, action_owner, action_row)]
    return run("make_keys", body, [((copies, 2, length), I32)], args)[0]


def fetch(cohorts, chunk, base, before=()):
    many = len(cohorts)
    count, _, tokens, _ = cohorts[0].shape
    rows, cols = chunk.shape[0] // 2, chunk.shape[1]

    def body(base_ref, chunk_ref, *refs):
        key_refs, before_refs, out_refs = refs[:many], refs[many:-many], refs[-many:]
        lane = lax.broadcasted_iota(I32, (tokens, LANES), 1)
        for m in range(many):
            for k in range(count):
                hot = []
                for table in range(2):
                    place = key_refs[m][k, table] - base_ref[0]
                    for start in range(0, rows, LANES):
                        hot.append(jnp.where(place == lane + start, 1.0, 0.0).astype(BF16))
                found = dot(jnp.concatenate(hot, axis=1), chunk_ref[...])
                if before_refs:
                    found = found + before_refs[m][k].astype(F32)
                out_refs[m][k] = found.astype(BF16)

    return run(
        "fetch",
        body,
        [((count, tokens, cols), BF16)] * many,
        [base.reshape(1), chunk, *cohorts, *before],
        smem=1,
    )


def gather_grad(keys, pieces, base, rows, before=(), out=BF16):
    count, _, tokens = keys.shape
    cols = pieces.shape[-1]

    def body(base_ref, key_ref, piece_ref, *refs):
        *before_refs, out_ref = refs
        piece = piece_ref[...].reshape(count * tokens, cols)
        row = lax.broadcasted_iota(I32, (rows, tokens), 0)
        for table in range(2):
            span = slice(table * rows, (table + 1) * rows)
            hot = []
            for k in range(count):
                place = key_ref[k, table : table + 1, :] - base_ref[0]
                hot.append(jnp.where(place == row, 1.0, 0.0).astype(BF16))
            sums = dot(jnp.concatenate(hot, axis=1), piece)
            for ref in before_refs:
                sums = sums + ref[span, :].astype(F32)
            out_ref[span, :] = sums.astype(out)

    return run(
        "gather_grad",
        body,
        [((2 * rows, cols), out)],
        [base.reshape(1), keys, pieces, *before],
        smem=1,
    )[0]


def sequence(pieces, cotangent, gain, w_proj, w_out):
    count = pieces.shape[0]
    length, width = cotangent.shape
    cols = width // count
    head_dim = width // HEADS
    factor = head_dim ** (-0.5)
    tile = min(256, length)
    step = min(256, 4 * width)

    def body(piece_ref, cot_ref, gain_ref, wp_ref, wo_ref, *refs):
        out_ref, grad_ref, normed_ref, dproj_ref, gated_ref = refs[:5]
        emb, act, slope, att, attn, dscale, dkey, dval = refs[5:]

        for k in range(count):
            emb[:, k * cols : (k + 1) * cols] = piece_ref[k]

        def norm_of(value):
            centred = value - jnp.mean(value, axis=-1, keepdims=True)
            scale = lax.rsqrt(jnp.mean(centred * centred, axis=-1, keepdims=True) + EPS)
            return centred * scale, scale

        def norm_back(upper, hat, scale):
            return scale * (
                upper
                - jnp.mean(upper, axis=-1, keepdims=True)
                - hat * jnp.mean(upper * hat, axis=-1, keepdims=True)
            )

        for at in range(0, length, tile):
            span = slice(at, at + tile)
            hat, _ = norm_of(emb[span, :].astype(F32))
            normed_ref[span, :] = (hat * gain_ref[...]).astype(BF16)

        normed = normed_ref[...]

        @pl.loop(0, 4 * width // step)
        def _(j):
            span = pl.ds(pl.multiple_of(j * step, step), step)
            proj = dot(normed, wp_ref[:, span])
            sig = sigmoid(proj)
            act[:, span] = (proj * sig).astype(BF16)
            slope[:, span] = sig * (1.0 + proj * (1.0 - sig))

        dkey[...] = jnp.zeros_like(dkey)
        dval[...] = jnp.zeros_like(dval)

        for at in range(0, length, tile):
            span = slice(at, at + tile)
            seen = at + tile
            past = slice(0, seen)
            keep = lax.broadcasted_iota(I32, (tile, seen), 1) <= at + lax.broadcasted_iota(
                I32, (tile, seen), 0
            )
            for h in range(HEADS):
                head = [slice(p * width + h * head_dim, p * width + (h + 1) * head_dim) for p in range(4)]
                scores = dot(act[span, head[2]], act[past, head[3]], NT) * factor
                sig = sigmoid(scores)
                soft = jnp.where(keep, scores * sig * (1.0 / length), 0.0).astype(BF16)
                attn[h, :, :seen] = soft
                grad = sig * (1.0 + scores * (1.0 - sig)) * (factor / length)
                dscale[h, :, :seen] = jnp.where(keep, grad, 0.0)
                att[:, head[0]] = dot(soft, act[past, head[1]])
            hat, scale = norm_of(att[...])
            gate = act[span, :width].astype(F32)
            gated = (hat * gate).astype(BF16)
            gated_ref[span, :] = gated
            out_ref[span, :] = (emb[span, :].astype(F32) + dot(gated, wo_ref[...])).astype(BF16)
            dgated = dot(cot_ref[span, :], wo_ref[...], NT)
            dproj_ref[span, :width] = (dgated * hat * slope[span, :width]).astype(BF16)
            datt = norm_back(dgated * gate, hat, scale).astype(BF16)
            for h in range(HEADS):
                head = [slice(p * width + h * head_dim, p * width + (h + 1) * head_dim) for p in range(4)]
                dhead = datt[:, head[0]]
                dattn = dot(dhead, act[past, head[1]], NT)
                dscores = (dattn * dscale[h, :, :seen]).astype(BF16)
                dquery = dot(dscores, act[past, head[3]])
                dproj_ref[span, head[2]] = (dquery * slope[span, head[2]]).astype(BF16)
                dkey[past, head[0]] += dot(dscores, act[span, head[2]], TN)
                dval[past, head[0]] += dot(attn[h, :, :seen], dhead, TN)

        dproj_ref[:, width : 2 * width] = (dval[...] * slope[:, width : 2 * width]).astype(BF16)
        dproj_ref[:, 3 * width :] = (dkey[...] * slope[:, 3 * width :]).astype(BF16)

        for at in range(0, length, tile):
            span = slice(at, at + tile)
            hat, scale = norm_of(emb[span, :].astype(F32))
            upper = dot(dproj_ref[span, :], wp_ref[...], NT) * gain_ref[...]
            grad = cot_ref[span, :].astype(F32) + norm_back(upper, hat, scale)
            for k in range(count):
                grad_ref[k, span, :] = grad[:, k * cols : (k + 1) * cols].astype(BF16)

    return run(
        "sequence",
        body,
        [
            ((length, width), BF16),
            ((count, length, cols), BF16),
            ((length, width), BF16),
            ((length, 4 * width), BF16),
            ((length, width), BF16),
        ],
        [pieces, cotangent, gain, w_proj, w_out],
        scratch=[
            pltpu.VMEM((length, width), BF16),
            pltpu.VMEM((length, 4 * width), BF16),
            pltpu.VMEM((length, 4 * width), F32),
            pltpu.VMEM((tile, width), F32),
            pltpu.VMEM((HEADS, tile, length), BF16),
            pltpu.VMEM((HEADS, tile, length), F32),
            pltpu.VMEM((length, width), F32),
            pltpu.VMEM((length, width), F32),
        ],
    )


def weight_grad(parity, normed, dproj, gated, cotangent, cores, line, blocks, before=()):
    length, width = normed.shape
    rows = width // (cores * line)
    half = width // cores
    edge = dproj.shape[1]
    total = edge + cotangent.shape[1]
    cols = total // blocks

    def body(parity_ref, n_ref, d_ref, g_ref, c_ref, *refs):
        *before_refs, out_ref = refs
        feature = lax.broadcasted_iota(I32, (width, half), 0)
        column = lax.broadcasted_iota(I32, (width, half), 1)
        wanted = (column // rows * cores + parity_ref[0]) * rows + column % rows
        pick = jnp.where(feature == wanted, 1.0, 0.0).astype(BF16)
        n_part = dot(n_ref[...], pick).astype(BF16)
        g_part = dot(g_ref[...], pick).astype(BF16)
        for k in range(blocks):
            first, last = k * cols, (k + 1) * cols
            parts = []
            if first < edge:
                parts.append(dot(n_part, d_ref[:, first : min(last, edge)], TN))
            if last > edge:
                parts.append(dot(g_part, c_ref[:, max(first, edge) - edge : last - edge], TN))
            sums = parts[0] if len(parts) == 1 else jnp.concatenate(parts, axis=1)
            for ref in before_refs:
                sums = sums + ref[k].astype(F32)
            out_ref[k] = sums.astype(BF16)

    return run(
        "weight_grad",
        body,
        [((blocks, half, cols), BF16)],
        [parity.reshape(1), normed, dproj, gated, cotangent, *before],
        smem=1,
    )[0]


def add_up(parts, copies):
    count, *shape = parts.shape

    def body(part_ref, out_ref):
        total = part_ref[0].astype(F32)
        for k in range(1, count):
            total = total + part_ref[k].astype(F32)
        for k in range(copies):
            out_ref[k] = total.astype(BF16)

    return run("add_up", body, [((copies, *shape), BF16)], [parts])[0]


def assemble(parts, edge):
    count, rows, cols = parts.shape
    total = cols * count

    def body(part_ref, left_ref, right_ref):
        for k in range(count):
            first, last = k * cols, (k + 1) * cols
            part = part_ref[k].astype(F32)
            cut = min(max(edge - first, 0), cols)
            if cut > 0:
                left_ref[:, first : first + cut] = part[:, :cut]
            if cut < cols:
                right_ref[:, first + cut - edge : last - edge] = part[:, cut:]

    return run("assemble", body, [((rows, edge), F32), ((rows, total - edge), F32)], [parts])


def local(
    item_table,
    action_table,
    item_owner,
    item_row,
    action_owner,
    action_row,
    input_norm_gain,
    w_proj,
    w_out,
    cotangent,
):
    grid = Grid()
    rows, width = item_table.shape
    replicas, line, cores = grid.replicas, grid.line, grid.cores
    cols = width // replicas

    def base_of(k):
        return ((grid.line_peer(k) * cores + grid.c) * rows).astype(I32)

    own = jnp.concatenate(
        [
            lax.dynamic_slice_in_dim(item_table, grid.r * cols, cols, 1),
            lax.dynamic_slice_in_dim(action_table, grid.r * cols, cols, 1),
        ],
        axis=0,
    )
    keys = make_keys(rows, item_owner, item_row, action_owner, action_row, replicas)

    held = [own] + [grid.over_line(own, k) for k in range(1, line)]
    bases = [base_of(k) for k in range(line)]
    cohorts = [grid.swap_replica(keys)]
    if cores == 2:
        cohorts.append(grid.over_pair(cohorts[0]))
    key_cols = [jnp.broadcast_to(k[..., None], (*k.shape, LANES)) for k in cohorts]

    found = ()
    for k in range(line - 1):
        found = fetch(key_cols, held[k], bases[k], found)
    found = [
        fetch(key_cols[m : m + 1], held[-1], bases[-1], found[m : m + 1])[0] for m in range(cores)
    ]
    pieces = found[0]
    for part in found[1:]:
        pieces = (pieces.astype(F32) + grid.over_pair(part).astype(F32)).astype(BF16)
    pieces = grid.swap_replica(pieces)

    layer_out, tokens, normed, dproj, gated = sequence(
        pieces, cotangent, input_norm_gain.reshape(1, width), w_proj, w_out
    )
    tokens = grid.swap_replica(tokens)

    def weights_of(m, before=()):
        parity = ((grid.c + m) % cores).astype(I32)
        return weight_grad(
            parity, normed, dproj, gated, cotangent, cores, line, replicas, before
        )

    parts = weights_of(0, [grid.over_pair(weights_of(m)) for m in range(1, cores)])
    parts = grid.swap_replica(parts)
    parts = add_up(parts, 1).reshape(line, width // grid.shards, parts.shape[-1])
    parts = grid.swap_line(parts)
    parts = grid.swap_replica(add_up(parts, replicas))
    grad_proj, grad_out = assemble(parts, 4 * width)

    tokens = [tokens] + [grid.over_pair(tokens)] * (cores - 1)
    table_grad = None
    for k in range(line - 1, -1, -1):
        total = ()
        for key, token in zip(cohorts, tokens):
            total = [gather_grad(key, token, bases[k], rows, total)]
        total = (grid.over_line(total[0], k) if k else total[0]).astype(F32)
        table_grad = total if table_grad is None else table_grad + total

    return layer_out, table_grad[:rows], table_grad[rows:], grad_proj, grad_out


def solution(mesh):
    tokens = ("replica", "sparse")
    in_specs = (
        P("sparse", None),
        P("sparse", None),
        P(tokens, None),
        P(tokens),
        P(tokens, None),
        P(tokens),
        P(),
        P(),
        P(),
        P(tokens, None),
    )
    out_specs = (
        P(tokens, None),
        P("sparse", "replica"),
        P("sparse", "replica"),
        P("sparse", None),
        P("sparse", None),
    )
    return jax.shard_map(local, mesh=mesh, in_specs=in_specs, out_specs=out_specs, check_vma=False)
```

time: 134 us -> 133 us (level)
  starting transfers between devices: 44 us -> 29.3 us
  blocking collectives: 0 us -> 8.44 us
  local copies, waits for them, and re-layouts: 3.94 us -> 11.5 us
  waiting for transfers between devices: 38.2 us -> 43.3 us
  Pallas kernels: 43 us -> 38.1 us
  other arithmetic: 3.63 us -> 1.07 us
    all_to_all x0 -> x5, waiting for transfers between devices: none -> 34.8 us  [the longest x4 27.8 us: swap_replica(): lax.all_to_all(value, 'replica', split_axis=0, concat_axis=0, tiled=True)]
    ppermute x15 -> x0, waiting for transfers between devices: 26.3 us -> none  [over_replica(): lax.ppermute(value, 'replica', [(i, self.peer(i, n, step)) for i in range...]
    ppermute x15 -> x0, starting transfers between devices: 20.5 us -> none  [over_replica(): lax.ppermute(value, 'replica', [(i, self.peer(i, n, step)) for i in range...]
    all_to_all x0 -> x5, starting transfers between devices: none -> 18.9 us  [the longest x4 14.2 us: swap_replica(): lax.all_to_all(value, 'replica', split_axis=0, concat_axis=0, tiled=True)]
    ppermute x9 -> x6, starting transfers between devices: 20.9 us -> 10.3 us  [over_line(): return lax.ppermute(value, 'sparse', pairs)]
    all_to_all x0 -> x1, blocking collectives: none -> 8.44 us  [swap_replica(): lax.all_to_all(value, 'replica', split_axis=0, concat_axis=0, tiled=True)]
    unnamed x8 -> x28, local copies, waits for them, and re-layouts: 1.35 us -> 8.53 us
    ppermute x9 -> x6, waiting for transfers between devices: 11.8 us -> 6.61 us  [over_line(): return lax.ppermute(value, 'sparse', pairs)]
  transfers between devices with their start and end apart: 33 -> 15, of which waited for: 17 -> 8; matrix products, arithmetic and copies ran while one was open for 4% -> 2% of each run, Pallas kernels for 16% -> 17%
where the time goes in v2:
time: 133 us
  waiting for transfers between devices  43.3 us (33%)
  Pallas kernels  38.1 us (29%)
  starting transfers between devices  29.3 us (22%)
  local copies, waits for them, and re-layouts  11.5 us (9%)
  blocking collectives  8.44 us (6%)
    pallas_call x20, Pallas kernels, run(): pl.pallas_call(body, out_shape=outs, in_specs=[in_smem] * smem + [in_vmem...  38.1 us
    all_to_all x4, waiting for transfers between devices, swap_replica(): lax.all_to_all(value, 'replica', split_axis=0, concat_axis=0, tiled=True)  27.8 us
    all_to_all x4, starting transfers between devices, swap_replica(): lax.all_to_all(value, 'replica', split_axis=0, concat_axis=0, tiled=True)  14.2 us
    ppermute x6, starting transfers between devices, over_line(): return lax.ppermute(value, 'sparse', pairs)  10.3 us
    unnamed x28, local copies, waits for them, and re-layouts  8.53 us
    all_to_all x1, blocking collectives, swap_replica(): lax.all_to_all(value, 'replica', split_axis=0, concat_axis=0, tiled=True)  8.44 us
    all_to_all x1, waiting for transfers between devices, swap_line(): lax.all_to_all(value, 'sparse', split_axis=0, concat_axis=0, axis_index_g...  7.05 us
    ppermute x6, waiting for transfers between devices, over_line(): return lax.ppermute(value, 'sparse', pairs)  6.61 us
  transfers between devices with their start and end apart: 15, of which 8 were waited for; matrix products, arithmetic and copies ran while one was open for 2% of the time, Pallas kernels for 17%

profile of v2, /device:TPU:0, one launch (start us, length us, event | category | flops | bytes accessed | tf_op | source)
XLA Modules:
  0.0 132.7 jit_solution(7538077967359562571)
XLA Ops:
  0.6 1.0 constant_dynamic-slice_fusion
  1.7 3.1 %collective-permute-start.3 = (bf16[1024,128]{1,0:T(8,128)(2,1)S(1)}, bf16[1024,128]{1,0:T(8,128)(2,1)S(1)}, u32[]{:S(2)}, u32[]{:S(2)}) collective-permute-start(bf16[1024,128]{1,0:T(8,128)(2,1)S(1)} %pad_maximum_fusion.chunk_ref), channel_id=1, source_target_pairs={{0,2},{1,3},{2,0},{3,1},{4,6},{5,7},{6,4},{7,5},{8,10},{9,11},{10,... | collective-permute-start | bytes 786440 | tf_op jit(solution)/shard_map/ppermute | solution.py:78
  4.8 2.6 %collective-permute-start.1 = (bf16[1024,128]{1,0:T(8,128)(2,1)S(1)}, bf16[1024,128]{1,0:T(8,128)(2,1)S(1)}, u32[]{:S(2)}, u32[]{:S(2)}) collective-permute-start(bf16[1024,128]{1,0:T(8,128)(2,1)S(1)} %pad_maximum_fusion.chunk_ref), channel_id=1, source_target_pairs={{0,4},{1,5},{2,6},{3,7},{4,0},{5,1},{6,2},{7,3},{8,12},{9,13},{10,... | collective-permute-start | bytes 786440 | tf_op jit(solution)/shard_map/ppermute | solution.py:78
  7.3 0.0 collective-permute-start
  7.3 0.7 copy-done.10
  8.0 0.7 copy-done.11
  8.7 0.7 copy-done.12
  9.4 0.7 copy-done.13
  10.1 8.4 %all_to_all.30.key_ref = s32[4,2,512]{2,1,0:T(2,128)S(1)} all-to-all(s32[4,2,512]{2,1,0:T(2,128)S(1)} %make_keys.1), channel_id=1, replica_groups=mesh['replica'=4,'sparse'=8] {'replica'}, dimensions={0} | all-to-all | bytes 32768 | tf_op jit(solution)/shard_map/all_to_all | solution.py:67
  18.5 1.2 collective-permute-done.2.key_ref
  19.7 0.6 broadcast_in_dim.5.refs_1_.refs_0_
  20.3 0.6 broadcast_in_dim.4.refs_0_
  20.9 2.3 %fetch.5 = (bf16[4,512,128]{2,1,0:T(8,128)(2,1)S(1)}, bf16[4,512,128]{2,1,0:T(8,128)(2,1)S(1)}) custom-call(s32[1]{0:T(128)} %bitcast.7.base_ref, bf16[1024,128]{1,0:T(8,128)(2,1)S(1)} %pad_maximum_fusion.chunk_ref, s32[4,2,512,128]{3,2,1,0:T(8,128)S(1)} %broadcast_in_dim.4.refs_0_, s32[4,2,512,128]{3,2,1,0:T(8,128)S(1)} %broadcast_in_dim.5.refs_1_.refs_0_), custom_call_target="tpu_custom_call" | custom-call | tf_op jit(solution)/shard_map/fetch/pallas_call | solution.py:33
  23.2 0.0 collective-permute-done.3.chunk_ref
  23.3 2.3 %fetch.6 = (bf16[4,512,128]{2,1,0:T(8,128)(2,1)S(1)}, bf16[4,512,128]{2,1,0:T(8,128)(2,1)S(1)}) custom-call(s32[1]{0:T(128)} %bitcast.6.base_ref, bf16[1024,128]{1,0:T(8,128)(2,1)S(1)} %collective-permute-done.3.chunk_ref, s32[4,2,512,128]{3,2,1,0:T(8,128)S(1)} %broadcast_in_dim.4.refs_0_, s32[4,2,512,128]{3,2,1,0:T(8,128)S(1)} %broadcast_in_dim.5.refs_1_.refs_0_, ...), custom_call_target="tpu_custom_call" | custom-call | tf_op jit(solution)/shard_map/fetch/pallas_call | solution.py:33
  25.6 0.5 collective-permute-done.1.chunk_ref
  26.1 2.3 %fetch.7 = (bf16[4,512,128]{2,1,0:T(8,128)(2,1)S(1)}, bf16[4,512,128]{2,1,0:T(8,128)(2,1)S(1)}) custom-call(s32[1]{0:T(128)} %bitcast.5.base_ref, bf16[1024,128]{1,0:T(8,128)(2,1)S(1)} %collective-permute-done.1.chunk_ref, s32[4,2,512,128]{3,2,1,0:T(8,128)S(1)} %broadcast_in_dim.4.refs_0_, s32[4,2,512,128]{3,2,1,0:T(8,128)S(1)} %broadcast_in_dim.5.refs_1_.refs_0_, ...), custom_call_target="tpu_custom_call" | custom-call | tf_op jit(solution)/shard_map/fetch/pallas_call | solution.py:33
  28.5 0.0 collective-permute-done.chunk_ref
  28.5 1.3 fetch.9
  29.7 0.1 collective-permute-start.4
  29.8 1.3 fetch.8
  31.1 0.0 copy-start.1
  31.1 0.0 copy-start.9
  31.1 0.6 collective-permute-done.4
  31.7 0.9 add_convert_fusion
  32.6 3.7 %all-to-all-start.1 = ((bf16[4,512,128]{2,1,0:T(8,128)(2,1)}), bf16[4,512,128]{2,1,0:T(8,128)(2,1)S(1)}, u32[]{:S(2)}, u32[]{:S(2)}) async-start(bf16[4,512,128]{2,1,0:T(8,128)(2,1)} %add_convert_fusion), calls=%async_computation.1 | async-start | bytes 1048576 | tf_op jit(solution)/shard_map/all_to_all | solution.py:67
  36.3 8.3 %all-to-all-done.1.piece_ref = bf16[4,512,128]{2,1,0:T(8,128)(2,1)S(1)} async-done(((bf16[4,512,128]{2,1,0:T(8,128)(2,1)}), bf16[4,512,128]{2,1,0:T(8,128)(2,1)S(1)}, u32[]{:S(2)}, u32[]{:S(2)}) %all-to-all-start.1) | async-done | bytes 524320 | tf_op jit(solution)/shard_map/all_to_all | solution.py:67
  44.7 1.6 %copy-done.6 = bf16[512,2048]{1,0:T(8,128)(2,1)S(1)} copy-done((bf16[512,2048]{1,0:T(8,128)(2,1)S(1)}, bf16[512,2048]{1,0:T(8,128)(2,1)}, u32[]{:S(2)}) %copy-start.6) | copy-done | bytes 2097176
  46.3 1.0 copy-done.7
  47.3 10.9 %sequence.1 = (bf16[512,512]{1,0:T(8,128)(2,1)}, bf16[4,512,128]{2,1,0:T(8,128)(2,1)S(1)}, bf16[512,512]{1,0:T(8,128)(2,1)S(1)}, bf16[512,2048]{1,0:T(8,128)(2,1)S(1)}, bf16[512,512]{1,0:T(8,128)(2,1)S(1)}) custom-call(bf16[4,512,128]{2,1,0:T(8,128)(2,1)S(1)} %all-to-all-done.1.piece_ref, bf16[512,512]{1,0:T(8,128)(2,1)S(1)} %copy-done.1, ...), custom_call_target="tpu_custom_call" | custom-call | tf_op jit(solution)/shard_map/sequence/pallas_call | solution.py:33
  58.2 0.0 copy-start.8
  58.3 2.5 %weight_grad.2 = bf16[4,256,640]{2,1,0:T(8,128)(2,1)} custom-call(s32[1]{0:T(128)} %bitcast.10.parity_ref, bf16[512,512]{1,0:T(8,128)(2,1)S(1)} %get-tuple-element.26.n_ref, bf16[512,2048]{1,0:T(8,128)(2,1)S(1)} %get-tuple-element.27.d_ref, bf16[512,512]{1,0:T(8,128)(2,1)S(1)} %get-tuple-element.28.g_ref, bf16[512,512]{1,0:T(8,128)(2,1)S(1)} %copy-done.1), custom_call_target="tpu_custom_call" | custom-call | tf_op jit(solution)/shard_map/weight_grad/pallas_call | solution.py:33
  60.7 0.1 collective-permute-start.9
  60.8 3.5 %all-to-all-start.2 = ((bf16[4,512,128]{2,1,0:T(8,128)(2,1)}), bf16[4,512,128]{2,1,0:T(8,128)(2,1)S(1)}, u32[]{:S(2)}, u32[]{:S(2)}) async-start(bf16[4,512,128]{2,1,0:T(8,128)(2,1)} %copy-done.8), calls=%async_computation.2 | async-start | bytes 1048576 | tf_op jit(solution)/shard_map/all_to_all | solution.py:67
  64.3 0.0 collective-permute-done.9.refs_0_
  64.3 1.0 copy-done.3
  65.4 1.0 copy-done.5
  66.4 2.7 %weight_grad.3 = bf16[4,256,640]{2,1,0:T(8,128)(2,1)S(1)} custom-call(s32[1]{0:T(128)} %bitcast.9.parity_ref, bf16[512,512]{1,0:T(8,128)(2,1)S(1)} %copy-done.3, bf16[512,2048]{1,0:T(8,128)(2,1)S(1)} %get-tuple-element.27.d_ref, bf16[512,512]{1,0:T(8,128)(2,1)S(1)} %copy-done.5, bf16[512,512]{1,0:T(8,128)(2,1)S(1)} %copy-done.1, ...), custom_call_target="tpu_custom_call" | custom-call | tf_op jit(solution)/shard_map/weight_grad/pallas_call | solution.py:33
  69.2 1.1 copy-done
  70.2 3.0 %all-to-all-done.2.piece_ref = bf16[4,512,128]{2,1,0:T(8,128)(2,1)S(1)} async-done(((bf16[4,512,128]{2,1,0:T(8,128)(2,1)}), bf16[4,512,128]{2,1,0:T(8,128)(2,1)S(1)}, u32[]{:S(2)}, u32[]{:S(2)}) %all-to-all-start.2) | async-done | bytes 524320 | tf_op jit(solution)/shard_map/all_to_all | solution.py:67
  73.2 3.5 %all-to-all-start.3 = ((bf16[4,256,640]{2,1,0:T(8,128)(2,1)}), bf16[4,256,640]{2,1,0:T(8,128)(2,1)S(1)}, u32[]{:S(2)}, u32[]{:S(2)}) async-start(bf16[4,256,640]{2,1,0:T(8,128)(2,1)} %copy-done), calls=%async_computation.3 | async-start | bytes 2621440 | tf_op jit(solution)/shard_map/all_to_all | solution.py:67
  76.8 0.1 collective-permute-start.5
  76.8 16.5 %all-to-all-done.3.part_ref = bf16[4,256,640]{2,1,0:T(8,128)(2,1)S(1)} async-done(((bf16[4,256,640]{2,1,0:T(8,128)(2,1)}), bf16[4,256,640]{2,1,0:T(8,128)(2,1)S(1)}, u32[]{:S(2)}, u32[]{:S(2)}) %all-to-all-start.3) | async-done | bytes 1310752 | tf_op jit(solution)/shard_map/all_to_all | solution.py:67
  93.3 0.9 add_up.2
  94.2 4.7 %all-to-all-start.4 = ((bf16[4,64,640]{2,1,0:T(8,128)(2,1)}), bf16[4,64,640]{2,1,0:T(8,128)(2,1)S(1)}, u32[]{:S(2)}, u32[]{:S(2)}) async-start(bf16[4,64,640]{2,1,0:T(8,128)(2,1)} %bitcast.11), calls=%async_computation.4 | async-start | bytes 655360 | tf_op jit(solution)/shard_map/all_to_all | solution.py:71
  98.9 1.2 gather_grad.8.refs_0_
  100.1 1.2 gather_grad.10.refs_0_
  101.4 1.2 gather_grad.12.refs_0_
  102.6 0.0 collective-permute-done.5.piece_ref
  102.6 1.2 gather_grad.9
  103.9 3.9 %collective-permute-start.6 = (bf16[1024,128]{1,0:T(8,128)(2,1)S(1)}, bf16[1024,128]{1,0:T(8,128)(2,1)S(1)}, u32[]{:S(2)}, u32[]{:S(2)}) collective-permute-start(bf16[1024,128]{1,0:T(8,128)(2,1)S(1)} %gather_grad.9), channel_id=1, source_target_pairs={{0,6},{1,7},{2,4},{3,5},{4,2},{5,3},{6,0},{7,1},{8,14},{9,15},{10,... | collective-permute-start | bytes 786440 | tf_op jit(solution)/shard_map/ppermute | solution.py:78
  107.8 1.2 gather_grad.11
  109.0 0.1 collective-permute-start.7
  109.1 1.2 gather_grad.13
  110.4 0.6 collective-permute-start.8
  111.0 1.2 gather_grad.14.refs_0_
  112.2 1.2 gather_grad.15
  113.5 7.1 %all-to-all-done.4.part_ref = bf16[4,64,640]{2,1,0:T(8,128)(2,1)S(1)} async-done(((bf16[4,64,640]{2,1,0:T(8,128)(2,1)}), bf16[4,64,640]{2,1,0:T(8,128)(2,1)S(1)}, u32[]{:S(2)}, u32[]{:S(2)}) %all-to-all-start.4) | async-done | bytes 327712 | tf_op jit(solution)/shard_map/all_to_all | solution.py:71
  120.5 0.8 add_up.3
  121.3 3.5 %all-to-all-start.5 = ((bf16[4,64,640]{2,1,0:T(8,128)(2,1)}), bf16[4,64,640]{2,1,0:T(8,128)(2,1)S(1)}, u32[]{:S(2)}, u32[]{:S(2)}) async-start(bf16[4,64,640]{2,1,0:T(8,128)(2,1)} %add_up.3), calls=%async_computation.5 | async-start | bytes 655360 | tf_op jit(solution)/shard_map/all_to_all | solution.py:67
  124.8 6.1 %collective-permute-done.7 = bf16[1024,128]{1,0:T(8,128)(2,1)S(1)} collective-permute-done((bf16[1024,128]{1,0:T(8,128)(2,1)S(1)}, bf16[1024,128]{1,0:T(8,128)(2,1)S(1)}, u32[]{:S(2)}, u32[]{:S(2)}) %collective-permute-start.7) | collective-permute-done | bytes 262176 | tf_op jit(solution)/shard_map/ppermute | solution.py:78
  130.9 0.1 convert_add_fusion
  131.0 0.8 fusion
  131.8 0.9 assemble.1
  (22 shorter events, 0.1 us)
Async XLA Ops:
  1.7 21.6 %collective-permute-start.3 = (bf16[1024,128]{1,0:T(8,128)(2,1)S(1)}, bf16[1024,128]{1,0:T(8,128)(2,1)S(1)}, u32[]{:S(2)}, u32[]{:S(2)}) collective-permute-start(bf16[1024,128]{1,0:T(8,128)(2,1)S(1)} %pad_maximum_fusion.chunk_ref), channel_id=1, source_target_pairs={{0,2},{1,3},{2,0},{3,1},{4,6},{5,7},{6,4},{7,5},{8,10},{9,11},{10,... | collective-permute-start | bytes 786440 | tf_op jit(solution)/shard_map/ppermute | solution.py:78
  4.8 21.4 %collective-permute-start.1 = (bf16[1024,128]{1,0:T(8,128)(2,1)S(1)}, bf16[1024,128]{1,0:T(8,128)(2,1)S(1)}, u32[]{:S(2)}, u32[]{:S(2)}) collective-permute-start(bf16[1024,128]{1,0:T(8,128)(2,1)S(1)} %pad_maximum_fusion.chunk_ref), channel_id=1, source_target_pairs={{0,4},{1,5},{2,6},{3,7},{4,0},{5,1},{6,2},{7,3},{8,12},{9,13},{10,... | collective-permute-start | bytes 786440 | tf_op jit(solution)/shard_map/ppermute | solution.py:78
  7.3 21.1 %collective-permute-start = (bf16[1024,128]{1,0:T(8,128)(2,1)S(1)}, bf16[1024,128]{1,0:T(8,128)(2,1)S(1)}, u32[]{:S(2)}, u32[]{:S(2)}) collective-permute-start(bf16[1024,128]{1,0:T(8,128)(2,1)S(1)} %pad_maximum_fusion.chunk_ref), channel_id=1, source_target_pairs={{0,6},{1,7},{2,4},{3,5},{4,2},{5,3},{6,0},{7,1},{8,14},{9,15},{10,... | collective-permute-start | bytes 786440 | tf_op jit(solution)/shard_map/ppermute | solution.py:78
  7.3 0.7 copy-start.10
  8.0 0.7 copy-start.11
  8.7 0.7 copy-start.12
  9.4 0.7 copy-start.13
  18.5 1.2 collective-permute-start.2
  29.7 2.0 %collective-permute-start.4 = (bf16[4,512,128]{2,1,0:T(8,128)(2,1)S(1)}, bf16[4,512,128]{2,1,0:T(8,128)(2,1)S(1)}, u32[]{:S(2)}, u32[]{:S(2)}) collective-permute-start(bf16[4,512,128]{2,1,0:T(8,128)(2,1)S(1)} %fetch.9), channel_id=1, source_target_pairs={{0,1},{1,0},{2,3},{3,2},{4,5},{5,4},{6,7},{7,6},{8,9},{9,8},{10,11... | collective-permute-start | bytes 1572872 | tf_op jit(solution)/shard_map/ppermute | solution.py:81
  31.1 13.6 %copy-start.1 = (bf16[512,512]{1,0:T(8,128)(2,1)S(1)}, bf16[512,512]{1,0:T(8,128)(2,1)}, u32[]{:S(2)}) copy-start(bf16[512,512]{1,0:T(8,128)(2,1)} %c_ref.3) | copy-start | bytes 1572868
  31.1 13.6 %copy-start.9 = (f32[512]{0:T(512)S(1)}, f32[512]{0:T(512)}, u32[]{:S(2)}) copy-start(f32[512]{0:T(512)} %param.16) | copy-start | bytes 6148
  32.6 12.0 %all-to-all-start.1 = ((bf16[4,512,128]{2,1,0:T(8,128)(2,1)}), bf16[4,512,128]{2,1,0:T(8,128)(2,1)S(1)}, u32[]{:S(2)}, u32[]{:S(2)}) async-start(bf16[4,512,128]{2,1,0:T(8,128)(2,1)} %add_convert_fusion), calls=%async_computation.1 | async-start | bytes 1048576 | tf_op jit(solution)/shard_map/all_to_all | solution.py:67
  44.7 1.6 %copy-start.6 = (bf16[512,2048]{1,0:T(8,128)(2,1)S(1)}, bf16[512,2048]{1,0:T(8,128)(2,1)}, u32[]{:S(2)}) copy-start(bf16[512,2048]{1,0:T(8,128)(2,1)} %wp_ref.1) | copy-start | bytes 6291460
  46.3 1.0 copy-start.7
  58.2 2.5 %copy-start.2 = (bf16[512,512]{1,0:T(8,128)(2,1)}, bf16[512,512]{1,0:T(8,128)(2,1)S(1)}, u32[]{:S(2)}) copy-start(bf16[512,512]{1,0:T(8,128)(2,1)S(1)} %get-tuple-element.26.n_ref) | copy-start | bytes 1572868
  58.2 2.5 %copy-start.4 = (bf16[512,512]{1,0:T(8,128)(2,1)}, bf16[512,512]{1,0:T(8,128)(2,1)S(1)}, u32[]{:S(2)}) copy-start(bf16[512,512]{1,0:T(8,128)(2,1)S(1)} %get-tuple-element.28.g_ref) | copy-start | bytes 1572868
  58.2 2.5 %copy-start.8 = (bf16[4,512,128]{2,1,0:T(8,128)(2,1)}, bf16[4,512,128]{2,1,0:T(8,128)(2,1)S(1)}, u32[]{:S(2)}) copy-start(bf16[4,512,128]{2,1,0:T(8,128)(2,1)S(1)} %get-tuple-element.25) | copy-start | bytes 1572868
  60.7 3.6 %collective-permute-start.9 = (bf16[4,256,640]{2,1,0:T(8,128)(2,1)}, bf16[4,256,640]{2,1,0:T(8,128)(2,1)}, u32[]{:S(2)}, u32[]{:S(2)}) collective-permute-start(bf16[4,256,640]{2,1,0:T(8,128)(2,1)} %weight_grad.2), channel_id=1, source_target_pairs={{0,1},{1,0},{2,3},{3,2},{4,5},{5,4},{6,7},{7,6},{8,9},{9,8},{10,11... | collective-permute-start | bytes 3932168 | tf_op jit(solution)/shard_map/ppermute | solution.py:81
  60.8 12.4 %all-to-all-start.2 = ((bf16[4,512,128]{2,1,0:T(8,128)(2,1)}), bf16[4,512,128]{2,1,0:T(8,128)(2,1)S(1)}, u32[]{:S(2)}, u32[]{:S(2)}) async-start(bf16[4,512,128]{2,1,0:T(8,128)(2,1)} %copy-done.8), calls=%async_computation.2 | async-start | bytes 1048576 | tf_op jit(solution)/shard_map/all_to_all | solution.py:67
  64.3 1.0 copy-start.3
  65.4 1.0 copy-start.5
  69.2 1.1 copy-start
  73.2 20.1 %all-to-all-start.3 = ((bf16[4,256,640]{2,1,0:T(8,128)(2,1)}), bf16[4,256,640]{2,1,0:T(8,128)(2,1)S(1)}, u32[]{:S(2)}, u32[]{:S(2)}) async-start(bf16[4,256,640]{2,1,0:T(8,128)(2,1)} %copy-done), calls=%async_computation.3 | async-start | bytes 2621440 | tf_op jit(solution)/shard_map/all_to_all | solution.py:67
  76.8 25.9 %collective-permute-start.5 = (bf16[4,512,128]{2,1,0:T(8,128)(2,1)S(1)}, bf16[4,512,128]{2,1,0:T(8,128)(2,1)S(1)}, u32[]{:S(2)}, u32[]{:S(2)}) collective-permute-start(bf16[4,512,128]{2,1,0:T(8,128)(2,1)S(1)} %all-to-all-done.2.piece_ref), channel_id=1, source_target_pairs={{0,1},{1,0},{2,3},{3,2},{4,5},{5,4},{6,7},{7,6},{8,9},{9,8},{10,11... | collective-permute-start | bytes 1572872 | tf_op jit(solution)/shard_map/ppermute | solution.py:81
  94.2 26.3 %all-to-all-start.4 = ((bf16[4,64,640]{2,1,0:T(8,128)(2,1)}), bf16[4,64,640]{2,1,0:T(8,128)(2,1)S(1)}, u32[]{:S(2)}, u32[]{:S(2)}) async-start(bf16[4,64,640]{2,1,0:T(8,128)(2,1)} %bitcast.11), calls=%async_computation.4 | async-start | bytes 655360 | tf_op jit(solution)/shard_map/all_to_all | solution.py:71
  103.9 20.9 %collective-permute-start.6 = (bf16[1024,128]{1,0:T(8,128)(2,1)S(1)}, bf16[1024,128]{1,0:T(8,128)(2,1)S(1)}, u32[]{:S(2)}, u32[]{:S(2)}) collective-permute-start(bf16[1024,128]{1,0:T(8,128)(2,1)S(1)} %gather_grad.9), channel_id=1, source_target_pairs={{0,6},{1,7},{2,4},{3,5},{4,2},{5,3},{6,0},{7,1},{8,14},{9,15},{10,... | collective-permute-start | bytes 786440 | tf_op jit(solution)/shard_map/ppermute | solution.py:78
  109.0 21.8 %collective-permute-start.7 = (bf16[1024,128]{1,0:T(8,128)(2,1)S(1)}, bf16[1024,128]{1,0:T(8,128)(2,1)S(1)}, u32[]{:S(2)}, u32[]{:S(2)}) collective-permute-start(bf16[1024,128]{1,0:T(8,128)(2,1)S(1)} %gather_grad.11), channel_id=1, source_target_pairs={{0,4},{1,5},{2,6},{3,7},{4,0},{5,1},{6,2},{7,3},{8,12},{9,13},{10,... | collective-permute-start | bytes 786440 | tf_op jit(solution)/shard_map/ppermute | solution.py:78
  110.4 20.5 %collective-permute-start.8 = (bf16[1024,128]{1,0:T(8,128)(2,1)S(1)}, bf16[1024,128]{1,0:T(8,128)(2,1)S(1)}, u32[]{:S(2)}, u32[]{:S(2)}) collective-permute-start(bf16[1024,128]{1,0:T(8,128)(2,1)S(1)} %gather_grad.13), channel_id=1, source_target_pairs={{0,2},{1,3},{2,0},{3,1},{4,6},{5,7},{6,4},{7,5},{8,10},{9,11},{10,... | collective-permute-start | bytes 786440 | tf_op jit(solution)/shard_map/ppermute | solution.py:78
  121.3 10.5 %all-to-all-start.5 = ((bf16[4,64,640]{2,1,0:T(8,128)(2,1)}), bf16[4,64,640]{2,1,0:T(8,128)(2,1)S(1)}, u32[]{:S(2)}, u32[]{:S(2)}) async-start(bf16[4,64,640]{2,1,0:T(8,128)(2,1)} %add_up.3), calls=%async_computation.5 | async-start | bytes 655360 | tf_op jit(solution)/shard_map/all_to_all | solution.py:67

commit v3 on v2

--- a/solution.py
+++ b/solution.py
@@ -26,14 +26,16 @@
     return 0.5 * jnp.tanh(0.5 * value) + 0.5
 
 
-def run(name, body, outs, args, smem=0, scratch=()):
+def run(name, body, outs, args, smem=0, hbm=0, scratch=()):
     outs = [jax.ShapeDtypeStruct(shape, dtype) for shape, dtype in outs]
     in_smem = pl.BlockSpec(memory_space=pltpu.SMEM)
+    in_hbm = pl.BlockSpec(memory_space=pltpu.HBM)
     in_vmem = pl.BlockSpec(memory_space=pltpu.VMEM)
+    places = [in_smem] * smem + [in_hbm] * hbm + [in_vmem] * (len(args) - smem - hbm)
     results = pl.pallas_call(
         body,
         out_shape=outs,
-        in_specs=[in_smem] * smem + [in_vmem] * (len(args) - smem),
+        in_specs=places,
         out_specs=[in_vmem] * len(outs),
         scratch_shapes=list(scratch),
         compiler_params=pltpu.CompilerParams(vmem_limit_bytes=VMEM_BYTES),
@@ -91,30 +93,35 @@
     length = item_row.shape[0]
 
     def body(*refs):
-        *in_refs, out_ref = refs
+        in_refs, out_ref, held, sems = refs[:4], refs[4], refs[5:9], refs[9]
+        moves = [pltpu.make_async_copy(in_refs[i], held[i], sems.at[i]) for i in range(4)]
+        for move in moves:
+            move.start()
+        for move in moves:
+            move.wait()
         for table in range(2):
-            owner, row = in_refs[2 * table : 2 * table + 2]
-            number = owner[...] * rows + row[...]
+            number = held[2 * table][...] * rows + held[2 * table + 1][...]
             for k in range(copies):
                 out_ref[k, table : table + 1, :] = number
 
     args = [a.reshape(1, length) for a in (item_owner, item_row, action_owner, action_row)]
-    return run("make_keys", body, [((copies, 2, length), I32)], args)[0]
-
-
-def fetch(cohorts, chunk, base, before=()):
+    scratch = [pltpu.VMEM((1, length), I32)] * 4 + [pltpu.SemaphoreType.DMA((4,))]
+    return run("make_keys", body, [((copies, 2, length), I32)], args, hbm=4, scratch=scratch)[0]
+
+
+def fetch(cohorts, chunk, base, blocks, before=()):
     many = len(cohorts)
     count, _, tokens, _ = cohorts[0].shape
     rows, cols = chunk.shape[0] // 2, chunk.shape[1]
 
-    def body(base_ref, chunk_ref, *refs):
+    def body(base_ref, block_ref, chunk_ref, *refs):
         key_refs, before_refs, out_refs = refs[:many], refs[many:-many], refs[-many:]
         lane = lax.broadcasted_iota(I32, (tokens, LANES), 1)
         for m in range(many):
             for k in range(count):
                 hot = []
                 for table in range(2):
-                    place = key_refs[m][k, table] - base_ref[0]
+                    place = key_refs[m][block_ref[k], table] - base_ref[0]
                     for start in range(0, rows, LANES):
                         hot.append(jnp.where(place == lane + start, 1.0, 0.0).astype(BF16))
                 found = dot(jnp.concatenate(hot, axis=1), chunk_ref[...])
@@ -126,26 +133,42 @@
         "fetch",
         body,
         [((count, tokens, cols), BF16)] * many,
-        [base.reshape(1), chunk, *cohorts, *before],
-        smem=1,
-    )
-
-
-def gather_grad(keys, pieces, base, rows, before=(), out=BF16):
-    count, _, tokens = keys.shape
-    cols = pieces.shape[-1]
-
-    def body(base_ref, key_ref, piece_ref, *refs):
-        *before_refs, out_ref = refs
-        piece = piece_ref[...].reshape(count * tokens, cols)
-        row = lax.broadcasted_iota(I32, (rows, tokens), 0)
+        [base.reshape(1), blocks, chunk, *cohorts, *before],
+        smem=2,
+    )
+
+
+def combine(parts):
+    count, *shape = parts[0].shape
+
+    def body(left_ref, right_ref, *out_refs):
+        for k in range(count):
+            total = left_ref[k].astype(F32) + right_ref[k].astype(F32)
+            out_refs[k][...] = total.astype(BF16)
+
+    return run("combine", body, [(tuple(shape), BF16)] * count, parts)
+
+
+def gather_grad(cohorts, tokens, base, blocks, rows, before=(), out=BF16):
+    many = len(cohorts)
+    count, _, length = cohorts[0].shape
+    cols = tokens[0].shape[-1]
+
+    def body(base_ref, block_ref, *refs):
+        key_refs, piece_refs = refs[:many], refs[many : 2 * many]
+        *before_refs, out_ref = refs[2 * many :]
+        row = lax.broadcasted_iota(I32, (rows, length), 0)
         for table in range(2):
             span = slice(table * rows, (table + 1) * rows)
-            hot = []
-            for k in range(count):
-                place = key_ref[k, table : table + 1, :] - base_ref[0]
-                hot.append(jnp.where(place == row, 1.0, 0.0).astype(BF16))
-            sums = dot(jnp.concatenate(hot, axis=1), piece)
+            sums = None
+            for m in range(many):
+                hot = []
+                for k in range(count):
+                    place = key_refs[m][block_ref[k], table : table + 1, :] - base_ref[0]
+                    hot.append(jnp.where(place == row, 1.0, 0.0).astype(BF16))
+                piece = piece_refs[m][...].reshape(count * length, cols)
+                part = dot(jnp.concatenate(hot, axis=1), piece)
+                sums = part if sums is None else sums + part
             for ref in before_refs:
                 sums = sums + ref[span, :].astype(F32)
             out_ref[span, :] = sums.astype(out)
@@ -154,13 +177,13 @@
         "gather_grad",
         body,
         [((2 * rows, cols), out)],
-        [base.reshape(1), keys, pieces, *before],
-        smem=1,
+        [base.reshape(1), blocks, *cohorts, *tokens, *before],
+        smem=2,
     )[0]
 
 
-def sequence(pieces, cotangent, gain, w_proj, w_out):
-    count = pieces.shape[0]
+def sequence(blocks, pieces, cotangent, gain, w_proj, w_out):
+    count = len(pieces)
     length, width = cotangent.shape
     cols = width // count
     head_dim = width // HEADS
@@ -168,12 +191,22 @@
     tile = min(256, length)
     step = min(256, 4 * width)
 
-    def body(piece_ref, cot_ref, gain_ref, wp_ref, wo_ref, *refs):
-        out_ref, grad_ref, normed_ref, dproj_ref, gated_ref = refs[:5]
-        emb, act, slope, att, attn, dscale, dkey, dval = refs[5:]
+    def body(block_ref, cot_in, wo_in, wp_in, gain_ref, *refs):
+        piece_refs, refs = refs[:count], refs[count:]
+        out_ref, *grad_refs = refs[: count + 1]
+        normed_ref, dproj_ref, gated_ref = refs[count + 1 : count + 4]
+        emb, act, slope, att, attn, dscale, dkey, dval, tok = refs[count + 4 : count + 13]
+        cot_ref, wo_ref, wp_ref, sems = refs[count + 13 :]
+        pairs = ((wp_in, wp_ref), (wo_in, wo_ref), (cot_in, cot_ref))
+        moves = [pltpu.make_async_copy(*pair, sems.at[i]) for i, pair in enumerate(pairs)]
+        for move in moves:
+            move.start()
+
+        def block(k):
+            return pl.ds(pl.multiple_of(block_ref[k] * cols, cols), cols)
 
         for k in range(count):
-            emb[:, k * cols : (k + 1) * cols] = piece_ref[k]
+            emb[:, block(k)] = piece_refs[k][...]
 
         def norm_of(value):
             centred = value - jnp.mean(value, axis=-1, keepdims=True)
@@ -193,6 +226,8 @@
             normed_ref[span, :] = (hat * gain_ref[...]).astype(BF16)
 
         normed = normed_ref[...]
+        for move in moves:
+            move.wait()
 
         @pl.loop(0, 4 * width // step)
         def _(j):
@@ -247,20 +282,24 @@
             hat, scale = norm_of(emb[span, :].astype(F32))
             upper = dot(dproj_ref[span, :], wp_ref[...], NT) * gain_ref[...]
             grad = cot_ref[span, :].astype(F32) + norm_back(upper, hat, scale)
-            for k in range(count):
-                grad_ref[k, span, :] = grad[:, k * cols : (k + 1) * cols].astype(BF16)
+            tok[span, :] = grad.astype(BF16)
+
+        for k in range(count):
+            grad_refs[k][...] = tok[:, block(k)]
 
     return run(
         "sequence",
         body,
         [
             ((length, width), BF16),
-            ((count, length, cols), BF16),
+            *[((length, cols), BF16)] * count,
             ((length, width), BF16),
             ((length, 4 * width), BF16),
             ((length, width), BF16),
         ],
-        [pieces, cotangent, gain, w_proj, w_out],
+        [blocks, cotangent, w_out, w_proj, gain, *pieces],
+        smem=1,
+        hbm=3,
         scratch=[
             pltpu.VMEM((length, width), BF16),
             pltpu.VMEM((length, 4 * width), BF16),
@@ -270,23 +309,30 @@
             pltpu.VMEM((HEADS, tile, length), F32),
             pltpu.VMEM((length, width), F32),
             pltpu.VMEM((length, width), F32),
+            pltpu.VMEM((length, width), BF16),
+            pltpu.VMEM((length, width), BF16),
+            pltpu.VMEM((width, width), BF16),
+            pltpu.VMEM((width, 4 * width), BF16),
+            pltpu.SemaphoreType.DMA((3,)),
         ],
     )
 
 
-def weight_grad(parity, normed, dproj, gated, cotangent, cores, line, blocks, before=()):
+def weight_grad(place, normed, dproj, gated, cotangent, cores, line, blocks, before=()):
     length, width = normed.shape
     rows = width // (cores * line)
     half = width // cores
     edge = dproj.shape[1]
     total = edge + cotangent.shape[1]
     cols = total // blocks
-
-    def body(parity_ref, n_ref, d_ref, g_ref, c_ref, *refs):
-        *before_refs, out_ref = refs
+    bits = blocks.bit_length() - 1
+    tall = half // bits
+
+    def body(place_ref, n_ref, d_ref, g_ref, c_ref, *refs):
+        before_refs, out_refs, scratch = refs[: len(before)], refs[len(before) : -1], refs[-1]
         feature = lax.broadcasted_iota(I32, (width, half), 0)
         column = lax.broadcasted_iota(I32, (width, half), 1)
-        wanted = (column // rows * cores + parity_ref[0]) * rows + column % rows
+        wanted = (column // rows * cores + place_ref[0]) * rows + column % rows
         pick = jnp.where(feature == wanted, 1.0, 0.0).astype(BF16)
         n_part = dot(n_ref[...], pick).astype(BF16)
         g_part = dot(g_ref[...], pick).astype(BF16)
@@ -298,47 +344,115 @@
             if last > edge:
                 parts.append(dot(g_part, c_ref[:, max(first, edge) - edge : last - edge], TN))
             sums = parts[0] if len(parts) == 1 else jnp.concatenate(parts, axis=1)
-            for ref in before_refs:
-                sums = sums + ref[k].astype(F32)
-            out_ref[k] = sums.astype(BF16)
-
+            if not before:
+                out_refs[0][k] = sums.astype(BF16)
+                continue
+            sums = sums + before_refs[0][k].astype(F32)
+            for p in range(bits):
+                at = sum((k >> (p + i) % bits & 1) << bits - 1 - i for i in range(bits))
+                scratch[p, at] = sums[p * tall : (p + 1) * tall]
+        if before:
+            for p in range(bits):
+                split_halves(scratch.at[p], place_ref[1 + p], out_refs[2 * p : 2 * p + 2])
+
+    outs = [((blocks, half, cols), BF16)]
+    if before:
+        kept = (blocks // 2, tall, cols)
+        outs = [(kept, F32), (kept, BF16)] * bits
     return run(
         "weight_grad",
         body,
-        [((blocks, half, cols), BF16)],
-        [parity.reshape(1), normed, dproj, gated, cotangent, *before],
+        outs,
+        [place, normed, dproj, gated, cotangent, *before],
         smem=1,
-    )[0]
-
-
-def add_up(parts, copies):
-    count, *shape = parts.shape
-
-    def body(part_ref, out_ref):
-        total = part_ref[0].astype(F32)
-        for k in range(1, count):
-            total = total + part_ref[k].astype(F32)
-        for k in range(copies):
-            out_ref[k] = total.astype(BF16)
-
-    return run("add_up", body, [((copies, *shape), BF16)], [parts])[0]
-
-
-def assemble(parts, edge):
-    count, rows, cols = parts.shape
-    total = cols * count
-
-    def body(part_ref, left_ref, right_ref):
+        scratch=[pltpu.VMEM((bits, blocks, tall, cols), F32)],
+    )
+
+
+def split_halves(ref, bit, out_refs):
+    count = ref.shape[0] // 2
+    for i, out_ref in enumerate(out_refs):
+        start = (bit ^ i) * count
         for k in range(count):
-            first, last = k * cols, (k + 1) * cols
-            part = part_ref[k].astype(F32)
-            cut = min(max(edge - first, 0), cols)
-            if cut > 0:
-                left_ref[:, first : first + cut] = part[:, :cut]
-            if cut < cols:
-                right_ref[:, first + cut - edge : last - edge] = part[:, cut:]
-
-    return run("assemble", body, [((rows, edge), F32), ((rows, total - edge), F32)], [parts])
+            out_ref[k] = ref[start + k].astype(out_ref.dtype)
+
+
+def fold(bits, kept, came):
+    count, tall, cols = kept[0].shape
+    many = len(kept)
+
+    def body(bit_ref, *refs):
+        kept_refs, came_refs, out_refs = refs[:many], refs[many : 2 * many], refs[2 * many : -1]
+        scratch = refs[-1]
+        for p in range(many):
+            for k in range(count):
+                scratch[p, k] = kept_refs[p][k] + came_refs[p][k].astype(F32)
+            split_halves(scratch.at[p], bit_ref[p], out_refs[2 * p : 2 * p + 2])
+
+    half = (count // 2, tall, cols)
+    return run(
+        "fold",
+        body,
+        [(half, F32), (half, BF16)] * many,
+        [bits, *kept, *came],
+        smem=1,
+        scratch=[pltpu.VMEM((many, count, tall, cols), F32)],
+    )
+
+
+def cut_line(planes, kept, came):
+    _, tall, cols = kept[0].shape
+    many, line = len(kept), planes.shape[0]
+    rows = many * tall // line
+
+    def body(plane_ref, *refs):
+        kept_refs, came_refs, out_refs = refs[:many], refs[many : 2 * many], refs[2 * many : -1]
+        scratch = refs[-1]
+        for p in range(many):
+            scratch[p * tall : (p + 1) * tall] = kept_refs[p][0] + came_refs[p][0].astype(F32)
+        for k in range(line):
+            span = pl.ds(pl.multiple_of(plane_ref[k] * rows, rows), rows)
+            out_refs[k][...] = scratch[span].astype(out_refs[k].dtype)
+
+    return run(
+        "cut_line",
+        body,
+        [((rows, cols), F32)] + [((rows, cols), BF16)] * (line - 1),
+        [planes, *kept, *came],
+        smem=1,
+        scratch=[pltpu.VMEM((many * tall, cols), F32)],
+    )
+
+
+def add_up(parts):
+    def body(*refs):
+        total = refs[0][...].astype(F32)
+        for ref in refs[1:-1]:
+            total = total + ref[...].astype(F32)
+        refs[-1][...] = total.astype(BF16)
+
+    return run("add_up", body, [(parts[0].shape, BF16)], parts)[0]
+
+
+def assemble(blocks, parts, edge):
+    rows, cols = parts[0].shape
+    total = cols * len(parts)
+
+    def body(block_ref, *refs):
+        part_refs, (left_ref, right_ref, held) = refs[: len(parts)], refs[len(parts) :]
+        for k, ref in enumerate(part_refs):
+            held[:, pl.ds(pl.multiple_of(block_ref[k] * cols, cols), cols)] = ref[...].astype(F32)
+        left_ref[...] = held[:, :edge]
+        right_ref[...] = held[:, edge:]
+
+    return run(
+        "assemble",
+        body,
+        [((rows, edge), F32), ((rows, total - edge), F32)],
+        [blocks, *parts],
+        smem=1,
+        scratch=[pltpu.VMEM((rows, total), F32)],
+    )
 
 
 def local(
@@ -377,43 +491,60 @@
         cohorts.append(grid.over_pair(cohorts[0]))
     key_cols = [jnp.broadcast_to(k[..., None], (*k.shape, LANES)) for k in cohorts]
 
+    blocks = jnp.stack([grid.replica_peer(k) for k in range(replicas)]).astype(I32)
+    planes = jnp.stack([grid.line_peer(k) for k in range(line)]).astype(I32)
+    bits = replicas.bit_length() - 1
+    swaps = [3, 1, 2] if replicas == 4 else list(range(1, replicas))
+
     found = ()
     for k in range(line - 1):
-        found = fetch(key_cols, held[k], bases[k], found)
+        found = fetch(key_cols, held[k], bases[k], blocks, found)
     found = [
-        fetch(key_cols[m : m + 1], held[-1], bases[-1], found[m : m + 1])[0] for m in range(cores)
+        fetch(key_cols[m : m + 1], held[-1], bases[-1], blocks, found[m : m + 1])[0]
+        for m in range(cores)
     ]
-    pieces = found[0]
-    for part in found[1:]:
-        pieces = (pieces.astype(F32) + grid.over_pair(part).astype(F32)).astype(BF16)
-    pieces = grid.swap_replica(pieces)
-
-    layer_out, tokens, normed, dproj, gated = sequence(
-        pieces, cotangent, input_norm_gain.reshape(1, width), w_proj, w_out
-    )
-    tokens = grid.swap_replica(tokens)
+    pieces = combine([found[0], grid.over_pair(found[1])])
+    for k in swaps:
+        pieces[k] = grid.over_replica(pieces[k], k)
+
+    layer_out, *rest = sequence(
+        blocks, pieces, cotangent, input_norm_gain.reshape(1, width), w_proj, w_out
+    )
+    tokens, (normed, dproj, gated) = rest[:replicas], rest[replicas:]
+    for k in swaps:
+        tokens[k] = grid.over_replica(tokens[k], k)
 
     def weights_of(m, before=()):
-        parity = ((grid.c + m) % cores).astype(I32)
-        return weight_grad(
-            parity, normed, dproj, gated, cotangent, cores, line, replicas, before
-        )
-
-    parts = weights_of(0, [grid.over_pair(weights_of(m)) for m in range(1, cores)])
-    parts = grid.swap_replica(parts)
-    parts = add_up(parts, 1).reshape(line, width // grid.shards, parts.shape[-1])
-    parts = grid.swap_line(parts)
-    parts = grid.swap_replica(add_up(parts, replicas))
-    grad_proj, grad_out = assemble(parts, 4 * width)
-
-    tokens = [tokens] + [grid.over_pair(tokens)] * (cores - 1)
-    table_grad = None
-    for k in range(line - 1, -1, -1):
-        total = ()
-        for key, token in zip(cohorts, tokens):
-            total = [gather_grad(key, token, bases[k], rows, total)]
-        total = (grid.over_line(total[0], k) if k else total[0]).astype(F32)
-        table_grad = total if table_grad is None else table_grad + total
+        place = [(grid.c + m) % cores] + [grid.r >> p & 1 for p in range(bits)]
+        place = jnp.stack(place).astype(I32)
+        args = (place, normed, dproj, gated, cotangent, cores, line, replicas, before)
+        return weight_grad(*args)
+
+    weights = weights_of(0, [grid.over_pair(weights_of(1)[0])])
+    tokens, weights = lax.optimization_barrier((tokens, weights))
+    tokens = jnp.stack(tokens)
+    there = grid.over_pair(tokens)
+    first = gather_grad(cohorts[:1], [tokens], bases[-1], blocks, rows)
+
+    sums = {line - 1: gather_grad(cohorts[1:], [there], bases[-1], blocks, rows, [first])}
+    for k in range(line - 2, -1, -1):
+        out = BF16 if k else F32
+        sums[k] = gather_grad(cohorts, [tokens, there], bases[k], blocks, rows, out=out)
+    table_grad = sums[0]
+    for k in range(line - 1, 0, -1):
+        table_grad = table_grad + grid.over_line(sums[k], k).astype(F32)
+
+    for step in range(bits):
+        kept, sent = weights[0::2], weights[1::2]
+        came = [grid.over_replica(sent[p], 1 << (p + step) % bits) for p in range(bits)]
+        if step < bits - 1:
+            turn = jnp.stack([grid.r >> (p + step + 1) % bits & 1 for p in range(bits)])
+            weights = fold(turn.astype(I32), kept, came)
+    parts = cut_line(planes, kept, came)
+    parts = [parts[0]] + [grid.over_line(parts[k], k) for k in range(1, line)]
+    total = add_up(parts)
+    parts = [total] + [grid.over_replica(total, k) for k in range(1, replicas)]
+    grad_proj, grad_out = assemble(blocks, parts, 4 * width)
 
     return layer_out, table_grad[:rows], table_grad[rows:], grad_proj, grad_out
 

time: 133 us -> 142 us (1.068)
  Pallas kernels: 38.1 us -> 46.9 us
  blocking collectives: 8.44 us -> 0 us
  waiting for transfers between devices: 43.3 us -> 47.8 us
  starting transfers between devices: 29.3 us -> 31.5 us
    ppermute x0 -> x13, waiting for transfers between devices: none -> 24.7 us  [over_replica(): lax.ppermute(value, 'replica', [(i, self.peer(i, n, step)) for i in range...]
    all_to_all x4 -> x1, waiting for transfers between devices: 27.8 us -> 4.71 us  [swap_replica(): lax.all_to_all(value, 'replica', split_axis=0, concat_axis=0, tiled=True)]
    ppermute x0 -> x13, starting transfers between devices: none -> 12.6 us  [over_replica(): lax.ppermute(value, 'replica', [(i, self.peer(i, n, step)) for i in range...]
    ppermute x6 -> x9, waiting for transfers between devices: 6.61 us -> 17.3 us  [over_line(): return lax.ppermute(value, 'sparse', pairs)]
    all_to_all x4 -> x1, starting transfers between devices: 14.2 us -> 3.95 us  [swap_replica(): lax.all_to_all(value, 'replica', split_axis=0, concat_axis=0, tiled=True)]
    pallas_call x20 -> x19, Pallas kernels: 38.1 us -> 46.9 us  [run(): pl.pallas_call(body, out_shape=outs, in_specs=places, out_specs=[in_vmem]...]
    all_to_all x1 -> x0, blocking collectives: 8.44 us -> none  [swap_replica(): lax.all_to_all(value, 'replica', split_axis=0, concat_axis=0, tiled=True)]
    all_to_all x1 -> x0, waiting for transfers between devices: 7.05 us -> none  [swap_line(): lax.all_to_all(value, 'sparse', split_axis=0, concat_axis=0, axis_index_g...]
  transfers between devices with their start and end apart: 15 -> 27, of which waited for: 8 -> 12; matrix products, arithmetic and copies ran while one was open for 2% -> 2% of each run, Pallas kernels for 17% -> 21%
where the time goes in v3:
time: 142 us; the launch traced here: 141 us
  waiting for transfers between devices  47.8 us (34%)
  Pallas kernels  46.9 us (33%)
  starting transfers between devices  31.5 us (22%)
  local copies, waits for them, and re-layouts  12.6 us (9%)
  other arithmetic  1.49 us (1%)
    pallas_call x19, Pallas kernels, run(): pl.pallas_call(body, out_shape=outs, in_specs=places, out_specs=[in_vmem]...  46.9 us
    ppermute x13, waiting for transfers between devices, over_replica(): lax.ppermute(value, 'replica', [(i, self.peer(i, n, step)) for i in range...  24.7 us
    ppermute x9, waiting for transfers between devices, over_line(): return lax.ppermute(value, 'sparse', pairs)  17.3 us
    ppermute x9, starting transfers between devices, over_line(): return lax.ppermute(value, 'sparse', pairs)  14.6 us
    ppermute x13, starting transfers between devices, over_replica(): lax.ppermute(value, 'replica', [(i, self.peer(i, n, step)) for i in range...  12.6 us
    unnamed x32, local copies, waits for them, and re-layouts  9.54 us
    all_to_all x1, waiting for transfers between devices, swap_replica(): lax.all_to_all(value, 'replica', split_axis=0, concat_axis=0, tiled=True)  4.71 us
    all_to_all x1, starting transfers between devices, swap_replica(): lax.all_to_all(value, 'replica', split_axis=0, concat_axis=0, tiled=True)  3.95 us
  transfers between devices with their start and end apart: 27, of which 12 were waited for; matrix products, arithmetic and copies ran while one was open for 2% of the time, Pallas kernels for 21%

profile of v3, /device:TPU:0, one launch (start us, length us, event | category | flops | bytes accessed | tf_op | source)
XLA Modules:
  0.0 141.1 jit_solution(14699043693983451546)
XLA Ops:
  0.6 1.0 constant_dynamic-slice_fusion
  1.7 3.1 %collective-permute-start.3 = (bf16[1024,128]{1,0:T(8,128)(2,1)S(1)}, bf16[1024,128]{1,0:T(8,128)(2,1)S(1)}, u32[]{:S(2)}, u32[]{:S(2)}) collective-permute-start(bf16[1024,128]{1,0:T(8,128)(2,1)S(1)} %pad_maximum_fusion.1.chunk_ref), channel_id=1, source_target_pairs={{0,2},{1,3},{2,0},{3,1},{4,6},{5,7},{6,4},{7,5},{8,10},{9,11},{10,... | collective-permute-start | bytes 786440 | tf_op jit(solution)/shard_map/ppermute | solution.py:80
  4.8 2.6 %collective-permute-start.1 = (bf16[1024,128]{1,0:T(8,128)(2,1)S(1)}, bf16[1024,128]{1,0:T(8,128)(2,1)S(1)}, u32[]{:S(2)}, u32[]{:S(2)}) collective-permute-start(bf16[1024,128]{1,0:T(8,128)(2,1)S(1)} %pad_maximum_fusion.1.chunk_ref), channel_id=1, source_target_pairs={{0,4},{1,5},{2,6},{3,7},{4,0},{5,1},{6,2},{7,3},{8,12},{9,13},{10,... | collective-permute-start | bytes 786440 | tf_op jit(solution)/shard_map/ppermute | solution.py:80
  7.3 0.7 copy-done.12
  8.0 0.7 copy-done.13
  8.7 0.7 copy-done.14
  9.4 0.7 copy-done.15
  10.1 0.7 make_keys.1
  10.7 3.9 %all-to-all-start = ((s32[4,2,512]{2,1,0:T(2,128)}), s32[4,2,512]{2,1,0:T(2,128)S(1)}, u32[]{:S(2)}, u32[]{:S(2)}) async-start(s32[4,2,512]{2,1,0:T(2,128)} %make_keys.1), calls=%async_computation | async-start | bytes 32768 | tf_op jit(solution)/shard_map/all_to_all | solution.py:69
  14.7 4.7 %all-to-all-done.refs_0_ = s32[4,2,512]{2,1,0:T(2,128)S(1)} async-done(((s32[4,2,512]{2,1,0:T(2,128)}), s32[4,2,512]{2,1,0:T(2,128)S(1)}, u32[]{:S(2)}, u32[]{:S(2)}) %all-to-all-start) | async-done | bytes 16416 | tf_op jit(solution)/shard_map/all_to_all | solution.py:69
  19.5 1.1 collective-permute-done.2.refs_1_.refs_0_
  20.6 0.6 broadcast_in_dim.5.refs_1_.refs_0_
  21.2 0.6 broadcast_in_dim.4.refs_0_
  21.8 2.9 %fetch.5 = (bf16[4,512,128]{2,1,0:T(8,128)(2,1)S(1)}, bf16[4,512,128]{2,1,0:T(8,128)(2,1)S(1)}) custom-call(s32[1]{0:T(128)} %bitcast.12.base_ref, s32[4]{0:T(128)S(1)} %pad_add_fusion.block_ref, bf16[1024,128]{1,0:T(8,128)(2,1)S(1)} %pad_maximum_fusion.1.chunk_ref, s32[4,2,512,128]{3,2,1,0:T(8,128)S(1)} %broadcast_in_dim.4.refs_0_, ...), custom_call_target="tpu_custom_call" | custom-call | tf_op jit(solution)/shard_map/fetch/pallas_call | solution.py:35
  24.7 2.9 %fetch.6 = (bf16[4,512,128]{2,1,0:T(8,128)(2,1)S(1)}, bf16[4,512,128]{2,1,0:T(8,128)(2,1)S(1)}) custom-call(s32[1]{0:T(128)} %bitcast.11.base_ref, s32[4]{0:T(128)S(1)} %pad_add_fusion.block_ref, bf16[1024,128]{1,0:T(8,128)(2,1)S(1)} %collective-permute-done.3.chunk_ref, s32[4,2,512,128]{3,2,1,0:T(8,128)S(1)} %broadcast_in_dim.4.refs_0_, ...), custom_call_target="tpu_custom_call" | custom-call | tf_op jit(solution)/shard_map/fetch/pallas_call | solution.py:35
  27.6 2.9 %fetch.7 = (bf16[4,512,128]{2,1,0:T(8,128)(2,1)S(1)}, bf16[4,512,128]{2,1,0:T(8,128)(2,1)S(1)}) custom-call(s32[1]{0:T(128)} %bitcast.10.base_ref, s32[4]{0:T(128)S(1)} %pad_add_fusion.block_ref, bf16[1024,128]{1,0:T(8,128)(2,1)S(1)} %collective-permute-done.1.chunk_ref, s32[4,2,512,128]{3,2,1,0:T(8,128)S(1)} %broadcast_in_dim.4.refs_0_, ...), custom_call_target="tpu_custom_call" | custom-call | tf_op jit(solution)/shard_map/fetch/pallas_call | solution.py:35
  30.5 1.8 %fetch.9 = bf16[4,512,128]{2,1,0:T(8,128)(2,1)S(1)} custom-call(s32[1]{0:T(128)} %bitcast.5.base_ref, s32[4]{0:T(128)S(1)} %pad_add_fusion.block_ref, bf16[1024,128]{1,0:T(8,128)(2,1)S(1)} %collective-permute-done.chunk_ref, s32[4,2,512,128]{3,2,1,0:T(8,128)S(1)} %broadcast_in_dim.5.refs_1_.refs_0_, bf16[4,512,128]{2,1,0:T(8,128)(2,1)S(1)} %get-tuple-element.50.refs_1_), custom_call_target="tpu_custom_call" | custom-call | tf_op jit(solution)/shard_map/fetch/pallas_call | solution.py:35
  32.5 1.8 %fetch.8.left_ref = bf16[4,512,128]{2,1,0:T(8,128)(2,1)S(1)} custom-call(s32[1]{0:T(128)} %bitcast.5.base_ref, s32[4]{0:T(128)S(1)} %pad_add_fusion.block_ref, bf16[1024,128]{1,0:T(8,128)(2,1)S(1)} %collective-permute-done.chunk_ref, s32[4,2,512,128]{3,2,1,0:T(8,128)S(1)} %broadcast_in_dim.4.refs_0_, bf16[4,512,128]{2,1,0:T(8,128)(2,1)S(1)} %get-tuple-element.49.refs_1_), custom_call_target="tpu_custom_call" | custom-call | tf_op jit(solution)/shard_map/fetch/pallas_call | solution.py:35
  34.4 0.7 collective-permute-start.5
  35.1 0.9 collective-permute-start.6
  36.0 2.0 %collective-permute-start.7 = (bf16[512,128]{1,0:T(8,128)(2,1)S(1)}, bf16[512,128]{1,0:T(8,128)(2,1)S(1)}, u32[]{:S(2)}, u32[]{:S(2)}) collective-permute-start(bf16[512,128]{1,0:T(8,128)(2,1)S(1)} %get-tuple-element.54), channel_id=1, source_target_pairs={{0,24},{8,16},{16,8},{24,0},{1,25},{9,17},{17,9},{25,1},{2,26},{10... | collective-permute-start | bytes 393224 | tf_op jit(solution)/shard_map/ppermute | solution.py:66
  38.1 2.7 %collective-permute-done.5.refs_1_ = bf16[512,128]{1,0:T(8,128)(2,1)S(1)} collective-permute-done((bf16[512,128]{1,0:T(8,128)(2,1)S(1)}, bf16[512,128]{1,0:T(8,128)(2,1)S(1)}, u32[]{:S(2)}, u32[]{:S(2)}) %collective-permute-start.5) | collective-permute-done | bytes 131104 | tf_op jit(solution)/shard_map/ppermute | solution.py:66
  40.8 2.5 %collective-permute-done.6.refs_2_ = bf16[512,128]{1,0:T(8,128)(2,1)S(1)} collective-permute-done((bf16[512,128]{1,0:T(8,128)(2,1)S(1)}, bf16[512,128]{1,0:T(8,128)(2,1)S(1)}, u32[]{:S(2)}, u32[]{:S(2)}) %collective-permute-start.6) | collective-permute-done | bytes 131104 | tf_op jit(solution)/shard_map/ppermute | solution.py:66
  43.4 0.7 copy-done.5
  44.0 0.7 copy-done.7
  44.7 1.6 %copy-done.3 = bf16[512,2048]{1,0:T(8,128)(2,1)S(1)} copy-done((bf16[512,2048]{1,0:T(8,128)(2,1)S(1)}, bf16[512,2048]{1,0:T(8,128)(2,1)}, u32[]{:S(2)}) %copy-start.3) | copy-done | bytes 2097176
  46.3 1.0 copy-done.4
  47.3 0.9 copy-done.6
  48.2 0.9 copy-done.8
  49.1 12.7 %sequence.1 = (bf16[512,512]{1,0:T(8,128)(2,1)}, bf16[512,128]{1,0:T(8,128)(2,1)S(1)}, bf16[512,128]{1,0:T(8,128)(2,1)}, bf16[512,128]{1,0:T(8,128)(2,1)}, bf16[...) custom-call(s32[4]{0:T(128)S(1)} %pad_add_fusion.block_ref, ...), custom_call_target="tpu_custom_call" | custom-call | tf_op jit(solution)/shard_map/sequence/pallas_call | solution.py:35
  61.8 3.1 %weight_grad.2 = bf16[4,256,640]{2,1,0:T(8,128)(2,1)} custom-call(s32[3]{0:T(128)S(1)} %add_add_fusion.1.place_ref, bf16[512,512]{1,0:T(8,128)(2,1)S(1)} %get-tuple-element.60.n_ref, bf16[512,2048]{1,0:T(8,128)(2,1)S(1)} %get-tuple-element.61.d_ref, bf16[512,512]{1,0:T(8,128)(2,1)S(1)} %get-tuple-element.62.g_ref, bf16[512,512]{1,0:T(8,128)(2,1)S(1)} %copy-done), custom_call_target="tpu_custom_call" | custom-call | tf_op jit(solution)/shard_map/weight_grad/pallas_call | solution.py:35
  64.9 1.5 %collective-permute-start.8 = (bf16[512,128]{1,0:T(8,128)(2,1)}, bf16[512,128]{1,0:T(8,128)(2,1)S(1)}, u32[]{:S(2)}, u32[]{:S(2)}) collective-permute-start(bf16[512,128]{1,0:T(8,128)(2,1)} %get-tuple-element.57), channel_id=1, source_target_pairs={{0,8},{8,0},{16,24},{24,16},{1,9},{9,1},{17,25},{25,17},{2,10},{10... | collective-permute-start | bytes 393224 | tf_op jit(solution)/shard_map/ppermute | solution.py:66
  66.4 0.6 collective-permute-start.9
  67.0 1.5 %collective-permute-start.10 = (bf16[512,128]{1,0:T(8,128)(2,1)}, bf16[512,128]{1,0:T(8,128)(2,1)}, u32[]{:S(2)}, u32[]{:S(2)}) collective-permute-start(bf16[512,128]{1,0:T(8,128)(2,1)} %get-tuple-element.59), channel_id=1, source_target_pairs={{0,24},{8,16},{16,8},{24,0},{1,25},{9,17},{17,9},{25,1},{2,26},{10... | collective-permute-start | bytes 393224 | tf_op jit(solution)/shard_map/ppermute | solution.py:66
  68.5 1.0 copy-done.2
  69.6 2.9 %weight_grad.3 = (f32[2,128,640]{2,1,0:T(8,128)S(1)}, bf16[2,128,640]{2,1,0:T(8,128)(2,1)S(1)}, f32[2,128,640]{2,1,0:T(8,128)S(1)}, bf16[2,128,640]{2,1,0:T(8,128)(2,1)S(1)}) custom-call(s32[3]{0:T(128)S(1)} %add_add_fusion.place_ref, bf16[512,512]{1,0:T(8,128)(2,1)S(1)} %get-tuple-element.60.n_ref, bf16[512,2048]{1,0:T(8,128)(2,1)S(1)} %get-tuple-element.61.d_ref, ...), custom_call_target="tpu_custom_call" | custom-call | tf_op jit(solution)/shard_map/weight_grad/pallas_call | solution.py:35
  72.5 2.5 %collective-permute-done.9 = bf16[512,128]{1,0:T(8,128)(2,1)S(1)} collective-permute-done((bf16[512,128]{1,0:T(8,128)(2,1)}, bf16[512,128]{1,0:T(8,128)(2,1)S(1)}, u32[]{:S(2)}, u32[]{:S(2)}) %collective-permute-start.9) | collective-permute-done | bytes 131104 | tf_op jit(solution)/shard_map/ppermute | solution.py:66
  75.0 0.6 collective-permute-start.16
  75.6 1.3 collective-permute-start.17
  76.8 1.0 pad_maximum_fusion.refs_2_.refs_1_
  78.0 6.0 %collective-permute-done.16.refs_2_ = bf16[2,128,640]{2,1,0:T(8,128)(2,1)S(1)} collective-permute-done((bf16[2,128,640]{2,1,0:T(8,128)(2,1)S(1)}, bf16[2,128,640]{2,1,0:T(8,128)(2,1)S(1)}, u32[]{:S(2)}, u32[]{:S(2)}) %collective-permute-start.16) | collective-permute-done | bytes 327712 | tf_op jit(solution)/shard_map/ppermute | solution.py:66
  83.9 0.5 collective-permute-done.17.refs_3_
  84.4 0.8 fold.1
  85.2 1.5 %collective-permute-start.18 = (bf16[1,128,640]{2,1,0:T(8,128)(2,1)S(1)}, bf16[1,128,640]{2,1,0:T(8,128)(2,1)S(1)}, u32[]{:S(2)}, u32[]{:S(2)}) collective-permute-start(bf16[1,128,640]{2,1,0:T(8,128)(2,1)S(1)} %get-tuple-element.77), channel_id=1, source_target_pairs={{0,16},{8,24},{16,0},{24,8},{1,17},{9,25},{17,1},{25,9},{2,18},{10... | collective-permute-start | bytes 491528 | tf_op jit(solution)/shard_map/ppermute | solution.py:66
  87.2 3.4 %collective-permute-done.18.refs_2_ = bf16[1,128,640]{2,1,0:T(8,128)(2,1)S(1)} collective-permute-done((bf16[1,128,640]{2,1,0:T(8,128)(2,1)S(1)}, bf16[1,128,640]{2,1,0:T(8,128)(2,1)S(1)}, u32[]{:S(2)}, u32[]{:S(2)}) %collective-permute-start.18) | collective-permute-done | bytes 163872 | tf_op jit(solution)/shard_map/ppermute | solution.py:66
  90.6 1.4 collective-permute-done.19.refs_3_
  92.0 0.6 cut_line.1
  92.6 1.3 collective-permute-start.20
  94.0 1.8 %gather_grad.6.refs_2_ = bf16[1024,128]{1,0:T(8,128)(2,1)S(1)} custom-call(s32[1]{0:T(128)} %bitcast.5.base_ref, s32[4]{0:T(128)S(1)} %pad_add_fusion.block_ref, s32[4,2,512]{2,1,0:T(2,128)S(1)} %all-to-all-done.refs_0_, bf16[4,512,128]{2,1,0:T(8,128)(2,1)S(1)} %pad_maximum_fusion.refs_2_.refs_1_), custom_call_target="tpu_custom_call" | custom-call | tf_op jit(solution)/shard_map/gather_grad/pallas_call | solution.py:35
  95.8 3.1 %gather_grad.8 = bf16[1024,128]{1,0:T(8,128)(2,1)S(1)} custom-call(s32[1]{0:T(128)} %bitcast.10.base_ref, s32[4]{0:T(128)S(1)} %pad_add_fusion.block_ref, s32[4,2,512]{2,1,0:T(2,128)S(1)} %all-to-all-done.refs_0_, s32[4,2,512]{2,1,0:T(2,128)S(1)} %collective-permute-done.2.refs_1_.refs_0_, bf16[4,512,128]{2,1,0:T(8,128)(2,1)S(1)} %pad_maximum_fusion.refs_2_.refs_1_, ...), custom_call_target="tpu_custom_call" | custom-call | tf_op jit(solution)/shard_map/gather_grad/pallas_call | solution.py:35
  98.8 2.9 %collective-permute-start.14 = (bf16[1024,128]{1,0:T(8,128)(2,1)S(1)}, bf16[1024,128]{1,0:T(8,128)(2,1)S(1)}, u32[]{:S(2)}, u32[]{:S(2)}) collective-permute-start(bf16[1024,128]{1,0:T(8,128)(2,1)S(1)} %gather_grad.8), channel_id=1, source_target_pairs={{0,4},{1,5},{2,6},{3,7},{4,0},{5,1},{6,2},{7,3},{8,12},{9,13},{10,... | collective-permute-start | bytes 786440 | tf_op jit(solution)/shard_map/ppermute | solution.py:80
  101.8 2.9 %gather_grad.9 = bf16[1024,128]{1,0:T(8,128)(2,1)S(1)} custom-call(s32[1]{0:T(128)} %bitcast.11.base_ref, s32[4]{0:T(128)S(1)} %pad_add_fusion.block_ref, s32[4,2,512]{2,1,0:T(2,128)S(1)} %all-to-all-done.refs_0_, s32[4,2,512]{2,1,0:T(2,128)S(1)} %collective-permute-done.2.refs_1_.refs_0_, bf16[4,512,128]{2,1,0:T(8,128)(2,1)S(1)} %pad_maximum_fusion.refs_2_.refs_1_, ...), custom_call_target="tpu_custom_call" | custom-call | tf_op jit(solution)/shard_map/gather_grad/pallas_call | solution.py:35
  104.9 1.8 %gather_grad.7 = bf16[1024,128]{1,0:T(8,128)(2,1)S(1)} custom-call(s32[1]{0:T(128)} %bitcast.5.base_ref, s32[4]{0:T(128)S(1)} %pad_add_fusion.block_ref, s32[4,2,512]{2,1,0:T(2,128)S(1)} %collective-permute-done.2.refs_1_.refs_0_, bf16[4,512,128]{2,1,0:T(8,128)(2,1)S(1)} %collective-permute-done.12.refs_3_.refs_1_, bf16[1024,128]{1,0:T(8,128)(2,1)S(1)} %gather_grad.6.refs_2_), custom_call_target="tpu_custom_call" | custom-call | tf_op jit(solution)/shard_map/gather_grad/pallas_call | solution.py:35
  106.6 1.4 %collective-permute-start.13 = (bf16[1024,128]{1,0:T(8,128)(2,1)S(1)}, bf16[1024,128]{1,0:T(8,128)(2,1)S(1)}, u32[]{:S(2)}, u32[]{:S(2)}) collective-permute-start(bf16[1024,128]{1,0:T(8,128)(2,1)S(1)} %gather_grad.7), channel_id=1, source_target_pairs={{0,6},{1,7},{2,4},{3,5},{4,2},{5,3},{6,0},{7,1},{8,14},{9,15},{10,... | collective-permute-start | bytes 786440 | tf_op jit(solution)/shard_map/ppermute | solution.py:80
  108.1 2.0 %collective-permute-start.21 = (bf16[64,640]{1,0:T(8,128)(2,1)S(1)}, bf16[64,640]{1,0:T(8,128)(2,1)S(1)}, u32[]{:S(2)}, u32[]{:S(2)}) collective-permute-start(bf16[64,640]{1,0:T(8,128)(2,1)S(1)} %get-tuple-element.81), channel_id=1, source_target_pairs={{0,4},{1,5},{2,6},{3,7},{4,0},{5,1},{6,2},{7,3},{8,12},{9,13},{10,... | collective-permute-start | bytes 245768 | tf_op jit(solution)/shard_map/ppermute | solution.py:80
  110.1 1.0 collective-permute-start.22
  111.0 17.2 %collective-permute-done.21.refs_2_ = bf16[64,640]{1,0:T(8,128)(2,1)S(1)} collective-permute-done((bf16[64,640]{1,0:T(8,128)(2,1)S(1)}, bf16[64,640]{1,0:T(8,128)(2,1)S(1)}, u32[]{:S(2)}, u32[]{:S(2)}) %collective-permute-start.21) | collective-permute-done | bytes 81952 | tf_op jit(solution)/shard_map/ppermute | solution.py:80
  128.3 1.2 collective-permute-start.25
  129.6 0.5 collective-permute-start.24
  130.1 4.1 %collective-permute-done.25.refs_3_ = bf16[64,640]{1,0:T(8,128)(2,1)S(1)} collective-permute-done((bf16[64,640]{1,0:T(8,128)(2,1)S(1)}, bf16[64,640]{1,0:T(8,128)(2,1)S(1)}, u32[]{:S(2)}, u32[]{:S(2)}) %collective-permute-start.25) | collective-permute-done | bytes 81952 | tf_op jit(solution)/shard_map/ppermute | solution.py:66
  134.3 2.9 %gather_grad.5 = f32[1024,128]{1,0:T(8,128)S(1)} custom-call(s32[1]{0:T(128)} %bitcast.12.base_ref, s32[4]{0:T(128)S(1)} %pad_add_fusion.block_ref, s32[4,2,512]{2,1,0:T(2,128)S(1)} %all-to-all-done.refs_0_, s32[4,2,512]{2,1,0:T(2,128)S(1)} %collective-permute-done.2.refs_1_.refs_0_, bf16[4,512,128]{2,1,0:T(8,128)(2,1)S(1)} %pad_maximum_fusion.refs_2_.refs_1_, ...), custom_call_target="tpu_custom_call" | custom-call | tf_op jit(solution)/shard_map/gather_grad/pallas_call | solution.py:35
  137.1 1.6 %collective-permute-done.23.refs_1_ = bf16[64,640]{1,0:T(8,128)(2,1)S(1)} collective-permute-done((bf16[64,640]{1,0:T(8,128)(2,1)S(1)}, bf16[64,640]{1,0:T(8,128)(2,1)S(1)}, u32[]{:S(2)}, u32[]{:S(2)}) %collective-permute-start.23) | collective-permute-done | bytes 81952 | tf_op jit(solution)/shard_map/ppermute | solution.py:66
  138.7 1.5 %assemble.1 = (f32[64,2048]{1,0:T(8,128)}, f32[64,512]{1,0:T(8,128)}) custom-call(s32[4]{0:T(128)S(1)} %pad_add_fusion.block_ref, bf16[64,640]{1,0:T(8,128)(2,1)S(1)} %add_up.1.refs_0_, bf16[64,640]{1,0:T(8,128)(2,1)S(1)} %collective-permute-done.23.refs_1_, bf16[64,640]{1,0:T(8,128)(2,1)S(1)} %collective-permute-done.24.refs_2_, ...), custom_call_target="tpu_custom_call" | custom-call | tf_op jit(solution)/shard_map/assemble/pallas_call | solution.py:35
  140.3 0.8 fusion
  (53 shorter events, 1.7 us)
Async XLA Ops:
  1.7 23.0 %collective-permute-start.3 = (bf16[1024,128]{1,0:T(8,128)(2,1)S(1)}, bf16[1024,128]{1,0:T(8,128)(2,1)S(1)}, u32[]{:S(2)}, u32[]{:S(2)}) collective-permute-start(bf16[1024,128]{1,0:T(8,128)(2,1)S(1)} %pad_maximum_fusion.1.chunk_ref), channel_id=1, source_target_pairs={{0,2},{1,3},{2,0},{3,1},{4,6},{5,7},{6,4},{7,5},{8,10},{9,11},{10,... | collective-permute-start | bytes 786440 | tf_op jit(solution)/shard_map/ppermute | solution.py:80
  4.8 22.8 %collective-permute-start.1 = (bf16[1024,128]{1,0:T(8,128)(2,1)S(1)}, bf16[1024,128]{1,0:T(8,128)(2,1)S(1)}, u32[]{:S(2)}, u32[]{:S(2)}) collective-permute-start(bf16[1024,128]{1,0:T(8,128)(2,1)S(1)} %pad_maximum_fusion.1.chunk_ref), channel_id=1, source_target_pairs={{0,4},{1,5},{2,6},{3,7},{4,0},{5,1},{6,2},{7,3},{8,12},{9,13},{10,... | collective-permute-start | bytes 786440 | tf_op jit(solution)/shard_map/ppermute | solution.py:80
  7.3 23.1 %collective-permute-start = (bf16[1024,128]{1,0:T(8,128)(2,1)S(1)}, bf16[1024,128]{1,0:T(8,128)(2,1)S(1)}, u32[]{:S(2)}, u32[]{:S(2)}) collective-permute-start(bf16[1024,128]{1,0:T(8,128)(2,1)S(1)} %pad_maximum_fusion.1.chunk_ref), channel_id=1, source_target_pairs={{0,6},{1,7},{2,4},{3,5},{4,2},{5,3},{6,0},{7,1},{8,14},{9,15},{10,... | collective-permute-start | bytes 786440 | tf_op jit(solution)/shard_map/ppermute | solution.py:80
  7.3 0.7 copy-start.12
  8.0 0.7 copy-start.13
  8.7 0.7 copy-start.14
  9.4 0.7 copy-start.15
  10.7 8.7 %all-to-all-start = ((s32[4,2,512]{2,1,0:T(2,128)}), s32[4,2,512]{2,1,0:T(2,128)S(1)}, u32[]{:S(2)}, u32[]{:S(2)}) async-start(s32[4,2,512]{2,1,0:T(2,128)} %make_keys.1), calls=%async_computation | async-start | bytes 32768 | tf_op jit(solution)/shard_map/all_to_all | solution.py:69
  19.4 1.2 collective-permute-start.2
  32.3 2.0 %collective-permute-start.4 = (bf16[4,512,128]{2,1,0:T(8,128)(2,1)S(1)}, bf16[4,512,128]{2,1,0:T(8,128)(2,1)S(1)}, u32[]{:S(2)}, u32[]{:S(2)}) collective-permute-start(bf16[4,512,128]{2,1,0:T(8,128)(2,1)S(1)} %fetch.9), channel_id=1, source_target_pairs={{0,1},{1,0},{2,3},{3,2},{4,5},{5,4},{6,7},{7,6},{8,9},{9,8},{10,11... | collective-permute-start | bytes 1572872 | tf_op jit(solution)/shard_map/ppermute | solution.py:83
  32.5 12.2 %copy-start = (bf16[512,512]{1,0:T(8,128)(2,1)S(1)}, bf16[512,512]{1,0:T(8,128)(2,1)}, u32[]{:S(2)}) copy-start(bf16[512,512]{1,0:T(8,128)(2,1)} %c_ref.3) | copy-start | bytes 1572868
  32.5 12.2 %copy-start.11 = (f32[512]{0:T(512)S(1)}, f32[512]{0:T(512)}, u32[]{:S(2)}) copy-start(f32[512]{0:T(512)} %param.16) | copy-start | bytes 6148
  34.4 6.4 %collective-permute-start.5 = (bf16[512,128]{1,0:T(8,128)(2,1)S(1)}, bf16[512,128]{1,0:T(8,128)(2,1)S(1)}, u32[]{:S(2)}, u32[]{:S(2)}) collective-permute-start(bf16[512,128]{1,0:T(8,128)(2,1)S(1)} %get-tuple-element.52), channel_id=1, source_target_pairs={{0,8},{8,0},{16,24},{24,16},{1,9},{9,1},{17,25},{25,17},{2,10},{10... | collective-permute-start | bytes 393224 | tf_op jit(solution)/shard_map/ppermute | solution.py:66
  35.1 8.3 %collective-permute-start.6 = (bf16[512,128]{1,0:T(8,128)(2,1)S(1)}, bf16[512,128]{1,0:T(8,128)(2,1)S(1)}, u32[]{:S(2)}, u32[]{:S(2)}) collective-permute-start(bf16[512,128]{1,0:T(8,128)(2,1)S(1)} %get-tuple-element.53), channel_id=1, source_target_pairs={{0,16},{8,24},{16,0},{24,8},{1,17},{9,25},{17,1},{25,9},{2,18},{10... | collective-permute-start | bytes 393224 | tf_op jit(solution)/shard_map/ppermute | solution.py:66
  36.0 8.0 %collective-permute-start.7 = (bf16[512,128]{1,0:T(8,128)(2,1)S(1)}, bf16[512,128]{1,0:T(8,128)(2,1)S(1)}, u32[]{:S(2)}, u32[]{:S(2)}) collective-permute-start(bf16[512,128]{1,0:T(8,128)(2,1)S(1)} %get-tuple-element.54), channel_id=1, source_target_pairs={{0,24},{8,16},{16,8},{24,0},{1,25},{9,17},{17,9},{25,1},{2,26},{10... | collective-permute-start | bytes 393224 | tf_op jit(solution)/shard_map/ppermute | solution.py:66
  43.4 0.7 copy-start.5
  44.0 0.7 copy-start.7
  44.7 1.6 %copy-start.3 = (bf16[512,2048]{1,0:T(8,128)(2,1)S(1)}, bf16[512,2048]{1,0:T(8,128)(2,1)}, u32[]{:S(2)}) copy-start(bf16[512,2048]{1,0:T(8,128)(2,1)} %wp_in.1) | copy-start | bytes 6291460
  46.3 1.0 copy-start.4
  47.3 0.9 copy-start.6
  48.2 0.9 copy-start.8
  61.8 3.1 %copy-start.1 = (bf16[512,512]{1,0:T(8,128)(2,1)}, bf16[512,512]{1,0:T(8,128)(2,1)S(1)}, u32[]{:S(2)}) copy-start(bf16[512,512]{1,0:T(8,128)(2,1)S(1)} %get-tuple-element.62.g_ref) | copy-start | bytes 1572868
  61.8 3.1 %copy-start.9 = (bf16[512,128]{1,0:T(8,128)(2,1)}, bf16[512,128]{1,0:T(8,128)(2,1)S(1)}, u32[]{:S(2)}) copy-start(bf16[512,128]{1,0:T(8,128)(2,1)S(1)} %get-tuple-element.67) | copy-start | bytes 393220
  64.9 3.6 %collective-permute-start.11 = (bf16[4,256,640]{2,1,0:T(8,128)(2,1)}, bf16[4,256,640]{2,1,0:T(8,128)(2,1)}, u32[]{:S(2)}, u32[]{:S(2)}) collective-permute-start(bf16[4,256,640]{2,1,0:T(8,128)(2,1)} %weight_grad.2), channel_id=1, source_target_pairs={{0,1},{1,0},{2,3},{3,2},{4,5},{5,4},{6,7},{7,6},{8,9},{9,8},{10,11... | collective-permute-start | bytes 3932168 | tf_op jit(solution)/shard_map/ppermute | solution.py:83
  64.9 7.6 %collective-permute-start.8 = (bf16[512,128]{1,0:T(8,128)(2,1)}, bf16[512,128]{1,0:T(8,128)(2,1)S(1)}, u32[]{:S(2)}, u32[]{:S(2)}) collective-permute-start(bf16[512,128]{1,0:T(8,128)(2,1)} %get-tuple-element.57), channel_id=1, source_target_pairs={{0,8},{8,0},{16,24},{24,16},{1,9},{9,1},{17,25},{25,17},{2,10},{10... | collective-permute-start | bytes 393224 | tf_op jit(solution)/shard_map/ppermute | solution.py:66
  66.4 8.6 %collective-permute-start.9 = (bf16[512,128]{1,0:T(8,128)(2,1)}, bf16[512,128]{1,0:T(8,128)(2,1)S(1)}, u32[]{:S(2)}, u32[]{:S(2)}) collective-permute-start(bf16[512,128]{1,0:T(8,128)(2,1)} %get-tuple-element.58), channel_id=1, source_target_pairs={{0,16},{8,24},{16,0},{24,8},{1,17},{9,25},{17,1},{25,9},{2,18},{10... | collective-permute-start | bytes 393224 | tf_op jit(solution)/shard_map/ppermute | solution.py:66
  67.0 8.0 %collective-permute-start.10 = (bf16[512,128]{1,0:T(8,128)(2,1)}, bf16[512,128]{1,0:T(8,128)(2,1)}, u32[]{:S(2)}, u32[]{:S(2)}) collective-permute-start(bf16[512,128]{1,0:T(8,128)(2,1)} %get-tuple-element.59), channel_id=1, source_target_pairs={{0,24},{8,16},{16,8},{24,0},{1,25},{9,17},{17,9},{25,1},{2,26},{10... | collective-permute-start | bytes 393224 | tf_op jit(solution)/shard_map/ppermute | solution.py:66
  68.5 1.0 copy-start.2
  69.6 7.3 %copy-start.10 = (bf16[512,128]{1,0:T(8,128)(2,1)S(1)}, bf16[512,128]{1,0:T(8,128)(2,1)}, u32[]{:S(2)}) copy-start(bf16[512,128]{1,0:T(8,128)(2,1)} %copy-done.9) | copy-start | bytes 393220
  75.0 8.9 %collective-permute-start.16 = (bf16[2,128,640]{2,1,0:T(8,128)(2,1)S(1)}, bf16[2,128,640]{2,1,0:T(8,128)(2,1)S(1)}, u32[]{:S(2)}, u32[]{:S(2)}) collective-permute-start(bf16[2,128,640]{2,1,0:T(8,128)(2,1)S(1)} %get-tuple-element.73), channel_id=1, source_target_pairs={{0,8},{8,0},{16,24},{24,16},{1,9},{9,1},{17,25},{25,17},{2,10},{10... | collective-permute-start | bytes 983048 | tf_op jit(solution)/shard_map/ppermute | solution.py:66
  75.6 8.9 %collective-permute-start.17 = (bf16[2,128,640]{2,1,0:T(8,128)(2,1)S(1)}, bf16[2,128,640]{2,1,0:T(8,128)(2,1)S(1)}, u32[]{:S(2)}, u32[]{:S(2)}) collective-permute-start(bf16[2,128,640]{2,1,0:T(8,128)(2,1)S(1)} %get-tuple-element.74), channel_id=1, source_target_pairs={{0,16},{8,24},{16,0},{24,8},{1,17},{9,25},{17,1},{25,9},{2,18},{10... | collective-permute-start | bytes 983048 | tf_op jit(solution)/shard_map/ppermute | solution.py:66
  77.8 17.9 %collective-permute-start.12 = (bf16[4,512,128]{2,1,0:T(8,128)(2,1)S(1)}, bf16[4,512,128]{2,1,0:T(8,128)(2,1)S(1)}, u32[]{:S(2)}, u32[]{:S(2)}) collective-permute-start(bf16[4,512,128]{2,1,0:T(8,128)(2,1)S(1)} %pad_maximum_fusion.refs_2_.refs_1_), channel_id=1, source_target_pairs={{0,1},{1,0},{2,3},{3,2},{4,5},{5,4},{6,7},{7,6},{8,9},{9,8},{10,11... | collective-permute-start | bytes 1572872 | tf_op jit(solution)/shard_map/ppermute | solution.py:83
  85.2 5.4 %collective-permute-start.18 = (bf16[1,128,640]{2,1,0:T(8,128)(2,1)S(1)}, bf16[1,128,640]{2,1,0:T(8,128)(2,1)S(1)}, u32[]{:S(2)}, u32[]{:S(2)}) collective-permute-start(bf16[1,128,640]{2,1,0:T(8,128)(2,1)S(1)} %get-tuple-element.77), channel_id=1, source_target_pairs={{0,16},{8,24},{16,0},{24,8},{1,17},{9,25},{17,1},{25,9},{2,18},{10... | collective-permute-start | bytes 491528 | tf_op jit(solution)/shard_map/ppermute | solution.py:66
  86.6 5.3 %collective-permute-start.19 = (bf16[1,128,640]{2,1,0:T(8,128)(2,1)S(1)}, bf16[1,128,640]{2,1,0:T(8,128)(2,1)S(1)}, u32[]{:S(2)}, u32[]{:S(2)}) collective-permute-start(bf16[1,128,640]{2,1,0:T(8,128)(2,1)S(1)} %get-tuple-element.78), channel_id=1, source_target_pairs={{0,8},{8,0},{16,24},{24,16},{1,9},{9,1},{17,25},{25,17},{2,10},{10... | collective-permute-start | bytes 491528 | tf_op jit(solution)/shard_map/ppermute | solution.py:66
  92.6 17.4 %collective-permute-start.20 = (bf16[64,640]{1,0:T(8,128)(2,1)S(1)}, bf16[64,640]{1,0:T(8,128)(2,1)S(1)}, u32[]{:S(2)}, u32[]{:S(2)}) collective-permute-start(bf16[64,640]{1,0:T(8,128)(2,1)S(1)} %get-tuple-element.80), channel_id=1, source_target_pairs={{0,2},{1,3},{2,0},{3,1},{4,6},{5,7},{6,4},{7,5},{8,10},{9,11},{10,... | collective-permute-start | bytes 245768 | tf_op jit(solution)/shard_map/ppermute | solution.py:80
  98.8 41.3 %collective-permute-start.14 = (bf16[1024,128]{1,0:T(8,128)(2,1)S(1)}, bf16[1024,128]{1,0:T(8,128)(2,1)S(1)}, u32[]{:S(2)}, u32[]{:S(2)}) collective-permute-start(bf16[1024,128]{1,0:T(8,128)(2,1)S(1)} %gather_grad.8), channel_id=1, source_target_pairs={{0,4},{1,5},{2,6},{3,7},{4,0},{5,1},{6,2},{7,3},{8,12},{9,13},{10,... | collective-permute-start | bytes 786440 | tf_op jit(solution)/shard_map/ppermute | solution.py:80
  104.7 35.5 %collective-permute-start.15 = (bf16[1024,128]{1,0:T(8,128)(2,1)S(1)}, bf16[1024,128]{1,0:T(8,128)(2,1)S(1)}, u32[]{:S(2)}, u32[]{:S(2)}) collective-permute-start(bf16[1024,128]{1,0:T(8,128)(2,1)S(1)} %gather_grad.9), channel_id=1, source_target_pairs={{0,2},{1,3},{2,0},{3,1},{4,6},{5,7},{6,4},{7,5},{8,10},{9,11},{10,... | collective-permute-start | bytes 786440 | tf_op jit(solution)/shard_map/ppermute | solution.py:80
  106.6 33.5 %collective-permute-start.13 = (bf16[1024,128]{1,0:T(8,128)(2,1)S(1)}, bf16[1024,128]{1,0:T(8,128)(2,1)S(1)}, u32[]{:S(2)}, u32[]{:S(2)}) collective-permute-start(bf16[1024,128]{1,0:T(8,128)(2,1)S(1)} %gather_grad.7), channel_id=1, source_target_pairs={{0,6},{1,7},{2,4},{3,5},{4,2},{5,3},{6,0},{7,1},{8,14},{9,15},{10,... | collective-permute-start | bytes 786440 | tf_op jit(solution)/shard_map/ppermute | solution.py:80
  108.1 20.2 %collective-permute-start.21 = (bf16[64,640]{1,0:T(8,128)(2,1)S(1)}, bf16[64,640]{1,0:T(8,128)(2,1)S(1)}, u32[]{:S(2)}, u32[]{:S(2)}) collective-permute-start(bf16[64,640]{1,0:T(8,128)(2,1)S(1)} %get-tuple-element.81), channel_id=1, source_target_pairs={{0,4},{1,5},{2,6},{3,7},{4,0},{5,1},{6,2},{7,3},{8,12},{9,13},{10,... | collective-permute-start | bytes 245768 | tf_op jit(solution)/shard_map/ppermute | solution.py:80
  110.1 18.2 %collective-permute-start.22 = (bf16[64,640]{1,0:T(8,128)(2,1)S(1)}, bf16[64,640]{1,0:T(8,128)(2,1)S(1)}, u32[]{:S(2)}, u32[]{:S(2)}) collective-permute-start(bf16[64,640]{1,0:T(8,128)(2,1)S(1)} %get-tuple-element.82), channel_id=1, source_target_pairs={{0,6},{1,7},{2,4},{3,5},{4,2},{5,3},{6,0},{7,1},{8,14},{9,15},{10,... | collective-permute-start | bytes 245768 | tf_op jit(solution)/shard_map/ppermute | solution.py:80
  128.3 5.9 %collective-permute-start.25 = (bf16[64,640]{1,0:T(8,128)(2,1)S(1)}, bf16[64,640]{1,0:T(8,128)(2,1)S(1)}, u32[]{:S(2)}, u32[]{:S(2)}) collective-permute-start(bf16[64,640]{1,0:T(8,128)(2,1)S(1)} %add_up.1.refs_0_), channel_id=1, source_target_pairs={{0,24},{8,16},{16,8},{24,0},{1,25},{9,17},{17,9},{25,1},{2,26},{10... | collective-permute-start | bytes 245768 | tf_op jit(solution)/shard_map/ppermute | solution.py:66
  129.6 7.5 %collective-permute-start.24 = (bf16[64,640]{1,0:T(8,128)(2,1)S(1)}, bf16[64,640]{1,0:T(8,128)(2,1)S(1)}, u32[]{:S(2)}, u32[]{:S(2)}) collective-permute-start(bf16[64,640]{1,0:T(8,128)(2,1)S(1)} %add_up.1.refs_0_), channel_id=1, source_target_pairs={{0,16},{8,24},{16,0},{24,8},{1,17},{9,25},{17,1},{25,9},{2,18},{10... | collective-permute-start | bytes 245768 | tf_op jit(solution)/shard_map/ppermute | solution.py:66
  134.2 4.4 %collective-permute-start.23 = (bf16[64,640]{1,0:T(8,128)(2,1)S(1)}, bf16[64,640]{1,0:T(8,128)(2,1)S(1)}, u32[]{:S(2)}, u32[]{:S(2)}) collective-permute-start(bf16[64,640]{1,0:T(8,128)(2,1)S(1)} %add_up.1.refs_0_), channel_id=1, source_target_pairs={{0,8},{8,0},{16,24},{24,16},{1,9},{9,1},{17,25},{25,17},{2,10},{10... | collective-permute-start | bytes 245768 | tf_op jit(solution)/shard_map/ppermute | solution.py:66

commit v4 on v3

--- a/solution.py
+++ b/solution.py
@@ -11,7 +11,7 @@
 F32 = jnp.float32
 BF16 = jnp.bfloat16
 I32 = jnp.int32
-VMEM_BYTES = 32 * 1024 * 1024
+MIB = 1024 * 1024
 
 NN = ((1,), (0,))
 NT = ((1,), (1,))
@@ -26,19 +26,18 @@
     return 0.5 * jnp.tanh(0.5 * value) + 0.5
 
 
-def run(name, body, outs, args, smem=0, hbm=0, scratch=()):
+def run(name, body, outs, args, smem=0, scratch=(), vmem=16):
     outs = [jax.ShapeDtypeStruct(shape, dtype) for shape, dtype in outs]
     in_smem = pl.BlockSpec(memory_space=pltpu.SMEM)
-    in_hbm = pl.BlockSpec(memory_space=pltpu.HBM)
     in_vmem = pl.BlockSpec(memory_space=pltpu.VMEM)
-    places = [in_smem] * smem + [in_hbm] * hbm + [in_vmem] * (len(args) - smem - hbm)
+    places = [in_smem] * smem + [in_vmem] * (len(args) - smem)
     results = pl.pallas_call(
         body,
         out_shape=outs,
         in_specs=places,
         out_specs=[in_vmem] * len(outs),
         scratch_shapes=list(scratch),
-        compiler_params=pltpu.CompilerParams(vmem_limit_bytes=VMEM_BYTES),
+        compiler_params=pltpu.CompilerParams(vmem_limit_bytes=vmem * MIB),
         cost_estimate=pl.CostEstimate(flops=0, bytes_accessed=0, transcendentals=0),
         name=name,
     )(*args)
@@ -56,85 +55,44 @@
         self.z = self.s // self.cores
         self.c = self.s % self.cores
 
-    def peer(self, index, size, step):
-        if size & (size - 1) == 0:
-            return index ^ step
-        return (step - index) % size
-
     def over_replica(self, value, step):
         n = self.replicas
-        return lax.ppermute(value, "replica", [(i, self.peer(i, n, step)) for i in range(n)])
-
-    def swap_replica(self, value):
-        return lax.all_to_all(value, "replica", split_axis=0, concat_axis=0, tiled=True)
-
-    def swap_line(self, value):
-        groups = [list(range(c, self.shards, self.cores)) for c in range(self.cores)]
-        return lax.all_to_all(
-            value, "sparse", split_axis=0, concat_axis=0, axis_index_groups=groups, tiled=True
-        )
+        return lax.ppermute(value, "replica", [(i, i ^ step) for i in range(n)])
 
     def over_line(self, value, step):
-        n, c = self.line, self.cores
-        pairs = [(i, self.peer(i // c, n, step) * c + i % c) for i in range(n * c)]
+        pairs = [(i, i ^ step * self.cores) for i in range(self.shards)]
         return lax.ppermute(value, "sparse", pairs)
 
     def over_pair(self, value):
         return lax.ppermute(value, "sparse", [(i, i ^ 1) for i in range(self.shards)])
 
-    def replica_peer(self, step):
-        return self.peer(self.r, self.replicas, step)
-
-    def line_peer(self, step):
-        return self.peer(self.z, self.line, step)
-
-
-def make_keys(rows, item_owner, item_row, action_owner, action_row, copies):
-    length = item_row.shape[0]
-
-    def body(*refs):
-        in_refs, out_ref, held, sems = refs[:4], refs[4], refs[5:9], refs[9]
-        moves = [pltpu.make_async_copy(in_refs[i], held[i], sems.at[i]) for i in range(4)]
-        for move in moves:
-            move.start()
-        for move in moves:
-            move.wait()
-        for table in range(2):
-            number = held[2 * table][...] * rows + held[2 * table + 1][...]
-            for k in range(copies):
-                out_ref[k, table : table + 1, :] = number
-
-    args = [a.reshape(1, length) for a in (item_owner, item_row, action_owner, action_row)]
-    scratch = [pltpu.VMEM((1, length), I32)] * 4 + [pltpu.SemaphoreType.DMA((4,))]
-    return run("make_keys", body, [((copies, 2, length), I32)], args, hbm=4, scratch=scratch)[0]
-
-
-def fetch(cohorts, chunk, base, blocks, before=()):
+
+def fetch(keys, cohorts, chunk, base, before=()):
     many = len(cohorts)
-    count, _, tokens, _ = cohorts[0].shape
+    count, _, _, tokens, _ = keys.shape
     rows, cols = chunk.shape[0] // 2, chunk.shape[1]
 
-    def body(base_ref, block_ref, chunk_ref, *refs):
-        key_refs, before_refs, out_refs = refs[:many], refs[many:-many], refs[-many:]
+    def body(base_ref, chunk_ref, key_ref, *refs):
+        before_refs, out_refs = refs[:-many], refs[-many:]
         lane = lax.broadcasted_iota(I32, (tokens, LANES), 1)
-        for m in range(many):
+        for i, m in enumerate(cohorts):
             for k in range(count):
                 hot = []
                 for table in range(2):
-                    place = key_refs[m][block_ref[k], table] - base_ref[0]
+                    place = key_ref[k, m, table] - base_ref[0]
                     for start in range(0, rows, LANES):
                         hot.append(jnp.where(place == lane + start, 1.0, 0.0).astype(BF16))
                 found = dot(jnp.concatenate(hot, axis=1), chunk_ref[...])
                 if before_refs:
-                    found = found + before_refs[m][k].astype(F32)
-                out_refs[m][k] = found.astype(BF16)
+                    found = found + before_refs[i][k].astype(F32)
+                out_refs[i][k] = found.astype(BF16)
 
     return run(
         "fetch",
         body,
         [((count, tokens, cols), BF16)] * many,
-        [base.reshape(1), blocks, chunk, *cohorts, *before],
-        smem=2,
+        [base.reshape(1), chunk, keys, *before],
+        smem=1,
     )
 
 
@@ -149,24 +107,23 @@
     return run("combine", body, [(tuple(shape), BF16)] * count, parts)
 
 
-def gather_grad(cohorts, tokens, base, blocks, rows, before=(), out=BF16):
+def gather_grad(keys, cohorts, tokens, base, rows, before=(), out=BF16):
     many = len(cohorts)
-    count, _, length = cohorts[0].shape
+    count, _, _, length = keys.shape
     cols = tokens[0].shape[-1]
 
-    def body(base_ref, block_ref, *refs):
-        key_refs, piece_refs = refs[:many], refs[many : 2 * many]
-        *before_refs, out_ref = refs[2 * many :]
+    def body(base_ref, key_ref, *refs):
+        piece_refs, before_refs, out_ref = refs[:many], refs[many:-1], refs[-1]
         row = lax.broadcasted_iota(I32, (rows, length), 0)
         for table in range(2):
             span = slice(table * rows, (table + 1) * rows)
             sums = None
-            for m in range(many):
+            for i, m in enumerate(cohorts):
                 hot = []
                 for k in range(count):
-                    place = key_refs[m][block_ref[k], table : table + 1, :] - base_ref[0]
+                    place = key_ref[k, m, table : table + 1, :] - base_ref[0]
                     hot.append(jnp.where(place == row, 1.0, 0.0).astype(BF16))
-                piece = piece_refs[m][...].reshape(count * length, cols)
+                piece = piece_refs[i][...].reshape(count * length, cols)
                 part = dot(jnp.concatenate(hot, axis=1), piece)
                 sums = part if sums is None else sums + part
             for ref in before_refs:
@@ -177,8 +134,8 @@
         "gather_grad",
         body,
         [((2 * rows, cols), out)],
-        [base.reshape(1), blocks, *cohorts, *tokens, *before],
-        smem=2,
+        [base.reshape(1), keys, *tokens, *before],
+        smem=1,
     )[0]
 
 
@@ -191,16 +148,11 @@
     tile = min(256, length)
     step = min(256, 4 * width)
 
-    def body(block_ref, cot_in, wo_in, wp_in, gain_ref, *refs):
+    def body(block_ref, cot_ref, wo_ref, wp_ref, gain_ref, *refs):
         piece_refs, refs = refs[:count], refs[count:]
         out_ref, *grad_refs = refs[: count + 1]
         normed_ref, dproj_ref, gated_ref = refs[count + 1 : count + 4]
-        emb, act, slope, att, attn, dscale, dkey, dval, tok = refs[count + 4 : count + 13]
-        cot_ref, wo_ref, wp_ref, sems = refs[count + 13 :]
-        pairs = ((wp_in, wp_ref), (wo_in, wo_ref), (cot_in, cot_ref))
-        moves = [pltpu.make_async_copy(*pair, sems.at[i]) for i, pair in enumerate(pairs)]
-        for move in moves:
-            move.start()
+        emb, act, slope, att, attn, dscale, dkey, dval, tok = refs[count + 4 :]
 
         def block(k):
             return pl.ds(pl.multiple_of(block_ref[k] * cols, cols), cols)
@@ -226,8 +178,6 @@
             normed_ref[span, :] = (hat * gain_ref[...]).astype(BF16)
 
         normed = normed_ref[...]
-        for move in moves:
-            move.wait()
 
         @pl.loop(0, 4 * width // step)
         def _(j):
@@ -299,7 +249,7 @@
         ],
         [blocks, cotangent, w_out, w_proj, gain, *pieces],
         smem=1,
-        hbm=3,
+        vmem=24,
         scratch=[
             pltpu.VMEM((length, width), BF16),
             pltpu.VMEM((length, 4 * width), BF16),
@@ -310,10 +260,6 @@
             pltpu.VMEM((length, width), F32),
             pltpu.VMEM((length, width), F32),
             pltpu.VMEM((length, width), BF16),
-            pltpu.VMEM((length, width), BF16),
-            pltpu.VMEM((width, width), BF16),
-            pltpu.VMEM((width, 4 * width), BF16),
-            pltpu.SemaphoreType.DMA((3,)),
         ],
     )
 
@@ -472,8 +418,11 @@
     replicas, line, cores = grid.replicas, grid.line, grid.cores
     cols = width // replicas
 
-    def base_of(k):
-        return ((grid.line_peer(k) * cores + grid.c) * rows).astype(I32)
+    bits = replicas.bit_length() - 1
+    swaps = [3, 1, 2] if replicas == 4 else list(range(1, replicas))
+    blocks = jnp.stack([grid.r ^ k for k in range(replicas)]).astype(I32)
+    planes = jnp.stack([grid.z ^ k for k in range(line)]).astype(I32)
+    bases = [(((grid.z ^ k) * cores + grid.c) * rows).astype(I32) for k in range(line)]
 
     own = jnp.concatenate(
         [
@@ -482,28 +431,31 @@
         ],
         axis=0,
     )
-    keys = make_keys(rows, item_owner, item_row, action_owner, action_row, replicas)
-
-    held = [own] + [grid.over_line(own, k) for k in range(1, line)]
-    bases = [base_of(k) for k in range(line)]
-    cohorts = [grid.swap_replica(keys)]
-    if cores == 2:
-        cohorts.append(grid.over_pair(cohorts[0]))
-    key_cols = [jnp.broadcast_to(k[..., None], (*k.shape, LANES)) for k in cohorts]
-
-    blocks = jnp.stack([grid.replica_peer(k) for k in range(replicas)]).astype(I32)
-    planes = jnp.stack([grid.line_peer(k) for k in range(line)]).astype(I32)
-    bits = replicas.bit_length() - 1
-    swaps = [3, 1, 2] if replicas == 4 else list(range(1, replicas))
+    keys = jnp.stack(
+        [
+            (item_owner * rows + item_row[:, None])[:, 0],
+            (action_owner * rows + action_row[:, None])[:, 0],
+        ]
+    ).astype(I32)
+
+    held = {0: own}
+    for low in reversed([1 << i for i in range(line.bit_length() - 1)]):
+        for k in range(low, line, 2 * low):
+            held[k] = grid.over_line(held[k ^ low], low)
+    order = sorted(held, key=lambda k: (bin(k).count("1"), k))
+
+    keys = jnp.stack([keys, grid.over_pair(keys)])
+    keys = jnp.stack([keys] + [grid.over_replica(keys, k) for k in range(1, replicas)])
+    key_cols = jnp.broadcast_to(keys[..., None], (*keys.shape, LANES))
+    both = list(range(cores))
 
     found = ()
-    for k in range(line - 1):
-        found = fetch(key_cols, held[k], bases[k], blocks, found)
-    found = [
-        fetch(key_cols[m : m + 1], held[-1], bases[-1], blocks, found[m : m + 1])[0]
-        for m in range(cores)
-    ]
-    pieces = combine([found[0], grid.over_pair(found[1])])
+    for k in order[:-1]:
+        found = fetch(key_cols, both, held[k], bases[k], found)
+    last = order[-1]
+    there = fetch(key_cols, both[1:], held[last], bases[last], found[1:])
+    here = fetch(key_cols, both[:1], held[last], bases[last], found[:1])
+    pieces = combine([here[0], grid.over_pair(there[0])])
     for k in swaps:
         pieces[k] = grid.over_replica(pieces[k], k)
 
@@ -521,27 +473,36 @@
         return weight_grad(*args)
 
     weights = weights_of(0, [grid.over_pair(weights_of(1)[0])])
-    tokens, weights = lax.optimization_barrier((tokens, weights))
+    tokens = lax.optimization_barrier((tokens, weights))[0]
     tokens = jnp.stack(tokens)
     there = grid.over_pair(tokens)
-    first = gather_grad(cohorts[:1], [tokens], bases[-1], blocks, rows)
-
-    sums = {line - 1: gather_grad(cohorts[1:], [there], bases[-1], blocks, rows, [first])}
-    for k in range(line - 2, -1, -1):
-        out = BF16 if k else F32
-        sums[k] = gather_grad(cohorts, [tokens, there], bases[k], blocks, rows, out=out)
+
+    sums = {}
+    for k in reversed(order):
+        if k == last:
+            first = gather_grad(keys, both[:1], [tokens], bases[k], rows)
+            sums[k] = gather_grad(keys, both[1:], [there], bases[k], rows, [first])
+            continue
+        low = (k & -k) or line
+        steps = [1 << i for i in range(low.bit_length() - 1)]
+        out = F32 if steps else BF16
+        total = gather_grad(keys, both, [tokens, there], bases[k], rows, out=out)
+        for step in steps:
+            total = total + grid.over_line(sums[k ^ step], step).astype(F32)
+        sums[k] = total.astype(BF16) if k else total
     table_grad = sums[0]
-    for k in range(line - 1, 0, -1):
-        table_grad = table_grad + grid.over_line(sums[k], k).astype(F32)
 
     for step in range(bits):
         kept, sent = weights[0::2], weights[1::2]
         came = [grid.over_replica(sent[p], 1 << (p + step) % bits) for p in range(bits)]
+        after = sums[last] if step < bits - 1 else sums[line // 2]
+        came = lax.optimization_barrier((came, after))[0]
         if step < bits - 1:
             turn = jnp.stack([grid.r >> (p + step + 1) % bits & 1 for p in range(bits)])
             weights = fold(turn.astype(I32), kept, came)
     parts = cut_line(planes, kept, came)
     parts = [parts[0]] + [grid.over_line(parts[k], k) for k in range(1, line)]
+    parts = lax.optimization_barrier((parts, table_grad))[0]
     total = add_up(parts)
     parts = [total] + [grid.over_replica(total, k) for k in range(1, replicas)]
     grad_proj, grad_out = assemble(blocks, parts, 4 * width)

time: 142 us -> 123 us (0.87)
  waiting for transfers between devices: 47.8 us -> 32.3 us
  Pallas kernels: 46.9 us -> 40.7 us
  starting transfers between devices: 31.5 us -> 34.8 us
    ppermute x13 -> x16, waiting for transfers between devices: 24.7 us -> 15.7 us  [over_replica(): return lax.ppermute(value, 'replica', [(i, i ^ step) for i in range(n)])]
    pallas_call x19 -> x18, Pallas kernels: 46.9 us -> 40.7 us  [run(): pl.pallas_call(body, out_shape=outs, in_specs=places, out_specs=[in_vmem]...]
    ppermute x13 -> x16, starting transfers between devices: 12.6 us -> 17.9 us  [over_replica(): return lax.ppermute(value, 'replica', [(i, i ^ step) for i in range(n)])]
    all_to_all x1 -> x0, waiting for transfers between devices: 4.71 us -> none  [swap_replica(): lax.all_to_all(value, 'replica', split_axis=0, concat_axis=0, tiled=True)]
    all_to_all x1 -> x0, starting transfers between devices: 3.95 us -> none  [swap_replica(): lax.all_to_all(value, 'replica', split_axis=0, concat_axis=0, tiled=True)]
    ppermute x9, waiting for transfers between devices: 17.3 us -> 14.9 us  [over_line(): return lax.ppermute(value, 'sparse', pairs)]
    ppermute x9, starting transfers between devices: 14.6 us -> 16.7 us  [over_line(): return lax.ppermute(value, 'sparse', pairs)]
    unnamed x32 -> x28, local copies, waits for them, and re-layouts: 9.54 us -> 9 us
  transfers between devices with their start and end apart: 27 -> 29, of which waited for: 12 -> 17; matrix products, arithmetic and copies ran while one was open for 2% -> 3% of each run, Pallas kernels for 21% -> 17%
where the time goes in v4:
time: 123 us
  Pallas kernels  40.7 us (33%)
  starting transfers between devices  34.8 us (28%)
  waiting for transfers between devices  32.3 us (26%)
  local copies, waits for them, and re-layouts  12 us (10%)
  other arithmetic  2.27 us (2%)
    pallas_call x18, Pallas kernels, run(): pl.pallas_call(body, out_shape=outs, in_specs=places, out_specs=[in_vmem]...  40.7 us
    ppermute x16, starting transfers between devices, over_replica(): return lax.ppermute(value, 'replica', [(i, i ^ step) for i in range(n)])  17.9 us
    ppermute x9, starting transfers between devices, over_line(): return lax.ppermute(value, 'sparse', pairs)  16.7 us
    ppermute x16, waiting for transfers between devices, over_replica(): return lax.ppermute(value, 'replica', [(i, i ^ step) for i in range(n)])  15.7 us
    ppermute x9, waiting for transfers between devices, over_line(): return lax.ppermute(value, 'sparse', pairs)  14.9 us
    unnamed x28, local copies, waits for them, and re-layouts  9 us
  transfers between devices with their start and end apart: 29, of which 17 were waited for; matrix products, arithmetic and copies ran while one was open for 3% of the time, Pallas kernels for 17%

profile of v4, /device:TPU:0, one launch (start us, length us, event | category | flops | bytes accessed | tf_op | source)
XLA Modules:
  0.0 123.0 jit_solution(6295261326122036518)
XLA Ops:
  0.6 1.0 constant_dynamic-slice_fusion
  1.7 4.1 %collective-permute-start = (bf16[1024,128]{1,0:T(8,128)(2,1)S(1)}, bf16[1024,128]{1,0:T(8,128)(2,1)S(1)}, u32[]{:S(2)}, u32[]{:S(2)}) collective-permute-start(bf16[1024,128]{1,0:T(8,128)(2,1)S(1)} %pad_maximum_fusion.1.chunk_ref), channel_id=1, source_target_pairs={{0,4},{1,5},{2,6},{3,7},{4,0},{5,1},{6,2},{7,3},{8,12},{9,13},{10,... | collective-permute-start | bytes 786440 | tf_op jit(solution)/shard_map/ppermute | solution.py:64
  5.8 1.6 %collective-permute-start.6 = (bf16[1024,128]{1,0:T(8,128)(2,1)S(1)}, bf16[1024,128]{1,0:T(8,128)(2,1)S(1)}, u32[]{:S(2)}, u32[]{:S(2)}) collective-permute-start(bf16[1024,128]{1,0:T(8,128)(2,1)S(1)} %pad_maximum_fusion.1.chunk_ref), channel_id=1, source_target_pairs={{0,2},{1,3},{2,0},{3,1},{4,6},{5,7},{6,4},{7,5},{8,10},{9,11},{10,... | collective-permute-start | bytes 786440 | tf_op jit(solution)/shard_map/ppermute | solution.py:64
  7.3 0.7 add_bitcast_fusion
  8.1 9.7 %collective-permute-done.chunk_ref = bf16[1024,128]{1,0:T(8,128)(2,1)S(1)} collective-permute-done((bf16[1024,128]{1,0:T(8,128)(2,1)S(1)}, bf16[1024,128]{1,0:T(8,128)(2,1)S(1)}, u32[]{:S(2)}, u32[]{:S(2)}) %collective-permute-start) | collective-permute-done | bytes 262176 | tf_op jit(solution)/shard_map/ppermute | solution.py:64
  17.8 0.6 collective-permute-start.1
  18.5 1.2 collective-permute-done.2
  19.7 1.5 %collective-permute-start.4 = (s32[2,2,512]{2,1,0:T(2,128)S(1)}, s32[2,2,512]{2,1,0:T(2,128)S(1)}, u32[]{:S(2)}, u32[]{:S(2)}) collective-permute-start(s32[2,2,512]{2,1,0:T(2,128)S(1)} %get-tuple-element.96), channel_id=1, source_target_pairs={{0,16},{8,24},{16,0},{24,8},{1,17},{9,25},{17,1},{25,9},{2,18},{10... | collective-permute-start | bytes 24584 | tf_op jit(solution)/shard_map/ppermute | solution.py:60
  21.2 1.5 %collective-permute-start.3 = (s32[2,2,512]{2,1,0:T(2,128)S(1)}, s32[2,2,512]{2,1,0:T(2,128)S(1)}, u32[]{:S(2)}, u32[]{:S(2)}) collective-permute-start(s32[2,2,512]{2,1,0:T(2,128)S(1)} %get-tuple-element.96), channel_id=1, source_target_pairs={{0,8},{8,0},{16,24},{24,16},{1,9},{9,1},{17,25},{25,17},{2,10},{10... | collective-permute-start | bytes 24584 | tf_op jit(solution)/shard_map/ppermute | solution.py:60
  23.3 1.5 %collective-permute-done.3 = s32[2,2,512]{2,1,0:T(2,128)S(1)} collective-permute-done((s32[2,2,512]{2,1,0:T(2,128)S(1)}, s32[2,2,512]{2,1,0:T(2,128)S(1)}, u32[]{:S(2)}, u32[]{:S(2)}) %collective-permute-start.3) | collective-permute-done | bytes 8224 | tf_op jit(solution)/shard_map/ppermute | solution.py:60
  24.8 2.4 %collective-permute-done.5 = s32[2,2,512]{2,1,0:T(2,128)S(1)} collective-permute-done((s32[2,2,512]{2,1,0:T(2,128)S(1)}, s32[2,2,512]{2,1,0:T(2,128)S(1)}, u32[]{:S(2)}, u32[]{:S(2)}) %collective-permute-start.5) | collective-permute-done | bytes 8224 | tf_op jit(solution)/shard_map/ppermute | solution.py:60
  27.2 1.2 broadcast_in_dim.14.key_ref
  28.5 2.3 %fetch.5 = (bf16[4,512,128]{2,1,0:T(8,128)(2,1)S(1)}, bf16[4,512,128]{2,1,0:T(8,128)(2,1)S(1)}) custom-call(s32[1]{0:T(128)} %bitcast.18.base_ref, bf16[1024,128]{1,0:T(8,128)(2,1)S(1)} %pad_maximum_fusion.1.chunk_ref, s32[4,2,2,512,128]{4,3,2,1,0:T(8,128)S(1)} %broadcast_in_dim.14.key_ref), custom_call_target="tpu_custom_call" | custom-call | tf_op jit(solution)/shard_map/fetch/pallas_call | solution.py:34
  30.8 2.3 %fetch.6 = (bf16[4,512,128]{2,1,0:T(8,128)(2,1)S(1)}, bf16[4,512,128]{2,1,0:T(8,128)(2,1)S(1)}) custom-call(s32[1]{0:T(128)} %bitcast.17.base_ref, bf16[1024,128]{1,0:T(8,128)(2,1)S(1)} %collective-permute-done.6.chunk_ref, s32[4,2,2,512,128]{4,3,2,1,0:T(8,128)S(1)} %broadcast_in_dim.14.key_ref, bf16[4,512,128]{2,1,0:T(8,128)(2,1)S(1)} %get-tuple-element.49.refs_0_, ...), custom_call_target="tpu_custom_call" | custom-call | tf_op jit(solution)/shard_map/fetch/pallas_call | solution.py:34
  33.2 2.3 %fetch.7 = (bf16[4,512,128]{2,1,0:T(8,128)(2,1)S(1)}, bf16[4,512,128]{2,1,0:T(8,128)(2,1)S(1)}) custom-call(s32[1]{0:T(128)} %bitcast.16.base_ref, bf16[1024,128]{1,0:T(8,128)(2,1)S(1)} %collective-permute-done.chunk_ref, s32[4,2,2,512,128]{4,3,2,1,0:T(8,128)S(1)} %broadcast_in_dim.14.key_ref, bf16[4,512,128]{2,1,0:T(8,128)(2,1)S(1)} %get-tuple-element.51.refs_0_, ...), custom_call_target="tpu_custom_call" | custom-call | tf_op jit(solution)/shard_map/fetch/pallas_call | solution.py:34
  35.5 1.2 %fetch.9 = bf16[4,512,128]{2,1,0:T(8,128)(2,1)S(1)} custom-call(s32[1]{0:T(128)} %bitcast.5.base_ref, bf16[1024,128]{1,0:T(8,128)(2,1)S(1)} %collective-permute-done.1.chunk_ref, s32[4,2,2,512,128]{4,3,2,1,0:T(8,128)S(1)} %broadcast_in_dim.14.key_ref, bf16[4,512,128]{2,1,0:T(8,128)(2,1)S(1)} %get-tuple-element.54.refs_0_), custom_call_target="tpu_custom_call" | custom-call | tf_op jit(solution)/shard_map/fetch/pallas_call | solution.py:34
  36.9 2.2 %copy-done.1 = s32[4,2,2,512,128]{4,3,2,1,0:T(8,128)S(1)} copy-done((s32[4,2,2,512,128]{4,3,2,1,0:T(8,128)S(1)}, s32[4,2,2,512,128]{4,3,2,1,0:T(8,128)}, u32[]{:S(2)}) %copy-start.1) | copy-done | bytes 4194328
  39.1 1.2 %fetch.8.left_ref = bf16[4,512,128]{2,1,0:T(8,128)(2,1)S(1)} custom-call(s32[1]{0:T(128)} %bitcast.5.base_ref, bf16[1024,128]{1,0:T(8,128)(2,1)S(1)} %collective-permute-done.1.chunk_ref, s32[4,2,2,512,128]{4,3,2,1,0:T(8,128)S(1)} %copy-done.1, bf16[4,512,128]{2,1,0:T(8,128)(2,1)S(1)} %get-tuple-element.53.refs_0_), custom_call_target="tpu_custom_call" | custom-call | tf_op jit(solution)/shard_map/fetch/pallas_call | solution.py:34
  40.5 0.6 collective-permute-start.8
  41.1 0.5 collective-permute-start.9
  41.6 2.5 %collective-permute-start.10 = (bf16[512,128]{1,0:T(8,128)(2,1)S(1)}, bf16[512,128]{1,0:T(8,128)(2,1)S(1)}, u32[]{:S(2)}, u32[]{:S(2)}) collective-permute-start(bf16[512,128]{1,0:T(8,128)(2,1)S(1)} %get-tuple-element.58), channel_id=1, source_target_pairs={{0,24},{8,16},{16,8},{24,0},{1,25},{9,17},{17,9},{25,1},{2,26},{10... | collective-permute-start | bytes 393224 | tf_op jit(solution)/shard_map/ppermute | solution.py:60
  44.2 2.6 %collective-permute-done.8.refs_1_ = bf16[512,128]{1,0:T(8,128)(2,1)S(1)} collective-permute-done((bf16[512,128]{1,0:T(8,128)(2,1)S(1)}, bf16[512,128]{1,0:T(8,128)(2,1)S(1)}, u32[]{:S(2)}, u32[]{:S(2)}) %collective-permute-start.8) | collective-permute-done | bytes 131104 | tf_op jit(solution)/shard_map/ppermute | solution.py:60
  46.8 2.7 %collective-permute-done.9.refs_2_ = bf16[512,128]{1,0:T(8,128)(2,1)S(1)} collective-permute-done((bf16[512,128]{1,0:T(8,128)(2,1)S(1)}, bf16[512,128]{1,0:T(8,128)(2,1)S(1)}, u32[]{:S(2)}, u32[]{:S(2)}) %collective-permute-start.9) | collective-permute-done | bytes 131104 | tf_op jit(solution)/shard_map/ppermute | solution.py:60
  49.5 0.7 copy-done.7
  50.1 0.7 copy-done.9
  50.8 1.6 %copy-done.5 = bf16[512,2048]{1,0:T(8,128)(2,1)S(1)} copy-done((bf16[512,2048]{1,0:T(8,128)(2,1)S(1)}, bf16[512,2048]{1,0:T(8,128)(2,1)}, u32[]{:S(2)}) %copy-start.5) | copy-done | bytes 2097176
  52.4 1.0 copy-done.6
  53.4 0.9 copy-done.8
  54.4 0.9 copy-done.10
  55.3 12.5 %sequence.1 = (bf16[512,512]{1,0:T(8,128)(2,1)}, bf16[512,128]{1,0:T(8,128)(2,1)S(1)}, bf16[512,128]{1,0:T(8,128)(2,1)}, bf16[512,128]{1,0:T(8,128)(2,1)}, bf16[...) custom-call(s32[4]{0:T(128)S(1)} %pad_add_fusion.3.block_ref, ...), custom_call_target="tpu_custom_call" | custom-call | tf_op jit(solution)/shard_map/sequence/pallas_call | solution.py:34
  67.7 3.1 %weight_grad.2 = bf16[4,256,640]{2,1,0:T(8,128)(2,1)} custom-call(s32[3]{0:T(128)S(1)} %add_add_fusion.1.place_ref, bf16[512,512]{1,0:T(8,128)(2,1)S(1)} %get-tuple-element.64.n_ref, bf16[512,2048]{1,0:T(8,128)(2,1)S(1)} %get-tuple-element.65.d_ref, bf16[512,512]{1,0:T(8,128)(2,1)S(1)} %get-tuple-element.66.g_ref, bf16[512,512]{1,0:T(8,128)(2,1)S(1)} %copy-done.2), custom_call_target="tpu_custom_call" | custom-call | tf_op jit(solution)/shard_map/weight_grad/pallas_call | solution.py:34
  70.8 1.6 %collective-permute-start.11 = (bf16[512,128]{1,0:T(8,128)(2,1)}, bf16[512,128]{1,0:T(8,128)(2,1)S(1)}, u32[]{:S(2)}, u32[]{:S(2)}) collective-permute-start(bf16[512,128]{1,0:T(8,128)(2,1)} %get-tuple-element.61), channel_id=1, source_target_pairs={{0,8},{8,0},{16,24},{24,16},{1,9},{9,1},{17,25},{25,17},{2,10},{10... | collective-permute-start | bytes 393224 | tf_op jit(solution)/shard_map/ppermute | solution.py:60
  72.4 0.5 collective-permute-start.12
  72.9 1.5 %collective-permute-start.13 = (bf16[512,128]{1,0:T(8,128)(2,1)}, bf16[512,128]{1,0:T(8,128)(2,1)}, u32[]{:S(2)}, u32[]{:S(2)}) collective-permute-start(bf16[512,128]{1,0:T(8,128)(2,1)} %get-tuple-element.63), channel_id=1, source_target_pairs={{0,24},{8,16},{16,8},{24,0},{1,25},{9,17},{17,9},{25,1},{2,26},{10... | collective-permute-start | bytes 393224 | tf_op jit(solution)/shard_map/ppermute | solution.py:60
  74.4 1.0 copy-done.4
  75.5 2.9 %weight_grad.3 = (f32[2,128,640]{2,1,0:T(8,128)S(1)}, bf16[2,128,640]{2,1,0:T(8,128)(2,1)S(1)}, f32[2,128,640]{2,1,0:T(8,128)S(1)}, bf16[2,128,640]{2,1,0:T(8,128)(2,1)S(1)}) custom-call(s32[3]{0:T(128)S(1)} %add_add_fusion.place_ref, bf16[512,512]{1,0:T(8,128)(2,1)S(1)} %get-tuple-element.64.n_ref, bf16[512,2048]{1,0:T(8,128)(2,1)S(1)} %get-tuple-element.65.d_ref, ...), custom_call_target="tpu_custom_call" | custom-call | tf_op jit(solution)/shard_map/weight_grad/pallas_call | solution.py:34
  78.4 2.5 %collective-permute-done.12 = bf16[512,128]{1,0:T(8,128)(2,1)S(1)} collective-permute-done((bf16[512,128]{1,0:T(8,128)(2,1)}, bf16[512,128]{1,0:T(8,128)(2,1)S(1)}, u32[]{:S(2)}, u32[]{:S(2)}) %collective-permute-start.12) | collective-permute-done | bytes 131104 | tf_op jit(solution)/shard_map/ppermute | solution.py:60
  81.0 1.0 pad_maximum_fusion.refs_0_
  82.0 1.2 %gather_grad.8.refs_1_ = bf16[1024,128]{1,0:T(8,128)(2,1)S(1)} custom-call(s32[1]{0:T(128)} %bitcast.5.base_ref, s32[4,2,2,512]{3,2,1,0:T(2,128)S(1)} %pad_add_fusion.key_ref, bf16[4,512,128]{2,1,0:T(8,128)(2,1)S(1)} %pad_maximum_fusion.refs_0_), custom_call_target="tpu_custom_call" | custom-call | tf_op jit(solution)/shard_map/gather_grad/pallas_call | solution.py:34
  83.3 0.7 collective-permute-done.15.refs_1_.refs_0_
  83.9 1.2 %gather_grad.9 = bf16[1024,128]{1,0:T(8,128)(2,1)S(1)} custom-call(s32[1]{0:T(128)} %bitcast.5.base_ref, s32[4,2,2,512]{3,2,1,0:T(2,128)S(1)} %pad_add_fusion.key_ref, bf16[4,512,128]{2,1,0:T(8,128)(2,1)S(1)} %collective-permute-done.15.refs_1_.refs_0_, bf16[1024,128]{1,0:T(8,128)(2,1)S(1)} %gather_grad.8.refs_1_), custom_call_target="tpu_custom_call" | custom-call | tf_op jit(solution)/shard_map/gather_grad/pallas_call | solution.py:34
  85.2 1.5 %collective-permute-start.17 = (bf16[1024,128]{1,0:T(8,128)(2,1)S(1)}, bf16[1024,128]{1,0:T(8,128)(2,1)S(1)}, u32[]{:S(2)}, u32[]{:S(2)}) collective-permute-start(bf16[1024,128]{1,0:T(8,128)(2,1)S(1)} %gather_grad.9), channel_id=1, source_target_pairs={{0,2},{1,3},{2,0},{3,1},{4,6},{5,7},{6,4},{7,5},{8,10},{9,11},{10,... | collective-permute-start | bytes 786440 | tf_op jit(solution)/shard_map/ppermute | solution.py:64
  86.7 0.5 collective-permute-start.19
  87.2 1.3 %collective-permute-start.20 = (bf16[2,128,640]{2,1,0:T(8,128)(2,1)S(1)}, bf16[2,128,640]{2,1,0:T(8,128)(2,1)S(1)}, u32[]{:S(2)}, u32[]{:S(2)}) collective-permute-start(bf16[2,128,640]{2,1,0:T(8,128)(2,1)S(1)} %get-tuple-element.70), channel_id=1, source_target_pairs={{0,16},{8,24},{16,0},{24,8},{1,17},{9,25},{17,1},{25,9},{2,18},{10... | collective-permute-start | bytes 983048 | tf_op jit(solution)/shard_map/ppermute | solution.py:60
  88.5 2.6 %gather_grad.6 = bf16[1024,128]{1,0:T(8,128)(2,1)S(1)} custom-call(s32[1]{0:T(128)} %bitcast.17.base_ref, s32[4,2,2,512]{3,2,1,0:T(2,128)S(1)} %pad_add_fusion.key_ref, bf16[4,512,128]{2,1,0:T(8,128)(2,1)S(1)} %pad_maximum_fusion.refs_0_, bf16[4,512,128]{2,1,0:T(8,128)(2,1)S(1)} %collective-permute-done.15.refs_1_.refs_0_), custom_call_target="tpu_custom_call" | custom-call | tf_op jit(solution)/shard_map/gather_grad/pallas_call | solution.py:34
  91.1 0.6 collective-permute-start.16
  91.7 2.3 %gather_grad.7 = f32[1024,128]{1,0:T(8,128)S(1)} custom-call(s32[1]{0:T(128)} %bitcast.16.base_ref, s32[4,2,2,512]{3,2,1,0:T(2,128)S(1)} %pad_add_fusion.key_ref, bf16[4,512,128]{2,1,0:T(8,128)(2,1)S(1)} %pad_maximum_fusion.refs_0_, bf16[4,512,128]{2,1,0:T(8,128)(2,1)S(1)} %collective-permute-done.15.refs_1_.refs_0_), custom_call_target="tpu_custom_call" | custom-call | tf_op jit(solution)/shard_map/gather_grad/pallas_call | solution.py:34
  94.1 3.8 %collective-permute-start.18 = (bf16[1024,128]{1,0:T(8,128)(2,1)S(1)}, bf16[1024,128]{1,0:T(8,128)(2,1)S(1)}, u32[]{:S(2)}, u32[]{:S(2)}) collective-permute-start(bf16[1024,128]{1,0:T(8,128)(2,1)S(1)} %add_convert_fusion), channel_id=1, source_target_pairs={{0,4},{1,5},{2,6},{3,7},{4,0},{5,1},{6,2},{7,3},{8,12},{9,13},{10,... | collective-permute-start | bytes 786440 | tf_op jit(solution)/shard_map/ppermute | solution.py:64
  98.0 0.8 fold.1
  98.7 0.6 collective-permute-start.21
  99.3 1.4 %collective-permute-start.22 = (bf16[1,128,640]{2,1,0:T(8,128)(2,1)S(1)}, bf16[1,128,640]{2,1,0:T(8,128)(2,1)S(1)}, u32[]{:S(2)}, u32[]{:S(2)}) collective-permute-start(bf16[1,128,640]{2,1,0:T(8,128)(2,1)S(1)} %get-tuple-element.80), channel_id=1, source_target_pairs={{0,8},{8,0},{16,24},{24,16},{1,9},{9,1},{17,25},{25,17},{2,10},{10... | collective-permute-start | bytes 491528 | tf_op jit(solution)/shard_map/ppermute | solution.py:60
  100.8 2.3 %gather_grad.5 = f32[1024,128]{1,0:T(8,128)S(1)} custom-call(s32[1]{0:T(128)} %bitcast.18.base_ref, s32[4,2,2,512]{3,2,1,0:T(2,128)S(1)} %pad_add_fusion.key_ref, bf16[4,512,128]{2,1,0:T(8,128)(2,1)S(1)} %pad_maximum_fusion.refs_0_, bf16[4,512,128]{2,1,0:T(8,128)(2,1)S(1)} %collective-permute-done.15.refs_1_.refs_0_), custom_call_target="tpu_custom_call" | custom-call | tf_op jit(solution)/shard_map/gather_grad/pallas_call | solution.py:34
  103.1 1.0 collective-permute-done.21.refs_2_
  104.6 0.6 cut_line.1
  105.3 3.2 %collective-permute-start.24 = (bf16[64,640]{1,0:T(8,128)(2,1)S(1)}, bf16[64,640]{1,0:T(8,128)(2,1)S(1)}, u32[]{:S(2)}, u32[]{:S(2)}) collective-permute-start(bf16[64,640]{1,0:T(8,128)(2,1)S(1)} %get-tuple-element.85), channel_id=1, source_target_pairs={{0,4},{1,5},{2,6},{3,7},{4,0},{5,1},{6,2},{7,3},{8,12},{9,13},{10,... | collective-permute-start | bytes 245768 | tf_op jit(solution)/shard_map/ppermute | solution.py:64
  108.5 1.2 collective-permute-start.25
  109.7 1.6 %collective-permute-done.18 = bf16[1024,128]{1,0:T(8,128)(2,1)S(1)} collective-permute-done((bf16[1024,128]{1,0:T(8,128)(2,1)S(1)}, bf16[1024,128]{1,0:T(8,128)(2,1)S(1)}, u32[]{:S(2)}, u32[]{:S(2)}) %collective-permute-start.18) | collective-permute-done | bytes 262176 | tf_op jit(solution)/shard_map/ppermute | solution.py:64
  111.8 3.1 %collective-permute-done.24.refs_2_ = bf16[64,640]{1,0:T(8,128)(2,1)S(1)} collective-permute-done((bf16[64,640]{1,0:T(8,128)(2,1)S(1)}, bf16[64,640]{1,0:T(8,128)(2,1)S(1)}, u32[]{:S(2)}, u32[]{:S(2)}) %collective-permute-start.24) | collective-permute-done | bytes 81952 | tf_op jit(solution)/shard_map/ppermute | solution.py:64
  115.0 1.7 %collective-permute-start.28 = (bf16[64,640]{1,0:T(8,128)(2,1)S(1)}, bf16[64,640]{1,0:T(8,128)(2,1)S(1)}, u32[]{:S(2)}, u32[]{:S(2)}) collective-permute-start(bf16[64,640]{1,0:T(8,128)(2,1)S(1)} %add_up.1.refs_0_), channel_id=1, source_target_pairs={{0,24},{8,16},{16,8},{24,0},{1,25},{9,17},{17,9},{25,1},{2,26},{10... | collective-permute-start | bytes 245768 | tf_op jit(solution)/shard_map/ppermute | solution.py:60
  117.1 1.4 %collective-permute-start.26 = (bf16[64,640]{1,0:T(8,128)(2,1)S(1)}, bf16[64,640]{1,0:T(8,128)(2,1)S(1)}, u32[]{:S(2)}, u32[]{:S(2)}) collective-permute-start(bf16[64,640]{1,0:T(8,128)(2,1)S(1)} %add_up.1.refs_0_), channel_id=1, source_target_pairs={{0,8},{8,0},{16,24},{24,16},{1,9},{9,1},{17,25},{25,17},{2,10},{10... | collective-permute-start | bytes 245768 | tf_op jit(solution)/shard_map/ppermute | solution.py:60
  118.5 0.8 fusion.2
  119.3 1.0 collective-permute-done.28.refs_3_
  120.4 0.9 collective-permute-done.27.refs_2_
  121.6 1.5 %assemble.1 = (f32[64,2048]{1,0:T(8,128)}, f32[64,512]{1,0:T(8,128)}) custom-call(s32[4]{0:T(128)S(1)} %pad_add_fusion.3.block_ref, bf16[64,640]{1,0:T(8,128)(2,1)S(1)} %add_up.1.refs_0_, bf16[64,640]{1,0:T(8,128)(2,1)S(1)} %collective-permute-done.26.refs_1_, bf16[64,640]{1,0:T(8,128)(2,1)S(1)} %collective-permute-done.27.refs_2_, ...), custom_call_target="tpu_custom_call" | custom-call | tf_op jit(solution)/shard_map/assemble/pallas_call | solution.py:34
  (56 shorter events, 3.4 us)
Async XLA Ops:
  1.7 16.1 %collective-permute-start = (bf16[1024,128]{1,0:T(8,128)(2,1)S(1)}, bf16[1024,128]{1,0:T(8,128)(2,1)S(1)}, u32[]{:S(2)}, u32[]{:S(2)}) collective-permute-start(bf16[1024,128]{1,0:T(8,128)(2,1)S(1)} %pad_maximum_fusion.1.chunk_ref), channel_id=1, source_target_pairs={{0,4},{1,5},{2,6},{3,7},{4,0},{5,1},{6,2},{7,3},{8,12},{9,13},{10,... | collective-permute-start | bytes 786440 | tf_op jit(solution)/shard_map/ppermute | solution.py:64
  5.8 25.0 %collective-permute-start.6 = (bf16[1024,128]{1,0:T(8,128)(2,1)S(1)}, bf16[1024,128]{1,0:T(8,128)(2,1)S(1)}, u32[]{:S(2)}, u32[]{:S(2)}) collective-permute-start(bf16[1024,128]{1,0:T(8,128)(2,1)S(1)} %pad_maximum_fusion.1.chunk_ref), channel_id=1, source_target_pairs={{0,2},{1,3},{2,0},{3,1},{4,6},{5,7},{6,4},{7,5},{8,10},{9,11},{10,... | collective-permute-start | bytes 786440 | tf_op jit(solution)/shard_map/ppermute | solution.py:64
  17.8 17.7 %collective-permute-start.1 = (bf16[1024,128]{1,0:T(8,128)(2,1)S(1)}, bf16[1024,128]{1,0:T(8,128)(2,1)S(1)}, u32[]{:S(2)}, u32[]{:S(2)}) collective-permute-start(bf16[1024,128]{1,0:T(8,128)(2,1)S(1)} %collective-permute-done.chunk_ref), channel_id=1, source_target_pairs={{0,2},{1,3},{2,0},{3,1},{4,6},{5,7},{6,4},{7,5},{8,10},{9,11},{10,... | collective-permute-start | bytes 786440 | tf_op jit(solution)/shard_map/ppermute | solution.py:64
  18.4 1.2 %collective-permute-start.2 = (s32[2,512]{1,0:T(2,128)S(1)}, s32[2,512]{1,0:T(2,128)S(1)}, u32[]{:S(2)}, u32[]{:S(2)}) collective-permute-start(s32[2,512]{1,0:T(2,128)S(1)} %get-tuple-element.98), channel_id=1, source_target_pairs={{0,1},{1,0},{2,3},{3,2},{4,5},{5,4},{6,7},{7,6},{8,9},{9,8},{10,11... | collective-permute-start | bytes 12296 | tf_op jit(solution)/shard_map/ppermute | solution.py:67
  19.7 3.7 %collective-permute-start.4 = (s32[2,2,512]{2,1,0:T(2,128)S(1)}, s32[2,2,512]{2,1,0:T(2,128)S(1)}, u32[]{:S(2)}, u32[]{:S(2)}) collective-permute-start(s32[2,2,512]{2,1,0:T(2,128)S(1)} %get-tuple-element.96), channel_id=1, source_target_pairs={{0,16},{8,24},{16,0},{24,8},{1,17},{9,25},{17,1},{25,9},{2,18},{10... | collective-permute-start | bytes 24584 | tf_op jit(solution)/shard_map/ppermute | solution.py:60
  21.2 3.7 %collective-permute-start.3 = (s32[2,2,512]{2,1,0:T(2,128)S(1)}, s32[2,2,512]{2,1,0:T(2,128)S(1)}, u32[]{:S(2)}, u32[]{:S(2)}) collective-permute-start(s32[2,2,512]{2,1,0:T(2,128)S(1)} %get-tuple-element.96), channel_id=1, source_target_pairs={{0,8},{8,0},{16,24},{24,16},{1,9},{9,1},{17,25},{25,17},{2,10},{10... | collective-permute-start | bytes 24584 | tf_op jit(solution)/shard_map/ppermute | solution.py:60
  22.7 4.5 %collective-permute-start.5 = (s32[2,2,512]{2,1,0:T(2,128)S(1)}, s32[2,2,512]{2,1,0:T(2,128)S(1)}, u32[]{:S(2)}, u32[]{:S(2)}) collective-permute-start(s32[2,2,512]{2,1,0:T(2,128)S(1)} %get-tuple-element.96), channel_id=1, source_target_pairs={{0,24},{8,16},{16,8},{24,0},{1,25},{9,17},{17,9},{25,1},{2,26},{10... | collective-permute-start | bytes 24584 | tf_op jit(solution)/shard_map/ppermute | solution.py:60
  28.5 7.1 %copy-start = (s32[4,2,2,512,128]{4,3,2,1,0:T(8,128)}, s32[4,2,2,512,128]{4,3,2,1,0:T(8,128)S(1)}, u32[]{:S(2)}) copy-start(s32[4,2,2,512,128]{4,3,2,1,0:T(8,128)S(1)} %broadcast_in_dim.14.key_ref) | copy-start | bytes 12582916
  36.8 3.5 %collective-permute-start.7 = (bf16[4,512,128]{2,1,0:T(8,128)(2,1)S(1)}, bf16[4,512,128]{2,1,0:T(8,128)(2,1)S(1)}, u32[]{:S(2)}, u32[]{:S(2)}) collective-permute-start(bf16[4,512,128]{2,1,0:T(8,128)(2,1)S(1)} %fetch.9), channel_id=1, source_target_pairs={{0,1},{1,0},{2,3},{3,2},{4,5},{5,4},{6,7},{7,6},{8,9},{9,8},{10,11... | collective-permute-start | bytes 1572872 | tf_op jit(solution)/shard_map/ppermute | solution.py:67
  36.9 2.2 %copy-start.1 = (s32[4,2,2,512,128]{4,3,2,1,0:T(8,128)S(1)}, s32[4,2,2,512,128]{4,3,2,1,0:T(8,128)}, u32[]{:S(2)}) copy-start(s32[4,2,2,512,128]{4,3,2,1,0:T(8,128)} %copy-done) | copy-start | bytes 12582916
  39.1 11.7 %copy-start.2 = (bf16[512,512]{1,0:T(8,128)(2,1)S(1)}, bf16[512,512]{1,0:T(8,128)(2,1)}, u32[]{:S(2)}) copy-start(bf16[512,512]{1,0:T(8,128)(2,1)} %c_ref.3) | copy-start | bytes 1572868
  39.1 11.7 %copy-start.13 = (f32[512]{0:T(512)S(1)}, f32[512]{0:T(512)}, u32[]{:S(2)}) copy-start(f32[512]{0:T(512)} %param.16) | copy-start | bytes 6148
  40.5 6.4 %collective-permute-start.8 = (bf16[512,128]{1,0:T(8,128)(2,1)S(1)}, bf16[512,128]{1,0:T(8,128)(2,1)S(1)}, u32[]{:S(2)}, u32[]{:S(2)}) collective-permute-start(bf16[512,128]{1,0:T(8,128)(2,1)S(1)} %get-tuple-element.56), channel_id=1, source_target_pairs={{0,8},{8,0},{16,24},{24,16},{1,9},{9,1},{17,25},{25,17},{2,10},{10... | collective-permute-start | bytes 393224 | tf_op jit(solution)/shard_map/ppermute | solution.py:60
  41.1 8.4 %collective-permute-start.9 = (bf16[512,128]{1,0:T(8,128)(2,1)S(1)}, bf16[512,128]{1,0:T(8,128)(2,1)S(1)}, u32[]{:S(2)}, u32[]{:S(2)}) collective-permute-start(bf16[512,128]{1,0:T(8,128)(2,1)S(1)} %get-tuple-element.57), channel_id=1, source_target_pairs={{0,16},{8,24},{16,0},{24,8},{1,17},{9,25},{17,1},{25,9},{2,18},{10... | collective-permute-start | bytes 393224 | tf_op jit(solution)/shard_map/ppermute | solution.py:60
  41.6 8.6 %collective-permute-start.10 = (bf16[512,128]{1,0:T(8,128)(2,1)S(1)}, bf16[512,128]{1,0:T(8,128)(2,1)S(1)}, u32[]{:S(2)}, u32[]{:S(2)}) collective-permute-start(bf16[512,128]{1,0:T(8,128)(2,1)S(1)} %get-tuple-element.58), channel_id=1, source_target_pairs={{0,24},{8,16},{16,8},{24,0},{1,25},{9,17},{17,9},{25,1},{2,26},{10... | collective-permute-start | bytes 393224 | tf_op jit(solution)/shard_map/ppermute | solution.py:60
  49.5 0.7 copy-start.7
  50.1 0.7 copy-start.9
  50.8 1.6 %copy-start.5 = (bf16[512,2048]{1,0:T(8,128)(2,1)S(1)}, bf16[512,2048]{1,0:T(8,128)(2,1)}, u32[]{:S(2)}) copy-start(bf16[512,2048]{1,0:T(8,128)(2,1)} %wp_ref.1) | copy-start | bytes 6291460
  52.4 1.0 copy-start.6
  53.4 0.9 copy-start.8
  54.3 0.9 copy-start.10
  67.7 3.1 %copy-start.3 = (bf16[512,512]{1,0:T(8,128)(2,1)}, bf16[512,512]{1,0:T(8,128)(2,1)S(1)}, u32[]{:S(2)}) copy-start(bf16[512,512]{1,0:T(8,128)(2,1)S(1)} %get-tuple-element.66.g_ref) | copy-start | bytes 1572868
  67.7 3.1 %copy-start.11 = (bf16[512,128]{1,0:T(8,128)(2,1)}, bf16[512,128]{1,0:T(8,128)(2,1)S(1)}, u32[]{:S(2)}) copy-start(bf16[512,128]{1,0:T(8,128)(2,1)S(1)} %get-tuple-element.71) | copy-start | bytes 393220
  70.8 3.6 %collective-permute-start.14 = (bf16[4,256,640]{2,1,0:T(8,128)(2,1)}, bf16[4,256,640]{2,1,0:T(8,128)(2,1)}, u32[]{:S(2)}, u32[]{:S(2)}) collective-permute-start(bf16[4,256,640]{2,1,0:T(8,128)(2,1)} %weight_grad.2), channel_id=1, source_target_pairs={{0,1},{1,0},{2,3},{3,2},{4,5},{5,4},{6,7},{7,6},{8,9},{9,8},{10,11... | collective-permute-start | bytes 3932168 | tf_op jit(solution)/shard_map/ppermute | solution.py:67
  70.8 7.6 %collective-permute-start.11 = (bf16[512,128]{1,0:T(8,128)(2,1)}, bf16[512,128]{1,0:T(8,128)(2,1)S(1)}, u32[]{:S(2)}, u32[]{:S(2)}) collective-permute-start(bf16[512,128]{1,0:T(8,128)(2,1)} %get-tuple-element.61), channel_id=1, source_target_pairs={{0,8},{8,0},{16,24},{24,16},{1,9},{9,1},{17,25},{25,17},{2,10},{10... | collective-permute-start | bytes 393224 | tf_op jit(solution)/shard_map/ppermute | solution.py:60
  72.4 8.6 %collective-permute-start.12 = (bf16[512,128]{1,0:T(8,128)(2,1)}, bf16[512,128]{1,0:T(8,128)(2,1)S(1)}, u32[]{:S(2)}, u32[]{:S(2)}) collective-permute-start(bf16[512,128]{1,0:T(8,128)(2,1)} %get-tuple-element.62), channel_id=1, source_target_pairs={{0,16},{8,24},{16,0},{24,8},{1,17},{9,25},{17,1},{25,9},{2,18},{10... | collective-permute-start | bytes 393224 | tf_op jit(solution)/shard_map/ppermute | solution.py:60
  72.9 8.1 %collective-permute-start.13 = (bf16[512,128]{1,0:T(8,128)(2,1)}, bf16[512,128]{1,0:T(8,128)(2,1)}, u32[]{:S(2)}, u32[]{:S(2)}) collective-permute-start(bf16[512,128]{1,0:T(8,128)(2,1)} %get-tuple-element.63), channel_id=1, source_target_pairs={{0,24},{8,16},{16,8},{24,0},{1,25},{9,17},{17,9},{25,1},{2,26},{10... | collective-permute-start | bytes 393224 | tf_op jit(solution)/shard_map/ppermute | solution.py:60
  74.4 1.0 copy-start.4
  75.5 5.5 %copy-start.12 = (bf16[512,128]{1,0:T(8,128)(2,1)S(1)}, bf16[512,128]{1,0:T(8,128)(2,1)}, u32[]{:S(2)}) copy-start(bf16[512,128]{1,0:T(8,128)(2,1)} %copy-done.11) | copy-start | bytes 393220
  81.9 2.0 %collective-permute-start.15 = (bf16[4,512,128]{2,1,0:T(8,128)(2,1)S(1)}, bf16[4,512,128]{2,1,0:T(8,128)(2,1)S(1)}, u32[]{:S(2)}, u32[]{:S(2)}) collective-permute-start(bf16[4,512,128]{2,1,0:T(8,128)(2,1)S(1)} %pad_maximum_fusion.refs_0_), channel_id=1, source_target_pairs={{0,1},{1,0},{2,3},{3,2},{4,5},{5,4},{6,7},{7,6},{8,9},{9,8},{10,11... | collective-permute-start | bytes 1572872 | tf_op jit(solution)/shard_map/ppermute | solution.py:67
  85.2 8.9 %collective-permute-start.17 = (bf16[1024,128]{1,0:T(8,128)(2,1)S(1)}, bf16[1024,128]{1,0:T(8,128)(2,1)S(1)}, u32[]{:S(2)}, u32[]{:S(2)}) collective-permute-start(bf16[1024,128]{1,0:T(8,128)(2,1)S(1)} %gather_grad.9), channel_id=1, source_target_pairs={{0,2},{1,3},{2,0},{3,1},{4,6},{5,7},{6,4},{7,5},{8,10},{9,11},{10,... | collective-permute-start | bytes 786440 | tf_op jit(solution)/shard_map/ppermute | solution.py:64
  86.7 11.3 %collective-permute-start.19 = (bf16[2,128,640]{2,1,0:T(8,128)(2,1)S(1)}, bf16[2,128,640]{2,1,0:T(8,128)(2,1)S(1)}, u32[]{:S(2)}, u32[]{:S(2)}) collective-permute-start(bf16[2,128,640]{2,1,0:T(8,128)(2,1)S(1)} %get-tuple-element.68), channel_id=1, source_target_pairs={{0,8},{8,0},{16,24},{24,16},{1,9},{9,1},{17,25},{25,17},{2,10},{10... | collective-permute-start | bytes 983048 | tf_op jit(solution)/shard_map/ppermute | solution.py:60
  87.2 10.8 %collective-permute-start.20 = (bf16[2,128,640]{2,1,0:T(8,128)(2,1)S(1)}, bf16[2,128,640]{2,1,0:T(8,128)(2,1)S(1)}, u32[]{:S(2)}, u32[]{:S(2)}) collective-permute-start(bf16[2,128,640]{2,1,0:T(8,128)(2,1)S(1)} %get-tuple-element.70), channel_id=1, source_target_pairs={{0,16},{8,24},{16,0},{24,8},{1,17},{9,25},{17,1},{25,9},{2,18},{10... | collective-permute-start | bytes 983048 | tf_op jit(solution)/shard_map/ppermute | solution.py:60
  91.1 18.7 %collective-permute-start.16 = (bf16[1024,128]{1,0:T(8,128)(2,1)S(1)}, bf16[1024,128]{1,0:T(8,128)(2,1)S(1)}, u32[]{:S(2)}, u32[]{:S(2)}) collective-permute-start(bf16[1024,128]{1,0:T(8,128)(2,1)S(1)} %gather_grad.6), channel_id=1, source_target_pairs={{0,2},{1,3},{2,0},{3,1},{4,6},{5,7},{6,4},{7,5},{8,10},{9,11},{10,... | collective-permute-start | bytes 786440 | tf_op jit(solution)/shard_map/ppermute | solution.py:64
  94.1 17.2 %collective-permute-start.18 = (bf16[1024,128]{1,0:T(8,128)(2,1)S(1)}, bf16[1024,128]{1,0:T(8,128)(2,1)S(1)}, u32[]{:S(2)}, u32[]{:S(2)}) collective-permute-start(bf16[1024,128]{1,0:T(8,128)(2,1)S(1)} %add_convert_fusion), channel_id=1, source_target_pairs={{0,4},{1,5},{2,6},{3,7},{4,0},{5,1},{6,2},{7,3},{8,12},{9,13},{10,... | collective-permute-start | bytes 786440 | tf_op jit(solution)/shard_map/ppermute | solution.py:64
  98.7 5.4 %collective-permute-start.21 = (bf16[1,128,640]{2,1,0:T(8,128)(2,1)S(1)}, bf16[1,128,640]{2,1,0:T(8,128)(2,1)S(1)}, u32[]{:S(2)}, u32[]{:S(2)}) collective-permute-start(bf16[1,128,640]{2,1,0:T(8,128)(2,1)S(1)} %get-tuple-element.79), channel_id=1, source_target_pairs={{0,16},{8,24},{16,0},{24,8},{1,17},{9,25},{17,1},{25,9},{2,18},{10... | collective-permute-start | bytes 491528 | tf_op jit(solution)/shard_map/ppermute | solution.py:60
  99.3 5.3 %collective-permute-start.22 = (bf16[1,128,640]{2,1,0:T(8,128)(2,1)S(1)}, bf16[1,128,640]{2,1,0:T(8,128)(2,1)S(1)}, u32[]{:S(2)}, u32[]{:S(2)}) collective-permute-start(bf16[1,128,640]{2,1,0:T(8,128)(2,1)S(1)} %get-tuple-element.80), channel_id=1, source_target_pairs={{0,8},{8,0},{16,24},{24,16},{1,9},{9,1},{17,25},{25,17},{2,10},{10... | collective-permute-start | bytes 491528 | tf_op jit(solution)/shard_map/ppermute | solution.py:60
  105.3 6.5 %collective-permute-start.23 = (bf16[64,640]{1,0:T(8,128)(2,1)S(1)}, bf16[64,640]{1,0:T(8,128)(2,1)S(1)}, u32[]{:S(2)}, u32[]{:S(2)}) collective-permute-start(bf16[64,640]{1,0:T(8,128)(2,1)S(1)} %get-tuple-element.84), channel_id=1, source_target_pairs={{0,2},{1,3},{2,0},{3,1},{4,6},{5,7},{6,4},{7,5},{8,10},{9,11},{10,... | collective-permute-start | bytes 245768 | tf_op jit(solution)/shard_map/ppermute | solution.py:64
  105.3 9.6 %collective-permute-start.24 = (bf16[64,640]{1,0:T(8,128)(2,1)S(1)}, bf16[64,640]{1,0:T(8,128)(2,1)S(1)}, u32[]{:S(2)}, u32[]{:S(2)}) collective-permute-start(bf16[64,640]{1,0:T(8,128)(2,1)S(1)} %get-tuple-element.85), channel_id=1, source_target_pairs={{0,4},{1,5},{2,6},{3,7},{4,0},{5,1},{6,2},{7,3},{8,12},{9,13},{10,... | collective-permute-start | bytes 245768 | tf_op jit(solution)/shard_map/ppermute | solution.py:64
  108.5 6.4 %collective-permute-start.25 = (bf16[64,640]{1,0:T(8,128)(2,1)S(1)}, bf16[64,640]{1,0:T(8,128)(2,1)S(1)}, u32[]{:S(2)}, u32[]{:S(2)}) collective-permute-start(bf16[64,640]{1,0:T(8,128)(2,1)S(1)} %get-tuple-element.86), channel_id=1, source_target_pairs={{0,6},{1,7},{2,4},{3,5},{4,2},{5,3},{6,0},{7,1},{8,14},{9,15},{10,... | collective-permute-start | bytes 245768 | tf_op jit(solution)/shard_map/ppermute | solution.py:64
  115.0 5.4 %collective-permute-start.28 = (bf16[64,640]{1,0:T(8,128)(2,1)S(1)}, bf16[64,640]{1,0:T(8,128)(2,1)S(1)}, u32[]{:S(2)}, u32[]{:S(2)}) collective-permute-start(bf16[64,640]{1,0:T(8,128)(2,1)S(1)} %add_up.1.refs_0_), channel_id=1, source_target_pairs={{0,24},{8,16},{16,8},{24,0},{1,25},{9,17},{17,9},{25,1},{2,26},{10... | collective-permute-start | bytes 245768 | tf_op jit(solution)/shard_map/ppermute | solution.py:60
  116.7 4.6 %collective-permute-start.27 = (bf16[64,640]{1,0:T(8,128)(2,1)S(1)}, bf16[64,640]{1,0:T(8,128)(2,1)S(1)}, u32[]{:S(2)}, u32[]{:S(2)}) collective-permute-start(bf16[64,640]{1,0:T(8,128)(2,1)S(1)} %add_up.1.refs_0_), channel_id=1, source_target_pairs={{0,16},{8,24},{16,0},{24,8},{1,17},{9,25},{17,1},{25,9},{2,18},{10... | collective-permute-start | bytes 245768 | tf_op jit(solution)/shard_map/ppermute | solution.py:60
  117.1 4.4 %collective-permute-start.26 = (bf16[64,640]{1,0:T(8,128)(2,1)S(1)}, bf16[64,640]{1,0:T(8,128)(2,1)S(1)}, u32[]{:S(2)}, u32[]{:S(2)}) collective-permute-start(bf16[64,640]{1,0:T(8,128)(2,1)S(1)} %add_up.1.refs_0_), channel_id=1, source_target_pairs={{0,8},{8,0},{16,24},{24,16},{1,9},{9,1},{17,25},{25,17},{2,10},{10... | collective-permute-start | bytes 245768 | tf_op jit(solution)/shard_map/ppermute | solution.py:60

commit v5 on v4

--- a/solution.py
+++ b/solution.py
@@ -26,8 +26,9 @@
     return 0.5 * jnp.tanh(0.5 * value) + 0.5
 
 
-def run(name, body, outs, args, smem=0, scratch=(), vmem=16):
+def run(name, body, outs, args, smem=0, scratch=(), vmem=16, flops=0):
     outs = [jax.ShapeDtypeStruct(shape, dtype) for shape, dtype in outs]
+    size = sum(a.size * a.dtype.itemsize for a in [*args, *outs])
     in_smem = pl.BlockSpec(memory_space=pltpu.SMEM)
     in_vmem = pl.BlockSpec(memory_space=pltpu.VMEM)
     places = [in_smem] * smem + [in_vmem] * (len(args) - smem)
@@ -38,7 +39,7 @@
         out_specs=[in_vmem] * len(outs),
         scratch_shapes=list(scratch),
         compiler_params=pltpu.CompilerParams(vmem_limit_bytes=vmem * MIB),
-        cost_estimate=pl.CostEstimate(flops=0, bytes_accessed=0, transcendentals=0),
+        cost_estimate=pl.CostEstimate(flops=flops, bytes_accessed=size, transcendentals=0),
         name=name,
     )(*args)
     return list(results)
@@ -93,6 +94,7 @@
         [((count, tokens, cols), BF16)] * many,
         [base.reshape(1), chunk, keys, *before],
         smem=1,
+        flops=2 * many * count * tokens * rows * cols,
     )
 
 
@@ -136,10 +138,11 @@
         [((2 * rows, cols), out)],
         [base.reshape(1), keys, *tokens, *before],
         smem=1,
+        flops=4 * many * count * length * 2 * rows * cols,
     )[0]
 
 
-def sequence(blocks, pieces, cotangent, gain, w_proj, w_out):
+def sequence(blocks, other, pieces, cotangent, gain, w_proj, w_out, cores, line):
     count = len(pieces)
     length, width = cotangent.shape
     cols = width // count
@@ -148,17 +151,17 @@
     tile = min(256, length)
     step = min(256, 4 * width)
 
-    def body(block_ref, cot_ref, wo_ref, wp_ref, gain_ref, *refs):
+    def body(block_ref, other_ref, cot_ref, wo_ref, wp_ref, gain_ref, *refs):
         piece_refs, refs = refs[:count], refs[count:]
         out_ref, *grad_refs = refs[: count + 1]
-        normed_ref, dproj_ref, gated_ref = refs[count + 1 : count + 4]
-        emb, act, slope, att, attn, dscale, dkey, dval, tok = refs[count + 4 :]
-
-        def block(k):
-            return pl.ds(pl.multiple_of(block_ref[k] * cols, cols), cols)
+        normed_ref, dproj_ref, gated_ref, weight_ref = refs[count + 1 : count + 5]
+        emb, act, slope, att, attn, dscale, dkey, dval, tok = refs[count + 5 :]
 
         for k in range(count):
-            emb[:, block(k)] = piece_refs[k][...]
+            emb[block_ref[k]] = piece_refs[k][...]
+
+        def embedded(span):
+            return jnp.concatenate([emb[k, span] for k in range(count)], axis=1).astype(F32)
 
         def norm_of(value):
             centred = value - jnp.mean(value, axis=-1, keepdims=True)
@@ -174,7 +177,7 @@
 
         for at in range(0, length, tile):
             span = slice(at, at + tile)
-            hat, _ = norm_of(emb[span, :].astype(F32))
+            hat, _ = norm_of(embedded(span))
             normed_ref[span, :] = (hat * gain_ref[...]).astype(BF16)
 
         normed = normed_ref[...]
@@ -210,7 +213,7 @@
             gate = act[span, :width].astype(F32)
             gated = (hat * gate).astype(BF16)
             gated_ref[span, :] = gated
-            out_ref[span, :] = (emb[span, :].astype(F32) + dot(gated, wo_ref[...])).astype(BF16)
+            out_ref[span, :] = (embedded(span) + dot(gated, wo_ref[...])).astype(BF16)
             dgated = dot(cot_ref[span, :], wo_ref[...], NT)
             dproj_ref[span, :width] = (dgated * hat * slope[span, :width]).astype(BF16)
             datt = norm_back(dgated * gate, hat, scale).astype(BF16)
@@ -229,13 +232,18 @@
 
         for at in range(0, length, tile):
             span = slice(at, at + tile)
-            hat, scale = norm_of(emb[span, :].astype(F32))
+            hat, scale = norm_of(embedded(span))
             upper = dot(dproj_ref[span, :], wp_ref[...], NT) * gain_ref[...]
             grad = cot_ref[span, :].astype(F32) + norm_back(upper, hat, scale)
-            tok[span, :] = grad.astype(BF16)
+            for k in range(count):
+                tok[k, span] = grad[:, k * cols : (k + 1) * cols].astype(BF16)
 
         for k in range(count):
-            grad_refs[k][...] = tok[:, block(k)]
+            grad_refs[k][...] = tok[block_ref[k]]
+
+        sums = weight_sums(other_ref[0], normed_ref, dproj_ref, gated_ref, cot_ref, cores, line, count)
+        for k in range(count):
+            weight_ref[k] = next(sums).astype(BF16)
 
     return run(
         "sequence",
@@ -246,12 +254,14 @@
             ((length, width), BF16),
             ((length, 4 * width), BF16),
             ((length, width), BF16),
+            ((count, width // cores, 5 * width // count), BF16),
         ],
-        [blocks, cotangent, w_out, w_proj, gain, *pieces],
-        smem=1,
+        [blocks, other, cotangent, w_out, w_proj, gain, *pieces],
+        smem=2,
         vmem=24,
+        flops=32 * length * width * width,
         scratch=[
-            pltpu.VMEM((length, width), BF16),
+            pltpu.VMEM((count, length, cols), BF16),
             pltpu.VMEM((length, 4 * width), BF16),
             pltpu.VMEM((length, 4 * width), F32),
             pltpu.VMEM((tile, width), F32),
@@ -259,59 +269,60 @@
             pltpu.VMEM((HEADS, tile, length), F32),
             pltpu.VMEM((length, width), F32),
             pltpu.VMEM((length, width), F32),
-            pltpu.VMEM((length, width), BF16),
+            pltpu.VMEM((count, length, cols), BF16),
         ],
     )
 
 
-def weight_grad(place, normed, dproj, gated, cotangent, cores, line, blocks, before=()):
-    length, width = normed.shape
+def weight_sums(core, n_ref, d_ref, g_ref, c_ref, cores, line, blocks):
+    length, width = n_ref.shape
     rows = width // (cores * line)
     half = width // cores
-    edge = dproj.shape[1]
-    total = edge + cotangent.shape[1]
-    cols = total // blocks
+    edge = d_ref.shape[1]
+    cols = (edge + c_ref.shape[1]) // blocks
+    feature = lax.broadcasted_iota(I32, (width, half), 0)
+    column = lax.broadcasted_iota(I32, (width, half), 1)
+    wanted = (column // rows * cores + core) * rows + column % rows
+    pick = jnp.where(feature == wanted, 1.0, 0.0).astype(BF16)
+    n_part = dot(n_ref[...], pick).astype(BF16)
+    g_part = dot(g_ref[...], pick).astype(BF16)
+    for k in range(blocks):
+        first, last = k * cols, (k + 1) * cols
+        parts = []
+        if first < edge:
+            parts.append(dot(n_part, d_ref[:, first : min(last, edge)], TN))
+        if last > edge:
+            parts.append(dot(g_part, c_ref[:, max(first, edge) - edge : last - edge], TN))
+        yield parts[0] if len(parts) == 1 else jnp.concatenate(parts, axis=1)
+
+
+def weight_grad(place, normed, dproj, gated, cotangent, before, line):
+    blocks, half, cols = before.shape
+    length, width = normed.shape
+    cores = width // half
     bits = blocks.bit_length() - 1
     tall = half // bits
 
-    def body(place_ref, n_ref, d_ref, g_ref, c_ref, *refs):
-        before_refs, out_refs, scratch = refs[: len(before)], refs[len(before) : -1], refs[-1]
-        feature = lax.broadcasted_iota(I32, (width, half), 0)
-        column = lax.broadcasted_iota(I32, (width, half), 1)
-        wanted = (column // rows * cores + place_ref[0]) * rows + column % rows
-        pick = jnp.where(feature == wanted, 1.0, 0.0).astype(BF16)
-        n_part = dot(n_ref[...], pick).astype(BF16)
-        g_part = dot(g_ref[...], pick).astype(BF16)
+    def body(place_ref, n_ref, d_ref, g_ref, c_ref, before_ref, *refs):
+        out_refs, scratch = refs[:-1], refs[-1]
+        sums = weight_sums(place_ref[0], n_ref, d_ref, g_ref, c_ref, cores, line, blocks)
         for k in range(blocks):
-            first, last = k * cols, (k + 1) * cols
-            parts = []
-            if first < edge:
-                parts.append(dot(n_part, d_ref[:, first : min(last, edge)], TN))
-            if last > edge:
-                parts.append(dot(g_part, c_ref[:, max(first, edge) - edge : last - edge], TN))
-            sums = parts[0] if len(parts) == 1 else jnp.concatenate(parts, axis=1)
-            if not before:
-                out_refs[0][k] = sums.astype(BF16)
-                continue
-            sums = sums + before_refs[0][k].astype(F32)
+            total = next(sums) + before_ref[k].astype(F32)
             for p in range(bits):
                 at = sum((k >> (p + i) % bits & 1) << bits - 1 - i for i in range(bits))
-                scratch[p, at] = sums[p * tall : (p + 1) * tall]
-        if before:
-            for p in range(bits):
-                split_halves(scratch.at[p], place_ref[1 + p], out_refs[2 * p : 2 * p + 2])
-
-    outs = [((blocks, half, cols), BF16)]
-    if before:
-        kept = (blocks // 2, tall, cols)
-        outs = [(kept, F32), (kept, BF16)] * bits
+                scratch[p, at] = total[p * tall : (p + 1) * tall]
+        for p in range(bits):
+            split_halves(scratch.at[p], place_ref[1 + p], out_refs[2 * p : 2 * p + 2])
+
+    kept = (blocks // 2, tall, cols)
     return run(
         "weight_grad",
         body,
-        outs,
-        [place, normed, dproj, gated, cotangent, *before],
+        [(kept, F32), (kept, BF16)] * bits,
+        [place, normed, dproj, gated, cotangent, before],
         smem=1,
         scratch=[pltpu.VMEM((bits, blocks, tall, cols), F32)],
+        flops=2 * length * half * (blocks * cols + 2 * width),
     )
 
 
@@ -387,9 +398,14 @@
     def body(block_ref, *refs):
         part_refs, (left_ref, right_ref, held) = refs[: len(parts)], refs[len(parts) :]
         for k, ref in enumerate(part_refs):
-            held[:, pl.ds(pl.multiple_of(block_ref[k] * cols, cols), cols)] = ref[...].astype(F32)
-        left_ref[...] = held[:, :edge]
-        right_ref[...] = held[:, edge:]
+            held[block_ref[k]] = ref[...].astype(F32)
+        for k in range(len(parts)):
+            first, last = k * cols, (k + 1) * cols
+            cut = min(max(edge - first, 0), cols)
+            if cut > 0:
+                left_ref[:, first : first + cut] = held[k, :, :cut]
+            if cut < cols:
+                right_ref[:, first + cut - edge : last - edge] = held[k, :, cut:]
 
     return run(
         "assemble",
@@ -397,7 +413,7 @@
         [((rows, edge), F32), ((rows, total - edge), F32)],
         [blocks, *parts],
         smem=1,
-        scratch=[pltpu.VMEM((rows, total), F32)],
+        scratch=[pltpu.VMEM((len(parts), rows, cols), F32)],
     )
 
 
@@ -438,14 +454,15 @@
         ]
     ).astype(I32)
 
+    keys = jnp.stack([keys, grid.over_pair(keys)])
+    keys = jnp.stack([keys] + [grid.over_replica(keys, k) for k in range(1, replicas)])
+
     held = {0: own}
     for low in reversed([1 << i for i in range(line.bit_length() - 1)]):
         for k in range(low, line, 2 * low):
             held[k] = grid.over_line(held[k ^ low], low)
     order = sorted(held, key=lambda k: (bin(k).count("1"), k))
 
-    keys = jnp.stack([keys, grid.over_pair(keys)])
-    keys = jnp.stack([keys] + [grid.over_replica(keys, k) for k in range(1, replicas)])
     key_cols = jnp.broadcast_to(keys[..., None], (*keys.shape, LANES))
     both = list(range(cores))
 
@@ -460,46 +477,55 @@
         pieces[k] = grid.over_replica(pieces[k], k)
 
     layer_out, *rest = sequence(
-        blocks, pieces, cotangent, input_norm_gain.reshape(1, width), w_proj, w_out
-    )
-    tokens, (normed, dproj, gated) = rest[:replicas], rest[replicas:]
+        blocks,
+        ((grid.c + 1) % cores).astype(I32).reshape(1),
+        pieces,
+        cotangent,
+        input_norm_gain.reshape(1, width),
+        w_proj,
+        w_out,
+        cores,
+        line,
+    )
+    tokens, (normed, dproj, gated, weights) = rest[:replicas], rest[replicas:]
     for k in swaps:
         tokens[k] = grid.over_replica(tokens[k], k)
 
-    def weights_of(m, before=()):
-        place = [(grid.c + m) % cores] + [grid.r >> p & 1 for p in range(bits)]
-        place = jnp.stack(place).astype(I32)
-        args = (place, normed, dproj, gated, cotangent, cores, line, replicas, before)
-        return weight_grad(*args)
-
-    weights = weights_of(0, [grid.over_pair(weights_of(1)[0])])
+    place = jnp.stack([grid.c] + [grid.r >> p & 1 for p in range(bits)]).astype(I32)
+    weights = grid.over_pair(weights)
+    weights = weight_grad(place, normed, dproj, gated, cotangent, weights, line)
     tokens = lax.optimization_barrier((tokens, weights))[0]
     tokens = jnp.stack(tokens)
     there = grid.over_pair(tokens)
 
+    def swap_weights(weights, step):
+        kept, sent = weights[0::2], weights[1::2]
+        return kept, [grid.over_replica(sent[p], 1 << (p + step) % bits) for p in range(bits)]
+
+    kept, came = swap_weights(weights, 0)
+    first = {k: gather_grad(keys, both[:1], [tokens], bases[k], rows) for k in order[-2:]}
+    there = lax.optimization_barrier((there, came, first))[0]
+
     sums = {}
     for k in reversed(order):
-        if k == last:
-            first = gather_grad(keys, both[:1], [tokens], bases[k], rows)
-            sums[k] = gather_grad(keys, both[1:], [there], bases[k], rows, [first])
-            continue
         low = (k & -k) or line
         steps = [1 << i for i in range(low.bit_length() - 1)]
         out = F32 if steps else BF16
-        total = gather_grad(keys, both, [tokens, there], bases[k], rows, out=out)
+        if k in first:
+            total = gather_grad(keys, both[1:], [there], bases[k], rows, [first[k]], out)
+        else:
+            total = gather_grad(keys, both, [tokens, there], bases[k], rows, out=out)
         for step in steps:
             total = total + grid.over_line(sums[k ^ step], step).astype(F32)
         sums[k] = total.astype(BF16) if k else total
     table_grad = sums[0]
 
-    for step in range(bits):
-        kept, sent = weights[0::2], weights[1::2]
-        came = [grid.over_replica(sent[p], 1 << (p + step) % bits) for p in range(bits)]
-        after = sums[last] if step < bits - 1 else sums[line // 2]
+    for step in range(1, bits + 1):
+        after = sums[last] if step < bits else sums[line // 2]
         came = lax.optimization_barrier((came, after))[0]
-        if step < bits - 1:
-            turn = jnp.stack([grid.r >> (p + step + 1) % bits & 1 for p in range(bits)])
-            weights = fold(turn.astype(I32), kept, came)
+        if step < bits:
+            turn = jnp.stack([grid.r >> (p + step) % bits & 1 for p in range(bits)])
+            kept, came = swap_weights(fold(turn.astype(I32), kept, came), step)
     parts = cut_line(planes, kept, came)
     parts = [parts[0]] + [grid.over_line(parts[k], k) for k in range(1, line)]
     parts = lax.optimization_barrier((parts, table_grad))[0]

time: 123 us -> 122 us (level)
  local copies, waits for them, and re-layouts: 12 us -> 14.5 us
  Pallas kernels: 40.7 us -> 38.6 us
    unnamed x28 -> x36, local copies, waits for them, and re-layouts: 9 us -> 11.5 us
    ppermute x16, waiting for transfers between devices: 15.7 us -> 17.9 us  [over_replica(): return lax.ppermute(value, 'replica', [(i, i ^ step) for i in range(n)])]
    pallas_call x18, Pallas kernels: 40.7 us -> 38.6 us  [run(): pl.pallas_call(body, out_shape=outs, in_specs=places, out_specs=[in_vmem]...]
    ppermute x9, waiting for transfers between devices: 14.9 us -> 12.9 us  [over_line(): return lax.ppermute(value, 'sparse', pairs)]
  transfers between devices with their start and end apart: 29 -> 29, of which waited for: 17 -> 16; matrix products, arithmetic and copies ran while one was open for 3% -> 3% of each run, Pallas kernels for 17% -> 17%
where the time goes in v5:
time: 122 us
  Pallas kernels  38.6 us (32%)
  starting transfers between devices  35.4 us (29%)
  waiting for transfers between devices  31.4 us (26%)
  local copies, waits for them, and re-layouts  14.5 us (12%)
  other arithmetic  1.29 us (1%)
    pallas_call x18, Pallas kernels, run(): pl.pallas_call(body, out_shape=outs, in_specs=places, out_specs=[in_vmem]...  38.6 us
    ppermute x16, starting transfers between devices, over_replica(): return lax.ppermute(value, 'replica', [(i, i ^ step) for i in range(n)])  18.6 us
    ppermute x16, waiting for transfers between devices, over_replica(): return lax.ppermute(value, 'replica', [(i, i ^ step) for i in range(n)])  17.9 us
    ppermute x9, starting transfers between devices, over_line(): return lax.ppermute(value, 'sparse', pairs)  16.5 us
    ppermute x9, waiting for transfers between devices, over_line(): return lax.ppermute(value, 'sparse', pairs)  12.9 us
    unnamed x36, local copies, waits for them, and re-layouts  11.5 us
  transfers between devices with their start and end apart: 29, of which 16 were waited for; matrix products, arithmetic and copies ran while one was open for 3% of the time, Pallas kernels for 17%

profile of v5, /device:TPU:0, one launch (start us, length us, event | category | flops | bytes accessed | tf_op | source)
XLA Modules:
  0.0 122.1 jit_solution(11408137287203772056)
XLA Ops:
  0.6 1.0 constant_dynamic-slice_fusion
  1.7 4.1 %collective-permute-start = (bf16[1024,128]{1,0:T(8,128)(2,1)S(1)}, bf16[1024,128]{1,0:T(8,128)(2,1)S(1)}, u32[]{:S(2)}, u32[]{:S(2)}) collective-permute-start(bf16[1024,128]{1,0:T(8,128)(2,1)S(1)} %pad_maximum_fusion.1.chunk_ref), channel_id=1, source_target_pairs={{0,4},{1,5},{2,6},{3,7},{4,0},{5,1},{6,2},{7,3},{8,12},{9,13},{10,... | collective-permute-start | bytes 786440 | tf_op jit(solution)/shard_map/ppermute | solution.py:65
  5.8 0.7 add_bitcast_fusion
  6.6 1.6 %collective-permute-start.6 = (bf16[1024,128]{1,0:T(8,128)(2,1)S(1)}, bf16[1024,128]{1,0:T(8,128)(2,1)S(1)}, u32[]{:S(2)}, u32[]{:S(2)}) collective-permute-start(bf16[1024,128]{1,0:T(8,128)(2,1)S(1)} %pad_maximum_fusion.1.chunk_ref), channel_id=1, source_target_pairs={{0,2},{1,3},{2,0},{3,1},{4,6},{5,7},{6,4},{7,5},{8,10},{9,11},{10,... | collective-permute-start | bytes 786440 | tf_op jit(solution)/shard_map/ppermute | solution.py:65
  8.2 1.6 %collective-permute-start.4 = (s32[2,2,512]{2,1,0:T(2,128)S(1)}, s32[2,2,512]{2,1,0:T(2,128)S(1)}, u32[]{:S(2)}, u32[]{:S(2)}) collective-permute-start(s32[2,2,512]{2,1,0:T(2,128)S(1)} %get-tuple-element.100), channel_id=1, source_target_pairs={{0,16},{8,24},{16,0},{24,8},{1,17},{9,25},{17,1},{25,9},{2,18},{10... | collective-permute-start | bytes 24584 | tf_op jit(solution)/shard_map/ppermute | solution.py:61
  9.8 1.5 %collective-permute-start.3 = (s32[2,2,512]{2,1,0:T(2,128)S(1)}, s32[2,2,512]{2,1,0:T(2,128)S(1)}, u32[]{:S(2)}, u32[]{:S(2)}) collective-permute-start(s32[2,2,512]{2,1,0:T(2,128)S(1)} %get-tuple-element.100), channel_id=1, source_target_pairs={{0,8},{8,0},{16,24},{24,16},{1,9},{9,1},{17,25},{25,17},{2,10},{10... | collective-permute-start | bytes 24584 | tf_op jit(solution)/shard_map/ppermute | solution.py:61
  11.8 6.0 %collective-permute-done.chunk_ref = bf16[1024,128]{1,0:T(8,128)(2,1)S(1)} collective-permute-done((bf16[1024,128]{1,0:T(8,128)(2,1)S(1)}, bf16[1024,128]{1,0:T(8,128)(2,1)S(1)}, u32[]{:S(2)}, u32[]{:S(2)}) %collective-permute-start) | collective-permute-done | bytes 262176 | tf_op jit(solution)/shard_map/ppermute | solution.py:65
  17.8 0.7 collective-permute-start.1
  18.5 1.2 %broadcast_in_dim.14.key_ref = s32[4,2,2,512,128]{4,3,2,1,0:T(8,128)S(1)} broadcast(s32[4,2,2,512]{3,2,1,0:T(2,128)S(1)} %pad_add_fusion.key_ref), dimensions={0,1,2,3} | broadcast | bytes 4227072 | tf_op jit(solution)/shard_map/broadcast_in_dim | solution.py:466
  19.7 2.3 %fetch.5 = (bf16[4,512,128]{2,1,0:T(8,128)(2,1)S(1)}, bf16[4,512,128]{2,1,0:T(8,128)(2,1)S(1)}) custom-call(s32[1]{0:T(128)} %bitcast.19.base_ref, bf16[1024,128]{1,0:T(8,128)(2,1)S(1)} %pad_maximum_fusion.1.chunk_ref, s32[4,2,2,512,128]{4,3,2,1,0:T(8,128)S(1)} %broadcast_in_dim.14.key_ref), custom_call_target="tpu_custom_call" | custom-call | flops 536870912 | bytes 5505028 | tf_op jit(solution)/shard_map/fetch/pallas_call | solution.py:35
  22.1 2.3 %fetch.6 = (bf16[4,512,128]{2,1,0:T(8,128)(2,1)S(1)}, bf16[4,512,128]{2,1,0:T(8,128)(2,1)S(1)}) custom-call(s32[1]{0:T(128)} %bitcast.18.base_ref, bf16[1024,128]{1,0:T(8,128)(2,1)S(1)} %collective-permute-done.6.chunk_ref, s32[4,2,2,512,128]{4,3,2,1,0:T(8,128)S(1)} %broadcast_in_dim.14.key_ref, bf16[4,512,128]{2,1,0:T(8,128)(2,1)S(1)} %get-tuple-element.51.refs_0_, ...), custom_call_target="tpu_custom_call" | custom-call | flops 536870912 | bytes 6553604 | tf_op jit(solution)/shard_map/fetch/pallas_call | solution.py:35
  24.4 2.3 %fetch.7 = (bf16[4,512,128]{2,1,0:T(8,128)(2,1)S(1)}, bf16[4,512,128]{2,1,0:T(8,128)(2,1)S(1)}) custom-call(s32[1]{0:T(128)} %bitcast.17.base_ref, bf16[1024,128]{1,0:T(8,128)(2,1)S(1)} %collective-permute-done.chunk_ref, s32[4,2,2,512,128]{4,3,2,1,0:T(8,128)S(1)} %broadcast_in_dim.14.key_ref, bf16[4,512,128]{2,1,0:T(8,128)(2,1)S(1)} %get-tuple-element.53.refs_0_, ...), custom_call_target="tpu_custom_call" | custom-call | flops 536870912 | bytes 6553604 | tf_op jit(solution)/shard_map/fetch/pallas_call | solution.py:35
  26.8 1.3 %fetch.9 = bf16[4,512,128]{2,1,0:T(8,128)(2,1)S(1)} custom-call(s32[1]{0:T(128)} %bitcast.6.base_ref, bf16[1024,128]{1,0:T(8,128)(2,1)S(1)} %collective-permute-done.1.chunk_ref, s32[4,2,2,512,128]{4,3,2,1,0:T(8,128)S(1)} %broadcast_in_dim.14.key_ref, bf16[4,512,128]{2,1,0:T(8,128)(2,1)S(1)} %get-tuple-element.56.refs_0_), custom_call_target="tpu_custom_call" | custom-call | flops 268435456 | bytes 5505028 | tf_op jit(solution)/shard_map/fetch/pallas_call | solution.py:35
  28.1 1.3 %fetch.8.left_ref = bf16[4,512,128]{2,1,0:T(8,128)(2,1)S(1)} custom-call(s32[1]{0:T(128)} %bitcast.6.base_ref, bf16[1024,128]{1,0:T(8,128)(2,1)S(1)} %collective-permute-done.1.chunk_ref, s32[4,2,2,512,128]{4,3,2,1,0:T(8,128)S(1)} %broadcast_in_dim.14.key_ref, bf16[4,512,128]{2,1,0:T(8,128)(2,1)S(1)} %get-tuple-element.55.refs_0_), custom_call_target="tpu_custom_call" | custom-call | flops 268435456 | bytes 5505028 | tf_op jit(solution)/shard_map/fetch/pallas_call | solution.py:35
  30.1 1.6 %collective-permute-start.8 = (bf16[512,128]{1,0:T(8,128)(2,1)S(1)}, bf16[512,128]{1,0:T(8,128)(2,1)S(1)}, u32[]{:S(2)}, u32[]{:S(2)}) collective-permute-start(bf16[512,128]{1,0:T(8,128)(2,1)S(1)} %get-tuple-element.58), channel_id=1, source_target_pairs={{0,8},{8,0},{16,24},{24,16},{1,9},{9,1},{17,25},{25,17},{2,10},{10... | collective-permute-start | bytes 393224 | tf_op jit(solution)/shard_map/ppermute | solution.py:61
  31.7 1.5 %collective-permute-start.9 = (bf16[512,128]{1,0:T(8,128)(2,1)S(1)}, bf16[512,128]{1,0:T(8,128)(2,1)S(1)}, u32[]{:S(2)}, u32[]{:S(2)}) collective-permute-start(bf16[512,128]{1,0:T(8,128)(2,1)S(1)} %get-tuple-element.59), channel_id=1, source_target_pairs={{0,16},{8,24},{16,0},{24,8},{1,17},{9,25},{17,1},{25,9},{2,18},{10... | collective-permute-start | bytes 393224 | tf_op jit(solution)/shard_map/ppermute | solution.py:61
  33.8 2.3 %collective-permute-done.8.refs_1_ = bf16[512,128]{1,0:T(8,128)(2,1)S(1)} collective-permute-done((bf16[512,128]{1,0:T(8,128)(2,1)S(1)}, bf16[512,128]{1,0:T(8,128)(2,1)S(1)}, u32[]{:S(2)}, u32[]{:S(2)}) %collective-permute-start.8) | collective-permute-done | bytes 131104 | tf_op jit(solution)/shard_map/ppermute | solution.py:61
  36.1 3.7 %collective-permute-done.9.refs_2_ = bf16[512,128]{1,0:T(8,128)(2,1)S(1)} collective-permute-done((bf16[512,128]{1,0:T(8,128)(2,1)S(1)}, bf16[512,128]{1,0:T(8,128)(2,1)S(1)}, u32[]{:S(2)}, u32[]{:S(2)}) %collective-permute-start.9) | collective-permute-done | bytes 131104 | tf_op jit(solution)/shard_map/ppermute | solution.py:61
  39.8 0.7 copy-done.10
  40.4 0.7 copy-done.12
  41.1 1.6 %copy-done.8 = bf16[512,2048]{1,0:T(8,128)(2,1)S(1)} copy-done((bf16[512,2048]{1,0:T(8,128)(2,1)S(1)}, bf16[512,2048]{1,0:T(8,128)(2,1)}, u32[]{:S(2)}) %copy-start.8) | copy-done | bytes 2097176
  42.7 0.9 copy-done.11
  43.6 0.9 copy-done.13
  44.5 14.1 %sequence.1 = (bf16[512,512]{1,0:T(8,128)(2,1)}, bf16[512,128]{1,0:T(8,128)(2,1)S(1)}, bf16[512,128]{1,0:T(8,128)(2,1)S(1)}, bf16[512,128]{1,0:T(8,128)(2,1)S(1)...) custom-call(s32[4]{0:T(128)S(1)} %pad_add_fusion.3.block_ref, ...), custom_call_target="tpu_custom_call" | custom-call | flops 4294967296 | bytes 9177108 | tf_op jit(solution)/shard_map/sequence/pallas_call | solution.py:35
  58.6 0.8 copy-done.2
  59.4 0.8 copy-done.4
  60.9 0.7 copy-done.14
  61.6 0.7 copy-done.15
  62.8 1.5 %collective-permute-start.12 = (bf16[512,128]{1,0:T(8,128)(2,1)}, bf16[512,128]{1,0:T(8,128)(2,1)S(1)}, u32[]{:S(2)}, u32[]{:S(2)}) collective-permute-start(bf16[512,128]{1,0:T(8,128)(2,1)} %copy-done.15), channel_id=1, source_target_pairs={{0,16},{8,24},{16,0},{24,8},{1,17},{9,25},{17,1},{25,9},{2,18},{10... | collective-permute-start | bytes 393224 | tf_op jit(solution)/shard_map/ppermute | solution.py:61
  64.3 1.4 %collective-permute-start.13 = (bf16[512,128]{1,0:T(8,128)(2,1)}, bf16[512,128]{1,0:T(8,128)(2,1)S(1)}, u32[]{:S(2)}, u32[]{:S(2)}) collective-permute-start(bf16[512,128]{1,0:T(8,128)(2,1)} %copy-done.14), channel_id=1, source_target_pairs={{0,24},{8,16},{16,8},{24,0},{1,25},{9,17},{17,9},{25,1},{2,26},{10... | collective-permute-start | bytes 393224 | tf_op jit(solution)/shard_map/ppermute | solution.py:61
  65.8 1.0 copy-done.1
  66.9 1.0 copy-done.3
  67.9 1.0 copy-done.5
  68.9 2.1 %weight_grad.1 = (f32[2,128,640]{2,1,0:T(8,128)S(1)}, bf16[2,128,640]{2,1,0:T(8,128)(2,1)S(1)}, f32[2,128,640]{2,1,0:T(8,128)S(1)}, bf16[2,128,640]{2,1,0:T(8,128)(2,1)S(1)}) custom-call(s32[3]{0:T(128)S(1)} %pad_add_fusion.4.place_ref, bf16[512,512]{1,0:T(8,128)(2,1)S(1)} %copy-done.3, bf16[512,2048]{1,0:T(8,128)(2,1)S(1)} %get-tuple-element.67.d_ref, ...), custom_call_target="tpu_custom_call" | custom-call | flops 939524096 | bytes 6946828 | tf_op jit(solution)/shard_map/weight_grad/pallas_call | solution.py:35
  71.1 1.0 collective-permute-done.13
  72.3 0.9 collective-permute-start.16
  73.1 1.5 %collective-permute-start.17 = (bf16[2,128,640]{2,1,0:T(8,128)(2,1)S(1)}, bf16[2,128,640]{2,1,0:T(8,128)(2,1)S(1)}, u32[]{:S(2)}, u32[]{:S(2)}) collective-permute-start(bf16[2,128,640]{2,1,0:T(8,128)(2,1)S(1)} %get-tuple-element.73), channel_id=1, source_target_pairs={{0,16},{8,24},{16,0},{24,8},{1,17},{9,25},{17,1},{25,9},{2,18},{10... | collective-permute-start | bytes 983048 | tf_op jit(solution)/shard_map/ppermute | solution.py:61
  74.7 1.2 %gather_grad.7.refs_1_ = bf16[1024,128]{1,0:T(8,128)(2,1)S(1)} custom-call(s32[1]{0:T(128)} %bitcast.6.base_ref, s32[4,2,2,512]{3,2,1,0:T(2,128)S(1)} %pad_add_fusion.key_ref, bf16[4,512,128]{2,1,0:T(8,128)(2,1)S(1)} %pad_maximum_fusion.refs_0_), custom_call_target="tpu_custom_call" | custom-call | flops 1073741824 | bytes 819204 | tf_op jit(solution)/shard_map/gather_grad/pallas_call | solution.py:35
  76.0 1.2 %gather_grad.6.refs_1_ = bf16[1024,128]{1,0:T(8,128)(2,1)S(1)} custom-call(s32[1]{0:T(128)} %bitcast.17.base_ref, s32[4,2,2,512]{3,2,1,0:T(2,128)S(1)} %pad_add_fusion.key_ref, bf16[4,512,128]{2,1,0:T(8,128)(2,1)S(1)} %pad_maximum_fusion.refs_0_), custom_call_target="tpu_custom_call" | custom-call | flops 1073741824 | bytes 819204 | tf_op jit(solution)/shard_map/gather_grad/pallas_call | solution.py:35
  77.2 5.2 %collective-permute-done.16.refs_2_ = bf16[2,128,640]{2,1,0:T(8,128)(2,1)S(1)} collective-permute-done((bf16[2,128,640]{2,1,0:T(8,128)(2,1)S(1)}, bf16[2,128,640]{2,1,0:T(8,128)(2,1)S(1)}, u32[]{:S(2)}, u32[]{:S(2)}) %collective-permute-start.16) | collective-permute-done | bytes 327712 | tf_op jit(solution)/shard_map/ppermute | solution.py:61
  82.9 1.5 %gather_grad.11 = bf16[1024,128]{1,0:T(8,128)(2,1)S(1)} custom-call(s32[1]{0:T(128)} %bitcast.6.base_ref, s32[4,2,2,512]{3,2,1,0:T(2,128)S(1)} %pad_add_fusion.key_ref, bf16[4,512,128]{2,1,0:T(8,128)(2,1)S(1)} %collective-permute-done.15.refs_1_.refs_0_, bf16[1024,128]{1,0:T(8,128)(2,1)S(1)} %gather_grad.7.refs_1_), custom_call_target="tpu_custom_call" | custom-call | flops 1073741824 | bytes 1081348 | tf_op jit(solution)/shard_map/gather_grad/pallas_call | solution.py:35
  84.4 1.5 %collective-permute-start.19 = (bf16[1024,128]{1,0:T(8,128)(2,1)S(1)}, bf16[1024,128]{1,0:T(8,128)(2,1)S(1)}, u32[]{:S(2)}, u32[]{:S(2)}) collective-permute-start(bf16[1024,128]{1,0:T(8,128)(2,1)S(1)} %gather_grad.11), channel_id=1, source_target_pairs={{0,2},{1,3},{2,0},{3,1},{4,6},{5,7},{6,4},{7,5},{8,10},{9,11},{10,... | collective-permute-start | bytes 786440 | tf_op jit(solution)/shard_map/ppermute | solution.py:65
  85.9 2.3 %gather_grad.9 = bf16[1024,128]{1,0:T(8,128)(2,1)S(1)} custom-call(s32[1]{0:T(128)} %bitcast.18.base_ref, s32[4,2,2,512]{3,2,1,0:T(2,128)S(1)} %pad_add_fusion.key_ref, bf16[4,512,128]{2,1,0:T(8,128)(2,1)S(1)} %pad_maximum_fusion.refs_0_, bf16[4,512,128]{2,1,0:T(8,128)(2,1)S(1)} %collective-permute-done.15.refs_1_.refs_0_), custom_call_target="tpu_custom_call" | custom-call | flops 2147483648 | bytes 1343492 | tf_op jit(solution)/shard_map/gather_grad/pallas_call | solution.py:35
  88.2 0.7 collective-permute-start.18
  88.9 1.2 %gather_grad.10 = f32[1024,128]{1,0:T(8,128)S(1)} custom-call(s32[1]{0:T(128)} %bitcast.17.base_ref, s32[4,2,2,512]{3,2,1,0:T(2,128)S(1)} %pad_add_fusion.key_ref, bf16[4,512,128]{2,1,0:T(8,128)(2,1)S(1)} %collective-permute-done.15.refs_1_.refs_0_, bf16[1024,128]{1,0:T(8,128)(2,1)S(1)} %gather_grad.6.refs_1_), custom_call_target="tpu_custom_call" | custom-call | flops 1073741824 | bytes 1343492 | tf_op jit(solution)/shard_map/gather_grad/pallas_call | solution.py:35
  90.1 3.6 %collective-permute-done.19 = bf16[1024,128]{1,0:T(8,128)(2,1)S(1)} collective-permute-done((bf16[1024,128]{1,0:T(8,128)(2,1)S(1)}, bf16[1024,128]{1,0:T(8,128)(2,1)S(1)}, u32[]{:S(2)}, u32[]{:S(2)}) %collective-permute-start.19) | collective-permute-done | bytes 262176 | tf_op jit(solution)/shard_map/ppermute | solution.py:65
  93.8 3.5 %collective-permute-start.20 = (bf16[1024,128]{1,0:T(8,128)(2,1)S(1)}, bf16[1024,128]{1,0:T(8,128)(2,1)S(1)}, u32[]{:S(2)}, u32[]{:S(2)}) collective-permute-start(bf16[1024,128]{1,0:T(8,128)(2,1)S(1)} %add_convert_fusion), channel_id=1, source_target_pairs={{0,4},{1,5},{2,6},{3,7},{4,0},{5,1},{6,2},{7,3},{8,12},{9,13},{10,... | collective-permute-start | bytes 786440 | tf_op jit(solution)/shard_map/ppermute | solution.py:65
  97.4 0.8 fold.1
  98.1 1.6 %collective-permute-start.21 = (bf16[1,128,640]{2,1,0:T(8,128)(2,1)S(1)}, bf16[1,128,640]{2,1,0:T(8,128)(2,1)S(1)}, u32[]{:S(2)}, u32[]{:S(2)}) collective-permute-start(bf16[1,128,640]{2,1,0:T(8,128)(2,1)S(1)} %get-tuple-element.83), channel_id=1, source_target_pairs={{0,16},{8,24},{16,0},{24,8},{1,17},{9,25},{17,1},{25,9},{2,18},{10... | collective-permute-start | bytes 491528 | tf_op jit(solution)/shard_map/ppermute | solution.py:61
  100.3 2.3 %gather_grad.8 = f32[1024,128]{1,0:T(8,128)S(1)} custom-call(s32[1]{0:T(128)} %bitcast.19.base_ref, s32[4,2,2,512]{3,2,1,0:T(2,128)S(1)} %pad_add_fusion.key_ref, bf16[4,512,128]{2,1,0:T(8,128)(2,1)S(1)} %pad_maximum_fusion.refs_0_, bf16[4,512,128]{2,1,0:T(8,128)(2,1)S(1)} %collective-permute-done.15.refs_1_.refs_0_), custom_call_target="tpu_custom_call" | custom-call | flops 2147483648 | bytes 1605636 | tf_op jit(solution)/shard_map/gather_grad/pallas_call | solution.py:35
  102.6 0.9 collective-permute-done.21.refs_2_
  103.5 1.5 %collective-permute-done.22.refs_3_ = bf16[1,128,640]{2,1,0:T(8,128)(2,1)S(1)} collective-permute-done((bf16[1,128,640]{2,1,0:T(8,128)(2,1)S(1)}, bf16[1,128,640]{2,1,0:T(8,128)(2,1)S(1)}, u32[]{:S(2)}, u32[]{:S(2)}) %collective-permute-start.22) | collective-permute-done | bytes 163872 | tf_op jit(solution)/shard_map/ppermute | solution.py:61
  105.8 0.9 collective-permute-start.24
  106.7 3.5 %collective-permute-start.25 = (bf16[64,640]{1,0:T(8,128)(2,1)S(1)}, bf16[64,640]{1,0:T(8,128)(2,1)S(1)}, u32[]{:S(2)}, u32[]{:S(2)}) collective-permute-start(bf16[64,640]{1,0:T(8,128)(2,1)S(1)} %get-tuple-element.90), channel_id=1, source_target_pairs={{0,6},{1,7},{2,4},{3,5},{4,2},{5,3},{6,0},{7,1},{8,14},{9,15},{10,... | collective-permute-start | bytes 245768 | tf_op jit(solution)/shard_map/ppermute | solution.py:65
  110.2 1.0 collective-permute-done.23.refs_1_
  111.7 1.9 %collective-permute-done.25.refs_3_ = bf16[64,640]{1,0:T(8,128)(2,1)S(1)} collective-permute-done((bf16[64,640]{1,0:T(8,128)(2,1)S(1)}, bf16[64,640]{1,0:T(8,128)(2,1)S(1)}, u32[]{:S(2)}, u32[]{:S(2)}) %collective-permute-start.25) | collective-permute-done | bytes 81952 | tf_op jit(solution)/shard_map/ppermute | solution.py:65
  113.6 1.4 %collective-permute-start.28 = (bf16[64,640]{1,0:T(8,128)(2,1)S(1)}, bf16[64,640]{1,0:T(8,128)(2,1)S(1)}, u32[]{:S(2)}, u32[]{:S(2)}) collective-permute-start(bf16[64,640]{1,0:T(8,128)(2,1)S(1)} %add_up.1.refs_0_), channel_id=1, source_target_pairs={{0,24},{8,16},{16,8},{24,0},{1,25},{9,17},{17,9},{25,1},{2,26},{10... | collective-permute-start | bytes 245768 | tf_op jit(solution)/shard_map/ppermute | solution.py:61
  115.0 1.2 collective-permute-start.27
  116.2 0.9 collective-permute-start.26
  117.1 0.8 fusion.2
  118.0 1.1 collective-permute-done.28.refs_3_
  119.0 0.8 collective-permute-done.27.refs_2_
  119.9 0.8 collective-permute-done.26.refs_1_
  120.7 1.5 %assemble.1 = (f32[64,2048]{1,0:T(8,128)}, f32[64,512]{1,0:T(8,128)}) custom-call(s32[4]{0:T(128)S(1)} %pad_add_fusion.3.block_ref, bf16[64,640]{1,0:T(8,128)(2,1)S(1)} %add_up.1.refs_0_, bf16[64,640]{1,0:T(8,128)(2,1)S(1)} %collective-permute-done.26.refs_1_, bf16[64,640]{1,0:T(8,128)(2,1)S(1)} %collective-permute-done.27.refs_2_, ...), custom_call_target="tpu_custom_call" | custom-call | bytes 983056 | tf_op jit(solution)/shard_map/assemble/pallas_call | solution.py:35
  (63 shorter events, 6.1 us)
Async XLA Ops:
  1.7 16.1 %collective-permute-start = (bf16[1024,128]{1,0:T(8,128)(2,1)S(1)}, bf16[1024,128]{1,0:T(8,128)(2,1)S(1)}, u32[]{:S(2)}, u32[]{:S(2)}) collective-permute-start(bf16[1024,128]{1,0:T(8,128)(2,1)S(1)} %pad_maximum_fusion.1.chunk_ref), channel_id=1, source_target_pairs={{0,4},{1,5},{2,6},{3,7},{4,0},{5,1},{6,2},{7,3},{8,12},{9,13},{10,... | collective-permute-start | bytes 786440 | tf_op jit(solution)/shard_map/ppermute | solution.py:65
  6.5 1.7 %collective-permute-start.2 = (s32[2,512]{1,0:T(2,128)S(1)}, s32[2,512]{1,0:T(2,128)S(1)}, u32[]{:S(2)}, u32[]{:S(2)}) collective-permute-start(s32[2,512]{1,0:T(2,128)S(1)} %get-tuple-element.102), channel_id=1, source_target_pairs={{0,1},{1,0},{2,3},{3,2},{4,5},{5,4},{6,7},{7,6},{8,9},{9,8},{10,11... | collective-permute-start | bytes 12296 | tf_op jit(solution)/shard_map/ppermute | solution.py:68
  6.6 15.5 %collective-permute-start.6 = (bf16[1024,128]{1,0:T(8,128)(2,1)S(1)}, bf16[1024,128]{1,0:T(8,128)(2,1)S(1)}, u32[]{:S(2)}, u32[]{:S(2)}) collective-permute-start(bf16[1024,128]{1,0:T(8,128)(2,1)S(1)} %pad_maximum_fusion.1.chunk_ref), channel_id=1, source_target_pairs={{0,2},{1,3},{2,0},{3,1},{4,6},{5,7},{6,4},{7,5},{8,10},{9,11},{10,... | collective-permute-start | bytes 786440 | tf_op jit(solution)/shard_map/ppermute | solution.py:65
  8.2 10.2 %collective-permute-start.4 = (s32[2,2,512]{2,1,0:T(2,128)S(1)}, s32[2,2,512]{2,1,0:T(2,128)S(1)}, u32[]{:S(2)}, u32[]{:S(2)}) collective-permute-start(s32[2,2,512]{2,1,0:T(2,128)S(1)} %get-tuple-element.100), channel_id=1, source_target_pairs={{0,16},{8,24},{16,0},{24,8},{1,17},{9,25},{17,1},{25,9},{2,18},{10... | collective-permute-start | bytes 24584 | tf_op jit(solution)/shard_map/ppermute | solution.py:61
  9.8 8.6 %collective-permute-start.3 = (s32[2,2,512]{2,1,0:T(2,128)S(1)}, s32[2,2,512]{2,1,0:T(2,128)S(1)}, u32[]{:S(2)}, u32[]{:S(2)}) collective-permute-start(s32[2,2,512]{2,1,0:T(2,128)S(1)} %get-tuple-element.100), channel_id=1, source_target_pairs={{0,8},{8,0},{16,24},{24,16},{1,9},{9,1},{17,25},{25,17},{2,10},{10... | collective-permute-start | bytes 24584 | tf_op jit(solution)/shard_map/ppermute | solution.py:61
  11.3 7.1 %collective-permute-start.5 = (s32[2,2,512]{2,1,0:T(2,128)S(1)}, s32[2,2,512]{2,1,0:T(2,128)S(1)}, u32[]{:S(2)}, u32[]{:S(2)}) collective-permute-start(s32[2,2,512]{2,1,0:T(2,128)S(1)} %get-tuple-element.100), channel_id=1, source_target_pairs={{0,24},{8,16},{16,8},{24,0},{1,25},{9,17},{17,9},{25,1},{2,26},{10... | collective-permute-start | bytes 24584 | tf_op jit(solution)/shard_map/ppermute | solution.py:61
  17.8 9.0 %collective-permute-start.1 = (bf16[1024,128]{1,0:T(8,128)(2,1)S(1)}, bf16[1024,128]{1,0:T(8,128)(2,1)S(1)}, u32[]{:S(2)}, u32[]{:S(2)}) collective-permute-start(bf16[1024,128]{1,0:T(8,128)(2,1)S(1)} %collective-permute-done.chunk_ref), channel_id=1, source_target_pairs={{0,2},{1,3},{2,0},{3,1},{4,6},{5,7},{6,4},{7,5},{8,10},{9,11},{10,... | collective-permute-start | bytes 786440 | tf_op jit(solution)/shard_map/ppermute | solution.py:65
  28.0 2.0 %collective-permute-start.7 = (bf16[4,512,128]{2,1,0:T(8,128)(2,1)S(1)}, bf16[4,512,128]{2,1,0:T(8,128)(2,1)S(1)}, u32[]{:S(2)}, u32[]{:S(2)}) collective-permute-start(bf16[4,512,128]{2,1,0:T(8,128)(2,1)S(1)} %fetch.9), channel_id=1, source_target_pairs={{0,1},{1,0},{2,3},{3,2},{4,5},{5,4},{6,7},{7,6},{8,9},{9,8},{10,11... | collective-permute-start | bytes 1572872 | tf_op jit(solution)/shard_map/ppermute | solution.py:68
  28.1 13.0 %copy-start = (bf16[512,512]{1,0:T(8,128)(2,1)S(1)}, bf16[512,512]{1,0:T(8,128)(2,1)}, u32[]{:S(2)}) copy-start(bf16[512,512]{1,0:T(8,128)(2,1)} %c_ref.1) | copy-start | bytes 1572868
  28.1 13.0 %copy-start.9 = (bf16[512,512]{1,0:T(8,128)(2,1)S(1)}, bf16[512,512]{1,0:T(8,128)(2,1)}, u32[]{:S(2)}) copy-start(bf16[512,512]{1,0:T(8,128)(2,1)} %wo_ref.1) | copy-start | bytes 1572868
  28.1 13.0 %copy-start.17 = (f32[512]{0:T(512)S(1)}, f32[512]{0:T(512)}, u32[]{:S(2)}) copy-start(f32[512]{0:T(512)} %param.16) | copy-start | bytes 6148
  30.1 5.9 %collective-permute-start.8 = (bf16[512,128]{1,0:T(8,128)(2,1)S(1)}, bf16[512,128]{1,0:T(8,128)(2,1)S(1)}, u32[]{:S(2)}, u32[]{:S(2)}) collective-permute-start(bf16[512,128]{1,0:T(8,128)(2,1)S(1)} %get-tuple-element.58), channel_id=1, source_target_pairs={{0,8},{8,0},{16,24},{24,16},{1,9},{9,1},{17,25},{25,17},{2,10},{10... | collective-permute-start | bytes 393224 | tf_op jit(solution)/shard_map/ppermute | solution.py:61
  31.7 8.1 %collective-permute-start.9 = (bf16[512,128]{1,0:T(8,128)(2,1)S(1)}, bf16[512,128]{1,0:T(8,128)(2,1)S(1)}, u32[]{:S(2)}, u32[]{:S(2)}) collective-permute-start(bf16[512,128]{1,0:T(8,128)(2,1)S(1)} %get-tuple-element.59), channel_id=1, source_target_pairs={{0,16},{8,24},{16,0},{24,8},{1,17},{9,25},{17,1},{25,9},{2,18},{10... | collective-permute-start | bytes 393224 | tf_op jit(solution)/shard_map/ppermute | solution.py:61
  33.2 7.2 %collective-permute-start.10 = (bf16[512,128]{1,0:T(8,128)(2,1)S(1)}, bf16[512,128]{1,0:T(8,128)(2,1)S(1)}, u32[]{:S(2)}, u32[]{:S(2)}) collective-permute-start(bf16[512,128]{1,0:T(8,128)(2,1)S(1)} %get-tuple-element.60), channel_id=1, source_target_pairs={{0,24},{8,16},{16,8},{24,0},{1,25},{9,17},{17,9},{25,1},{2,26},{10... | collective-permute-start | bytes 393224 | tf_op jit(solution)/shard_map/ppermute | solution.py:61
  39.8 0.7 copy-start.10
  40.4 0.7 copy-start.12
  41.1 1.6 %copy-start.8 = (bf16[512,2048]{1,0:T(8,128)(2,1)S(1)}, bf16[512,2048]{1,0:T(8,128)(2,1)}, u32[]{:S(2)}) copy-start(bf16[512,2048]{1,0:T(8,128)(2,1)} %wp_ref.1) | copy-start | bytes 6291460
  42.7 0.9 copy-start.11
  43.6 0.9 copy-start.13
  58.6 0.8 copy-start.2
  59.4 0.8 copy-start.4
  60.2 0.6 copy-start.6
  60.9 0.7 copy-start.14
  61.5 0.7 copy-start.15
  61.5 0.7 copy-start.16
  62.2 3.6 %collective-permute-start.14 = (bf16[4,256,640]{2,1,0:T(8,128)(2,1)}, bf16[4,256,640]{2,1,0:T(8,128)(2,1)S(1)}, u32[]{:S(2)}, u32[]{:S(2)}) collective-permute-start(bf16[4,256,640]{2,1,0:T(8,128)(2,1)} %get-tuple-element.69), channel_id=1, source_target_pairs={{0,1},{1,0},{2,3},{3,2},{4,5},{5,4},{6,7},{7,6},{8,9},{9,8},{10,11... | collective-permute-start | bytes 3932168 | tf_op jit(solution)/shard_map/ppermute | solution.py:68
  62.2 8.8 %collective-permute-start.11 = (bf16[512,128]{1,0:T(8,128)(2,1)}, bf16[512,128]{1,0:T(8,128)(2,1)S(1)}, u32[]{:S(2)}, u32[]{:S(2)}) collective-permute-start(bf16[512,128]{1,0:T(8,128)(2,1)} %copy-done.16), channel_id=1, source_target_pairs={{0,8},{8,0},{16,24},{24,16},{1,9},{9,1},{17,25},{25,17},{2,10},{10... | collective-permute-start | bytes 393224 | tf_op jit(solution)/shard_map/ppermute | solution.py:61
  62.8 8.3 %collective-permute-start.12 = (bf16[512,128]{1,0:T(8,128)(2,1)}, bf16[512,128]{1,0:T(8,128)(2,1)S(1)}, u32[]{:S(2)}, u32[]{:S(2)}) collective-permute-start(bf16[512,128]{1,0:T(8,128)(2,1)} %copy-done.15), channel_id=1, source_target_pairs={{0,16},{8,24},{16,0},{24,8},{1,17},{9,25},{17,1},{25,9},{2,18},{10... | collective-permute-start | bytes 393224 | tf_op jit(solution)/shard_map/ppermute | solution.py:61
  64.3 7.8 %collective-permute-start.13 = (bf16[512,128]{1,0:T(8,128)(2,1)}, bf16[512,128]{1,0:T(8,128)(2,1)S(1)}, u32[]{:S(2)}, u32[]{:S(2)}) collective-permute-start(bf16[512,128]{1,0:T(8,128)(2,1)} %copy-done.14), channel_id=1, source_target_pairs={{0,24},{8,16},{16,8},{24,0},{1,25},{9,17},{17,9},{25,1},{2,26},{10... | collective-permute-start | bytes 393224 | tf_op jit(solution)/shard_map/ppermute | solution.py:61
  65.8 1.0 copy-start.1
  66.9 1.0 copy-start.3
  67.9 1.0 copy-start.5
  68.9 3.2 %copy-start.7 = (bf16[512,128]{1,0:T(8,128)(2,1)S(1)}, bf16[512,128]{1,0:T(8,128)(2,1)}, u32[]{:S(2)}) copy-start(bf16[512,128]{1,0:T(8,128)(2,1)} %copy-done.6) | copy-start | bytes 393220
  72.2 10.7 %collective-permute-start.15 = (bf16[4,512,128]{2,1,0:T(8,128)(2,1)S(1)}, bf16[4,512,128]{2,1,0:T(8,128)(2,1)S(1)}, u32[]{:S(2)}, u32[]{:S(2)}) collective-permute-start(bf16[4,512,128]{2,1,0:T(8,128)(2,1)S(1)} %pad_maximum_fusion.refs_0_), channel_id=1, source_target_pairs={{0,1},{1,0},{2,3},{3,2},{4,5},{5,4},{6,7},{7,6},{8,9},{9,8},{10,11... | collective-permute-start | bytes 1572872 | tf_op jit(solution)/shard_map/ppermute | solution.py:68
  72.3 10.1 %collective-permute-start.16 = (bf16[2,128,640]{2,1,0:T(8,128)(2,1)S(1)}, bf16[2,128,640]{2,1,0:T(8,128)(2,1)S(1)}, u32[]{:S(2)}, u32[]{:S(2)}) collective-permute-start(bf16[2,128,640]{2,1,0:T(8,128)(2,1)S(1)} %get-tuple-element.71), channel_id=1, source_target_pairs={{0,8},{8,0},{16,24},{24,16},{1,9},{9,1},{17,25},{25,17},{2,10},{10... | collective-permute-start | bytes 983048 | tf_op jit(solution)/shard_map/ppermute | solution.py:61
  73.1 9.8 %collective-permute-start.17 = (bf16[2,128,640]{2,1,0:T(8,128)(2,1)S(1)}, bf16[2,128,640]{2,1,0:T(8,128)(2,1)S(1)}, u32[]{:S(2)}, u32[]{:S(2)}) collective-permute-start(bf16[2,128,640]{2,1,0:T(8,128)(2,1)S(1)} %get-tuple-element.73), channel_id=1, source_target_pairs={{0,16},{8,24},{16,0},{24,8},{1,17},{9,25},{17,1},{25,9},{2,18},{10... | collective-permute-start | bytes 983048 | tf_op jit(solution)/shard_map/ppermute | solution.py:61
  84.4 9.3 %collective-permute-start.19 = (bf16[1024,128]{1,0:T(8,128)(2,1)S(1)}, bf16[1024,128]{1,0:T(8,128)(2,1)S(1)}, u32[]{:S(2)}, u32[]{:S(2)}) collective-permute-start(bf16[1024,128]{1,0:T(8,128)(2,1)S(1)} %gather_grad.11), channel_id=1, source_target_pairs={{0,2},{1,3},{2,0},{3,1},{4,6},{5,7},{6,4},{7,5},{8,10},{9,11},{10,... | collective-permute-start | bytes 786440 | tf_op jit(solution)/shard_map/ppermute | solution.py:65
  88.2 21.9 %collective-permute-start.18 = (bf16[1024,128]{1,0:T(8,128)(2,1)S(1)}, bf16[1024,128]{1,0:T(8,128)(2,1)S(1)}, u32[]{:S(2)}, u32[]{:S(2)}) collective-permute-start(bf16[1024,128]{1,0:T(8,128)(2,1)S(1)} %gather_grad.9), channel_id=1, source_target_pairs={{0,2},{1,3},{2,0},{3,1},{4,6},{5,7},{6,4},{7,5},{8,10},{9,11},{10,... | collective-permute-start | bytes 786440 | tf_op jit(solution)/shard_map/ppermute | solution.py:65
  93.8 16.4 %collective-permute-start.20 = (bf16[1024,128]{1,0:T(8,128)(2,1)S(1)}, bf16[1024,128]{1,0:T(8,128)(2,1)S(1)}, u32[]{:S(2)}, u32[]{:S(2)}) collective-permute-start(bf16[1024,128]{1,0:T(8,128)(2,1)S(1)} %add_convert_fusion), channel_id=1, source_target_pairs={{0,4},{1,5},{2,6},{3,7},{4,0},{5,1},{6,2},{7,3},{8,12},{9,13},{10,... | collective-permute-start | bytes 786440 | tf_op jit(solution)/shard_map/ppermute | solution.py:65
  98.1 5.4 %collective-permute-start.21 = (bf16[1,128,640]{2,1,0:T(8,128)(2,1)S(1)}, bf16[1,128,640]{2,1,0:T(8,128)(2,1)S(1)}, u32[]{:S(2)}, u32[]{:S(2)}) collective-permute-start(bf16[1,128,640]{2,1,0:T(8,128)(2,1)S(1)} %get-tuple-element.83), channel_id=1, source_target_pairs={{0,16},{8,24},{16,0},{24,8},{1,17},{9,25},{17,1},{25,9},{2,18},{10... | collective-permute-start | bytes 491528 | tf_op jit(solution)/shard_map/ppermute | solution.py:61
  99.7 5.3 %collective-permute-start.22 = (bf16[1,128,640]{2,1,0:T(8,128)(2,1)S(1)}, bf16[1,128,640]{2,1,0:T(8,128)(2,1)S(1)}, u32[]{:S(2)}, u32[]{:S(2)}) collective-permute-start(bf16[1,128,640]{2,1,0:T(8,128)(2,1)S(1)} %get-tuple-element.84), channel_id=1, source_target_pairs={{0,8},{8,0},{16,24},{24,16},{1,9},{9,1},{17,25},{25,17},{2,10},{10... | collective-permute-start | bytes 491528 | tf_op jit(solution)/shard_map/ppermute | solution.py:61
  105.7 5.5 %collective-permute-start.23 = (bf16[64,640]{1,0:T(8,128)(2,1)S(1)}, bf16[64,640]{1,0:T(8,128)(2,1)S(1)}, u32[]{:S(2)}, u32[]{:S(2)}) collective-permute-start(bf16[64,640]{1,0:T(8,128)(2,1)S(1)} %get-tuple-element.88), channel_id=1, source_target_pairs={{0,2},{1,3},{2,0},{3,1},{4,6},{5,7},{6,4},{7,5},{8,10},{9,11},{10,... | collective-permute-start | bytes 245768 | tf_op jit(solution)/shard_map/ppermute | solution.py:65
  105.8 5.9 %collective-permute-start.24 = (bf16[64,640]{1,0:T(8,128)(2,1)S(1)}, bf16[64,640]{1,0:T(8,128)(2,1)S(1)}, u32[]{:S(2)}, u32[]{:S(2)}) collective-permute-start(bf16[64,640]{1,0:T(8,128)(2,1)S(1)} %get-tuple-element.89), channel_id=1, source_target_pairs={{0,4},{1,5},{2,6},{3,7},{4,0},{5,1},{6,2},{7,3},{8,12},{9,13},{10,... | collective-permute-start | bytes 245768 | tf_op jit(solution)/shard_map/ppermute | solution.py:65
  106.7 6.9 %collective-permute-start.25 = (bf16[64,640]{1,0:T(8,128)(2,1)S(1)}, bf16[64,640]{1,0:T(8,128)(2,1)S(1)}, u32[]{:S(2)}, u32[]{:S(2)}) collective-permute-start(bf16[64,640]{1,0:T(8,128)(2,1)S(1)} %get-tuple-element.90), channel_id=1, source_target_pairs={{0,6},{1,7},{2,4},{3,5},{4,2},{5,3},{6,0},{7,1},{8,14},{9,15},{10,... | collective-permute-start | bytes 245768 | tf_op jit(solution)/shard_map/ppermute | solution.py:65
  113.6 5.4 %collective-permute-start.28 = (bf16[64,640]{1,0:T(8,128)(2,1)S(1)}, bf16[64,640]{1,0:T(8,128)(2,1)S(1)}, u32[]{:S(2)}, u32[]{:S(2)}) collective-permute-start(bf16[64,640]{1,0:T(8,128)(2,1)S(1)} %add_up.1.refs_0_), channel_id=1, source_target_pairs={{0,24},{8,16},{16,8},{24,0},{1,25},{9,17},{17,9},{25,1},{2,26},{10... | collective-permute-start | bytes 245768 | tf_op jit(solution)/shard_map/ppermute | solution.py:61
  115.0 4.9 %collective-permute-start.27 = (bf16[64,640]{1,0:T(8,128)(2,1)S(1)}, bf16[64,640]{1,0:T(8,128)(2,1)S(1)}, u32[]{:S(2)}, u32[]{:S(2)}) collective-permute-start(bf16[64,640]{1,0:T(8,128)(2,1)S(1)} %add_up.1.refs_0_), channel_id=1, source_target_pairs={{0,16},{8,24},{16,0},{24,8},{1,17},{9,25},{17,1},{25,9},{2,18},{10... | collective-permute-start | bytes 245768 | tf_op jit(solution)/shard_map/ppermute | solution.py:61
  116.2 4.4 %collective-permute-start.26 = (bf16[64,640]{1,0:T(8,128)(2,1)S(1)}, bf16[64,640]{1,0:T(8,128)(2,1)S(1)}, u32[]{:S(2)}, u32[]{:S(2)}) collective-permute-start(bf16[64,640]{1,0:T(8,128)(2,1)S(1)} %add_up.1.refs_0_), channel_id=1, source_target_pairs={{0,8},{8,0},{16,24},{24,16},{1,9},{9,1},{17,25},{25,17},{2,10},{10... | collective-permute-start | bytes 245768 | tf_op jit(solution)/shard_map/ppermute | solution.py:61

commit v6 on v5

--- a/solution.py
+++ b/solution.py
@@ -68,19 +68,27 @@
         return lax.ppermute(value, "sparse", [(i, i ^ 1) for i in range(self.shards)])
 
 
-def fetch(keys, cohorts, chunk, base, before=()):
+R, Z, C = range(3)
+
+
+def first_row(ids, step, cores, rows):
+    return ((ids[Z] ^ step) * cores + ids[C]) * rows
+
+
+def fetch(ids, keys, cohorts, chunk, step, before=()):
     many = len(cohorts)
-    count, _, _, tokens, _ = keys.shape
+    count, cores, _, tokens, _ = keys.shape
     rows, cols = chunk.shape[0] // 2, chunk.shape[1]
 
-    def body(base_ref, chunk_ref, key_ref, *refs):
+    def body(ids, chunk_ref, key_ref, *refs):
         before_refs, out_refs = refs[:-many], refs[-many:]
+        base = first_row(ids, step, cores, rows)
         lane = lax.broadcasted_iota(I32, (tokens, LANES), 1)
         for i, m in enumerate(cohorts):
             for k in range(count):
                 hot = []
                 for table in range(2):
-                    place = key_ref[k, m, table] - base_ref[0]
+                    place = key_ref[k, m, table] - base
                     for start in range(0, rows, LANES):
                         hot.append(jnp.where(place == lane + start, 1.0, 0.0).astype(BF16))
                 found = dot(jnp.concatenate(hot, axis=1), chunk_ref[...])
@@ -92,7 +100,7 @@
         "fetch",
         body,
         [((count, tokens, cols), BF16)] * many,
-        [base.reshape(1), chunk, keys, *before],
+        [ids, chunk, keys, *before],
         smem=1,
         flops=2 * many * count * tokens * rows * cols,
     )
@@ -109,12 +117,38 @@
     return run("combine", body, [(tuple(shape), BF16)] * count, parts)
 
 
-def gather_grad(keys, cohorts, tokens, base, rows, before=(), out=BF16):
+def pack(parts):
+    def body(*refs):
+        for k, ref in enumerate(refs[:-1]):
+            refs[-1][k] = ref[...]
+
+    shape, dtype = parts[0].shape, parts[0].dtype
+    return run("pack", body, [((len(parts), *shape), dtype)], parts)[0]
+
+
+def add_up(parts, cuts=1, out=BF16):
+    rows, cols = parts[0].shape
+    tall = rows // cuts
+
+    def body(*refs):
+        part_refs, out_refs = refs[: len(parts)], refs[len(parts) :]
+        for i in range(cuts):
+            span = slice(i * tall, (i + 1) * tall)
+            total = part_refs[0][span, :].astype(F32)
+            for ref in part_refs[1:]:
+                total = total + ref[span, :].astype(F32)
+            out_refs[i][...] = total.astype(out)
+
+    return run("add_up", body, [((tall, cols), out)] * cuts, parts)
+
+
+def gather_grad(ids, keys, cohorts, tokens, step, rows, before=(), out=BF16):
     many = len(cohorts)
-    count, _, _, length = keys.shape
+    count, cores, _, length = keys.shape
     cols = tokens[0].shape[-1]
 
-    def body(base_ref, key_ref, *refs):
+    def body(ids, key_ref, *refs):
+        base = first_row(ids, step, cores, rows)
         piece_refs, before_refs, out_ref = refs[:many], refs[many:-1], refs[-1]
         row = lax.broadcasted_iota(I32, (rows, length), 0)
         for table in range(2):
@@ -123,7 +157,7 @@
             for i, m in enumerate(cohorts):
                 hot = []
                 for k in range(count):
-                    place = key_ref[k, m, table : table + 1, :] - base_ref[0]
+                    place = key_ref[k, m, table : table + 1, :] - base
                     hot.append(jnp.where(place == row, 1.0, 0.0).astype(BF16))
                 piece = piece_refs[i][...].reshape(count * length, cols)
                 part = dot(jnp.concatenate(hot, axis=1), piece)
@@ -136,13 +170,13 @@
         "gather_grad",
         body,
         [((2 * rows, cols), out)],
-        [base.reshape(1), keys, *tokens, *before],
+        [ids, keys, *tokens, *before],
         smem=1,
         flops=4 * many * count * length * 2 * rows * cols,
     )[0]
 
 
-def sequence(blocks, other, pieces, cotangent, gain, w_proj, w_out, cores, line):
+def sequence(ids, pieces, cotangent, gain, w_proj, w_out, cores, line):
     count = len(pieces)
     length, width = cotangent.shape
     cols = width // count
@@ -151,14 +185,14 @@
     tile = min(256, length)
     step = min(256, 4 * width)
 
-    def body(block_ref, other_ref, cot_ref, wo_ref, wp_ref, gain_ref, *refs):
+    def body(ids, cot_ref, wo_ref, wp_ref, gain_ref, *refs):
         piece_refs, refs = refs[:count], refs[count:]
         out_ref, *grad_refs = refs[: count + 1]
         normed_ref, dproj_ref, gated_ref, weight_ref = refs[count + 1 : count + 5]
         emb, act, slope, att, attn, dscale, dkey, dval, tok = refs[count + 5 :]
 
         for k in range(count):
-            emb[block_ref[k]] = piece_refs[k][...]
+            emb[ids[R] ^ k] = piece_refs[k][...]
 
         def embedded(span):
             return jnp.concatenate([emb[k, span] for k in range(count)], axis=1).astype(F32)
@@ -239,9 +273,10 @@
                 tok[k, span] = grad[:, k * cols : (k + 1) * cols].astype(BF16)
 
         for k in range(count):
-            grad_refs[k][...] = tok[block_ref[k]]
-
-        sums = weight_sums(other_ref[0], normed_ref, dproj_ref, gated_ref, cot_ref, cores, line, count)
+            grad_refs[k][...] = tok[ids[R] ^ k]
+
+        other = (ids[C] + 1) % cores
+        sums = weight_sums(other, normed_ref, dproj_ref, gated_ref, cot_ref, cores, line, count)
         for k in range(count):
             weight_ref[k] = next(sums).astype(BF16)
 
@@ -256,8 +291,8 @@
             ((length, width), BF16),
             ((count, width // cores, 5 * width // count), BF16),
         ],
-        [blocks, other, cotangent, w_out, w_proj, gain, *pieces],
-        smem=2,
+        [ids, cotangent, w_out, w_proj, gain, *pieces],
+        smem=1,
         vmem=24,
         flops=32 * length * width * width,
         scratch=[
@@ -296,30 +331,30 @@
         yield parts[0] if len(parts) == 1 else jnp.concatenate(parts, axis=1)
 
 
-def weight_grad(place, normed, dproj, gated, cotangent, before, line):
+def weight_grad(ids, normed, dproj, gated, cotangent, before, line):
     blocks, half, cols = before.shape
     length, width = normed.shape
     cores = width // half
     bits = blocks.bit_length() - 1
     tall = half // bits
 
-    def body(place_ref, n_ref, d_ref, g_ref, c_ref, before_ref, *refs):
+    def body(ids, n_ref, d_ref, g_ref, c_ref, before_ref, *refs):
         out_refs, scratch = refs[:-1], refs[-1]
-        sums = weight_sums(place_ref[0], n_ref, d_ref, g_ref, c_ref, cores, line, blocks)
+        sums = weight_sums(ids[C], n_ref, d_ref, g_ref, c_ref, cores, line, blocks)
         for k in range(blocks):
             total = next(sums) + before_ref[k].astype(F32)
             for p in range(bits):
                 at = sum((k >> (p + i) % bits & 1) << bits - 1 - i for i in range(bits))
                 scratch[p, at] = total[p * tall : (p + 1) * tall]
         for p in range(bits):
-            split_halves(scratch.at[p], place_ref[1 + p], out_refs[2 * p : 2 * p + 2])
+            split_halves(scratch.at[p], ids[R] >> p & 1, out_refs[2 * p : 2 * p + 2])
 
     kept = (blocks // 2, tall, cols)
     return run(
         "weight_grad",
         body,
         [(kept, F32), (kept, BF16)] * bits,
-        [place, normed, dproj, gated, cotangent, before],
+        [ids, normed, dproj, gated, cotangent, before],
         smem=1,
         scratch=[pltpu.VMEM((bits, blocks, tall, cols), F32)],
         flops=2 * length * half * (blocks * cols + 2 * width),
@@ -334,71 +369,61 @@
             out_ref[k] = ref[start + k].astype(out_ref.dtype)
 
 
-def fold(bits, kept, came):
+def fold(ids, kept, came, step):
     count, tall, cols = kept[0].shape
     many = len(kept)
 
-    def body(bit_ref, *refs):
+    def body(ids, *refs):
         kept_refs, came_refs, out_refs = refs[:many], refs[many : 2 * many], refs[2 * many : -1]
         scratch = refs[-1]
         for p in range(many):
             for k in range(count):
                 scratch[p, k] = kept_refs[p][k] + came_refs[p][k].astype(F32)
-            split_halves(scratch.at[p], bit_ref[p], out_refs[2 * p : 2 * p + 2])
+            split_halves(scratch.at[p], ids[R] >> (p + step) % many & 1, out_refs[2 * p : 2 * p + 2])
 
     half = (count // 2, tall, cols)
     return run(
         "fold",
         body,
         [(half, F32), (half, BF16)] * many,
-        [bits, *kept, *came],
+        [ids, *kept, *came],
         smem=1,
         scratch=[pltpu.VMEM((many, count, tall, cols), F32)],
     )
 
 
-def cut_line(planes, kept, came):
+def cut_line(ids, kept, came, line):
     _, tall, cols = kept[0].shape
-    many, line = len(kept), planes.shape[0]
+    many = len(kept)
     rows = many * tall // line
 
-    def body(plane_ref, *refs):
+    def body(ids, *refs):
         kept_refs, came_refs, out_refs = refs[:many], refs[many : 2 * many], refs[2 * many : -1]
         scratch = refs[-1]
         for p in range(many):
             scratch[p * tall : (p + 1) * tall] = kept_refs[p][0] + came_refs[p][0].astype(F32)
         for k in range(line):
-            span = pl.ds(pl.multiple_of(plane_ref[k] * rows, rows), rows)
+            span = pl.ds(pl.multiple_of((ids[Z] ^ k) * rows, rows), rows)
             out_refs[k][...] = scratch[span].astype(out_refs[k].dtype)
 
     return run(
         "cut_line",
         body,
         [((rows, cols), F32)] + [((rows, cols), BF16)] * (line - 1),
-        [planes, *kept, *came],
+        [ids, *kept, *came],
         smem=1,
         scratch=[pltpu.VMEM((many * tall, cols), F32)],
     )
 
 
-def add_up(parts):
-    def body(*refs):
-        total = refs[0][...].astype(F32)
-        for ref in refs[1:-1]:
-            total = total + ref[...].astype(F32)
-        refs[-1][...] = total.astype(BF16)
-
-    return run("add_up", body, [(parts[0].shape, BF16)], parts)[0]
-
-
-def assemble(blocks, parts, edge):
+def assemble(ids, parts, edge):
     rows, cols = parts[0].shape
     total = cols * len(parts)
 
-    def body(block_ref, *refs):
+    def body(ids, *refs):
         part_refs, (left_ref, right_ref, held) = refs[: len(parts)], refs[len(parts) :]
         for k, ref in enumerate(part_refs):
-            held[block_ref[k]] = ref[...].astype(F32)
+            held[ids[R] ^ k] = ref[...].astype(F32)
         for k in range(len(parts)):
             first, last = k * cols, (k + 1) * cols
             cut = min(max(edge - first, 0), cols)
@@ -411,7 +436,7 @@
         "assemble",
         body,
         [((rows, edge), F32), ((rows, total - edge), F32)],
-        [blocks, *parts],
+        [ids, *parts],
         smem=1,
         scratch=[pltpu.VMEM((len(parts), rows, cols), F32)],
     )
@@ -436,9 +461,7 @@
 
     bits = replicas.bit_length() - 1
     swaps = [3, 1, 2] if replicas == 4 else list(range(1, replicas))
-    blocks = jnp.stack([grid.r ^ k for k in range(replicas)]).astype(I32)
-    planes = jnp.stack([grid.z ^ k for k in range(line)]).astype(I32)
-    bases = [(((grid.z ^ k) * cores + grid.c) * rows).astype(I32) for k in range(line)]
+    ids = jnp.stack([grid.r, grid.z, grid.c]).astype(I32)
 
     own = jnp.concatenate(
         [
@@ -468,34 +491,24 @@
 
     found = ()
     for k in order[:-1]:
-        found = fetch(key_cols, both, held[k], bases[k], found)
+        found = fetch(ids, key_cols, both, held[k], k, found)
     last = order[-1]
-    there = fetch(key_cols, both[1:], held[last], bases[last], found[1:])
-    here = fetch(key_cols, both[:1], held[last], bases[last], found[:1])
+    there = fetch(ids, key_cols, both[1:], held[last], last, found[1:])
+    here = fetch(ids, key_cols, both[:1], held[last], last, found[:1])
     pieces = combine([here[0], grid.over_pair(there[0])])
     for k in swaps:
         pieces[k] = grid.over_replica(pieces[k], k)
 
-    layer_out, *rest = sequence(
-        blocks,
-        ((grid.c + 1) % cores).astype(I32).reshape(1),
-        pieces,
-        cotangent,
-        input_norm_gain.reshape(1, width),
-        w_proj,
-        w_out,
-        cores,
-        line,
-    )
+    gain = input_norm_gain.reshape(1, width)
+    layer_out, *rest = sequence(ids, pieces, cotangent, gain, w_proj, w_out, cores, line)
     tokens, (normed, dproj, gated, weights) = rest[:replicas], rest[replicas:]
     for k in swaps:
         tokens[k] = grid.over_replica(tokens[k], k)
 
-    place = jnp.stack([grid.c] + [grid.r >> p & 1 for p in range(bits)]).astype(I32)
     weights = grid.over_pair(weights)
-    weights = weight_grad(place, normed, dproj, gated, cotangent, weights, line)
+    weights = weight_grad(ids, normed, dproj, gated, cotangent, weights, line)
     tokens = lax.optimization_barrier((tokens, weights))[0]
-    tokens = jnp.stack(tokens)
+    tokens = pack(tokens)
     there = grid.over_pair(tokens)
 
     def swap_weights(weights, step):
@@ -503,8 +516,7 @@
         return kept, [grid.over_replica(sent[p], 1 << (p + step) % bits) for p in range(bits)]
 
     kept, came = swap_weights(weights, 0)
-    first = {k: gather_grad(keys, both[:1], [tokens], bases[k], rows) for k in order[-2:]}
-    there = lax.optimization_barrier((there, came, first))[0]
+    first = {k: gather_grad(ids, keys, both[:1], [tokens], k, rows) for k in order[-2:]}
 
     sums = {}
     for k in reversed(order):
@@ -512,28 +524,29 @@
         steps = [1 << i for i in range(low.bit_length() - 1)]
         out = F32 if steps else BF16
         if k in first:
-            total = gather_grad(keys, both[1:], [there], bases[k], rows, [first[k]], out)
+            sums[k] = gather_grad(ids, keys, both[1:], [there], k, rows, [first[k]], out)
         else:
-            total = gather_grad(keys, both, [tokens, there], bases[k], rows, out=out)
-        for step in steps:
-            total = total + grid.over_line(sums[k ^ step], step).astype(F32)
-        sums[k] = total.astype(BF16) if k else total
-    table_grad = sums[0]
+            if k == 1:
+                there = lax.optimization_barrier((there, came))[0]
+            sums[k] = gather_grad(ids, keys, both, [tokens, there], k, rows, out=out)
+        if steps:
+            parts = [sums[k]] + [grid.over_line(sums[k ^ step], step) for step in steps]
+            sums[k] = add_up(parts, 1, BF16)[0] if k else add_up(parts, 2, F32)
+    item_grad, action_grad = sums[0]
 
     for step in range(1, bits + 1):
         after = sums[last] if step < bits else sums[line // 2]
         came = lax.optimization_barrier((came, after))[0]
         if step < bits:
-            turn = jnp.stack([grid.r >> (p + step) % bits & 1 for p in range(bits)])
-            kept, came = swap_weights(fold(turn.astype(I32), kept, came), step)
-    parts = cut_line(planes, kept, came)
+            kept, came = swap_weights(fold(ids, kept, came, step), step)
+    parts = cut_line(ids, kept, came, line)
     parts = [parts[0]] + [grid.over_line(parts[k], k) for k in range(1, line)]
-    parts = lax.optimization_barrier((parts, table_grad))[0]
-    total = add_up(parts)
+    parts = lax.optimization_barrier((parts, item_grad))[0]
+    total = add_up(parts)[0]
     parts = [total] + [grid.over_replica(total, k) for k in range(1, replicas)]
-    grad_proj, grad_out = assemble(blocks, parts, 4 * width)
-
-    return layer_out, table_grad[:rows], table_grad[rows:], grad_proj, grad_out
+    grad_proj, grad_out = assemble(ids, parts, 4 * width)
+
+    return layer_out, item_grad, action_grad, grad_proj, grad_out
 
 
 def solution(mesh):

time: 122 us -> 114 us (0.934)
  local copies, waits for them, and re-layouts: 14.5 us -> 2.25 us
  Pallas kernels: 38.6 us -> 45.2 us
  waiting for transfers between devices: 31.4 us -> 29.9 us
    unnamed x36 -> x8, local copies, waits for them, and re-layouts: 11.5 us -> 0.03 us
    pallas_call x18 -> x21, Pallas kernels: 38.6 us -> 45.2 us  [run(): pl.pallas_call(body, out_shape=outs, in_specs=places, out_specs=[in_vmem]...]
    ppermute x16, waiting for transfers between devices: 17.9 us -> 15.3 us  [over_replica(): return lax.ppermute(value, 'replica', [(i, i ^ step) for i in range(n)])]
    ppermute x9, waiting for transfers between devices: 12.9 us -> 14.5 us  [over_line(): return lax.ppermute(value, 'sparse', pairs)]
  transfers between devices with their start and end apart: 29 -> 29, of which waited for: 16 -> 13; matrix products, arithmetic and copies ran while one was open for 3% -> 2% of each run, Pallas kernels for 17% -> 25%
where the time goes in v6:
time: 114 us
  Pallas kernels  45.2 us (40%)
  starting transfers between devices  34.9 us (31%)
  waiting for transfers between devices  29.9 us (26%)
  local copies, waits for them, and re-layouts  2.25 us (2%)
    pallas_call x21, Pallas kernels, run(): pl.pallas_call(body, out_shape=outs, in_specs=places, out_specs=[in_vmem]...  45.2 us
    ppermute x16, starting transfers between devices, over_replica(): return lax.ppermute(value, 'replica', [(i, i ^ step) for i in range(n)])  18.6 us
    ppermute x9, starting transfers between devices, over_line(): return lax.ppermute(value, 'sparse', pairs)  16 us
    ppermute x16, waiting for transfers between devices, over_replica(): return lax.ppermute(value, 'replica', [(i, i ^ step) for i in range(n)])  15.3 us
    ppermute x9, waiting for transfers between devices, over_line(): return lax.ppermute(value, 'sparse', pairs)  14.5 us
  transfers between devices with their start and end apart: 29, of which 13 were waited for; matrix products, arithmetic and copies ran while one was open for 2% of the time, Pallas kernels for 25%

profile of v6, /device:TPU:0, one launch (start us, length us, event | category | flops | bytes accessed | tf_op | source)
XLA Modules:
  0.0 113.9 jit_solution(13818369010202258952)
XLA Ops:
  0.6 1.0 constant_dynamic-slice_fusion
  1.7 4.1 %collective-permute-start = (bf16[1024,128]{1,0:T(8,128)(2,1)S(1)}, bf16[1024,128]{1,0:T(8,128)(2,1)S(1)}, u32[]{:S(2)}, u32[]{:S(2)}) collective-permute-start(bf16[1024,128]{1,0:T(8,128)(2,1)S(1)} %pad_maximum_fusion.chunk_ref), channel_id=1, source_target_pairs={{0,4},{1,5},{2,6},{3,7},{4,0},{5,1},{6,2},{7,3},{8,12},{9,13},{10,... | collective-permute-start | bytes 786440 | tf_op jit(solution)/shard_map/ppermute | solution.py:65
  5.8 0.7 add_bitcast_fusion
  6.5 0.1 collective-permute-start.2
  6.6 1.6 %collective-permute-start.6 = (bf16[1024,128]{1,0:T(8,128)(2,1)S(1)}, bf16[1024,128]{1,0:T(8,128)(2,1)S(1)}, u32[]{:S(2)}, u32[]{:S(2)}) collective-permute-start(bf16[1024,128]{1,0:T(8,128)(2,1)S(1)} %pad_maximum_fusion.chunk_ref), channel_id=1, source_target_pairs={{0,2},{1,3},{2,0},{3,1},{4,6},{5,7},{6,4},{7,5},{8,10},{9,11},{10,... | collective-permute-start | bytes 786440 | tf_op jit(solution)/shard_map/ppermute | solution.py:65
  8.2 1.6 %collective-permute-start.4 = (s32[2,2,512]{2,1,0:T(2,128)S(1)}, s32[2,2,512]{2,1,0:T(2,128)S(1)}, u32[]{:S(2)}, u32[]{:S(2)}) collective-permute-start(s32[2,2,512]{2,1,0:T(2,128)S(1)} %get-tuple-element.102), channel_id=1, source_target_pairs={{0,16},{8,24},{16,0},{24,8},{1,17},{9,25},{17,1},{25,9},{2,18},{10... | collective-permute-start | bytes 24584 | tf_op jit(solution)/shard_map/ppermute | solution.py:61
  9.8 1.5 %collective-permute-start.3 = (s32[2,2,512]{2,1,0:T(2,128)S(1)}, s32[2,2,512]{2,1,0:T(2,128)S(1)}, u32[]{:S(2)}, u32[]{:S(2)}) collective-permute-start(s32[2,2,512]{2,1,0:T(2,128)S(1)} %get-tuple-element.102), channel_id=1, source_target_pairs={{0,8},{8,0},{16,24},{24,16},{1,9},{9,1},{17,25},{25,17},{2,10},{10... | collective-permute-start | bytes 24584 | tf_op jit(solution)/shard_map/ppermute | solution.py:61
  11.3 0.5 collective-permute-start.5
  11.8 0.1 pad_add_fusion.3.ids
  11.9 5.9 %collective-permute-done.chunk_ref = bf16[1024,128]{1,0:T(8,128)(2,1)S(1)} collective-permute-done((bf16[1024,128]{1,0:T(8,128)(2,1)S(1)}, bf16[1024,128]{1,0:T(8,128)(2,1)S(1)}, u32[]{:S(2)}, u32[]{:S(2)}) %collective-permute-start) | collective-permute-done | bytes 262176 | tf_op jit(solution)/shard_map/ppermute | solution.py:65
  17.8 0.7 collective-permute-start.1
  18.5 1.2 %broadcast_in_dim.14.key_ref = s32[4,2,2,512,128]{4,3,2,1,0:T(8,128)S(1)} broadcast(s32[4,2,2,512]{3,2,1,0:T(2,128)S(1)} %pad_add_fusion.key_ref), dimensions={0,1,2,3} | broadcast | bytes 4227072 | tf_op jit(solution)/shard_map/broadcast_in_dim | solution.py:489
  19.7 2.9 %fetch.5 = (bf16[4,512,128]{2,1,0:T(8,128)(2,1)S(1)}, bf16[4,512,128]{2,1,0:T(8,128)(2,1)S(1)}) custom-call(s32[3]{0:T(128)S(1)} %pad_add_fusion.3.ids, bf16[1024,128]{1,0:T(8,128)(2,1)S(1)} %pad_maximum_fusion.chunk_ref, s32[4,2,2,512,128]{4,3,2,1,0:T(8,128)S(1)} %broadcast_in_dim.14.key_ref), custom_call_target="tpu_custom_call" | custom-call | flops 536870912 | bytes 5505036 | tf_op jit(solution)/shard_map/fetch/pallas_call | solution.py:35
  22.6 2.9 %fetch.6 = (bf16[4,512,128]{2,1,0:T(8,128)(2,1)S(1)}, bf16[4,512,128]{2,1,0:T(8,128)(2,1)S(1)}) custom-call(s32[3]{0:T(128)S(1)} %pad_add_fusion.3.ids, bf16[1024,128]{1,0:T(8,128)(2,1)S(1)} %collective-permute-done.6.chunk_ref, s32[4,2,2,512,128]{4,3,2,1,0:T(8,128)S(1)} %broadcast_in_dim.14.key_ref, bf16[4,512,128]{2,1,0:T(8,128)(2,1)S(1)} %get-tuple-element.53.refs_0_, ...), custom_call_target="tpu_custom_call" | custom-call | flops 536870912 | bytes 6553612 | tf_op jit(solution)/shard_map/fetch/pallas_call | solution.py:35
  25.5 2.9 %fetch.7 = (bf16[4,512,128]{2,1,0:T(8,128)(2,1)S(1)}, bf16[4,512,128]{2,1,0:T(8,128)(2,1)S(1)}) custom-call(s32[3]{0:T(128)S(1)} %pad_add_fusion.3.ids, bf16[1024,128]{1,0:T(8,128)(2,1)S(1)} %collective-permute-done.chunk_ref, s32[4,2,2,512,128]{4,3,2,1,0:T(8,128)S(1)} %broadcast_in_dim.14.key_ref, bf16[4,512,128]{2,1,0:T(8,128)(2,1)S(1)} %get-tuple-element.55.refs_0_, ...), custom_call_target="tpu_custom_call" | custom-call | flops 536870912 | bytes 6553612 | tf_op jit(solution)/shard_map/fetch/pallas_call | solution.py:35
  28.4 1.8 %fetch.9 = bf16[4,512,128]{2,1,0:T(8,128)(2,1)S(1)} custom-call(s32[3]{0:T(128)S(1)} %pad_add_fusion.3.ids, bf16[1024,128]{1,0:T(8,128)(2,1)S(1)} %collective-permute-done.1.chunk_ref, s32[4,2,2,512,128]{4,3,2,1,0:T(8,128)S(1)} %broadcast_in_dim.14.key_ref, bf16[4,512,128]{2,1,0:T(8,128)(2,1)S(1)} %get-tuple-element.58.refs_0_), custom_call_target="tpu_custom_call" | custom-call | flops 268435456 | bytes 5505036 | tf_op jit(solution)/shard_map/fetch/pallas_call | solution.py:35
  30.2 0.1 collective-permute-start.7
  30.3 1.8 %fetch.8.left_ref = bf16[4,512,128]{2,1,0:T(8,128)(2,1)S(1)} custom-call(s32[3]{0:T(128)S(1)} %pad_add_fusion.3.ids, bf16[1024,128]{1,0:T(8,128)(2,1)S(1)} %collective-permute-done.1.chunk_ref, s32[4,2,2,512,128]{4,3,2,1,0:T(8,128)S(1)} %broadcast_in_dim.14.key_ref, bf16[4,512,128]{2,1,0:T(8,128)(2,1)S(1)} %get-tuple-element.57.refs_0_), custom_call_target="tpu_custom_call" | custom-call | flops 268435456 | bytes 5505036 | tf_op jit(solution)/shard_map/fetch/pallas_call | solution.py:35
  32.1 0.1 collective-permute-done.7.right_ref
  32.1 0.1 combine.1
  32.3 1.6 %collective-permute-start.8 = (bf16[512,128]{1,0:T(8,128)(2,1)S(1)}, bf16[512,128]{1,0:T(8,128)(2,1)S(1)}, u32[]{:S(2)}, u32[]{:S(2)}) collective-permute-start(bf16[512,128]{1,0:T(8,128)(2,1)S(1)} %get-tuple-element.60), channel_id=1, source_target_pairs={{0,8},{8,0},{16,24},{24,16},{1,9},{9,1},{17,25},{25,17},{2,10},{10... | collective-permute-start | bytes 393224 | tf_op jit(solution)/shard_map/ppermute | solution.py:61
  33.8 1.5 %collective-permute-start.9 = (bf16[512,128]{1,0:T(8,128)(2,1)S(1)}, bf16[512,128]{1,0:T(8,128)(2,1)S(1)}, u32[]{:S(2)}, u32[]{:S(2)}) collective-permute-start(bf16[512,128]{1,0:T(8,128)(2,1)S(1)} %get-tuple-element.61), channel_id=1, source_target_pairs={{0,16},{8,24},{16,0},{24,8},{1,17},{9,25},{17,1},{25,9},{2,18},{10... | collective-permute-start | bytes 393224 | tf_op jit(solution)/shard_map/ppermute | solution.py:61
  35.4 0.5 collective-permute-start.10
  35.8 2.7 %collective-permute-done.8.refs_1_ = bf16[512,128]{1,0:T(8,128)(2,1)S(1)} collective-permute-done((bf16[512,128]{1,0:T(8,128)(2,1)S(1)}, bf16[512,128]{1,0:T(8,128)(2,1)S(1)}, u32[]{:S(2)}, u32[]{:S(2)}) %collective-permute-start.8) | collective-permute-done | bytes 131104 | tf_op jit(solution)/shard_map/ppermute | solution.py:61
  38.5 3.7 %collective-permute-done.9.refs_2_ = bf16[512,128]{1,0:T(8,128)(2,1)S(1)} collective-permute-done((bf16[512,128]{1,0:T(8,128)(2,1)S(1)}, bf16[512,128]{1,0:T(8,128)(2,1)S(1)}, u32[]{:S(2)}, u32[]{:S(2)}) %collective-permute-start.9) | collective-permute-done | bytes 131104 | tf_op jit(solution)/shard_map/ppermute | solution.py:61
  42.2 13.7 %sequence.1 = (bf16[512,512]{1,0:T(8,128)(2,1)}, bf16[512,128]{1,0:T(8,128)(2,1)S(1)}, bf16[512,128]{1,0:T(8,128)(2,1)S(1)}, bf16[512,128]{1,0:T(8,128)(2,1)S(1)...) custom-call(s32[3]{0:T(128)S(1)} %pad_add_fusion.3.ids, ...), custom_call_target="tpu_custom_call" | custom-call | flops 4294967296 | bytes 9177100 | tf_op jit(solution)/shard_map/sequence/pallas_call | solution.py:35
  55.9 1.2 %collective-permute-start.11 = (bf16[512,128]{1,0:T(8,128)(2,1)S(1)}, bf16[512,128]{1,0:T(8,128)(2,1)S(1)}, u32[]{:S(2)}, u32[]{:S(2)}) collective-permute-start(bf16[512,128]{1,0:T(8,128)(2,1)S(1)} %get-tuple-element.65), channel_id=1, source_target_pairs={{0,8},{8,0},{16,24},{24,16},{1,9},{9,1},{17,25},{25,17},{2,10},{10... | collective-permute-start | bytes 393224 | tf_op jit(solution)/shard_map/ppermute | solution.py:61
  57.1 0.8 collective-permute-start.12
  58.0 1.4 %collective-permute-start.13 = (bf16[512,128]{1,0:T(8,128)(2,1)S(1)}, bf16[512,128]{1,0:T(8,128)(2,1)S(1)}, u32[]{:S(2)}, u32[]{:S(2)}) collective-permute-start(bf16[512,128]{1,0:T(8,128)(2,1)S(1)} %get-tuple-element.67), channel_id=1, source_target_pairs={{0,24},{8,16},{16,8},{24,0},{1,25},{9,17},{17,9},{25,1},{2,26},{10... | collective-permute-start | bytes 393224 | tf_op jit(solution)/shard_map/ppermute | solution.py:61
  59.4 2.3 %weight_grad.1 = (f32[2,128,640]{2,1,0:T(8,128)S(1)}, bf16[2,128,640]{2,1,0:T(8,128)(2,1)S(1)}, f32[2,128,640]{2,1,0:T(8,128)S(1)}, bf16[2,128,640]{2,1,0:T(8,128)(2,1)S(1)}) custom-call(s32[3]{0:T(128)S(1)} %pad_add_fusion.3.ids, bf16[512,512]{1,0:T(8,128)(2,1)S(1)} %get-tuple-element.68.n_ref, bf16[512,2048]{1,0:T(8,128)(2,1)S(1)} %get-tuple-element.69.d_ref, ...), custom_call_target="tpu_custom_call" | custom-call | flops 939524096 | bytes 6946828 | tf_op jit(solution)/shard_map/weight_grad/pallas_call | solution.py:35
  61.7 0.5 collective-permute-done.11.refs_1_
  62.2 1.8 %collective-permute-done.12.refs_2_ = bf16[512,128]{1,0:T(8,128)(2,1)S(1)} collective-permute-done((bf16[512,128]{1,0:T(8,128)(2,1)S(1)}, bf16[512,128]{1,0:T(8,128)(2,1)S(1)}, u32[]{:S(2)}, u32[]{:S(2)}) %collective-permute-start.12) | collective-permute-done | bytes 131104 | tf_op jit(solution)/shard_map/ppermute | solution.py:61
  63.9 1.6 %collective-permute-done.13.refs_3_ = bf16[512,128]{1,0:T(8,128)(2,1)S(1)} collective-permute-done((bf16[512,128]{1,0:T(8,128)(2,1)S(1)}, bf16[512,128]{1,0:T(8,128)(2,1)S(1)}, u32[]{:S(2)}, u32[]{:S(2)}) %collective-permute-start.13) | collective-permute-done | bytes 131104 | tf_op jit(solution)/shard_map/ppermute | solution.py:61
  65.6 0.1 collective-permute-start.15
  65.7 0.9 collective-permute-start.16
  66.5 1.5 %collective-permute-start.17 = (bf16[2,128,640]{2,1,0:T(8,128)(2,1)S(1)}, bf16[2,128,640]{2,1,0:T(8,128)(2,1)S(1)}, u32[]{:S(2)}, u32[]{:S(2)}) collective-permute-start(bf16[2,128,640]{2,1,0:T(8,128)(2,1)S(1)} %get-tuple-element.75), channel_id=1, source_target_pairs={{0,16},{8,24},{16,0},{24,8},{1,17},{9,25},{17,1},{25,9},{2,18},{10... | collective-permute-start | bytes 983048 | tf_op jit(solution)/shard_map/ppermute | solution.py:61
  68.1 1.8 %gather_grad.10.refs_1_ = bf16[1024,128]{1,0:T(8,128)(2,1)S(1)} custom-call(s32[3]{0:T(128)S(1)} %pad_add_fusion.3.ids, s32[4,2,2,512]{3,2,1,0:T(2,128)S(1)} %pad_add_fusion.key_ref, bf16[4,512,128]{2,1,0:T(8,128)(2,1)S(1)} %pack.1.refs_0_), custom_call_target="tpu_custom_call" | custom-call | flops 1073741824 | bytes 819212 | tf_op jit(solution)/shard_map/gather_grad/pallas_call | solution.py:35
  69.9 1.8 %gather_grad.8.refs_1_ = bf16[1024,128]{1,0:T(8,128)(2,1)S(1)} custom-call(s32[3]{0:T(128)S(1)} %pad_add_fusion.3.ids, s32[4,2,2,512]{3,2,1,0:T(2,128)S(1)} %pad_add_fusion.key_ref, bf16[4,512,128]{2,1,0:T(8,128)(2,1)S(1)} %pack.1.refs_0_), custom_call_target="tpu_custom_call" | custom-call | flops 1073741824 | bytes 819212 | tf_op jit(solution)/shard_map/gather_grad/pallas_call | solution.py:35
  71.7 2.0 %gather_grad.11 = bf16[1024,128]{1,0:T(8,128)(2,1)S(1)} custom-call(s32[3]{0:T(128)S(1)} %pad_add_fusion.3.ids, s32[4,2,2,512]{3,2,1,0:T(2,128)S(1)} %pad_add_fusion.key_ref, bf16[4,512,128]{2,1,0:T(8,128)(2,1)S(1)} %collective-permute-done.15.refs_1_.refs_0_, bf16[1024,128]{1,0:T(8,128)(2,1)S(1)} %gather_grad.10.refs_1_), custom_call_target="tpu_custom_call" | custom-call | flops 1073741824 | bytes 1081356 | tf_op jit(solution)/shard_map/gather_grad/pallas_call | solution.py:35
  73.7 1.5 %collective-permute-start.19 = (bf16[1024,128]{1,0:T(8,128)(2,1)S(1)}, bf16[1024,128]{1,0:T(8,128)(2,1)S(1)}, u32[]{:S(2)}, u32[]{:S(2)}) collective-permute-start(bf16[1024,128]{1,0:T(8,128)(2,1)S(1)} %gather_grad.11), channel_id=1, source_target_pairs={{0,2},{1,3},{2,0},{3,1},{4,6},{5,7},{6,4},{7,5},{8,10},{9,11},{10,... | collective-permute-start | bytes 786440 | tf_op jit(solution)/shard_map/ppermute | solution.py:65
  75.2 0.7 collective-permute-done.16.refs_2_
  75.8 0.5 collective-permute-done.17.refs_3_
  76.3 0.8 fold.1
  77.1 1.6 %collective-permute-start.21 = (bf16[1,128,640]{2,1,0:T(8,128)(2,1)S(1)}, bf16[1,128,640]{2,1,0:T(8,128)(2,1)S(1)}, u32[]{:S(2)}, u32[]{:S(2)}) collective-permute-start(bf16[1,128,640]{2,1,0:T(8,128)(2,1)S(1)} %get-tuple-element.87), channel_id=1, source_target_pairs={{0,16},{8,24},{16,0},{24,8},{1,17},{9,25},{17,1},{25,9},{2,18},{10... | collective-permute-start | bytes 491528 | tf_op jit(solution)/shard_map/ppermute | solution.py:61
  78.7 0.5 collective-permute-start.22
  79.2 2.9 %gather_grad.7 = bf16[1024,128]{1,0:T(8,128)(2,1)S(1)} custom-call(s32[3]{0:T(128)S(1)} %pad_add_fusion.3.ids, s32[4,2,2,512]{3,2,1,0:T(2,128)S(1)} %pad_add_fusion.key_ref, bf16[4,512,128]{2,1,0:T(8,128)(2,1)S(1)} %pack.1.refs_0_, bf16[4,512,128]{2,1,0:T(8,128)(2,1)S(1)} %collective-permute-done.15.refs_1_.refs_0_), custom_call_target="tpu_custom_call" | custom-call | flops 2147483648 | bytes 1343500 | tf_op jit(solution)/shard_map/gather_grad/pallas_call | solution.py:35
  82.1 1.5 %collective-permute-start.18 = (bf16[1024,128]{1,0:T(8,128)(2,1)S(1)}, bf16[1024,128]{1,0:T(8,128)(2,1)S(1)}, u32[]{:S(2)}, u32[]{:S(2)}) collective-permute-start(bf16[1024,128]{1,0:T(8,128)(2,1)S(1)} %gather_grad.7), channel_id=1, source_target_pairs={{0,2},{1,3},{2,0},{3,1},{4,6},{5,7},{6,4},{7,5},{8,10},{9,11},{10,... | collective-permute-start | bytes 786440 | tf_op jit(solution)/shard_map/ppermute | solution.py:65
  83.6 1.8 %gather_grad.9.refs_0_ = f32[1024,128]{1,0:T(8,128)S(1)} custom-call(s32[3]{0:T(128)S(1)} %pad_add_fusion.3.ids, s32[4,2,2,512]{3,2,1,0:T(2,128)S(1)} %pad_add_fusion.key_ref, bf16[4,512,128]{2,1,0:T(8,128)(2,1)S(1)} %collective-permute-done.15.refs_1_.refs_0_, bf16[1024,128]{1,0:T(8,128)(2,1)S(1)} %gather_grad.8.refs_1_), custom_call_target="tpu_custom_call" | custom-call | flops 1073741824 | bytes 1343500 | tf_op jit(solution)/shard_map/gather_grad/pallas_call | solution.py:35
  85.4 0.1 add_up.3
  85.5 2.1 %collective-permute-start.20 = (bf16[1024,128]{1,0:T(8,128)(2,1)S(1)}, bf16[1024,128]{1,0:T(8,128)(2,1)S(1)}, u32[]{:S(2)}, u32[]{:S(2)}) collective-permute-start(bf16[1024,128]{1,0:T(8,128)(2,1)S(1)} %add_up.3), channel_id=1, source_target_pairs={{0,4},{1,5},{2,6},{3,7},{4,0},{5,1},{6,2},{7,3},{8,12},{9,13},{10,... | collective-permute-start | bytes 786440 | tf_op jit(solution)/shard_map/ppermute | solution.py:65
  87.6 0.6 cut_line.1
  88.2 2.1 %collective-permute-start.23 = (bf16[64,640]{1,0:T(8,128)(2,1)S(1)}, bf16[64,640]{1,0:T(8,128)(2,1)S(1)}, u32[]{:S(2)}, u32[]{:S(2)}) collective-permute-start(bf16[64,640]{1,0:T(8,128)(2,1)S(1)} %get-tuple-element.92), channel_id=1, source_target_pairs={{0,2},{1,3},{2,0},{3,1},{4,6},{5,7},{6,4},{7,5},{8,10},{9,11},{10,... | collective-permute-start | bytes 245768 | tf_op jit(solution)/shard_map/ppermute | solution.py:65
  90.3 2.4 %collective-permute-start.25 = (bf16[64,640]{1,0:T(8,128)(2,1)S(1)}, bf16[64,640]{1,0:T(8,128)(2,1)S(1)}, u32[]{:S(2)}, u32[]{:S(2)}) collective-permute-start(bf16[64,640]{1,0:T(8,128)(2,1)S(1)} %get-tuple-element.94), channel_id=1, source_target_pairs={{0,6},{1,7},{2,4},{3,5},{4,2},{5,3},{6,0},{7,1},{8,14},{9,15},{10,... | collective-permute-start | bytes 245768 | tf_op jit(solution)/shard_map/ppermute | solution.py:65
  92.7 2.9 %gather_grad.6.refs_0_ = f32[1024,128]{1,0:T(8,128)S(1)} custom-call(s32[3]{0:T(128)S(1)} %pad_add_fusion.3.ids, s32[4,2,2,512]{3,2,1,0:T(2,128)S(1)} %pad_add_fusion.key_ref, bf16[4,512,128]{2,1,0:T(8,128)(2,1)S(1)} %pack.1.refs_0_, bf16[4,512,128]{2,1,0:T(8,128)(2,1)S(1)} %collective-permute-done.15.refs_1_.refs_0_), custom_call_target="tpu_custom_call" | custom-call | flops 2147483648 | bytes 1605644 | tf_op jit(solution)/shard_map/gather_grad/pallas_call | solution.py:35
  95.6 8.5 %collective-permute-done.20.refs_2_ = bf16[1024,128]{1,0:T(8,128)(2,1)S(1)} collective-permute-done((bf16[1024,128]{1,0:T(8,128)(2,1)S(1)}, bf16[1024,128]{1,0:T(8,128)(2,1)S(1)}, u32[]{:S(2)}, u32[]{:S(2)}) %collective-permute-start.20) | collective-permute-done | bytes 262176 | tf_op jit(solution)/shard_map/ppermute | solution.py:65
  104.1 0.8 add_up.4
  105.0 0.0 collective-permute-done.24.refs_2_
  105.1 1.4 %collective-permute-start.28 = (bf16[64,640]{1,0:T(8,128)(2,1)S(1)}, bf16[64,640]{1,0:T(8,128)(2,1)S(1)}, u32[]{:S(2)}, u32[]{:S(2)}) collective-permute-start(bf16[64,640]{1,0:T(8,128)(2,1)S(1)} %add_up.5.refs_0_), channel_id=1, source_target_pairs={{0,24},{8,16},{16,8},{24,0},{1,25},{9,17},{17,9},{25,1},{2,26},{10... | collective-permute-start | bytes 245768 | tf_op jit(solution)/shard_map/ppermute | solution.py:61
  106.5 1.5 %collective-permute-start.27 = (bf16[64,640]{1,0:T(8,128)(2,1)S(1)}, bf16[64,640]{1,0:T(8,128)(2,1)S(1)}, u32[]{:S(2)}, u32[]{:S(2)}) collective-permute-start(bf16[64,640]{1,0:T(8,128)(2,1)S(1)} %add_up.5.refs_0_), channel_id=1, source_target_pairs={{0,16},{8,24},{16,0},{24,8},{1,17},{9,25},{17,1},{25,9},{2,18},{10... | collective-permute-start | bytes 245768 | tf_op jit(solution)/shard_map/ppermute | solution.py:61
  108.0 0.6 collective-permute-start.26
  108.6 1.9 %collective-permute-done.28.refs_3_ = bf16[64,640]{1,0:T(8,128)(2,1)S(1)} collective-permute-done((bf16[64,640]{1,0:T(8,128)(2,1)S(1)}, bf16[64,640]{1,0:T(8,128)(2,1)S(1)}, u32[]{:S(2)}, u32[]{:S(2)}) %collective-permute-start.28) | collective-permute-done | bytes 81952 | tf_op jit(solution)/shard_map/ppermute | solution.py:61
  110.5 0.8 collective-permute-done.27.refs_2_
  111.3 1.1 collective-permute-done.26.refs_1_
  112.4 1.5 %assemble.1 = (f32[64,2048]{1,0:T(8,128)}, f32[64,512]{1,0:T(8,128)}) custom-call(s32[3]{0:T(128)S(1)} %pad_add_fusion.3.ids, bf16[64,640]{1,0:T(8,128)(2,1)S(1)} %add_up.5.refs_0_, bf16[64,640]{1,0:T(8,128)(2,1)S(1)} %collective-permute-done.26.refs_1_, bf16[64,640]{1,0:T(8,128)(2,1)S(1)} %collective-permute-done.27.refs_2_, ...), custom_call_target="tpu_custom_call" | custom-call | bytes 983052 | tf_op jit(solution)/shard_map/assemble/pallas_call | solution.py:35
  (31 shorter events, 0.2 us)
Async XLA Ops:
  1.7 16.1 %collective-permute-start = (bf16[1024,128]{1,0:T(8,128)(2,1)S(1)}, bf16[1024,128]{1,0:T(8,128)(2,1)S(1)}, u32[]{:S(2)}, u32[]{:S(2)}) collective-permute-start(bf16[1024,128]{1,0:T(8,128)(2,1)S(1)} %pad_maximum_fusion.chunk_ref), channel_id=1, source_target_pairs={{0,4},{1,5},{2,6},{3,7},{4,0},{5,1},{6,2},{7,3},{8,12},{9,13},{10,... | collective-permute-start | bytes 786440 | tf_op jit(solution)/shard_map/ppermute | solution.py:65
  6.5 1.7 %collective-permute-start.2 = (s32[2,512]{1,0:T(2,128)S(1)}, s32[2,512]{1,0:T(2,128)S(1)}, u32[]{:S(2)}, u32[]{:S(2)}) collective-permute-start(s32[2,512]{1,0:T(2,128)S(1)} %get-tuple-element.104), channel_id=1, source_target_pairs={{0,1},{1,0},{2,3},{3,2},{4,5},{5,4},{6,7},{7,6},{8,9},{9,8},{10,11... | collective-permute-start | bytes 12296 | tf_op jit(solution)/shard_map/ppermute | solution.py:68
  6.6 16.0 %collective-permute-start.6 = (bf16[1024,128]{1,0:T(8,128)(2,1)S(1)}, bf16[1024,128]{1,0:T(8,128)(2,1)S(1)}, u32[]{:S(2)}, u32[]{:S(2)}) collective-permute-start(bf16[1024,128]{1,0:T(8,128)(2,1)S(1)} %pad_maximum_fusion.chunk_ref), channel_id=1, source_target_pairs={{0,2},{1,3},{2,0},{3,1},{4,6},{5,7},{6,4},{7,5},{8,10},{9,11},{10,... | collective-permute-start | bytes 786440 | tf_op jit(solution)/shard_map/ppermute | solution.py:65
  8.2 10.2 %collective-permute-start.4 = (s32[2,2,512]{2,1,0:T(2,128)S(1)}, s32[2,2,512]{2,1,0:T(2,128)S(1)}, u32[]{:S(2)}, u32[]{:S(2)}) collective-permute-start(s32[2,2,512]{2,1,0:T(2,128)S(1)} %get-tuple-element.102), channel_id=1, source_target_pairs={{0,16},{8,24},{16,0},{24,8},{1,17},{9,25},{17,1},{25,9},{2,18},{10... | collective-permute-start | bytes 24584 | tf_op jit(solution)/shard_map/ppermute | solution.py:61
  9.8 8.6 %collective-permute-start.3 = (s32[2,2,512]{2,1,0:T(2,128)S(1)}, s32[2,2,512]{2,1,0:T(2,128)S(1)}, u32[]{:S(2)}, u32[]{:S(2)}) collective-permute-start(s32[2,2,512]{2,1,0:T(2,128)S(1)} %get-tuple-element.102), channel_id=1, source_target_pairs={{0,8},{8,0},{16,24},{24,16},{1,9},{9,1},{17,25},{25,17},{2,10},{10... | collective-permute-start | bytes 24584 | tf_op jit(solution)/shard_map/ppermute | solution.py:61
  11.3 7.1 %collective-permute-start.5 = (s32[2,2,512]{2,1,0:T(2,128)S(1)}, s32[2,2,512]{2,1,0:T(2,128)S(1)}, u32[]{:S(2)}, u32[]{:S(2)}) collective-permute-start(s32[2,2,512]{2,1,0:T(2,128)S(1)} %get-tuple-element.102), channel_id=1, source_target_pairs={{0,24},{8,16},{16,8},{24,0},{1,25},{9,17},{17,9},{25,1},{2,26},{10... | collective-permute-start | bytes 24584 | tf_op jit(solution)/shard_map/ppermute | solution.py:61
  17.8 10.6 %collective-permute-start.1 = (bf16[1024,128]{1,0:T(8,128)(2,1)S(1)}, bf16[1024,128]{1,0:T(8,128)(2,1)S(1)}, u32[]{:S(2)}, u32[]{:S(2)}) collective-permute-start(bf16[1024,128]{1,0:T(8,128)(2,1)S(1)} %collective-permute-done.chunk_ref), channel_id=1, source_target_pairs={{0,2},{1,3},{2,0},{3,1},{4,6},{5,7},{6,4},{7,5},{8,10},{9,11},{10,... | collective-permute-start | bytes 786440 | tf_op jit(solution)/shard_map/ppermute | solution.py:65
  30.2 2.0 %collective-permute-start.7 = (bf16[4,512,128]{2,1,0:T(8,128)(2,1)S(1)}, bf16[4,512,128]{2,1,0:T(8,128)(2,1)S(1)}, u32[]{:S(2)}, u32[]{:S(2)}) collective-permute-start(bf16[4,512,128]{2,1,0:T(8,128)(2,1)S(1)} %fetch.9), channel_id=1, source_target_pairs={{0,1},{1,0},{2,3},{3,2},{4,5},{5,4},{6,7},{7,6},{8,9},{9,8},{10,11... | collective-permute-start | bytes 1572872 | tf_op jit(solution)/shard_map/ppermute | solution.py:68
  30.3 11.9 %copy-start = (bf16[512,512]{1,0:T(8,128)(2,1)S(1)}, bf16[512,512]{1,0:T(8,128)(2,1)}, u32[]{:S(2)}) copy-start(bf16[512,512]{1,0:T(8,128)(2,1)} %c_ref.1) | copy-start | bytes 1572868
  30.3 11.9 %copy-start.1 = (bf16[512,2048]{1,0:T(8,128)(2,1)S(1)}, bf16[512,2048]{1,0:T(8,128)(2,1)}, u32[]{:S(2)}) copy-start(bf16[512,2048]{1,0:T(8,128)(2,1)} %wp_ref.1) | copy-start | bytes 6291460
  30.3 11.9 %copy-start.2 = (bf16[512,512]{1,0:T(8,128)(2,1)S(1)}, bf16[512,512]{1,0:T(8,128)(2,1)}, u32[]{:S(2)}) copy-start(bf16[512,512]{1,0:T(8,128)(2,1)} %wo_ref.1) | copy-start | bytes 1572868
  30.3 11.9 %copy-start.3 = (f32[512]{0:T(512)S(1)}, f32[512]{0:T(512)}, u32[]{:S(2)}) copy-start(f32[512]{0:T(512)} %param.16) | copy-start | bytes 6148
  32.3 6.2 %collective-permute-start.8 = (bf16[512,128]{1,0:T(8,128)(2,1)S(1)}, bf16[512,128]{1,0:T(8,128)(2,1)S(1)}, u32[]{:S(2)}, u32[]{:S(2)}) collective-permute-start(bf16[512,128]{1,0:T(8,128)(2,1)S(1)} %get-tuple-element.60), channel_id=1, source_target_pairs={{0,8},{8,0},{16,24},{24,16},{1,9},{9,1},{17,25},{25,17},{2,10},{10... | collective-permute-start | bytes 393224 | tf_op jit(solution)/shard_map/ppermute | solution.py:61
  33.8 8.4 %collective-permute-start.9 = (bf16[512,128]{1,0:T(8,128)(2,1)S(1)}, bf16[512,128]{1,0:T(8,128)(2,1)S(1)}, u32[]{:S(2)}, u32[]{:S(2)}) collective-permute-start(bf16[512,128]{1,0:T(8,128)(2,1)S(1)} %get-tuple-element.61), channel_id=1, source_target_pairs={{0,16},{8,24},{16,0},{24,8},{1,17},{9,25},{17,1},{25,9},{2,18},{10... | collective-permute-start | bytes 393224 | tf_op jit(solution)/shard_map/ppermute | solution.py:61
  35.4 6.8 %collective-permute-start.10 = (bf16[512,128]{1,0:T(8,128)(2,1)S(1)}, bf16[512,128]{1,0:T(8,128)(2,1)S(1)}, u32[]{:S(2)}, u32[]{:S(2)}) collective-permute-start(bf16[512,128]{1,0:T(8,128)(2,1)S(1)} %get-tuple-element.62), channel_id=1, source_target_pairs={{0,24},{8,16},{16,8},{24,0},{1,25},{9,17},{17,9},{25,1},{2,26},{10... | collective-permute-start | bytes 393224 | tf_op jit(solution)/shard_map/ppermute | solution.py:61
  55.9 3.5 %collective-permute-start.14 = (bf16[4,256,640]{2,1,0:T(8,128)(2,1)S(1)}, bf16[4,256,640]{2,1,0:T(8,128)(2,1)S(1)}, u32[]{:S(2)}, u32[]{:S(2)}) collective-permute-start(bf16[4,256,640]{2,1,0:T(8,128)(2,1)S(1)} %get-tuple-element.71), channel_id=1, source_target_pairs={{0,1},{1,0},{2,3},{3,2},{4,5},{5,4},{6,7},{7,6},{8,9},{9,8},{10,11... | collective-permute-start | bytes 3932168 | tf_op jit(solution)/shard_map/ppermute | solution.py:68
  55.9 6.3 %collective-permute-start.11 = (bf16[512,128]{1,0:T(8,128)(2,1)S(1)}, bf16[512,128]{1,0:T(8,128)(2,1)S(1)}, u32[]{:S(2)}, u32[]{:S(2)}) collective-permute-start(bf16[512,128]{1,0:T(8,128)(2,1)S(1)} %get-tuple-element.65), channel_id=1, source_target_pairs={{0,8},{8,0},{16,24},{24,16},{1,9},{9,1},{17,25},{25,17},{2,10},{10... | collective-permute-start | bytes 393224 | tf_op jit(solution)/shard_map/ppermute | solution.py:61
  57.1 6.8 %collective-permute-start.12 = (bf16[512,128]{1,0:T(8,128)(2,1)S(1)}, bf16[512,128]{1,0:T(8,128)(2,1)S(1)}, u32[]{:S(2)}, u32[]{:S(2)}) collective-permute-start(bf16[512,128]{1,0:T(8,128)(2,1)S(1)} %get-tuple-element.66), channel_id=1, source_target_pairs={{0,16},{8,24},{16,0},{24,8},{1,17},{9,25},{17,1},{25,9},{2,18},{10... | collective-permute-start | bytes 393224 | tf_op jit(solution)/shard_map/ppermute | solution.py:61
  58.0 7.6 %collective-permute-start.13 = (bf16[512,128]{1,0:T(8,128)(2,1)S(1)}, bf16[512,128]{1,0:T(8,128)(2,1)S(1)}, u32[]{:S(2)}, u32[]{:S(2)}) collective-permute-start(bf16[512,128]{1,0:T(8,128)(2,1)S(1)} %get-tuple-element.67), channel_id=1, source_target_pairs={{0,24},{8,16},{16,8},{24,0},{1,25},{9,17},{17,9},{25,1},{2,26},{10... | collective-permute-start | bytes 393224 | tf_op jit(solution)/shard_map/ppermute | solution.py:61
  65.6 6.0 %collective-permute-start.15 = (bf16[4,512,128]{2,1,0:T(8,128)(2,1)S(1)}, bf16[4,512,128]{2,1,0:T(8,128)(2,1)S(1)}, u32[]{:S(2)}, u32[]{:S(2)}) collective-permute-start(bf16[4,512,128]{2,1,0:T(8,128)(2,1)S(1)} %pack.1.refs_0_), channel_id=1, source_target_pairs={{0,1},{1,0},{2,3},{3,2},{4,5},{5,4},{6,7},{7,6},{8,9},{9,8},{10,11... | collective-permute-start | bytes 1572872 | tf_op jit(solution)/shard_map/ppermute | solution.py:68
  65.7 10.1 %collective-permute-start.16 = (bf16[2,128,640]{2,1,0:T(8,128)(2,1)S(1)}, bf16[2,128,640]{2,1,0:T(8,128)(2,1)S(1)}, u32[]{:S(2)}, u32[]{:S(2)}) collective-permute-start(bf16[2,128,640]{2,1,0:T(8,128)(2,1)S(1)} %get-tuple-element.73), channel_id=1, source_target_pairs={{0,8},{8,0},{16,24},{24,16},{1,9},{9,1},{17,25},{25,17},{2,10},{10... | collective-permute-start | bytes 983048 | tf_op jit(solution)/shard_map/ppermute | solution.py:61
  66.5 9.8 %collective-permute-start.17 = (bf16[2,128,640]{2,1,0:T(8,128)(2,1)S(1)}, bf16[2,128,640]{2,1,0:T(8,128)(2,1)S(1)}, u32[]{:S(2)}, u32[]{:S(2)}) collective-permute-start(bf16[2,128,640]{2,1,0:T(8,128)(2,1)S(1)} %get-tuple-element.75), channel_id=1, source_target_pairs={{0,16},{8,24},{16,0},{24,8},{1,17},{9,25},{17,1},{25,9},{2,18},{10... | collective-permute-start | bytes 983048 | tf_op jit(solution)/shard_map/ppermute | solution.py:61
  73.7 11.7 %collective-permute-start.19 = (bf16[1024,128]{1,0:T(8,128)(2,1)S(1)}, bf16[1024,128]{1,0:T(8,128)(2,1)S(1)}, u32[]{:S(2)}, u32[]{:S(2)}) collective-permute-start(bf16[1024,128]{1,0:T(8,128)(2,1)S(1)} %gather_grad.11), channel_id=1, source_target_pairs={{0,2},{1,3},{2,0},{3,1},{4,6},{5,7},{6,4},{7,5},{8,10},{9,11},{10,... | collective-permute-start | bytes 786440 | tf_op jit(solution)/shard_map/ppermute | solution.py:65
  77.1 10.4 %collective-permute-start.21 = (bf16[1,128,640]{2,1,0:T(8,128)(2,1)S(1)}, bf16[1,128,640]{2,1,0:T(8,128)(2,1)S(1)}, u32[]{:S(2)}, u32[]{:S(2)}) collective-permute-start(bf16[1,128,640]{2,1,0:T(8,128)(2,1)S(1)} %get-tuple-element.87), channel_id=1, source_target_pairs={{0,16},{8,24},{16,0},{24,8},{1,17},{9,25},{17,1},{25,9},{2,18},{10... | collective-permute-start | bytes 491528 | tf_op jit(solution)/shard_map/ppermute | solution.py:61
  78.7 8.9 %collective-permute-start.22 = (bf16[1,128,640]{2,1,0:T(8,128)(2,1)S(1)}, bf16[1,128,640]{2,1,0:T(8,128)(2,1)S(1)}, u32[]{:S(2)}, u32[]{:S(2)}) collective-permute-start(bf16[1,128,640]{2,1,0:T(8,128)(2,1)S(1)} %get-tuple-element.88), channel_id=1, source_target_pairs={{0,8},{8,0},{16,24},{24,16},{1,9},{9,1},{17,25},{25,17},{2,10},{10... | collective-permute-start | bytes 491528 | tf_op jit(solution)/shard_map/ppermute | solution.py:61
  82.1 13.5 %collective-permute-start.18 = (bf16[1024,128]{1,0:T(8,128)(2,1)S(1)}, bf16[1024,128]{1,0:T(8,128)(2,1)S(1)}, u32[]{:S(2)}, u32[]{:S(2)}) collective-permute-start(bf16[1024,128]{1,0:T(8,128)(2,1)S(1)} %gather_grad.7), channel_id=1, source_target_pairs={{0,2},{1,3},{2,0},{3,1},{4,6},{5,7},{6,4},{7,5},{8,10},{9,11},{10,... | collective-permute-start | bytes 786440 | tf_op jit(solution)/shard_map/ppermute | solution.py:65
  85.5 18.7 %collective-permute-start.20 = (bf16[1024,128]{1,0:T(8,128)(2,1)S(1)}, bf16[1024,128]{1,0:T(8,128)(2,1)S(1)}, u32[]{:S(2)}, u32[]{:S(2)}) collective-permute-start(bf16[1024,128]{1,0:T(8,128)(2,1)S(1)} %add_up.3), channel_id=1, source_target_pairs={{0,4},{1,5},{2,6},{3,7},{4,0},{5,1},{6,2},{7,3},{8,12},{9,13},{10,... | collective-permute-start | bytes 786440 | tf_op jit(solution)/shard_map/ppermute | solution.py:65
  88.2 16.7 %collective-permute-start.23 = (bf16[64,640]{1,0:T(8,128)(2,1)S(1)}, bf16[64,640]{1,0:T(8,128)(2,1)S(1)}, u32[]{:S(2)}, u32[]{:S(2)}) collective-permute-start(bf16[64,640]{1,0:T(8,128)(2,1)S(1)} %get-tuple-element.92), channel_id=1, source_target_pairs={{0,2},{1,3},{2,0},{3,1},{4,6},{5,7},{6,4},{7,5},{8,10},{9,11},{10,... | collective-permute-start | bytes 245768 | tf_op jit(solution)/shard_map/ppermute | solution.py:65
  90.3 14.7 %collective-permute-start.24 = (bf16[64,640]{1,0:T(8,128)(2,1)S(1)}, bf16[64,640]{1,0:T(8,128)(2,1)S(1)}, u32[]{:S(2)}, u32[]{:S(2)}) collective-permute-start(bf16[64,640]{1,0:T(8,128)(2,1)S(1)} %get-tuple-element.93), channel_id=1, source_target_pairs={{0,4},{1,5},{2,6},{3,7},{4,0},{5,1},{6,2},{7,3},{8,12},{9,13},{10,... | collective-permute-start | bytes 245768 | tf_op jit(solution)/shard_map/ppermute | solution.py:65
  90.3 14.7 %collective-permute-start.25 = (bf16[64,640]{1,0:T(8,128)(2,1)S(1)}, bf16[64,640]{1,0:T(8,128)(2,1)S(1)}, u32[]{:S(2)}, u32[]{:S(2)}) collective-permute-start(bf16[64,640]{1,0:T(8,128)(2,1)S(1)} %get-tuple-element.94), channel_id=1, source_target_pairs={{0,6},{1,7},{2,4},{3,5},{4,2},{5,3},{6,0},{7,1},{8,14},{9,15},{10,... | collective-permute-start | bytes 245768 | tf_op jit(solution)/shard_map/ppermute | solution.py:65
  105.1 5.4 %collective-permute-start.28 = (bf16[64,640]{1,0:T(8,128)(2,1)S(1)}, bf16[64,640]{1,0:T(8,128)(2,1)S(1)}, u32[]{:S(2)}, u32[]{:S(2)}) collective-permute-start(bf16[64,640]{1,0:T(8,128)(2,1)S(1)} %add_up.5.refs_0_), channel_id=1, source_target_pairs={{0,24},{8,16},{16,8},{24,0},{1,25},{9,17},{17,9},{25,1},{2,26},{10... | collective-permute-start | bytes 245768 | tf_op jit(solution)/shard_map/ppermute | solution.py:61
  106.5 4.9 %collective-permute-start.27 = (bf16[64,640]{1,0:T(8,128)(2,1)S(1)}, bf16[64,640]{1,0:T(8,128)(2,1)S(1)}, u32[]{:S(2)}, u32[]{:S(2)}) collective-permute-start(bf16[64,640]{1,0:T(8,128)(2,1)S(1)} %add_up.5.refs_0_), channel_id=1, source_target_pairs={{0,16},{8,24},{16,0},{24,8},{1,17},{9,25},{17,1},{25,9},{2,18},{10... | collective-permute-start | bytes 245768 | tf_op jit(solution)/shard_map/ppermute | solution.py:61
  108.0 4.4 %collective-permute-start.26 = (bf16[64,640]{1,0:T(8,128)(2,1)S(1)}, bf16[64,640]{1,0:T(8,128)(2,1)S(1)}, u32[]{:S(2)}, u32[]{:S(2)}) collective-permute-start(bf16[64,640]{1,0:T(8,128)(2,1)S(1)} %add_up.5.refs_0_), channel_id=1, source_target_pairs={{0,8},{8,0},{16,24},{24,16},{1,9},{9,1},{17,25},{25,17},{2,10},{10... | collective-permute-start | bytes 245768 | tf_op jit(solution)/shard_map/ppermute | solution.py:61

commit v7 on v5

--- a/solution.py
+++ b/solution.py
@@ -68,7 +68,7 @@
         return lax.ppermute(value, "sparse", [(i, i ^ 1) for i in range(self.shards)])
 
 
-def fetch(keys, cohorts, chunk, base, before=()):
+def fetch(base, keys, cohorts, chunk, before=()):
     many = len(cohorts)
     count, _, _, tokens, _ = keys.shape
     rows, cols = chunk.shape[0] // 2, chunk.shape[1]
@@ -92,7 +92,7 @@
         "fetch",
         body,
         [((count, tokens, cols), BF16)] * many,
-        [base.reshape(1), chunk, keys, *before],
+        [base, chunk, keys, *before],
         smem=1,
         flops=2 * many * count * tokens * rows * cols,
     )
@@ -109,13 +109,50 @@
     return run("combine", body, [(tuple(shape), BF16)] * count, parts)
 
 
-def gather_grad(keys, cohorts, tokens, base, rows, before=(), out=BF16):
+def pack(parts):
+    def body(*refs):
+        for k, ref in enumerate(refs[:-1]):
+            refs[-1][k] = ref[...]
+
+    shape, dtype = parts[0].shape, parts[0].dtype
+    return run("pack", body, [((len(parts), *shape), dtype)], parts)[0]
+
+
+def add_up(parts):
+    def body(*refs):
+        total = refs[0][...].astype(F32)
+        for ref in refs[1:-1]:
+            total = total + ref[...].astype(F32)
+        refs[-1][...] = total.astype(BF16)
+
+    return run("add_up", body, [(parts[0].shape, BF16)], parts)[0]
+
+
+def table_sums(here, whole, halves):
+    rows, cols = here.shape[0] // 2, here.shape[1]
+
+    def body(here_ref, *refs):
+        whole_refs, half_refs, out_refs = refs[: len(whole)], refs[len(whole) : -2], refs[-2:]
+        for i in range(2):
+            span = slice(i * rows, (i + 1) * rows)
+            total = here_ref[span, :]
+            for ref in whole_refs:
+                total = total + ref[span, :].astype(F32)
+            for ref in half_refs[i::2]:
+                total = total + ref[...].astype(F32)
+            out_refs[i][...] = total
+
+    return run("table_sums", body, [((rows, cols), F32)] * 2, [here, *whole, *halves])
+
+
+def gather_grad(base, keys, cohorts, tokens, rows, before=(), out=BF16, apart=False):
     many = len(cohorts)
     count, _, _, length = keys.shape
     cols = tokens[0].shape[-1]
 
     def body(base_ref, key_ref, *refs):
-        piece_refs, before_refs, out_ref = refs[:many], refs[many:-1], refs[-1]
+        piece_refs, before_refs = refs[:many], refs[many : many + len(before)]
+        out_refs = refs[many + len(before) :]
         row = lax.broadcasted_iota(I32, (rows, length), 0)
         for table in range(2):
             span = slice(table * rows, (table + 1) * rows)
@@ -130,19 +167,22 @@
                 sums = part if sums is None else sums + part
             for ref in before_refs:
                 sums = sums + ref[span, :].astype(F32)
-            out_ref[span, :] = sums.astype(out)
+            if apart:
+                out_refs[table][...] = sums.astype(out)
+            else:
+                out_refs[0][span, :] = sums.astype(out)
 
     return run(
         "gather_grad",
         body,
-        [((2 * rows, cols), out)],
-        [base.reshape(1), keys, *tokens, *before],
+        [((rows, cols), out)] * 2 if apart else [((2 * rows, cols), out)],
+        [base, keys, *tokens, *before],
         smem=1,
         flops=4 * many * count * length * 2 * rows * cols,
-    )[0]
-
-
-def sequence(blocks, other, pieces, cotangent, gain, w_proj, w_out, cores, line):
+    )
+
+
+def sequence(replica, core, pieces, cotangent, gain, w_proj, w_out, cores, line):
     count = len(pieces)
     length, width = cotangent.shape
     cols = width // count
@@ -151,14 +191,14 @@
     tile = min(256, length)
     step = min(256, 4 * width)
 
-    def body(block_ref, other_ref, cot_ref, wo_ref, wp_ref, gain_ref, *refs):
+    def body(r_ref, core_ref, cot_ref, wo_ref, wp_ref, gain_ref, *refs):
         piece_refs, refs = refs[:count], refs[count:]
         out_ref, *grad_refs = refs[: count + 1]
         normed_ref, dproj_ref, gated_ref, weight_ref = refs[count + 1 : count + 5]
         emb, act, slope, att, attn, dscale, dkey, dval, tok = refs[count + 5 :]
 
         for k in range(count):
-            emb[block_ref[k]] = piece_refs[k][...]
+            emb[r_ref[0] ^ k] = piece_refs[k][...]
 
         def embedded(span):
             return jnp.concatenate([emb[k, span] for k in range(count)], axis=1).astype(F32)
@@ -239,9 +279,10 @@
                 tok[k, span] = grad[:, k * cols : (k + 1) * cols].astype(BF16)
 
         for k in range(count):
-            grad_refs[k][...] = tok[block_ref[k]]
-
-        sums = weight_sums(other_ref[0], normed_ref, dproj_ref, gated_ref, cot_ref, cores, line, count)
+            grad_refs[k][...] = tok[r_ref[0] ^ k]
+
+        other = (core_ref[0] + 1) % cores
+        sums = weight_sums(other, normed_ref, dproj_ref, gated_ref, cot_ref, cores, line, count)
         for k in range(count):
             weight_ref[k] = next(sums).astype(BF16)
 
@@ -256,7 +297,7 @@
             ((length, width), BF16),
             ((count, width // cores, 5 * width // count), BF16),
         ],
-        [blocks, other, cotangent, w_out, w_proj, gain, *pieces],
+        [replica, core, cotangent, w_out, w_proj, gain, *pieces],
         smem=2,
         vmem=24,
         flops=32 * length * width * width,
@@ -296,31 +337,31 @@
         yield parts[0] if len(parts) == 1 else jnp.concatenate(parts, axis=1)
 
 
-def weight_grad(place, normed, dproj, gated, cotangent, before, line):
+def weight_grad(replica, core, normed, dproj, gated, cotangent, before, line):
     blocks, half, cols = before.shape
     length, width = normed.shape
     cores = width // half
     bits = blocks.bit_length() - 1
     tall = half // bits
 
-    def body(place_ref, n_ref, d_ref, g_ref, c_ref, before_ref, *refs):
+    def body(r_ref, core_ref, n_ref, d_ref, g_ref, c_ref, before_ref, *refs):
         out_refs, scratch = refs[:-1], refs[-1]
-        sums = weight_sums(place_ref[0], n_ref, d_ref, g_ref, c_ref, cores, line, blocks)
+        sums = weight_sums(core_ref[0], n_ref, d_ref, g_ref, c_ref, cores, line, blocks)
         for k in range(blocks):
             total = next(sums) + before_ref[k].astype(F32)
             for p in range(bits):
                 at = sum((k >> (p + i) % bits & 1) << bits - 1 - i for i in range(bits))
                 scratch[p, at] = total[p * tall : (p + 1) * tall]
         for p in range(bits):
-            split_halves(scratch.at[p], place_ref[1 + p], out_refs[2 * p : 2 * p + 2])
+            split_halves(scratch.at[p], r_ref[0] >> p & 1, out_refs[2 * p : 2 * p + 2])
 
     kept = (blocks // 2, tall, cols)
     return run(
         "weight_grad",
         body,
         [(kept, F32), (kept, BF16)] * bits,
-        [place, normed, dproj, gated, cotangent, before],
-        smem=1,
+        [replica, core, normed, dproj, gated, cotangent, before],
+        smem=2,
         scratch=[pltpu.VMEM((bits, blocks, tall, cols), F32)],
         flops=2 * length * half * (blocks * cols + 2 * width),
     )
@@ -334,71 +375,61 @@
             out_ref[k] = ref[start + k].astype(out_ref.dtype)
 
 
-def fold(bits, kept, came):
+def fold(replica, kept, came, step):
     count, tall, cols = kept[0].shape
     many = len(kept)
 
-    def body(bit_ref, *refs):
+    def body(r_ref, *refs):
         kept_refs, came_refs, out_refs = refs[:many], refs[many : 2 * many], refs[2 * many : -1]
         scratch = refs[-1]
         for p in range(many):
             for k in range(count):
                 scratch[p, k] = kept_refs[p][k] + came_refs[p][k].astype(F32)
-            split_halves(scratch.at[p], bit_ref[p], out_refs[2 * p : 2 * p + 2])
+            split_halves(scratch.at[p], r_ref[0] >> (p + step) % many & 1, out_refs[2 * p : 2 * p + 2])
 
     half = (count // 2, tall, cols)
     return run(
         "fold",
         body,
         [(half, F32), (half, BF16)] * many,
-        [bits, *kept, *came],
+        [replica, *kept, *came],
         smem=1,
         scratch=[pltpu.VMEM((many, count, tall, cols), F32)],
     )
 
 
-def cut_line(planes, kept, came):
+def cut_line(place, kept, came, line):
     _, tall, cols = kept[0].shape
-    many, line = len(kept), planes.shape[0]
+    many = len(kept)
     rows = many * tall // line
 
-    def body(plane_ref, *refs):
+    def body(place_ref, *refs):
         kept_refs, came_refs, out_refs = refs[:many], refs[many : 2 * many], refs[2 * many : -1]
         scratch = refs[-1]
         for p in range(many):
             scratch[p * tall : (p + 1) * tall] = kept_refs[p][0] + came_refs[p][0].astype(F32)
         for k in range(line):
-            span = pl.ds(pl.multiple_of(plane_ref[k] * rows, rows), rows)
+            span = pl.ds(pl.multiple_of((place_ref[0] ^ k) * rows, rows), rows)
             out_refs[k][...] = scratch[span].astype(out_refs[k].dtype)
 
     return run(
         "cut_line",
         body,
         [((rows, cols), F32)] + [((rows, cols), BF16)] * (line - 1),
-        [planes, *kept, *came],
+        [place, *kept, *came],
         smem=1,
         scratch=[pltpu.VMEM((many * tall, cols), F32)],
     )
 
 
-def add_up(parts):
-    def body(*refs):
-        total = refs[0][...].astype(F32)
-        for ref in refs[1:-1]:
-            total = total + ref[...].astype(F32)
-        refs[-1][...] = total.astype(BF16)
-
-    return run("add_up", body, [(parts[0].shape, BF16)], parts)[0]
-
-
-def assemble(blocks, parts, edge):
+def assemble(replica, parts, edge):
     rows, cols = parts[0].shape
     total = cols * len(parts)
 
-    def body(block_ref, *refs):
+    def body(r_ref, *refs):
         part_refs, (left_ref, right_ref, held) = refs[: len(parts)], refs[len(parts) :]
         for k, ref in enumerate(part_refs):
-            held[block_ref[k]] = ref[...].astype(F32)
+            held[r_ref[0] ^ k] = ref[...].astype(F32)
         for k in range(len(parts)):
             first, last = k * cols, (k + 1) * cols
             cut = min(max(edge - first, 0), cols)
@@ -411,7 +442,7 @@
         "assemble",
         body,
         [((rows, edge), F32), ((rows, total - edge), F32)],
-        [blocks, *parts],
+        [replica, *parts],
         smem=1,
         scratch=[pltpu.VMEM((len(parts), rows, cols), F32)],
     )
@@ -436,9 +467,8 @@
 
     bits = replicas.bit_length() - 1
     swaps = [3, 1, 2] if replicas == 4 else list(range(1, replicas))
-    blocks = jnp.stack([grid.r ^ k for k in range(replicas)]).astype(I32)
-    planes = jnp.stack([grid.z ^ k for k in range(line)]).astype(I32)
-    bases = [(((grid.z ^ k) * cores + grid.c) * rows).astype(I32) for k in range(line)]
+    replica, place, core = (i.astype(I32).reshape(1) for i in (grid.r, grid.z, grid.c))
+    bases = [((place ^ k) * cores + core) * rows for k in range(line)]
 
     own = jnp.concatenate(
         [
@@ -468,72 +498,67 @@
 
     found = ()
     for k in order[:-1]:
-        found = fetch(key_cols, both, held[k], bases[k], found)
+        found = fetch(bases[k], key_cols, both, held[k], found)
     last = order[-1]
-    there = fetch(key_cols, both[1:], held[last], bases[last], found[1:])
-    here = fetch(key_cols, both[:1], held[last], bases[last], found[:1])
+    there = fetch(bases[last], key_cols, both[1:], held[last], found[1:])
+    here = fetch(bases[last], key_cols, both[:1], held[last], found[:1])
     pieces = combine([here[0], grid.over_pair(there[0])])
     for k in swaps:
         pieces[k] = grid.over_replica(pieces[k], k)
 
+    gain = input_norm_gain.reshape(1, width)
     layer_out, *rest = sequence(
-        blocks,
-        ((grid.c + 1) % cores).astype(I32).reshape(1),
-        pieces,
-        cotangent,
-        input_norm_gain.reshape(1, width),
-        w_proj,
-        w_out,
-        cores,
-        line,
+        replica, core, pieces, cotangent, gain, w_proj, w_out, cores, line
     )
     tokens, (normed, dproj, gated, weights) = rest[:replicas], rest[replicas:]
     for k in swaps:
         tokens[k] = grid.over_replica(tokens[k], k)
 
-    place = jnp.stack([grid.c] + [grid.r >> p & 1 for p in range(bits)]).astype(I32)
     weights = grid.over_pair(weights)
-    weights = weight_grad(place, normed, dproj, gated, cotangent, weights, line)
+    weights = weight_grad(replica, core, normed, dproj, gated, cotangent, weights, line)
     tokens = lax.optimization_barrier((tokens, weights))[0]
-    tokens = jnp.stack(tokens)
+    tokens = pack(tokens)
     there = grid.over_pair(tokens)
 
     def swap_weights(weights, step):
         kept, sent = weights[0::2], weights[1::2]
         return kept, [grid.over_replica(sent[p], 1 << (p + step) % bits) for p in range(bits)]
 
-    kept, came = swap_weights(weights, 0)
-    first = {k: gather_grad(keys, both[:1], [tokens], bases[k], rows) for k in order[-2:]}
-    there = lax.optimization_barrier((there, came, first))[0]
-
-    sums = {}
+    kept, swapped = swap_weights(weights, 0)
+
+    sums, raw, both_there = {}, {}, [tokens, there]
     for k in reversed(order):
         low = (k & -k) or line
         steps = [1 << i for i in range(low.bit_length() - 1)]
         out = F32 if steps else BF16
-        if k in first:
-            total = gather_grad(keys, both[1:], [there], bases[k], rows, [first[k]], out)
+        if k == last:
+            first = gather_grad(bases[k], keys, both[:1], [tokens], rows)
+            raw[k] = gather_grad(bases[k], keys, both[1:], [there], rows, first, out)
         else:
-            total = gather_grad(keys, both, [tokens, there], bases[k], rows, out=out)
-        for step in steps:
-            total = total + grid.over_line(sums[k ^ step], step).astype(F32)
-        sums[k] = total.astype(BF16) if k else total
-    table_grad = sums[0]
+            if k == 1 and line > 2:
+                both_there = lax.optimization_barrier((both_there, sums[line // 2]))[0]
+            raw[k] = gather_grad(bases[k], keys, both, both_there, rows, out=out)
+        came = [[grid.over_line(part, step) for part in sums[k ^ step]] for step in steps]
+        if k == 0:
+            whole = [parts[0] for parts in came if len(parts) == 1]
+            halves = [part for parts in came if len(parts) == 2 for part in parts]
+            item_grad, action_grad = table_sums(raw[k][0], whole, halves)
+        else:
+            sums[k] = [add_up(raw[k] + [parts[0] for parts in came])] if steps else raw[k]
 
     for step in range(1, bits + 1):
-        after = sums[last] if step < bits else sums[line // 2]
-        came = lax.optimization_barrier((came, after))[0]
+        after = raw[line // 2] if step < bits else sums[line // 2]
+        swapped = lax.optimization_barrier((swapped, after))[0]
         if step < bits:
-            turn = jnp.stack([grid.r >> (p + step) % bits & 1 for p in range(bits)])
-            kept, came = swap_weights(fold(turn.astype(I32), kept, came), step)
-    parts = cut_line(planes, kept, came)
+            kept, swapped = swap_weights(fold(replica, kept, swapped, step), step)
+    parts = cut_line(place, kept, swapped, line)
     parts = [parts[0]] + [grid.over_line(parts[k], k) for k in range(1, line)]
-    parts = lax.optimization_barrier((parts, table_grad))[0]
+    parts = lax.optimization_barrier((parts, item_grad))[0]
     total = add_up(parts)
     parts = [total] + [grid.over_replica(total, k) for k in range(1, replicas)]
-    grad_proj, grad_out = assemble(blocks, parts, 4 * width)
-
-    return layer_out, table_grad[:rows], table_grad[rows:], grad_proj, grad_out
+    grad_proj, grad_out = assemble(replica, parts, 4 * width)
+
+    return layer_out, item_grad, action_grad, grad_proj, grad_out
 
 
 def solution(mesh):

time: 122 us -> 108 us (0.89)
  local copies, waits for them, and re-layouts: 14.5 us -> 2.25 us
  Pallas kernels: 38.6 us -> 36.4 us
    unnamed x36 -> x8, local copies, waits for them, and re-layouts: 11.5 us -> 0.03 us
    ppermute x9, waiting for transfers between devices: 12.9 us -> 15.7 us  [over_line(): return lax.ppermute(value, 'sparse', pairs)]
    pallas_call x18 -> x20, Pallas kernels: 38.6 us -> 36.4 us  [run(): pl.pallas_call(body, out_shape=outs, in_specs=places, out_specs=[in_vmem]...]
    ppermute x16, waiting for transfers between devices: 17.9 us -> 16 us  [over_replica(): return lax.ppermute(value, 'replica', [(i, i ^ step) for i in range(n)])]
  transfers between devices with their start and end apart: 29 -> 29, of which waited for: 16 -> 15; matrix products, arithmetic and copies ran while one was open for 3% -> 2% of each run, Pallas kernels for 17% -> 19%
where the time goes in v7:
time: 108 us
  Pallas kernels  36.4 us (34%)
  starting transfers between devices  35 us (32%)
  waiting for transfers between devices  32.3 us (30%)
  local copies, waits for them, and re-layouts  2.25 us (2%)
    pallas_call x20, Pallas kernels, run(): pl.pallas_call(body, out_shape=outs, in_specs=places, out_specs=[in_vmem]...  36.4 us
    ppermute x16, starting transfers between devices, over_replica(): return lax.ppermute(value, 'replica', [(i, i ^ step) for i in range(n)])  18.6 us
    ppermute x9, starting transfers between devices, over_line(): return lax.ppermute(value, 'sparse', pairs)  16.1 us
    ppermute x16, waiting for transfers between devices, over_replica(): return lax.ppermute(value, 'replica', [(i, i ^ step) for i in range(n)])  16 us
    ppermute x9, waiting for transfers between devices, over_line(): return lax.ppermute(value, 'sparse', pairs)  15.7 us
  transfers between devices with their start and end apart: 29, of which 15 were waited for; matrix products, arithmetic and copies ran while one was open for 2% of the time, Pallas kernels for 19%

profile of v7, /device:TPU:0, one launch (start us, length us, event | category | flops | bytes accessed | tf_op | source)
XLA Modules:
  0.0 107.5 jit_solution(4258374632981483097)
XLA Ops:
  0.6 1.0 constant_dynamic-slice_fusion
  1.7 4.1 %collective-permute-start = (bf16[1024,128]{1,0:T(8,128)(2,1)S(1)}, bf16[1024,128]{1,0:T(8,128)(2,1)S(1)}, u32[]{:S(2)}, u32[]{:S(2)}) collective-permute-start(bf16[1024,128]{1,0:T(8,128)(2,1)S(1)} %pad_maximum_fusion.chunk_ref), channel_id=1, source_target_pairs={{0,4},{1,5},{2,6},{3,7},{4,0},{5,1},{6,2},{7,3},{8,12},{9,13},{10,... | collective-permute-start | bytes 786440 | tf_op jit(solution)/shard_map/ppermute | solution.py:65
  5.8 0.7 add_bitcast_fusion
  6.5 0.1 collective-permute-start.2
  6.6 1.6 %collective-permute-start.6 = (bf16[1024,128]{1,0:T(8,128)(2,1)S(1)}, bf16[1024,128]{1,0:T(8,128)(2,1)S(1)}, u32[]{:S(2)}, u32[]{:S(2)}) collective-permute-start(bf16[1024,128]{1,0:T(8,128)(2,1)S(1)} %pad_maximum_fusion.chunk_ref), channel_id=1, source_target_pairs={{0,2},{1,3},{2,0},{3,1},{4,6},{5,7},{6,4},{7,5},{8,10},{9,11},{10,... | collective-permute-start | bytes 786440 | tf_op jit(solution)/shard_map/ppermute | solution.py:65
  8.2 1.6 %collective-permute-start.4 = (s32[2,2,512]{2,1,0:T(2,128)S(1)}, s32[2,2,512]{2,1,0:T(2,128)S(1)}, u32[]{:S(2)}, u32[]{:S(2)}) collective-permute-start(s32[2,2,512]{2,1,0:T(2,128)S(1)} %get-tuple-element.104), channel_id=1, source_target_pairs={{0,16},{8,24},{16,0},{24,8},{1,17},{9,25},{17,1},{25,9},{2,18},{10... | collective-permute-start | bytes 24584 | tf_op jit(solution)/shard_map/ppermute | solution.py:61
  9.8 1.5 %collective-permute-start.3 = (s32[2,2,512]{2,1,0:T(2,128)S(1)}, s32[2,2,512]{2,1,0:T(2,128)S(1)}, u32[]{:S(2)}, u32[]{:S(2)}) collective-permute-start(s32[2,2,512]{2,1,0:T(2,128)S(1)} %get-tuple-element.104), channel_id=1, source_target_pairs={{0,8},{8,0},{16,24},{24,16},{1,9},{9,1},{17,25},{25,17},{2,10},{10... | collective-permute-start | bytes 24584 | tf_op jit(solution)/shard_map/ppermute | solution.py:61
  11.3 0.5 collective-permute-start.5
  11.8 6.0 %collective-permute-done.chunk_ref = bf16[1024,128]{1,0:T(8,128)(2,1)S(1)} collective-permute-done((bf16[1024,128]{1,0:T(8,128)(2,1)S(1)}, bf16[1024,128]{1,0:T(8,128)(2,1)S(1)}, u32[]{:S(2)}, u32[]{:S(2)}) %collective-permute-start) | collective-permute-done | bytes 262176 | tf_op jit(solution)/shard_map/ppermute | solution.py:65
  17.8 0.7 collective-permute-start.1
  18.5 1.2 %broadcast_in_dim.14.key_ref = s32[4,2,2,512,128]{4,3,2,1,0:T(8,128)S(1)} broadcast(s32[4,2,2,512]{3,2,1,0:T(2,128)S(1)} %pad_add_fusion.key_ref), dimensions={0,1,2,3} | broadcast | bytes 4227072 | tf_op jit(solution)/shard_map/broadcast_in_dim | solution.py:496
  19.7 2.3 %fetch.5 = (bf16[4,512,128]{2,1,0:T(8,128)(2,1)S(1)}, bf16[4,512,128]{2,1,0:T(8,128)(2,1)S(1)}) custom-call(s32[1]{0:T(128)S(6)} %mul.44.base_ref, bf16[1024,128]{1,0:T(8,128)(2,1)S(1)} %pad_maximum_fusion.chunk_ref, s32[4,2,2,512,128]{4,3,2,1,0:T(8,128)S(1)} %broadcast_in_dim.14.key_ref), custom_call_target="tpu_custom_call" | custom-call | flops 536870912 | bytes 5505028 | tf_op jit(solution)/shard_map/fetch/pallas_call | solution.py:35
  22.1 2.3 %fetch.6 = (bf16[4,512,128]{2,1,0:T(8,128)(2,1)S(1)}, bf16[4,512,128]{2,1,0:T(8,128)(2,1)S(1)}) custom-call(s32[1]{0:T(128)S(6)} %mul.42.base_ref, bf16[1024,128]{1,0:T(8,128)(2,1)S(1)} %collective-permute-done.6.chunk_ref, s32[4,2,2,512,128]{4,3,2,1,0:T(8,128)S(1)} %broadcast_in_dim.14.key_ref, bf16[4,512,128]{2,1,0:T(8,128)(2,1)S(1)} %get-tuple-element.54.refs_0_, ...), custom_call_target="tpu_custom_call" | custom-call | flops 536870912 | bytes 6553604 | tf_op jit(solution)/shard_map/fetch/pallas_call | solution.py:35
  24.4 2.3 %fetch.7 = (bf16[4,512,128]{2,1,0:T(8,128)(2,1)S(1)}, bf16[4,512,128]{2,1,0:T(8,128)(2,1)S(1)}) custom-call(s32[1]{0:T(128)S(6)} %mul.40.base_ref, bf16[1024,128]{1,0:T(8,128)(2,1)S(1)} %collective-permute-done.chunk_ref, s32[4,2,2,512,128]{4,3,2,1,0:T(8,128)S(1)} %broadcast_in_dim.14.key_ref, bf16[4,512,128]{2,1,0:T(8,128)(2,1)S(1)} %get-tuple-element.56.refs_0_, ...), custom_call_target="tpu_custom_call" | custom-call | flops 536870912 | bytes 6553604 | tf_op jit(solution)/shard_map/fetch/pallas_call | solution.py:35
  26.8 1.2 %fetch.9 = bf16[4,512,128]{2,1,0:T(8,128)(2,1)S(1)} custom-call(s32[1]{0:T(128)S(6)} %mul.35.base_ref, bf16[1024,128]{1,0:T(8,128)(2,1)S(1)} %collective-permute-done.1.chunk_ref, s32[4,2,2,512,128]{4,3,2,1,0:T(8,128)S(1)} %broadcast_in_dim.14.key_ref, bf16[4,512,128]{2,1,0:T(8,128)(2,1)S(1)} %get-tuple-element.59.refs_0_), custom_call_target="tpu_custom_call" | custom-call | flops 268435456 | bytes 5505028 | tf_op jit(solution)/shard_map/fetch/pallas_call | solution.py:35
  28.0 0.1 collective-permute-start.7
  28.2 1.2 %fetch.8.left_ref = bf16[4,512,128]{2,1,0:T(8,128)(2,1)S(1)} custom-call(s32[1]{0:T(128)S(6)} %mul.35.base_ref, bf16[1024,128]{1,0:T(8,128)(2,1)S(1)} %collective-permute-done.1.chunk_ref, s32[4,2,2,512,128]{4,3,2,1,0:T(8,128)S(1)} %broadcast_in_dim.14.key_ref, bf16[4,512,128]{2,1,0:T(8,128)(2,1)S(1)} %get-tuple-element.58.refs_0_), custom_call_target="tpu_custom_call" | custom-call | flops 268435456 | bytes 5505028 | tf_op jit(solution)/shard_map/fetch/pallas_call | solution.py:35
  29.4 0.6 collective-permute-done.7.right_ref
  30.0 0.1 combine.1
  30.2 1.6 %collective-permute-start.8 = (bf16[512,128]{1,0:T(8,128)(2,1)S(1)}, bf16[512,128]{1,0:T(8,128)(2,1)S(1)}, u32[]{:S(2)}, u32[]{:S(2)}) collective-permute-start(bf16[512,128]{1,0:T(8,128)(2,1)S(1)} %get-tuple-element.61), channel_id=1, source_target_pairs={{0,8},{8,0},{16,24},{24,16},{1,9},{9,1},{17,25},{25,17},{2,10},{10... | collective-permute-start | bytes 393224 | tf_op jit(solution)/shard_map/ppermute | solution.py:61
  31.7 1.5 %collective-permute-start.9 = (bf16[512,128]{1,0:T(8,128)(2,1)S(1)}, bf16[512,128]{1,0:T(8,128)(2,1)S(1)}, u32[]{:S(2)}, u32[]{:S(2)}) collective-permute-start(bf16[512,128]{1,0:T(8,128)(2,1)S(1)} %get-tuple-element.62), channel_id=1, source_target_pairs={{0,16},{8,24},{16,0},{24,8},{1,17},{9,25},{17,1},{25,9},{2,18},{10... | collective-permute-start | bytes 393224 | tf_op jit(solution)/shard_map/ppermute | solution.py:61
  33.2 0.5 collective-permute-start.10
  33.7 2.4 %collective-permute-done.8.refs_1_ = bf16[512,128]{1,0:T(8,128)(2,1)S(1)} collective-permute-done((bf16[512,128]{1,0:T(8,128)(2,1)S(1)}, bf16[512,128]{1,0:T(8,128)(2,1)S(1)}, u32[]{:S(2)}, u32[]{:S(2)}) %collective-permute-start.8) | collective-permute-done | bytes 131104 | tf_op jit(solution)/shard_map/ppermute | solution.py:61
  36.1 3.7 %collective-permute-done.9.refs_2_ = bf16[512,128]{1,0:T(8,128)(2,1)S(1)} collective-permute-done((bf16[512,128]{1,0:T(8,128)(2,1)S(1)}, bf16[512,128]{1,0:T(8,128)(2,1)S(1)}, u32[]{:S(2)}, u32[]{:S(2)}) %collective-permute-start.9) | collective-permute-done | bytes 131104 | tf_op jit(solution)/shard_map/ppermute | solution.py:61
  39.8 13.1 %sequence.1 = (bf16[512,512]{1,0:T(8,128)(2,1)}, bf16[512,128]{1,0:T(8,128)(2,1)S(1)}, bf16[512,128]{1,0:T(8,128)(2,1)S(1)}, bf16[512,128]{1,0:T(8,128)(2,1)S(1)...) custom-call(s32[1]{0:T(128)} %bitcast.r_ref, ...), custom_call_target="tpu_custom_call" | custom-call | flops 4294967296 | bytes 9177096 | tf_op jit(solution)/shard_map/sequence/pallas_call | solution.py:35
  53.0 1.2 %collective-permute-start.11 = (bf16[512,128]{1,0:T(8,128)(2,1)S(1)}, bf16[512,128]{1,0:T(8,128)(2,1)S(1)}, u32[]{:S(2)}, u32[]{:S(2)}) collective-permute-start(bf16[512,128]{1,0:T(8,128)(2,1)S(1)} %get-tuple-element.66), channel_id=1, source_target_pairs={{0,8},{8,0},{16,24},{24,16},{1,9},{9,1},{17,25},{25,17},{2,10},{10... | collective-permute-start | bytes 393224 | tf_op jit(solution)/shard_map/ppermute | solution.py:61
  54.2 0.8 collective-permute-start.12
  55.0 1.4 %collective-permute-start.13 = (bf16[512,128]{1,0:T(8,128)(2,1)S(1)}, bf16[512,128]{1,0:T(8,128)(2,1)S(1)}, u32[]{:S(2)}, u32[]{:S(2)}) collective-permute-start(bf16[512,128]{1,0:T(8,128)(2,1)S(1)} %get-tuple-element.68), channel_id=1, source_target_pairs={{0,24},{8,16},{16,8},{24,0},{1,25},{9,17},{17,9},{25,1},{2,26},{10... | collective-permute-start | bytes 393224 | tf_op jit(solution)/shard_map/ppermute | solution.py:61
  56.5 1.7 %weight_grad.1 = (f32[2,128,640]{2,1,0:T(8,128)S(1)}, bf16[2,128,640]{2,1,0:T(8,128)(2,1)S(1)}, f32[2,128,640]{2,1,0:T(8,128)S(1)}, bf16[2,128,640]{2,1,0:T(8,128)(2,1)S(1)}) custom-call(s32[1]{0:T(128)} %bitcast.r_ref, s32[1]{0:T(128)} %bitcast.1.core_ref, bf16[512,512]{1,0:T(8,128)(2,1)S(1)} %get-tuple-element.69.n_ref, ...), custom_call_target="tpu_custom_call" | custom-call | flops 939524096 | bytes 6946824 | tf_op jit(solution)/shard_map/weight_grad/pallas_call | solution.py:35
  58.2 1.1 %collective-permute-done.11.refs_1_ = bf16[512,128]{1,0:T(8,128)(2,1)S(1)} collective-permute-done((bf16[512,128]{1,0:T(8,128)(2,1)S(1)}, bf16[512,128]{1,0:T(8,128)(2,1)S(1)}, u32[]{:S(2)}, u32[]{:S(2)}) %collective-permute-start.11) | collective-permute-done | bytes 131104 | tf_op jit(solution)/shard_map/ppermute | solution.py:61
  59.3 1.7 %collective-permute-done.12.refs_2_ = bf16[512,128]{1,0:T(8,128)(2,1)S(1)} collective-permute-done((bf16[512,128]{1,0:T(8,128)(2,1)S(1)}, bf16[512,128]{1,0:T(8,128)(2,1)S(1)}, u32[]{:S(2)}, u32[]{:S(2)}) %collective-permute-start.12) | collective-permute-done | bytes 131104 | tf_op jit(solution)/shard_map/ppermute | solution.py:61
  61.0 1.6 %collective-permute-done.13.refs_3_ = bf16[512,128]{1,0:T(8,128)(2,1)S(1)} collective-permute-done((bf16[512,128]{1,0:T(8,128)(2,1)S(1)}, bf16[512,128]{1,0:T(8,128)(2,1)S(1)}, u32[]{:S(2)}, u32[]{:S(2)}) %collective-permute-start.13) | collective-permute-done | bytes 131104 | tf_op jit(solution)/shard_map/ppermute | solution.py:61
  62.7 0.1 collective-permute-start.15
  62.8 0.9 collective-permute-start.19
  63.6 1.5 %collective-permute-start.20 = (bf16[2,128,640]{2,1,0:T(8,128)(2,1)S(1)}, bf16[2,128,640]{2,1,0:T(8,128)(2,1)S(1)}, u32[]{:S(2)}, u32[]{:S(2)}) collective-permute-start(bf16[2,128,640]{2,1,0:T(8,128)(2,1)S(1)} %get-tuple-element.76), channel_id=1, source_target_pairs={{0,16},{8,24},{16,0},{24,8},{1,17},{9,25},{17,1},{25,9},{2,18},{10... | collective-permute-start | bytes 983048 | tf_op jit(solution)/shard_map/ppermute | solution.py:61
  65.1 1.2 %gather_grad.6.refs_1_ = bf16[1024,128]{1,0:T(8,128)(2,1)S(1)} custom-call(s32[1]{0:T(128)S(6)} %mul.35.base_ref, s32[4,2,2,512]{3,2,1,0:T(2,128)S(1)} %pad_add_fusion.key_ref, bf16[4,512,128]{2,1,0:T(8,128)(2,1)S(1)} %pack.1.refs_0_), custom_call_target="tpu_custom_call" | custom-call | flops 1073741824 | bytes 819204 | tf_op jit(solution)/shard_map/gather_grad/pallas_call | solution.py:35
  66.4 1.2 %gather_grad.7 = bf16[1024,128]{1,0:T(8,128)(2,1)S(1)} custom-call(s32[1]{0:T(128)S(6)} %mul.35.base_ref, s32[4,2,2,512]{3,2,1,0:T(2,128)S(1)} %pad_add_fusion.key_ref, bf16[4,512,128]{2,1,0:T(8,128)(2,1)S(1)} %collective-permute-done.15.refs_1_.refs_0_, bf16[1024,128]{1,0:T(8,128)(2,1)S(1)} %gather_grad.6.refs_1_), custom_call_target="tpu_custom_call" | custom-call | flops 1073741824 | bytes 1081348 | tf_op jit(solution)/shard_map/gather_grad/pallas_call | solution.py:35
  67.6 1.5 %collective-permute-start.16 = (bf16[1024,128]{1,0:T(8,128)(2,1)S(1)}, bf16[1024,128]{1,0:T(8,128)(2,1)S(1)}, u32[]{:S(2)}, u32[]{:S(2)}) collective-permute-start(bf16[1024,128]{1,0:T(8,128)(2,1)S(1)} %gather_grad.7), channel_id=1, source_target_pairs={{0,2},{1,3},{2,0},{3,1},{4,6},{5,7},{6,4},{7,5},{8,10},{9,11},{10,... | collective-permute-start | bytes 786440 | tf_op jit(solution)/shard_map/ppermute | solution.py:65
  69.1 2.5 %gather_grad.5.refs_0_ = f32[1024,128]{1,0:T(8,128)S(1)} custom-call(s32[1]{0:T(128)S(6)} %mul.40.base_ref, s32[4,2,2,512]{3,2,1,0:T(2,128)S(1)} %pad_add_fusion.key_ref, bf16[4,512,128]{2,1,0:T(8,128)(2,1)S(1)} %pack.1.refs_0_, bf16[4,512,128]{2,1,0:T(8,128)(2,1)S(1)} %collective-permute-done.15.refs_1_.refs_0_), custom_call_target="tpu_custom_call" | custom-call | flops 2147483648 | bytes 1605636 | tf_op jit(solution)/shard_map/gather_grad/pallas_call | solution.py:35
  71.7 1.2 %collective-permute-done.19.refs_2_ = bf16[2,128,640]{2,1,0:T(8,128)(2,1)S(1)} collective-permute-done((bf16[2,128,640]{2,1,0:T(8,128)(2,1)S(1)}, bf16[2,128,640]{2,1,0:T(8,128)(2,1)S(1)}, u32[]{:S(2)}, u32[]{:S(2)}) %collective-permute-start.19) | collective-permute-done | bytes 327712 | tf_op jit(solution)/shard_map/ppermute | solution.py:61
  72.9 0.5 collective-permute-done.20.refs_3_
  73.4 0.3 fold.1
  73.7 1.6 %collective-permute-start.21 = (bf16[1,128,640]{2,1,0:T(8,128)(2,1)S(1)}, bf16[1,128,640]{2,1,0:T(8,128)(2,1)S(1)}, u32[]{:S(2)}, u32[]{:S(2)}) collective-permute-start(bf16[1,128,640]{2,1,0:T(8,128)(2,1)S(1)} %get-tuple-element.89), channel_id=1, source_target_pairs={{0,16},{8,24},{16,0},{24,8},{1,17},{9,25},{17,1},{25,9},{2,18},{10... | collective-permute-start | bytes 491528 | tf_op jit(solution)/shard_map/ppermute | solution.py:61
  75.2 0.5 collective-permute-start.22
  75.8 0.1 add_up.2
  75.9 2.3 %gather_grad.9 = bf16[1024,128]{1,0:T(8,128)(2,1)S(1)} custom-call(s32[1]{0:T(128)S(6)} %mul.42.base_ref, s32[4,2,2,512]{3,2,1,0:T(2,128)S(1)} %pad_add_fusion.key_ref, bf16[4,512,128]{2,1,0:T(8,128)(2,1)S(1)} %pack.1.refs_0_, bf16[4,512,128]{2,1,0:T(8,128)(2,1)S(1)} %collective-permute-done.15.refs_1_.refs_0_), custom_call_target="tpu_custom_call" | custom-call | flops 2147483648 | bytes 1343492 | tf_op jit(solution)/shard_map/gather_grad/pallas_call | solution.py:35
  78.2 1.5 %collective-permute-start.17 = (bf16[1024,128]{1,0:T(8,128)(2,1)S(1)}, bf16[1024,128]{1,0:T(8,128)(2,1)S(1)}, u32[]{:S(2)}, u32[]{:S(2)}) collective-permute-start(bf16[1024,128]{1,0:T(8,128)(2,1)S(1)} %gather_grad.9), channel_id=1, source_target_pairs={{0,2},{1,3},{2,0},{3,1},{4,6},{5,7},{6,4},{7,5},{8,10},{9,11},{10,... | collective-permute-start | bytes 786440 | tf_op jit(solution)/shard_map/ppermute | solution.py:65
  79.7 2.3 %collective-permute-start.18 = (bf16[1024,128]{1,0:T(8,128)(2,1)S(1)}, bf16[1024,128]{1,0:T(8,128)(2,1)S(1)}, u32[]{:S(2)}, u32[]{:S(2)}) collective-permute-start(bf16[1024,128]{1,0:T(8,128)(2,1)S(1)} %add_up.2), channel_id=1, source_target_pairs={{0,4},{1,5},{2,6},{3,7},{4,0},{5,1},{6,2},{7,3},{8,12},{9,13},{10,... | collective-permute-start | bytes 786440 | tf_op jit(solution)/shard_map/ppermute | solution.py:65
  82.0 0.1 cut_line.1
  82.1 1.8 %collective-permute-start.23 = (bf16[64,640]{1,0:T(8,128)(2,1)S(1)}, bf16[64,640]{1,0:T(8,128)(2,1)S(1)}, u32[]{:S(2)}, u32[]{:S(2)}) collective-permute-start(bf16[64,640]{1,0:T(8,128)(2,1)S(1)} %get-tuple-element.94), channel_id=1, source_target_pairs={{0,2},{1,3},{2,0},{3,1},{4,6},{5,7},{6,4},{7,5},{8,10},{9,11},{10,... | collective-permute-start | bytes 245768 | tf_op jit(solution)/shard_map/ppermute | solution.py:65
  83.9 0.3 collective-permute-start.24
  84.2 2.3 %collective-permute-start.25 = (bf16[64,640]{1,0:T(8,128)(2,1)S(1)}, bf16[64,640]{1,0:T(8,128)(2,1)S(1)}, u32[]{:S(2)}, u32[]{:S(2)}) collective-permute-start(bf16[64,640]{1,0:T(8,128)(2,1)S(1)} %get-tuple-element.96), channel_id=1, source_target_pairs={{0,6},{1,7},{2,4},{3,5},{4,2},{5,3},{6,0},{7,1},{8,14},{9,15},{10,... | collective-permute-start | bytes 245768 | tf_op jit(solution)/shard_map/ppermute | solution.py:65
  86.5 2.3 %gather_grad.8.here_ref = f32[1024,128]{1,0:T(8,128)S(1)} custom-call(s32[1]{0:T(128)S(6)} %mul.44.base_ref, s32[4,2,2,512]{3,2,1,0:T(2,128)S(1)} %pad_add_fusion.key_ref, bf16[4,512,128]{2,1,0:T(8,128)(2,1)S(1)} %pack.1.refs_0_, bf16[4,512,128]{2,1,0:T(8,128)(2,1)S(1)} %collective-permute-done.15.refs_1_.refs_0_), custom_call_target="tpu_custom_call" | custom-call | flops 2147483648 | bytes 1605636 | tf_op jit(solution)/shard_map/gather_grad/pallas_call | solution.py:35
  88.9 3.6 %collective-permute-done.17.refs_0_ = bf16[1024,128]{1,0:T(8,128)(2,1)S(1)} collective-permute-done((bf16[1024,128]{1,0:T(8,128)(2,1)S(1)}, bf16[1024,128]{1,0:T(8,128)(2,1)S(1)}, u32[]{:S(2)}, u32[]{:S(2)}) %collective-permute-start.17) | collective-permute-done | bytes 262176 | tf_op jit(solution)/shard_map/ppermute | solution.py:65
  92.4 3.7 %collective-permute-done.18.refs_1_ = bf16[1024,128]{1,0:T(8,128)(2,1)S(1)} collective-permute-done((bf16[1024,128]{1,0:T(8,128)(2,1)S(1)}, bf16[1024,128]{1,0:T(8,128)(2,1)S(1)}, u32[]{:S(2)}, u32[]{:S(2)}) %collective-permute-start.18) | collective-permute-done | bytes 262176 | tf_op jit(solution)/shard_map/ppermute | solution.py:65
  96.1 0.8 table_sums.1
  96.9 2.4 %collective-permute-done.24.refs_2_ = bf16[64,640]{1,0:T(8,128)(2,1)S(1)} collective-permute-done((bf16[64,640]{1,0:T(8,128)(2,1)S(1)}, bf16[64,640]{1,0:T(8,128)(2,1)S(1)}, u32[]{:S(2)}, u32[]{:S(2)}) %collective-permute-start.24) | collective-permute-done | bytes 81952 | tf_op jit(solution)/shard_map/ppermute | solution.py:65
  99.4 1.3 %collective-permute-start.28 = (bf16[64,640]{1,0:T(8,128)(2,1)S(1)}, bf16[64,640]{1,0:T(8,128)(2,1)S(1)}, u32[]{:S(2)}, u32[]{:S(2)}) collective-permute-start(bf16[64,640]{1,0:T(8,128)(2,1)S(1)} %add_up.3.refs_0_), channel_id=1, source_target_pairs={{0,24},{8,16},{16,8},{24,0},{1,25},{9,17},{17,9},{25,1},{2,26},{10... | collective-permute-start | bytes 245768 | tf_op jit(solution)/shard_map/ppermute | solution.py:61
  100.7 1.5 %collective-permute-start.27 = (bf16[64,640]{1,0:T(8,128)(2,1)S(1)}, bf16[64,640]{1,0:T(8,128)(2,1)S(1)}, u32[]{:S(2)}, u32[]{:S(2)}) collective-permute-start(bf16[64,640]{1,0:T(8,128)(2,1)S(1)} %add_up.3.refs_0_), channel_id=1, source_target_pairs={{0,16},{8,24},{16,0},{24,8},{1,17},{9,25},{17,1},{25,9},{2,18},{10... | collective-permute-start | bytes 245768 | tf_op jit(solution)/shard_map/ppermute | solution.py:61
  102.2 0.7 collective-permute-start.26
  102.9 1.9 %collective-permute-done.28.refs_3_ = bf16[64,640]{1,0:T(8,128)(2,1)S(1)} collective-permute-done((bf16[64,640]{1,0:T(8,128)(2,1)S(1)}, bf16[64,640]{1,0:T(8,128)(2,1)S(1)}, u32[]{:S(2)}, u32[]{:S(2)}) %collective-permute-start.28) | collective-permute-done | bytes 81952 | tf_op jit(solution)/shard_map/ppermute | solution.py:61
  104.8 0.8 collective-permute-done.27.refs_2_
  105.6 1.0 collective-permute-done.26.refs_1_
  106.6 0.9 assemble.1
  (29 shorter events, 0.2 us)
Async XLA Ops:
  1.7 16.1 %collective-permute-start = (bf16[1024,128]{1,0:T(8,128)(2,1)S(1)}, bf16[1024,128]{1,0:T(8,128)(2,1)S(1)}, u32[]{:S(2)}, u32[]{:S(2)}) collective-permute-start(bf16[1024,128]{1,0:T(8,128)(2,1)S(1)} %pad_maximum_fusion.chunk_ref), channel_id=1, source_target_pairs={{0,4},{1,5},{2,6},{3,7},{4,0},{5,1},{6,2},{7,3},{8,12},{9,13},{10,... | collective-permute-start | bytes 786440 | tf_op jit(solution)/shard_map/ppermute | solution.py:65
  6.5 1.7 %collective-permute-start.2 = (s32[2,512]{1,0:T(2,128)S(1)}, s32[2,512]{1,0:T(2,128)S(1)}, u32[]{:S(2)}, u32[]{:S(2)}) collective-permute-start(s32[2,512]{1,0:T(2,128)S(1)} %get-tuple-element.106), channel_id=1, source_target_pairs={{0,1},{1,0},{2,3},{3,2},{4,5},{5,4},{6,7},{7,6},{8,9},{9,8},{10,11... | collective-permute-start | bytes 12296 | tf_op jit(solution)/shard_map/ppermute | solution.py:68
  6.6 15.5 %collective-permute-start.6 = (bf16[1024,128]{1,0:T(8,128)(2,1)S(1)}, bf16[1024,128]{1,0:T(8,128)(2,1)S(1)}, u32[]{:S(2)}, u32[]{:S(2)}) collective-permute-start(bf16[1024,128]{1,0:T(8,128)(2,1)S(1)} %pad_maximum_fusion.chunk_ref), channel_id=1, source_target_pairs={{0,2},{1,3},{2,0},{3,1},{4,6},{5,7},{6,4},{7,5},{8,10},{9,11},{10,... | collective-permute-start | bytes 786440 | tf_op jit(solution)/shard_map/ppermute | solution.py:65
  8.2 10.2 %collective-permute-start.4 = (s32[2,2,512]{2,1,0:T(2,128)S(1)}, s32[2,2,512]{2,1,0:T(2,128)S(1)}, u32[]{:S(2)}, u32[]{:S(2)}) collective-permute-start(s32[2,2,512]{2,1,0:T(2,128)S(1)} %get-tuple-element.104), channel_id=1, source_target_pairs={{0,16},{8,24},{16,0},{24,8},{1,17},{9,25},{17,1},{25,9},{2,18},{10... | collective-permute-start | bytes 24584 | tf_op jit(solution)/shard_map/ppermute | solution.py:61
  9.8 8.6 %collective-permute-start.3 = (s32[2,2,512]{2,1,0:T(2,128)S(1)}, s32[2,2,512]{2,1,0:T(2,128)S(1)}, u32[]{:S(2)}, u32[]{:S(2)}) collective-permute-start(s32[2,2,512]{2,1,0:T(2,128)S(1)} %get-tuple-element.104), channel_id=1, source_target_pairs={{0,8},{8,0},{16,24},{24,16},{1,9},{9,1},{17,25},{25,17},{2,10},{10... | collective-permute-start | bytes 24584 | tf_op jit(solution)/shard_map/ppermute | solution.py:61
  11.3 7.1 %collective-permute-start.5 = (s32[2,2,512]{2,1,0:T(2,128)S(1)}, s32[2,2,512]{2,1,0:T(2,128)S(1)}, u32[]{:S(2)}, u32[]{:S(2)}) collective-permute-start(s32[2,2,512]{2,1,0:T(2,128)S(1)} %get-tuple-element.104), channel_id=1, source_target_pairs={{0,24},{8,16},{16,8},{24,0},{1,25},{9,17},{17,9},{25,1},{2,26},{10... | collective-permute-start | bytes 24584 | tf_op jit(solution)/shard_map/ppermute | solution.py:61
  17.8 9.0 %collective-permute-start.1 = (bf16[1024,128]{1,0:T(8,128)(2,1)S(1)}, bf16[1024,128]{1,0:T(8,128)(2,1)S(1)}, u32[]{:S(2)}, u32[]{:S(2)}) collective-permute-start(bf16[1024,128]{1,0:T(8,128)(2,1)S(1)} %collective-permute-done.chunk_ref), channel_id=1, source_target_pairs={{0,2},{1,3},{2,0},{3,1},{4,6},{5,7},{6,4},{7,5},{8,10},{9,11},{10,... | collective-permute-start | bytes 786440 | tf_op jit(solution)/shard_map/ppermute | solution.py:65
  28.0 2.0 %collective-permute-start.7 = (bf16[4,512,128]{2,1,0:T(8,128)(2,1)S(1)}, bf16[4,512,128]{2,1,0:T(8,128)(2,1)S(1)}, u32[]{:S(2)}, u32[]{:S(2)}) collective-permute-start(bf16[4,512,128]{2,1,0:T(8,128)(2,1)S(1)} %fetch.9), channel_id=1, source_target_pairs={{0,1},{1,0},{2,3},{3,2},{4,5},{5,4},{6,7},{7,6},{8,9},{9,8},{10,11... | collective-permute-start | bytes 1572872 | tf_op jit(solution)/shard_map/ppermute | solution.py:68
  28.1 11.7 %copy-start = (bf16[512,512]{1,0:T(8,128)(2,1)S(1)}, bf16[512,512]{1,0:T(8,128)(2,1)}, u32[]{:S(2)}) copy-start(bf16[512,512]{1,0:T(8,128)(2,1)} %c_ref.1) | copy-start | bytes 1572868
  28.1 11.7 %copy-start.1 = (bf16[512,2048]{1,0:T(8,128)(2,1)S(1)}, bf16[512,2048]{1,0:T(8,128)(2,1)}, u32[]{:S(2)}) copy-start(bf16[512,2048]{1,0:T(8,128)(2,1)} %wp_ref.1) | copy-start | bytes 6291460
  28.1 11.6 %copy-start.2 = (bf16[512,512]{1,0:T(8,128)(2,1)S(1)}, bf16[512,512]{1,0:T(8,128)(2,1)}, u32[]{:S(2)}) copy-start(bf16[512,512]{1,0:T(8,128)(2,1)} %wo_ref.1) | copy-start | bytes 1572868
  28.2 11.6 %copy-start.3 = (f32[512]{0:T(512)S(1)}, f32[512]{0:T(512)}, u32[]{:S(2)}) copy-start(f32[512]{0:T(512)} %param.16) | copy-start | bytes 6148
  30.2 5.9 %collective-permute-start.8 = (bf16[512,128]{1,0:T(8,128)(2,1)S(1)}, bf16[512,128]{1,0:T(8,128)(2,1)S(1)}, u32[]{:S(2)}, u32[]{:S(2)}) collective-permute-start(bf16[512,128]{1,0:T(8,128)(2,1)S(1)} %get-tuple-element.61), channel_id=1, source_target_pairs={{0,8},{8,0},{16,24},{24,16},{1,9},{9,1},{17,25},{25,17},{2,10},{10... | collective-permute-start | bytes 393224 | tf_op jit(solution)/shard_map/ppermute | solution.py:61
  31.7 8.1 %collective-permute-start.9 = (bf16[512,128]{1,0:T(8,128)(2,1)S(1)}, bf16[512,128]{1,0:T(8,128)(2,1)S(1)}, u32[]{:S(2)}, u32[]{:S(2)}) collective-permute-start(bf16[512,128]{1,0:T(8,128)(2,1)S(1)} %get-tuple-element.62), channel_id=1, source_target_pairs={{0,16},{8,24},{16,0},{24,8},{1,17},{9,25},{17,1},{25,9},{2,18},{10... | collective-permute-start | bytes 393224 | tf_op jit(solution)/shard_map/ppermute | solution.py:61
  33.2 6.5 %collective-permute-start.10 = (bf16[512,128]{1,0:T(8,128)(2,1)S(1)}, bf16[512,128]{1,0:T(8,128)(2,1)S(1)}, u32[]{:S(2)}, u32[]{:S(2)}) collective-permute-start(bf16[512,128]{1,0:T(8,128)(2,1)S(1)} %get-tuple-element.63), channel_id=1, source_target_pairs={{0,24},{8,16},{16,8},{24,0},{1,25},{9,17},{17,9},{25,1},{2,26},{10... | collective-permute-start | bytes 393224 | tf_op jit(solution)/shard_map/ppermute | solution.py:61
  53.0 3.5 %collective-permute-start.14 = (bf16[4,256,640]{2,1,0:T(8,128)(2,1)S(1)}, bf16[4,256,640]{2,1,0:T(8,128)(2,1)S(1)}, u32[]{:S(2)}, u32[]{:S(2)}) collective-permute-start(bf16[4,256,640]{2,1,0:T(8,128)(2,1)S(1)} %get-tuple-element.72), channel_id=1, source_target_pairs={{0,1},{1,0},{2,3},{3,2},{4,5},{5,4},{6,7},{7,6},{8,9},{9,8},{10,11... | collective-permute-start | bytes 3932168 | tf_op jit(solution)/shard_map/ppermute | solution.py:68
  53.0 6.3 %collective-permute-start.11 = (bf16[512,128]{1,0:T(8,128)(2,1)S(1)}, bf16[512,128]{1,0:T(8,128)(2,1)S(1)}, u32[]{:S(2)}, u32[]{:S(2)}) collective-permute-start(bf16[512,128]{1,0:T(8,128)(2,1)S(1)} %get-tuple-element.66), channel_id=1, source_target_pairs={{0,8},{8,0},{16,24},{24,16},{1,9},{9,1},{17,25},{25,17},{2,10},{10... | collective-permute-start | bytes 393224 | tf_op jit(solution)/shard_map/ppermute | solution.py:61
  54.2 6.8 %collective-permute-start.12 = (bf16[512,128]{1,0:T(8,128)(2,1)S(1)}, bf16[512,128]{1,0:T(8,128)(2,1)S(1)}, u32[]{:S(2)}, u32[]{:S(2)}) collective-permute-start(bf16[512,128]{1,0:T(8,128)(2,1)S(1)} %get-tuple-element.67), channel_id=1, source_target_pairs={{0,16},{8,24},{16,0},{24,8},{1,17},{9,25},{17,1},{25,9},{2,18},{10... | collective-permute-start | bytes 393224 | tf_op jit(solution)/shard_map/ppermute | solution.py:61
  55.0 7.6 %collective-permute-start.13 = (bf16[512,128]{1,0:T(8,128)(2,1)S(1)}, bf16[512,128]{1,0:T(8,128)(2,1)S(1)}, u32[]{:S(2)}, u32[]{:S(2)}) collective-permute-start(bf16[512,128]{1,0:T(8,128)(2,1)S(1)} %get-tuple-element.68), channel_id=1, source_target_pairs={{0,24},{8,16},{16,8},{24,0},{1,25},{9,17},{17,9},{25,1},{2,26},{10... | collective-permute-start | bytes 393224 | tf_op jit(solution)/shard_map/ppermute | solution.py:61
  62.7 3.7 %collective-permute-start.15 = (bf16[4,512,128]{2,1,0:T(8,128)(2,1)S(1)}, bf16[4,512,128]{2,1,0:T(8,128)(2,1)S(1)}, u32[]{:S(2)}, u32[]{:S(2)}) collective-permute-start(bf16[4,512,128]{2,1,0:T(8,128)(2,1)S(1)} %pack.1.refs_0_), channel_id=1, source_target_pairs={{0,1},{1,0},{2,3},{3,2},{4,5},{5,4},{6,7},{7,6},{8,9},{9,8},{10,11... | collective-permute-start | bytes 1572872 | tf_op jit(solution)/shard_map/ppermute | solution.py:68
  62.8 10.1 %collective-permute-start.19 = (bf16[2,128,640]{2,1,0:T(8,128)(2,1)S(1)}, bf16[2,128,640]{2,1,0:T(8,128)(2,1)S(1)}, u32[]{:S(2)}, u32[]{:S(2)}) collective-permute-start(bf16[2,128,640]{2,1,0:T(8,128)(2,1)S(1)} %get-tuple-element.74), channel_id=1, source_target_pairs={{0,8},{8,0},{16,24},{24,16},{1,9},{9,1},{17,25},{25,17},{2,10},{10... | collective-permute-start | bytes 983048 | tf_op jit(solution)/shard_map/ppermute | solution.py:61
  63.6 9.8 %collective-permute-start.20 = (bf16[2,128,640]{2,1,0:T(8,128)(2,1)S(1)}, bf16[2,128,640]{2,1,0:T(8,128)(2,1)S(1)}, u32[]{:S(2)}, u32[]{:S(2)}) collective-permute-start(bf16[2,128,640]{2,1,0:T(8,128)(2,1)S(1)} %get-tuple-element.76), channel_id=1, source_target_pairs={{0,16},{8,24},{16,0},{24,8},{1,17},{9,25},{17,1},{25,9},{2,18},{10... | collective-permute-start | bytes 983048 | tf_op jit(solution)/shard_map/ppermute | solution.py:61
  67.6 8.2 %collective-permute-start.16 = (bf16[1024,128]{1,0:T(8,128)(2,1)S(1)}, bf16[1024,128]{1,0:T(8,128)(2,1)S(1)}, u32[]{:S(2)}, u32[]{:S(2)}) collective-permute-start(bf16[1024,128]{1,0:T(8,128)(2,1)S(1)} %gather_grad.7), channel_id=1, source_target_pairs={{0,2},{1,3},{2,0},{3,1},{4,6},{5,7},{6,4},{7,5},{8,10},{9,11},{10,... | collective-permute-start | bytes 786440 | tf_op jit(solution)/shard_map/ppermute | solution.py:65
  73.7 8.3 %collective-permute-start.21 = (bf16[1,128,640]{2,1,0:T(8,128)(2,1)S(1)}, bf16[1,128,640]{2,1,0:T(8,128)(2,1)S(1)}, u32[]{:S(2)}, u32[]{:S(2)}) collective-permute-start(bf16[1,128,640]{2,1,0:T(8,128)(2,1)S(1)} %get-tuple-element.89), channel_id=1, source_target_pairs={{0,16},{8,24},{16,0},{24,8},{1,17},{9,25},{17,1},{25,9},{2,18},{10... | collective-permute-start | bytes 491528 | tf_op jit(solution)/shard_map/ppermute | solution.py:61
  75.2 6.8 %collective-permute-start.22 = (bf16[1,128,640]{2,1,0:T(8,128)(2,1)S(1)}, bf16[1,128,640]{2,1,0:T(8,128)(2,1)S(1)}, u32[]{:S(2)}, u32[]{:S(2)}) collective-permute-start(bf16[1,128,640]{2,1,0:T(8,128)(2,1)S(1)} %get-tuple-element.90), channel_id=1, source_target_pairs={{0,8},{8,0},{16,24},{24,16},{1,9},{9,1},{17,25},{25,17},{2,10},{10... | collective-permute-start | bytes 491528 | tf_op jit(solution)/shard_map/ppermute | solution.py:61
  78.2 14.2 %collective-permute-start.17 = (bf16[1024,128]{1,0:T(8,128)(2,1)S(1)}, bf16[1024,128]{1,0:T(8,128)(2,1)S(1)}, u32[]{:S(2)}, u32[]{:S(2)}) collective-permute-start(bf16[1024,128]{1,0:T(8,128)(2,1)S(1)} %gather_grad.9), channel_id=1, source_target_pairs={{0,2},{1,3},{2,0},{3,1},{4,6},{5,7},{6,4},{7,5},{8,10},{9,11},{10,... | collective-permute-start | bytes 786440 | tf_op jit(solution)/shard_map/ppermute | solution.py:65
  79.7 16.4 %collective-permute-start.18 = (bf16[1024,128]{1,0:T(8,128)(2,1)S(1)}, bf16[1024,128]{1,0:T(8,128)(2,1)S(1)}, u32[]{:S(2)}, u32[]{:S(2)}) collective-permute-start(bf16[1024,128]{1,0:T(8,128)(2,1)S(1)} %add_up.2), channel_id=1, source_target_pairs={{0,4},{1,5},{2,6},{3,7},{4,0},{5,1},{6,2},{7,3},{8,12},{9,13},{10,... | collective-permute-start | bytes 786440 | tf_op jit(solution)/shard_map/ppermute | solution.py:65
  82.1 14.8 %collective-permute-start.23 = (bf16[64,640]{1,0:T(8,128)(2,1)S(1)}, bf16[64,640]{1,0:T(8,128)(2,1)S(1)}, u32[]{:S(2)}, u32[]{:S(2)}) collective-permute-start(bf16[64,640]{1,0:T(8,128)(2,1)S(1)} %get-tuple-element.94), channel_id=1, source_target_pairs={{0,2},{1,3},{2,0},{3,1},{4,6},{5,7},{6,4},{7,5},{8,10},{9,11},{10,... | collective-permute-start | bytes 245768 | tf_op jit(solution)/shard_map/ppermute | solution.py:65
  83.9 15.4 %collective-permute-start.24 = (bf16[64,640]{1,0:T(8,128)(2,1)S(1)}, bf16[64,640]{1,0:T(8,128)(2,1)S(1)}, u32[]{:S(2)}, u32[]{:S(2)}) collective-permute-start(bf16[64,640]{1,0:T(8,128)(2,1)S(1)} %get-tuple-element.95), channel_id=1, source_target_pairs={{0,4},{1,5},{2,6},{3,7},{4,0},{5,1},{6,2},{7,3},{8,12},{9,13},{10,... | collective-permute-start | bytes 245768 | tf_op jit(solution)/shard_map/ppermute | solution.py:65
  84.2 15.1 %collective-permute-start.25 = (bf16[64,640]{1,0:T(8,128)(2,1)S(1)}, bf16[64,640]{1,0:T(8,128)(2,1)S(1)}, u32[]{:S(2)}, u32[]{:S(2)}) collective-permute-start(bf16[64,640]{1,0:T(8,128)(2,1)S(1)} %get-tuple-element.96), channel_id=1, source_target_pairs={{0,6},{1,7},{2,4},{3,5},{4,2},{5,3},{6,0},{7,1},{8,14},{9,15},{10,... | collective-permute-start | bytes 245768 | tf_op jit(solution)/shard_map/ppermute | solution.py:65
  99.4 5.5 %collective-permute-start.28 = (bf16[64,640]{1,0:T(8,128)(2,1)S(1)}, bf16[64,640]{1,0:T(8,128)(2,1)S(1)}, u32[]{:S(2)}, u32[]{:S(2)}) collective-permute-start(bf16[64,640]{1,0:T(8,128)(2,1)S(1)} %add_up.3.refs_0_), channel_id=1, source_target_pairs={{0,24},{8,16},{16,8},{24,0},{1,25},{9,17},{17,9},{25,1},{2,26},{10... | collective-permute-start | bytes 245768 | tf_op jit(solution)/shard_map/ppermute | solution.py:61
  100.7 5.0 %collective-permute-start.27 = (bf16[64,640]{1,0:T(8,128)(2,1)S(1)}, bf16[64,640]{1,0:T(8,128)(2,1)S(1)}, u32[]{:S(2)}, u32[]{:S(2)}) collective-permute-start(bf16[64,640]{1,0:T(8,128)(2,1)S(1)} %add_up.3.refs_0_), channel_id=1, source_target_pairs={{0,16},{8,24},{16,0},{24,8},{1,17},{9,25},{17,1},{25,9},{2,18},{10... | collective-permute-start | bytes 245768 | tf_op jit(solution)/shard_map/ppermute | solution.py:61
  102.2 4.4 %collective-permute-start.26 = (bf16[64,640]{1,0:T(8,128)(2,1)S(1)}, bf16[64,640]{1,0:T(8,128)(2,1)S(1)}, u32[]{:S(2)}, u32[]{:S(2)}) collective-permute-start(bf16[64,640]{1,0:T(8,128)(2,1)S(1)} %add_up.3.refs_0_), channel_id=1, source_target_pairs={{0,8},{8,0},{16,24},{24,16},{1,9},{9,1},{17,25},{25,17},{2,10},{10... | collective-permute-start | bytes 245768 | tf_op jit(solution)/shard_map/ppermute | solution.py:61

commit v8 on v7

--- a/solution.py
+++ b/solution.py
@@ -12,6 +12,7 @@
 BF16 = jnp.bfloat16
 I32 = jnp.int32
 MIB = 1024 * 1024
+EARLY = 6 * 10**9
 
 NN = ((1,), (0,))
 NT = ((1,), (1,))
@@ -128,31 +129,34 @@
     return run("add_up", body, [(parts[0].shape, BF16)], parts)[0]
 
 
-def table_sums(here, whole, halves):
+def table_sums(here, came, out, flops=0):
     rows, cols = here.shape[0] // 2, here.shape[1]
+    cuts = 2 if out else 1
 
     def body(here_ref, *refs):
-        whole_refs, half_refs, out_refs = refs[: len(whole)], refs[len(whole) : -2], refs[-2:]
+        came_refs, out_refs = refs[:-cuts], refs[-cuts:]
         for i in range(2):
             span = slice(i * rows, (i + 1) * rows)
             total = here_ref[span, :]
-            for ref in whole_refs:
+            for ref in came_refs:
                 total = total + ref[span, :].astype(F32)
-            for ref in half_refs[i::2]:
-                total = total + ref[...].astype(F32)
-            out_refs[i][...] = total
-
-    return run("table_sums", body, [((rows, cols), F32)] * 2, [here, *whole, *halves])
-
-
-def gather_grad(base, keys, cohorts, tokens, rows, before=(), out=BF16, apart=False):
+            if out:
+                out_refs[i][...] = total
+            else:
+                out_refs[0][span, :] = total
+
+    outs = [((2 * rows // cuts, cols), F32)] * cuts
+    return run("table_sums", body, outs, [here, *came], flops=flops)
+
+
+def gather_grad(base, keys, cohorts, tokens, rows, before=(), out=BF16):
     many = len(cohorts)
     count, _, _, length = keys.shape
     cols = tokens[0].shape[-1]
 
     def body(base_ref, key_ref, *refs):
         piece_refs, before_refs = refs[:many], refs[many : many + len(before)]
-        out_refs = refs[many + len(before) :]
+        out_ref = refs[-1]
         row = lax.broadcasted_iota(I32, (rows, length), 0)
         for table in range(2):
             span = slice(table * rows, (table + 1) * rows)
@@ -167,15 +171,12 @@
                 sums = part if sums is None else sums + part
             for ref in before_refs:
                 sums = sums + ref[span, :].astype(F32)
-            if apart:
-                out_refs[table][...] = sums.astype(out)
-            else:
-                out_refs[0][span, :] = sums.astype(out)
+            out_ref[span, :] = sums.astype(out)
 
     return run(
         "gather_grad",
         body,
-        [((rows, cols), out)] * 2 if apart else [((2 * rows, cols), out)],
+        [((2 * rows, cols), out)],
         [base, keys, *tokens, *before],
         smem=1,
         flops=4 * many * count * length * 2 * rows * cols,
@@ -410,16 +411,29 @@
             scratch[p * tall : (p + 1) * tall] = kept_refs[p][0] + came_refs[p][0].astype(F32)
         for k in range(line):
             span = pl.ds(pl.multiple_of((place_ref[0] ^ k) * rows, rows), rows)
-            out_refs[k][...] = scratch[span].astype(out_refs[k].dtype)
-
+            out_refs[k % 2][k // 2] = scratch[span].astype(out_refs[k % 2].dtype)
+
+    half = (line // 2, rows, cols)
     return run(
         "cut_line",
         body,
-        [((rows, cols), F32)] + [((rows, cols), BF16)] * (line - 1),
+        [(half, F32), (half, BF16)],
         [place, *kept, *came],
         smem=1,
         scratch=[pltpu.VMEM((many * tall, cols), F32)],
     )
+
+
+def fold_line(kept, came):
+    count, rows, cols = kept.shape
+
+    def body(kept_ref, came_ref, *out_refs):
+        for k in range(count):
+            total = kept_ref[k] + came_ref[k].astype(F32)
+            out_refs[k % 2][k // 2] = total.astype(out_refs[k % 2].dtype)
+
+    half = (count // 2, rows, cols)
+    return run("fold_line", body, [(half, F32), (half, BF16)], [kept, came])
 
 
 def assemble(replica, parts, edge):
@@ -538,21 +552,26 @@
             if k == 1 and line > 2:
                 both_there = lax.optimization_barrier((both_there, sums[line // 2]))[0]
             raw[k] = gather_grad(bases[k], keys, both, both_there, rows, out=out)
-        came = [[grid.over_line(part, step) for part in sums[k ^ step]] for step in steps]
+        came = [grid.over_line(sums[k ^ step], step) for step in steps]
         if k == 0:
-            whole = [parts[0] for parts in came if len(parts) == 1]
-            halves = [part for parts in came if len(parts) == 2 for part in parts]
-            item_grad, action_grad = table_sums(raw[k][0], whole, halves)
+            table = raw[k]
+            if len(came) > 1:
+                table = table_sums(table[0], came[1:], out=False, flops=EARLY)
+            item_grad, action_grad = table_sums(table[0], came[:1], out=True)
         else:
-            sums[k] = [add_up(raw[k] + [parts[0] for parts in came])] if steps else raw[k]
+            sums[k] = add_up(raw[k] + came) if steps else raw[k][0]
 
     for step in range(1, bits + 1):
         after = raw[line // 2] if step < bits else sums[line // 2]
         swapped = lax.optimization_barrier((swapped, after))[0]
         if step < bits:
             kept, swapped = swap_weights(fold(replica, kept, swapped, step), step)
-    parts = cut_line(place, kept, swapped, line)
-    parts = [parts[0]] + [grid.over_line(parts[k], k) for k in range(1, line)]
+    kept, sent = cut_line(place, kept, swapped, line)
+    step = 1
+    while step < line // 2:
+        kept, sent = fold_line(kept, grid.over_line(sent, step))
+        step *= 2
+    parts = [kept[0], grid.over_line(sent, step)[0]]
     parts = lax.optimization_barrier((parts, item_grad))[0]
     total = add_up(parts)
     parts = [total] + [grid.over_replica(total, k) for k in range(1, replicas)]

time: 108 us -> 107 us (level)
  starting transfers between devices: 35 us -> 32.5 us
  waiting for transfers between devices: 32.3 us -> 33.6 us
    ppermute x9 -> x8, starting transfers between devices: 16.1 us -> 13.6 us  [over_line(): return lax.ppermute(value, 'sparse', pairs)]
    ppermute x9 -> x8, waiting for transfers between devices: 15.7 us -> 16.7 us  [over_line(): return lax.ppermute(value, 'sparse', pairs)]
    pallas_call x20 -> x22, Pallas kernels: 36.4 us -> 36.4 us  [run(): pl.pallas_call(body, out_shape=outs, in_specs=places, out_specs=[in_vmem]...]
  transfers between devices with their start and end apart: 29 -> 28, of which waited for: 15 -> 16; matrix products, arithmetic and copies ran while one was open for 2% -> 2% of each run, Pallas kernels for 19% -> 20%
where the time goes in v8:
time: 107 us; the launch traced here: 106 us
  Pallas kernels  36.4 us (34%)
  waiting for transfers between devices  33.6 us (31%)
  starting transfers between devices  32.5 us (30%)
  local copies, waits for them, and re-layouts  2.25 us (2%)
    pallas_call x22, Pallas kernels, run(): pl.pallas_call(body, out_shape=outs, in_specs=places, out_specs=[in_vmem]...  36.4 us
    ppermute x16, starting transfers between devices, over_replica(): return lax.ppermute(value, 'replica', [(i, i ^ step) for i in range(n)])  18.6 us
    ppermute x8, waiting for transfers between devices, over_line(): return lax.ppermute(value, 'sparse', pairs)  16.7 us
    ppermute x16, waiting for transfers between devices, over_replica(): return lax.ppermute(value, 'replica', [(i, i ^ step) for i in range(n)])  16.3 us
    ppermute x8, starting transfers between devices, over_line(): return lax.ppermute(value, 'sparse', pairs)  13.6 us
  transfers between devices with their start and end apart: 28, of which 16 were waited for; matrix products, arithmetic and copies ran while one was open for 2% of the time, Pallas kernels for 20%

profile of v8, /device:TPU:0, one launch (start us, length us, event | category | flops | bytes accessed | tf_op | source)
XLA Modules:
  0.0 106.4 jit_solution(9123991644623868622)
XLA Ops:
  0.6 1.0 constant_dynamic-slice_fusion
  1.7 4.1 %collective-permute-start = (bf16[1024,128]{1,0:T(8,128)(2,1)S(1)}, bf16[1024,128]{1,0:T(8,128)(2,1)S(1)}, u32[]{:S(2)}, u32[]{:S(2)}) collective-permute-start(bf16[1024,128]{1,0:T(8,128)(2,1)S(1)} %pad_maximum_fusion.chunk_ref), channel_id=1, source_target_pairs={{0,4},{1,5},{2,6},{3,7},{4,0},{5,1},{6,2},{7,3},{8,12},{9,13},{10,... | collective-permute-start | bytes 786440 | tf_op jit(solution)/shard_map/ppermute | solution.py:66
  5.8 0.7 add_bitcast_fusion
  6.5 0.1 collective-permute-start.2
  6.6 1.6 %collective-permute-start.6 = (bf16[1024,128]{1,0:T(8,128)(2,1)S(1)}, bf16[1024,128]{1,0:T(8,128)(2,1)S(1)}, u32[]{:S(2)}, u32[]{:S(2)}) collective-permute-start(bf16[1024,128]{1,0:T(8,128)(2,1)S(1)} %pad_maximum_fusion.chunk_ref), channel_id=1, source_target_pairs={{0,2},{1,3},{2,0},{3,1},{4,6},{5,7},{6,4},{7,5},{8,10},{9,11},{10,... | collective-permute-start | bytes 786440 | tf_op jit(solution)/shard_map/ppermute | solution.py:66
  8.2 1.6 %collective-permute-start.4 = (s32[2,2,512]{2,1,0:T(2,128)S(1)}, s32[2,2,512]{2,1,0:T(2,128)S(1)}, u32[]{:S(2)}, u32[]{:S(2)}) collective-permute-start(s32[2,2,512]{2,1,0:T(2,128)S(1)} %get-tuple-element.100), channel_id=1, source_target_pairs={{0,16},{8,24},{16,0},{24,8},{1,17},{9,25},{17,1},{25,9},{2,18},{10... | collective-permute-start | bytes 24584 | tf_op jit(solution)/shard_map/ppermute | solution.py:62
  9.8 1.5 %collective-permute-start.3 = (s32[2,2,512]{2,1,0:T(2,128)S(1)}, s32[2,2,512]{2,1,0:T(2,128)S(1)}, u32[]{:S(2)}, u32[]{:S(2)}) collective-permute-start(s32[2,2,512]{2,1,0:T(2,128)S(1)} %get-tuple-element.100), channel_id=1, source_target_pairs={{0,8},{8,0},{16,24},{24,16},{1,9},{9,1},{17,25},{25,17},{2,10},{10... | collective-permute-start | bytes 24584 | tf_op jit(solution)/shard_map/ppermute | solution.py:62
  11.3 0.5 collective-permute-start.5
  11.8 6.0 %collective-permute-done.chunk_ref = bf16[1024,128]{1,0:T(8,128)(2,1)S(1)} collective-permute-done((bf16[1024,128]{1,0:T(8,128)(2,1)S(1)}, bf16[1024,128]{1,0:T(8,128)(2,1)S(1)}, u32[]{:S(2)}, u32[]{:S(2)}) %collective-permute-start) | collective-permute-done | bytes 262176 | tf_op jit(solution)/shard_map/ppermute | solution.py:66
  17.8 0.7 collective-permute-start.1
  18.5 1.2 %broadcast_in_dim.14.key_ref = s32[4,2,2,512,128]{4,3,2,1,0:T(8,128)S(1)} broadcast(s32[4,2,2,512]{3,2,1,0:T(2,128)S(1)} %pad_add_fusion.key_ref), dimensions={0,1,2,3} | broadcast | bytes 4227072 | tf_op jit(solution)/shard_map/broadcast_in_dim | solution.py:510
  19.7 2.3 %fetch.5 = (bf16[4,512,128]{2,1,0:T(8,128)(2,1)S(1)}, bf16[4,512,128]{2,1,0:T(8,128)(2,1)S(1)}) custom-call(s32[1]{0:T(128)S(6)} %mul.44.base_ref, bf16[1024,128]{1,0:T(8,128)(2,1)S(1)} %pad_maximum_fusion.chunk_ref, s32[4,2,2,512,128]{4,3,2,1,0:T(8,128)S(1)} %broadcast_in_dim.14.key_ref), custom_call_target="tpu_custom_call" | custom-call | flops 536870912 | bytes 5505028 | tf_op jit(solution)/shard_map/fetch/pallas_call | solution.py:36
  22.1 2.3 %fetch.6 = (bf16[4,512,128]{2,1,0:T(8,128)(2,1)S(1)}, bf16[4,512,128]{2,1,0:T(8,128)(2,1)S(1)}) custom-call(s32[1]{0:T(128)S(6)} %mul.42.base_ref, bf16[1024,128]{1,0:T(8,128)(2,1)S(1)} %collective-permute-done.6.chunk_ref, s32[4,2,2,512,128]{4,3,2,1,0:T(8,128)S(1)} %broadcast_in_dim.14.key_ref, bf16[4,512,128]{2,1,0:T(8,128)(2,1)S(1)} %get-tuple-element.52.refs_0_, ...), custom_call_target="tpu_custom_call" | custom-call | flops 536870912 | bytes 6553604 | tf_op jit(solution)/shard_map/fetch/pallas_call | solution.py:36
  24.4 2.3 %fetch.7 = (bf16[4,512,128]{2,1,0:T(8,128)(2,1)S(1)}, bf16[4,512,128]{2,1,0:T(8,128)(2,1)S(1)}) custom-call(s32[1]{0:T(128)S(6)} %mul.40.base_ref, bf16[1024,128]{1,0:T(8,128)(2,1)S(1)} %collective-permute-done.chunk_ref, s32[4,2,2,512,128]{4,3,2,1,0:T(8,128)S(1)} %broadcast_in_dim.14.key_ref, bf16[4,512,128]{2,1,0:T(8,128)(2,1)S(1)} %get-tuple-element.54.refs_0_, ...), custom_call_target="tpu_custom_call" | custom-call | flops 536870912 | bytes 6553604 | tf_op jit(solution)/shard_map/fetch/pallas_call | solution.py:36
  26.8 1.3 %fetch.9 = bf16[4,512,128]{2,1,0:T(8,128)(2,1)S(1)} custom-call(s32[1]{0:T(128)S(6)} %mul.35.base_ref, bf16[1024,128]{1,0:T(8,128)(2,1)S(1)} %collective-permute-done.1.chunk_ref, s32[4,2,2,512,128]{4,3,2,1,0:T(8,128)S(1)} %broadcast_in_dim.14.key_ref, bf16[4,512,128]{2,1,0:T(8,128)(2,1)S(1)} %get-tuple-element.57.refs_0_), custom_call_target="tpu_custom_call" | custom-call | flops 268435456 | bytes 5505028 | tf_op jit(solution)/shard_map/fetch/pallas_call | solution.py:36
  28.0 0.1 collective-permute-start.7
  28.2 1.2 %fetch.8.left_ref = bf16[4,512,128]{2,1,0:T(8,128)(2,1)S(1)} custom-call(s32[1]{0:T(128)S(6)} %mul.35.base_ref, bf16[1024,128]{1,0:T(8,128)(2,1)S(1)} %collective-permute-done.1.chunk_ref, s32[4,2,2,512,128]{4,3,2,1,0:T(8,128)S(1)} %broadcast_in_dim.14.key_ref, bf16[4,512,128]{2,1,0:T(8,128)(2,1)S(1)} %get-tuple-element.56.refs_0_), custom_call_target="tpu_custom_call" | custom-call | flops 268435456 | bytes 5505028 | tf_op jit(solution)/shard_map/fetch/pallas_call | solution.py:36
  29.4 0.6 collective-permute-done.7.right_ref
  30.0 0.1 combine.1
  30.1 1.6 %collective-permute-start.8 = (bf16[512,128]{1,0:T(8,128)(2,1)S(1)}, bf16[512,128]{1,0:T(8,128)(2,1)S(1)}, u32[]{:S(2)}, u32[]{:S(2)}) collective-permute-start(bf16[512,128]{1,0:T(8,128)(2,1)S(1)} %get-tuple-element.59), channel_id=1, source_target_pairs={{0,8},{8,0},{16,24},{24,16},{1,9},{9,1},{17,25},{25,17},{2,10},{10... | collective-permute-start | bytes 393224 | tf_op jit(solution)/shard_map/ppermute | solution.py:62
  31.7 1.5 %collective-permute-start.9 = (bf16[512,128]{1,0:T(8,128)(2,1)S(1)}, bf16[512,128]{1,0:T(8,128)(2,1)S(1)}, u32[]{:S(2)}, u32[]{:S(2)}) collective-permute-start(bf16[512,128]{1,0:T(8,128)(2,1)S(1)} %get-tuple-element.60), channel_id=1, source_target_pairs={{0,16},{8,24},{16,0},{24,8},{1,17},{9,25},{17,1},{25,9},{2,18},{10... | collective-permute-start | bytes 393224 | tf_op jit(solution)/shard_map/ppermute | solution.py:62
  33.2 0.5 collective-permute-start.10
  33.7 2.4 %collective-permute-done.8.refs_1_ = bf16[512,128]{1,0:T(8,128)(2,1)S(1)} collective-permute-done((bf16[512,128]{1,0:T(8,128)(2,1)S(1)}, bf16[512,128]{1,0:T(8,128)(2,1)S(1)}, u32[]{:S(2)}, u32[]{:S(2)}) %collective-permute-start.8) | collective-permute-done | bytes 131104 | tf_op jit(solution)/shard_map/ppermute | solution.py:62
  36.1 3.7 %collective-permute-done.9.refs_2_ = bf16[512,128]{1,0:T(8,128)(2,1)S(1)} collective-permute-done((bf16[512,128]{1,0:T(8,128)(2,1)S(1)}, bf16[512,128]{1,0:T(8,128)(2,1)S(1)}, u32[]{:S(2)}, u32[]{:S(2)}) %collective-permute-start.9) | collective-permute-done | bytes 131104 | tf_op jit(solution)/shard_map/ppermute | solution.py:62
  39.8 13.1 %sequence.1 = (bf16[512,512]{1,0:T(8,128)(2,1)}, bf16[512,128]{1,0:T(8,128)(2,1)S(1)}, bf16[512,128]{1,0:T(8,128)(2,1)S(1)}, bf16[512,128]{1,0:T(8,128)(2,1)S(1)...) custom-call(s32[1]{0:T(128)} %bitcast.r_ref, ...), custom_call_target="tpu_custom_call" | custom-call | flops 4294967296 | bytes 9177096 | tf_op jit(solution)/shard_map/sequence/pallas_call | solution.py:36
  53.0 1.2 %collective-permute-start.11 = (bf16[512,128]{1,0:T(8,128)(2,1)S(1)}, bf16[512,128]{1,0:T(8,128)(2,1)S(1)}, u32[]{:S(2)}, u32[]{:S(2)}) collective-permute-start(bf16[512,128]{1,0:T(8,128)(2,1)S(1)} %get-tuple-element.64), channel_id=1, source_target_pairs={{0,8},{8,0},{16,24},{24,16},{1,9},{9,1},{17,25},{25,17},{2,10},{10... | collective-permute-start | bytes 393224 | tf_op jit(solution)/shard_map/ppermute | solution.py:62
  54.2 0.8 collective-permute-start.12
  55.0 1.4 %collective-permute-start.13 = (bf16[512,128]{1,0:T(8,128)(2,1)S(1)}, bf16[512,128]{1,0:T(8,128)(2,1)S(1)}, u32[]{:S(2)}, u32[]{:S(2)}) collective-permute-start(bf16[512,128]{1,0:T(8,128)(2,1)S(1)} %get-tuple-element.66), channel_id=1, source_target_pairs={{0,24},{8,16},{16,8},{24,0},{1,25},{9,17},{17,9},{25,1},{2,26},{10... | collective-permute-start | bytes 393224 | tf_op jit(solution)/shard_map/ppermute | solution.py:62
  56.5 1.7 %weight_grad.1 = (f32[2,128,640]{2,1,0:T(8,128)S(1)}, bf16[2,128,640]{2,1,0:T(8,128)(2,1)S(1)}, f32[2,128,640]{2,1,0:T(8,128)S(1)}, bf16[2,128,640]{2,1,0:T(8,128)(2,1)S(1)}) custom-call(s32[1]{0:T(128)} %bitcast.r_ref, s32[1]{0:T(128)} %bitcast.1.core_ref, bf16[512,512]{1,0:T(8,128)(2,1)S(1)} %get-tuple-element.67.n_ref, ...), custom_call_target="tpu_custom_call" | custom-call | flops 939524096 | bytes 6946824 | tf_op jit(solution)/shard_map/weight_grad/pallas_call | solution.py:36
  58.2 1.1 %collective-permute-done.11.refs_1_ = bf16[512,128]{1,0:T(8,128)(2,1)S(1)} collective-permute-done((bf16[512,128]{1,0:T(8,128)(2,1)S(1)}, bf16[512,128]{1,0:T(8,128)(2,1)S(1)}, u32[]{:S(2)}, u32[]{:S(2)}) %collective-permute-start.11) | collective-permute-done | bytes 131104 | tf_op jit(solution)/shard_map/ppermute | solution.py:62
  59.3 1.7 %collective-permute-done.12.refs_2_ = bf16[512,128]{1,0:T(8,128)(2,1)S(1)} collective-permute-done((bf16[512,128]{1,0:T(8,128)(2,1)S(1)}, bf16[512,128]{1,0:T(8,128)(2,1)S(1)}, u32[]{:S(2)}, u32[]{:S(2)}) %collective-permute-start.12) | collective-permute-done | bytes 131104 | tf_op jit(solution)/shard_map/ppermute | solution.py:62
  61.0 1.6 %collective-permute-done.13.refs_3_ = bf16[512,128]{1,0:T(8,128)(2,1)S(1)} collective-permute-done((bf16[512,128]{1,0:T(8,128)(2,1)S(1)}, bf16[512,128]{1,0:T(8,128)(2,1)S(1)}, u32[]{:S(2)}, u32[]{:S(2)}) %collective-permute-start.13) | collective-permute-done | bytes 131104 | tf_op jit(solution)/shard_map/ppermute | solution.py:62
  62.7 0.1 collective-permute-start.15
  62.8 0.9 collective-permute-start.19
  63.6 1.5 %collective-permute-start.20 = (bf16[2,128,640]{2,1,0:T(8,128)(2,1)S(1)}, bf16[2,128,640]{2,1,0:T(8,128)(2,1)S(1)}, u32[]{:S(2)}, u32[]{:S(2)}) collective-permute-start(bf16[2,128,640]{2,1,0:T(8,128)(2,1)S(1)} %get-tuple-element.74), channel_id=1, source_target_pairs={{0,16},{8,24},{16,0},{24,8},{1,17},{9,25},{17,1},{25,9},{2,18},{10... | collective-permute-start | bytes 983048 | tf_op jit(solution)/shard_map/ppermute | solution.py:62
  65.1 1.2 %gather_grad.6.refs_1_ = bf16[1024,128]{1,0:T(8,128)(2,1)S(1)} custom-call(s32[1]{0:T(128)S(6)} %mul.35.base_ref, s32[4,2,2,512]{3,2,1,0:T(2,128)S(1)} %pad_add_fusion.key_ref, bf16[4,512,128]{2,1,0:T(8,128)(2,1)S(1)} %pack.1.refs_0_), custom_call_target="tpu_custom_call" | custom-call | flops 1073741824 | bytes 819204 | tf_op jit(solution)/shard_map/gather_grad/pallas_call | solution.py:36
  66.4 1.2 %gather_grad.7 = bf16[1024,128]{1,0:T(8,128)(2,1)S(1)} custom-call(s32[1]{0:T(128)S(6)} %mul.35.base_ref, s32[4,2,2,512]{3,2,1,0:T(2,128)S(1)} %pad_add_fusion.key_ref, bf16[4,512,128]{2,1,0:T(8,128)(2,1)S(1)} %collective-permute-done.15.refs_1_.refs_0_, bf16[1024,128]{1,0:T(8,128)(2,1)S(1)} %gather_grad.6.refs_1_), custom_call_target="tpu_custom_call" | custom-call | flops 1073741824 | bytes 1081348 | tf_op jit(solution)/shard_map/gather_grad/pallas_call | solution.py:36
  67.6 1.5 %collective-permute-start.16 = (bf16[1024,128]{1,0:T(8,128)(2,1)S(1)}, bf16[1024,128]{1,0:T(8,128)(2,1)S(1)}, u32[]{:S(2)}, u32[]{:S(2)}) collective-permute-start(bf16[1024,128]{1,0:T(8,128)(2,1)S(1)} %gather_grad.7), channel_id=1, source_target_pairs={{0,2},{1,3},{2,0},{3,1},{4,6},{5,7},{6,4},{7,5},{8,10},{9,11},{10,... | collective-permute-start | bytes 786440 | tf_op jit(solution)/shard_map/ppermute | solution.py:66
  69.1 2.5 %gather_grad.5.refs_0_ = f32[1024,128]{1,0:T(8,128)S(1)} custom-call(s32[1]{0:T(128)S(6)} %mul.40.base_ref, s32[4,2,2,512]{3,2,1,0:T(2,128)S(1)} %pad_add_fusion.key_ref, bf16[4,512,128]{2,1,0:T(8,128)(2,1)S(1)} %pack.1.refs_0_, bf16[4,512,128]{2,1,0:T(8,128)(2,1)S(1)} %collective-permute-done.15.refs_1_.refs_0_), custom_call_target="tpu_custom_call" | custom-call | flops 2147483648 | bytes 1605636 | tf_op jit(solution)/shard_map/gather_grad/pallas_call | solution.py:36
  71.7 1.2 %collective-permute-done.19.refs_2_ = bf16[2,128,640]{2,1,0:T(8,128)(2,1)S(1)} collective-permute-done((bf16[2,128,640]{2,1,0:T(8,128)(2,1)S(1)}, bf16[2,128,640]{2,1,0:T(8,128)(2,1)S(1)}, u32[]{:S(2)}, u32[]{:S(2)}) %collective-permute-start.19) | collective-permute-done | bytes 327712 | tf_op jit(solution)/shard_map/ppermute | solution.py:62
  72.9 0.5 collective-permute-done.20.refs_3_
  73.4 0.3 fold.1
  73.7 1.6 %collective-permute-start.21 = (bf16[1,128,640]{2,1,0:T(8,128)(2,1)S(1)}, bf16[1,128,640]{2,1,0:T(8,128)(2,1)S(1)}, u32[]{:S(2)}, u32[]{:S(2)}) collective-permute-start(bf16[1,128,640]{2,1,0:T(8,128)(2,1)S(1)} %get-tuple-element.87), channel_id=1, source_target_pairs={{0,16},{8,24},{16,0},{24,8},{1,17},{9,25},{17,1},{25,9},{2,18},{10... | collective-permute-start | bytes 491528 | tf_op jit(solution)/shard_map/ppermute | solution.py:62
  75.2 0.5 collective-permute-start.22
  75.8 0.1 add_up.2
  75.9 3.5 %collective-permute-start.17 = (bf16[1024,128]{1,0:T(8,128)(2,1)S(1)}, bf16[1024,128]{1,0:T(8,128)(2,1)S(1)}, u32[]{:S(2)}, u32[]{:S(2)}) collective-permute-start(bf16[1024,128]{1,0:T(8,128)(2,1)S(1)} %add_up.2), channel_id=1, source_target_pairs={{0,4},{1,5},{2,6},{3,7},{4,0},{5,1},{6,2},{7,3},{8,12},{9,13},{10,... | collective-permute-start | bytes 786440 | tf_op jit(solution)/shard_map/ppermute | solution.py:66
  79.4 1.2 %collective-permute-done.22.refs_3_ = bf16[1,128,640]{2,1,0:T(8,128)(2,1)S(1)} collective-permute-done((bf16[1,128,640]{2,1,0:T(8,128)(2,1)S(1)}, bf16[1,128,640]{2,1,0:T(8,128)(2,1)S(1)}, u32[]{:S(2)}, u32[]{:S(2)}) %collective-permute-start.22) | collective-permute-done | bytes 163872 | tf_op jit(solution)/shard_map/ppermute | solution.py:62
  80.6 0.1 cut_line.1
  80.7 1.5 %collective-permute-start.23 = (bf16[2,64,640]{2,1,0:T(8,128)(2,1)S(1)}, bf16[2,64,640]{2,1,0:T(8,128)(2,1)S(1)}, u32[]{:S(2)}, u32[]{:S(2)}) collective-permute-start(bf16[2,64,640]{2,1,0:T(8,128)(2,1)S(1)} %get-tuple-element.92), channel_id=1, source_target_pairs={{0,2},{1,3},{2,0},{3,1},{4,6},{5,7},{6,4},{7,5},{8,10},{9,11},{10,... | collective-permute-start | bytes 491528 | tf_op jit(solution)/shard_map/ppermute | solution.py:66
  82.1 2.3 %gather_grad.9 = bf16[1024,128]{1,0:T(8,128)(2,1)S(1)} custom-call(s32[1]{0:T(128)S(6)} %mul.42.base_ref, s32[4,2,2,512]{3,2,1,0:T(2,128)S(1)} %pad_add_fusion.key_ref, bf16[4,512,128]{2,1,0:T(8,128)(2,1)S(1)} %pack.1.refs_0_, bf16[4,512,128]{2,1,0:T(8,128)(2,1)S(1)} %collective-permute-done.15.refs_1_.refs_0_), custom_call_target="tpu_custom_call" | custom-call | flops 2147483648 | bytes 1343492 | tf_op jit(solution)/shard_map/gather_grad/pallas_call | solution.py:36
  84.5 0.7 collective-permute-start.18
  85.1 2.3 %gather_grad.8.here_ref = f32[1024,128]{1,0:T(8,128)S(1)} custom-call(s32[1]{0:T(128)S(6)} %mul.44.base_ref, s32[4,2,2,512]{3,2,1,0:T(2,128)S(1)} %pad_add_fusion.key_ref, bf16[4,512,128]{2,1,0:T(8,128)(2,1)S(1)} %pack.1.refs_0_, bf16[4,512,128]{2,1,0:T(8,128)(2,1)S(1)} %collective-permute-done.15.refs_1_.refs_0_), custom_call_target="tpu_custom_call" | custom-call | flops 2147483648 | bytes 1605636 | tf_op jit(solution)/shard_map/gather_grad/pallas_call | solution.py:36
  87.5 6.2 %collective-permute-done.23.came_ref = bf16[2,64,640]{2,1,0:T(8,128)(2,1)S(1)} collective-permute-done((bf16[2,64,640]{2,1,0:T(8,128)(2,1)S(1)}, bf16[2,64,640]{2,1,0:T(8,128)(2,1)S(1)}, u32[]{:S(2)}, u32[]{:S(2)}) %collective-permute-start.23) | collective-permute-done | bytes 163872 | tf_op jit(solution)/shard_map/ppermute | solution.py:66
  93.7 0.1 collective-permute-start.24
  93.8 4.2 %collective-permute-done.18.refs_0_ = bf16[1024,128]{1,0:T(8,128)(2,1)S(1)} collective-permute-done((bf16[1024,128]{1,0:T(8,128)(2,1)S(1)}, bf16[1024,128]{1,0:T(8,128)(2,1)S(1)}, u32[]{:S(2)}, u32[]{:S(2)}) %collective-permute-start.18) | collective-permute-done | bytes 262176 | tf_op jit(solution)/shard_map/ppermute | solution.py:66
  98.0 0.8 table_sums.3
  98.8 0.3 collective-permute-done.24
  99.1 1.2 %collective-permute-start.27 = (bf16[64,640]{1,0:T(8,128)(2,1)S(1)}, bf16[64,640]{1,0:T(8,128)(2,1)S(1)}, u32[]{:S(2)}, u32[]{:S(2)}) collective-permute-start(bf16[64,640]{1,0:T(8,128)(2,1)S(1)} %add_up.3.refs_0_), channel_id=1, source_target_pairs={{0,24},{8,16},{16,8},{24,0},{1,25},{9,17},{17,9},{25,1},{2,26},{10... | collective-permute-start | bytes 245768 | tf_op jit(solution)/shard_map/ppermute | solution.py:62
  100.4 0.7 collective-permute-start.26
  101.1 1.6 %collective-permute-start.25 = (bf16[64,640]{1,0:T(8,128)(2,1)S(1)}, bf16[64,640]{1,0:T(8,128)(2,1)S(1)}, u32[]{:S(2)}, u32[]{:S(2)}) collective-permute-start(bf16[64,640]{1,0:T(8,128)(2,1)S(1)} %add_up.3.refs_0_), channel_id=1, source_target_pairs={{0,8},{8,0},{16,24},{24,16},{1,9},{9,1},{17,25},{25,17},{2,10},{10... | collective-permute-start | bytes 245768 | tf_op jit(solution)/shard_map/ppermute | solution.py:62
  102.7 1.9 %collective-permute-done.27.refs_3_ = bf16[64,640]{1,0:T(8,128)(2,1)S(1)} collective-permute-done((bf16[64,640]{1,0:T(8,128)(2,1)S(1)}, bf16[64,640]{1,0:T(8,128)(2,1)S(1)}, u32[]{:S(2)}, u32[]{:S(2)}) %collective-permute-start.27) | collective-permute-done | bytes 81952 | tf_op jit(solution)/shard_map/ppermute | solution.py:62
  104.6 0.8 collective-permute-done.26.refs_2_
  105.4 0.1 collective-permute-done.25.refs_1_
  105.5 0.9 assemble.1
  (29 shorter events, 0.3 us)
Async XLA Ops:
  1.7 16.1 %collective-permute-start = (bf16[1024,128]{1,0:T(8,128)(2,1)S(1)}, bf16[1024,128]{1,0:T(8,128)(2,1)S(1)}, u32[]{:S(2)}, u32[]{:S(2)}) collective-permute-start(bf16[1024,128]{1,0:T(8,128)(2,1)S(1)} %pad_maximum_fusion.chunk_ref), channel_id=1, source_target_pairs={{0,4},{1,5},{2,6},{3,7},{4,0},{5,1},{6,2},{7,3},{8,12},{9,13},{10,... | collective-permute-start | bytes 786440 | tf_op jit(solution)/shard_map/ppermute | solution.py:66
  6.5 1.7 %collective-permute-start.2 = (s32[2,512]{1,0:T(2,128)S(1)}, s32[2,512]{1,0:T(2,128)S(1)}, u32[]{:S(2)}, u32[]{:S(2)}) collective-permute-start(s32[2,512]{1,0:T(2,128)S(1)} %get-tuple-element.102), channel_id=1, source_target_pairs={{0,1},{1,0},{2,3},{3,2},{4,5},{5,4},{6,7},{7,6},{8,9},{9,8},{10,11... | collective-permute-start | bytes 12296 | tf_op jit(solution)/shard_map/ppermute | solution.py:69
  6.6 15.5 %collective-permute-start.6 = (bf16[1024,128]{1,0:T(8,128)(2,1)S(1)}, bf16[1024,128]{1,0:T(8,128)(2,1)S(1)}, u32[]{:S(2)}, u32[]{:S(2)}) collective-permute-start(bf16[1024,128]{1,0:T(8,128)(2,1)S(1)} %pad_maximum_fusion.chunk_ref), channel_id=1, source_target_pairs={{0,2},{1,3},{2,0},{3,1},{4,6},{5,7},{6,4},{7,5},{8,10},{9,11},{10,... | collective-permute-start | bytes 786440 | tf_op jit(solution)/shard_map/ppermute | solution.py:66
  8.2 10.2 %collective-permute-start.4 = (s32[2,2,512]{2,1,0:T(2,128)S(1)}, s32[2,2,512]{2,1,0:T(2,128)S(1)}, u32[]{:S(2)}, u32[]{:S(2)}) collective-permute-start(s32[2,2,512]{2,1,0:T(2,128)S(1)} %get-tuple-element.100), channel_id=1, source_target_pairs={{0,16},{8,24},{16,0},{24,8},{1,17},{9,25},{17,1},{25,9},{2,18},{10... | collective-permute-start | bytes 24584 | tf_op jit(solution)/shard_map/ppermute | solution.py:62
  9.8 8.6 %collective-permute-start.3 = (s32[2,2,512]{2,1,0:T(2,128)S(1)}, s32[2,2,512]{2,1,0:T(2,128)S(1)}, u32[]{:S(2)}, u32[]{:S(2)}) collective-permute-start(s32[2,2,512]{2,1,0:T(2,128)S(1)} %get-tuple-element.100), channel_id=1, source_target_pairs={{0,8},{8,0},{16,24},{24,16},{1,9},{9,1},{17,25},{25,17},{2,10},{10... | collective-permute-start | bytes 24584 | tf_op jit(solution)/shard_map/ppermute | solution.py:62
  11.3 7.1 %collective-permute-start.5 = (s32[2,2,512]{2,1,0:T(2,128)S(1)}, s32[2,2,512]{2,1,0:T(2,128)S(1)}, u32[]{:S(2)}, u32[]{:S(2)}) collective-permute-start(s32[2,2,512]{2,1,0:T(2,128)S(1)} %get-tuple-element.100), channel_id=1, source_target_pairs={{0,24},{8,16},{16,8},{24,0},{1,25},{9,17},{17,9},{25,1},{2,26},{10... | collective-permute-start | bytes 24584 | tf_op jit(solution)/shard_map/ppermute | solution.py:62
  17.8 9.0 %collective-permute-start.1 = (bf16[1024,128]{1,0:T(8,128)(2,1)S(1)}, bf16[1024,128]{1,0:T(8,128)(2,1)S(1)}, u32[]{:S(2)}, u32[]{:S(2)}) collective-permute-start(bf16[1024,128]{1,0:T(8,128)(2,1)S(1)} %collective-permute-done.chunk_ref), channel_id=1, source_target_pairs={{0,2},{1,3},{2,0},{3,1},{4,6},{5,7},{6,4},{7,5},{8,10},{9,11},{10,... | collective-permute-start | bytes 786440 | tf_op jit(solution)/shard_map/ppermute | solution.py:66
  28.0 2.0 %collective-permute-start.7 = (bf16[4,512,128]{2,1,0:T(8,128)(2,1)S(1)}, bf16[4,512,128]{2,1,0:T(8,128)(2,1)S(1)}, u32[]{:S(2)}, u32[]{:S(2)}) collective-permute-start(bf16[4,512,128]{2,1,0:T(8,128)(2,1)S(1)} %fetch.9), channel_id=1, source_target_pairs={{0,1},{1,0},{2,3},{3,2},{4,5},{5,4},{6,7},{7,6},{8,9},{9,8},{10,11... | collective-permute-start | bytes 1572872 | tf_op jit(solution)/shard_map/ppermute | solution.py:69
  28.1 11.7 %copy-start = (bf16[512,512]{1,0:T(8,128)(2,1)S(1)}, bf16[512,512]{1,0:T(8,128)(2,1)}, u32[]{:S(2)}) copy-start(bf16[512,512]{1,0:T(8,128)(2,1)} %c_ref.1) | copy-start | bytes 1572868
  28.1 11.7 %copy-start.1 = (bf16[512,2048]{1,0:T(8,128)(2,1)S(1)}, bf16[512,2048]{1,0:T(8,128)(2,1)}, u32[]{:S(2)}) copy-start(bf16[512,2048]{1,0:T(8,128)(2,1)} %wp_ref.1) | copy-start | bytes 6291460
  28.1 11.7 %copy-start.2 = (bf16[512,512]{1,0:T(8,128)(2,1)S(1)}, bf16[512,512]{1,0:T(8,128)(2,1)}, u32[]{:S(2)}) copy-start(bf16[512,512]{1,0:T(8,128)(2,1)} %wo_ref.1) | copy-start | bytes 1572868
  28.1 11.7 %copy-start.3 = (f32[512]{0:T(512)S(1)}, f32[512]{0:T(512)}, u32[]{:S(2)}) copy-start(f32[512]{0:T(512)} %param.16) | copy-start | bytes 6148
  30.1 5.9 %collective-permute-start.8 = (bf16[512,128]{1,0:T(8,128)(2,1)S(1)}, bf16[512,128]{1,0:T(8,128)(2,1)S(1)}, u32[]{:S(2)}, u32[]{:S(2)}) collective-permute-start(bf16[512,128]{1,0:T(8,128)(2,1)S(1)} %get-tuple-element.59), channel_id=1, source_target_pairs={{0,8},{8,0},{16,24},{24,16},{1,9},{9,1},{17,25},{25,17},{2,10},{10... | collective-permute-start | bytes 393224 | tf_op jit(solution)/shard_map/ppermute | solution.py:62
  31.7 8.1 %collective-permute-start.9 = (bf16[512,128]{1,0:T(8,128)(2,1)S(1)}, bf16[512,128]{1,0:T(8,128)(2,1)S(1)}, u32[]{:S(2)}, u32[]{:S(2)}) collective-permute-start(bf16[512,128]{1,0:T(8,128)(2,1)S(1)} %get-tuple-element.60), channel_id=1, source_target_pairs={{0,16},{8,24},{16,0},{24,8},{1,17},{9,25},{17,1},{25,9},{2,18},{10... | collective-permute-start | bytes 393224 | tf_op jit(solution)/shard_map/ppermute | solution.py:62
  33.2 6.6 %collective-permute-start.10 = (bf16[512,128]{1,0:T(8,128)(2,1)S(1)}, bf16[512,128]{1,0:T(8,128)(2,1)S(1)}, u32[]{:S(2)}, u32[]{:S(2)}) collective-permute-start(bf16[512,128]{1,0:T(8,128)(2,1)S(1)} %get-tuple-element.61), channel_id=1, source_target_pairs={{0,24},{8,16},{16,8},{24,0},{1,25},{9,17},{17,9},{25,1},{2,26},{10... | collective-permute-start | bytes 393224 | tf_op jit(solution)/shard_map/ppermute | solution.py:62
  53.0 3.5 %collective-permute-start.14 = (bf16[4,256,640]{2,1,0:T(8,128)(2,1)S(1)}, bf16[4,256,640]{2,1,0:T(8,128)(2,1)S(1)}, u32[]{:S(2)}, u32[]{:S(2)}) collective-permute-start(bf16[4,256,640]{2,1,0:T(8,128)(2,1)S(1)} %get-tuple-element.70), channel_id=1, source_target_pairs={{0,1},{1,0},{2,3},{3,2},{4,5},{5,4},{6,7},{7,6},{8,9},{9,8},{10,11... | collective-permute-start | bytes 3932168 | tf_op jit(solution)/shard_map/ppermute | solution.py:69
  53.0 6.3 %collective-permute-start.11 = (bf16[512,128]{1,0:T(8,128)(2,1)S(1)}, bf16[512,128]{1,0:T(8,128)(2,1)S(1)}, u32[]{:S(2)}, u32[]{:S(2)}) collective-permute-start(bf16[512,128]{1,0:T(8,128)(2,1)S(1)} %get-tuple-element.64), channel_id=1, source_target_pairs={{0,8},{8,0},{16,24},{24,16},{1,9},{9,1},{17,25},{25,17},{2,10},{10... | collective-permute-start | bytes 393224 | tf_op jit(solution)/shard_map/ppermute | solution.py:62
  54.2 6.8 %collective-permute-start.12 = (bf16[512,128]{1,0:T(8,128)(2,1)S(1)}, bf16[512,128]{1,0:T(8,128)(2,1)S(1)}, u32[]{:S(2)}, u32[]{:S(2)}) collective-permute-start(bf16[512,128]{1,0:T(8,128)(2,1)S(1)} %get-tuple-element.65), channel_id=1, source_target_pairs={{0,16},{8,24},{16,0},{24,8},{1,17},{9,25},{17,1},{25,9},{2,18},{10... | collective-permute-start | bytes 393224 | tf_op jit(solution)/shard_map/ppermute | solution.py:62
  55.0 7.6 %collective-permute-start.13 = (bf16[512,128]{1,0:T(8,128)(2,1)S(1)}, bf16[512,128]{1,0:T(8,128)(2,1)S(1)}, u32[]{:S(2)}, u32[]{:S(2)}) collective-permute-start(bf16[512,128]{1,0:T(8,128)(2,1)S(1)} %get-tuple-element.66), channel_id=1, source_target_pairs={{0,24},{8,16},{16,8},{24,0},{1,25},{9,17},{17,9},{25,1},{2,26},{10... | collective-permute-start | bytes 393224 | tf_op jit(solution)/shard_map/ppermute | solution.py:62
  62.7 3.7 %collective-permute-start.15 = (bf16[4,512,128]{2,1,0:T(8,128)(2,1)S(1)}, bf16[4,512,128]{2,1,0:T(8,128)(2,1)S(1)}, u32[]{:S(2)}, u32[]{:S(2)}) collective-permute-start(bf16[4,512,128]{2,1,0:T(8,128)(2,1)S(1)} %pack.1.refs_0_), channel_id=1, source_target_pairs={{0,1},{1,0},{2,3},{3,2},{4,5},{5,4},{6,7},{7,6},{8,9},{9,8},{10,11... | collective-permute-start | bytes 1572872 | tf_op jit(solution)/shard_map/ppermute | solution.py:69
  62.8 10.1 %collective-permute-start.19 = (bf16[2,128,640]{2,1,0:T(8,128)(2,1)S(1)}, bf16[2,128,640]{2,1,0:T(8,128)(2,1)S(1)}, u32[]{:S(2)}, u32[]{:S(2)}) collective-permute-start(bf16[2,128,640]{2,1,0:T(8,128)(2,1)S(1)} %get-tuple-element.72), channel_id=1, source_target_pairs={{0,8},{8,0},{16,24},{24,16},{1,9},{9,1},{17,25},{25,17},{2,10},{10... | collective-permute-start | bytes 983048 | tf_op jit(solution)/shard_map/ppermute | solution.py:62
  63.6 9.8 %collective-permute-start.20 = (bf16[2,128,640]{2,1,0:T(8,128)(2,1)S(1)}, bf16[2,128,640]{2,1,0:T(8,128)(2,1)S(1)}, u32[]{:S(2)}, u32[]{:S(2)}) collective-permute-start(bf16[2,128,640]{2,1,0:T(8,128)(2,1)S(1)} %get-tuple-element.74), channel_id=1, source_target_pairs={{0,16},{8,24},{16,0},{24,8},{1,17},{9,25},{17,1},{25,9},{2,18},{10... | collective-permute-start | bytes 983048 | tf_op jit(solution)/shard_map/ppermute | solution.py:62
  67.6 8.2 %collective-permute-start.16 = (bf16[1024,128]{1,0:T(8,128)(2,1)S(1)}, bf16[1024,128]{1,0:T(8,128)(2,1)S(1)}, u32[]{:S(2)}, u32[]{:S(2)}) collective-permute-start(bf16[1024,128]{1,0:T(8,128)(2,1)S(1)} %gather_grad.7), channel_id=1, source_target_pairs={{0,2},{1,3},{2,0},{3,1},{4,6},{5,7},{6,4},{7,5},{8,10},{9,11},{10,... | collective-permute-start | bytes 786440 | tf_op jit(solution)/shard_map/ppermute | solution.py:66
  73.7 5.7 %collective-permute-start.21 = (bf16[1,128,640]{2,1,0:T(8,128)(2,1)S(1)}, bf16[1,128,640]{2,1,0:T(8,128)(2,1)S(1)}, u32[]{:S(2)}, u32[]{:S(2)}) collective-permute-start(bf16[1,128,640]{2,1,0:T(8,128)(2,1)S(1)} %get-tuple-element.87), channel_id=1, source_target_pairs={{0,16},{8,24},{16,0},{24,8},{1,17},{9,25},{17,1},{25,9},{2,18},{10... | collective-permute-start | bytes 491528 | tf_op jit(solution)/shard_map/ppermute | solution.py:62
  75.2 5.3 %collective-permute-start.22 = (bf16[1,128,640]{2,1,0:T(8,128)(2,1)S(1)}, bf16[1,128,640]{2,1,0:T(8,128)(2,1)S(1)}, u32[]{:S(2)}, u32[]{:S(2)}) collective-permute-start(bf16[1,128,640]{2,1,0:T(8,128)(2,1)S(1)} %get-tuple-element.88), channel_id=1, source_target_pairs={{0,8},{8,0},{16,24},{24,16},{1,9},{9,1},{17,25},{25,17},{2,10},{10... | collective-permute-start | bytes 491528 | tf_op jit(solution)/shard_map/ppermute | solution.py:62
  75.9 17.9 %collective-permute-start.17 = (bf16[1024,128]{1,0:T(8,128)(2,1)S(1)}, bf16[1024,128]{1,0:T(8,128)(2,1)S(1)}, u32[]{:S(2)}, u32[]{:S(2)}) collective-permute-start(bf16[1024,128]{1,0:T(8,128)(2,1)S(1)} %add_up.2), channel_id=1, source_target_pairs={{0,4},{1,5},{2,6},{3,7},{4,0},{5,1},{6,2},{7,3},{8,12},{9,13},{10,... | collective-permute-start | bytes 786440 | tf_op jit(solution)/shard_map/ppermute | solution.py:66
  80.7 13.0 %collective-permute-start.23 = (bf16[2,64,640]{2,1,0:T(8,128)(2,1)S(1)}, bf16[2,64,640]{2,1,0:T(8,128)(2,1)S(1)}, u32[]{:S(2)}, u32[]{:S(2)}) collective-permute-start(bf16[2,64,640]{2,1,0:T(8,128)(2,1)S(1)} %get-tuple-element.92), channel_id=1, source_target_pairs={{0,2},{1,3},{2,0},{3,1},{4,6},{5,7},{6,4},{7,5},{8,10},{9,11},{10,... | collective-permute-start | bytes 491528 | tf_op jit(solution)/shard_map/ppermute | solution.py:66
  84.5 13.5 %collective-permute-start.18 = (bf16[1024,128]{1,0:T(8,128)(2,1)S(1)}, bf16[1024,128]{1,0:T(8,128)(2,1)S(1)}, u32[]{:S(2)}, u32[]{:S(2)}) collective-permute-start(bf16[1024,128]{1,0:T(8,128)(2,1)S(1)} %gather_grad.9), channel_id=1, source_target_pairs={{0,2},{1,3},{2,0},{3,1},{4,6},{5,7},{6,4},{7,5},{8,10},{9,11},{10,... | collective-permute-start | bytes 786440 | tf_op jit(solution)/shard_map/ppermute | solution.py:66
  93.7 5.4 %collective-permute-start.24 = (bf16[1,64,640]{2,1,0:T(8,128)(2,1)S(1)}, bf16[1,64,640]{2,1,0:T(8,128)(2,1)S(1)}, u32[]{:S(2)}, u32[]{:S(2)}) collective-permute-start(bf16[1,64,640]{2,1,0:T(8,128)(2,1)S(1)} %get-tuple-element.94), channel_id=1, source_target_pairs={{0,4},{1,5},{2,6},{3,7},{4,0},{5,1},{6,2},{7,3},{8,12},{9,13},{10,... | collective-permute-start | bytes 245768 | tf_op jit(solution)/shard_map/ppermute | solution.py:66
  99.1 5.5 %collective-permute-start.27 = (bf16[64,640]{1,0:T(8,128)(2,1)S(1)}, bf16[64,640]{1,0:T(8,128)(2,1)S(1)}, u32[]{:S(2)}, u32[]{:S(2)}) collective-permute-start(bf16[64,640]{1,0:T(8,128)(2,1)S(1)} %add_up.3.refs_0_), channel_id=1, source_target_pairs={{0,24},{8,16},{16,8},{24,0},{1,25},{9,17},{17,9},{25,1},{2,26},{10... | collective-permute-start | bytes 245768 | tf_op jit(solution)/shard_map/ppermute | solution.py:62
  100.4 5.0 %collective-permute-start.26 = (bf16[64,640]{1,0:T(8,128)(2,1)S(1)}, bf16[64,640]{1,0:T(8,128)(2,1)S(1)}, u32[]{:S(2)}, u32[]{:S(2)}) collective-permute-start(bf16[64,640]{1,0:T(8,128)(2,1)S(1)} %add_up.3.refs_0_), channel_id=1, source_target_pairs={{0,16},{8,24},{16,0},{24,8},{1,17},{9,25},{17,1},{25,9},{2,18},{10... | collective-permute-start | bytes 245768 | tf_op jit(solution)/shard_map/ppermute | solution.py:62
  101.1 4.4 %collective-permute-start.25 = (bf16[64,640]{1,0:T(8,128)(2,1)S(1)}, bf16[64,640]{1,0:T(8,128)(2,1)S(1)}, u32[]{:S(2)}, u32[]{:S(2)}) collective-permute-start(bf16[64,640]{1,0:T(8,128)(2,1)S(1)} %add_up.3.refs_0_), channel_id=1, source_target_pairs={{0,8},{8,0},{16,24},{24,16},{1,9},{9,1},{17,25},{25,17},{2,10},{10... | collective-permute-start | bytes 245768 | tf_op jit(solution)/shard_map/ppermute | solution.py:62

commit v9 on v8

--- a/solution.py
+++ b/solution.py
@@ -60,6 +60,9 @@
     def over_replica(self, value, step):
         n = self.replicas
         return lax.ppermute(value, "replica", [(i, i ^ step) for i in range(n)])
+
+    def swap_replica(self, value):
+        return lax.all_to_all(value, "replica", split_axis=0, concat_axis=0, tiled=True)
 
     def over_line(self, value, step):
         pairs = [(i, i ^ step * self.cores) for i in range(self.shards)]
@@ -338,77 +341,36 @@
         yield parts[0] if len(parts) == 1 else jnp.concatenate(parts, axis=1)
 
 
-def weight_grad(replica, core, normed, dproj, gated, cotangent, before, line):
+def weight_grad(core, normed, dproj, gated, cotangent, before, line):
     blocks, half, cols = before.shape
     length, width = normed.shape
     cores = width // half
-    bits = blocks.bit_length() - 1
-    tall = half // bits
-
-    def body(r_ref, core_ref, n_ref, d_ref, g_ref, c_ref, before_ref, *refs):
-        out_refs, scratch = refs[:-1], refs[-1]
+
+    def body(core_ref, n_ref, d_ref, g_ref, c_ref, before_ref, out_ref):
         sums = weight_sums(core_ref[0], n_ref, d_ref, g_ref, c_ref, cores, line, blocks)
         for k in range(blocks):
-            total = next(sums) + before_ref[k].astype(F32)
-            for p in range(bits):
-                at = sum((k >> (p + i) % bits & 1) << bits - 1 - i for i in range(bits))
-                scratch[p, at] = total[p * tall : (p + 1) * tall]
-        for p in range(bits):
-            split_halves(scratch.at[p], r_ref[0] >> p & 1, out_refs[2 * p : 2 * p + 2])
-
-    kept = (blocks // 2, tall, cols)
+            out_ref[k] = (next(sums) + before_ref[k].astype(F32)).astype(BF16)
+
     return run(
         "weight_grad",
         body,
-        [(kept, F32), (kept, BF16)] * bits,
-        [replica, core, normed, dproj, gated, cotangent, before],
-        smem=2,
-        scratch=[pltpu.VMEM((bits, blocks, tall, cols), F32)],
+        [(before.shape, BF16)],
+        [core, normed, dproj, gated, cotangent, before],
+        smem=1,
         flops=2 * length * half * (blocks * cols + 2 * width),
-    )
-
-
-def split_halves(ref, bit, out_refs):
-    count = ref.shape[0] // 2
-    for i, out_ref in enumerate(out_refs):
-        start = (bit ^ i) * count
-        for k in range(count):
-            out_ref[k] = ref[start + k].astype(out_ref.dtype)
-
-
-def fold(replica, kept, came, step):
-    count, tall, cols = kept[0].shape
-    many = len(kept)
-
-    def body(r_ref, *refs):
-        kept_refs, came_refs, out_refs = refs[:many], refs[many : 2 * many], refs[2 * many : -1]
-        scratch = refs[-1]
-        for p in range(many):
-            for k in range(count):
-                scratch[p, k] = kept_refs[p][k] + came_refs[p][k].astype(F32)
-            split_halves(scratch.at[p], r_ref[0] >> (p + step) % many & 1, out_refs[2 * p : 2 * p + 2])
-
-    half = (count // 2, tall, cols)
-    return run(
-        "fold",
-        body,
-        [(half, F32), (half, BF16)] * many,
-        [replica, *kept, *came],
-        smem=1,
-        scratch=[pltpu.VMEM((many, count, tall, cols), F32)],
-    )
-
-
-def cut_line(place, kept, came, line):
-    _, tall, cols = kept[0].shape
-    many = len(kept)
-    rows = many * tall // line
-
-    def body(place_ref, *refs):
-        kept_refs, came_refs, out_refs = refs[:many], refs[many : 2 * many], refs[2 * many : -1]
-        scratch = refs[-1]
-        for p in range(many):
-            scratch[p * tall : (p + 1) * tall] = kept_refs[p][0] + came_refs[p][0].astype(F32)
+    )[0]
+
+
+def cut_line(place, parts, line):
+    count, tall, cols = parts.shape
+    rows = tall // line
+
+    def body(place_ref, part_ref, *refs):
+        out_refs, scratch = refs[:2], refs[2]
+        total = part_ref[0].astype(F32)
+        for k in range(1, count):
+            total = total + part_ref[k].astype(F32)
+        scratch[...] = total
         for k in range(line):
             span = pl.ds(pl.multiple_of((place_ref[0] ^ k) * rows, rows), rows)
             out_refs[k % 2][k // 2] = scratch[span].astype(out_refs[k % 2].dtype)
@@ -418,9 +380,9 @@
         "cut_line",
         body,
         [(half, F32), (half, BF16)],
-        [place, *kept, *came],
+        [place, parts],
         smem=1,
-        scratch=[pltpu.VMEM((many * tall, cols), F32)],
+        scratch=[pltpu.VMEM((tall, cols), F32)],
     )
 
 
@@ -479,7 +441,6 @@
     replicas, line, cores = grid.replicas, grid.line, grid.cores
     cols = width // replicas
 
-    bits = replicas.bit_length() - 1
     swaps = [3, 1, 2] if replicas == 4 else list(range(1, replicas))
     replica, place, core = (i.astype(I32).reshape(1) for i in (grid.r, grid.z, grid.c))
     bases = [((place ^ k) * cores + core) * rows for k in range(line)]
@@ -529,16 +490,12 @@
         tokens[k] = grid.over_replica(tokens[k], k)
 
     weights = grid.over_pair(weights)
-    weights = weight_grad(replica, core, normed, dproj, gated, cotangent, weights, line)
+    weights = weight_grad(core, normed, dproj, gated, cotangent, weights, line)
     tokens = lax.optimization_barrier((tokens, weights))[0]
     tokens = pack(tokens)
     there = grid.over_pair(tokens)
 
-    def swap_weights(weights, step):
-        kept, sent = weights[0::2], weights[1::2]
-        return kept, [grid.over_replica(sent[p], 1 << (p + step) % bits) for p in range(bits)]
-
-    kept, swapped = swap_weights(weights, 0)
+    weights = grid.swap_replica(weights)
 
     sums, raw, both_there = {}, {}, [tokens, there]
     for k in reversed(order):
@@ -561,12 +518,8 @@
         else:
             sums[k] = add_up(raw[k] + came) if steps else raw[k][0]
 
-    for step in range(1, bits + 1):
-        after = raw[line // 2] if step < bits else sums[line // 2]
-        swapped = lax.optimization_barrier((swapped, after))[0]
-        if step < bits:
-            kept, swapped = swap_weights(fold(replica, kept, swapped, step), step)
-    kept, sent = cut_line(place, kept, swapped, line)
+    weights = lax.optimization_barrier((weights, sums[line // 2]))[0]
+    kept, sent = cut_line(place, weights, line)
     step = 1
     while step < line // 2:
         kept, sent = fold_line(kept, grid.over_line(sent, step))

time: 107 us -> 115 us (1.075)
  waiting for transfers between devices: 33.6 us -> 42.1 us
    ppermute x8, waiting for transfers between devices: 16.7 us -> 27.3 us  [over_line(): return lax.ppermute(value, 'sparse', pairs)]
    ppermute x16 -> x12, starting transfers between devices: 18.6 us -> 14.1 us  [over_replica(): return lax.ppermute(value, 'replica', [(i, i ^ step) for i in range(n)])]
    all_to_all x0 -> x1, starting transfers between devices: none -> 3.77 us  [swap_replica(): lax.all_to_all(value, 'replica', split_axis=0, concat_axis=0, tiled=True)]
    ppermute x16 -> x12, waiting for transfers between devices: 16.3 us -> 14.2 us  [over_replica(): return lax.ppermute(value, 'replica', [(i, i ^ step) for i in range(n)])]
    pallas_call x22 -> x21, Pallas kernels: 36.4 us -> 37 us  [run(): pl.pallas_call(body, out_shape=outs, in_specs=places, out_specs=[in_vmem]...]
  transfers between devices with their start and end apart: 28 -> 25, of which waited for: 16 -> 12; matrix products, arithmetic and copies ran while one was open for 2% -> 2% of each run, Pallas kernels for 20% -> 19%
where the time goes in v9:
time: 115 us
  waiting for transfers between devices  42.1 us (37%)
  Pallas kernels  37 us (32%)
  starting transfers between devices  31.8 us (28%)
  local copies, waits for them, and re-layouts  2.25 us (2%)
    pallas_call x21, Pallas kernels, run(): pl.pallas_call(body, out_shape=outs, in_specs=places, out_specs=[in_vmem]...  37 us
    ppermute x8, waiting for transfers between devices, over_line(): return lax.ppermute(value, 'sparse', pairs)  27.3 us
    ppermute x12, waiting for transfers between devices, over_replica(): return lax.ppermute(value, 'replica', [(i, i ^ step) for i in range(n)])  14.2 us
    ppermute x12, starting transfers between devices, over_replica(): return lax.ppermute(value, 'replica', [(i, i ^ step) for i in range(n)])  14.1 us
    ppermute x8, starting transfers between devices, over_line(): return lax.ppermute(value, 'sparse', pairs)  13.6 us
    all_to_all x1, starting transfers between devices, swap_replica(): lax.all_to_all(value, 'replica', split_axis=0, concat_axis=0, tiled=True)  3.77 us
  transfers between devices with their start and end apart: 25, of which 12 were waited for; matrix products, arithmetic and copies ran while one was open for 2% of the time, Pallas kernels for 19%

profile of v9, /device:TPU:0, one launch (start us, length us, event | category | flops | bytes accessed | tf_op | source)
XLA Modules:
  0.0 114.8 jit_solution(7396121295902364296)
XLA Ops:
  0.6 1.0 constant_dynamic-slice_fusion
  1.7 4.1 %collective-permute-start = (bf16[1024,128]{1,0:T(8,128)(2,1)S(1)}, bf16[1024,128]{1,0:T(8,128)(2,1)S(1)}, u32[]{:S(2)}, u32[]{:S(2)}) collective-permute-start(bf16[1024,128]{1,0:T(8,128)(2,1)S(1)} %pad_maximum_fusion.chunk_ref), channel_id=1, source_target_pairs={{0,4},{1,5},{2,6},{3,7},{4,0},{5,1},{6,2},{7,3},{8,12},{9,13},{10,... | collective-permute-start | bytes 786440 | tf_op jit(solution)/shard_map/ppermute | solution.py:69
  5.8 0.7 add_bitcast_fusion
  6.5 0.1 collective-permute-start.2
  6.6 1.6 %collective-permute-start.6 = (bf16[1024,128]{1,0:T(8,128)(2,1)S(1)}, bf16[1024,128]{1,0:T(8,128)(2,1)S(1)}, u32[]{:S(2)}, u32[]{:S(2)}) collective-permute-start(bf16[1024,128]{1,0:T(8,128)(2,1)S(1)} %pad_maximum_fusion.chunk_ref), channel_id=1, source_target_pairs={{0,2},{1,3},{2,0},{3,1},{4,6},{5,7},{6,4},{7,5},{8,10},{9,11},{10,... | collective-permute-start | bytes 786440 | tf_op jit(solution)/shard_map/ppermute | solution.py:69
  8.2 0.0 collective-permute-done.2
  8.2 1.6 %collective-permute-start.3 = (s32[2,2,512]{2,1,0:T(2,128)S(1)}, s32[2,2,512]{2,1,0:T(2,128)S(1)}, u32[]{:S(2)}, u32[]{:S(2)}) collective-permute-start(s32[2,2,512]{2,1,0:T(2,128)S(1)} %get-tuple-element.78), channel_id=1, source_target_pairs={{0,8},{8,0},{16,24},{24,16},{1,9},{9,1},{17,25},{25,17},{2,10},{10... | collective-permute-start | bytes 24584 | tf_op jit(solution)/shard_map/ppermute | solution.py:62
  9.8 1.5 %collective-permute-start.4 = (s32[2,2,512]{2,1,0:T(2,128)S(1)}, s32[2,2,512]{2,1,0:T(2,128)S(1)}, u32[]{:S(2)}, u32[]{:S(2)}) collective-permute-start(s32[2,2,512]{2,1,0:T(2,128)S(1)} %get-tuple-element.78), channel_id=1, source_target_pairs={{0,16},{8,24},{16,0},{24,8},{1,17},{9,25},{17,1},{25,9},{2,18},{10... | collective-permute-start | bytes 24584 | tf_op jit(solution)/shard_map/ppermute | solution.py:62
  11.3 0.5 collective-permute-start.5
  11.8 6.0 %collective-permute-done.chunk_ref = bf16[1024,128]{1,0:T(8,128)(2,1)S(1)} collective-permute-done((bf16[1024,128]{1,0:T(8,128)(2,1)S(1)}, bf16[1024,128]{1,0:T(8,128)(2,1)S(1)}, u32[]{:S(2)}, u32[]{:S(2)}) %collective-permute-start) | collective-permute-done | bytes 262176 | tf_op jit(solution)/shard_map/ppermute | solution.py:69
  17.8 0.7 collective-permute-start.1
  18.5 0.0 collective-permute-done.3
  18.5 0.0 collective-permute-done.4
  18.5 1.2 %broadcast_in_dim.14.key_ref = s32[4,2,2,512,128]{4,3,2,1,0:T(8,128)S(1)} broadcast(s32[4,2,2,512]{3,2,1,0:T(2,128)S(1)} %pad_add_fusion.key_ref), dimensions={0,1,2,3} | broadcast | bytes 4227072 | tf_op jit(solution)/shard_map/broadcast_in_dim | solution.py:471
  19.7 2.3 %fetch.5 = (bf16[4,512,128]{2,1,0:T(8,128)(2,1)S(1)}, bf16[4,512,128]{2,1,0:T(8,128)(2,1)S(1)}) custom-call(s32[1]{0:T(128)S(6)} %mul.44.base_ref, bf16[1024,128]{1,0:T(8,128)(2,1)S(1)} %pad_maximum_fusion.chunk_ref, s32[4,2,2,512,128]{4,3,2,1,0:T(8,128)S(1)} %broadcast_in_dim.14.key_ref), custom_call_target="tpu_custom_call" | custom-call | flops 536870912 | bytes 5505028 | tf_op jit(solution)/shard_map/fetch/pallas_call | solution.py:36
  22.1 2.3 %fetch.6 = (bf16[4,512,128]{2,1,0:T(8,128)(2,1)S(1)}, bf16[4,512,128]{2,1,0:T(8,128)(2,1)S(1)}) custom-call(s32[1]{0:T(128)S(6)} %mul.42.base_ref, bf16[1024,128]{1,0:T(8,128)(2,1)S(1)} %collective-permute-done.6.chunk_ref, s32[4,2,2,512,128]{4,3,2,1,0:T(8,128)S(1)} %broadcast_in_dim.14.key_ref, bf16[4,512,128]{2,1,0:T(8,128)(2,1)S(1)} %get-tuple-element.41.refs_0_, ...), custom_call_target="tpu_custom_call" | custom-call | flops 536870912 | bytes 6553604 | tf_op jit(solution)/shard_map/fetch/pallas_call | solution.py:36
  24.4 2.3 %fetch.7 = (bf16[4,512,128]{2,1,0:T(8,128)(2,1)S(1)}, bf16[4,512,128]{2,1,0:T(8,128)(2,1)S(1)}) custom-call(s32[1]{0:T(128)S(6)} %mul.40.base_ref, bf16[1024,128]{1,0:T(8,128)(2,1)S(1)} %collective-permute-done.chunk_ref, s32[4,2,2,512,128]{4,3,2,1,0:T(8,128)S(1)} %broadcast_in_dim.14.key_ref, bf16[4,512,128]{2,1,0:T(8,128)(2,1)S(1)} %get-tuple-element.43.refs_0_, ...), custom_call_target="tpu_custom_call" | custom-call | flops 536870912 | bytes 6553604 | tf_op jit(solution)/shard_map/fetch/pallas_call | solution.py:36
  26.8 1.3 %fetch.9 = bf16[4,512,128]{2,1,0:T(8,128)(2,1)S(1)} custom-call(s32[1]{0:T(128)S(6)} %mul.35.base_ref, bf16[1024,128]{1,0:T(8,128)(2,1)S(1)} %collective-permute-done.1.chunk_ref, s32[4,2,2,512,128]{4,3,2,1,0:T(8,128)S(1)} %broadcast_in_dim.14.key_ref, bf16[4,512,128]{2,1,0:T(8,128)(2,1)S(1)} %get-tuple-element.46.refs_0_), custom_call_target="tpu_custom_call" | custom-call | flops 268435456 | bytes 5505028 | tf_op jit(solution)/shard_map/fetch/pallas_call | solution.py:36
  28.0 0.1 collective-permute-start.7
  28.1 0.0 copy-start
  28.1 0.0 copy-start.1
  28.1 0.0 copy-start.2
  28.1 0.0 copy-start.3
  28.2 1.2 %fetch.8.left_ref = bf16[4,512,128]{2,1,0:T(8,128)(2,1)S(1)} custom-call(s32[1]{0:T(128)S(6)} %mul.35.base_ref, bf16[1024,128]{1,0:T(8,128)(2,1)S(1)} %collective-permute-done.1.chunk_ref, s32[4,2,2,512,128]{4,3,2,1,0:T(8,128)S(1)} %broadcast_in_dim.14.key_ref, bf16[4,512,128]{2,1,0:T(8,128)(2,1)S(1)} %get-tuple-element.45.refs_0_), custom_call_target="tpu_custom_call" | custom-call | flops 268435456 | bytes 5505028 | tf_op jit(solution)/shard_map/fetch/pallas_call | solution.py:36
  29.4 0.6 collective-permute-done.7.right_ref
  30.0 0.1 combine.1
  30.1 2.5 %collective-permute-start.10 = (bf16[512,128]{1,0:T(8,128)(2,1)S(1)}, bf16[512,128]{1,0:T(8,128)(2,1)S(1)}, u32[]{:S(2)}, u32[]{:S(2)}) collective-permute-start(bf16[512,128]{1,0:T(8,128)(2,1)S(1)} %get-tuple-element.50), channel_id=1, source_target_pairs={{0,24},{8,16},{16,8},{24,0},{1,25},{9,17},{17,9},{25,1},{2,26},{10... | collective-permute-start | bytes 393224 | tf_op jit(solution)/shard_map/ppermute | solution.py:62
  32.7 0.5 collective-permute-start.8
  33.2 0.5 collective-permute-start.9
  33.7 3.7 %collective-permute-done.10.refs_3_ = bf16[512,128]{1,0:T(8,128)(2,1)S(1)} collective-permute-done((bf16[512,128]{1,0:T(8,128)(2,1)S(1)}, bf16[512,128]{1,0:T(8,128)(2,1)S(1)}, u32[]{:S(2)}, u32[]{:S(2)}) %collective-permute-start.10) | collective-permute-done | bytes 131104 | tf_op jit(solution)/shard_map/ppermute | solution.py:62
  37.4 2.1 %collective-permute-done.8.refs_1_ = bf16[512,128]{1,0:T(8,128)(2,1)S(1)} collective-permute-done((bf16[512,128]{1,0:T(8,128)(2,1)S(1)}, bf16[512,128]{1,0:T(8,128)(2,1)S(1)}, u32[]{:S(2)}, u32[]{:S(2)}) %collective-permute-start.8) | collective-permute-done | bytes 131104 | tf_op jit(solution)/shard_map/ppermute | solution.py:62
  39.6 13.1 %sequence.1 = (bf16[512,512]{1,0:T(8,128)(2,1)}, bf16[512,128]{1,0:T(8,128)(2,1)S(1)}, bf16[512,128]{1,0:T(8,128)(2,1)S(1)}, bf16[512,128]{1,0:T(8,128)(2,1)S(1)...) custom-call(s32[1]{0:T(128)} %bitcast.r_ref, ...), custom_call_target="tpu_custom_call" | custom-call | flops 4294967296 | bytes 9177096 | tf_op jit(solution)/shard_map/sequence/pallas_call | solution.py:36
  52.7 1.5 %collective-permute-start.11 = (bf16[512,128]{1,0:T(8,128)(2,1)S(1)}, bf16[512,128]{1,0:T(8,128)(2,1)S(1)}, u32[]{:S(2)}, u32[]{:S(2)}) collective-permute-start(bf16[512,128]{1,0:T(8,128)(2,1)S(1)} %get-tuple-element.53), channel_id=1, source_target_pairs={{0,8},{8,0},{16,24},{24,16},{1,9},{9,1},{17,25},{25,17},{2,10},{10... | collective-permute-start | bytes 393224 | tf_op jit(solution)/shard_map/ppermute | solution.py:62
  54.2 1.5 %collective-permute-start.12 = (bf16[512,128]{1,0:T(8,128)(2,1)S(1)}, bf16[512,128]{1,0:T(8,128)(2,1)S(1)}, u32[]{:S(2)}, u32[]{:S(2)}) collective-permute-start(bf16[512,128]{1,0:T(8,128)(2,1)S(1)} %get-tuple-element.54), channel_id=1, source_target_pairs={{0,16},{8,24},{16,0},{24,8},{1,17},{9,25},{17,1},{25,9},{2,18},{10... | collective-permute-start | bytes 393224 | tf_op jit(solution)/shard_map/ppermute | solution.py:62
  55.7 0.5 collective-permute-start.13
  56.2 2.6 %weight_grad.1 = bf16[4,256,640]{2,1,0:T(8,128)(2,1)} custom-call(s32[1]{0:T(128)} %bitcast.1.core_ref, bf16[512,512]{1,0:T(8,128)(2,1)S(1)} %get-tuple-element.56.n_ref, bf16[512,2048]{1,0:T(8,128)(2,1)S(1)} %get-tuple-element.57.d_ref, bf16[512,512]{1,0:T(8,128)(2,1)S(1)} %get-tuple-element.58.g_ref, bf16[512,512]{1,0:T(8,128)(2,1)S(1)} %copy-done, ...), custom_call_target="tpu_custom_call" | custom-call | flops 939524096 | bytes 6291460 | tf_op jit(solution)/shard_map/weight_grad/pallas_call | solution.py:36
  58.7 0.2 collective-permute-done.11.refs_1_
  59.0 3.6 %collective-permute-done.12.refs_2_ = bf16[512,128]{1,0:T(8,128)(2,1)S(1)} collective-permute-done((bf16[512,128]{1,0:T(8,128)(2,1)S(1)}, bf16[512,128]{1,0:T(8,128)(2,1)S(1)}, u32[]{:S(2)}, u32[]{:S(2)}) %collective-permute-start.12) | collective-permute-done | bytes 131104 | tf_op jit(solution)/shard_map/ppermute | solution.py:62
  62.7 0.1 collective-permute-start.15
  62.7 3.8 %all-to-all-start = ((bf16[4,256,640]{2,1,0:T(8,128)(2,1)}), bf16[4,256,640]{2,1,0:T(8,128)(2,1)S(1)}, u32[]{:S(2)}, u32[]{:S(2)}) async-start(bf16[4,256,640]{2,1,0:T(8,128)(2,1)} %weight_grad.1), calls=%async_computation | async-start | bytes 2621440 | tf_op jit(solution)/shard_map/all_to_all | solution.py:65
  66.5 1.2 %gather_grad.6.refs_1_ = bf16[1024,128]{1,0:T(8,128)(2,1)S(1)} custom-call(s32[1]{0:T(128)S(6)} %mul.35.base_ref, s32[4,2,2,512]{3,2,1,0:T(2,128)S(1)} %pad_add_fusion.key_ref, bf16[4,512,128]{2,1,0:T(8,128)(2,1)S(1)} %pack.1.refs_0_), custom_call_target="tpu_custom_call" | custom-call | flops 1073741824 | bytes 819204 | tf_op jit(solution)/shard_map/gather_grad/pallas_call | solution.py:36
  67.8 1.2 %gather_grad.7 = bf16[1024,128]{1,0:T(8,128)(2,1)S(1)} custom-call(s32[1]{0:T(128)S(6)} %mul.35.base_ref, s32[4,2,2,512]{3,2,1,0:T(2,128)S(1)} %pad_add_fusion.key_ref, bf16[4,512,128]{2,1,0:T(8,128)(2,1)S(1)} %collective-permute-done.15.refs_1_.refs_0_, bf16[1024,128]{1,0:T(8,128)(2,1)S(1)} %gather_grad.6.refs_1_), custom_call_target="tpu_custom_call" | custom-call | flops 1073741824 | bytes 1081348 | tf_op jit(solution)/shard_map/gather_grad/pallas_call | solution.py:36
  69.0 1.5 %collective-permute-start.16 = (bf16[1024,128]{1,0:T(8,128)(2,1)S(1)}, bf16[1024,128]{1,0:T(8,128)(2,1)S(1)}, u32[]{:S(2)}, u32[]{:S(2)}) collective-permute-start(bf16[1024,128]{1,0:T(8,128)(2,1)S(1)} %gather_grad.7), channel_id=1, source_target_pairs={{0,2},{1,3},{2,0},{3,1},{4,6},{5,7},{6,4},{7,5},{8,10},{9,11},{10,... | collective-permute-start | bytes 786440 | tf_op jit(solution)/shard_map/ppermute | solution.py:69
  70.5 2.3 %gather_grad.5.refs_0_ = f32[1024,128]{1,0:T(8,128)S(1)} custom-call(s32[1]{0:T(128)S(6)} %mul.40.base_ref, s32[4,2,2,512]{3,2,1,0:T(2,128)S(1)} %pad_add_fusion.key_ref, bf16[4,512,128]{2,1,0:T(8,128)(2,1)S(1)} %pack.1.refs_0_, bf16[4,512,128]{2,1,0:T(8,128)(2,1)S(1)} %collective-permute-done.15.refs_1_.refs_0_), custom_call_target="tpu_custom_call" | custom-call | flops 2147483648 | bytes 1605636 | tf_op jit(solution)/shard_map/gather_grad/pallas_call | solution.py:36
  72.8 5.0 %collective-permute-done.16.refs_1_ = bf16[1024,128]{1,0:T(8,128)(2,1)S(1)} collective-permute-done((bf16[1024,128]{1,0:T(8,128)(2,1)S(1)}, bf16[1024,128]{1,0:T(8,128)(2,1)S(1)}, u32[]{:S(2)}, u32[]{:S(2)}) %collective-permute-start.16) | collective-permute-done | bytes 262176 | tf_op jit(solution)/shard_map/ppermute | solution.py:69
  77.8 0.1 add_up.2
  77.9 3.5 %collective-permute-start.17 = (bf16[1024,128]{1,0:T(8,128)(2,1)S(1)}, bf16[1024,128]{1,0:T(8,128)(2,1)S(1)}, u32[]{:S(2)}, u32[]{:S(2)}) collective-permute-start(bf16[1024,128]{1,0:T(8,128)(2,1)S(1)} %add_up.2), channel_id=1, source_target_pairs={{0,4},{1,5},{2,6},{3,7},{4,0},{5,1},{6,2},{7,3},{8,12},{9,13},{10,... | collective-permute-start | bytes 786440 | tf_op jit(solution)/shard_map/ppermute | solution.py:69
  81.4 2.3 %gather_grad.9 = bf16[1024,128]{1,0:T(8,128)(2,1)S(1)} custom-call(s32[1]{0:T(128)S(6)} %mul.42.base_ref, s32[4,2,2,512]{3,2,1,0:T(2,128)S(1)} %pad_add_fusion.key_ref, bf16[4,512,128]{2,1,0:T(8,128)(2,1)S(1)} %pack.1.refs_0_, bf16[4,512,128]{2,1,0:T(8,128)(2,1)S(1)} %collective-permute-done.15.refs_1_.refs_0_), custom_call_target="tpu_custom_call" | custom-call | flops 2147483648 | bytes 1343492 | tf_op jit(solution)/shard_map/gather_grad/pallas_call | solution.py:36
  83.7 0.4 collective-permute-start.18
  84.1 0.3 cut_line.1
  84.3 1.8 %collective-permute-start.19 = (bf16[2,64,640]{2,1,0:T(8,128)(2,1)S(1)}, bf16[2,64,640]{2,1,0:T(8,128)(2,1)S(1)}, u32[]{:S(2)}, u32[]{:S(2)}) collective-permute-start(bf16[2,64,640]{2,1,0:T(8,128)(2,1)S(1)} %get-tuple-element.70), channel_id=1, source_target_pairs={{0,2},{1,3},{2,0},{3,1},{4,6},{5,7},{6,4},{7,5},{8,10},{9,11},{10,... | collective-permute-start | bytes 491528 | tf_op jit(solution)/shard_map/ppermute | solution.py:69
  86.1 2.3 %gather_grad.8.here_ref = f32[1024,128]{1,0:T(8,128)S(1)} custom-call(s32[1]{0:T(128)S(6)} %mul.44.base_ref, s32[4,2,2,512]{3,2,1,0:T(2,128)S(1)} %pad_add_fusion.key_ref, bf16[4,512,128]{2,1,0:T(8,128)(2,1)S(1)} %pack.1.refs_0_, bf16[4,512,128]{2,1,0:T(8,128)(2,1)S(1)} %collective-permute-done.15.refs_1_.refs_0_), custom_call_target="tpu_custom_call" | custom-call | flops 2147483648 | bytes 1605636 | tf_op jit(solution)/shard_map/gather_grad/pallas_call | solution.py:36
  88.5 11.9 %collective-permute-done.19.came_ref = bf16[2,64,640]{2,1,0:T(8,128)(2,1)S(1)} collective-permute-done((bf16[2,64,640]{2,1,0:T(8,128)(2,1)S(1)}, bf16[2,64,640]{2,1,0:T(8,128)(2,1)S(1)}, u32[]{:S(2)}, u32[]{:S(2)}) %collective-permute-start.19) | collective-permute-done | bytes 163872 | tf_op jit(solution)/shard_map/ppermute | solution.py:69
  100.4 0.1 collective-permute-start.20
  100.5 0.1 table_sums.2.here_ref
  100.6 0.8 table_sums.3
  101.4 4.4 %collective-permute-done.20 = bf16[1,64,640]{2,1,0:T(8,128)(2,1)S(1)} collective-permute-done((bf16[1,64,640]{2,1,0:T(8,128)(2,1)S(1)}, bf16[1,64,640]{2,1,0:T(8,128)(2,1)S(1)}, u32[]{:S(2)}, u32[]{:S(2)}) %collective-permute-start.20) | collective-permute-done | bytes 81952 | tf_op jit(solution)/shard_map/ppermute | solution.py:69
  105.8 1.2 %collective-permute-start.21 = (bf16[64,640]{1,0:T(8,128)(2,1)S(1)}, bf16[64,640]{1,0:T(8,128)(2,1)S(1)}, u32[]{:S(2)}, u32[]{:S(2)}) collective-permute-start(bf16[64,640]{1,0:T(8,128)(2,1)S(1)} %add_up.3.refs_0_), channel_id=1, source_target_pairs={{0,8},{8,0},{16,24},{24,16},{1,9},{9,1},{17,25},{25,17},{2,10},{10... | collective-permute-start | bytes 245768 | tf_op jit(solution)/shard_map/ppermute | solution.py:62
  107.1 1.5 %collective-permute-start.22 = (bf16[64,640]{1,0:T(8,128)(2,1)S(1)}, bf16[64,640]{1,0:T(8,128)(2,1)S(1)}, u32[]{:S(2)}, u32[]{:S(2)}) collective-permute-start(bf16[64,640]{1,0:T(8,128)(2,1)S(1)} %add_up.3.refs_0_), channel_id=1, source_target_pairs={{0,16},{8,24},{16,0},{24,8},{1,17},{9,25},{17,1},{25,9},{2,18},{10... | collective-permute-start | bytes 245768 | tf_op jit(solution)/shard_map/ppermute | solution.py:62
  108.5 0.9 collective-permute-start.23
  109.4 1.0 collective-permute-done.21.refs_1_
  110.4 1.2 %collective-permute-done.22.refs_2_ = bf16[64,640]{1,0:T(8,128)(2,1)S(1)} collective-permute-done((bf16[64,640]{1,0:T(8,128)(2,1)S(1)}, bf16[64,640]{1,0:T(8,128)(2,1)S(1)}, u32[]{:S(2)}, u32[]{:S(2)}) %collective-permute-start.22) | collective-permute-done | bytes 81952 | tf_op jit(solution)/shard_map/ppermute | solution.py:62
  111.5 2.4 %collective-permute-done.23.refs_3_ = bf16[64,640]{1,0:T(8,128)(2,1)S(1)} collective-permute-done((bf16[64,640]{1,0:T(8,128)(2,1)S(1)}, bf16[64,640]{1,0:T(8,128)(2,1)S(1)}, u32[]{:S(2)}, u32[]{:S(2)}) %collective-permute-start.23) | collective-permute-done | bytes 81952 | tf_op jit(solution)/shard_map/ppermute | solution.py:62
  113.9 0.9 assemble.1
  (22 shorter events, 0.2 us)
Async XLA Ops:
  1.7 16.1 %collective-permute-start = (bf16[1024,128]{1,0:T(8,128)(2,1)S(1)}, bf16[1024,128]{1,0:T(8,128)(2,1)S(1)}, u32[]{:S(2)}, u32[]{:S(2)}) collective-permute-start(bf16[1024,128]{1,0:T(8,128)(2,1)S(1)} %pad_maximum_fusion.chunk_ref), channel_id=1, source_target_pairs={{0,4},{1,5},{2,6},{3,7},{4,0},{5,1},{6,2},{7,3},{8,12},{9,13},{10,... | collective-permute-start | bytes 786440 | tf_op jit(solution)/shard_map/ppermute | solution.py:69
  6.5 1.7 %collective-permute-start.2 = (s32[2,512]{1,0:T(2,128)S(1)}, s32[2,512]{1,0:T(2,128)S(1)}, u32[]{:S(2)}, u32[]{:S(2)}) collective-permute-start(s32[2,512]{1,0:T(2,128)S(1)} %get-tuple-element.80), channel_id=1, source_target_pairs={{0,1},{1,0},{2,3},{3,2},{4,5},{5,4},{6,7},{7,6},{8,9},{9,8},{10,11... | collective-permute-start | bytes 12296 | tf_op jit(solution)/shard_map/ppermute | solution.py:72
  6.6 15.5 %collective-permute-start.6 = (bf16[1024,128]{1,0:T(8,128)(2,1)S(1)}, bf16[1024,128]{1,0:T(8,128)(2,1)S(1)}, u32[]{:S(2)}, u32[]{:S(2)}) collective-permute-start(bf16[1024,128]{1,0:T(8,128)(2,1)S(1)} %pad_maximum_fusion.chunk_ref), channel_id=1, source_target_pairs={{0,2},{1,3},{2,0},{3,1},{4,6},{5,7},{6,4},{7,5},{8,10},{9,11},{10,... | collective-permute-start | bytes 786440 | tf_op jit(solution)/shard_map/ppermute | solution.py:69
  8.2 10.2 %collective-permute-start.3 = (s32[2,2,512]{2,1,0:T(2,128)S(1)}, s32[2,2,512]{2,1,0:T(2,128)S(1)}, u32[]{:S(2)}, u32[]{:S(2)}) collective-permute-start(s32[2,2,512]{2,1,0:T(2,128)S(1)} %get-tuple-element.78), channel_id=1, source_target_pairs={{0,8},{8,0},{16,24},{24,16},{1,9},{9,1},{17,25},{25,17},{2,10},{10... | collective-permute-start | bytes 24584 | tf_op jit(solution)/shard_map/ppermute | solution.py:62
  9.8 8.7 %collective-permute-start.4 = (s32[2,2,512]{2,1,0:T(2,128)S(1)}, s32[2,2,512]{2,1,0:T(2,128)S(1)}, u32[]{:S(2)}, u32[]{:S(2)}) collective-permute-start(s32[2,2,512]{2,1,0:T(2,128)S(1)} %get-tuple-element.78), channel_id=1, source_target_pairs={{0,16},{8,24},{16,0},{24,8},{1,17},{9,25},{17,1},{25,9},{2,18},{10... | collective-permute-start | bytes 24584 | tf_op jit(solution)/shard_map/ppermute | solution.py:62
  11.3 7.1 %collective-permute-start.5 = (s32[2,2,512]{2,1,0:T(2,128)S(1)}, s32[2,2,512]{2,1,0:T(2,128)S(1)}, u32[]{:S(2)}, u32[]{:S(2)}) collective-permute-start(s32[2,2,512]{2,1,0:T(2,128)S(1)} %get-tuple-element.78), channel_id=1, source_target_pairs={{0,24},{8,16},{16,8},{24,0},{1,25},{9,17},{17,9},{25,1},{2,26},{10... | collective-permute-start | bytes 24584 | tf_op jit(solution)/shard_map/ppermute | solution.py:62
  17.8 9.0 %collective-permute-start.1 = (bf16[1024,128]{1,0:T(8,128)(2,1)S(1)}, bf16[1024,128]{1,0:T(8,128)(2,1)S(1)}, u32[]{:S(2)}, u32[]{:S(2)}) collective-permute-start(bf16[1024,128]{1,0:T(8,128)(2,1)S(1)} %collective-permute-done.chunk_ref), channel_id=1, source_target_pairs={{0,2},{1,3},{2,0},{3,1},{4,6},{5,7},{6,4},{7,5},{8,10},{9,11},{10,... | collective-permute-start | bytes 786440 | tf_op jit(solution)/shard_map/ppermute | solution.py:69
  28.0 2.0 %collective-permute-start.7 = (bf16[4,512,128]{2,1,0:T(8,128)(2,1)S(1)}, bf16[4,512,128]{2,1,0:T(8,128)(2,1)S(1)}, u32[]{:S(2)}, u32[]{:S(2)}) collective-permute-start(bf16[4,512,128]{2,1,0:T(8,128)(2,1)S(1)} %fetch.9), channel_id=1, source_target_pairs={{0,1},{1,0},{2,3},{3,2},{4,5},{5,4},{6,7},{7,6},{8,9},{9,8},{10,11... | collective-permute-start | bytes 1572872 | tf_op jit(solution)/shard_map/ppermute | solution.py:72
  28.1 11.4 %copy-start = (bf16[512,512]{1,0:T(8,128)(2,1)S(1)}, bf16[512,512]{1,0:T(8,128)(2,1)}, u32[]{:S(2)}) copy-start(bf16[512,512]{1,0:T(8,128)(2,1)} %c_ref.1) | copy-start | bytes 1572868
  28.1 11.4 %copy-start.1 = (bf16[512,2048]{1,0:T(8,128)(2,1)S(1)}, bf16[512,2048]{1,0:T(8,128)(2,1)}, u32[]{:S(2)}) copy-start(bf16[512,2048]{1,0:T(8,128)(2,1)} %wp_ref.1) | copy-start | bytes 6291460
  28.1 11.4 %copy-start.2 = (bf16[512,512]{1,0:T(8,128)(2,1)S(1)}, bf16[512,512]{1,0:T(8,128)(2,1)}, u32[]{:S(2)}) copy-start(bf16[512,512]{1,0:T(8,128)(2,1)} %wo_ref.1) | copy-start | bytes 1572868
  28.1 11.4 %copy-start.3 = (f32[512]{0:T(512)S(1)}, f32[512]{0:T(512)}, u32[]{:S(2)}) copy-start(f32[512]{0:T(512)} %param.16) | copy-start | bytes 6148
  30.1 7.3 %collective-permute-start.10 = (bf16[512,128]{1,0:T(8,128)(2,1)S(1)}, bf16[512,128]{1,0:T(8,128)(2,1)S(1)}, u32[]{:S(2)}, u32[]{:S(2)}) collective-permute-start(bf16[512,128]{1,0:T(8,128)(2,1)S(1)} %get-tuple-element.50), channel_id=1, source_target_pairs={{0,24},{8,16},{16,8},{24,0},{1,25},{9,17},{17,9},{25,1},{2,26},{10... | collective-permute-start | bytes 393224 | tf_op jit(solution)/shard_map/ppermute | solution.py:62
  32.7 6.9 %collective-permute-start.8 = (bf16[512,128]{1,0:T(8,128)(2,1)S(1)}, bf16[512,128]{1,0:T(8,128)(2,1)S(1)}, u32[]{:S(2)}, u32[]{:S(2)}) collective-permute-start(bf16[512,128]{1,0:T(8,128)(2,1)S(1)} %get-tuple-element.48), channel_id=1, source_target_pairs={{0,8},{8,0},{16,24},{24,16},{1,9},{9,1},{17,25},{25,17},{2,10},{10... | collective-permute-start | bytes 393224 | tf_op jit(solution)/shard_map/ppermute | solution.py:62
  33.2 6.3 %collective-permute-start.9 = (bf16[512,128]{1,0:T(8,128)(2,1)S(1)}, bf16[512,128]{1,0:T(8,128)(2,1)S(1)}, u32[]{:S(2)}, u32[]{:S(2)}) collective-permute-start(bf16[512,128]{1,0:T(8,128)(2,1)S(1)} %get-tuple-element.49), channel_id=1, source_target_pairs={{0,16},{8,24},{16,0},{24,8},{1,17},{9,25},{17,1},{25,9},{2,18},{10... | collective-permute-start | bytes 393224 | tf_op jit(solution)/shard_map/ppermute | solution.py:62
  52.7 3.5 %collective-permute-start.14 = (bf16[4,256,640]{2,1,0:T(8,128)(2,1)S(1)}, bf16[4,256,640]{2,1,0:T(8,128)(2,1)S(1)}, u32[]{:S(2)}, u32[]{:S(2)}) collective-permute-start(bf16[4,256,640]{2,1,0:T(8,128)(2,1)S(1)} %get-tuple-element.59), channel_id=1, source_target_pairs={{0,1},{1,0},{2,3},{3,2},{4,5},{5,4},{6,7},{7,6},{8,9},{9,8},{10,11... | collective-permute-start | bytes 3932168 | tf_op jit(solution)/shard_map/ppermute | solution.py:72
  52.7 6.3 %collective-permute-start.11 = (bf16[512,128]{1,0:T(8,128)(2,1)S(1)}, bf16[512,128]{1,0:T(8,128)(2,1)S(1)}, u32[]{:S(2)}, u32[]{:S(2)}) collective-permute-start(bf16[512,128]{1,0:T(8,128)(2,1)S(1)} %get-tuple-element.53), channel_id=1, source_target_pairs={{0,8},{8,0},{16,24},{24,16},{1,9},{9,1},{17,25},{25,17},{2,10},{10... | collective-permute-start | bytes 393224 | tf_op jit(solution)/shard_map/ppermute | solution.py:62
  54.2 8.4 %collective-permute-start.12 = (bf16[512,128]{1,0:T(8,128)(2,1)S(1)}, bf16[512,128]{1,0:T(8,128)(2,1)S(1)}, u32[]{:S(2)}, u32[]{:S(2)}) collective-permute-start(bf16[512,128]{1,0:T(8,128)(2,1)S(1)} %get-tuple-element.54), channel_id=1, source_target_pairs={{0,16},{8,24},{16,0},{24,8},{1,17},{9,25},{17,1},{25,9},{2,18},{10... | collective-permute-start | bytes 393224 | tf_op jit(solution)/shard_map/ppermute | solution.py:62
  55.7 7.0 %collective-permute-start.13 = (bf16[512,128]{1,0:T(8,128)(2,1)S(1)}, bf16[512,128]{1,0:T(8,128)(2,1)S(1)}, u32[]{:S(2)}, u32[]{:S(2)}) collective-permute-start(bf16[512,128]{1,0:T(8,128)(2,1)S(1)} %get-tuple-element.55), channel_id=1, source_target_pairs={{0,24},{8,16},{16,8},{24,0},{1,25},{9,17},{17,9},{25,1},{2,26},{10... | collective-permute-start | bytes 393224 | tf_op jit(solution)/shard_map/ppermute | solution.py:62
  62.7 5.1 %collective-permute-start.15 = (bf16[4,512,128]{2,1,0:T(8,128)(2,1)S(1)}, bf16[4,512,128]{2,1,0:T(8,128)(2,1)S(1)}, u32[]{:S(2)}, u32[]{:S(2)}) collective-permute-start(bf16[4,512,128]{2,1,0:T(8,128)(2,1)S(1)} %pack.1.refs_0_), channel_id=1, source_target_pairs={{0,1},{1,0},{2,3},{3,2},{4,5},{5,4},{6,7},{7,6},{8,9},{9,8},{10,11... | collective-permute-start | bytes 1572872 | tf_op jit(solution)/shard_map/ppermute | solution.py:72
  62.7 21.3 %all-to-all-start = ((bf16[4,256,640]{2,1,0:T(8,128)(2,1)}), bf16[4,256,640]{2,1,0:T(8,128)(2,1)S(1)}, u32[]{:S(2)}, u32[]{:S(2)}) async-start(bf16[4,256,640]{2,1,0:T(8,128)(2,1)} %weight_grad.1), calls=%async_computation | async-start | bytes 2621440 | tf_op jit(solution)/shard_map/all_to_all | solution.py:65
  69.0 8.8 %collective-permute-start.16 = (bf16[1024,128]{1,0:T(8,128)(2,1)S(1)}, bf16[1024,128]{1,0:T(8,128)(2,1)S(1)}, u32[]{:S(2)}, u32[]{:S(2)}) collective-permute-start(bf16[1024,128]{1,0:T(8,128)(2,1)S(1)} %gather_grad.7), channel_id=1, source_target_pairs={{0,2},{1,3},{2,0},{3,1},{4,6},{5,7},{6,4},{7,5},{8,10},{9,11},{10,... | collective-permute-start | bytes 786440 | tf_op jit(solution)/shard_map/ppermute | solution.py:69
  77.9 22.6 %collective-permute-start.17 = (bf16[1024,128]{1,0:T(8,128)(2,1)S(1)}, bf16[1024,128]{1,0:T(8,128)(2,1)S(1)}, u32[]{:S(2)}, u32[]{:S(2)}) collective-permute-start(bf16[1024,128]{1,0:T(8,128)(2,1)S(1)} %add_up.2), channel_id=1, source_target_pairs={{0,4},{1,5},{2,6},{3,7},{4,0},{5,1},{6,2},{7,3},{8,12},{9,13},{10,... | collective-permute-start | bytes 786440 | tf_op jit(solution)/shard_map/ppermute | solution.py:69
  83.7 16.9 %collective-permute-start.18 = (bf16[1024,128]{1,0:T(8,128)(2,1)S(1)}, bf16[1024,128]{1,0:T(8,128)(2,1)S(1)}, u32[]{:S(2)}, u32[]{:S(2)}) collective-permute-start(bf16[1024,128]{1,0:T(8,128)(2,1)S(1)} %gather_grad.9), channel_id=1, source_target_pairs={{0,2},{1,3},{2,0},{3,1},{4,6},{5,7},{6,4},{7,5},{8,10},{9,11},{10,... | collective-permute-start | bytes 786440 | tf_op jit(solution)/shard_map/ppermute | solution.py:69
  84.3 16.0 %collective-permute-start.19 = (bf16[2,64,640]{2,1,0:T(8,128)(2,1)S(1)}, bf16[2,64,640]{2,1,0:T(8,128)(2,1)S(1)}, u32[]{:S(2)}, u32[]{:S(2)}) collective-permute-start(bf16[2,64,640]{2,1,0:T(8,128)(2,1)S(1)} %get-tuple-element.70), channel_id=1, source_target_pairs={{0,2},{1,3},{2,0},{3,1},{4,6},{5,7},{6,4},{7,5},{8,10},{9,11},{10,... | collective-permute-start | bytes 491528 | tf_op jit(solution)/shard_map/ppermute | solution.py:69
  100.4 5.4 %collective-permute-start.20 = (bf16[1,64,640]{2,1,0:T(8,128)(2,1)S(1)}, bf16[1,64,640]{2,1,0:T(8,128)(2,1)S(1)}, u32[]{:S(2)}, u32[]{:S(2)}) collective-permute-start(bf16[1,64,640]{2,1,0:T(8,128)(2,1)S(1)} %get-tuple-element.72), channel_id=1, source_target_pairs={{0,4},{1,5},{2,6},{3,7},{4,0},{5,1},{6,2},{7,3},{8,12},{9,13},{10,... | collective-permute-start | bytes 245768 | tf_op jit(solution)/shard_map/ppermute | solution.py:69
  105.8 4.5 %collective-permute-start.21 = (bf16[64,640]{1,0:T(8,128)(2,1)S(1)}, bf16[64,640]{1,0:T(8,128)(2,1)S(1)}, u32[]{:S(2)}, u32[]{:S(2)}) collective-permute-start(bf16[64,640]{1,0:T(8,128)(2,1)S(1)} %add_up.3.refs_0_), channel_id=1, source_target_pairs={{0,8},{8,0},{16,24},{24,16},{1,9},{9,1},{17,25},{25,17},{2,10},{10... | collective-permute-start | bytes 245768 | tf_op jit(solution)/shard_map/ppermute | solution.py:62
  107.1 4.4 %collective-permute-start.22 = (bf16[64,640]{1,0:T(8,128)(2,1)S(1)}, bf16[64,640]{1,0:T(8,128)(2,1)S(1)}, u32[]{:S(2)}, u32[]{:S(2)}) collective-permute-start(bf16[64,640]{1,0:T(8,128)(2,1)S(1)} %add_up.3.refs_0_), channel_id=1, source_target_pairs={{0,16},{8,24},{16,0},{24,8},{1,17},{9,25},{17,1},{25,9},{2,18},{10... | collective-permute-start | bytes 245768 | tf_op jit(solution)/shard_map/ppermute | solution.py:62
  108.5 5.3 %collective-permute-start.23 = (bf16[64,640]{1,0:T(8,128)(2,1)S(1)}, bf16[64,640]{1,0:T(8,128)(2,1)S(1)}, u32[]{:S(2)}, u32[]{:S(2)}) collective-permute-start(bf16[64,640]{1,0:T(8,128)(2,1)S(1)} %add_up.3.refs_0_), channel_id=1, source_target_pairs={{0,24},{8,16},{16,8},{24,0},{1,25},{9,17},{17,9},{25,1},{2,26},{10... | collective-permute-start | bytes 245768 | tf_op jit(solution)/shard_map/ppermute | solution.py:62

commit v10 on v8

--- a/solution.py
+++ b/solution.py
@@ -129,24 +129,16 @@
     return run("add_up", body, [(parts[0].shape, BF16)], parts)[0]
 
 
-def table_sums(here, came, out, flops=0):
-    rows, cols = here.shape[0] // 2, here.shape[1]
-    cuts = 2 if out else 1
-
-    def body(here_ref, *refs):
-        came_refs, out_refs = refs[:-cuts], refs[-cuts:]
-        for i in range(2):
+def table_sums(here, came, cuts):
+    rows, cols = here.shape[0] // cuts, here.shape[1]
+
+    def body(here_ref, came_ref, *out_refs):
+        for i in range(cuts):
             span = slice(i * rows, (i + 1) * rows)
-            total = here_ref[span, :]
-            for ref in came_refs:
-                total = total + ref[span, :].astype(F32)
-            if out:
-                out_refs[i][...] = total
-            else:
-                out_refs[0][span, :] = total
-
-    outs = [((2 * rows // cuts, cols), F32)] * cuts
-    return run("table_sums", body, outs, [here, *came], flops=flops)
+            out_refs[i][...] = here_ref[span, :] + came_ref[span, :].astype(F32)
+
+    outs = [((rows, cols), F32)] * cuts
+    return run("table_sums", body, outs, [here, came], flops=EARLY)
 
 
 def gather_grad(base, keys, cohorts, tokens, rows, before=(), out=BF16):
@@ -549,20 +541,21 @@
             first = gather_grad(bases[k], keys, both[:1], [tokens], rows)
             raw[k] = gather_grad(bases[k], keys, both[1:], [there], rows, first, out)
         else:
-            if k == 1 and line > 2:
-                both_there = lax.optimization_barrier((both_there, sums[line // 2]))[0]
+            after = {1: raw[last], 0: sums.get(line // 2)}.get(k)
+            if after is not None:
+                both_there = lax.optimization_barrier((both_there, after))[0]
             raw[k] = gather_grad(bases[k], keys, both, both_there, rows, out=out)
         came = [grid.over_line(sums[k ^ step], step) for step in steps]
         if k == 0:
-            table = raw[k]
-            if len(came) > 1:
-                table = table_sums(table[0], came[1:], out=False, flops=EARLY)
-            item_grad, action_grad = table_sums(table[0], came[:1], out=True)
+            near, table = came[0], raw[k][0]
+            for part in came[:-1]:
+                table = table_sums(table, part, 1)[0]
+            item_grad, action_grad = table_sums(table, came[-1], 2)
         else:
             sums[k] = add_up(raw[k] + came) if steps else raw[k][0]
 
     for step in range(1, bits + 1):
-        after = raw[line // 2] if step < bits else sums[line // 2]
+        after = [raw[1], raw[line // 2]] if step < bits else [near, sums[line // 2]]
         swapped = lax.optimization_barrier((swapped, after))[0]
         if step < bits:
             kept, swapped = swap_weights(fold(replica, kept, swapped, step), step)

time: 107 us -> 106 us (level)
    ppermute x16, waiting for transfers between devices: 16.3 us -> 14 us  [over_replica(): return lax.ppermute(value, 'replica', [(i, i ^ step) for i in range(n)])]
    ppermute x8, waiting for transfers between devices: 16.7 us -> 18.5 us  [over_line(): return lax.ppermute(value, 'sparse', pairs)]
  transfers between devices with their start and end apart: 28 -> 28, of which waited for: 16 -> 15; matrix products, arithmetic and copies ran while one was open for 2% -> 2% of each run, Pallas kernels for 20% -> 20%
where the time goes in v10:
time: 106 us
  Pallas kernels  36.5 us (34%)
  waiting for transfers between devices  33.1 us (31%)
  starting transfers between devices  32.6 us (31%)
  local copies, waits for them, and re-layouts  2.25 us (2%)
    pallas_call x22, Pallas kernels, run(): pl.pallas_call(body, out_shape=outs, in_specs=places, out_specs=[in_vmem]...  36.5 us
    ppermute x8, waiting for transfers between devices, over_line(): return lax.ppermute(value, 'sparse', pairs)  18.5 us
    ppermute x16, starting transfers between devices, over_replica(): return lax.ppermute(value, 'replica', [(i, i ^ step) for i in range(n)])  18.3 us
    ppermute x8, starting transfers between devices, over_line(): return lax.ppermute(value, 'sparse', pairs)  14 us
    ppermute x16, waiting for transfers between devices, over_replica(): return lax.ppermute(value, 'replica', [(i, i ^ step) for i in range(n)])  14 us
  transfers between devices with their start and end apart: 28, of which 15 were waited for; matrix products, arithmetic and copies ran while one was open for 2% of the time, Pallas kernels for 20%

profile of v10, /device:TPU:0, one launch (start us, length us, event | category | flops | bytes accessed | tf_op | source)
XLA Modules:
  0.0 106.1 jit_solution(1857264511278068861)
XLA Ops:
  0.6 1.0 constant_dynamic-slice_fusion
  1.7 4.1 %collective-permute-start = (bf16[1024,128]{1,0:T(8,128)(2,1)S(1)}, bf16[1024,128]{1,0:T(8,128)(2,1)S(1)}, u32[]{:S(2)}, u32[]{:S(2)}) collective-permute-start(bf16[1024,128]{1,0:T(8,128)(2,1)S(1)} %pad_maximum_fusion.chunk_ref), channel_id=1, source_target_pairs={{0,4},{1,5},{2,6},{3,7},{4,0},{5,1},{6,2},{7,3},{8,12},{9,13},{10,... | collective-permute-start | bytes 786440 | tf_op jit(solution)/shard_map/ppermute | solution.py:66
  5.8 0.7 add_bitcast_fusion
  6.5 0.1 collective-permute-start.2
  6.6 1.6 %collective-permute-start.6 = (bf16[1024,128]{1,0:T(8,128)(2,1)S(1)}, bf16[1024,128]{1,0:T(8,128)(2,1)S(1)}, u32[]{:S(2)}, u32[]{:S(2)}) collective-permute-start(bf16[1024,128]{1,0:T(8,128)(2,1)S(1)} %pad_maximum_fusion.chunk_ref), channel_id=1, source_target_pairs={{0,2},{1,3},{2,0},{3,1},{4,6},{5,7},{6,4},{7,5},{8,10},{9,11},{10,... | collective-permute-start | bytes 786440 | tf_op jit(solution)/shard_map/ppermute | solution.py:66
  8.2 1.6 %collective-permute-start.4 = (s32[2,2,512]{2,1,0:T(2,128)S(1)}, s32[2,2,512]{2,1,0:T(2,128)S(1)}, u32[]{:S(2)}, u32[]{:S(2)}) collective-permute-start(s32[2,2,512]{2,1,0:T(2,128)S(1)} %get-tuple-element.104), channel_id=1, source_target_pairs={{0,16},{8,24},{16,0},{24,8},{1,17},{9,25},{17,1},{25,9},{2,18},{10... | collective-permute-start | bytes 24584 | tf_op jit(solution)/shard_map/ppermute | solution.py:62
  9.8 1.5 %collective-permute-start.3 = (s32[2,2,512]{2,1,0:T(2,128)S(1)}, s32[2,2,512]{2,1,0:T(2,128)S(1)}, u32[]{:S(2)}, u32[]{:S(2)}) collective-permute-start(s32[2,2,512]{2,1,0:T(2,128)S(1)} %get-tuple-element.104), channel_id=1, source_target_pairs={{0,8},{8,0},{16,24},{24,16},{1,9},{9,1},{17,25},{25,17},{2,10},{10... | collective-permute-start | bytes 24584 | tf_op jit(solution)/shard_map/ppermute | solution.py:62
  11.3 0.5 collective-permute-start.5
  11.8 6.0 %collective-permute-done.chunk_ref = bf16[1024,128]{1,0:T(8,128)(2,1)S(1)} collective-permute-done((bf16[1024,128]{1,0:T(8,128)(2,1)S(1)}, bf16[1024,128]{1,0:T(8,128)(2,1)S(1)}, u32[]{:S(2)}, u32[]{:S(2)}) %collective-permute-start) | collective-permute-done | bytes 262176 | tf_op jit(solution)/shard_map/ppermute | solution.py:66
  17.8 0.7 collective-permute-start.1
  18.5 1.2 %broadcast_in_dim.14.key_ref = s32[4,2,2,512,128]{4,3,2,1,0:T(8,128)S(1)} broadcast(s32[4,2,2,512]{3,2,1,0:T(2,128)S(1)} %pad_add_fusion.key_ref), dimensions={0,1,2,3} | broadcast | bytes 4227072 | tf_op jit(solution)/shard_map/broadcast_in_dim | solution.py:502
  19.7 2.3 %fetch.5 = (bf16[4,512,128]{2,1,0:T(8,128)(2,1)S(1)}, bf16[4,512,128]{2,1,0:T(8,128)(2,1)S(1)}) custom-call(s32[1]{0:T(128)S(6)} %mul.44.base_ref, bf16[1024,128]{1,0:T(8,128)(2,1)S(1)} %pad_maximum_fusion.chunk_ref, s32[4,2,2,512,128]{4,3,2,1,0:T(8,128)S(1)} %broadcast_in_dim.14.key_ref), custom_call_target="tpu_custom_call" | custom-call | flops 536870912 | bytes 5505028 | tf_op jit(solution)/shard_map/fetch/pallas_call | solution.py:36
  22.1 2.3 %fetch.6 = (bf16[4,512,128]{2,1,0:T(8,128)(2,1)S(1)}, bf16[4,512,128]{2,1,0:T(8,128)(2,1)S(1)}) custom-call(s32[1]{0:T(128)S(6)} %mul.42.base_ref, bf16[1024,128]{1,0:T(8,128)(2,1)S(1)} %collective-permute-done.6.chunk_ref, s32[4,2,2,512,128]{4,3,2,1,0:T(8,128)S(1)} %broadcast_in_dim.14.key_ref, bf16[4,512,128]{2,1,0:T(8,128)(2,1)S(1)} %get-tuple-element.54.refs_0_, ...), custom_call_target="tpu_custom_call" | custom-call | flops 536870912 | bytes 6553604 | tf_op jit(solution)/shard_map/fetch/pallas_call | solution.py:36
  24.4 2.3 %fetch.7 = (bf16[4,512,128]{2,1,0:T(8,128)(2,1)S(1)}, bf16[4,512,128]{2,1,0:T(8,128)(2,1)S(1)}) custom-call(s32[1]{0:T(128)S(6)} %mul.40.base_ref, bf16[1024,128]{1,0:T(8,128)(2,1)S(1)} %collective-permute-done.chunk_ref, s32[4,2,2,512,128]{4,3,2,1,0:T(8,128)S(1)} %broadcast_in_dim.14.key_ref, bf16[4,512,128]{2,1,0:T(8,128)(2,1)S(1)} %get-tuple-element.56.refs_0_, ...), custom_call_target="tpu_custom_call" | custom-call | flops 536870912 | bytes 6553604 | tf_op jit(solution)/shard_map/fetch/pallas_call | solution.py:36
  26.8 1.3 %fetch.9 = bf16[4,512,128]{2,1,0:T(8,128)(2,1)S(1)} custom-call(s32[1]{0:T(128)S(6)} %mul.35.base_ref, bf16[1024,128]{1,0:T(8,128)(2,1)S(1)} %collective-permute-done.1.chunk_ref, s32[4,2,2,512,128]{4,3,2,1,0:T(8,128)S(1)} %broadcast_in_dim.14.key_ref, bf16[4,512,128]{2,1,0:T(8,128)(2,1)S(1)} %get-tuple-element.59.refs_0_), custom_call_target="tpu_custom_call" | custom-call | flops 268435456 | bytes 5505028 | tf_op jit(solution)/shard_map/fetch/pallas_call | solution.py:36
  28.0 0.1 collective-permute-start.7
  28.1 0.0 copy-start
  28.2 1.2 %fetch.8.left_ref = bf16[4,512,128]{2,1,0:T(8,128)(2,1)S(1)} custom-call(s32[1]{0:T(128)S(6)} %mul.35.base_ref, bf16[1024,128]{1,0:T(8,128)(2,1)S(1)} %collective-permute-done.1.chunk_ref, s32[4,2,2,512,128]{4,3,2,1,0:T(8,128)S(1)} %broadcast_in_dim.14.key_ref, bf16[4,512,128]{2,1,0:T(8,128)(2,1)S(1)} %get-tuple-element.58.refs_0_), custom_call_target="tpu_custom_call" | custom-call | flops 268435456 | bytes 5505028 | tf_op jit(solution)/shard_map/fetch/pallas_call | solution.py:36
  29.4 0.6 collective-permute-done.7.right_ref
  30.0 0.1 combine.1
  30.1 1.6 %collective-permute-start.8 = (bf16[512,128]{1,0:T(8,128)(2,1)S(1)}, bf16[512,128]{1,0:T(8,128)(2,1)S(1)}, u32[]{:S(2)}, u32[]{:S(2)}) collective-permute-start(bf16[512,128]{1,0:T(8,128)(2,1)S(1)} %get-tuple-element.61), channel_id=1, source_target_pairs={{0,8},{8,0},{16,24},{24,16},{1,9},{9,1},{17,25},{25,17},{2,10},{10... | collective-permute-start | bytes 393224 | tf_op jit(solution)/shard_map/ppermute | solution.py:62
  31.7 1.5 %collective-permute-start.9 = (bf16[512,128]{1,0:T(8,128)(2,1)S(1)}, bf16[512,128]{1,0:T(8,128)(2,1)S(1)}, u32[]{:S(2)}, u32[]{:S(2)}) collective-permute-start(bf16[512,128]{1,0:T(8,128)(2,1)S(1)} %get-tuple-element.62), channel_id=1, source_target_pairs={{0,16},{8,24},{16,0},{24,8},{1,17},{9,25},{17,1},{25,9},{2,18},{10... | collective-permute-start | bytes 393224 | tf_op jit(solution)/shard_map/ppermute | solution.py:62
  33.2 0.5 collective-permute-start.10
  33.7 2.4 %collective-permute-done.8.refs_1_ = bf16[512,128]{1,0:T(8,128)(2,1)S(1)} collective-permute-done((bf16[512,128]{1,0:T(8,128)(2,1)S(1)}, bf16[512,128]{1,0:T(8,128)(2,1)S(1)}, u32[]{:S(2)}, u32[]{:S(2)}) %collective-permute-start.8) | collective-permute-done | bytes 131104 | tf_op jit(solution)/shard_map/ppermute | solution.py:62
  36.1 3.7 %collective-permute-done.9.refs_2_ = bf16[512,128]{1,0:T(8,128)(2,1)S(1)} collective-permute-done((bf16[512,128]{1,0:T(8,128)(2,1)S(1)}, bf16[512,128]{1,0:T(8,128)(2,1)S(1)}, u32[]{:S(2)}, u32[]{:S(2)}) %collective-permute-start.9) | collective-permute-done | bytes 131104 | tf_op jit(solution)/shard_map/ppermute | solution.py:62
  39.8 13.1 %sequence.1 = (bf16[512,512]{1,0:T(8,128)(2,1)}, bf16[512,128]{1,0:T(8,128)(2,1)S(1)}, bf16[512,128]{1,0:T(8,128)(2,1)S(1)}, bf16[512,128]{1,0:T(8,128)(2,1)S(1)...) custom-call(s32[1]{0:T(128)} %bitcast.r_ref, ...), custom_call_target="tpu_custom_call" | custom-call | flops 4294967296 | bytes 9177096 | tf_op jit(solution)/shard_map/sequence/pallas_call | solution.py:36
  53.0 1.2 %collective-permute-start.11 = (bf16[512,128]{1,0:T(8,128)(2,1)S(1)}, bf16[512,128]{1,0:T(8,128)(2,1)S(1)}, u32[]{:S(2)}, u32[]{:S(2)}) collective-permute-start(bf16[512,128]{1,0:T(8,128)(2,1)S(1)} %get-tuple-element.66), channel_id=1, source_target_pairs={{0,8},{8,0},{16,24},{24,16},{1,9},{9,1},{17,25},{25,17},{2,10},{10... | collective-permute-start | bytes 393224 | tf_op jit(solution)/shard_map/ppermute | solution.py:62
  54.2 0.8 collective-permute-start.12
  55.0 1.4 %collective-permute-start.13 = (bf16[512,128]{1,0:T(8,128)(2,1)S(1)}, bf16[512,128]{1,0:T(8,128)(2,1)S(1)}, u32[]{:S(2)}, u32[]{:S(2)}) collective-permute-start(bf16[512,128]{1,0:T(8,128)(2,1)S(1)} %get-tuple-element.68), channel_id=1, source_target_pairs={{0,24},{8,16},{16,8},{24,0},{1,25},{9,17},{17,9},{25,1},{2,26},{10... | collective-permute-start | bytes 393224 | tf_op jit(solution)/shard_map/ppermute | solution.py:62
  56.5 1.7 %weight_grad.1 = (f32[2,128,640]{2,1,0:T(8,128)S(1)}, bf16[2,128,640]{2,1,0:T(8,128)(2,1)S(1)}, f32[2,128,640]{2,1,0:T(8,128)S(1)}, bf16[2,128,640]{2,1,0:T(8,128)(2,1)S(1)}) custom-call(s32[1]{0:T(128)} %bitcast.r_ref, s32[1]{0:T(128)} %bitcast.1.core_ref, bf16[512,512]{1,0:T(8,128)(2,1)S(1)} %get-tuple-element.69.n_ref, ...), custom_call_target="tpu_custom_call" | custom-call | flops 939524096 | bytes 6946824 | tf_op jit(solution)/shard_map/weight_grad/pallas_call | solution.py:36
  58.2 1.1 %collective-permute-done.11.refs_1_ = bf16[512,128]{1,0:T(8,128)(2,1)S(1)} collective-permute-done((bf16[512,128]{1,0:T(8,128)(2,1)S(1)}, bf16[512,128]{1,0:T(8,128)(2,1)S(1)}, u32[]{:S(2)}, u32[]{:S(2)}) %collective-permute-start.11) | collective-permute-done | bytes 131104 | tf_op jit(solution)/shard_map/ppermute | solution.py:62
  59.3 1.7 %collective-permute-done.12.refs_2_ = bf16[512,128]{1,0:T(8,128)(2,1)S(1)} collective-permute-done((bf16[512,128]{1,0:T(8,128)(2,1)S(1)}, bf16[512,128]{1,0:T(8,128)(2,1)S(1)}, u32[]{:S(2)}, u32[]{:S(2)}) %collective-permute-start.12) | collective-permute-done | bytes 131104 | tf_op jit(solution)/shard_map/ppermute | solution.py:62
  61.0 1.6 %collective-permute-done.13.refs_3_ = bf16[512,128]{1,0:T(8,128)(2,1)S(1)} collective-permute-done((bf16[512,128]{1,0:T(8,128)(2,1)S(1)}, bf16[512,128]{1,0:T(8,128)(2,1)S(1)}, u32[]{:S(2)}, u32[]{:S(2)}) %collective-permute-start.13) | collective-permute-done | bytes 131104 | tf_op jit(solution)/shard_map/ppermute | solution.py:62
  62.7 0.1 collective-permute-start.15
  62.8 0.9 collective-permute-start.19
  63.6 1.5 %collective-permute-start.20 = (bf16[2,128,640]{2,1,0:T(8,128)(2,1)S(1)}, bf16[2,128,640]{2,1,0:T(8,128)(2,1)S(1)}, u32[]{:S(2)}, u32[]{:S(2)}) collective-permute-start(bf16[2,128,640]{2,1,0:T(8,128)(2,1)S(1)} %get-tuple-element.76), channel_id=1, source_target_pairs={{0,16},{8,24},{16,0},{24,8},{1,17},{9,25},{17,1},{25,9},{2,18},{10... | collective-permute-start | bytes 983048 | tf_op jit(solution)/shard_map/ppermute | solution.py:62
  65.1 1.2 %gather_grad.5.refs_1_ = bf16[1024,128]{1,0:T(8,128)(2,1)S(1)} custom-call(s32[1]{0:T(128)S(6)} %mul.35.base_ref, s32[4,2,2,512]{3,2,1,0:T(2,128)S(1)} %pad_add_fusion.key_ref, bf16[4,512,128]{2,1,0:T(8,128)(2,1)S(1)} %pack.1.refs_0_), custom_call_target="tpu_custom_call" | custom-call | flops 1073741824 | bytes 819204 | tf_op jit(solution)/shard_map/gather_grad/pallas_call | solution.py:36
  66.4 1.2 %gather_grad.6 = bf16[1024,128]{1,0:T(8,128)(2,1)S(1)} custom-call(s32[1]{0:T(128)S(6)} %mul.35.base_ref, s32[4,2,2,512]{3,2,1,0:T(2,128)S(1)} %pad_add_fusion.key_ref, bf16[4,512,128]{2,1,0:T(8,128)(2,1)S(1)} %collective-permute-done.15.refs_0_.refs_1_, bf16[1024,128]{1,0:T(8,128)(2,1)S(1)} %gather_grad.5.refs_1_), custom_call_target="tpu_custom_call" | custom-call | flops 1073741824 | bytes 1081348 | tf_op jit(solution)/shard_map/gather_grad/pallas_call | solution.py:36
  67.6 1.5 %collective-permute-start.16 = (bf16[1024,128]{1,0:T(8,128)(2,1)S(1)}, bf16[1024,128]{1,0:T(8,128)(2,1)S(1)}, u32[]{:S(2)}, u32[]{:S(2)}) collective-permute-start(bf16[1024,128]{1,0:T(8,128)(2,1)S(1)} %gather_grad.6), channel_id=1, source_target_pairs={{0,2},{1,3},{2,0},{3,1},{4,6},{5,7},{6,4},{7,5},{8,10},{9,11},{10,... | collective-permute-start | bytes 786440 | tf_op jit(solution)/shard_map/ppermute | solution.py:66
  69.1 2.6 %gather_grad.9 = bf16[1024,128]{1,0:T(8,128)(2,1)S(1)} custom-call(s32[1]{0:T(128)S(6)} %mul.42.base_ref, s32[4,2,2,512]{3,2,1,0:T(2,128)S(1)} %pad_add_fusion.key_ref, bf16[4,512,128]{2,1,0:T(8,128)(2,1)S(1)} %pack.1.refs_0_, bf16[4,512,128]{2,1,0:T(8,128)(2,1)S(1)} %collective-permute-done.15.refs_0_.refs_1_), custom_call_target="tpu_custom_call" | custom-call | flops 2147483648 | bytes 1343492 | tf_op jit(solution)/shard_map/gather_grad/pallas_call | solution.py:36
  71.7 0.7 collective-permute-start.17
  72.3 2.3 %gather_grad.7.refs_0_ = f32[1024,128]{1,0:T(8,128)S(1)} custom-call(s32[1]{0:T(128)S(6)} %mul.40.base_ref, s32[4,2,2,512]{3,2,1,0:T(2,128)S(1)} %pad_add_fusion.key_ref, bf16[4,512,128]{2,1,0:T(8,128)(2,1)S(1)} %pack.1.refs_0_, bf16[4,512,128]{2,1,0:T(8,128)(2,1)S(1)} %collective-permute-done.15.refs_0_.refs_1_), custom_call_target="tpu_custom_call" | custom-call | flops 2147483648 | bytes 1605636 | tf_op jit(solution)/shard_map/gather_grad/pallas_call | solution.py:36
  74.7 0.3 fold.1
  74.9 0.6 collective-permute-start.21
  75.5 1.2 %collective-permute-start.22 = (bf16[1,128,640]{2,1,0:T(8,128)(2,1)S(1)}, bf16[1,128,640]{2,1,0:T(8,128)(2,1)S(1)}, u32[]{:S(2)}, u32[]{:S(2)}) collective-permute-start(bf16[1,128,640]{2,1,0:T(8,128)(2,1)S(1)} %get-tuple-element.92), channel_id=1, source_target_pairs={{0,8},{8,0},{16,24},{24,16},{1,9},{9,1},{17,25},{25,17},{2,10},{10... | collective-permute-start | bytes 491528 | tf_op jit(solution)/shard_map/ppermute | solution.py:62
  76.8 0.1 collective-permute-done.16.refs_1_
  76.9 3.5 %collective-permute-start.18 = (bf16[1024,128]{1,0:T(8,128)(2,1)S(1)}, bf16[1024,128]{1,0:T(8,128)(2,1)S(1)}, u32[]{:S(2)}, u32[]{:S(2)}) collective-permute-start(bf16[1024,128]{1,0:T(8,128)(2,1)S(1)} %add_up.2), channel_id=1, source_target_pairs={{0,4},{1,5},{2,6},{3,7},{4,0},{5,1},{6,2},{7,3},{8,12},{9,13},{10,... | collective-permute-start | bytes 786440 | tf_op jit(solution)/shard_map/ppermute | solution.py:66
  80.5 0.4 collective-permute-done.22.refs_3_
  80.8 5.0 %collective-permute-done.17.came_ref = bf16[1024,128]{1,0:T(8,128)(2,1)S(1)} collective-permute-done((bf16[1024,128]{1,0:T(8,128)(2,1)S(1)}, bf16[1024,128]{1,0:T(8,128)(2,1)S(1)}, u32[]{:S(2)}, u32[]{:S(2)}) %collective-permute-start.17) | collective-permute-done | bytes 262176 | tf_op jit(solution)/shard_map/ppermute | solution.py:66
  85.8 0.1 cut_line.1
  85.9 0.1 collective-permute-start.23
  86.0 2.3 %gather_grad.8.here_ref = f32[1024,128]{1,0:T(8,128)S(1)} custom-call(s32[1]{0:T(128)S(6)} %mul.44.base_ref, s32[4,2,2,512]{3,2,1,0:T(2,128)S(1)} %pad_add_fusion.key_ref, bf16[4,512,128]{2,1,0:T(8,128)(2,1)S(1)} %pack.1.refs_0_, bf16[4,512,128]{2,1,0:T(8,128)(2,1)S(1)} %collective-permute-done.15.refs_0_.refs_1_), custom_call_target="tpu_custom_call" | custom-call | flops 2147483648 | bytes 1605636 | tf_op jit(solution)/shard_map/gather_grad/pallas_call | solution.py:36
  88.4 0.1 table_sums.2.here_ref
  88.4 3.8 %collective-permute-done.23.came_ref = bf16[2,64,640]{2,1,0:T(8,128)(2,1)S(1)} collective-permute-done((bf16[2,64,640]{2,1,0:T(8,128)(2,1)S(1)}, bf16[2,64,640]{2,1,0:T(8,128)(2,1)S(1)}, u32[]{:S(2)}, u32[]{:S(2)}) %collective-permute-start.23) | collective-permute-done | bytes 163872 | tf_op jit(solution)/shard_map/ppermute | solution.py:66
  92.3 1.9 %collective-permute-start.24 = (bf16[1,64,640]{2,1,0:T(8,128)(2,1)S(1)}, bf16[1,64,640]{2,1,0:T(8,128)(2,1)S(1)}, u32[]{:S(2)}, u32[]{:S(2)}) collective-permute-start(bf16[1,64,640]{2,1,0:T(8,128)(2,1)S(1)} %get-tuple-element.98), channel_id=1, source_target_pairs={{0,4},{1,5},{2,6},{3,7},{4,0},{5,1},{6,2},{7,3},{8,12},{9,13},{10,... | collective-permute-start | bytes 245768 | tf_op jit(solution)/shard_map/ppermute | solution.py:66
  94.1 0.8 table_sums.3
  95.0 3.6 %collective-permute-done.24 = bf16[1,64,640]{2,1,0:T(8,128)(2,1)S(1)} collective-permute-done((bf16[1,64,640]{2,1,0:T(8,128)(2,1)S(1)}, bf16[1,64,640]{2,1,0:T(8,128)(2,1)S(1)}, u32[]{:S(2)}, u32[]{:S(2)}) %collective-permute-start.24) | collective-permute-done | bytes 81952 | tf_op jit(solution)/shard_map/ppermute | solution.py:66
  98.6 1.9 %collective-permute-start.27 = (bf16[64,640]{1,0:T(8,128)(2,1)S(1)}, bf16[64,640]{1,0:T(8,128)(2,1)S(1)}, u32[]{:S(2)}, u32[]{:S(2)}) collective-permute-start(bf16[64,640]{1,0:T(8,128)(2,1)S(1)} %add_up.3.refs_0_), channel_id=1, source_target_pairs={{0,24},{8,16},{16,8},{24,0},{1,25},{9,17},{17,9},{25,1},{2,26},{10... | collective-permute-start | bytes 245768 | tf_op jit(solution)/shard_map/ppermute | solution.py:62
  100.5 0.3 collective-permute-start.26
  100.8 1.4 %collective-permute-start.25 = (bf16[64,640]{1,0:T(8,128)(2,1)S(1)}, bf16[64,640]{1,0:T(8,128)(2,1)S(1)}, u32[]{:S(2)}, u32[]{:S(2)}) collective-permute-start(bf16[64,640]{1,0:T(8,128)(2,1)S(1)} %add_up.3.refs_0_), channel_id=1, source_target_pairs={{0,8},{8,0},{16,24},{24,16},{1,9},{9,1},{17,25},{25,17},{2,10},{10... | collective-permute-start | bytes 245768 | tf_op jit(solution)/shard_map/ppermute | solution.py:62
  102.2 1.9 %collective-permute-done.27.refs_3_ = bf16[64,640]{1,0:T(8,128)(2,1)S(1)} collective-permute-done((bf16[64,640]{1,0:T(8,128)(2,1)S(1)}, bf16[64,640]{1,0:T(8,128)(2,1)S(1)}, u32[]{:S(2)}, u32[]{:S(2)}) %collective-permute-start.27) | collective-permute-done | bytes 81952 | tf_op jit(solution)/shard_map/ppermute | solution.py:62
  104.0 0.9 collective-permute-done.26.refs_2_
  104.9 0.3 collective-permute-done.25.refs_1_
  105.2 0.9 assemble.1
  (29 shorter events, 0.2 us)
Async XLA Ops:
  1.7 16.1 %collective-permute-start = (bf16[1024,128]{1,0:T(8,128)(2,1)S(1)}, bf16[1024,128]{1,0:T(8,128)(2,1)S(1)}, u32[]{:S(2)}, u32[]{:S(2)}) collective-permute-start(bf16[1024,128]{1,0:T(8,128)(2,1)S(1)} %pad_maximum_fusion.chunk_ref), channel_id=1, source_target_pairs={{0,4},{1,5},{2,6},{3,7},{4,0},{5,1},{6,2},{7,3},{8,12},{9,13},{10,... | collective-permute-start | bytes 786440 | tf_op jit(solution)/shard_map/ppermute | solution.py:66
  6.5 1.7 %collective-permute-start.2 = (s32[2,512]{1,0:T(2,128)S(1)}, s32[2,512]{1,0:T(2,128)S(1)}, u32[]{:S(2)}, u32[]{:S(2)}) collective-permute-start(s32[2,512]{1,0:T(2,128)S(1)} %get-tuple-element.106), channel_id=1, source_target_pairs={{0,1},{1,0},{2,3},{3,2},{4,5},{5,4},{6,7},{7,6},{8,9},{9,8},{10,11... | collective-permute-start | bytes 12296 | tf_op jit(solution)/shard_map/ppermute | solution.py:69
  6.6 15.5 %collective-permute-start.6 = (bf16[1024,128]{1,0:T(8,128)(2,1)S(1)}, bf16[1024,128]{1,0:T(8,128)(2,1)S(1)}, u32[]{:S(2)}, u32[]{:S(2)}) collective-permute-start(bf16[1024,128]{1,0:T(8,128)(2,1)S(1)} %pad_maximum_fusion.chunk_ref), channel_id=1, source_target_pairs={{0,2},{1,3},{2,0},{3,1},{4,6},{5,7},{6,4},{7,5},{8,10},{9,11},{10,... | collective-permute-start | bytes 786440 | tf_op jit(solution)/shard_map/ppermute | solution.py:66
  8.2 10.2 %collective-permute-start.4 = (s32[2,2,512]{2,1,0:T(2,128)S(1)}, s32[2,2,512]{2,1,0:T(2,128)S(1)}, u32[]{:S(2)}, u32[]{:S(2)}) collective-permute-start(s32[2,2,512]{2,1,0:T(2,128)S(1)} %get-tuple-element.104), channel_id=1, source_target_pairs={{0,16},{8,24},{16,0},{24,8},{1,17},{9,25},{17,1},{25,9},{2,18},{10... | collective-permute-start | bytes 24584 | tf_op jit(solution)/shard_map/ppermute | solution.py:62
  9.8 8.6 %collective-permute-start.3 = (s32[2,2,512]{2,1,0:T(2,128)S(1)}, s32[2,2,512]{2,1,0:T(2,128)S(1)}, u32[]{:S(2)}, u32[]{:S(2)}) collective-permute-start(s32[2,2,512]{2,1,0:T(2,128)S(1)} %get-tuple-element.104), channel_id=1, source_target_pairs={{0,8},{8,0},{16,24},{24,16},{1,9},{9,1},{17,25},{25,17},{2,10},{10... | collective-permute-start | bytes 24584 | tf_op jit(solution)/shard_map/ppermute | solution.py:62
  11.3 7.1 %collective-permute-start.5 = (s32[2,2,512]{2,1,0:T(2,128)S(1)}, s32[2,2,512]{2,1,0:T(2,128)S(1)}, u32[]{:S(2)}, u32[]{:S(2)}) collective-permute-start(s32[2,2,512]{2,1,0:T(2,128)S(1)} %get-tuple-element.104), channel_id=1, source_target_pairs={{0,24},{8,16},{16,8},{24,0},{1,25},{9,17},{17,9},{25,1},{2,26},{10... | collective-permute-start | bytes 24584 | tf_op jit(solution)/shard_map/ppermute | solution.py:62
  17.8 9.0 %collective-permute-start.1 = (bf16[1024,128]{1,0:T(8,128)(2,1)S(1)}, bf16[1024,128]{1,0:T(8,128)(2,1)S(1)}, u32[]{:S(2)}, u32[]{:S(2)}) collective-permute-start(bf16[1024,128]{1,0:T(8,128)(2,1)S(1)} %collective-permute-done.chunk_ref), channel_id=1, source_target_pairs={{0,2},{1,3},{2,0},{3,1},{4,6},{5,7},{6,4},{7,5},{8,10},{9,11},{10,... | collective-permute-start | bytes 786440 | tf_op jit(solution)/shard_map/ppermute | solution.py:66
  28.0 2.0 %collective-permute-start.7 = (bf16[4,512,128]{2,1,0:T(8,128)(2,1)S(1)}, bf16[4,512,128]{2,1,0:T(8,128)(2,1)S(1)}, u32[]{:S(2)}, u32[]{:S(2)}) collective-permute-start(bf16[4,512,128]{2,1,0:T(8,128)(2,1)S(1)} %fetch.9), channel_id=1, source_target_pairs={{0,1},{1,0},{2,3},{3,2},{4,5},{5,4},{6,7},{7,6},{8,9},{9,8},{10,11... | collective-permute-start | bytes 1572872 | tf_op jit(solution)/shard_map/ppermute | solution.py:69
  28.1 11.7 %copy-start = (bf16[512,512]{1,0:T(8,128)(2,1)S(1)}, bf16[512,512]{1,0:T(8,128)(2,1)}, u32[]{:S(2)}) copy-start(bf16[512,512]{1,0:T(8,128)(2,1)} %c_ref.1) | copy-start | bytes 1572868
  28.1 11.7 %copy-start.1 = (bf16[512,2048]{1,0:T(8,128)(2,1)S(1)}, bf16[512,2048]{1,0:T(8,128)(2,1)}, u32[]{:S(2)}) copy-start(bf16[512,2048]{1,0:T(8,128)(2,1)} %wp_ref.1) | copy-start | bytes 6291460
  28.1 11.7 %copy-start.2 = (bf16[512,512]{1,0:T(8,128)(2,1)S(1)}, bf16[512,512]{1,0:T(8,128)(2,1)}, u32[]{:S(2)}) copy-start(bf16[512,512]{1,0:T(8,128)(2,1)} %wo_ref.1) | copy-start | bytes 1572868
  28.1 11.7 %copy-start.3 = (f32[512]{0:T(512)S(1)}, f32[512]{0:T(512)}, u32[]{:S(2)}) copy-start(f32[512]{0:T(512)} %param.16) | copy-start | bytes 6148
  30.1 5.9 %collective-permute-start.8 = (bf16[512,128]{1,0:T(8,128)(2,1)S(1)}, bf16[512,128]{1,0:T(8,128)(2,1)S(1)}, u32[]{:S(2)}, u32[]{:S(2)}) collective-permute-start(bf16[512,128]{1,0:T(8,128)(2,1)S(1)} %get-tuple-element.61), channel_id=1, source_target_pairs={{0,8},{8,0},{16,24},{24,16},{1,9},{9,1},{17,25},{25,17},{2,10},{10... | collective-permute-start | bytes 393224 | tf_op jit(solution)/shard_map/ppermute | solution.py:62
  31.7 8.1 %collective-permute-start.9 = (bf16[512,128]{1,0:T(8,128)(2,1)S(1)}, bf16[512,128]{1,0:T(8,128)(2,1)S(1)}, u32[]{:S(2)}, u32[]{:S(2)}) collective-permute-start(bf16[512,128]{1,0:T(8,128)(2,1)S(1)} %get-tuple-element.62), channel_id=1, source_target_pairs={{0,16},{8,24},{16,0},{24,8},{1,17},{9,25},{17,1},{25,9},{2,18},{10... | collective-permute-start | bytes 393224 | tf_op jit(solution)/shard_map/ppermute | solution.py:62
  33.2 6.6 %collective-permute-start.10 = (bf16[512,128]{1,0:T(8,128)(2,1)S(1)}, bf16[512,128]{1,0:T(8,128)(2,1)S(1)}, u32[]{:S(2)}, u32[]{:S(2)}) collective-permute-start(bf16[512,128]{1,0:T(8,128)(2,1)S(1)} %get-tuple-element.63), channel_id=1, source_target_pairs={{0,24},{8,16},{16,8},{24,0},{1,25},{9,17},{17,9},{25,1},{2,26},{10... | collective-permute-start | bytes 393224 | tf_op jit(solution)/shard_map/ppermute | solution.py:62
  53.0 3.5 %collective-permute-start.14 = (bf16[4,256,640]{2,1,0:T(8,128)(2,1)S(1)}, bf16[4,256,640]{2,1,0:T(8,128)(2,1)S(1)}, u32[]{:S(2)}, u32[]{:S(2)}) collective-permute-start(bf16[4,256,640]{2,1,0:T(8,128)(2,1)S(1)} %get-tuple-element.72), channel_id=1, source_target_pairs={{0,1},{1,0},{2,3},{3,2},{4,5},{5,4},{6,7},{7,6},{8,9},{9,8},{10,11... | collective-permute-start | bytes 3932168 | tf_op jit(solution)/shard_map/ppermute | solution.py:69
  53.0 6.3 %collective-permute-start.11 = (bf16[512,128]{1,0:T(8,128)(2,1)S(1)}, bf16[512,128]{1,0:T(8,128)(2,1)S(1)}, u32[]{:S(2)}, u32[]{:S(2)}) collective-permute-start(bf16[512,128]{1,0:T(8,128)(2,1)S(1)} %get-tuple-element.66), channel_id=1, source_target_pairs={{0,8},{8,0},{16,24},{24,16},{1,9},{9,1},{17,25},{25,17},{2,10},{10... | collective-permute-start | bytes 393224 | tf_op jit(solution)/shard_map/ppermute | solution.py:62
  54.2 6.8 %collective-permute-start.12 = (bf16[512,128]{1,0:T(8,128)(2,1)S(1)}, bf16[512,128]{1,0:T(8,128)(2,1)S(1)}, u32[]{:S(2)}, u32[]{:S(2)}) collective-permute-start(bf16[512,128]{1,0:T(8,128)(2,1)S(1)} %get-tuple-element.67), channel_id=1, source_target_pairs={{0,16},{8,24},{16,0},{24,8},{1,17},{9,25},{17,1},{25,9},{2,18},{10... | collective-permute-start | bytes 393224 | tf_op jit(solution)/shard_map/ppermute | solution.py:62
  55.0 7.6 %collective-permute-start.13 = (bf16[512,128]{1,0:T(8,128)(2,1)S(1)}, bf16[512,128]{1,0:T(8,128)(2,1)S(1)}, u32[]{:S(2)}, u32[]{:S(2)}) collective-permute-start(bf16[512,128]{1,0:T(8,128)(2,1)S(1)} %get-tuple-element.68), channel_id=1, source_target_pairs={{0,24},{8,16},{16,8},{24,0},{1,25},{9,17},{17,9},{25,1},{2,26},{10... | collective-permute-start | bytes 393224 | tf_op jit(solution)/shard_map/ppermute | solution.py:62
  62.7 3.7 %collective-permute-start.15 = (bf16[4,512,128]{2,1,0:T(8,128)(2,1)S(1)}, bf16[4,512,128]{2,1,0:T(8,128)(2,1)S(1)}, u32[]{:S(2)}, u32[]{:S(2)}) collective-permute-start(bf16[4,512,128]{2,1,0:T(8,128)(2,1)S(1)} %pack.1.refs_0_), channel_id=1, source_target_pairs={{0,1},{1,0},{2,3},{3,2},{4,5},{5,4},{6,7},{7,6},{8,9},{9,8},{10,11... | collective-permute-start | bytes 1572872 | tf_op jit(solution)/shard_map/ppermute | solution.py:69
  62.8 11.9 %collective-permute-start.19 = (bf16[2,128,640]{2,1,0:T(8,128)(2,1)S(1)}, bf16[2,128,640]{2,1,0:T(8,128)(2,1)S(1)}, u32[]{:S(2)}, u32[]{:S(2)}) collective-permute-start(bf16[2,128,640]{2,1,0:T(8,128)(2,1)S(1)} %get-tuple-element.74), channel_id=1, source_target_pairs={{0,8},{8,0},{16,24},{24,16},{1,9},{9,1},{17,25},{25,17},{2,10},{10... | collective-permute-start | bytes 983048 | tf_op jit(solution)/shard_map/ppermute | solution.py:62
  63.6 11.1 %collective-permute-start.20 = (bf16[2,128,640]{2,1,0:T(8,128)(2,1)S(1)}, bf16[2,128,640]{2,1,0:T(8,128)(2,1)S(1)}, u32[]{:S(2)}, u32[]{:S(2)}) collective-permute-start(bf16[2,128,640]{2,1,0:T(8,128)(2,1)S(1)} %get-tuple-element.76), channel_id=1, source_target_pairs={{0,16},{8,24},{16,0},{24,8},{1,17},{9,25},{17,1},{25,9},{2,18},{10... | collective-permute-start | bytes 983048 | tf_op jit(solution)/shard_map/ppermute | solution.py:62
  67.6 9.3 %collective-permute-start.16 = (bf16[1024,128]{1,0:T(8,128)(2,1)S(1)}, bf16[1024,128]{1,0:T(8,128)(2,1)S(1)}, u32[]{:S(2)}, u32[]{:S(2)}) collective-permute-start(bf16[1024,128]{1,0:T(8,128)(2,1)S(1)} %gather_grad.6), channel_id=1, source_target_pairs={{0,2},{1,3},{2,0},{3,1},{4,6},{5,7},{6,4},{7,5},{8,10},{9,11},{10,... | collective-permute-start | bytes 786440 | tf_op jit(solution)/shard_map/ppermute | solution.py:66
  71.7 14.2 %collective-permute-start.17 = (bf16[1024,128]{1,0:T(8,128)(2,1)S(1)}, bf16[1024,128]{1,0:T(8,128)(2,1)S(1)}, u32[]{:S(2)}, u32[]{:S(2)}) collective-permute-start(bf16[1024,128]{1,0:T(8,128)(2,1)S(1)} %gather_grad.9), channel_id=1, source_target_pairs={{0,2},{1,3},{2,0},{3,1},{4,6},{5,7},{6,4},{7,5},{8,10},{9,11},{10,... | collective-permute-start | bytes 786440 | tf_op jit(solution)/shard_map/ppermute | solution.py:66
  74.9 5.5 %collective-permute-start.21 = (bf16[1,128,640]{2,1,0:T(8,128)(2,1)S(1)}, bf16[1,128,640]{2,1,0:T(8,128)(2,1)S(1)}, u32[]{:S(2)}, u32[]{:S(2)}) collective-permute-start(bf16[1,128,640]{2,1,0:T(8,128)(2,1)S(1)} %get-tuple-element.91), channel_id=1, source_target_pairs={{0,16},{8,24},{16,0},{24,8},{1,17},{9,25},{17,1},{25,9},{2,18},{10... | collective-permute-start | bytes 491528 | tf_op jit(solution)/shard_map/ppermute | solution.py:62
  75.5 5.3 %collective-permute-start.22 = (bf16[1,128,640]{2,1,0:T(8,128)(2,1)S(1)}, bf16[1,128,640]{2,1,0:T(8,128)(2,1)S(1)}, u32[]{:S(2)}, u32[]{:S(2)}) collective-permute-start(bf16[1,128,640]{2,1,0:T(8,128)(2,1)S(1)} %get-tuple-element.92), channel_id=1, source_target_pairs={{0,8},{8,0},{16,24},{24,16},{1,9},{9,1},{17,25},{25,17},{2,10},{10... | collective-permute-start | bytes 491528 | tf_op jit(solution)/shard_map/ppermute | solution.py:62
  76.9 17.2 %collective-permute-start.18 = (bf16[1024,128]{1,0:T(8,128)(2,1)S(1)}, bf16[1024,128]{1,0:T(8,128)(2,1)S(1)}, u32[]{:S(2)}, u32[]{:S(2)}) collective-permute-start(bf16[1024,128]{1,0:T(8,128)(2,1)S(1)} %add_up.2), channel_id=1, source_target_pairs={{0,4},{1,5},{2,6},{3,7},{4,0},{5,1},{6,2},{7,3},{8,12},{9,13},{10,... | collective-permute-start | bytes 786440 | tf_op jit(solution)/shard_map/ppermute | solution.py:66
  85.9 6.3 %collective-permute-start.23 = (bf16[2,64,640]{2,1,0:T(8,128)(2,1)S(1)}, bf16[2,64,640]{2,1,0:T(8,128)(2,1)S(1)}, u32[]{:S(2)}, u32[]{:S(2)}) collective-permute-start(bf16[2,64,640]{2,1,0:T(8,128)(2,1)S(1)} %get-tuple-element.96), channel_id=1, source_target_pairs={{0,2},{1,3},{2,0},{3,1},{4,6},{5,7},{6,4},{7,5},{8,10},{9,11},{10,... | collective-permute-start | bytes 491528 | tf_op jit(solution)/shard_map/ppermute | solution.py:66
  92.3 6.3 %collective-permute-start.24 = (bf16[1,64,640]{2,1,0:T(8,128)(2,1)S(1)}, bf16[1,64,640]{2,1,0:T(8,128)(2,1)S(1)}, u32[]{:S(2)}, u32[]{:S(2)}) collective-permute-start(bf16[1,64,640]{2,1,0:T(8,128)(2,1)S(1)} %get-tuple-element.98), channel_id=1, source_target_pairs={{0,4},{1,5},{2,6},{3,7},{4,0},{5,1},{6,2},{7,3},{8,12},{9,13},{10,... | collective-permute-start | bytes 245768 | tf_op jit(solution)/shard_map/ppermute | solution.py:66
  98.6 5.4 %collective-permute-start.27 = (bf16[64,640]{1,0:T(8,128)(2,1)S(1)}, bf16[64,640]{1,0:T(8,128)(2,1)S(1)}, u32[]{:S(2)}, u32[]{:S(2)}) collective-permute-start(bf16[64,640]{1,0:T(8,128)(2,1)S(1)} %add_up.3.refs_0_), channel_id=1, source_target_pairs={{0,24},{8,16},{16,8},{24,0},{1,25},{9,17},{17,9},{25,1},{2,26},{10... | collective-permute-start | bytes 245768 | tf_op jit(solution)/shard_map/ppermute | solution.py:62
  100.5 4.4 %collective-permute-start.26 = (bf16[64,640]{1,0:T(8,128)(2,1)S(1)}, bf16[64,640]{1,0:T(8,128)(2,1)S(1)}, u32[]{:S(2)}, u32[]{:S(2)}) collective-permute-start(bf16[64,640]{1,0:T(8,128)(2,1)S(1)} %add_up.3.refs_0_), channel_id=1, source_target_pairs={{0,16},{8,24},{16,0},{24,8},{1,17},{9,25},{17,1},{25,9},{2,18},{10... | collective-permute-start | bytes 245768 | tf_op jit(solution)/shard_map/ppermute | solution.py:62
  100.8 4.4 %collective-permute-start.25 = (bf16[64,640]{1,0:T(8,128)(2,1)S(1)}, bf16[64,640]{1,0:T(8,128)(2,1)S(1)}, u32[]{:S(2)}, u32[]{:S(2)}) collective-permute-start(bf16[64,640]{1,0:T(8,128)(2,1)S(1)} %add_up.3.refs_0_), channel_id=1, source_target_pairs={{0,8},{8,0},{16,24},{24,16},{1,9},{9,1},{17,25},{25,17},{2,10},{10... | collective-permute-start | bytes 245768 | tf_op jit(solution)/shard_map/ppermute | solution.py:62

commit v11 on v10

--- a/solution.py
+++ b/solution.py
@@ -13,6 +13,7 @@
 I32 = jnp.int32
 MIB = 1024 * 1024
 EARLY = 6 * 10**9
+LATE = 40 * 10**9
 
 NN = ((1,), (0,))
 NT = ((1,), (1,))
@@ -116,7 +117,7 @@
             refs[-1][k] = ref[...]
 
     shape, dtype = parts[0].shape, parts[0].dtype
-    return run("pack", body, [((len(parts), *shape), dtype)], parts)[0]
+    return run("pack", body, [((len(parts), *shape), dtype)], parts, flops=LATE)[0]
 
 
 def add_up(parts):
@@ -522,15 +523,13 @@
 
     weights = grid.over_pair(weights)
     weights = weight_grad(replica, core, normed, dproj, gated, cotangent, weights, line)
-    tokens = lax.optimization_barrier((tokens, weights))[0]
-    tokens = pack(tokens)
-    there = grid.over_pair(tokens)
-
     def swap_weights(weights, step):
         kept, sent = weights[0::2], weights[1::2]
         return kept, [grid.over_replica(sent[p], 1 << (p + step) % bits) for p in range(bits)]
 
     kept, swapped = swap_weights(weights, 0)
+    tokens = lax.optimization_barrier((pack(tokens), swapped))[0]
+    there = grid.over_pair(tokens)
 
     sums, raw, both_there = {}, {}, [tokens, there]
     for k in reversed(order):
@@ -547,7 +546,7 @@
             raw[k] = gather_grad(bases[k], keys, both, both_there, rows, out=out)
         came = [grid.over_line(sums[k ^ step], step) for step in steps]
         if k == 0:
-            near, table = came[0], raw[k][0]
+            table = raw[k][0]
             for part in came[:-1]:
                 table = table_sums(table, part, 1)[0]
             item_grad, action_grad = table_sums(table, came[-1], 2)
@@ -555,17 +554,17 @@
             sums[k] = add_up(raw[k] + came) if steps else raw[k][0]
 
     for step in range(1, bits + 1):
-        after = [raw[1], raw[line // 2]] if step < bits else [near, sums[line // 2]]
-        swapped = lax.optimization_barrier((swapped, after))[0]
         if step < bits:
             kept, swapped = swap_weights(fold(replica, kept, swapped, step), step)
+    swapped = lax.optimization_barrier((swapped, raw[1]))[0]
     kept, sent = cut_line(place, kept, swapped, line)
     step = 1
     while step < line // 2:
-        kept, sent = fold_line(kept, grid.over_line(sent, step))
+        came = lax.optimization_barrier((grid.over_line(sent, step), sums[line // 2]))[0]
+        kept, sent = fold_line(kept, came)
         step *= 2
     parts = [kept[0], grid.over_line(sent, step)[0]]
-    parts = lax.optimization_barrier((parts, item_grad))[0]
+    parts = lax.optimization_barrier((parts, raw[0]))[0]
     total = add_up(parts)
     parts = [total] + [grid.over_replica(total, k) for k in range(1, replicas)]
     grad_proj, grad_out = assemble(replica, parts, 4 * width)

time: 106 us -> 113 us (1.066)
  waiting for transfers between devices: 33.1 us -> 38.4 us
    ppermute x16, waiting for transfers between devices: 14 us -> 18.3 us  [over_replica(): return lax.ppermute(value, 'replica', [(i, i ^ step) for i in range(n)])]
  transfers between devices with their start and end apart: 28 -> 28, of which waited for: 15 -> 14; matrix products, arithmetic and copies ran while one was open for 2% -> 2% of each run, Pallas kernels for 20% -> 19%
where the time goes in v11:
time: 113 us; the launch traced here: 112 us
  waiting for transfers between devices  38.4 us (34%)
  Pallas kernels  36.4 us (32%)
  starting transfers between devices  33.7 us (30%)
  local copies, waits for them, and re-layouts  2.25 us (2%)
    pallas_call x22, Pallas kernels, run(): pl.pallas_call(body, out_shape=outs, in_specs=places, out_specs=[in_vmem]...  36.4 us
    ppermute x8, waiting for transfers between devices, over_line(): return lax.ppermute(value, 'sparse', pairs)  19.5 us
    ppermute x16, starting transfers between devices, over_replica(): return lax.ppermute(value, 'replica', [(i, i ^ step) for i in range(n)])  18.7 us
    ppermute x16, waiting for transfers between devices, over_replica(): return lax.ppermute(value, 'replica', [(i, i ^ step) for i in range(n)])  18.3 us
    ppermute x8, starting transfers between devices, over_line(): return lax.ppermute(value, 'sparse', pairs)  14.9 us
  transfers between devices with their start and end apart: 28, of which 14 were waited for; matrix products, arithmetic and copies ran while one was open for 2% of the time, Pallas kernels for 19%

profile of v11, /device:TPU:0, one launch (start us, length us, event | category | flops | bytes accessed | tf_op | source)
XLA Modules:
  0.0 112.4 jit_solution(14922459962252617469)
XLA Ops:
  0.6 1.0 constant_dynamic-slice_fusion
  1.7 4.1 %collective-permute-start = (bf16[1024,128]{1,0:T(8,128)(2,1)S(1)}, bf16[1024,128]{1,0:T(8,128)(2,1)S(1)}, u32[]{:S(2)}, u32[]{:S(2)}) collective-permute-start(bf16[1024,128]{1,0:T(8,128)(2,1)S(1)} %pad_maximum_fusion.chunk_ref), channel_id=1, source_target_pairs={{0,4},{1,5},{2,6},{3,7},{4,0},{5,1},{6,2},{7,3},{8,12},{9,13},{10,... | collective-permute-start | bytes 786440 | tf_op jit(solution)/shard_map/ppermute | solution.py:67
  5.8 0.7 add_bitcast_fusion
  6.5 0.1 collective-permute-start.2
  6.6 1.6 %collective-permute-start.6 = (bf16[1024,128]{1,0:T(8,128)(2,1)S(1)}, bf16[1024,128]{1,0:T(8,128)(2,1)S(1)}, u32[]{:S(2)}, u32[]{:S(2)}) collective-permute-start(bf16[1024,128]{1,0:T(8,128)(2,1)S(1)} %pad_maximum_fusion.chunk_ref), channel_id=1, source_target_pairs={{0,2},{1,3},{2,0},{3,1},{4,6},{5,7},{6,4},{7,5},{8,10},{9,11},{10,... | collective-permute-start | bytes 786440 | tf_op jit(solution)/shard_map/ppermute | solution.py:67
  8.2 1.6 %collective-permute-start.4 = (s32[2,2,512]{2,1,0:T(2,128)S(1)}, s32[2,2,512]{2,1,0:T(2,128)S(1)}, u32[]{:S(2)}, u32[]{:S(2)}) collective-permute-start(s32[2,2,512]{2,1,0:T(2,128)S(1)} %get-tuple-element.96), channel_id=1, source_target_pairs={{0,16},{8,24},{16,0},{24,8},{1,17},{9,25},{17,1},{25,9},{2,18},{10... | collective-permute-start | bytes 24584 | tf_op jit(solution)/shard_map/ppermute | solution.py:63
  9.8 1.5 %collective-permute-start.3 = (s32[2,2,512]{2,1,0:T(2,128)S(1)}, s32[2,2,512]{2,1,0:T(2,128)S(1)}, u32[]{:S(2)}, u32[]{:S(2)}) collective-permute-start(s32[2,2,512]{2,1,0:T(2,128)S(1)} %get-tuple-element.96), channel_id=1, source_target_pairs={{0,8},{8,0},{16,24},{24,16},{1,9},{9,1},{17,25},{25,17},{2,10},{10... | collective-permute-start | bytes 24584 | tf_op jit(solution)/shard_map/ppermute | solution.py:63
  11.3 0.5 collective-permute-start.5
  11.8 6.0 %collective-permute-done.chunk_ref = bf16[1024,128]{1,0:T(8,128)(2,1)S(1)} collective-permute-done((bf16[1024,128]{1,0:T(8,128)(2,1)S(1)}, bf16[1024,128]{1,0:T(8,128)(2,1)S(1)}, u32[]{:S(2)}, u32[]{:S(2)}) %collective-permute-start) | collective-permute-done | bytes 262176 | tf_op jit(solution)/shard_map/ppermute | solution.py:67
  17.8 0.7 collective-permute-start.1
  18.5 1.2 %broadcast_in_dim.14.key_ref = s32[4,2,2,512,128]{4,3,2,1,0:T(8,128)S(1)} broadcast(s32[4,2,2,512]{3,2,1,0:T(2,128)S(1)} %pad_add_fusion.key_ref), dimensions={0,1,2,3} | broadcast | bytes 4227072 | tf_op jit(solution)/shard_map/broadcast_in_dim | solution.py:503
  19.7 2.3 %fetch.5 = (bf16[4,512,128]{2,1,0:T(8,128)(2,1)S(1)}, bf16[4,512,128]{2,1,0:T(8,128)(2,1)S(1)}) custom-call(s32[1]{0:T(128)S(6)} %mul.44.base_ref, bf16[1024,128]{1,0:T(8,128)(2,1)S(1)} %pad_maximum_fusion.chunk_ref, s32[4,2,2,512,128]{4,3,2,1,0:T(8,128)S(1)} %broadcast_in_dim.14.key_ref), custom_call_target="tpu_custom_call" | custom-call | flops 536870912 | bytes 5505028 | tf_op jit(solution)/shard_map/fetch/pallas_call | solution.py:37
  22.1 2.3 %fetch.6 = (bf16[4,512,128]{2,1,0:T(8,128)(2,1)S(1)}, bf16[4,512,128]{2,1,0:T(8,128)(2,1)S(1)}) custom-call(s32[1]{0:T(128)S(6)} %mul.42.base_ref, bf16[1024,128]{1,0:T(8,128)(2,1)S(1)} %collective-permute-done.6.chunk_ref, s32[4,2,2,512,128]{4,3,2,1,0:T(8,128)S(1)} %broadcast_in_dim.14.key_ref, bf16[4,512,128]{2,1,0:T(8,128)(2,1)S(1)} %get-tuple-element.50.refs_0_, ...), custom_call_target="tpu_custom_call" | custom-call | flops 536870912 | bytes 6553604 | tf_op jit(solution)/shard_map/fetch/pallas_call | solution.py:37
  24.4 2.3 %fetch.7 = (bf16[4,512,128]{2,1,0:T(8,128)(2,1)S(1)}, bf16[4,512,128]{2,1,0:T(8,128)(2,1)S(1)}) custom-call(s32[1]{0:T(128)S(6)} %mul.40.base_ref, bf16[1024,128]{1,0:T(8,128)(2,1)S(1)} %collective-permute-done.chunk_ref, s32[4,2,2,512,128]{4,3,2,1,0:T(8,128)S(1)} %broadcast_in_dim.14.key_ref, bf16[4,512,128]{2,1,0:T(8,128)(2,1)S(1)} %get-tuple-element.52.refs_0_, ...), custom_call_target="tpu_custom_call" | custom-call | flops 536870912 | bytes 6553604 | tf_op jit(solution)/shard_map/fetch/pallas_call | solution.py:37
  26.8 1.3 %fetch.9 = bf16[4,512,128]{2,1,0:T(8,128)(2,1)S(1)} custom-call(s32[1]{0:T(128)S(6)} %mul.35.base_ref, bf16[1024,128]{1,0:T(8,128)(2,1)S(1)} %collective-permute-done.1.chunk_ref, s32[4,2,2,512,128]{4,3,2,1,0:T(8,128)S(1)} %broadcast_in_dim.14.key_ref, bf16[4,512,128]{2,1,0:T(8,128)(2,1)S(1)} %get-tuple-element.55.refs_0_), custom_call_target="tpu_custom_call" | custom-call | flops 268435456 | bytes 5505028 | tf_op jit(solution)/shard_map/fetch/pallas_call | solution.py:37
  28.0 0.1 collective-permute-start.7
  28.1 0.0 copy-start
  28.1 0.0 copy-start.1
  28.1 0.0 copy-start.2
  28.1 0.0 copy-start.3
  28.2 1.2 %fetch.8.left_ref = bf16[4,512,128]{2,1,0:T(8,128)(2,1)S(1)} custom-call(s32[1]{0:T(128)S(6)} %mul.35.base_ref, bf16[1024,128]{1,0:T(8,128)(2,1)S(1)} %collective-permute-done.1.chunk_ref, s32[4,2,2,512,128]{4,3,2,1,0:T(8,128)S(1)} %broadcast_in_dim.14.key_ref, bf16[4,512,128]{2,1,0:T(8,128)(2,1)S(1)} %get-tuple-element.54.refs_0_), custom_call_target="tpu_custom_call" | custom-call | flops 268435456 | bytes 5505028 | tf_op jit(solution)/shard_map/fetch/pallas_call | solution.py:37
  29.4 0.6 collective-permute-done.7.right_ref
  30.0 0.1 combine.1
  30.1 1.6 %collective-permute-start.8 = (bf16[512,128]{1,0:T(8,128)(2,1)S(1)}, bf16[512,128]{1,0:T(8,128)(2,1)S(1)}, u32[]{:S(2)}, u32[]{:S(2)}) collective-permute-start(bf16[512,128]{1,0:T(8,128)(2,1)S(1)} %get-tuple-element.57), channel_id=1, source_target_pairs={{0,8},{8,0},{16,24},{24,16},{1,9},{9,1},{17,25},{25,17},{2,10},{10... | collective-permute-start | bytes 393224 | tf_op jit(solution)/shard_map/ppermute | solution.py:63
  31.7 1.5 %collective-permute-start.9 = (bf16[512,128]{1,0:T(8,128)(2,1)S(1)}, bf16[512,128]{1,0:T(8,128)(2,1)S(1)}, u32[]{:S(2)}, u32[]{:S(2)}) collective-permute-start(bf16[512,128]{1,0:T(8,128)(2,1)S(1)} %get-tuple-element.58), channel_id=1, source_target_pairs={{0,16},{8,24},{16,0},{24,8},{1,17},{9,25},{17,1},{25,9},{2,18},{10... | collective-permute-start | bytes 393224 | tf_op jit(solution)/shard_map/ppermute | solution.py:63
  33.2 0.5 collective-permute-start.10
  33.7 2.4 %collective-permute-done.8.refs_1_ = bf16[512,128]{1,0:T(8,128)(2,1)S(1)} collective-permute-done((bf16[512,128]{1,0:T(8,128)(2,1)S(1)}, bf16[512,128]{1,0:T(8,128)(2,1)S(1)}, u32[]{:S(2)}, u32[]{:S(2)}) %collective-permute-start.8) | collective-permute-done | bytes 131104 | tf_op jit(solution)/shard_map/ppermute | solution.py:63
  36.1 3.7 %collective-permute-done.9.refs_2_ = bf16[512,128]{1,0:T(8,128)(2,1)S(1)} collective-permute-done((bf16[512,128]{1,0:T(8,128)(2,1)S(1)}, bf16[512,128]{1,0:T(8,128)(2,1)S(1)}, u32[]{:S(2)}, u32[]{:S(2)}) %collective-permute-start.9) | collective-permute-done | bytes 131104 | tf_op jit(solution)/shard_map/ppermute | solution.py:63
  39.8 13.1 %sequence.1 = (bf16[512,512]{1,0:T(8,128)(2,1)}, bf16[512,128]{1,0:T(8,128)(2,1)S(1)}, bf16[512,128]{1,0:T(8,128)(2,1)S(1)}, bf16[512,128]{1,0:T(8,128)(2,1)S(1)...) custom-call(s32[1]{0:T(128)} %bitcast.r_ref, ...), custom_call_target="tpu_custom_call" | custom-call | flops 4294967296 | bytes 9177096 | tf_op jit(solution)/shard_map/sequence/pallas_call | solution.py:37
  53.0 1.2 %collective-permute-start.11 = (bf16[512,128]{1,0:T(8,128)(2,1)S(1)}, bf16[512,128]{1,0:T(8,128)(2,1)S(1)}, u32[]{:S(2)}, u32[]{:S(2)}) collective-permute-start(bf16[512,128]{1,0:T(8,128)(2,1)S(1)} %get-tuple-element.62), channel_id=1, source_target_pairs={{0,8},{8,0},{16,24},{24,16},{1,9},{9,1},{17,25},{25,17},{2,10},{10... | collective-permute-start | bytes 393224 | tf_op jit(solution)/shard_map/ppermute | solution.py:63
  54.2 0.8 collective-permute-start.12
  55.0 1.4 %collective-permute-start.13 = (bf16[512,128]{1,0:T(8,128)(2,1)S(1)}, bf16[512,128]{1,0:T(8,128)(2,1)S(1)}, u32[]{:S(2)}, u32[]{:S(2)}) collective-permute-start(bf16[512,128]{1,0:T(8,128)(2,1)S(1)} %get-tuple-element.64), channel_id=1, source_target_pairs={{0,24},{8,16},{16,8},{24,0},{1,25},{9,17},{17,9},{25,1},{2,26},{10... | collective-permute-start | bytes 393224 | tf_op jit(solution)/shard_map/ppermute | solution.py:63
  56.5 1.7 %weight_grad.1 = (f32[2,128,640]{2,1,0:T(8,128)S(1)}, bf16[2,128,640]{2,1,0:T(8,128)(2,1)S(1)}, f32[2,128,640]{2,1,0:T(8,128)S(1)}, bf16[2,128,640]{2,1,0:T(8,128)(2,1)S(1)}) custom-call(s32[1]{0:T(128)} %bitcast.r_ref, s32[1]{0:T(128)} %bitcast.1.core_ref, bf16[512,512]{1,0:T(8,128)(2,1)S(1)} %get-tuple-element.65.n_ref, ...), custom_call_target="tpu_custom_call" | custom-call | flops 939524096 | bytes 6946824 | tf_op jit(solution)/shard_map/weight_grad/pallas_call | solution.py:37
  58.2 1.3 %collective-permute-start.15 = (bf16[2,128,640]{2,1,0:T(8,128)(2,1)S(1)}, bf16[2,128,640]{2,1,0:T(8,128)(2,1)S(1)}, u32[]{:S(2)}, u32[]{:S(2)}) collective-permute-start(bf16[2,128,640]{2,1,0:T(8,128)(2,1)S(1)} %get-tuple-element.69), channel_id=1, source_target_pairs={{0,8},{8,0},{16,24},{24,16},{1,9},{9,1},{17,25},{25,17},{2,10},{10... | collective-permute-start | bytes 983048 | tf_op jit(solution)/shard_map/ppermute | solution.py:63
  59.5 0.8 collective-permute-start.16
  60.3 0.4 collective-permute-done.12.refs_2_
  60.7 2.3 %collective-permute-done.13.refs_3_ = bf16[512,128]{1,0:T(8,128)(2,1)S(1)} collective-permute-done((bf16[512,128]{1,0:T(8,128)(2,1)S(1)}, bf16[512,128]{1,0:T(8,128)(2,1)S(1)}, u32[]{:S(2)}, u32[]{:S(2)}) %collective-permute-start.13) | collective-permute-done | bytes 131104 | tf_op jit(solution)/shard_map/ppermute | solution.py:63
  63.0 5.7 %collective-permute-done.15.refs_2_ = bf16[2,128,640]{2,1,0:T(8,128)(2,1)S(1)} collective-permute-done((bf16[2,128,640]{2,1,0:T(8,128)(2,1)S(1)}, bf16[2,128,640]{2,1,0:T(8,128)(2,1)S(1)}, u32[]{:S(2)}, u32[]{:S(2)}) %collective-permute-start.15) | collective-permute-done | bytes 327712 | tf_op jit(solution)/shard_map/ppermute | solution.py:63
  68.7 0.9 collective-permute-done.16.refs_3_
  69.7 0.3 fold.1
  69.9 0.9 collective-permute-start.21
  70.8 1.5 %collective-permute-start.22 = (bf16[1,128,640]{2,1,0:T(8,128)(2,1)S(1)}, bf16[1,128,640]{2,1,0:T(8,128)(2,1)S(1)}, u32[]{:S(2)}, u32[]{:S(2)}) collective-permute-start(bf16[1,128,640]{2,1,0:T(8,128)(2,1)S(1)} %get-tuple-element.83), channel_id=1, source_target_pairs={{0,8},{8,0},{16,24},{24,16},{1,9},{9,1},{17,25},{25,17},{2,10},{10... | collective-permute-start | bytes 491528 | tf_op jit(solution)/shard_map/ppermute | solution.py:63
  72.3 1.2 %gather_grad.5.refs_1_ = bf16[1024,128]{1,0:T(8,128)(2,1)S(1)} custom-call(s32[1]{0:T(128)S(6)} %mul.35.base_ref, s32[4,2,2,512]{3,2,1,0:T(2,128)S(1)} %pad_add_fusion.key_ref, bf16[4,512,128]{2,1,0:T(8,128)(2,1)S(1)} %pack.1.refs_0_), custom_call_target="tpu_custom_call" | custom-call | flops 1073741824 | bytes 819204 | tf_op jit(solution)/shard_map/gather_grad/pallas_call | solution.py:37
  73.5 1.2 %gather_grad.6 = bf16[1024,128]{1,0:T(8,128)(2,1)S(1)} custom-call(s32[1]{0:T(128)S(6)} %mul.35.base_ref, s32[4,2,2,512]{3,2,1,0:T(2,128)S(1)} %pad_add_fusion.key_ref, bf16[4,512,128]{2,1,0:T(8,128)(2,1)S(1)} %collective-permute-done.17.refs_0_.refs_1_, bf16[1024,128]{1,0:T(8,128)(2,1)S(1)} %gather_grad.5.refs_1_), custom_call_target="tpu_custom_call" | custom-call | flops 1073741824 | bytes 1081348 | tf_op jit(solution)/shard_map/gather_grad/pallas_call | solution.py:37
  74.8 1.5 %collective-permute-start.18 = (bf16[1024,128]{1,0:T(8,128)(2,1)S(1)}, bf16[1024,128]{1,0:T(8,128)(2,1)S(1)}, u32[]{:S(2)}, u32[]{:S(2)}) collective-permute-start(bf16[1024,128]{1,0:T(8,128)(2,1)S(1)} %gather_grad.6), channel_id=1, source_target_pairs={{0,2},{1,3},{2,0},{3,1},{4,6},{5,7},{6,4},{7,5},{8,10},{9,11},{10,... | collective-permute-start | bytes 786440 | tf_op jit(solution)/shard_map/ppermute | solution.py:67
  76.3 2.5 %gather_grad.9 = bf16[1024,128]{1,0:T(8,128)(2,1)S(1)} custom-call(s32[1]{0:T(128)S(6)} %mul.42.base_ref, s32[4,2,2,512]{3,2,1,0:T(2,128)S(1)} %pad_add_fusion.key_ref, bf16[4,512,128]{2,1,0:T(8,128)(2,1)S(1)} %pack.1.refs_0_, bf16[4,512,128]{2,1,0:T(8,128)(2,1)S(1)} %collective-permute-done.17.refs_0_.refs_1_), custom_call_target="tpu_custom_call" | custom-call | flops 2147483648 | bytes 1343492 | tf_op jit(solution)/shard_map/gather_grad/pallas_call | solution.py:37
  78.8 0.7 collective-permute-start.19
  79.5 0.1 cut_line.1
  79.6 1.5 %collective-permute-start.23 = (bf16[2,64,640]{2,1,0:T(8,128)(2,1)S(1)}, bf16[2,64,640]{2,1,0:T(8,128)(2,1)S(1)}, u32[]{:S(2)}, u32[]{:S(2)}) collective-permute-start(bf16[2,64,640]{2,1,0:T(8,128)(2,1)S(1)} %get-tuple-element.87), channel_id=1, source_target_pairs={{0,2},{1,3},{2,0},{3,1},{4,6},{5,7},{6,4},{7,5},{8,10},{9,11},{10,... | collective-permute-start | bytes 491528 | tf_op jit(solution)/shard_map/ppermute | solution.py:67
  81.1 2.3 %gather_grad.7.refs_0_ = f32[1024,128]{1,0:T(8,128)S(1)} custom-call(s32[1]{0:T(128)S(6)} %mul.40.base_ref, s32[4,2,2,512]{3,2,1,0:T(2,128)S(1)} %pad_add_fusion.key_ref, bf16[4,512,128]{2,1,0:T(8,128)(2,1)S(1)} %pack.1.refs_0_, bf16[4,512,128]{2,1,0:T(8,128)(2,1)S(1)} %collective-permute-done.17.refs_0_.refs_1_), custom_call_target="tpu_custom_call" | custom-call | flops 2147483648 | bytes 1605636 | tf_op jit(solution)/shard_map/gather_grad/pallas_call | solution.py:37
  83.4 0.6 collective-permute-done.18.refs_1_
  84.1 3.5 %collective-permute-start.20 = (bf16[1024,128]{1,0:T(8,128)(2,1)S(1)}, bf16[1024,128]{1,0:T(8,128)(2,1)S(1)}, u32[]{:S(2)}, u32[]{:S(2)}) collective-permute-start(bf16[1024,128]{1,0:T(8,128)(2,1)S(1)} %add_up.2), channel_id=1, source_target_pairs={{0,4},{1,5},{2,6},{3,7},{4,0},{5,1},{6,2},{7,3},{8,12},{9,13},{10,... | collective-permute-start | bytes 786440 | tf_op jit(solution)/shard_map/ppermute | solution.py:67
  87.6 10.2 %collective-permute-done.23.came_ref = bf16[2,64,640]{2,1,0:T(8,128)(2,1)S(1)} collective-permute-done((bf16[2,64,640]{2,1,0:T(8,128)(2,1)S(1)}, bf16[2,64,640]{2,1,0:T(8,128)(2,1)S(1)}, u32[]{:S(2)}, u32[]{:S(2)}) %collective-permute-start.23) | collective-permute-done | bytes 163872 | tf_op jit(solution)/shard_map/ppermute | solution.py:67
  97.8 1.3 %collective-permute-start.24 = (bf16[1,64,640]{2,1,0:T(8,128)(2,1)S(1)}, bf16[1,64,640]{2,1,0:T(8,128)(2,1)S(1)}, u32[]{:S(2)}, u32[]{:S(2)}) collective-permute-start(bf16[1,64,640]{2,1,0:T(8,128)(2,1)S(1)} %get-tuple-element.90), channel_id=1, source_target_pairs={{0,4},{1,5},{2,6},{3,7},{4,0},{5,1},{6,2},{7,3},{8,12},{9,13},{10,... | collective-permute-start | bytes 245768 | tf_op jit(solution)/shard_map/ppermute | solution.py:67
  99.1 2.3 %gather_grad.8.here_ref = f32[1024,128]{1,0:T(8,128)S(1)} custom-call(s32[1]{0:T(128)S(6)} %mul.44.base_ref, s32[4,2,2,512]{3,2,1,0:T(2,128)S(1)} %pad_add_fusion.key_ref, bf16[4,512,128]{2,1,0:T(8,128)(2,1)S(1)} %pack.1.refs_0_, bf16[4,512,128]{2,1,0:T(8,128)(2,1)S(1)} %collective-permute-done.17.refs_0_.refs_1_), custom_call_target="tpu_custom_call" | custom-call | flops 2147483648 | bytes 1605636 | tf_op jit(solution)/shard_map/gather_grad/pallas_call | solution.py:37
  101.4 2.7 %collective-permute-done.24 = bf16[1,64,640]{2,1,0:T(8,128)(2,1)S(1)} collective-permute-done((bf16[1,64,640]{2,1,0:T(8,128)(2,1)S(1)}, bf16[1,64,640]{2,1,0:T(8,128)(2,1)S(1)}, u32[]{:S(2)}, u32[]{:S(2)}) %collective-permute-start.24) | collective-permute-done | bytes 81952 | tf_op jit(solution)/shard_map/ppermute | solution.py:67
  104.2 1.2 %collective-permute-start.27 = (bf16[64,640]{1,0:T(8,128)(2,1)S(1)}, bf16[64,640]{1,0:T(8,128)(2,1)S(1)}, u32[]{:S(2)}, u32[]{:S(2)}) collective-permute-start(bf16[64,640]{1,0:T(8,128)(2,1)S(1)} %add_up.3.refs_0_), channel_id=1, source_target_pairs={{0,24},{8,16},{16,8},{24,0},{1,25},{9,17},{17,9},{25,1},{2,26},{10... | collective-permute-start | bytes 245768 | tf_op jit(solution)/shard_map/ppermute | solution.py:63
  105.4 0.8 collective-permute-start.26
  106.2 1.5 %collective-permute-start.25 = (bf16[64,640]{1,0:T(8,128)(2,1)S(1)}, bf16[64,640]{1,0:T(8,128)(2,1)S(1)}, u32[]{:S(2)}, u32[]{:S(2)}) collective-permute-start(bf16[64,640]{1,0:T(8,128)(2,1)S(1)} %add_up.3.refs_0_), channel_id=1, source_target_pairs={{0,8},{8,0},{16,24},{24,16},{1,9},{9,1},{17,25},{25,17},{2,10},{10... | collective-permute-start | bytes 245768 | tf_op jit(solution)/shard_map/ppermute | solution.py:63
  107.8 1.9 %collective-permute-done.27.refs_3_ = bf16[64,640]{1,0:T(8,128)(2,1)S(1)} collective-permute-done((bf16[64,640]{1,0:T(8,128)(2,1)S(1)}, bf16[64,640]{1,0:T(8,128)(2,1)S(1)}, u32[]{:S(2)}, u32[]{:S(2)}) %collective-permute-start.27) | collective-permute-done | bytes 81952 | tf_op jit(solution)/shard_map/ppermute | solution.py:63
  109.6 0.8 collective-permute-done.26.refs_2_
  110.5 0.2 collective-permute-done.25.refs_1_
  110.7 0.9 assemble.1
  111.6 0.8 table_sums.3
  (29 shorter events, 0.3 us)
Async XLA Ops:
  1.7 16.1 %collective-permute-start = (bf16[1024,128]{1,0:T(8,128)(2,1)S(1)}, bf16[1024,128]{1,0:T(8,128)(2,1)S(1)}, u32[]{:S(2)}, u32[]{:S(2)}) collective-permute-start(bf16[1024,128]{1,0:T(8,128)(2,1)S(1)} %pad_maximum_fusion.chunk_ref), channel_id=1, source_target_pairs={{0,4},{1,5},{2,6},{3,7},{4,0},{5,1},{6,2},{7,3},{8,12},{9,13},{10,... | collective-permute-start | bytes 786440 | tf_op jit(solution)/shard_map/ppermute | solution.py:67
  6.5 1.7 %collective-permute-start.2 = (s32[2,512]{1,0:T(2,128)S(1)}, s32[2,512]{1,0:T(2,128)S(1)}, u32[]{:S(2)}, u32[]{:S(2)}) collective-permute-start(s32[2,512]{1,0:T(2,128)S(1)} %get-tuple-element.98), channel_id=1, source_target_pairs={{0,1},{1,0},{2,3},{3,2},{4,5},{5,4},{6,7},{7,6},{8,9},{9,8},{10,11... | collective-permute-start | bytes 12296 | tf_op jit(solution)/shard_map/ppermute | solution.py:70
  6.6 15.5 %collective-permute-start.6 = (bf16[1024,128]{1,0:T(8,128)(2,1)S(1)}, bf16[1024,128]{1,0:T(8,128)(2,1)S(1)}, u32[]{:S(2)}, u32[]{:S(2)}) collective-permute-start(bf16[1024,128]{1,0:T(8,128)(2,1)S(1)} %pad_maximum_fusion.chunk_ref), channel_id=1, source_target_pairs={{0,2},{1,3},{2,0},{3,1},{4,6},{5,7},{6,4},{7,5},{8,10},{9,11},{10,... | collective-permute-start | bytes 786440 | tf_op jit(solution)/shard_map/ppermute | solution.py:67
  8.2 10.2 %collective-permute-start.4 = (s32[2,2,512]{2,1,0:T(2,128)S(1)}, s32[2,2,512]{2,1,0:T(2,128)S(1)}, u32[]{:S(2)}, u32[]{:S(2)}) collective-permute-start(s32[2,2,512]{2,1,0:T(2,128)S(1)} %get-tuple-element.96), channel_id=1, source_target_pairs={{0,16},{8,24},{16,0},{24,8},{1,17},{9,25},{17,1},{25,9},{2,18},{10... | collective-permute-start | bytes 24584 | tf_op jit(solution)/shard_map/ppermute | solution.py:63
  9.8 8.6 %collective-permute-start.3 = (s32[2,2,512]{2,1,0:T(2,128)S(1)}, s32[2,2,512]{2,1,0:T(2,128)S(1)}, u32[]{:S(2)}, u32[]{:S(2)}) collective-permute-start(s32[2,2,512]{2,1,0:T(2,128)S(1)} %get-tuple-element.96), channel_id=1, source_target_pairs={{0,8},{8,0},{16,24},{24,16},{1,9},{9,1},{17,25},{25,17},{2,10},{10... | collective-permute-start | bytes 24584 | tf_op jit(solution)/shard_map/ppermute | solution.py:63
  11.3 7.1 %collective-permute-start.5 = (s32[2,2,512]{2,1,0:T(2,128)S(1)}, s32[2,2,512]{2,1,0:T(2,128)S(1)}, u32[]{:S(2)}, u32[]{:S(2)}) collective-permute-start(s32[2,2,512]{2,1,0:T(2,128)S(1)} %get-tuple-element.96), channel_id=1, source_target_pairs={{0,24},{8,16},{16,8},{24,0},{1,25},{9,17},{17,9},{25,1},{2,26},{10... | collective-permute-start | bytes 24584 | tf_op jit(solution)/shard_map/ppermute | solution.py:63
  17.8 9.0 %collective-permute-start.1 = (bf16[1024,128]{1,0:T(8,128)(2,1)S(1)}, bf16[1024,128]{1,0:T(8,128)(2,1)S(1)}, u32[]{:S(2)}, u32[]{:S(2)}) collective-permute-start(bf16[1024,128]{1,0:T(8,128)(2,1)S(1)} %collective-permute-done.chunk_ref), channel_id=1, source_target_pairs={{0,2},{1,3},{2,0},{3,1},{4,6},{5,7},{6,4},{7,5},{8,10},{9,11},{10,... | collective-permute-start | bytes 786440 | tf_op jit(solution)/shard_map/ppermute | solution.py:67
  28.0 2.0 %collective-permute-start.7 = (bf16[4,512,128]{2,1,0:T(8,128)(2,1)S(1)}, bf16[4,512,128]{2,1,0:T(8,128)(2,1)S(1)}, u32[]{:S(2)}, u32[]{:S(2)}) collective-permute-start(bf16[4,512,128]{2,1,0:T(8,128)(2,1)S(1)} %fetch.9), channel_id=1, source_target_pairs={{0,1},{1,0},{2,3},{3,2},{4,5},{5,4},{6,7},{7,6},{8,9},{9,8},{10,11... | collective-permute-start | bytes 1572872 | tf_op jit(solution)/shard_map/ppermute | solution.py:70
  28.1 11.7 %copy-start = (bf16[512,512]{1,0:T(8,128)(2,1)S(1)}, bf16[512,512]{1,0:T(8,128)(2,1)}, u32[]{:S(2)}) copy-start(bf16[512,512]{1,0:T(8,128)(2,1)} %c_ref.1) | copy-start | bytes 1572868
  28.1 11.7 %copy-start.1 = (bf16[512,2048]{1,0:T(8,128)(2,1)S(1)}, bf16[512,2048]{1,0:T(8,128)(2,1)}, u32[]{:S(2)}) copy-start(bf16[512,2048]{1,0:T(8,128)(2,1)} %wp_ref.1) | copy-start | bytes 6291460
  28.1 11.7 %copy-start.2 = (bf16[512,512]{1,0:T(8,128)(2,1)S(1)}, bf16[512,512]{1,0:T(8,128)(2,1)}, u32[]{:S(2)}) copy-start(bf16[512,512]{1,0:T(8,128)(2,1)} %wo_ref.1) | copy-start | bytes 1572868
  28.1 11.7 %copy-start.3 = (f32[512]{0:T(512)S(1)}, f32[512]{0:T(512)}, u32[]{:S(2)}) copy-start(f32[512]{0:T(512)} %param.16) | copy-start | bytes 6148
  30.1 5.9 %collective-permute-start.8 = (bf16[512,128]{1,0:T(8,128)(2,1)S(1)}, bf16[512,128]{1,0:T(8,128)(2,1)S(1)}, u32[]{:S(2)}, u32[]{:S(2)}) collective-permute-start(bf16[512,128]{1,0:T(8,128)(2,1)S(1)} %get-tuple-element.57), channel_id=1, source_target_pairs={{0,8},{8,0},{16,24},{24,16},{1,9},{9,1},{17,25},{25,17},{2,10},{10... | collective-permute-start | bytes 393224 | tf_op jit(solution)/shard_map/ppermute | solution.py:63
  31.7 8.1 %collective-permute-start.9 = (bf16[512,128]{1,0:T(8,128)(2,1)S(1)}, bf16[512,128]{1,0:T(8,128)(2,1)S(1)}, u32[]{:S(2)}, u32[]{:S(2)}) collective-permute-start(bf16[512,128]{1,0:T(8,128)(2,1)S(1)} %get-tuple-element.58), channel_id=1, source_target_pairs={{0,16},{8,24},{16,0},{24,8},{1,17},{9,25},{17,1},{25,9},{2,18},{10... | collective-permute-start | bytes 393224 | tf_op jit(solution)/shard_map/ppermute | solution.py:63
  33.2 6.6 %collective-permute-start.10 = (bf16[512,128]{1,0:T(8,128)(2,1)S(1)}, bf16[512,128]{1,0:T(8,128)(2,1)S(1)}, u32[]{:S(2)}, u32[]{:S(2)}) collective-permute-start(bf16[512,128]{1,0:T(8,128)(2,1)S(1)} %get-tuple-element.59), channel_id=1, source_target_pairs={{0,24},{8,16},{16,8},{24,0},{1,25},{9,17},{17,9},{25,1},{2,26},{10... | collective-permute-start | bytes 393224 | tf_op jit(solution)/shard_map/ppermute | solution.py:63
  53.0 3.5 %collective-permute-start.14 = (bf16[4,256,640]{2,1,0:T(8,128)(2,1)S(1)}, bf16[4,256,640]{2,1,0:T(8,128)(2,1)S(1)}, u32[]{:S(2)}, u32[]{:S(2)}) collective-permute-start(bf16[4,256,640]{2,1,0:T(8,128)(2,1)S(1)} %get-tuple-element.68), channel_id=1, source_target_pairs={{0,1},{1,0},{2,3},{3,2},{4,5},{5,4},{6,7},{7,6},{8,9},{9,8},{10,11... | collective-permute-start | bytes 3932168 | tf_op jit(solution)/shard_map/ppermute | solution.py:70
  53.0 7.3 %collective-permute-start.11 = (bf16[512,128]{1,0:T(8,128)(2,1)S(1)}, bf16[512,128]{1,0:T(8,128)(2,1)S(1)}, u32[]{:S(2)}, u32[]{:S(2)}) collective-permute-start(bf16[512,128]{1,0:T(8,128)(2,1)S(1)} %get-tuple-element.62), channel_id=1, source_target_pairs={{0,8},{8,0},{16,24},{24,16},{1,9},{9,1},{17,25},{25,17},{2,10},{10... | collective-permute-start | bytes 393224 | tf_op jit(solution)/shard_map/ppermute | solution.py:63
  54.2 6.5 %collective-permute-start.12 = (bf16[512,128]{1,0:T(8,128)(2,1)S(1)}, bf16[512,128]{1,0:T(8,128)(2,1)S(1)}, u32[]{:S(2)}, u32[]{:S(2)}) collective-permute-start(bf16[512,128]{1,0:T(8,128)(2,1)S(1)} %get-tuple-element.63), channel_id=1, source_target_pairs={{0,16},{8,24},{16,0},{24,8},{1,17},{9,25},{17,1},{25,9},{2,18},{10... | collective-permute-start | bytes 393224 | tf_op jit(solution)/shard_map/ppermute | solution.py:63
  55.0 8.0 %collective-permute-start.13 = (bf16[512,128]{1,0:T(8,128)(2,1)S(1)}, bf16[512,128]{1,0:T(8,128)(2,1)S(1)}, u32[]{:S(2)}, u32[]{:S(2)}) collective-permute-start(bf16[512,128]{1,0:T(8,128)(2,1)S(1)} %get-tuple-element.64), channel_id=1, source_target_pairs={{0,24},{8,16},{16,8},{24,0},{1,25},{9,17},{17,9},{25,1},{2,26},{10... | collective-permute-start | bytes 393224 | tf_op jit(solution)/shard_map/ppermute | solution.py:63
  58.2 10.6 %collective-permute-start.15 = (bf16[2,128,640]{2,1,0:T(8,128)(2,1)S(1)}, bf16[2,128,640]{2,1,0:T(8,128)(2,1)S(1)}, u32[]{:S(2)}, u32[]{:S(2)}) collective-permute-start(bf16[2,128,640]{2,1,0:T(8,128)(2,1)S(1)} %get-tuple-element.69), channel_id=1, source_target_pairs={{0,8},{8,0},{16,24},{24,16},{1,9},{9,1},{17,25},{25,17},{2,10},{10... | collective-permute-start | bytes 983048 | tf_op jit(solution)/shard_map/ppermute | solution.py:63
  59.5 10.2 %collective-permute-start.16 = (bf16[2,128,640]{2,1,0:T(8,128)(2,1)S(1)}, bf16[2,128,640]{2,1,0:T(8,128)(2,1)S(1)}, u32[]{:S(2)}, u32[]{:S(2)}) collective-permute-start(bf16[2,128,640]{2,1,0:T(8,128)(2,1)S(1)} %get-tuple-element.70), channel_id=1, source_target_pairs={{0,16},{8,24},{16,0},{24,8},{1,17},{9,25},{17,1},{25,9},{2,18},{10... | collective-permute-start | bytes 983048 | tf_op jit(solution)/shard_map/ppermute | solution.py:63
  69.6 3.9 %collective-permute-start.17 = (bf16[4,512,128]{2,1,0:T(8,128)(2,1)S(1)}, bf16[4,512,128]{2,1,0:T(8,128)(2,1)S(1)}, u32[]{:S(2)}, u32[]{:S(2)}) collective-permute-start(bf16[4,512,128]{2,1,0:T(8,128)(2,1)S(1)} %pack.1.refs_0_), channel_id=1, source_target_pairs={{0,1},{1,0},{2,3},{3,2},{4,5},{5,4},{6,7},{7,6},{8,9},{9,8},{10,11... | collective-permute-start | bytes 1572872 | tf_op jit(solution)/shard_map/ppermute | solution.py:70
  69.9 9.6 %collective-permute-start.21 = (bf16[1,128,640]{2,1,0:T(8,128)(2,1)S(1)}, bf16[1,128,640]{2,1,0:T(8,128)(2,1)S(1)}, u32[]{:S(2)}, u32[]{:S(2)}) collective-permute-start(bf16[1,128,640]{2,1,0:T(8,128)(2,1)S(1)} %get-tuple-element.82), channel_id=1, source_target_pairs={{0,16},{8,24},{16,0},{24,8},{1,17},{9,25},{17,1},{25,9},{2,18},{10... | collective-permute-start | bytes 491528 | tf_op jit(solution)/shard_map/ppermute | solution.py:63
  70.8 8.7 %collective-permute-start.22 = (bf16[1,128,640]{2,1,0:T(8,128)(2,1)S(1)}, bf16[1,128,640]{2,1,0:T(8,128)(2,1)S(1)}, u32[]{:S(2)}, u32[]{:S(2)}) collective-permute-start(bf16[1,128,640]{2,1,0:T(8,128)(2,1)S(1)} %get-tuple-element.83), channel_id=1, source_target_pairs={{0,8},{8,0},{16,24},{24,16},{1,9},{9,1},{17,25},{25,17},{2,10},{10... | collective-permute-start | bytes 491528 | tf_op jit(solution)/shard_map/ppermute | solution.py:63
  74.8 9.2 %collective-permute-start.18 = (bf16[1024,128]{1,0:T(8,128)(2,1)S(1)}, bf16[1024,128]{1,0:T(8,128)(2,1)S(1)}, u32[]{:S(2)}, u32[]{:S(2)}) collective-permute-start(bf16[1024,128]{1,0:T(8,128)(2,1)S(1)} %gather_grad.6), channel_id=1, source_target_pairs={{0,2},{1,3},{2,0},{3,1},{4,6},{5,7},{6,4},{7,5},{8,10},{9,11},{10,... | collective-permute-start | bytes 786440 | tf_op jit(solution)/shard_map/ppermute | solution.py:67
  78.8 28.9 %collective-permute-start.19 = (bf16[1024,128]{1,0:T(8,128)(2,1)S(1)}, bf16[1024,128]{1,0:T(8,128)(2,1)S(1)}, u32[]{:S(2)}, u32[]{:S(2)}) collective-permute-start(bf16[1024,128]{1,0:T(8,128)(2,1)S(1)} %gather_grad.9), channel_id=1, source_target_pairs={{0,2},{1,3},{2,0},{3,1},{4,6},{5,7},{6,4},{7,5},{8,10},{9,11},{10,... | collective-permute-start | bytes 786440 | tf_op jit(solution)/shard_map/ppermute | solution.py:67
  79.6 18.1 %collective-permute-start.23 = (bf16[2,64,640]{2,1,0:T(8,128)(2,1)S(1)}, bf16[2,64,640]{2,1,0:T(8,128)(2,1)S(1)}, u32[]{:S(2)}, u32[]{:S(2)}) collective-permute-start(bf16[2,64,640]{2,1,0:T(8,128)(2,1)S(1)} %get-tuple-element.87), channel_id=1, source_target_pairs={{0,2},{1,3},{2,0},{3,1},{4,6},{5,7},{6,4},{7,5},{8,10},{9,11},{10,... | collective-permute-start | bytes 491528 | tf_op jit(solution)/shard_map/ppermute | solution.py:67
  84.1 27.5 %collective-permute-start.20 = (bf16[1024,128]{1,0:T(8,128)(2,1)S(1)}, bf16[1024,128]{1,0:T(8,128)(2,1)S(1)}, u32[]{:S(2)}, u32[]{:S(2)}) collective-permute-start(bf16[1024,128]{1,0:T(8,128)(2,1)S(1)} %add_up.2), channel_id=1, source_target_pairs={{0,4},{1,5},{2,6},{3,7},{4,0},{5,1},{6,2},{7,3},{8,12},{9,13},{10,... | collective-permute-start | bytes 786440 | tf_op jit(solution)/shard_map/ppermute | solution.py:67
  97.8 6.4 %collective-permute-start.24 = (bf16[1,64,640]{2,1,0:T(8,128)(2,1)S(1)}, bf16[1,64,640]{2,1,0:T(8,128)(2,1)S(1)}, u32[]{:S(2)}, u32[]{:S(2)}) collective-permute-start(bf16[1,64,640]{2,1,0:T(8,128)(2,1)S(1)} %get-tuple-element.90), channel_id=1, source_target_pairs={{0,4},{1,5},{2,6},{3,7},{4,0},{5,1},{6,2},{7,3},{8,12},{9,13},{10,... | collective-permute-start | bytes 245768 | tf_op jit(solution)/shard_map/ppermute | solution.py:67
  104.2 5.5 %collective-permute-start.27 = (bf16[64,640]{1,0:T(8,128)(2,1)S(1)}, bf16[64,640]{1,0:T(8,128)(2,1)S(1)}, u32[]{:S(2)}, u32[]{:S(2)}) collective-permute-start(bf16[64,640]{1,0:T(8,128)(2,1)S(1)} %add_up.3.refs_0_), channel_id=1, source_target_pairs={{0,24},{8,16},{16,8},{24,0},{1,25},{9,17},{17,9},{25,1},{2,26},{10... | collective-permute-start | bytes 245768 | tf_op jit(solution)/shard_map/ppermute | solution.py:63
  105.4 5.0 %collective-permute-start.26 = (bf16[64,640]{1,0:T(8,128)(2,1)S(1)}, bf16[64,640]{1,0:T(8,128)(2,1)S(1)}, u32[]{:S(2)}, u32[]{:S(2)}) collective-permute-start(bf16[64,640]{1,0:T(8,128)(2,1)S(1)} %add_up.3.refs_0_), channel_id=1, source_target_pairs={{0,16},{8,24},{16,0},{24,8},{1,17},{9,25},{17,1},{25,9},{2,18},{10... | collective-permute-start | bytes 245768 | tf_op jit(solution)/shard_map/ppermute | solution.py:63
  106.2 4.4 %collective-permute-start.25 = (bf16[64,640]{1,0:T(8,128)(2,1)S(1)}, bf16[64,640]{1,0:T(8,128)(2,1)S(1)}, u32[]{:S(2)}, u32[]{:S(2)}) collective-permute-start(bf16[64,640]{1,0:T(8,128)(2,1)S(1)} %add_up.3.refs_0_), channel_id=1, source_target_pairs={{0,8},{8,0},{16,24},{24,16},{1,9},{9,1},{17,25},{25,17},{2,10},{10... | collective-permute-start | bytes 245768 | tf_op jit(solution)/shard_map/ppermute | solution.py:63

commit v12 on v10

--- a/solution.py
+++ b/solution.py
@@ -215,33 +215,31 @@
 
         normed = normed_ref[...]
 
-        @pl.loop(0, 4 * width // step)
-        def _(j):
-            span = pl.ds(pl.multiple_of(j * step, step), step)
+        for at in range(0, 4 * width, step):
+            span = slice(at, at + step)
             proj = dot(normed, wp_ref[:, span])
             sig = sigmoid(proj)
-            act[:, span] = (proj * sig).astype(BF16)
-            slope[:, span] = sig * (1.0 + proj * (1.0 - sig))
-
-        dkey[...] = jnp.zeros_like(dkey)
-        dval[...] = jnp.zeros_like(dval)
-
-        for at in range(0, length, tile):
+            soft = proj * sig
+            act[:, span] = soft.astype(BF16)
+            slope[:, span] = sig + soft * (1.0 - sig)
+
+        for at in reversed(range(0, length, tile)):
             span = slice(at, at + tile)
             seen = at + tile
             past = slice(0, seen)
             keep = lax.broadcasted_iota(I32, (tile, seen), 1) <= at + lax.broadcasted_iota(
                 I32, (tile, seen), 0
             )
+            weight = jnp.where(keep, 1.0 / length, 0.0)
+            weight_back = jnp.where(keep, factor / length, 0.0)
             for h in range(HEADS):
                 head = [slice(p * width + h * head_dim, p * width + (h + 1) * head_dim) for p in range(4)]
                 scores = dot(act[span, head[2]], act[past, head[3]], NT) * factor
                 sig = sigmoid(scores)
-                soft = jnp.where(keep, scores * sig * (1.0 / length), 0.0).astype(BF16)
-                attn[h, :, :seen] = soft
-                grad = sig * (1.0 + scores * (1.0 - sig)) * (factor / length)
-                dscale[h, :, :seen] = jnp.where(keep, grad, 0.0)
-                att[:, head[0]] = dot(soft, act[past, head[1]])
+                soft = scores * sig
+                attn[h, :, :seen] = (soft * weight).astype(BF16)
+                dscale[h, :, :seen] = (sig + soft * (1.0 - sig)) * weight_back
+                att[:, head[0]] = dot(attn[h, :, :seen], act[past, head[1]])
             hat, scale = norm_of(att[...])
             gate = act[span, :width].astype(F32)
             gated = (hat * gate).astype(BF16)
@@ -257,16 +255,21 @@
                 dscores = (dattn * dscale[h, :, :seen]).astype(BF16)
                 dquery = dot(dscores, act[past, head[3]])
                 dproj_ref[span, head[2]] = (dquery * slope[span, head[2]]).astype(BF16)
-                dkey[past, head[0]] += dot(dscores, act[span, head[2]], TN)
-                dval[past, head[0]] += dot(attn[h, :, :seen], dhead, TN)
+                back = dot(dscores, act[span, head[2]], TN), dot(attn[h, :, :seen], dhead, TN)
+                for ref, part in zip((dkey, dval), back):
+                    if seen == length:
+                        ref[past, head[0]] = part
+                    else:
+                        ref[past, head[0]] += part
 
         dproj_ref[:, width : 2 * width] = (dval[...] * slope[:, width : 2 * width]).astype(BF16)
         dproj_ref[:, 3 * width :] = (dkey[...] * slope[:, 3 * width :]).astype(BF16)
 
+        dkey[...] = dot(dproj_ref[...], wp_ref[...], NT)
         for at in range(0, length, tile):
             span = slice(at, at + tile)
             hat, scale = norm_of(embedded(span))
-            upper = dot(dproj_ref[span, :], wp_ref[...], NT) * gain_ref[...]
+            upper = dkey[span, :] * gain_ref[...]
             grad = cot_ref[span, :].astype(F32) + norm_back(upper, hat, scale)
             for k in range(count):
                 tok[k, span] = grad[:, k * cols : (k + 1) * cols].astype(BF16)
@@ -547,7 +550,7 @@
             raw[k] = gather_grad(bases[k], keys, both, both_there, rows, out=out)
         came = [grid.over_line(sums[k ^ step], step) for step in steps]
         if k == 0:
-            near, table = came[0], raw[k][0]
+            table = raw[k][0]
             for part in came[:-1]:
                 table = table_sums(table, part, 1)[0]
             item_grad, action_grad = table_sums(table, came[-1], 2)
@@ -555,17 +558,18 @@
             sums[k] = add_up(raw[k] + came) if steps else raw[k][0]
 
     for step in range(1, bits + 1):
-        after = [raw[1], raw[line // 2]] if step < bits else [near, sums[line // 2]]
+        after = raw[1] if step < bits else [raw[1], sums[line // 2]]
         swapped = lax.optimization_barrier((swapped, after))[0]
         if step < bits:
             kept, swapped = swap_weights(fold(replica, kept, swapped, step), step)
     kept, sent = cut_line(place, kept, swapped, line)
     step = 1
     while step < line // 2:
-        kept, sent = fold_line(kept, grid.over_line(sent, step))
+        came = lax.optimization_barrier((grid.over_line(sent, step), sums[line // 2]))[0]
+        kept, sent = fold_line(kept, came)
         step *= 2
     parts = [kept[0], grid.over_line(sent, step)[0]]
-    parts = lax.optimization_barrier((parts, item_grad))[0]
+    parts = lax.optimization_barrier((parts, raw[0]))[0]
     total = add_up(parts)
     parts = [total] + [grid.over_replica(total, k) for k in range(1, replicas)]
     grad_proj, grad_out = assemble(replica, parts, 4 * width)

time: 106 us -> 102 us (0.962)
  waiting for transfers between devices: 33.1 us -> 28.5 us
  starting transfers between devices: 32.6 us -> 35.2 us
  Pallas kernels: 36.5 us -> 34.4 us
    ppermute x8, waiting for transfers between devices: 18.5 us -> 13.9 us  [over_line(): return lax.ppermute(value, 'sparse', pairs)]
    ppermute x8, starting transfers between devices: 14 us -> 16.3 us  [over_line(): return lax.ppermute(value, 'sparse', pairs)]
    pallas_call x22, Pallas kernels: 36.5 us -> 34.4 us  [run(): pl.pallas_call(body, out_shape=outs, in_specs=places, out_specs=[in_vmem]...]
  transfers between devices with their start and end apart: 28 -> 28, of which waited for: 15 -> 14; matrix products, arithmetic and copies ran while one was open for 2% -> 2% of each run, Pallas kernels for 20% -> 21%
where the time goes in v12:
time: 102 us
  starting transfers between devices  35.2 us (35%)
  Pallas kernels  34.4 us (34%)
  waiting for transfers between devices  28.5 us (28%)
  local copies, waits for them, and re-layouts  2.25 us (2%)
    pallas_call x22, Pallas kernels, run(): pl.pallas_call(body, out_shape=outs, in_specs=places, out_specs=[in_vmem]...  34.4 us
    ppermute x16, starting transfers between devices, over_replica(): return lax.ppermute(value, 'replica', [(i, i ^ step) for i in range(n)])  18.7 us
    ppermute x8, starting transfers between devices, over_line(): return lax.ppermute(value, 'sparse', pairs)  16.3 us
    ppermute x8, waiting for transfers between devices, over_line(): return lax.ppermute(value, 'sparse', pairs)  13.9 us
    ppermute x16, waiting for transfers between devices, over_replica(): return lax.ppermute(value, 'replica', [(i, i ^ step) for i in range(n)])  13.9 us
  transfers between devices with their start and end apart: 28, of which 14 were waited for; matrix products, arithmetic and copies ran while one was open for 2% of the time, Pallas kernels for 21%

profile of v12, /device:TPU:0, one launch (start us, length us, event | category | flops | bytes accessed | tf_op | source)
XLA Modules:
  0.0 102.1 jit_solution(3514161557100372569)
XLA Ops:
  0.6 1.0 constant_dynamic-slice_fusion
  1.7 4.1 %collective-permute-start = (bf16[1024,128]{1,0:T(8,128)(2,1)S(1)}, bf16[1024,128]{1,0:T(8,128)(2,1)S(1)}, u32[]{:S(2)}, u32[]{:S(2)}) collective-permute-start(bf16[1024,128]{1,0:T(8,128)(2,1)S(1)} %pad_maximum_fusion.chunk_ref), channel_id=1, source_target_pairs={{0,4},{1,5},{2,6},{3,7},{4,0},{5,1},{6,2},{7,3},{8,12},{9,13},{10,... | collective-permute-start | bytes 786440 | tf_op jit(solution)/shard_map/ppermute | solution.py:66
  5.8 0.7 add_bitcast_fusion
  6.5 0.1 collective-permute-start.2
  6.6 1.6 %collective-permute-start.6 = (bf16[1024,128]{1,0:T(8,128)(2,1)S(1)}, bf16[1024,128]{1,0:T(8,128)(2,1)S(1)}, u32[]{:S(2)}, u32[]{:S(2)}) collective-permute-start(bf16[1024,128]{1,0:T(8,128)(2,1)S(1)} %pad_maximum_fusion.chunk_ref), channel_id=1, source_target_pairs={{0,2},{1,3},{2,0},{3,1},{4,6},{5,7},{6,4},{7,5},{8,10},{9,11},{10,... | collective-permute-start | bytes 786440 | tf_op jit(solution)/shard_map/ppermute | solution.py:66
  8.2 1.6 %collective-permute-start.4 = (s32[2,2,512]{2,1,0:T(2,128)S(1)}, s32[2,2,512]{2,1,0:T(2,128)S(1)}, u32[]{:S(2)}, u32[]{:S(2)}) collective-permute-start(s32[2,2,512]{2,1,0:T(2,128)S(1)} %get-tuple-element.106), channel_id=1, source_target_pairs={{0,16},{8,24},{16,0},{24,8},{1,17},{9,25},{17,1},{25,9},{2,18},{10... | collective-permute-start | bytes 24584 | tf_op jit(solution)/shard_map/ppermute | solution.py:62
  9.8 1.5 %collective-permute-start.3 = (s32[2,2,512]{2,1,0:T(2,128)S(1)}, s32[2,2,512]{2,1,0:T(2,128)S(1)}, u32[]{:S(2)}, u32[]{:S(2)}) collective-permute-start(s32[2,2,512]{2,1,0:T(2,128)S(1)} %get-tuple-element.106), channel_id=1, source_target_pairs={{0,8},{8,0},{16,24},{24,16},{1,9},{9,1},{17,25},{25,17},{2,10},{10... | collective-permute-start | bytes 24584 | tf_op jit(solution)/shard_map/ppermute | solution.py:62
  11.3 0.5 collective-permute-start.5
  11.8 6.0 %collective-permute-done.chunk_ref = bf16[1024,128]{1,0:T(8,128)(2,1)S(1)} collective-permute-done((bf16[1024,128]{1,0:T(8,128)(2,1)S(1)}, bf16[1024,128]{1,0:T(8,128)(2,1)S(1)}, u32[]{:S(2)}, u32[]{:S(2)}) %collective-permute-start) | collective-permute-done | bytes 262176 | tf_op jit(solution)/shard_map/ppermute | solution.py:66
  17.8 0.7 collective-permute-start.1
  18.5 1.2 %broadcast_in_dim.14.key_ref = s32[4,2,2,512,128]{4,3,2,1,0:T(8,128)S(1)} broadcast(s32[4,2,2,512]{3,2,1,0:T(2,128)S(1)} %pad_add_fusion.key_ref), dimensions={0,1,2,3} | broadcast | bytes 4227072 | tf_op jit(solution)/shard_map/broadcast_in_dim | solution.py:505
  19.7 2.3 %fetch.5 = (bf16[4,512,128]{2,1,0:T(8,128)(2,1)S(1)}, bf16[4,512,128]{2,1,0:T(8,128)(2,1)S(1)}) custom-call(s32[1]{0:T(128)S(6)} %mul.44.base_ref, bf16[1024,128]{1,0:T(8,128)(2,1)S(1)} %pad_maximum_fusion.chunk_ref, s32[4,2,2,512,128]{4,3,2,1,0:T(8,128)S(1)} %broadcast_in_dim.14.key_ref), custom_call_target="tpu_custom_call" | custom-call | flops 536870912 | bytes 5505028 | tf_op jit(solution)/shard_map/fetch/pallas_call | solution.py:36
  22.1 2.3 %fetch.6 = (bf16[4,512,128]{2,1,0:T(8,128)(2,1)S(1)}, bf16[4,512,128]{2,1,0:T(8,128)(2,1)S(1)}) custom-call(s32[1]{0:T(128)S(6)} %mul.42.base_ref, bf16[1024,128]{1,0:T(8,128)(2,1)S(1)} %collective-permute-done.6.chunk_ref, s32[4,2,2,512,128]{4,3,2,1,0:T(8,128)S(1)} %broadcast_in_dim.14.key_ref, bf16[4,512,128]{2,1,0:T(8,128)(2,1)S(1)} %get-tuple-element.55.refs_0_, ...), custom_call_target="tpu_custom_call" | custom-call | flops 536870912 | bytes 6553604 | tf_op jit(solution)/shard_map/fetch/pallas_call | solution.py:36
  24.4 2.3 %fetch.7 = (bf16[4,512,128]{2,1,0:T(8,128)(2,1)S(1)}, bf16[4,512,128]{2,1,0:T(8,128)(2,1)S(1)}) custom-call(s32[1]{0:T(128)S(6)} %mul.40.base_ref, bf16[1024,128]{1,0:T(8,128)(2,1)S(1)} %collective-permute-done.chunk_ref, s32[4,2,2,512,128]{4,3,2,1,0:T(8,128)S(1)} %broadcast_in_dim.14.key_ref, bf16[4,512,128]{2,1,0:T(8,128)(2,1)S(1)} %get-tuple-element.57.refs_0_, ...), custom_call_target="tpu_custom_call" | custom-call | flops 536870912 | bytes 6553604 | tf_op jit(solution)/shard_map/fetch/pallas_call | solution.py:36
  26.8 1.3 %fetch.9 = bf16[4,512,128]{2,1,0:T(8,128)(2,1)S(1)} custom-call(s32[1]{0:T(128)S(6)} %mul.35.base_ref, bf16[1024,128]{1,0:T(8,128)(2,1)S(1)} %collective-permute-done.1.chunk_ref, s32[4,2,2,512,128]{4,3,2,1,0:T(8,128)S(1)} %broadcast_in_dim.14.key_ref, bf16[4,512,128]{2,1,0:T(8,128)(2,1)S(1)} %get-tuple-element.60.refs_0_), custom_call_target="tpu_custom_call" | custom-call | flops 268435456 | bytes 5505028 | tf_op jit(solution)/shard_map/fetch/pallas_call | solution.py:36
  28.0 0.1 collective-permute-start.7
  28.1 0.0 copy-start
  28.2 1.2 %fetch.8.left_ref = bf16[4,512,128]{2,1,0:T(8,128)(2,1)S(1)} custom-call(s32[1]{0:T(128)S(6)} %mul.35.base_ref, bf16[1024,128]{1,0:T(8,128)(2,1)S(1)} %collective-permute-done.1.chunk_ref, s32[4,2,2,512,128]{4,3,2,1,0:T(8,128)S(1)} %broadcast_in_dim.14.key_ref, bf16[4,512,128]{2,1,0:T(8,128)(2,1)S(1)} %get-tuple-element.59.refs_0_), custom_call_target="tpu_custom_call" | custom-call | flops 268435456 | bytes 5505028 | tf_op jit(solution)/shard_map/fetch/pallas_call | solution.py:36
  29.4 0.6 collective-permute-done.7.right_ref
  30.0 0.1 combine.1
  30.1 1.6 %collective-permute-start.8 = (bf16[512,128]{1,0:T(8,128)(2,1)S(1)}, bf16[512,128]{1,0:T(8,128)(2,1)S(1)}, u32[]{:S(2)}, u32[]{:S(2)}) collective-permute-start(bf16[512,128]{1,0:T(8,128)(2,1)S(1)} %get-tuple-element.62), channel_id=1, source_target_pairs={{0,8},{8,0},{16,24},{24,16},{1,9},{9,1},{17,25},{25,17},{2,10},{10... | collective-permute-start | bytes 393224 | tf_op jit(solution)/shard_map/ppermute | solution.py:62
  31.7 1.5 %collective-permute-start.9 = (bf16[512,128]{1,0:T(8,128)(2,1)S(1)}, bf16[512,128]{1,0:T(8,128)(2,1)S(1)}, u32[]{:S(2)}, u32[]{:S(2)}) collective-permute-start(bf16[512,128]{1,0:T(8,128)(2,1)S(1)} %get-tuple-element.63), channel_id=1, source_target_pairs={{0,16},{8,24},{16,0},{24,8},{1,17},{9,25},{17,1},{25,9},{2,18},{10... | collective-permute-start | bytes 393224 | tf_op jit(solution)/shard_map/ppermute | solution.py:62
  33.2 0.5 collective-permute-start.10
  33.7 2.4 %collective-permute-done.8.refs_1_ = bf16[512,128]{1,0:T(8,128)(2,1)S(1)} collective-permute-done((bf16[512,128]{1,0:T(8,128)(2,1)S(1)}, bf16[512,128]{1,0:T(8,128)(2,1)S(1)}, u32[]{:S(2)}, u32[]{:S(2)}) %collective-permute-start.8) | collective-permute-done | bytes 131104 | tf_op jit(solution)/shard_map/ppermute | solution.py:62
  36.1 3.7 %collective-permute-done.9.refs_2_ = bf16[512,128]{1,0:T(8,128)(2,1)S(1)} collective-permute-done((bf16[512,128]{1,0:T(8,128)(2,1)S(1)}, bf16[512,128]{1,0:T(8,128)(2,1)S(1)}, u32[]{:S(2)}, u32[]{:S(2)}) %collective-permute-start.9) | collective-permute-done | bytes 131104 | tf_op jit(solution)/shard_map/ppermute | solution.py:62
  39.8 11.1 %sequence.1 = (bf16[512,512]{1,0:T(8,128)(2,1)}, bf16[512,128]{1,0:T(8,128)(2,1)S(1)}, bf16[512,128]{1,0:T(8,128)(2,1)S(1)}, bf16[512,128]{1,0:T(8,128)(2,1)S(1)...) custom-call(s32[1]{0:T(128)} %bitcast.r_ref, ...), custom_call_target="tpu_custom_call" | custom-call | flops 4294967296 | bytes 9177096 | tf_op jit(solution)/shard_map/sequence/pallas_call | solution.py:36
  51.0 0.1 collective-permute-start.14
  51.0 1.3 %collective-permute-start.11 = (bf16[512,128]{1,0:T(8,128)(2,1)S(1)}, bf16[512,128]{1,0:T(8,128)(2,1)S(1)}, u32[]{:S(2)}, u32[]{:S(2)}) collective-permute-start(bf16[512,128]{1,0:T(8,128)(2,1)S(1)} %get-tuple-element.67), channel_id=1, source_target_pairs={{0,8},{8,0},{16,24},{24,16},{1,9},{9,1},{17,25},{25,17},{2,10},{10... | collective-permute-start | bytes 393224 | tf_op jit(solution)/shard_map/ppermute | solution.py:62
  52.3 0.8 collective-permute-start.12
  53.1 1.4 %collective-permute-start.13 = (bf16[512,128]{1,0:T(8,128)(2,1)S(1)}, bf16[512,128]{1,0:T(8,128)(2,1)S(1)}, u32[]{:S(2)}, u32[]{:S(2)}) collective-permute-start(bf16[512,128]{1,0:T(8,128)(2,1)S(1)} %get-tuple-element.69), channel_id=1, source_target_pairs={{0,24},{8,16},{16,8},{24,0},{1,25},{9,17},{17,9},{25,1},{2,26},{10... | collective-permute-start | bytes 393224 | tf_op jit(solution)/shard_map/ppermute | solution.py:62
  54.6 1.7 %weight_grad.1 = (f32[2,128,640]{2,1,0:T(8,128)S(1)}, bf16[2,128,640]{2,1,0:T(8,128)(2,1)S(1)}, f32[2,128,640]{2,1,0:T(8,128)S(1)}, bf16[2,128,640]{2,1,0:T(8,128)(2,1)S(1)}) custom-call(s32[1]{0:T(128)} %bitcast.r_ref, s32[1]{0:T(128)} %bitcast.1.core_ref, bf16[512,512]{1,0:T(8,128)(2,1)S(1)} %get-tuple-element.70.n_ref, ...), custom_call_target="tpu_custom_call" | custom-call | flops 939524096 | bytes 6946824 | tf_op jit(solution)/shard_map/weight_grad/pallas_call | solution.py:36
  56.3 1.1 %collective-permute-done.11.refs_1_ = bf16[512,128]{1,0:T(8,128)(2,1)S(1)} collective-permute-done((bf16[512,128]{1,0:T(8,128)(2,1)S(1)}, bf16[512,128]{1,0:T(8,128)(2,1)S(1)}, u32[]{:S(2)}, u32[]{:S(2)}) %collective-permute-start.11) | collective-permute-done | bytes 131104 | tf_op jit(solution)/shard_map/ppermute | solution.py:62
  57.4 1.7 %collective-permute-done.12.refs_2_ = bf16[512,128]{1,0:T(8,128)(2,1)S(1)} collective-permute-done((bf16[512,128]{1,0:T(8,128)(2,1)S(1)}, bf16[512,128]{1,0:T(8,128)(2,1)S(1)}, u32[]{:S(2)}, u32[]{:S(2)}) %collective-permute-start.12) | collective-permute-done | bytes 131104 | tf_op jit(solution)/shard_map/ppermute | solution.py:62
  59.1 1.6 %collective-permute-done.13.refs_3_ = bf16[512,128]{1,0:T(8,128)(2,1)S(1)} collective-permute-done((bf16[512,128]{1,0:T(8,128)(2,1)S(1)}, bf16[512,128]{1,0:T(8,128)(2,1)S(1)}, u32[]{:S(2)}, u32[]{:S(2)}) %collective-permute-start.13) | collective-permute-done | bytes 131104 | tf_op jit(solution)/shard_map/ppermute | solution.py:62
  60.7 0.1 collective-permute-start.15
  60.8 0.9 collective-permute-start.19
  61.7 1.5 %collective-permute-start.20 = (bf16[2,128,640]{2,1,0:T(8,128)(2,1)S(1)}, bf16[2,128,640]{2,1,0:T(8,128)(2,1)S(1)}, u32[]{:S(2)}, u32[]{:S(2)}) collective-permute-start(bf16[2,128,640]{2,1,0:T(8,128)(2,1)S(1)} %get-tuple-element.77), channel_id=1, source_target_pairs={{0,16},{8,24},{16,0},{24,8},{1,17},{9,25},{17,1},{25,9},{2,18},{10... | collective-permute-start | bytes 983048 | tf_op jit(solution)/shard_map/ppermute | solution.py:62
  63.2 1.2 %gather_grad.5.refs_1_ = bf16[1024,128]{1,0:T(8,128)(2,1)S(1)} custom-call(s32[1]{0:T(128)S(6)} %mul.35.base_ref, s32[4,2,2,512]{3,2,1,0:T(2,128)S(1)} %pad_add_fusion.key_ref, bf16[4,512,128]{2,1,0:T(8,128)(2,1)S(1)} %pack.1.refs_0_), custom_call_target="tpu_custom_call" | custom-call | flops 1073741824 | bytes 819204 | tf_op jit(solution)/shard_map/gather_grad/pallas_call | solution.py:36
  64.4 1.2 %gather_grad.6 = bf16[1024,128]{1,0:T(8,128)(2,1)S(1)} custom-call(s32[1]{0:T(128)S(6)} %mul.35.base_ref, s32[4,2,2,512]{3,2,1,0:T(2,128)S(1)} %pad_add_fusion.key_ref, bf16[4,512,128]{2,1,0:T(8,128)(2,1)S(1)} %collective-permute-done.15.refs_0_.refs_1_, bf16[1024,128]{1,0:T(8,128)(2,1)S(1)} %gather_grad.5.refs_1_), custom_call_target="tpu_custom_call" | custom-call | flops 1073741824 | bytes 1081348 | tf_op jit(solution)/shard_map/gather_grad/pallas_call | solution.py:36
  65.7 1.5 %collective-permute-start.16 = (bf16[1024,128]{1,0:T(8,128)(2,1)S(1)}, bf16[1024,128]{1,0:T(8,128)(2,1)S(1)}, u32[]{:S(2)}, u32[]{:S(2)}) collective-permute-start(bf16[1024,128]{1,0:T(8,128)(2,1)S(1)} %gather_grad.6), channel_id=1, source_target_pairs={{0,2},{1,3},{2,0},{3,1},{4,6},{5,7},{6,4},{7,5},{8,10},{9,11},{10,... | collective-permute-start | bytes 786440 | tf_op jit(solution)/shard_map/ppermute | solution.py:66
  67.2 2.3 %gather_grad.9 = bf16[1024,128]{1,0:T(8,128)(2,1)S(1)} custom-call(s32[1]{0:T(128)S(6)} %mul.42.base_ref, s32[4,2,2,512]{3,2,1,0:T(2,128)S(1)} %pad_add_fusion.key_ref, bf16[4,512,128]{2,1,0:T(8,128)(2,1)S(1)} %pack.1.refs_0_, bf16[4,512,128]{2,1,0:T(8,128)(2,1)S(1)} %collective-permute-done.15.refs_0_.refs_1_), custom_call_target="tpu_custom_call" | custom-call | flops 2147483648 | bytes 1343492 | tf_op jit(solution)/shard_map/gather_grad/pallas_call | solution.py:36
  69.5 0.7 collective-permute-start.17
  70.2 0.8 collective-permute-done.19.refs_2_
  70.9 0.5 collective-permute-done.20.refs_3_
  71.5 0.2 fold.1
  71.7 1.6 %collective-permute-start.21 = (bf16[1,128,640]{2,1,0:T(8,128)(2,1)S(1)}, bf16[1,128,640]{2,1,0:T(8,128)(2,1)S(1)}, u32[]{:S(2)}, u32[]{:S(2)}) collective-permute-start(bf16[1,128,640]{2,1,0:T(8,128)(2,1)S(1)} %get-tuple-element.92), channel_id=1, source_target_pairs={{0,16},{8,24},{16,0},{24,8},{1,17},{9,25},{17,1},{25,9},{2,18},{10... | collective-permute-start | bytes 491528 | tf_op jit(solution)/shard_map/ppermute | solution.py:62
  73.3 0.5 collective-permute-start.22
  73.8 2.5 %gather_grad.7.refs_0_ = f32[1024,128]{1,0:T(8,128)S(1)} custom-call(s32[1]{0:T(128)S(6)} %mul.40.base_ref, s32[4,2,2,512]{3,2,1,0:T(2,128)S(1)} %pad_add_fusion.key_ref, bf16[4,512,128]{2,1,0:T(8,128)(2,1)S(1)} %pack.1.refs_0_, bf16[4,512,128]{2,1,0:T(8,128)(2,1)S(1)} %collective-permute-done.15.refs_0_.refs_1_), custom_call_target="tpu_custom_call" | custom-call | flops 2147483648 | bytes 1605636 | tf_op jit(solution)/shard_map/gather_grad/pallas_call | solution.py:36
  76.4 3.5 %collective-permute-start.18 = (bf16[1024,128]{1,0:T(8,128)(2,1)S(1)}, bf16[1024,128]{1,0:T(8,128)(2,1)S(1)}, u32[]{:S(2)}, u32[]{:S(2)}) collective-permute-start(bf16[1024,128]{1,0:T(8,128)(2,1)S(1)} %add_up.2), channel_id=1, source_target_pairs={{0,4},{1,5},{2,6},{3,7},{4,0},{5,1},{6,2},{7,3},{8,12},{9,13},{10,... | collective-permute-start | bytes 786440 | tf_op jit(solution)/shard_map/ppermute | solution.py:66
  80.0 0.1 cut_line.1
  80.1 0.1 collective-permute-start.23
  80.2 2.3 %gather_grad.8.here_ref = f32[1024,128]{1,0:T(8,128)S(1)} custom-call(s32[1]{0:T(128)S(6)} %mul.44.base_ref, s32[4,2,2,512]{3,2,1,0:T(2,128)S(1)} %pad_add_fusion.key_ref, bf16[4,512,128]{2,1,0:T(8,128)(2,1)S(1)} %pack.1.refs_0_, bf16[4,512,128]{2,1,0:T(8,128)(2,1)S(1)} %collective-permute-done.15.refs_0_.refs_1_), custom_call_target="tpu_custom_call" | custom-call | flops 2147483648 | bytes 1605636 | tf_op jit(solution)/shard_map/gather_grad/pallas_call | solution.py:36
  82.5 5.6 %collective-permute-done.23.came_ref = bf16[2,64,640]{2,1,0:T(8,128)(2,1)S(1)} collective-permute-done((bf16[2,64,640]{2,1,0:T(8,128)(2,1)S(1)}, bf16[2,64,640]{2,1,0:T(8,128)(2,1)S(1)}, u32[]{:S(2)}, u32[]{:S(2)}) %collective-permute-start.23) | collective-permute-done | bytes 163872 | tf_op jit(solution)/shard_map/ppermute | solution.py:66
  88.1 4.1 %collective-permute-start.24 = (bf16[1,64,640]{2,1,0:T(8,128)(2,1)S(1)}, bf16[1,64,640]{2,1,0:T(8,128)(2,1)S(1)}, u32[]{:S(2)}, u32[]{:S(2)}) collective-permute-start(bf16[1,64,640]{2,1,0:T(8,128)(2,1)S(1)} %get-tuple-element.100), channel_id=1, source_target_pairs={{0,4},{1,5},{2,6},{3,7},{4,0},{5,1},{6,2},{7,3},{8,12},{9,13},{10,... | collective-permute-start | bytes 245768 | tf_op jit(solution)/shard_map/ppermute | solution.py:66
  92.2 0.1 table_sums.2.here_ref
  92.3 2.4 %collective-permute-done.24 = bf16[1,64,640]{2,1,0:T(8,128)(2,1)S(1)} collective-permute-done((bf16[1,64,640]{2,1,0:T(8,128)(2,1)S(1)}, bf16[1,64,640]{2,1,0:T(8,128)(2,1)S(1)}, u32[]{:S(2)}, u32[]{:S(2)}) %collective-permute-start.24) | collective-permute-done | bytes 81952 | tf_op jit(solution)/shard_map/ppermute | solution.py:66
  94.7 1.2 %collective-permute-start.27 = (bf16[64,640]{1,0:T(8,128)(2,1)S(1)}, bf16[64,640]{1,0:T(8,128)(2,1)S(1)}, u32[]{:S(2)}, u32[]{:S(2)}) collective-permute-start(bf16[64,640]{1,0:T(8,128)(2,1)S(1)} %add_up.3.refs_0_), channel_id=1, source_target_pairs={{0,24},{8,16},{16,8},{24,0},{1,25},{9,17},{17,9},{25,1},{2,26},{10... | collective-permute-start | bytes 245768 | tf_op jit(solution)/shard_map/ppermute | solution.py:62
  95.9 0.9 collective-permute-start.26
  96.8 1.4 %collective-permute-start.25 = (bf16[64,640]{1,0:T(8,128)(2,1)S(1)}, bf16[64,640]{1,0:T(8,128)(2,1)S(1)}, u32[]{:S(2)}, u32[]{:S(2)}) collective-permute-start(bf16[64,640]{1,0:T(8,128)(2,1)S(1)} %add_up.3.refs_0_), channel_id=1, source_target_pairs={{0,8},{8,0},{16,24},{24,16},{1,9},{9,1},{17,25},{25,17},{2,10},{10... | collective-permute-start | bytes 245768 | tf_op jit(solution)/shard_map/ppermute | solution.py:62
  98.2 0.8 table_sums.3
  99.1 1.1 %collective-permute-done.27.refs_3_ = bf16[64,640]{1,0:T(8,128)(2,1)S(1)} collective-permute-done((bf16[64,640]{1,0:T(8,128)(2,1)S(1)}, bf16[64,640]{1,0:T(8,128)(2,1)S(1)}, u32[]{:S(2)}, u32[]{:S(2)}) %collective-permute-start.27) | collective-permute-done | bytes 81952 | tf_op jit(solution)/shard_map/ppermute | solution.py:62
  100.1 0.8 collective-permute-done.26.refs_2_
  100.9 0.3 collective-permute-done.25.refs_1_
  101.2 0.9 assemble.1
  (29 shorter events, 0.2 us)
Async XLA Ops:
  1.7 16.1 %collective-permute-start = (bf16[1024,128]{1,0:T(8,128)(2,1)S(1)}, bf16[1024,128]{1,0:T(8,128)(2,1)S(1)}, u32[]{:S(2)}, u32[]{:S(2)}) collective-permute-start(bf16[1024,128]{1,0:T(8,128)(2,1)S(1)} %pad_maximum_fusion.chunk_ref), channel_id=1, source_target_pairs={{0,4},{1,5},{2,6},{3,7},{4,0},{5,1},{6,2},{7,3},{8,12},{9,13},{10,... | collective-permute-start | bytes 786440 | tf_op jit(solution)/shard_map/ppermute | solution.py:66
  6.5 1.7 %collective-permute-start.2 = (s32[2,512]{1,0:T(2,128)S(1)}, s32[2,512]{1,0:T(2,128)S(1)}, u32[]{:S(2)}, u32[]{:S(2)}) collective-permute-start(s32[2,512]{1,0:T(2,128)S(1)} %get-tuple-element.108), channel_id=1, source_target_pairs={{0,1},{1,0},{2,3},{3,2},{4,5},{5,4},{6,7},{7,6},{8,9},{9,8},{10,11... | collective-permute-start | bytes 12296 | tf_op jit(solution)/shard_map/ppermute | solution.py:69
  6.6 15.5 %collective-permute-start.6 = (bf16[1024,128]{1,0:T(8,128)(2,1)S(1)}, bf16[1024,128]{1,0:T(8,128)(2,1)S(1)}, u32[]{:S(2)}, u32[]{:S(2)}) collective-permute-start(bf16[1024,128]{1,0:T(8,128)(2,1)S(1)} %pad_maximum_fusion.chunk_ref), channel_id=1, source_target_pairs={{0,2},{1,3},{2,0},{3,1},{4,6},{5,7},{6,4},{7,5},{8,10},{9,11},{10,... | collective-permute-start | bytes 786440 | tf_op jit(solution)/shard_map/ppermute | solution.py:66
  8.2 10.2 %collective-permute-start.4 = (s32[2,2,512]{2,1,0:T(2,128)S(1)}, s32[2,2,512]{2,1,0:T(2,128)S(1)}, u32[]{:S(2)}, u32[]{:S(2)}) collective-permute-start(s32[2,2,512]{2,1,0:T(2,128)S(1)} %get-tuple-element.106), channel_id=1, source_target_pairs={{0,16},{8,24},{16,0},{24,8},{1,17},{9,25},{17,1},{25,9},{2,18},{10... | collective-permute-start | bytes 24584 | tf_op jit(solution)/shard_map/ppermute | solution.py:62
  9.8 8.6 %collective-permute-start.3 = (s32[2,2,512]{2,1,0:T(2,128)S(1)}, s32[2,2,512]{2,1,0:T(2,128)S(1)}, u32[]{:S(2)}, u32[]{:S(2)}) collective-permute-start(s32[2,2,512]{2,1,0:T(2,128)S(1)} %get-tuple-element.106), channel_id=1, source_target_pairs={{0,8},{8,0},{16,24},{24,16},{1,9},{9,1},{17,25},{25,17},{2,10},{10... | collective-permute-start | bytes 24584 | tf_op jit(solution)/shard_map/ppermute | solution.py:62
  11.3 7.1 %collective-permute-start.5 = (s32[2,2,512]{2,1,0:T(2,128)S(1)}, s32[2,2,512]{2,1,0:T(2,128)S(1)}, u32[]{:S(2)}, u32[]{:S(2)}) collective-permute-start(s32[2,2,512]{2,1,0:T(2,128)S(1)} %get-tuple-element.106), channel_id=1, source_target_pairs={{0,24},{8,16},{16,8},{24,0},{1,25},{9,17},{17,9},{25,1},{2,26},{10... | collective-permute-start | bytes 24584 | tf_op jit(solution)/shard_map/ppermute | solution.py:62
  17.8 9.0 %collective-permute-start.1 = (bf16[1024,128]{1,0:T(8,128)(2,1)S(1)}, bf16[1024,128]{1,0:T(8,128)(2,1)S(1)}, u32[]{:S(2)}, u32[]{:S(2)}) collective-permute-start(bf16[1024,128]{1,0:T(8,128)(2,1)S(1)} %collective-permute-done.chunk_ref), channel_id=1, source_target_pairs={{0,2},{1,3},{2,0},{3,1},{4,6},{5,7},{6,4},{7,5},{8,10},{9,11},{10,... | collective-permute-start | bytes 786440 | tf_op jit(solution)/shard_map/ppermute | solution.py:66
  28.0 2.0 %collective-permute-start.7 = (bf16[4,512,128]{2,1,0:T(8,128)(2,1)S(1)}, bf16[4,512,128]{2,1,0:T(8,128)(2,1)S(1)}, u32[]{:S(2)}, u32[]{:S(2)}) collective-permute-start(bf16[4,512,128]{2,1,0:T(8,128)(2,1)S(1)} %fetch.9), channel_id=1, source_target_pairs={{0,1},{1,0},{2,3},{3,2},{4,5},{5,4},{6,7},{7,6},{8,9},{9,8},{10,11... | collective-permute-start | bytes 1572872 | tf_op jit(solution)/shard_map/ppermute | solution.py:69
  28.1 11.7 %copy-start = (bf16[512,512]{1,0:T(8,128)(2,1)S(1)}, bf16[512,512]{1,0:T(8,128)(2,1)}, u32[]{:S(2)}) copy-start(bf16[512,512]{1,0:T(8,128)(2,1)} %c_ref.1) | copy-start | bytes 1572868
  28.1 11.7 %copy-start.1 = (bf16[512,2048]{1,0:T(8,128)(2,1)S(1)}, bf16[512,2048]{1,0:T(8,128)(2,1)}, u32[]{:S(2)}) copy-start(bf16[512,2048]{1,0:T(8,128)(2,1)} %wp_ref.1) | copy-start | bytes 6291460
  28.1 11.7 %copy-start.2 = (bf16[512,512]{1,0:T(8,128)(2,1)S(1)}, bf16[512,512]{1,0:T(8,128)(2,1)}, u32[]{:S(2)}) copy-start(bf16[512,512]{1,0:T(8,128)(2,1)} %wo_ref.1) | copy-start | bytes 1572868
  28.1 11.7 %copy-start.3 = (f32[512]{0:T(512)S(1)}, f32[512]{0:T(512)}, u32[]{:S(2)}) copy-start(f32[512]{0:T(512)} %param.16) | copy-start | bytes 6148
  30.1 5.9 %collective-permute-start.8 = (bf16[512,128]{1,0:T(8,128)(2,1)S(1)}, bf16[512,128]{1,0:T(8,128)(2,1)S(1)}, u32[]{:S(2)}, u32[]{:S(2)}) collective-permute-start(bf16[512,128]{1,0:T(8,128)(2,1)S(1)} %get-tuple-element.62), channel_id=1, source_target_pairs={{0,8},{8,0},{16,24},{24,16},{1,9},{9,1},{17,25},{25,17},{2,10},{10... | collective-permute-start | bytes 393224 | tf_op jit(solution)/shard_map/ppermute | solution.py:62
  31.7 8.1 %collective-permute-start.9 = (bf16[512,128]{1,0:T(8,128)(2,1)S(1)}, bf16[512,128]{1,0:T(8,128)(2,1)S(1)}, u32[]{:S(2)}, u32[]{:S(2)}) collective-permute-start(bf16[512,128]{1,0:T(8,128)(2,1)S(1)} %get-tuple-element.63), channel_id=1, source_target_pairs={{0,16},{8,24},{16,0},{24,8},{1,17},{9,25},{17,1},{25,9},{2,18},{10... | collective-permute-start | bytes 393224 | tf_op jit(solution)/shard_map/ppermute | solution.py:62
  33.2 6.6 %collective-permute-start.10 = (bf16[512,128]{1,0:T(8,128)(2,1)S(1)}, bf16[512,128]{1,0:T(8,128)(2,1)S(1)}, u32[]{:S(2)}, u32[]{:S(2)}) collective-permute-start(bf16[512,128]{1,0:T(8,128)(2,1)S(1)} %get-tuple-element.64), channel_id=1, source_target_pairs={{0,24},{8,16},{16,8},{24,0},{1,25},{9,17},{17,9},{25,1},{2,26},{10... | collective-permute-start | bytes 393224 | tf_op jit(solution)/shard_map/ppermute | solution.py:62
  51.0 3.6 %collective-permute-start.14 = (bf16[4,256,640]{2,1,0:T(8,128)(2,1)S(1)}, bf16[4,256,640]{2,1,0:T(8,128)(2,1)S(1)}, u32[]{:S(2)}, u32[]{:S(2)}) collective-permute-start(bf16[4,256,640]{2,1,0:T(8,128)(2,1)S(1)} %get-tuple-element.73), channel_id=1, source_target_pairs={{0,1},{1,0},{2,3},{3,2},{4,5},{5,4},{6,7},{7,6},{8,9},{9,8},{10,11... | collective-permute-start | bytes 3932168 | tf_op jit(solution)/shard_map/ppermute | solution.py:69
  51.0 6.4 %collective-permute-start.11 = (bf16[512,128]{1,0:T(8,128)(2,1)S(1)}, bf16[512,128]{1,0:T(8,128)(2,1)S(1)}, u32[]{:S(2)}, u32[]{:S(2)}) collective-permute-start(bf16[512,128]{1,0:T(8,128)(2,1)S(1)} %get-tuple-element.67), channel_id=1, source_target_pairs={{0,8},{8,0},{16,24},{24,16},{1,9},{9,1},{17,25},{25,17},{2,10},{10... | collective-permute-start | bytes 393224 | tf_op jit(solution)/shard_map/ppermute | solution.py:62
  52.3 6.8 %collective-permute-start.12 = (bf16[512,128]{1,0:T(8,128)(2,1)S(1)}, bf16[512,128]{1,0:T(8,128)(2,1)S(1)}, u32[]{:S(2)}, u32[]{:S(2)}) collective-permute-start(bf16[512,128]{1,0:T(8,128)(2,1)S(1)} %get-tuple-element.68), channel_id=1, source_target_pairs={{0,16},{8,24},{16,0},{24,8},{1,17},{9,25},{17,1},{25,9},{2,18},{10... | collective-permute-start | bytes 393224 | tf_op jit(solution)/shard_map/ppermute | solution.py:62
  53.1 7.6 %collective-permute-start.13 = (bf16[512,128]{1,0:T(8,128)(2,1)S(1)}, bf16[512,128]{1,0:T(8,128)(2,1)S(1)}, u32[]{:S(2)}, u32[]{:S(2)}) collective-permute-start(bf16[512,128]{1,0:T(8,128)(2,1)S(1)} %get-tuple-element.69), channel_id=1, source_target_pairs={{0,24},{8,16},{16,8},{24,0},{1,25},{9,17},{17,9},{25,1},{2,26},{10... | collective-permute-start | bytes 393224 | tf_op jit(solution)/shard_map/ppermute | solution.py:62
  60.7 3.7 %collective-permute-start.15 = (bf16[4,512,128]{2,1,0:T(8,128)(2,1)S(1)}, bf16[4,512,128]{2,1,0:T(8,128)(2,1)S(1)}, u32[]{:S(2)}, u32[]{:S(2)}) collective-permute-start(bf16[4,512,128]{2,1,0:T(8,128)(2,1)S(1)} %pack.1.refs_0_), channel_id=1, source_target_pairs={{0,1},{1,0},{2,3},{3,2},{4,5},{5,4},{6,7},{7,6},{8,9},{9,8},{10,11... | collective-permute-start | bytes 1572872 | tf_op jit(solution)/shard_map/ppermute | solution.py:69
  60.8 10.1 %collective-permute-start.19 = (bf16[2,128,640]{2,1,0:T(8,128)(2,1)S(1)}, bf16[2,128,640]{2,1,0:T(8,128)(2,1)S(1)}, u32[]{:S(2)}, u32[]{:S(2)}) collective-permute-start(bf16[2,128,640]{2,1,0:T(8,128)(2,1)S(1)} %get-tuple-element.75), channel_id=1, source_target_pairs={{0,8},{8,0},{16,24},{24,16},{1,9},{9,1},{17,25},{25,17},{2,10},{10... | collective-permute-start | bytes 983048 | tf_op jit(solution)/shard_map/ppermute | solution.py:62
  61.7 9.8 %collective-permute-start.20 = (bf16[2,128,640]{2,1,0:T(8,128)(2,1)S(1)}, bf16[2,128,640]{2,1,0:T(8,128)(2,1)S(1)}, u32[]{:S(2)}, u32[]{:S(2)}) collective-permute-start(bf16[2,128,640]{2,1,0:T(8,128)(2,1)S(1)} %get-tuple-element.77), channel_id=1, source_target_pairs={{0,16},{8,24},{16,0},{24,8},{1,17},{9,25},{17,1},{25,9},{2,18},{10... | collective-permute-start | bytes 983048 | tf_op jit(solution)/shard_map/ppermute | solution.py:62
  65.7 10.7 %collective-permute-start.16 = (bf16[1024,128]{1,0:T(8,128)(2,1)S(1)}, bf16[1024,128]{1,0:T(8,128)(2,1)S(1)}, u32[]{:S(2)}, u32[]{:S(2)}) collective-permute-start(bf16[1024,128]{1,0:T(8,128)(2,1)S(1)} %gather_grad.6), channel_id=1, source_target_pairs={{0,2},{1,3},{2,0},{3,1},{4,6},{5,7},{6,4},{7,5},{8,10},{9,11},{10,... | collective-permute-start | bytes 786440 | tf_op jit(solution)/shard_map/ppermute | solution.py:66
  69.5 22.7 %collective-permute-start.17 = (bf16[1024,128]{1,0:T(8,128)(2,1)S(1)}, bf16[1024,128]{1,0:T(8,128)(2,1)S(1)}, u32[]{:S(2)}, u32[]{:S(2)}) collective-permute-start(bf16[1024,128]{1,0:T(8,128)(2,1)S(1)} %gather_grad.9), channel_id=1, source_target_pairs={{0,2},{1,3},{2,0},{3,1},{4,6},{5,7},{6,4},{7,5},{8,10},{9,11},{10,... | collective-permute-start | bytes 786440 | tf_op jit(solution)/shard_map/ppermute | solution.py:66
  71.7 8.2 %collective-permute-start.21 = (bf16[1,128,640]{2,1,0:T(8,128)(2,1)S(1)}, bf16[1,128,640]{2,1,0:T(8,128)(2,1)S(1)}, u32[]{:S(2)}, u32[]{:S(2)}) collective-permute-start(bf16[1,128,640]{2,1,0:T(8,128)(2,1)S(1)} %get-tuple-element.92), channel_id=1, source_target_pairs={{0,16},{8,24},{16,0},{24,8},{1,17},{9,25},{17,1},{25,9},{2,18},{10... | collective-permute-start | bytes 491528 | tf_op jit(solution)/shard_map/ppermute | solution.py:62
  73.3 6.7 %collective-permute-start.22 = (bf16[1,128,640]{2,1,0:T(8,128)(2,1)S(1)}, bf16[1,128,640]{2,1,0:T(8,128)(2,1)S(1)}, u32[]{:S(2)}, u32[]{:S(2)}) collective-permute-start(bf16[1,128,640]{2,1,0:T(8,128)(2,1)S(1)} %get-tuple-element.93), channel_id=1, source_target_pairs={{0,8},{8,0},{16,24},{24,16},{1,9},{9,1},{17,25},{25,17},{2,10},{10... | collective-permute-start | bytes 491528 | tf_op jit(solution)/shard_map/ppermute | solution.py:62
  76.4 21.8 %collective-permute-start.18 = (bf16[1024,128]{1,0:T(8,128)(2,1)S(1)}, bf16[1024,128]{1,0:T(8,128)(2,1)S(1)}, u32[]{:S(2)}, u32[]{:S(2)}) collective-permute-start(bf16[1024,128]{1,0:T(8,128)(2,1)S(1)} %add_up.2), channel_id=1, source_target_pairs={{0,4},{1,5},{2,6},{3,7},{4,0},{5,1},{6,2},{7,3},{8,12},{9,13},{10,... | collective-permute-start | bytes 786440 | tf_op jit(solution)/shard_map/ppermute | solution.py:66
  80.1 8.0 %collective-permute-start.23 = (bf16[2,64,640]{2,1,0:T(8,128)(2,1)S(1)}, bf16[2,64,640]{2,1,0:T(8,128)(2,1)S(1)}, u32[]{:S(2)}, u32[]{:S(2)}) collective-permute-start(bf16[2,64,640]{2,1,0:T(8,128)(2,1)S(1)} %get-tuple-element.97), channel_id=1, source_target_pairs={{0,2},{1,3},{2,0},{3,1},{4,6},{5,7},{6,4},{7,5},{8,10},{9,11},{10,... | collective-permute-start | bytes 491528 | tf_op jit(solution)/shard_map/ppermute | solution.py:66
  88.1 6.5 %collective-permute-start.24 = (bf16[1,64,640]{2,1,0:T(8,128)(2,1)S(1)}, bf16[1,64,640]{2,1,0:T(8,128)(2,1)S(1)}, u32[]{:S(2)}, u32[]{:S(2)}) collective-permute-start(bf16[1,64,640]{2,1,0:T(8,128)(2,1)S(1)} %get-tuple-element.100), channel_id=1, source_target_pairs={{0,4},{1,5},{2,6},{3,7},{4,0},{5,1},{6,2},{7,3},{8,12},{9,13},{10,... | collective-permute-start | bytes 245768 | tf_op jit(solution)/shard_map/ppermute | solution.py:66
  94.7 5.5 %collective-permute-start.27 = (bf16[64,640]{1,0:T(8,128)(2,1)S(1)}, bf16[64,640]{1,0:T(8,128)(2,1)S(1)}, u32[]{:S(2)}, u32[]{:S(2)}) collective-permute-start(bf16[64,640]{1,0:T(8,128)(2,1)S(1)} %add_up.3.refs_0_), channel_id=1, source_target_pairs={{0,24},{8,16},{16,8},{24,0},{1,25},{9,17},{17,9},{25,1},{2,26},{10... | collective-permute-start | bytes 245768 | tf_op jit(solution)/shard_map/ppermute | solution.py:62
  95.9 5.1 %collective-permute-start.26 = (bf16[64,640]{1,0:T(8,128)(2,1)S(1)}, bf16[64,640]{1,0:T(8,128)(2,1)S(1)}, u32[]{:S(2)}, u32[]{:S(2)}) collective-permute-start(bf16[64,640]{1,0:T(8,128)(2,1)S(1)} %add_up.3.refs_0_), channel_id=1, source_target_pairs={{0,16},{8,24},{16,0},{24,8},{1,17},{9,25},{17,1},{25,9},{2,18},{10... | collective-permute-start | bytes 245768 | tf_op jit(solution)/shard_map/ppermute | solution.py:62
  96.8 4.4 %collective-permute-start.25 = (bf16[64,640]{1,0:T(8,128)(2,1)S(1)}, bf16[64,640]{1,0:T(8,128)(2,1)S(1)}, u32[]{:S(2)}, u32[]{:S(2)}) collective-permute-start(bf16[64,640]{1,0:T(8,128)(2,1)S(1)} %add_up.3.refs_0_), channel_id=1, source_target_pairs={{0,8},{8,0},{16,24},{24,16},{1,9},{9,1},{17,25},{25,17},{2,10},{10... | collective-permute-start | bytes 245768 | tf_op jit(solution)/shard_map/ppermute | solution.py:62

commit v13 on v12

--- a/solution.py
+++ b/solution.py
@@ -558,7 +558,7 @@
             sums[k] = add_up(raw[k] + came) if steps else raw[k][0]
 
     for step in range(1, bits + 1):
-        after = raw[1] if step < bits else [raw[1], sums[line // 2]]
+        after = raw[1] if step < bits else [raw[1], raw[line // 2]]
         swapped = lax.optimization_barrier((swapped, after))[0]
         if step < bits:
             kept, swapped = swap_weights(fold(replica, kept, swapped, step), step)
@@ -569,7 +569,7 @@
         kept, sent = fold_line(kept, came)
         step *= 2
     parts = [kept[0], grid.over_line(sent, step)[0]]
-    parts = lax.optimization_barrier((parts, raw[0]))[0]
+    parts = lax.optimization_barrier((parts, table))[0]
     total = add_up(parts)
     parts = [total] + [grid.over_replica(total, k) for k in range(1, replicas)]
     grad_proj, grad_out = assemble(replica, parts, 4 * width)

time: 102 us -> 105 us (1.029)
  waiting for transfers between devices: 28.5 us -> 32.6 us
  starting transfers between devices: 35.2 us -> 33.9 us
    ppermute x16, waiting for transfers between devices: 13.9 us -> 17 us  [over_replica(): return lax.ppermute(value, 'replica', [(i, i ^ step) for i in range(n)])]
    ppermute x8, starting transfers between devices: 16.3 us -> 14.9 us  [over_line(): return lax.ppermute(value, 'sparse', pairs)]
  transfers between devices with their start and end apart: 28 -> 28, of which waited for: 14 -> 16; matrix products, arithmetic and copies ran while one was open for 2% -> 2% of each run, Pallas kernels for 21% -> 20%
where the time goes in v13:
time: 105 us
  Pallas kernels  34.4 us (33%)
  starting transfers between devices  33.9 us (32%)
  waiting for transfers between devices  32.6 us (31%)
  local copies, waits for them, and re-layouts  2.25 us (2%)
    pallas_call x22, Pallas kernels, run(): pl.pallas_call(body, out_shape=outs, in_specs=places, out_specs=[in_vmem]...  34.4 us
    ppermute x16, starting transfers between devices, over_replica(): return lax.ppermute(value, 'replica', [(i, i ^ step) for i in range(n)])  18.7 us
    ppermute x16, waiting for transfers between devices, over_replica(): return lax.ppermute(value, 'replica', [(i, i ^ step) for i in range(n)])  17 us
    ppermute x8, waiting for transfers between devices, over_line(): return lax.ppermute(value, 'sparse', pairs)  15 us
    ppermute x8, starting transfers between devices, over_line(): return lax.ppermute(value, 'sparse', pairs)  14.9 us
  transfers between devices with their start and end apart: 28, of which 16 were waited for; matrix products, arithmetic and copies ran while one was open for 2% of the time, Pallas kernels for 20%

profile of v13, /device:TPU:0, one launch (start us, length us, event | category | flops | bytes accessed | tf_op | source)
XLA Modules:
  0.0 104.9 jit_solution(3631413274476369160)
XLA Ops:
  0.6 1.0 constant_dynamic-slice_fusion
  1.7 4.1 %collective-permute-start = (bf16[1024,128]{1,0:T(8,128)(2,1)S(1)}, bf16[1024,128]{1,0:T(8,128)(2,1)S(1)}, u32[]{:S(2)}, u32[]{:S(2)}) collective-permute-start(bf16[1024,128]{1,0:T(8,128)(2,1)S(1)} %pad_maximum_fusion.chunk_ref), channel_id=1, source_target_pairs={{0,4},{1,5},{2,6},{3,7},{4,0},{5,1},{6,2},{7,3},{8,12},{9,13},{10,... | collective-permute-start | bytes 786440 | tf_op jit(solution)/shard_map/ppermute | solution.py:66
  5.8 0.7 add_bitcast_fusion
  6.5 0.1 collective-permute-start.2
  6.6 1.6 %collective-permute-start.6 = (bf16[1024,128]{1,0:T(8,128)(2,1)S(1)}, bf16[1024,128]{1,0:T(8,128)(2,1)S(1)}, u32[]{:S(2)}, u32[]{:S(2)}) collective-permute-start(bf16[1024,128]{1,0:T(8,128)(2,1)S(1)} %pad_maximum_fusion.chunk_ref), channel_id=1, source_target_pairs={{0,2},{1,3},{2,0},{3,1},{4,6},{5,7},{6,4},{7,5},{8,10},{9,11},{10,... | collective-permute-start | bytes 786440 | tf_op jit(solution)/shard_map/ppermute | solution.py:66
  8.2 1.6 %collective-permute-start.4 = (s32[2,2,512]{2,1,0:T(2,128)S(1)}, s32[2,2,512]{2,1,0:T(2,128)S(1)}, u32[]{:S(2)}, u32[]{:S(2)}) collective-permute-start(s32[2,2,512]{2,1,0:T(2,128)S(1)} %get-tuple-element.106), channel_id=1, source_target_pairs={{0,16},{8,24},{16,0},{24,8},{1,17},{9,25},{17,1},{25,9},{2,18},{10... | collective-permute-start | bytes 24584 | tf_op jit(solution)/shard_map/ppermute | solution.py:62
  9.8 1.5 %collective-permute-start.3 = (s32[2,2,512]{2,1,0:T(2,128)S(1)}, s32[2,2,512]{2,1,0:T(2,128)S(1)}, u32[]{:S(2)}, u32[]{:S(2)}) collective-permute-start(s32[2,2,512]{2,1,0:T(2,128)S(1)} %get-tuple-element.106), channel_id=1, source_target_pairs={{0,8},{8,0},{16,24},{24,16},{1,9},{9,1},{17,25},{25,17},{2,10},{10... | collective-permute-start | bytes 24584 | tf_op jit(solution)/shard_map/ppermute | solution.py:62
  11.3 0.5 collective-permute-start.5
  11.8 6.0 %collective-permute-done.chunk_ref = bf16[1024,128]{1,0:T(8,128)(2,1)S(1)} collective-permute-done((bf16[1024,128]{1,0:T(8,128)(2,1)S(1)}, bf16[1024,128]{1,0:T(8,128)(2,1)S(1)}, u32[]{:S(2)}, u32[]{:S(2)}) %collective-permute-start) | collective-permute-done | bytes 262176 | tf_op jit(solution)/shard_map/ppermute | solution.py:66
  17.8 0.7 collective-permute-start.1
  18.5 1.2 %broadcast_in_dim.14.key_ref = s32[4,2,2,512,128]{4,3,2,1,0:T(8,128)S(1)} broadcast(s32[4,2,2,512]{3,2,1,0:T(2,128)S(1)} %pad_add_fusion.key_ref), dimensions={0,1,2,3} | broadcast | bytes 4227072 | tf_op jit(solution)/shard_map/broadcast_in_dim | solution.py:505
  19.7 2.3 %fetch.5 = (bf16[4,512,128]{2,1,0:T(8,128)(2,1)S(1)}, bf16[4,512,128]{2,1,0:T(8,128)(2,1)S(1)}) custom-call(s32[1]{0:T(128)S(6)} %mul.44.base_ref, bf16[1024,128]{1,0:T(8,128)(2,1)S(1)} %pad_maximum_fusion.chunk_ref, s32[4,2,2,512,128]{4,3,2,1,0:T(8,128)S(1)} %broadcast_in_dim.14.key_ref), custom_call_target="tpu_custom_call" | custom-call | flops 536870912 | bytes 5505028 | tf_op jit(solution)/shard_map/fetch/pallas_call | solution.py:36
  22.1 2.3 %fetch.6 = (bf16[4,512,128]{2,1,0:T(8,128)(2,1)S(1)}, bf16[4,512,128]{2,1,0:T(8,128)(2,1)S(1)}) custom-call(s32[1]{0:T(128)S(6)} %mul.42.base_ref, bf16[1024,128]{1,0:T(8,128)(2,1)S(1)} %collective-permute-done.6.chunk_ref, s32[4,2,2,512,128]{4,3,2,1,0:T(8,128)S(1)} %broadcast_in_dim.14.key_ref, bf16[4,512,128]{2,1,0:T(8,128)(2,1)S(1)} %get-tuple-element.55.refs_0_, ...), custom_call_target="tpu_custom_call" | custom-call | flops 536870912 | bytes 6553604 | tf_op jit(solution)/shard_map/fetch/pallas_call | solution.py:36
  24.4 2.3 %fetch.7 = (bf16[4,512,128]{2,1,0:T(8,128)(2,1)S(1)}, bf16[4,512,128]{2,1,0:T(8,128)(2,1)S(1)}) custom-call(s32[1]{0:T(128)S(6)} %mul.40.base_ref, bf16[1024,128]{1,0:T(8,128)(2,1)S(1)} %collective-permute-done.chunk_ref, s32[4,2,2,512,128]{4,3,2,1,0:T(8,128)S(1)} %broadcast_in_dim.14.key_ref, bf16[4,512,128]{2,1,0:T(8,128)(2,1)S(1)} %get-tuple-element.57.refs_0_, ...), custom_call_target="tpu_custom_call" | custom-call | flops 536870912 | bytes 6553604 | tf_op jit(solution)/shard_map/fetch/pallas_call | solution.py:36
  26.8 1.3 %fetch.9 = bf16[4,512,128]{2,1,0:T(8,128)(2,1)S(1)} custom-call(s32[1]{0:T(128)S(6)} %mul.35.base_ref, bf16[1024,128]{1,0:T(8,128)(2,1)S(1)} %collective-permute-done.1.chunk_ref, s32[4,2,2,512,128]{4,3,2,1,0:T(8,128)S(1)} %broadcast_in_dim.14.key_ref, bf16[4,512,128]{2,1,0:T(8,128)(2,1)S(1)} %get-tuple-element.60.refs_0_), custom_call_target="tpu_custom_call" | custom-call | flops 268435456 | bytes 5505028 | tf_op jit(solution)/shard_map/fetch/pallas_call | solution.py:36
  28.0 0.1 collective-permute-start.7
  28.2 1.2 %fetch.8.left_ref = bf16[4,512,128]{2,1,0:T(8,128)(2,1)S(1)} custom-call(s32[1]{0:T(128)S(6)} %mul.35.base_ref, bf16[1024,128]{1,0:T(8,128)(2,1)S(1)} %collective-permute-done.1.chunk_ref, s32[4,2,2,512,128]{4,3,2,1,0:T(8,128)S(1)} %broadcast_in_dim.14.key_ref, bf16[4,512,128]{2,1,0:T(8,128)(2,1)S(1)} %get-tuple-element.59.refs_0_), custom_call_target="tpu_custom_call" | custom-call | flops 268435456 | bytes 5505028 | tf_op jit(solution)/shard_map/fetch/pallas_call | solution.py:36
  29.4 0.6 collective-permute-done.7.right_ref
  30.0 0.1 combine.1
  30.1 1.6 %collective-permute-start.8 = (bf16[512,128]{1,0:T(8,128)(2,1)S(1)}, bf16[512,128]{1,0:T(8,128)(2,1)S(1)}, u32[]{:S(2)}, u32[]{:S(2)}) collective-permute-start(bf16[512,128]{1,0:T(8,128)(2,1)S(1)} %get-tuple-element.62), channel_id=1, source_target_pairs={{0,8},{8,0},{16,24},{24,16},{1,9},{9,1},{17,25},{25,17},{2,10},{10... | collective-permute-start | bytes 393224 | tf_op jit(solution)/shard_map/ppermute | solution.py:62
  31.7 1.5 %collective-permute-start.9 = (bf16[512,128]{1,0:T(8,128)(2,1)S(1)}, bf16[512,128]{1,0:T(8,128)(2,1)S(1)}, u32[]{:S(2)}, u32[]{:S(2)}) collective-permute-start(bf16[512,128]{1,0:T(8,128)(2,1)S(1)} %get-tuple-element.63), channel_id=1, source_target_pairs={{0,16},{8,24},{16,0},{24,8},{1,17},{9,25},{17,1},{25,9},{2,18},{10... | collective-permute-start | bytes 393224 | tf_op jit(solution)/shard_map/ppermute | solution.py:62
  33.2 0.5 collective-permute-start.10
  33.7 2.4 %collective-permute-done.8.refs_1_ = bf16[512,128]{1,0:T(8,128)(2,1)S(1)} collective-permute-done((bf16[512,128]{1,0:T(8,128)(2,1)S(1)}, bf16[512,128]{1,0:T(8,128)(2,1)S(1)}, u32[]{:S(2)}, u32[]{:S(2)}) %collective-permute-start.8) | collective-permute-done | bytes 131104 | tf_op jit(solution)/shard_map/ppermute | solution.py:62
  36.1 3.7 %collective-permute-done.9.refs_2_ = bf16[512,128]{1,0:T(8,128)(2,1)S(1)} collective-permute-done((bf16[512,128]{1,0:T(8,128)(2,1)S(1)}, bf16[512,128]{1,0:T(8,128)(2,1)S(1)}, u32[]{:S(2)}, u32[]{:S(2)}) %collective-permute-start.9) | collective-permute-done | bytes 131104 | tf_op jit(solution)/shard_map/ppermute | solution.py:62
  39.8 11.1 %sequence.1 = (bf16[512,512]{1,0:T(8,128)(2,1)}, bf16[512,128]{1,0:T(8,128)(2,1)S(1)}, bf16[512,128]{1,0:T(8,128)(2,1)S(1)}, bf16[512,128]{1,0:T(8,128)(2,1)S(1)...) custom-call(s32[1]{0:T(128)} %bitcast.r_ref, ...), custom_call_target="tpu_custom_call" | custom-call | flops 4294967296 | bytes 9177096 | tf_op jit(solution)/shard_map/sequence/pallas_call | solution.py:36
  51.0 0.1 collective-permute-start.14
  51.0 1.3 %collective-permute-start.11 = (bf16[512,128]{1,0:T(8,128)(2,1)S(1)}, bf16[512,128]{1,0:T(8,128)(2,1)S(1)}, u32[]{:S(2)}, u32[]{:S(2)}) collective-permute-start(bf16[512,128]{1,0:T(8,128)(2,1)S(1)} %get-tuple-element.67), channel_id=1, source_target_pairs={{0,8},{8,0},{16,24},{24,16},{1,9},{9,1},{17,25},{25,17},{2,10},{10... | collective-permute-start | bytes 393224 | tf_op jit(solution)/shard_map/ppermute | solution.py:62
  52.3 0.8 collective-permute-start.12
  53.1 1.4 %collective-permute-start.13 = (bf16[512,128]{1,0:T(8,128)(2,1)S(1)}, bf16[512,128]{1,0:T(8,128)(2,1)S(1)}, u32[]{:S(2)}, u32[]{:S(2)}) collective-permute-start(bf16[512,128]{1,0:T(8,128)(2,1)S(1)} %get-tuple-element.69), channel_id=1, source_target_pairs={{0,24},{8,16},{16,8},{24,0},{1,25},{9,17},{17,9},{25,1},{2,26},{10... | collective-permute-start | bytes 393224 | tf_op jit(solution)/shard_map/ppermute | solution.py:62
  54.6 1.7 %weight_grad.1 = (f32[2,128,640]{2,1,0:T(8,128)S(1)}, bf16[2,128,640]{2,1,0:T(8,128)(2,1)S(1)}, f32[2,128,640]{2,1,0:T(8,128)S(1)}, bf16[2,128,640]{2,1,0:T(8,128)(2,1)S(1)}) custom-call(s32[1]{0:T(128)} %bitcast.r_ref, s32[1]{0:T(128)} %bitcast.1.core_ref, bf16[512,512]{1,0:T(8,128)(2,1)S(1)} %get-tuple-element.70.n_ref, ...), custom_call_target="tpu_custom_call" | custom-call | flops 939524096 | bytes 6946824 | tf_op jit(solution)/shard_map/weight_grad/pallas_call | solution.py:36
  56.3 1.1 %collective-permute-done.11.refs_1_ = bf16[512,128]{1,0:T(8,128)(2,1)S(1)} collective-permute-done((bf16[512,128]{1,0:T(8,128)(2,1)S(1)}, bf16[512,128]{1,0:T(8,128)(2,1)S(1)}, u32[]{:S(2)}, u32[]{:S(2)}) %collective-permute-start.11) | collective-permute-done | bytes 131104 | tf_op jit(solution)/shard_map/ppermute | solution.py:62
  57.4 1.7 %collective-permute-done.12.refs_2_ = bf16[512,128]{1,0:T(8,128)(2,1)S(1)} collective-permute-done((bf16[512,128]{1,0:T(8,128)(2,1)S(1)}, bf16[512,128]{1,0:T(8,128)(2,1)S(1)}, u32[]{:S(2)}, u32[]{:S(2)}) %collective-permute-start.12) | collective-permute-done | bytes 131104 | tf_op jit(solution)/shard_map/ppermute | solution.py:62
  59.1 1.6 %collective-permute-done.13.refs_3_ = bf16[512,128]{1,0:T(8,128)(2,1)S(1)} collective-permute-done((bf16[512,128]{1,0:T(8,128)(2,1)S(1)}, bf16[512,128]{1,0:T(8,128)(2,1)S(1)}, u32[]{:S(2)}, u32[]{:S(2)}) %collective-permute-start.13) | collective-permute-done | bytes 131104 | tf_op jit(solution)/shard_map/ppermute | solution.py:62
  60.7 0.1 collective-permute-start.15
  60.8 0.9 collective-permute-start.19
  61.7 1.5 %collective-permute-start.20 = (bf16[2,128,640]{2,1,0:T(8,128)(2,1)S(1)}, bf16[2,128,640]{2,1,0:T(8,128)(2,1)S(1)}, u32[]{:S(2)}, u32[]{:S(2)}) collective-permute-start(bf16[2,128,640]{2,1,0:T(8,128)(2,1)S(1)} %get-tuple-element.77), channel_id=1, source_target_pairs={{0,16},{8,24},{16,0},{24,8},{1,17},{9,25},{17,1},{25,9},{2,18},{10... | collective-permute-start | bytes 983048 | tf_op jit(solution)/shard_map/ppermute | solution.py:62
  63.2 1.2 %gather_grad.5.refs_1_ = bf16[1024,128]{1,0:T(8,128)(2,1)S(1)} custom-call(s32[1]{0:T(128)S(6)} %mul.35.base_ref, s32[4,2,2,512]{3,2,1,0:T(2,128)S(1)} %pad_add_fusion.key_ref, bf16[4,512,128]{2,1,0:T(8,128)(2,1)S(1)} %pack.1.refs_0_), custom_call_target="tpu_custom_call" | custom-call | flops 1073741824 | bytes 819204 | tf_op jit(solution)/shard_map/gather_grad/pallas_call | solution.py:36
  64.4 1.2 %gather_grad.6 = bf16[1024,128]{1,0:T(8,128)(2,1)S(1)} custom-call(s32[1]{0:T(128)S(6)} %mul.35.base_ref, s32[4,2,2,512]{3,2,1,0:T(2,128)S(1)} %pad_add_fusion.key_ref, bf16[4,512,128]{2,1,0:T(8,128)(2,1)S(1)} %collective-permute-done.15.refs_0_.refs_1_, bf16[1024,128]{1,0:T(8,128)(2,1)S(1)} %gather_grad.5.refs_1_), custom_call_target="tpu_custom_call" | custom-call | flops 1073741824 | bytes 1081348 | tf_op jit(solution)/shard_map/gather_grad/pallas_call | solution.py:36
  65.7 1.5 %collective-permute-start.16 = (bf16[1024,128]{1,0:T(8,128)(2,1)S(1)}, bf16[1024,128]{1,0:T(8,128)(2,1)S(1)}, u32[]{:S(2)}, u32[]{:S(2)}) collective-permute-start(bf16[1024,128]{1,0:T(8,128)(2,1)S(1)} %gather_grad.6), channel_id=1, source_target_pairs={{0,2},{1,3},{2,0},{3,1},{4,6},{5,7},{6,4},{7,5},{8,10},{9,11},{10,... | collective-permute-start | bytes 786440 | tf_op jit(solution)/shard_map/ppermute | solution.py:66
  67.2 2.3 %gather_grad.9 = bf16[1024,128]{1,0:T(8,128)(2,1)S(1)} custom-call(s32[1]{0:T(128)S(6)} %mul.42.base_ref, s32[4,2,2,512]{3,2,1,0:T(2,128)S(1)} %pad_add_fusion.key_ref, bf16[4,512,128]{2,1,0:T(8,128)(2,1)S(1)} %pack.1.refs_0_, bf16[4,512,128]{2,1,0:T(8,128)(2,1)S(1)} %collective-permute-done.15.refs_0_.refs_1_), custom_call_target="tpu_custom_call" | custom-call | flops 2147483648 | bytes 1343492 | tf_op jit(solution)/shard_map/gather_grad/pallas_call | solution.py:36
  69.5 0.7 collective-permute-start.17
  70.2 0.8 collective-permute-done.19.refs_2_
  70.9 0.5 collective-permute-done.20.refs_3_
  71.5 0.3 fold.1
  71.7 1.6 %collective-permute-start.21 = (bf16[1,128,640]{2,1,0:T(8,128)(2,1)S(1)}, bf16[1,128,640]{2,1,0:T(8,128)(2,1)S(1)}, u32[]{:S(2)}, u32[]{:S(2)}) collective-permute-start(bf16[1,128,640]{2,1,0:T(8,128)(2,1)S(1)} %get-tuple-element.92), channel_id=1, source_target_pairs={{0,16},{8,24},{16,0},{24,8},{1,17},{9,25},{17,1},{25,9},{2,18},{10... | collective-permute-start | bytes 491528 | tf_op jit(solution)/shard_map/ppermute | solution.py:62
  73.3 0.5 collective-permute-start.22
  73.8 2.5 %gather_grad.7.refs_0_ = f32[1024,128]{1,0:T(8,128)S(1)} custom-call(s32[1]{0:T(128)S(6)} %mul.40.base_ref, s32[4,2,2,512]{3,2,1,0:T(2,128)S(1)} %pad_add_fusion.key_ref, bf16[4,512,128]{2,1,0:T(8,128)(2,1)S(1)} %pack.1.refs_0_, bf16[4,512,128]{2,1,0:T(8,128)(2,1)S(1)} %collective-permute-done.15.refs_0_.refs_1_), custom_call_target="tpu_custom_call" | custom-call | flops 2147483648 | bytes 1605636 | tf_op jit(solution)/shard_map/gather_grad/pallas_call | solution.py:36
  76.4 0.8 collective-permute-done.21.refs_2_
  77.2 1.4 %collective-permute-done.22.refs_3_ = bf16[1,128,640]{2,1,0:T(8,128)(2,1)S(1)} collective-permute-done((bf16[1,128,640]{2,1,0:T(8,128)(2,1)S(1)}, bf16[1,128,640]{2,1,0:T(8,128)(2,1)S(1)}, u32[]{:S(2)}, u32[]{:S(2)}) %collective-permute-start.22) | collective-permute-done | bytes 163872 | tf_op jit(solution)/shard_map/ppermute | solution.py:62
  78.6 0.1 cut_line.1
  78.7 1.5 %collective-permute-start.23 = (bf16[2,64,640]{2,1,0:T(8,128)(2,1)S(1)}, bf16[2,64,640]{2,1,0:T(8,128)(2,1)S(1)}, u32[]{:S(2)}, u32[]{:S(2)}) collective-permute-start(bf16[2,64,640]{2,1,0:T(8,128)(2,1)S(1)} %get-tuple-element.97), channel_id=1, source_target_pairs={{0,2},{1,3},{2,0},{3,1},{4,6},{5,7},{6,4},{7,5},{8,10},{9,11},{10,... | collective-permute-start | bytes 491528 | tf_op jit(solution)/shard_map/ppermute | solution.py:66
  80.3 2.1 %collective-permute-start.18 = (bf16[1024,128]{1,0:T(8,128)(2,1)S(1)}, bf16[1024,128]{1,0:T(8,128)(2,1)S(1)}, u32[]{:S(2)}, u32[]{:S(2)}) collective-permute-start(bf16[1024,128]{1,0:T(8,128)(2,1)S(1)} %add_up.2), channel_id=1, source_target_pairs={{0,4},{1,5},{2,6},{3,7},{4,0},{5,1},{6,2},{7,3},{8,12},{9,13},{10,... | collective-permute-start | bytes 786440 | tf_op jit(solution)/shard_map/ppermute | solution.py:66
  82.4 2.3 %gather_grad.8.here_ref = f32[1024,128]{1,0:T(8,128)S(1)} custom-call(s32[1]{0:T(128)S(6)} %mul.44.base_ref, s32[4,2,2,512]{3,2,1,0:T(2,128)S(1)} %pad_add_fusion.key_ref, bf16[4,512,128]{2,1,0:T(8,128)(2,1)S(1)} %pack.1.refs_0_, bf16[4,512,128]{2,1,0:T(8,128)(2,1)S(1)} %collective-permute-done.15.refs_0_.refs_1_), custom_call_target="tpu_custom_call" | custom-call | flops 2147483648 | bytes 1605636 | tf_op jit(solution)/shard_map/gather_grad/pallas_call | solution.py:36
  84.7 2.0 %collective-permute-done.23.came_ref = bf16[2,64,640]{2,1,0:T(8,128)(2,1)S(1)} collective-permute-done((bf16[2,64,640]{2,1,0:T(8,128)(2,1)S(1)}, bf16[2,64,640]{2,1,0:T(8,128)(2,1)S(1)}, u32[]{:S(2)}, u32[]{:S(2)}) %collective-permute-start.23) | collective-permute-done | bytes 163872 | tf_op jit(solution)/shard_map/ppermute | solution.py:66
  86.7 2.8 %collective-permute-start.24 = (bf16[1,64,640]{2,1,0:T(8,128)(2,1)S(1)}, bf16[1,64,640]{2,1,0:T(8,128)(2,1)S(1)}, u32[]{:S(2)}, u32[]{:S(2)}) collective-permute-start(bf16[1,64,640]{2,1,0:T(8,128)(2,1)S(1)} %get-tuple-element.100), channel_id=1, source_target_pairs={{0,4},{1,5},{2,6},{3,7},{4,0},{5,1},{6,2},{7,3},{8,12},{9,13},{10,... | collective-permute-start | bytes 245768 | tf_op jit(solution)/shard_map/ppermute | solution.py:66
  89.5 7.0 %collective-permute-done.24 = bf16[1,64,640]{2,1,0:T(8,128)(2,1)S(1)} collective-permute-done((bf16[1,64,640]{2,1,0:T(8,128)(2,1)S(1)}, bf16[1,64,640]{2,1,0:T(8,128)(2,1)S(1)}, u32[]{:S(2)}, u32[]{:S(2)}) %collective-permute-start.24) | collective-permute-done | bytes 81952 | tf_op jit(solution)/shard_map/ppermute | solution.py:66
  96.5 1.2 %collective-permute-start.27 = (bf16[64,640]{1,0:T(8,128)(2,1)S(1)}, bf16[64,640]{1,0:T(8,128)(2,1)S(1)}, u32[]{:S(2)}, u32[]{:S(2)}) collective-permute-start(bf16[64,640]{1,0:T(8,128)(2,1)S(1)} %add_up.3.refs_0_), channel_id=1, source_target_pairs={{0,24},{8,16},{16,8},{24,0},{1,25},{9,17},{17,9},{25,1},{2,26},{10... | collective-permute-start | bytes 245768 | tf_op jit(solution)/shard_map/ppermute | solution.py:62
  97.8 0.9 collective-permute-start.26
  98.7 1.4 %collective-permute-start.25 = (bf16[64,640]{1,0:T(8,128)(2,1)S(1)}, bf16[64,640]{1,0:T(8,128)(2,1)S(1)}, u32[]{:S(2)}, u32[]{:S(2)}) collective-permute-start(bf16[64,640]{1,0:T(8,128)(2,1)S(1)} %add_up.3.refs_0_), channel_id=1, source_target_pairs={{0,8},{8,0},{16,24},{24,16},{1,9},{9,1},{17,25},{25,17},{2,10},{10... | collective-permute-start | bytes 245768 | tf_op jit(solution)/shard_map/ppermute | solution.py:62
  100.1 1.9 %collective-permute-done.27.refs_3_ = bf16[64,640]{1,0:T(8,128)(2,1)S(1)} collective-permute-done((bf16[64,640]{1,0:T(8,128)(2,1)S(1)}, bf16[64,640]{1,0:T(8,128)(2,1)S(1)}, u32[]{:S(2)}, u32[]{:S(2)}) %collective-permute-start.27) | collective-permute-done | bytes 81952 | tf_op jit(solution)/shard_map/ppermute | solution.py:62
  102.0 0.8 collective-permute-done.26.refs_2_
  102.8 0.3 collective-permute-done.25.refs_1_
  103.1 0.9 assemble.1
  104.0 0.8 table_sums.3
  (29 shorter events, 0.3 us)
Async XLA Ops:
  1.7 16.1 %collective-permute-start = (bf16[1024,128]{1,0:T(8,128)(2,1)S(1)}, bf16[1024,128]{1,0:T(8,128)(2,1)S(1)}, u32[]{:S(2)}, u32[]{:S(2)}) collective-permute-start(bf16[1024,128]{1,0:T(8,128)(2,1)S(1)} %pad_maximum_fusion.chunk_ref), channel_id=1, source_target_pairs={{0,4},{1,5},{2,6},{3,7},{4,0},{5,1},{6,2},{7,3},{8,12},{9,13},{10,... | collective-permute-start | bytes 786440 | tf_op jit(solution)/shard_map/ppermute | solution.py:66
  6.5 1.7 %collective-permute-start.2 = (s32[2,512]{1,0:T(2,128)S(1)}, s32[2,512]{1,0:T(2,128)S(1)}, u32[]{:S(2)}, u32[]{:S(2)}) collective-permute-start(s32[2,512]{1,0:T(2,128)S(1)} %get-tuple-element.108), channel_id=1, source_target_pairs={{0,1},{1,0},{2,3},{3,2},{4,5},{5,4},{6,7},{7,6},{8,9},{9,8},{10,11... | collective-permute-start | bytes 12296 | tf_op jit(solution)/shard_map/ppermute | solution.py:69
  6.6 15.5 %collective-permute-start.6 = (bf16[1024,128]{1,0:T(8,128)(2,1)S(1)}, bf16[1024,128]{1,0:T(8,128)(2,1)S(1)}, u32[]{:S(2)}, u32[]{:S(2)}) collective-permute-start(bf16[1024,128]{1,0:T(8,128)(2,1)S(1)} %pad_maximum_fusion.chunk_ref), channel_id=1, source_target_pairs={{0,2},{1,3},{2,0},{3,1},{4,6},{5,7},{6,4},{7,5},{8,10},{9,11},{10,... | collective-permute-start | bytes 786440 | tf_op jit(solution)/shard_map/ppermute | solution.py:66
  8.2 10.2 %collective-permute-start.4 = (s32[2,2,512]{2,1,0:T(2,128)S(1)}, s32[2,2,512]{2,1,0:T(2,128)S(1)}, u32[]{:S(2)}, u32[]{:S(2)}) collective-permute-start(s32[2,2,512]{2,1,0:T(2,128)S(1)} %get-tuple-element.106), channel_id=1, source_target_pairs={{0,16},{8,24},{16,0},{24,8},{1,17},{9,25},{17,1},{25,9},{2,18},{10... | collective-permute-start | bytes 24584 | tf_op jit(solution)/shard_map/ppermute | solution.py:62
  9.8 8.6 %collective-permute-start.3 = (s32[2,2,512]{2,1,0:T(2,128)S(1)}, s32[2,2,512]{2,1,0:T(2,128)S(1)}, u32[]{:S(2)}, u32[]{:S(2)}) collective-permute-start(s32[2,2,512]{2,1,0:T(2,128)S(1)} %get-tuple-element.106), channel_id=1, source_target_pairs={{0,8},{8,0},{16,24},{24,16},{1,9},{9,1},{17,25},{25,17},{2,10},{10... | collective-permute-start | bytes 24584 | tf_op jit(solution)/shard_map/ppermute | solution.py:62
  11.3 7.1 %collective-permute-start.5 = (s32[2,2,512]{2,1,0:T(2,128)S(1)}, s32[2,2,512]{2,1,0:T(2,128)S(1)}, u32[]{:S(2)}, u32[]{:S(2)}) collective-permute-start(s32[2,2,512]{2,1,0:T(2,128)S(1)} %get-tuple-element.106), channel_id=1, source_target_pairs={{0,24},{8,16},{16,8},{24,0},{1,25},{9,17},{17,9},{25,1},{2,26},{10... | collective-permute-start | bytes 24584 | tf_op jit(solution)/shard_map/ppermute | solution.py:62
  17.8 9.0 %collective-permute-start.1 = (bf16[1024,128]{1,0:T(8,128)(2,1)S(1)}, bf16[1024,128]{1,0:T(8,128)(2,1)S(1)}, u32[]{:S(2)}, u32[]{:S(2)}) collective-permute-start(bf16[1024,128]{1,0:T(8,128)(2,1)S(1)} %collective-permute-done.chunk_ref), channel_id=1, source_target_pairs={{0,2},{1,3},{2,0},{3,1},{4,6},{5,7},{6,4},{7,5},{8,10},{9,11},{10,... | collective-permute-start | bytes 786440 | tf_op jit(solution)/shard_map/ppermute | solution.py:66
  28.0 2.0 %collective-permute-start.7 = (bf16[4,512,128]{2,1,0:T(8,128)(2,1)S(1)}, bf16[4,512,128]{2,1,0:T(8,128)(2,1)S(1)}, u32[]{:S(2)}, u32[]{:S(2)}) collective-permute-start(bf16[4,512,128]{2,1,0:T(8,128)(2,1)S(1)} %fetch.9), channel_id=1, source_target_pairs={{0,1},{1,0},{2,3},{3,2},{4,5},{5,4},{6,7},{7,6},{8,9},{9,8},{10,11... | collective-permute-start | bytes 1572872 | tf_op jit(solution)/shard_map/ppermute | solution.py:69
  28.1 11.7 %copy-start = (bf16[512,512]{1,0:T(8,128)(2,1)S(1)}, bf16[512,512]{1,0:T(8,128)(2,1)}, u32[]{:S(2)}) copy-start(bf16[512,512]{1,0:T(8,128)(2,1)} %c_ref.1) | copy-start | bytes 1572868
  28.1 11.7 %copy-start.1 = (bf16[512,2048]{1,0:T(8,128)(2,1)S(1)}, bf16[512,2048]{1,0:T(8,128)(2,1)}, u32[]{:S(2)}) copy-start(bf16[512,2048]{1,0:T(8,128)(2,1)} %wp_ref.1) | copy-start | bytes 6291460
  28.1 11.7 %copy-start.2 = (bf16[512,512]{1,0:T(8,128)(2,1)S(1)}, bf16[512,512]{1,0:T(8,128)(2,1)}, u32[]{:S(2)}) copy-start(bf16[512,512]{1,0:T(8,128)(2,1)} %wo_ref.1) | copy-start | bytes 1572868
  28.1 11.7 %copy-start.3 = (f32[512]{0:T(512)S(1)}, f32[512]{0:T(512)}, u32[]{:S(2)}) copy-start(f32[512]{0:T(512)} %param.16) | copy-start | bytes 6148
  30.1 5.9 %collective-permute-start.8 = (bf16[512,128]{1,0:T(8,128)(2,1)S(1)}, bf16[512,128]{1,0:T(8,128)(2,1)S(1)}, u32[]{:S(2)}, u32[]{:S(2)}) collective-permute-start(bf16[512,128]{1,0:T(8,128)(2,1)S(1)} %get-tuple-element.62), channel_id=1, source_target_pairs={{0,8},{8,0},{16,24},{24,16},{1,9},{9,1},{17,25},{25,17},{2,10},{10... | collective-permute-start | bytes 393224 | tf_op jit(solution)/shard_map/ppermute | solution.py:62
  31.7 8.1 %collective-permute-start.9 = (bf16[512,128]{1,0:T(8,128)(2,1)S(1)}, bf16[512,128]{1,0:T(8,128)(2,1)S(1)}, u32[]{:S(2)}, u32[]{:S(2)}) collective-permute-start(bf16[512,128]{1,0:T(8,128)(2,1)S(1)} %get-tuple-element.63), channel_id=1, source_target_pairs={{0,16},{8,24},{16,0},{24,8},{1,17},{9,25},{17,1},{25,9},{2,18},{10... | collective-permute-start | bytes 393224 | tf_op jit(solution)/shard_map/ppermute | solution.py:62
  33.2 6.6 %collective-permute-start.10 = (bf16[512,128]{1,0:T(8,128)(2,1)S(1)}, bf16[512,128]{1,0:T(8,128)(2,1)S(1)}, u32[]{:S(2)}, u32[]{:S(2)}) collective-permute-start(bf16[512,128]{1,0:T(8,128)(2,1)S(1)} %get-tuple-element.64), channel_id=1, source_target_pairs={{0,24},{8,16},{16,8},{24,0},{1,25},{9,17},{17,9},{25,1},{2,26},{10... | collective-permute-start | bytes 393224 | tf_op jit(solution)/shard_map/ppermute | solution.py:62
  51.0 3.6 %collective-permute-start.14 = (bf16[4,256,640]{2,1,0:T(8,128)(2,1)S(1)}, bf16[4,256,640]{2,1,0:T(8,128)(2,1)S(1)}, u32[]{:S(2)}, u32[]{:S(2)}) collective-permute-start(bf16[4,256,640]{2,1,0:T(8,128)(2,1)S(1)} %get-tuple-element.73), channel_id=1, source_target_pairs={{0,1},{1,0},{2,3},{3,2},{4,5},{5,4},{6,7},{7,6},{8,9},{9,8},{10,11... | collective-permute-start | bytes 3932168 | tf_op jit(solution)/shard_map/ppermute | solution.py:69
  51.0 6.4 %collective-permute-start.11 = (bf16[512,128]{1,0:T(8,128)(2,1)S(1)}, bf16[512,128]{1,0:T(8,128)(2,1)S(1)}, u32[]{:S(2)}, u32[]{:S(2)}) collective-permute-start(bf16[512,128]{1,0:T(8,128)(2,1)S(1)} %get-tuple-element.67), channel_id=1, source_target_pairs={{0,8},{8,0},{16,24},{24,16},{1,9},{9,1},{17,25},{25,17},{2,10},{10... | collective-permute-start | bytes 393224 | tf_op jit(solution)/shard_map/ppermute | solution.py:62
  52.3 6.8 %collective-permute-start.12 = (bf16[512,128]{1,0:T(8,128)(2,1)S(1)}, bf16[512,128]{1,0:T(8,128)(2,1)S(1)}, u32[]{:S(2)}, u32[]{:S(2)}) collective-permute-start(bf16[512,128]{1,0:T(8,128)(2,1)S(1)} %get-tuple-element.68), channel_id=1, source_target_pairs={{0,16},{8,24},{16,0},{24,8},{1,17},{9,25},{17,1},{25,9},{2,18},{10... | collective-permute-start | bytes 393224 | tf_op jit(solution)/shard_map/ppermute | solution.py:62
  53.1 7.6 %collective-permute-start.13 = (bf16[512,128]{1,0:T(8,128)(2,1)S(1)}, bf16[512,128]{1,0:T(8,128)(2,1)S(1)}, u32[]{:S(2)}, u32[]{:S(2)}) collective-permute-start(bf16[512,128]{1,0:T(8,128)(2,1)S(1)} %get-tuple-element.69), channel_id=1, source_target_pairs={{0,24},{8,16},{16,8},{24,0},{1,25},{9,17},{17,9},{25,1},{2,26},{10... | collective-permute-start | bytes 393224 | tf_op jit(solution)/shard_map/ppermute | solution.py:62
  60.7 3.7 %collective-permute-start.15 = (bf16[4,512,128]{2,1,0:T(8,128)(2,1)S(1)}, bf16[4,512,128]{2,1,0:T(8,128)(2,1)S(1)}, u32[]{:S(2)}, u32[]{:S(2)}) collective-permute-start(bf16[4,512,128]{2,1,0:T(8,128)(2,1)S(1)} %pack.1.refs_0_), channel_id=1, source_target_pairs={{0,1},{1,0},{2,3},{3,2},{4,5},{5,4},{6,7},{7,6},{8,9},{9,8},{10,11... | collective-permute-start | bytes 1572872 | tf_op jit(solution)/shard_map/ppermute | solution.py:69
  60.8 10.1 %collective-permute-start.19 = (bf16[2,128,640]{2,1,0:T(8,128)(2,1)S(1)}, bf16[2,128,640]{2,1,0:T(8,128)(2,1)S(1)}, u32[]{:S(2)}, u32[]{:S(2)}) collective-permute-start(bf16[2,128,640]{2,1,0:T(8,128)(2,1)S(1)} %get-tuple-element.75), channel_id=1, source_target_pairs={{0,8},{8,0},{16,24},{24,16},{1,9},{9,1},{17,25},{25,17},{2,10},{10... | collective-permute-start | bytes 983048 | tf_op jit(solution)/shard_map/ppermute | solution.py:62
  61.7 9.8 %collective-permute-start.20 = (bf16[2,128,640]{2,1,0:T(8,128)(2,1)S(1)}, bf16[2,128,640]{2,1,0:T(8,128)(2,1)S(1)}, u32[]{:S(2)}, u32[]{:S(2)}) collective-permute-start(bf16[2,128,640]{2,1,0:T(8,128)(2,1)S(1)} %get-tuple-element.77), channel_id=1, source_target_pairs={{0,16},{8,24},{16,0},{24,8},{1,17},{9,25},{17,1},{25,9},{2,18},{10... | collective-permute-start | bytes 983048 | tf_op jit(solution)/shard_map/ppermute | solution.py:62
  65.7 14.5 %collective-permute-start.16 = (bf16[1024,128]{1,0:T(8,128)(2,1)S(1)}, bf16[1024,128]{1,0:T(8,128)(2,1)S(1)}, u32[]{:S(2)}, u32[]{:S(2)}) collective-permute-start(bf16[1024,128]{1,0:T(8,128)(2,1)S(1)} %gather_grad.6), channel_id=1, source_target_pairs={{0,2},{1,3},{2,0},{3,1},{4,6},{5,7},{6,4},{7,5},{8,10},{9,11},{10,... | collective-permute-start | bytes 786440 | tf_op jit(solution)/shard_map/ppermute | solution.py:66
  69.5 20.0 %collective-permute-start.17 = (bf16[1024,128]{1,0:T(8,128)(2,1)S(1)}, bf16[1024,128]{1,0:T(8,128)(2,1)S(1)}, u32[]{:S(2)}, u32[]{:S(2)}) collective-permute-start(bf16[1024,128]{1,0:T(8,128)(2,1)S(1)} %gather_grad.9), channel_id=1, source_target_pairs={{0,2},{1,3},{2,0},{3,1},{4,6},{5,7},{6,4},{7,5},{8,10},{9,11},{10,... | collective-permute-start | bytes 786440 | tf_op jit(solution)/shard_map/ppermute | solution.py:66
  71.7 5.5 %collective-permute-start.21 = (bf16[1,128,640]{2,1,0:T(8,128)(2,1)S(1)}, bf16[1,128,640]{2,1,0:T(8,128)(2,1)S(1)}, u32[]{:S(2)}, u32[]{:S(2)}) collective-permute-start(bf16[1,128,640]{2,1,0:T(8,128)(2,1)S(1)} %get-tuple-element.92), channel_id=1, source_target_pairs={{0,16},{8,24},{16,0},{24,8},{1,17},{9,25},{17,1},{25,9},{2,18},{10... | collective-permute-start | bytes 491528 | tf_op jit(solution)/shard_map/ppermute | solution.py:62
  73.3 5.3 %collective-permute-start.22 = (bf16[1,128,640]{2,1,0:T(8,128)(2,1)S(1)}, bf16[1,128,640]{2,1,0:T(8,128)(2,1)S(1)}, u32[]{:S(2)}, u32[]{:S(2)}) collective-permute-start(bf16[1,128,640]{2,1,0:T(8,128)(2,1)S(1)} %get-tuple-element.93), channel_id=1, source_target_pairs={{0,8},{8,0},{16,24},{24,16},{1,9},{9,1},{17,25},{25,17},{2,10},{10... | collective-permute-start | bytes 491528 | tf_op jit(solution)/shard_map/ppermute | solution.py:62
  78.7 8.0 %collective-permute-start.23 = (bf16[2,64,640]{2,1,0:T(8,128)(2,1)S(1)}, bf16[2,64,640]{2,1,0:T(8,128)(2,1)S(1)}, u32[]{:S(2)}, u32[]{:S(2)}) collective-permute-start(bf16[2,64,640]{2,1,0:T(8,128)(2,1)S(1)} %get-tuple-element.97), channel_id=1, source_target_pairs={{0,2},{1,3},{2,0},{3,1},{4,6},{5,7},{6,4},{7,5},{8,10},{9,11},{10,... | collective-permute-start | bytes 491528 | tf_op jit(solution)/shard_map/ppermute | solution.py:66
  80.3 23.8 %collective-permute-start.18 = (bf16[1024,128]{1,0:T(8,128)(2,1)S(1)}, bf16[1024,128]{1,0:T(8,128)(2,1)S(1)}, u32[]{:S(2)}, u32[]{:S(2)}) collective-permute-start(bf16[1024,128]{1,0:T(8,128)(2,1)S(1)} %add_up.2), channel_id=1, source_target_pairs={{0,4},{1,5},{2,6},{3,7},{4,0},{5,1},{6,2},{7,3},{8,12},{9,13},{10,... | collective-permute-start | bytes 786440 | tf_op jit(solution)/shard_map/ppermute | solution.py:66
  86.7 9.8 %collective-permute-start.24 = (bf16[1,64,640]{2,1,0:T(8,128)(2,1)S(1)}, bf16[1,64,640]{2,1,0:T(8,128)(2,1)S(1)}, u32[]{:S(2)}, u32[]{:S(2)}) collective-permute-start(bf16[1,64,640]{2,1,0:T(8,128)(2,1)S(1)} %get-tuple-element.100), channel_id=1, source_target_pairs={{0,4},{1,5},{2,6},{3,7},{4,0},{5,1},{6,2},{7,3},{8,12},{9,13},{10,... | collective-permute-start | bytes 245768 | tf_op jit(solution)/shard_map/ppermute | solution.py:66
  96.5 5.5 %collective-permute-start.27 = (bf16[64,640]{1,0:T(8,128)(2,1)S(1)}, bf16[64,640]{1,0:T(8,128)(2,1)S(1)}, u32[]{:S(2)}, u32[]{:S(2)}) collective-permute-start(bf16[64,640]{1,0:T(8,128)(2,1)S(1)} %add_up.3.refs_0_), channel_id=1, source_target_pairs={{0,24},{8,16},{16,8},{24,0},{1,25},{9,17},{17,9},{25,1},{2,26},{10... | collective-permute-start | bytes 245768 | tf_op jit(solution)/shard_map/ppermute | solution.py:62
  97.8 5.0 %collective-permute-start.26 = (bf16[64,640]{1,0:T(8,128)(2,1)S(1)}, bf16[64,640]{1,0:T(8,128)(2,1)S(1)}, u32[]{:S(2)}, u32[]{:S(2)}) collective-permute-start(bf16[64,640]{1,0:T(8,128)(2,1)S(1)} %add_up.3.refs_0_), channel_id=1, source_target_pairs={{0,16},{8,24},{16,0},{24,8},{1,17},{9,25},{17,1},{25,9},{2,18},{10... | collective-permute-start | bytes 245768 | tf_op jit(solution)/shard_map/ppermute | solution.py:62
  98.7 4.4 %collective-permute-start.25 = (bf16[64,640]{1,0:T(8,128)(2,1)S(1)}, bf16[64,640]{1,0:T(8,128)(2,1)S(1)}, u32[]{:S(2)}, u32[]{:S(2)}) collective-permute-start(bf16[64,640]{1,0:T(8,128)(2,1)S(1)} %add_up.3.refs_0_), channel_id=1, source_target_pairs={{0,8},{8,0},{16,24},{24,16},{1,9},{9,1},{17,25},{25,17},{2,10},{10... | collective-permute-start | bytes 245768 | tf_op jit(solution)/shard_map/ppermute | solution.py:62

commit v14 on v12

--- a/solution.py
+++ b/solution.py
@@ -95,7 +95,7 @@
         [((count, tokens, cols), BF16)] * many,
         [base, chunk, keys, *before],
         smem=1,
-        flops=2 * many * count * tokens * rows * cols,
+        flops=(4 if before else 0) * many * count * tokens * rows * cols,
     )
 
 
@@ -496,17 +496,20 @@
     keys = jnp.stack([keys, grid.over_pair(keys)])
     keys = jnp.stack([keys] + [grid.over_replica(keys, k) for k in range(1, replicas)])
 
+    key_cols = jnp.broadcast_to(keys[..., None], (*keys.shape, LANES))
+    both = list(range(cores))
+    found = fetch(bases[0], key_cols, both, own)
+
     held = {0: own}
     for low in reversed([1 << i for i in range(line.bit_length() - 1)]):
         for k in range(low, line, 2 * low):
-            held[k] = grid.over_line(held[k ^ low], low)
+            source = held[k ^ low]
+            if k != low:
+                source = lax.optimization_barrier((source, found))[0]
+            held[k] = grid.over_line(source, low)
     order = sorted(held, key=lambda k: (bin(k).count("1"), k))
 
-    key_cols = jnp.broadcast_to(keys[..., None], (*keys.shape, LANES))
-    both = list(range(cores))
-
-    found = ()
-    for k in order[:-1]:
+    for k in order[1:-1]:
         found = fetch(bases[k], key_cols, both, held[k], found)
     last = order[-1]
     there = fetch(bases[last], key_cols, both[1:], held[last], found[1:])

time: 102 us -> 100 us (0.980)
  waiting for transfers between devices: 28.5 us -> 25.4 us
  starting transfers between devices: 35.2 us -> 36.4 us
    ppermute x8, waiting for transfers between devices: 13.9 us -> 7.49 us  [over_line(): return lax.ppermute(value, 'sparse', pairs)]
    ppermute x16, waiting for transfers between devices: 13.9 us -> 17.3 us  [over_replica(): return lax.ppermute(value, 'replica', [(i, i ^ step) for i in range(n)])]
    ppermute x8, starting transfers between devices: 16.3 us -> 17.8 us  [over_line(): return lax.ppermute(value, 'sparse', pairs)]
  transfers between devices with their start and end apart: 28 -> 28, of which waited for: 14 -> 16; matrix products, arithmetic and copies ran while one was open for 2% -> 2% of each run, Pallas kernels for 21% -> 21%
where the time goes in v14:
time: 100 us
  starting transfers between devices  36.4 us (36%)
  Pallas kernels  34.4 us (34%)
  waiting for transfers between devices  25.4 us (25%)
  local copies, waits for them, and re-layouts  2.24 us (2%)
    pallas_call x22, Pallas kernels, run(): pl.pallas_call(body, out_shape=outs, in_specs=places, out_specs=[in_vmem]...  34.4 us
    ppermute x16, starting transfers between devices, over_replica(): return lax.ppermute(value, 'replica', [(i, i ^ step) for i in range(n)])  18.3 us
    ppermute x8, starting transfers between devices, over_line(): return lax.ppermute(value, 'sparse', pairs)  17.8 us
    ppermute x16, waiting for transfers between devices, over_replica(): return lax.ppermute(value, 'replica', [(i, i ^ step) for i in range(n)])  17.3 us
    ppermute x8, waiting for transfers between devices, over_line(): return lax.ppermute(value, 'sparse', pairs)  7.49 us
  transfers between devices with their start and end apart: 28, of which 16 were waited for; matrix products, arithmetic and copies ran while one was open for 2% of the time, Pallas kernels for 21%

profile of v14, /device:TPU:0, one launch (start us, length us, event | category | flops | bytes accessed | tf_op | source)
XLA Modules:
  0.0 100.2 jit_solution(11508634228188401420)
XLA Ops:
  0.6 1.0 constant_dynamic-slice_fusion
  1.7 4.1 %collective-permute-start = (bf16[1024,128]{1,0:T(8,128)(2,1)S(1)}, bf16[1024,128]{1,0:T(8,128)(2,1)S(1)}, u32[]{:S(2)}, u32[]{:S(2)}) collective-permute-start(bf16[1024,128]{1,0:T(8,128)(2,1)S(1)} %pad_maximum_fusion.chunk_ref), channel_id=1, source_target_pairs={{0,4},{1,5},{2,6},{3,7},{4,0},{5,1},{6,2},{7,3},{8,12},{9,13},{10,... | collective-permute-start | bytes 786440 | tf_op jit(solution)/shard_map/ppermute | solution.py:66
  5.8 0.7 add_bitcast_fusion
  6.5 0.1 collective-permute-start.1
  6.6 1.6 %collective-permute-start.6 = (bf16[1024,128]{1,0:T(8,128)(2,1)S(1)}, bf16[1024,128]{1,0:T(8,128)(2,1)S(1)}, u32[]{:S(2)}, u32[]{:S(2)}) collective-permute-start(bf16[1024,128]{1,0:T(8,128)(2,1)S(1)} %pad_maximum_fusion.chunk_ref), channel_id=1, source_target_pairs={{0,2},{1,3},{2,0},{3,1},{4,6},{5,7},{6,4},{7,5},{8,10},{9,11},{10,... | collective-permute-start | bytes 786440 | tf_op jit(solution)/shard_map/ppermute | solution.py:66
  8.2 1.6 %collective-permute-start.3 = (s32[2,2,512]{2,1,0:T(2,128)S(1)}, s32[2,2,512]{2,1,0:T(2,128)S(1)}, u32[]{:S(2)}, u32[]{:S(2)}) collective-permute-start(s32[2,2,512]{2,1,0:T(2,128)S(1)} %get-tuple-element.108), channel_id=1, source_target_pairs={{0,16},{8,24},{16,0},{24,8},{1,17},{9,25},{17,1},{25,9},{2,18},{10... | collective-permute-start | bytes 24584 | tf_op jit(solution)/shard_map/ppermute | solution.py:62
  9.8 1.5 %collective-permute-start.2 = (s32[2,2,512]{2,1,0:T(2,128)S(1)}, s32[2,2,512]{2,1,0:T(2,128)S(1)}, u32[]{:S(2)}, u32[]{:S(2)}) collective-permute-start(s32[2,2,512]{2,1,0:T(2,128)S(1)} %get-tuple-element.108), channel_id=1, source_target_pairs={{0,8},{8,0},{16,24},{24,16},{1,9},{9,1},{17,25},{25,17},{2,10},{10... | collective-permute-start | bytes 24584 | tf_op jit(solution)/shard_map/ppermute | solution.py:62
  11.3 0.5 collective-permute-start.4
  11.8 0.2 collective-permute-done.3
  12.0 1.5 %collective-permute-done.2 = s32[2,2,512]{2,1,0:T(2,128)S(1)} collective-permute-done((s32[2,2,512]{2,1,0:T(2,128)S(1)}, s32[2,2,512]{2,1,0:T(2,128)S(1)}, u32[]{:S(2)}, u32[]{:S(2)}) %collective-permute-start.2) | collective-permute-done | bytes 8224 | tf_op jit(solution)/shard_map/ppermute | solution.py:62
  13.5 2.4 %collective-permute-done.4 = s32[2,2,512]{2,1,0:T(2,128)S(1)} collective-permute-done((s32[2,2,512]{2,1,0:T(2,128)S(1)}, s32[2,2,512]{2,1,0:T(2,128)S(1)}, u32[]{:S(2)}, u32[]{:S(2)}) %collective-permute-start.4) | collective-permute-done | bytes 8224 | tf_op jit(solution)/shard_map/ppermute | solution.py:62
  15.9 1.2 %broadcast_in_dim.14.key_ref = s32[4,2,2,512,128]{4,3,2,1,0:T(8,128)S(1)} broadcast(s32[4,2,2,512]{3,2,1,0:T(2,128)S(1)} %pad_add_fusion.key_ref), dimensions={0,1,2,3} | broadcast | bytes 4227072 | tf_op jit(solution)/shard_map/broadcast_in_dim | solution.py:499
  17.1 2.3 %fetch.5 = (bf16[4,512,128]{2,1,0:T(8,128)(2,1)S(1)}, bf16[4,512,128]{2,1,0:T(8,128)(2,1)S(1)}) custom-call(s32[1]{0:T(128)S(6)} %mul.38.base_ref, bf16[1024,128]{1,0:T(8,128)(2,1)S(1)} %pad_maximum_fusion.chunk_ref, s32[4,2,2,512,128]{4,3,2,1,0:T(8,128)S(1)} %broadcast_in_dim.14.key_ref), custom_call_target="tpu_custom_call" | custom-call | bytes 5505028 | tf_op jit(solution)/shard_map/fetch/pallas_call | solution.py:36
  19.5 1.1 %collective-permute-start.5 = (bf16[1024,128]{1,0:T(8,128)(2,1)S(1)}, bf16[1024,128]{1,0:T(8,128)(2,1)S(1)}, u32[]{:S(2)}, u32[]{:S(2)}) collective-permute-start(bf16[1024,128]{1,0:T(8,128)(2,1)S(1)} %collective-permute-done.chunk_ref), channel_id=1, source_target_pairs={{0,2},{1,3},{2,0},{3,1},{4,6},{5,7},{6,4},{7,5},{8,10},{9,11},{10,... | collective-permute-start | bytes 786440 | tf_op jit(solution)/shard_map/ppermute | solution.py:66
  20.5 2.3 %fetch.6 = (bf16[4,512,128]{2,1,0:T(8,128)(2,1)S(1)}, bf16[4,512,128]{2,1,0:T(8,128)(2,1)S(1)}) custom-call(s32[1]{0:T(128)S(6)} %mul.44.base_ref, bf16[1024,128]{1,0:T(8,128)(2,1)S(1)} %collective-permute-done.6.chunk_ref, s32[4,2,2,512,128]{4,3,2,1,0:T(8,128)S(1)} %broadcast_in_dim.14.key_ref, bf16[4,512,128]{2,1,0:T(8,128)(2,1)S(1)} %get-tuple-element.56.refs_0_, ...), custom_call_target="tpu_custom_call" | custom-call | flops 1073741824 | bytes 6553604 | tf_op jit(solution)/shard_map/fetch/pallas_call | solution.py:36
  22.9 2.3 %fetch.7 = (bf16[4,512,128]{2,1,0:T(8,128)(2,1)S(1)}, bf16[4,512,128]{2,1,0:T(8,128)(2,1)S(1)}) custom-call(s32[1]{0:T(128)S(6)} %mul.42.base_ref, bf16[1024,128]{1,0:T(8,128)(2,1)S(1)} %collective-permute-done.chunk_ref, s32[4,2,2,512,128]{4,3,2,1,0:T(8,128)S(1)} %broadcast_in_dim.14.key_ref, bf16[4,512,128]{2,1,0:T(8,128)(2,1)S(1)} %get-tuple-element.59.refs_0_, ...), custom_call_target="tpu_custom_call" | custom-call | flops 1073741824 | bytes 6553604 | tf_op jit(solution)/shard_map/fetch/pallas_call | solution.py:36
  25.2 1.2 %collective-permute-done.5.chunk_ref = bf16[1024,128]{1,0:T(8,128)(2,1)S(1)} collective-permute-done((bf16[1024,128]{1,0:T(8,128)(2,1)S(1)}, bf16[1024,128]{1,0:T(8,128)(2,1)S(1)}, u32[]{:S(2)}, u32[]{:S(2)}) %collective-permute-start.5) | collective-permute-done | bytes 262176 | tf_op jit(solution)/shard_map/ppermute | solution.py:66
  26.5 1.2 %fetch.9 = bf16[4,512,128]{2,1,0:T(8,128)(2,1)S(1)} custom-call(s32[1]{0:T(128)S(6)} %mul.35.base_ref, bf16[1024,128]{1,0:T(8,128)(2,1)S(1)} %collective-permute-done.5.chunk_ref, s32[4,2,2,512,128]{4,3,2,1,0:T(8,128)S(1)} %broadcast_in_dim.14.key_ref, bf16[4,512,128]{2,1,0:T(8,128)(2,1)S(1)} %get-tuple-element.62.refs_0_), custom_call_target="tpu_custom_call" | custom-call | flops 536870912 | bytes 5505028 | tf_op jit(solution)/shard_map/fetch/pallas_call | solution.py:36
  27.7 0.1 collective-permute-start.7
  27.9 1.2 %fetch.8.left_ref = bf16[4,512,128]{2,1,0:T(8,128)(2,1)S(1)} custom-call(s32[1]{0:T(128)S(6)} %mul.35.base_ref, bf16[1024,128]{1,0:T(8,128)(2,1)S(1)} %collective-permute-done.5.chunk_ref, s32[4,2,2,512,128]{4,3,2,1,0:T(8,128)S(1)} %broadcast_in_dim.14.key_ref, bf16[4,512,128]{2,1,0:T(8,128)(2,1)S(1)} %get-tuple-element.61.refs_0_), custom_call_target="tpu_custom_call" | custom-call | flops 536870912 | bytes 5505028 | tf_op jit(solution)/shard_map/fetch/pallas_call | solution.py:36
  29.1 0.6 collective-permute-done.7.right_ref
  29.7 0.1 combine.1
  29.8 0.6 collective-permute-start.8
  30.5 1.4 %collective-permute-start.9 = (bf16[512,128]{1,0:T(8,128)(2,1)S(1)}, bf16[512,128]{1,0:T(8,128)(2,1)S(1)}, u32[]{:S(2)}, u32[]{:S(2)}) collective-permute-start(bf16[512,128]{1,0:T(8,128)(2,1)S(1)} %get-tuple-element.65), channel_id=1, source_target_pairs={{0,16},{8,24},{16,0},{24,8},{1,17},{9,25},{17,1},{25,9},{2,18},{10... | collective-permute-start | bytes 393224 | tf_op jit(solution)/shard_map/ppermute | solution.py:62
  31.9 1.5 %collective-permute-start.10 = (bf16[512,128]{1,0:T(8,128)(2,1)S(1)}, bf16[512,128]{1,0:T(8,128)(2,1)S(1)}, u32[]{:S(2)}, u32[]{:S(2)}) collective-permute-start(bf16[512,128]{1,0:T(8,128)(2,1)S(1)} %get-tuple-element.66), channel_id=1, source_target_pairs={{0,24},{8,16},{16,8},{24,0},{1,25},{9,17},{17,9},{25,1},{2,26},{10... | collective-permute-start | bytes 393224 | tf_op jit(solution)/shard_map/ppermute | solution.py:62
  33.4 2.9 %collective-permute-done.8.refs_1_ = bf16[512,128]{1,0:T(8,128)(2,1)S(1)} collective-permute-done((bf16[512,128]{1,0:T(8,128)(2,1)S(1)}, bf16[512,128]{1,0:T(8,128)(2,1)S(1)}, u32[]{:S(2)}, u32[]{:S(2)}) %collective-permute-start.8) | collective-permute-done | bytes 131104 | tf_op jit(solution)/shard_map/ppermute | solution.py:62
  36.3 2.3 %collective-permute-done.9.refs_2_ = bf16[512,128]{1,0:T(8,128)(2,1)S(1)} collective-permute-done((bf16[512,128]{1,0:T(8,128)(2,1)S(1)}, bf16[512,128]{1,0:T(8,128)(2,1)S(1)}, u32[]{:S(2)}, u32[]{:S(2)}) %collective-permute-start.9) | collective-permute-done | bytes 131104 | tf_op jit(solution)/shard_map/ppermute | solution.py:62
  38.6 11.1 %sequence.1 = (bf16[512,512]{1,0:T(8,128)(2,1)}, bf16[512,128]{1,0:T(8,128)(2,1)S(1)}, bf16[512,128]{1,0:T(8,128)(2,1)S(1)}, bf16[512,128]{1,0:T(8,128)(2,1)S(1)...) custom-call(s32[1]{0:T(128)} %bitcast.r_ref, ...), custom_call_target="tpu_custom_call" | custom-call | flops 4294967296 | bytes 9177096 | tf_op jit(solution)/shard_map/sequence/pallas_call | solution.py:36
  49.7 0.1 collective-permute-start.14
  49.8 1.5 %collective-permute-start.11 = (bf16[512,128]{1,0:T(8,128)(2,1)S(1)}, bf16[512,128]{1,0:T(8,128)(2,1)S(1)}, u32[]{:S(2)}, u32[]{:S(2)}) collective-permute-start(bf16[512,128]{1,0:T(8,128)(2,1)S(1)} %get-tuple-element.69), channel_id=1, source_target_pairs={{0,8},{8,0},{16,24},{24,16},{1,9},{9,1},{17,25},{25,17},{2,10},{10... | collective-permute-start | bytes 393224 | tf_op jit(solution)/shard_map/ppermute | solution.py:62
  51.3 0.5 collective-permute-start.12
  51.8 1.5 %collective-permute-start.13 = (bf16[512,128]{1,0:T(8,128)(2,1)S(1)}, bf16[512,128]{1,0:T(8,128)(2,1)S(1)}, u32[]{:S(2)}, u32[]{:S(2)}) collective-permute-start(bf16[512,128]{1,0:T(8,128)(2,1)S(1)} %get-tuple-element.71), channel_id=1, source_target_pairs={{0,24},{8,16},{16,8},{24,0},{1,25},{9,17},{17,9},{25,1},{2,26},{10... | collective-permute-start | bytes 393224 | tf_op jit(solution)/shard_map/ppermute | solution.py:62
  53.3 1.7 %weight_grad.1 = (f32[2,128,640]{2,1,0:T(8,128)S(1)}, bf16[2,128,640]{2,1,0:T(8,128)(2,1)S(1)}, f32[2,128,640]{2,1,0:T(8,128)S(1)}, bf16[2,128,640]{2,1,0:T(8,128)(2,1)S(1)}) custom-call(s32[1]{0:T(128)} %bitcast.r_ref, s32[1]{0:T(128)} %bitcast.1.core_ref, bf16[512,512]{1,0:T(8,128)(2,1)S(1)} %get-tuple-element.72.n_ref, ...), custom_call_target="tpu_custom_call" | custom-call | flops 939524096 | bytes 6946824 | tf_op jit(solution)/shard_map/weight_grad/pallas_call | solution.py:36
  55.0 1.0 %collective-permute-done.11.refs_1_ = bf16[512,128]{1,0:T(8,128)(2,1)S(1)} collective-permute-done((bf16[512,128]{1,0:T(8,128)(2,1)S(1)}, bf16[512,128]{1,0:T(8,128)(2,1)S(1)}, u32[]{:S(2)}, u32[]{:S(2)}) %collective-permute-start.11) | collective-permute-done | bytes 131104 | tf_op jit(solution)/shard_map/ppermute | solution.py:62
  56.0 3.6 %collective-permute-done.12.refs_2_ = bf16[512,128]{1,0:T(8,128)(2,1)S(1)} collective-permute-done((bf16[512,128]{1,0:T(8,128)(2,1)S(1)}, bf16[512,128]{1,0:T(8,128)(2,1)S(1)}, u32[]{:S(2)}, u32[]{:S(2)}) %collective-permute-start.12) | collective-permute-done | bytes 131104 | tf_op jit(solution)/shard_map/ppermute | solution.py:62
  59.7 0.1 collective-permute-start.15
  59.8 0.6 collective-permute-start.19
  60.4 1.4 %collective-permute-start.20 = (bf16[2,128,640]{2,1,0:T(8,128)(2,1)S(1)}, bf16[2,128,640]{2,1,0:T(8,128)(2,1)S(1)}, u32[]{:S(2)}, u32[]{:S(2)}) collective-permute-start(bf16[2,128,640]{2,1,0:T(8,128)(2,1)S(1)} %get-tuple-element.79), channel_id=1, source_target_pairs={{0,16},{8,24},{16,0},{24,8},{1,17},{9,25},{17,1},{25,9},{2,18},{10... | collective-permute-start | bytes 983048 | tf_op jit(solution)/shard_map/ppermute | solution.py:62
  61.8 1.2 %gather_grad.5.refs_1_ = bf16[1024,128]{1,0:T(8,128)(2,1)S(1)} custom-call(s32[1]{0:T(128)S(6)} %mul.35.base_ref, s32[4,2,2,512]{3,2,1,0:T(2,128)S(1)} %pad_add_fusion.key_ref, bf16[4,512,128]{2,1,0:T(8,128)(2,1)S(1)} %pack.1.refs_0_), custom_call_target="tpu_custom_call" | custom-call | flops 1073741824 | bytes 819204 | tf_op jit(solution)/shard_map/gather_grad/pallas_call | solution.py:36
  63.1 1.2 %gather_grad.6 = bf16[1024,128]{1,0:T(8,128)(2,1)S(1)} custom-call(s32[1]{0:T(128)S(6)} %mul.35.base_ref, s32[4,2,2,512]{3,2,1,0:T(2,128)S(1)} %pad_add_fusion.key_ref, bf16[4,512,128]{2,1,0:T(8,128)(2,1)S(1)} %collective-permute-done.15.refs_0_.refs_1_, bf16[1024,128]{1,0:T(8,128)(2,1)S(1)} %gather_grad.5.refs_1_), custom_call_target="tpu_custom_call" | custom-call | flops 1073741824 | bytes 1081348 | tf_op jit(solution)/shard_map/gather_grad/pallas_call | solution.py:36
  64.3 1.3 %collective-permute-start.16 = (bf16[1024,128]{1,0:T(8,128)(2,1)S(1)}, bf16[1024,128]{1,0:T(8,128)(2,1)S(1)}, u32[]{:S(2)}, u32[]{:S(2)}) collective-permute-start(bf16[1024,128]{1,0:T(8,128)(2,1)S(1)} %gather_grad.6), channel_id=1, source_target_pairs={{0,2},{1,3},{2,0},{3,1},{4,6},{5,7},{6,4},{7,5},{8,10},{9,11},{10,... | collective-permute-start | bytes 786440 | tf_op jit(solution)/shard_map/ppermute | solution.py:66
  65.7 2.3 %gather_grad.9 = bf16[1024,128]{1,0:T(8,128)(2,1)S(1)} custom-call(s32[1]{0:T(128)S(6)} %mul.44.base_ref, s32[4,2,2,512]{3,2,1,0:T(2,128)S(1)} %pad_add_fusion.key_ref, bf16[4,512,128]{2,1,0:T(8,128)(2,1)S(1)} %pack.1.refs_0_, bf16[4,512,128]{2,1,0:T(8,128)(2,1)S(1)} %collective-permute-done.15.refs_0_.refs_1_), custom_call_target="tpu_custom_call" | custom-call | flops 2147483648 | bytes 1343492 | tf_op jit(solution)/shard_map/gather_grad/pallas_call | solution.py:36
  68.0 0.9 collective-permute-start.17
  68.8 1.1 %collective-permute-done.19.refs_2_ = bf16[2,128,640]{2,1,0:T(8,128)(2,1)S(1)} collective-permute-done((bf16[2,128,640]{2,1,0:T(8,128)(2,1)S(1)}, bf16[2,128,640]{2,1,0:T(8,128)(2,1)S(1)}, u32[]{:S(2)}, u32[]{:S(2)}) %collective-permute-start.19) | collective-permute-done | bytes 327712 | tf_op jit(solution)/shard_map/ppermute | solution.py:62
  69.9 0.3 collective-permute-done.20.refs_3_
  70.2 0.2 fold.1
  70.5 1.5 %collective-permute-start.21 = (bf16[1,128,640]{2,1,0:T(8,128)(2,1)S(1)}, bf16[1,128,640]{2,1,0:T(8,128)(2,1)S(1)}, u32[]{:S(2)}, u32[]{:S(2)}) collective-permute-start(bf16[1,128,640]{2,1,0:T(8,128)(2,1)S(1)} %get-tuple-element.94), channel_id=1, source_target_pairs={{0,16},{8,24},{16,0},{24,8},{1,17},{9,25},{17,1},{25,9},{2,18},{10... | collective-permute-start | bytes 491528 | tf_op jit(solution)/shard_map/ppermute | solution.py:62
  71.9 0.6 collective-permute-start.22
  72.5 2.5 %gather_grad.7.refs_0_ = f32[1024,128]{1,0:T(8,128)S(1)} custom-call(s32[1]{0:T(128)S(6)} %mul.42.base_ref, s32[4,2,2,512]{3,2,1,0:T(2,128)S(1)} %pad_add_fusion.key_ref, bf16[4,512,128]{2,1,0:T(8,128)(2,1)S(1)} %pack.1.refs_0_, bf16[4,512,128]{2,1,0:T(8,128)(2,1)S(1)} %collective-permute-done.15.refs_0_.refs_1_), custom_call_target="tpu_custom_call" | custom-call | flops 2147483648 | bytes 1605636 | tf_op jit(solution)/shard_map/gather_grad/pallas_call | solution.py:36
  75.1 2.9 %collective-permute-start.18 = (bf16[1024,128]{1,0:T(8,128)(2,1)S(1)}, bf16[1024,128]{1,0:T(8,128)(2,1)S(1)}, u32[]{:S(2)}, u32[]{:S(2)}) collective-permute-start(bf16[1024,128]{1,0:T(8,128)(2,1)S(1)} %add_up.2), channel_id=1, source_target_pairs={{0,4},{1,5},{2,6},{3,7},{4,0},{5,1},{6,2},{7,3},{8,12},{9,13},{10,... | collective-permute-start | bytes 786440 | tf_op jit(solution)/shard_map/ppermute | solution.py:66
  78.1 0.1 cut_line.1
  78.2 1.8 %collective-permute-start.23 = (bf16[2,64,640]{2,1,0:T(8,128)(2,1)S(1)}, bf16[2,64,640]{2,1,0:T(8,128)(2,1)S(1)}, u32[]{:S(2)}, u32[]{:S(2)}) collective-permute-start(bf16[2,64,640]{2,1,0:T(8,128)(2,1)S(1)} %get-tuple-element.99), channel_id=1, source_target_pairs={{0,2},{1,3},{2,0},{3,1},{4,6},{5,7},{6,4},{7,5},{8,10},{9,11},{10,... | collective-permute-start | bytes 491528 | tf_op jit(solution)/shard_map/ppermute | solution.py:66
  80.0 2.3 %gather_grad.8.here_ref = f32[1024,128]{1,0:T(8,128)S(1)} custom-call(s32[1]{0:T(128)S(6)} %mul.38.base_ref, s32[4,2,2,512]{3,2,1,0:T(2,128)S(1)} %pad_add_fusion.key_ref, bf16[4,512,128]{2,1,0:T(8,128)(2,1)S(1)} %pack.1.refs_0_, bf16[4,512,128]{2,1,0:T(8,128)(2,1)S(1)} %collective-permute-done.15.refs_0_.refs_1_), custom_call_target="tpu_custom_call" | custom-call | flops 2147483648 | bytes 1605636 | tf_op jit(solution)/shard_map/gather_grad/pallas_call | solution.py:36
  82.3 3.9 %collective-permute-done.23.came_ref = bf16[2,64,640]{2,1,0:T(8,128)(2,1)S(1)} collective-permute-done((bf16[2,64,640]{2,1,0:T(8,128)(2,1)S(1)}, bf16[2,64,640]{2,1,0:T(8,128)(2,1)S(1)}, u32[]{:S(2)}, u32[]{:S(2)}) %collective-permute-start.23) | collective-permute-done | bytes 163872 | tf_op jit(solution)/shard_map/ppermute | solution.py:66
  86.2 4.1 %collective-permute-start.24 = (bf16[1,64,640]{2,1,0:T(8,128)(2,1)S(1)}, bf16[1,64,640]{2,1,0:T(8,128)(2,1)S(1)}, u32[]{:S(2)}, u32[]{:S(2)}) collective-permute-start(bf16[1,64,640]{2,1,0:T(8,128)(2,1)S(1)} %get-tuple-element.102), channel_id=1, source_target_pairs={{0,4},{1,5},{2,6},{3,7},{4,0},{5,1},{6,2},{7,3},{8,12},{9,13},{10,... | collective-permute-start | bytes 245768 | tf_op jit(solution)/shard_map/ppermute | solution.py:66
  90.4 2.4 %collective-permute-done.24 = bf16[1,64,640]{2,1,0:T(8,128)(2,1)S(1)} collective-permute-done((bf16[1,64,640]{2,1,0:T(8,128)(2,1)S(1)}, bf16[1,64,640]{2,1,0:T(8,128)(2,1)S(1)}, u32[]{:S(2)}, u32[]{:S(2)}) %collective-permute-start.24) | collective-permute-done | bytes 81952 | tf_op jit(solution)/shard_map/ppermute | solution.py:66
  92.7 1.2 %collective-permute-start.27 = (bf16[64,640]{1,0:T(8,128)(2,1)S(1)}, bf16[64,640]{1,0:T(8,128)(2,1)S(1)}, u32[]{:S(2)}, u32[]{:S(2)}) collective-permute-start(bf16[64,640]{1,0:T(8,128)(2,1)S(1)} %add_up.3.refs_0_), channel_id=1, source_target_pairs={{0,24},{8,16},{16,8},{24,0},{1,25},{9,17},{17,9},{25,1},{2,26},{10... | collective-permute-start | bytes 245768 | tf_op jit(solution)/shard_map/ppermute | solution.py:62
  94.0 0.8 collective-permute-start.26
  94.8 1.5 %collective-permute-start.25 = (bf16[64,640]{1,0:T(8,128)(2,1)S(1)}, bf16[64,640]{1,0:T(8,128)(2,1)S(1)}, u32[]{:S(2)}, u32[]{:S(2)}) collective-permute-start(bf16[64,640]{1,0:T(8,128)(2,1)S(1)} %add_up.3.refs_0_), channel_id=1, source_target_pairs={{0,8},{8,0},{16,24},{24,16},{1,9},{9,1},{17,25},{25,17},{2,10},{10... | collective-permute-start | bytes 245768 | tf_op jit(solution)/shard_map/ppermute | solution.py:62
  96.3 0.8 table_sums.3
  97.1 1.1 %collective-permute-done.27.refs_3_ = bf16[64,640]{1,0:T(8,128)(2,1)S(1)} collective-permute-done((bf16[64,640]{1,0:T(8,128)(2,1)S(1)}, bf16[64,640]{1,0:T(8,128)(2,1)S(1)}, u32[]{:S(2)}, u32[]{:S(2)}) %collective-permute-start.27) | collective-permute-done | bytes 81952 | tf_op jit(solution)/shard_map/ppermute | solution.py:62
  98.2 0.8 collective-permute-done.26.refs_2_
  99.0 0.2 collective-permute-done.25.refs_1_
  99.2 0.9 assemble.1
  (29 shorter events, 0.3 us)
Async XLA Ops:
  1.7 17.8 %collective-permute-start = (bf16[1024,128]{1,0:T(8,128)(2,1)S(1)}, bf16[1024,128]{1,0:T(8,128)(2,1)S(1)}, u32[]{:S(2)}, u32[]{:S(2)}) collective-permute-start(bf16[1024,128]{1,0:T(8,128)(2,1)S(1)} %pad_maximum_fusion.chunk_ref), channel_id=1, source_target_pairs={{0,4},{1,5},{2,6},{3,7},{4,0},{5,1},{6,2},{7,3},{8,12},{9,13},{10,... | collective-permute-start | bytes 786440 | tf_op jit(solution)/shard_map/ppermute | solution.py:66
  6.5 1.7 %collective-permute-start.1 = (s32[2,512]{1,0:T(2,128)S(1)}, s32[2,512]{1,0:T(2,128)S(1)}, u32[]{:S(2)}, u32[]{:S(2)}) collective-permute-start(s32[2,512]{1,0:T(2,128)S(1)} %get-tuple-element.110), channel_id=1, source_target_pairs={{0,1},{1,0},{2,3},{3,2},{4,5},{5,4},{6,7},{7,6},{8,9},{9,8},{10,11... | collective-permute-start | bytes 12296 | tf_op jit(solution)/shard_map/ppermute | solution.py:69
  6.6 13.9 %collective-permute-start.6 = (bf16[1024,128]{1,0:T(8,128)(2,1)S(1)}, bf16[1024,128]{1,0:T(8,128)(2,1)S(1)}, u32[]{:S(2)}, u32[]{:S(2)}) collective-permute-start(bf16[1024,128]{1,0:T(8,128)(2,1)S(1)} %pad_maximum_fusion.chunk_ref), channel_id=1, source_target_pairs={{0,2},{1,3},{2,0},{3,1},{4,6},{5,7},{6,4},{7,5},{8,10},{9,11},{10,... | collective-permute-start | bytes 786440 | tf_op jit(solution)/shard_map/ppermute | solution.py:66
  8.2 3.7 %collective-permute-start.3 = (s32[2,2,512]{2,1,0:T(2,128)S(1)}, s32[2,2,512]{2,1,0:T(2,128)S(1)}, u32[]{:S(2)}, u32[]{:S(2)}) collective-permute-start(s32[2,2,512]{2,1,0:T(2,128)S(1)} %get-tuple-element.108), channel_id=1, source_target_pairs={{0,16},{8,24},{16,0},{24,8},{1,17},{9,25},{17,1},{25,9},{2,18},{10... | collective-permute-start | bytes 24584 | tf_op jit(solution)/shard_map/ppermute | solution.py:62
  9.8 3.7 %collective-permute-start.2 = (s32[2,2,512]{2,1,0:T(2,128)S(1)}, s32[2,2,512]{2,1,0:T(2,128)S(1)}, u32[]{:S(2)}, u32[]{:S(2)}) collective-permute-start(s32[2,2,512]{2,1,0:T(2,128)S(1)} %get-tuple-element.108), channel_id=1, source_target_pairs={{0,8},{8,0},{16,24},{24,16},{1,9},{9,1},{17,25},{25,17},{2,10},{10... | collective-permute-start | bytes 24584 | tf_op jit(solution)/shard_map/ppermute | solution.py:62
  11.3 4.5 %collective-permute-start.4 = (s32[2,2,512]{2,1,0:T(2,128)S(1)}, s32[2,2,512]{2,1,0:T(2,128)S(1)}, u32[]{:S(2)}, u32[]{:S(2)}) collective-permute-start(s32[2,2,512]{2,1,0:T(2,128)S(1)} %get-tuple-element.108), channel_id=1, source_target_pairs={{0,24},{8,16},{16,8},{24,0},{1,25},{9,17},{17,9},{25,1},{2,26},{10... | collective-permute-start | bytes 24584 | tf_op jit(solution)/shard_map/ppermute | solution.py:62
  19.5 7.0 %collective-permute-start.5 = (bf16[1024,128]{1,0:T(8,128)(2,1)S(1)}, bf16[1024,128]{1,0:T(8,128)(2,1)S(1)}, u32[]{:S(2)}, u32[]{:S(2)}) collective-permute-start(bf16[1024,128]{1,0:T(8,128)(2,1)S(1)} %collective-permute-done.chunk_ref), channel_id=1, source_target_pairs={{0,2},{1,3},{2,0},{3,1},{4,6},{5,7},{6,4},{7,5},{8,10},{9,11},{10,... | collective-permute-start | bytes 786440 | tf_op jit(solution)/shard_map/ppermute | solution.py:66
  27.7 2.0 %collective-permute-start.7 = (bf16[4,512,128]{2,1,0:T(8,128)(2,1)S(1)}, bf16[4,512,128]{2,1,0:T(8,128)(2,1)S(1)}, u32[]{:S(2)}, u32[]{:S(2)}) collective-permute-start(bf16[4,512,128]{2,1,0:T(8,128)(2,1)S(1)} %fetch.9), channel_id=1, source_target_pairs={{0,1},{1,0},{2,3},{3,2},{4,5},{5,4},{6,7},{7,6},{8,9},{9,8},{10,11... | collective-permute-start | bytes 1572872 | tf_op jit(solution)/shard_map/ppermute | solution.py:69
  27.8 10.7 %copy-start = (bf16[512,512]{1,0:T(8,128)(2,1)S(1)}, bf16[512,512]{1,0:T(8,128)(2,1)}, u32[]{:S(2)}) copy-start(bf16[512,512]{1,0:T(8,128)(2,1)} %c_ref.1) | copy-start | bytes 1572868
  27.8 10.7 %copy-start.1 = (bf16[512,2048]{1,0:T(8,128)(2,1)S(1)}, bf16[512,2048]{1,0:T(8,128)(2,1)}, u32[]{:S(2)}) copy-start(bf16[512,2048]{1,0:T(8,128)(2,1)} %wp_ref.1) | copy-start | bytes 6291460
  27.8 10.7 %copy-start.2 = (bf16[512,512]{1,0:T(8,128)(2,1)S(1)}, bf16[512,512]{1,0:T(8,128)(2,1)}, u32[]{:S(2)}) copy-start(bf16[512,512]{1,0:T(8,128)(2,1)} %wo_ref.1) | copy-start | bytes 1572868
  27.8 10.7 %copy-start.3 = (f32[512]{0:T(512)S(1)}, f32[512]{0:T(512)}, u32[]{:S(2)}) copy-start(f32[512]{0:T(512)} %param.16) | copy-start | bytes 6148
  29.8 6.4 %collective-permute-start.8 = (bf16[512,128]{1,0:T(8,128)(2,1)S(1)}, bf16[512,128]{1,0:T(8,128)(2,1)S(1)}, u32[]{:S(2)}, u32[]{:S(2)}) collective-permute-start(bf16[512,128]{1,0:T(8,128)(2,1)S(1)} %get-tuple-element.64), channel_id=1, source_target_pairs={{0,8},{8,0},{16,24},{24,16},{1,9},{9,1},{17,25},{25,17},{2,10},{10... | collective-permute-start | bytes 393224 | tf_op jit(solution)/shard_map/ppermute | solution.py:62
  30.5 8.1 %collective-permute-start.9 = (bf16[512,128]{1,0:T(8,128)(2,1)S(1)}, bf16[512,128]{1,0:T(8,128)(2,1)S(1)}, u32[]{:S(2)}, u32[]{:S(2)}) collective-permute-start(bf16[512,128]{1,0:T(8,128)(2,1)S(1)} %get-tuple-element.65), channel_id=1, source_target_pairs={{0,16},{8,24},{16,0},{24,8},{1,17},{9,25},{17,1},{25,9},{2,18},{10... | collective-permute-start | bytes 393224 | tf_op jit(solution)/shard_map/ppermute | solution.py:62
  31.9 6.7 %collective-permute-start.10 = (bf16[512,128]{1,0:T(8,128)(2,1)S(1)}, bf16[512,128]{1,0:T(8,128)(2,1)S(1)}, u32[]{:S(2)}, u32[]{:S(2)}) collective-permute-start(bf16[512,128]{1,0:T(8,128)(2,1)S(1)} %get-tuple-element.66), channel_id=1, source_target_pairs={{0,24},{8,16},{16,8},{24,0},{1,25},{9,17},{17,9},{25,1},{2,26},{10... | collective-permute-start | bytes 393224 | tf_op jit(solution)/shard_map/ppermute | solution.py:62
  49.7 3.6 %collective-permute-start.14 = (bf16[4,256,640]{2,1,0:T(8,128)(2,1)S(1)}, bf16[4,256,640]{2,1,0:T(8,128)(2,1)S(1)}, u32[]{:S(2)}, u32[]{:S(2)}) collective-permute-start(bf16[4,256,640]{2,1,0:T(8,128)(2,1)S(1)} %get-tuple-element.75), channel_id=1, source_target_pairs={{0,1},{1,0},{2,3},{3,2},{4,5},{5,4},{6,7},{7,6},{8,9},{9,8},{10,11... | collective-permute-start | bytes 3932168 | tf_op jit(solution)/shard_map/ppermute | solution.py:69
  49.8 6.3 %collective-permute-start.11 = (bf16[512,128]{1,0:T(8,128)(2,1)S(1)}, bf16[512,128]{1,0:T(8,128)(2,1)S(1)}, u32[]{:S(2)}, u32[]{:S(2)}) collective-permute-start(bf16[512,128]{1,0:T(8,128)(2,1)S(1)} %get-tuple-element.69), channel_id=1, source_target_pairs={{0,8},{8,0},{16,24},{24,16},{1,9},{9,1},{17,25},{25,17},{2,10},{10... | collective-permute-start | bytes 393224 | tf_op jit(solution)/shard_map/ppermute | solution.py:62
  51.3 8.4 %collective-permute-start.12 = (bf16[512,128]{1,0:T(8,128)(2,1)S(1)}, bf16[512,128]{1,0:T(8,128)(2,1)S(1)}, u32[]{:S(2)}, u32[]{:S(2)}) collective-permute-start(bf16[512,128]{1,0:T(8,128)(2,1)S(1)} %get-tuple-element.70), channel_id=1, source_target_pairs={{0,16},{8,24},{16,0},{24,8},{1,17},{9,25},{17,1},{25,9},{2,18},{10... | collective-permute-start | bytes 393224 | tf_op jit(solution)/shard_map/ppermute | solution.py:62
  51.8 7.9 %collective-permute-start.13 = (bf16[512,128]{1,0:T(8,128)(2,1)S(1)}, bf16[512,128]{1,0:T(8,128)(2,1)S(1)}, u32[]{:S(2)}, u32[]{:S(2)}) collective-permute-start(bf16[512,128]{1,0:T(8,128)(2,1)S(1)} %get-tuple-element.71), channel_id=1, source_target_pairs={{0,24},{8,16},{16,8},{24,0},{1,25},{9,17},{17,9},{25,1},{2,26},{10... | collective-permute-start | bytes 393224 | tf_op jit(solution)/shard_map/ppermute | solution.py:62
  59.7 3.4 %collective-permute-start.15 = (bf16[4,512,128]{2,1,0:T(8,128)(2,1)S(1)}, bf16[4,512,128]{2,1,0:T(8,128)(2,1)S(1)}, u32[]{:S(2)}, u32[]{:S(2)}) collective-permute-start(bf16[4,512,128]{2,1,0:T(8,128)(2,1)S(1)} %pack.1.refs_0_), channel_id=1, source_target_pairs={{0,1},{1,0},{2,3},{3,2},{4,5},{5,4},{6,7},{7,6},{8,9},{9,8},{10,11... | collective-permute-start | bytes 1572872 | tf_op jit(solution)/shard_map/ppermute | solution.py:69
  59.8 10.1 %collective-permute-start.19 = (bf16[2,128,640]{2,1,0:T(8,128)(2,1)S(1)}, bf16[2,128,640]{2,1,0:T(8,128)(2,1)S(1)}, u32[]{:S(2)}, u32[]{:S(2)}) collective-permute-start(bf16[2,128,640]{2,1,0:T(8,128)(2,1)S(1)} %get-tuple-element.77), channel_id=1, source_target_pairs={{0,8},{8,0},{16,24},{24,16},{1,9},{9,1},{17,25},{25,17},{2,10},{10... | collective-permute-start | bytes 983048 | tf_op jit(solution)/shard_map/ppermute | solution.py:62
  60.4 9.8 %collective-permute-start.20 = (bf16[2,128,640]{2,1,0:T(8,128)(2,1)S(1)}, bf16[2,128,640]{2,1,0:T(8,128)(2,1)S(1)}, u32[]{:S(2)}, u32[]{:S(2)}) collective-permute-start(bf16[2,128,640]{2,1,0:T(8,128)(2,1)S(1)} %get-tuple-element.79), channel_id=1, source_target_pairs={{0,16},{8,24},{16,0},{24,8},{1,17},{9,25},{17,1},{25,9},{2,18},{10... | collective-permute-start | bytes 983048 | tf_op jit(solution)/shard_map/ppermute | solution.py:62
  64.3 10.7 %collective-permute-start.16 = (bf16[1024,128]{1,0:T(8,128)(2,1)S(1)}, bf16[1024,128]{1,0:T(8,128)(2,1)S(1)}, u32[]{:S(2)}, u32[]{:S(2)}) collective-permute-start(bf16[1024,128]{1,0:T(8,128)(2,1)S(1)} %gather_grad.6), channel_id=1, source_target_pairs={{0,2},{1,3},{2,0},{3,1},{4,6},{5,7},{6,4},{7,5},{8,10},{9,11},{10,... | collective-permute-start | bytes 786440 | tf_op jit(solution)/shard_map/ppermute | solution.py:66
  68.0 22.3 %collective-permute-start.17 = (bf16[1024,128]{1,0:T(8,128)(2,1)S(1)}, bf16[1024,128]{1,0:T(8,128)(2,1)S(1)}, u32[]{:S(2)}, u32[]{:S(2)}) collective-permute-start(bf16[1024,128]{1,0:T(8,128)(2,1)S(1)} %gather_grad.9), channel_id=1, source_target_pairs={{0,2},{1,3},{2,0},{3,1},{4,6},{5,7},{6,4},{7,5},{8,10},{9,11},{10,... | collective-permute-start | bytes 786440 | tf_op jit(solution)/shard_map/ppermute | solution.py:66
  70.5 7.6 %collective-permute-start.21 = (bf16[1,128,640]{2,1,0:T(8,128)(2,1)S(1)}, bf16[1,128,640]{2,1,0:T(8,128)(2,1)S(1)}, u32[]{:S(2)}, u32[]{:S(2)}) collective-permute-start(bf16[1,128,640]{2,1,0:T(8,128)(2,1)S(1)} %get-tuple-element.94), channel_id=1, source_target_pairs={{0,16},{8,24},{16,0},{24,8},{1,17},{9,25},{17,1},{25,9},{2,18},{10... | collective-permute-start | bytes 491528 | tf_op jit(solution)/shard_map/ppermute | solution.py:62
  71.9 6.1 %collective-permute-start.22 = (bf16[1,128,640]{2,1,0:T(8,128)(2,1)S(1)}, bf16[1,128,640]{2,1,0:T(8,128)(2,1)S(1)}, u32[]{:S(2)}, u32[]{:S(2)}) collective-permute-start(bf16[1,128,640]{2,1,0:T(8,128)(2,1)S(1)} %get-tuple-element.95), channel_id=1, source_target_pairs={{0,8},{8,0},{16,24},{24,16},{1,9},{9,1},{17,25},{25,17},{2,10},{10... | collective-permute-start | bytes 491528 | tf_op jit(solution)/shard_map/ppermute | solution.py:62
  75.1 21.2 %collective-permute-start.18 = (bf16[1024,128]{1,0:T(8,128)(2,1)S(1)}, bf16[1024,128]{1,0:T(8,128)(2,1)S(1)}, u32[]{:S(2)}, u32[]{:S(2)}) collective-permute-start(bf16[1024,128]{1,0:T(8,128)(2,1)S(1)} %add_up.2), channel_id=1, source_target_pairs={{0,4},{1,5},{2,6},{3,7},{4,0},{5,1},{6,2},{7,3},{8,12},{9,13},{10,... | collective-permute-start | bytes 786440 | tf_op jit(solution)/shard_map/ppermute | solution.py:66
  78.2 8.0 %collective-permute-start.23 = (bf16[2,64,640]{2,1,0:T(8,128)(2,1)S(1)}, bf16[2,64,640]{2,1,0:T(8,128)(2,1)S(1)}, u32[]{:S(2)}, u32[]{:S(2)}) collective-permute-start(bf16[2,64,640]{2,1,0:T(8,128)(2,1)S(1)} %get-tuple-element.99), channel_id=1, source_target_pairs={{0,2},{1,3},{2,0},{3,1},{4,6},{5,7},{6,4},{7,5},{8,10},{9,11},{10,... | collective-permute-start | bytes 491528 | tf_op jit(solution)/shard_map/ppermute | solution.py:66
  86.2 6.5 %collective-permute-start.24 = (bf16[1,64,640]{2,1,0:T(8,128)(2,1)S(1)}, bf16[1,64,640]{2,1,0:T(8,128)(2,1)S(1)}, u32[]{:S(2)}, u32[]{:S(2)}) collective-permute-start(bf16[1,64,640]{2,1,0:T(8,128)(2,1)S(1)} %get-tuple-element.102), channel_id=1, source_target_pairs={{0,4},{1,5},{2,6},{3,7},{4,0},{5,1},{6,2},{7,3},{8,12},{9,13},{10,... | collective-permute-start | bytes 245768 | tf_op jit(solution)/shard_map/ppermute | solution.py:66
  92.7 5.5 %collective-permute-start.27 = (bf16[64,640]{1,0:T(8,128)(2,1)S(1)}, bf16[64,640]{1,0:T(8,128)(2,1)S(1)}, u32[]{:S(2)}, u32[]{:S(2)}) collective-permute-start(bf16[64,640]{1,0:T(8,128)(2,1)S(1)} %add_up.3.refs_0_), channel_id=1, source_target_pairs={{0,24},{8,16},{16,8},{24,0},{1,25},{9,17},{17,9},{25,1},{2,26},{10... | collective-permute-start | bytes 245768 | tf_op jit(solution)/shard_map/ppermute | solution.py:62
  94.0 5.1 %collective-permute-start.26 = (bf16[64,640]{1,0:T(8,128)(2,1)S(1)}, bf16[64,640]{1,0:T(8,128)(2,1)S(1)}, u32[]{:S(2)}, u32[]{:S(2)}) collective-permute-start(bf16[64,640]{1,0:T(8,128)(2,1)S(1)} %add_up.3.refs_0_), channel_id=1, source_target_pairs={{0,16},{8,24},{16,0},{24,8},{1,17},{9,25},{17,1},{25,9},{2,18},{10... | collective-permute-start | bytes 245768 | tf_op jit(solution)/shard_map/ppermute | solution.py:62
  94.8 4.4 %collective-permute-start.25 = (bf16[64,640]{1,0:T(8,128)(2,1)S(1)}, bf16[64,640]{1,0:T(8,128)(2,1)S(1)}, u32[]{:S(2)}, u32[]{:S(2)}) collective-permute-start(bf16[64,640]{1,0:T(8,128)(2,1)S(1)} %add_up.3.refs_0_), channel_id=1, source_target_pairs={{0,8},{8,0},{16,24},{24,16},{1,9},{9,1},{17,25},{25,17},{2,10},{10... | collective-permute-start | bytes 245768 | tf_op jit(solution)/shard_map/ppermute | solution.py:62
